TPU v7x, 32 devices: a whole 2x2x4 slice. The times are simulated.
32 devices in a mesh: groups: 2 (over y), pool: 4 (over z), tensor: 4 (over x, core).
Axes of the slice: x: 2, y: 2, z: 4, core: 2. Of those that a mesh axis runs over, the one named last changes fastest.
Arguments:
- tokens: bfloat16 [8192, 8192], P(('groups', 'pool'), 'tensor'), parts along dimension 0, may hold values from -6 to 6
- value_weight: bfloat16 [8192, 1024], P('tensor'), may hold values from -0.0625 to 0.0625
- adapter_down_weight: bfloat16 [32, 8192, 64], P(('groups', 'pool'), 'tensor'), parts along dimension 0, may hold values from -0.0625 to 0.0625
- adapter_up_weight: bfloat16 [32, 64, 1024], P(('groups', 'pool'), None, 'tensor'), parts along dimension 0, may hold values from -0.75 to 0.75
- adapter_of_block: int32 [8, 8], P(('groups', 'pool')), parts along dimension 0, may hold values from 0 to 15, as said below
- adapter_pool_slot: int32 [32], P('groups'), parts along dimension 0, may hold values from 0 to 15, as said below
- live_block_tokens: int32 [8, 8], P(('groups', 'pool')), parts along dimension 0, may hold values from 1 to 128, 576 in all within a row
Outputs:
- value_rows: bfloat16 [8192, 1024], P(('groups', 'pool'), 'tensor'), parts along dimension 0
There are 2 independent parts, one for each index of `groups`. A program takes and returns all parts, laid end to end along the dimension named above; an argument that names none is the same for every part. Nothing has to cross between parts.
Inputs may be any that keep to these rules, and one draw needn't show every extreme that they name: `adapter_of_block`: adapter numbers below 16. The blocks of one index of pool use adapters whose slots lie on at most 2 blocks' worth of any one pool index (slot s lies on pool index s // 4); in every draw some pool index holds the adapter of 2 blocks of every pool index. `adapter_pool_slot`: each slot holds exactly one adapter.
All inputs are finite; a program needn't handle non-finite values.
Results may differ from a plain program's by a relative error of at most 0.0033.
Values may be sent and summed in bfloat16 or wider, within the bound.
No kernel may reach another device: no remote copies, remote signals or barrier semaphores. Data moves between devices by JAX's collectives and lax.ppermute only.
A program may use at most 192 MiB of HBM per device.

v0:
```python
import jax
import jax.numpy as jnp
from jax import lax
from jax.sharding import PartitionSpec as P

ADAPTER_SCALE = 0.5


def on_device(
    tokens,
    value_weight,
    adapter_down_weight,
    adapter_up_weight,
    adapter_of_block,
    adapter_pool_slot,
    live_block_tokens,
):
    pool_size = lax.axis_size("pool")
    row_count, width_local = tokens.shape
    blocks_on_shard = adapter_of_block.shape[1]
    rows_by_block = row_count // blocks_on_shard
    shard_output_width = adapter_up_weight.shape[2]
    blocks_per_holder = adapter_down_weight.shape[0]
    capacity = -(-blocks_on_shard // pool_size)
    base_part = jnp.dot(tokens, value_weight, preferred_element_type=jnp.float32)
    base_output_sum = lax.psum_scatter(base_part, "tensor", scatter_dimension=1, tiled=True)
    block_names = adapter_of_block[0]
    table_hits = (
        block_names[:, None] == jnp.arange(adapter_pool_slot.shape[0], dtype=jnp.int32)[None, :]
    )
    slot_ids = jnp.sum(jnp.where(table_hits, adapter_pool_slot[None, :], 0), axis=1)
    owners = slot_ids // blocks_per_holder
    local_slot = slot_ids % blocks_per_holder
    order_ids = jnp.arange(blocks_on_shard, dtype=jnp.int32)
    same_owner = (owners[:, None] == owners[None, :]) & (order_ids[:, None] < order_ids[None, :])
    rank_in_owner = jnp.sum(same_owner.astype(jnp.int32), axis=0)
    target = owners * capacity + rank_in_owner
    requests = jnp.full((pool_size * capacity,), -1, jnp.int32).at[target].set(local_slot)
    requests = requests.reshape(pool_size, capacity)
    row_blocks = tokens.reshape(blocks_on_shard, rows_by_block, width_local)
    outgoing = jnp.zeros((pool_size * capacity, rows_by_block, width_local), tokens.dtype)
    outgoing = (
        outgoing.at[target].set(row_blocks).reshape(pool_size, capacity, rows_by_block, width_local)
    )
    arrived = lax.all_to_all(outgoing, "pool", split_axis=0, concat_axis=0, tiled=True)
    wanted = lax.all_to_all(requests, "pool", split_axis=0, concat_axis=0, tiled=True)
    picked_pool_slots = jnp.clip(wanted, 0, blocks_per_holder - 1)
    down_weight_panels = adapter_down_weight[picked_pool_slots]
    up_weight_panels = adapter_up_weight[picked_pool_slots]
    partial_value = jnp.einsum(
        "pkbd,pkdr->pkbr", arrived, down_weight_panels, preferred_element_type=jnp.float32
    )
    shrunk = lax.psum(partial_value, "tensor").astype(jnp.bfloat16)
    adapter_delta_rows = jnp.einsum(
        "pkbr,pkro->pkbo", shrunk, up_weight_panels, preferred_element_type=jnp.float32
    )
    returned = lax.all_to_all(adapter_delta_rows, "pool", split_axis=0, concat_axis=0, tiled=True)
    adapter_delta_blocks = returned.reshape(
        pool_size * capacity, rows_by_block, shard_output_width
    )[target]
    live_rows = jnp.arange(rows_by_block, dtype=jnp.int32)[None, :] < live_block_tokens[0][:, None]
    combined_output = (
        base_output_sum.reshape(blocks_on_shard, rows_by_block, shard_output_width)
        + ADAPTER_SCALE * adapter_delta_blocks
    )
    combined_output = jnp.where(
        live_rows[:, :, None], combined_output, jnp.zeros_like(combined_output)
    )
    return combined_output.reshape(row_count, shard_output_width).astype(jnp.bfloat16)


def solution(mesh):
    return jax.shard_map(
        on_device,
        mesh=mesh,
        in_specs=(
            P(("groups", "pool"), "tensor"),
            P("tensor", None),
            P(("groups", "pool"), "tensor", None),
            P(("groups", "pool"), None, "tensor"),
            P(("groups", "pool"), None),
            P("groups"),
            P(("groups", "pool"), None),
        ),
        out_specs=P(("groups", "pool"), "tensor"),
        check_vma=False,
    )
```

profile of v0, /device:TPU:0, one launch (start us, length us, event | category | flops | bytes accessed | tf_op | source)
XLA Modules:
  0.0 186.0 jit_solution(18393859989401830967)
XLA Ops:
  6.5 0.0 copy-start
  6.5 0.9 select_reduce_fusion
  7.5 0.1 convert_reduce_fusion
  7.6 0.6 scatter_custom_fusion.1
  8.2 0.7 all_to_all.13
  8.9 6.3 %all-to-all-start.1 = ((s32[4,1,2]{2,1,0:T(1,128)}), s32[4,1,2]{2,1,0:T(1,128)S(1)}, u32[]{:S(2)}, u32[]{:S(2)}) async-start(s32[4,1,2]{2,1,0:T(1,128)} %bitcast.8), calls=%async_computation.2 | async-start | bytes 4096 | tf_op jit(solution)/shard_map/all_to_all | solution.py:46
  15.2 2.5 %broadcast_in_dim.22 = bf16[8,128,2048]{2,1,0:T(8,128)(2,1)} broadcast(bf16[]{:T(256)} %constant.18.clone.1), dimensions={} | broadcast | bytes 4194306 | tf_op jit(solution)/shard_map/broadcast_in_dim | solution.py:41
  17.7 11.0 %scatter_fusion = bf16[8,128,2048]{2,1,0:T(8,128)(2,1)} fusion(bf16[8,128,2048]{2,1,0:T(8,128)(2,1)} %broadcast_in_dim.22, s32[8]{0:T(128)S(1)} %fusion.6, bf16[8,128,2048]{2,1,0:T(8,128)(2,1)} %bitcast.45), kind=kCustom, calls=%fused_computation.3 | custom fusion | bytes 12582944 | tf_op jit(solution)/shard_map/scatter | solution.py:43
  28.6 0.0 all-to-all-done.1
  28.6 5.2 %all-to-all-start = ((bf16[4,2,128,2048]{3,2,1,0:T(8,128)(2,1)}), bf16[4,2,128,2048]{3,2,1,0:T(8,128)(2,1)}, u32[]{:S(2)}, u32[]{:S(2)}) async-start(bf16[4,2,128,2048]{3,2,1,0:T(8,128)(2,1)} %bitcast.42), calls=%async_computation.1 | async-start | bytes 8388608 | tf_op jit(solution)/shard_map/all_to_all | solution.py:45
  33.8 0.0 reduce-scatter.2.cloned.1.call-start
  33.8 9.9 %fusion.9 = f32[1024,1024]{1,0:T(8,128)} fusion(bf16[1024,2048]{1,0:T(8,128)(2,1)} %param.7, bf16[2048,1024]{1,0:T(8,128)(2,1)} %param.8), kind=kOutput, calls=%fused_computation.36 | convolution fusion | flops 4294967296 | bytes 12582912 | tf_op jit(solution)/shard_map/dot_general | solution.py:25
  43.7 0.0 reduce-scatter.2.cloned.1.call-update
  43.7 0.1 copy.19
  43.8 0.1 copy.20
  43.9 0.1 reshape.156
  44.0 0.0 copy-done
  44.0 0.0 copy-start.1
  44.0 0.7 gather_fusion
  44.7 0.2 copy-done.1
  44.9 1.3 gather_fusion.1
  46.2 80.7 %all-to-all-done = bf16[4,2,128,2048]{3,2,1,0:T(8,128)(2,1)} async-done(((bf16[4,2,128,2048]{3,2,1,0:T(8,128)(2,1)}), bf16[4,2,128,2048]{3,2,1,0:T(8,128)(2,1)}, u32[]{:S(2)}, u32[]{:S(2)}) %all-to-all-start) | async-done | bytes 4194336 | tf_op jit(solution)/shard_map/all_to_all | solution.py:45
  126.8 0.0 copy-start.2
  126.8 3.8 %fusion.10 = f32[4,2,128,64]{2,3,1,0:T(8,128)S(1)} fusion(bf16[4,2,128,2048]{3,2,1,0:T(8,128)(2,1)} %all-to-all-done, bf16[4,2,2048,64]{2,3,1,0:T(8,128)(2,1)S(1)} %bitcast.43), kind=kOutput, calls=%fused_computation.37 | convolution fusion | flops 268435456 | bytes 6553600 | tf_op jit(solution)/shard_map/pkbd,pkdr->pkbr/dot_general | solution.py:50
  130.6 13.5 %all-reduce.1 = bf16[4,2,128,64]{2,3,1,0:T(8,128)(2,1)S(1)} all-reduce(f32[4,2,128,64]{2,3,1,0:T(8,128)S(1)} %fusion.10), channel_id=1, replica_groups=mesh['groups'=2,'pool'=4,'tensor'=4] {'tensor'}, use_global_device_ids=true, to_apply=%region_5.6 | all-reduce | flops 65536 | bytes 393216 | tf_op jit(solution)/shard_map/psum | solution.py:53
  144.1 2.3 %fusion.11 = f32[4,2,128,256]{3,2,1,0:T(8,128)} fusion(bf16[4,2,128,64]{2,3,1,0:T(8,128)(2,1)S(1)} %all-reduce.1, bf16[4,2,64,256]{3,2,1,0:T(8,128)(2,1)} %bitcast.46), kind=kOutput, calls=%fused_computation.38 | convolution fusion | flops 33554432 | bytes 1441792 | tf_op jit(solution)/shard_map/pkbr,pkro->pkbo/dot_general | solution.py:54
  146.4 3.5 %all-to-all-start.2 = ((f32[4,2,128,256]{3,2,1,0:T(8,128)}), f32[4,2,128,256]{3,2,1,0:T(8,128)S(1)}, u32[]{:S(2)}, u32[]{:S(2)}) async-start(f32[4,2,128,256]{3,2,1,0:T(8,128)} %fusion.11), calls=%async_computation.3 | async-start | bytes 2097152 | tf_op jit(solution)/shard_map/all_to_all | solution.py:57
  149.9 0.0 copy-done.2
  149.9 0.1 fusion.4
  150.0 26.2 %all-to-all-done.2 = f32[4,2,128,256]{3,2,1,0:T(8,128)S(1)} async-done(((f32[4,2,128,256]{3,2,1,0:T(8,128)}), f32[4,2,128,256]{3,2,1,0:T(8,128)S(1)}, u32[]{:S(2)}, u32[]{:S(2)}) %all-to-all-start.2) | async-done | bytes 1048608 | tf_op jit(solution)/shard_map/all_to_all | solution.py:57
  176.2 0.6 gather_fusion.2
  176.8 0.1 broadcast_multiply_fusion
  176.9 0.0 reduce-scatter.2.cloned.1.call-done
  176.9 2.2 %fusion.1 = bf16[1024,256]{1,0:T(8,128)(2,1)} fusion(f32[1024,256]{1,0:T(8,128)} %reduce-scatter.2.cloned.1.call-done, f32[8,128,256]{2,1,0:T(8,128)S(1)} %broadcast_multiply_fusion, pred[1024]{0:T(1024)(128)(4,1)S(1)} %fusion.4), kind=kLoop, calls=%fused_computation.7 | loop fusion | flops 786432 | bytes 2622464 | tf_op jit(solution)/shard_map/convert_element_type | solution.py:69
  (5 shorter events, 0.1 us)
Async XLA Ops:
  6.5 37.5 %copy-start = (bf16[4,2048,64]{1,2,0:T(8,128)(2,1)S(1)}, bf16[4,2048,64]{1,2,0:T(8,128)(2,1)}, u32[]{:S(2)}) copy-start(bf16[4,2048,64]{1,2,0:T(8,128)(2,1)} %param.9) | copy-start | bytes 3145732
  8.9 19.8 %all-to-all-start.1 = ((s32[4,1,2]{2,1,0:T(1,128)}), s32[4,1,2]{2,1,0:T(1,128)S(1)}, u32[]{:S(2)}, u32[]{:S(2)}) async-start(s32[4,1,2]{2,1,0:T(1,128)} %bitcast.8), calls=%async_computation.2 | async-start | bytes 4096 | tf_op jit(solution)/shard_map/all_to_all | solution.py:46
  28.6 98.2 %all-to-all-start = ((bf16[4,2,128,2048]{3,2,1,0:T(8,128)(2,1)}), bf16[4,2,128,2048]{3,2,1,0:T(8,128)(2,1)}, u32[]{:S(2)}, u32[]{:S(2)}) async-start(bf16[4,2,128,2048]{3,2,1,0:T(8,128)(2,1)} %bitcast.42), calls=%async_computation.1 | async-start | bytes 8388608 | tf_op jit(solution)/shard_map/all_to_all | solution.py:45
  33.8 143.1 %reduce-scatter.2.cloned.1.call-start = ((), (), s32[]{:S(2)}) async-start(), calls=%async_computation.4 | async-start | bytes 5242880 | tf_op jit(solution)/shard_map/reduce_scatter | solution.py:26
  44.0 0.9 copy-start.1
  126.8 23.1 %copy-start.2 = (s32[1,8]{1,0:T(1,128)S(1)}, s32[1,8]{1,0:T(1,128)}, u32[]{:S(2)}) copy-start(s32[1,8]{1,0:T(1,128)} %param.13) | copy-start | bytes 100
  146.4 29.8 %all-to-all-start.2 = ((f32[4,2,128,256]{3,2,1,0:T(8,128)}), f32[4,2,128,256]{3,2,1,0:T(8,128)S(1)}, u32[]{:S(2)}, u32[]{:S(2)}) async-start(f32[4,2,128,256]{3,2,1,0:T(8,128)} %fusion.11), calls=%async_computation.3 | async-start | bytes 2097152 | tf_op jit(solution)/shard_map/all_to_all | solution.py:57
Sparse Core Ops, SparseCore 0:
  43.8 45.8 reduce-scatter.1
where the time goes:
time: 187 us; the launch traced here: 186 us
  waiting for transfers between devices  107 us (57%)
  local copies, waits for them, and re-layouts  17.8 us (10%)
  matrix products  15.9 us (9%)
  starting transfers between devices  15 us (8%)
  blocking collectives  13.5 us (7%)
  between operations  13.5 us (7%)
  other arithmetic  3.47 us (2%)
    all_to_all x1, waiting for transfers between devices, on_device(): lax.all_to_all(outgoing, 'pool', split_axis=0, concat_axis=0, tiled=True)  80.7 us
    all_to_all x1, waiting for transfers between devices, on_device(): lax.all_to_all(adapter_delta_rows, 'pool', split_axis=0, concat_axis=0, t...  26.2 us
    psum x1, blocking collectives, on_device(): shrunk = lax.psum(partial_value, 'tensor').astype(jnp.bfloat16)  13.5 us
    scatter x1, local copies, waits for them, and re-layouts, on_device(): outgoing.at[target].set(row_blocks)  11 us
    dot_general x1, matrix products, on_device(): jnp.dot(tokens, value_weight, preferred_element_type=jnp.float32)  9.88 us
    all_to_all x1, starting transfers between devices, on_device(): lax.all_to_all(requests, 'pool', split_axis=0, concat_axis=0, tiled=True)  6.32 us
    all_to_all x1, starting transfers between devices, on_device(): lax.all_to_all(outgoing, 'pool', split_axis=0, concat_axis=0, tiled=True)  5.17 us
    dot_general x1, matrix products, on_device(): jnp.einsum('pkbd,pkdr->pkbr', arrived, down_weight_panels, preferred_elem...  3.76 us
  transfers between devices with their start and end apart: 4, of which 2 were waited for; matrix products, arithmetic and copies ran while one was open for 17% of the time, Pallas kernels for 0%

commit v1 on v0

v1 whole, which is shorter than its diff:
```python
import functools

import jax
import jax.numpy as jnp
from jax import lax
from jax.experimental import pallas as pl
from jax.experimental.pallas import tpu as pltpu
from jax.sharding import PartitionSpec as P

ADAPTER_SCALE = 0.5
ROW_TILE = 256
VMEM_BYTES = 32 * 1024 * 1024


def swap(value, axis, distance):
    pairs = [(i, i ^ distance) for i in range(lax.axis_size(axis))]
    return lax.ppermute(value, axis, pairs)


def base_kernel(chunks, tokens_ref, weight_ref, part_ref):
    del chunks
    tile = min(ROW_TILE, tokens_ref.shape[0])

    @pl.loop(0, tokens_ref.shape[0] // tile)
    def _(step):
        rows = pl.ds(pl.multiple_of(step * tile, tile), tile)
        part_ref[0, rows, :] = jnp.dot(
            tokens_ref[rows, :], weight_ref[...], preferred_element_type=jnp.float32
        )


def base_chunks(tokens, weight, chunks, width):
    rows, depth = tokens.shape
    count = chunks.shape[0]
    return pl.pallas_call(
        base_kernel,
        grid_spec=pltpu.PrefetchScalarGridSpec(
            num_scalar_prefetch=1,
            grid=(count,),
            in_specs=[
                pl.BlockSpec((rows, depth), lambda i, c: (0, 0)),
                pl.BlockSpec((depth, width), lambda i, c: (0, c[i])),
            ],
            out_specs=pl.BlockSpec((1, rows, width), lambda i, c: (i, 0, 0)),
        ),
        out_shape=jax.ShapeDtypeStruct((count, rows, width), jnp.float32),
        compiler_params=pltpu.CompilerParams(vmem_limit_bytes=VMEM_BYTES),
        cost_estimate=pl.CostEstimate(
            flops=2 * rows * depth * width * count,
            bytes_accessed=2 * rows * depth + (2 * depth + 4 * rows) * width * count,
            transcendentals=0,
        ),
    )(chunks, tokens, weight)


def pack_kernel(slots, down_ref, up_ref, *rest):
    del slots
    out_ref = rest[-1]
    depth = down_ref.shape[2]
    out_ref[:, :, :depth] = down_ref[...]
    out_ref[:, :, depth:] = up_ref[...]


def pack_panels(slots, down, up, after=None):
    count = slots.shape[0]
    rank, depth = down.shape[1:]
    width = up.shape[2]
    gate = [] if after is None else [after]
    return pl.pallas_call(
        pack_kernel,
        grid_spec=pltpu.PrefetchScalarGridSpec(
            num_scalar_prefetch=1,
            grid=(count,),
            in_specs=[
                pl.BlockSpec((1, rank, depth), lambda i, s: (s[i], 0, 0)),
                pl.BlockSpec((1, rank, width), lambda i, s: (s[i], 0, 0)),
            ]
            + [pl.BlockSpec(memory_space=pl.ANY)] * len(gate),
            out_specs=pl.BlockSpec((1, rank, depth + width), lambda i, s: (i, 0, 0)),
        ),
        out_shape=jax.ShapeDtypeStruct((count, rank, depth + width), down.dtype),
        compiler_params=pltpu.CompilerParams(vmem_limit_bytes=VMEM_BYTES),
    )(slots, down, up, *gate)


def shrink_kernel(scalars, token_ref, *refs):
    out_ref = refs[-1]

    def term(panel):
        out_ref[0] = lax.dot_general(
            panel, token_ref[0], (((1,), (1,)), ((), ())), preferred_element_type=jnp.float32
        )

    if len(refs) == 2:
        term(refs[0][0])
    else:
        term(jnp.where(scalars[0] != 0, refs[0][0], refs[1][0]))


def panel_spec(shape, column, row):
    return pl.BlockSpec(shape, lambda i, s: (s[row + i], 0, column))


def shrink(row_blocks, blocks, sources, first):
    count = blocks.shape[0]
    rows_by_block, depth = row_blocks.shape[1:]
    rank = sources[0][0].shape[1]
    scalars = jnp.concatenate([first.astype(jnp.int32)[None], blocks] + [s[1] for s in sources])
    specs = [pl.BlockSpec((1, rows_by_block, depth), lambda i, s: (s[1 + i], 0, 0))]
    for number in range(len(sources)):
        specs.append(panel_spec((1, rank, depth), 0, 1 + count * (number + 1)))
    return pl.pallas_call(
        shrink_kernel,
        grid_spec=pltpu.PrefetchScalarGridSpec(
            num_scalar_prefetch=1,
            grid=(count,),
            in_specs=specs,
            out_specs=pl.BlockSpec((1, rank, rows_by_block), lambda i, s: (i, 0, 0)),
        ),
        out_shape=jax.ShapeDtypeStruct((count, rank, rows_by_block), jnp.float32),
        compiler_params=pltpu.CompilerParams(vmem_limit_bytes=VMEM_BYTES),
        cost_estimate=pl.CostEstimate(
            flops=2 * rank * depth * rows_by_block * count,
            bytes_accessed=2 * depth * (rank + rows_by_block) * count,
            transcendentals=0,
        ),
    )(scalars, row_blocks, *[s[0] for s in sources])


def combine_kernel(count, part_count, up_count, scalars, *refs):
    parts = refs[:part_count]
    mine_ref, far_ref = refs[part_count : part_count + 2]
    ups = refs[part_count + 2 : part_count + 2 + up_count]
    out_ref = refs[-1]
    total = parts[0][0]
    for part in parts[1:]:
        total = total + part[0]
    up = ups[0][0] if up_count == 1 else jnp.where(scalars[0] != 0, ups[0][0], ups[1][0])
    delta = lax.dot_general(
        total.astype(jnp.bfloat16), up, (((0,), (0,)), ((), ())), preferred_element_type=jnp.float32
    )
    live = scalars[1 + count + pl.program_id(0)]
    row = lax.broadcasted_iota(jnp.int32, delta.shape, 0)
    value = mine_ref[...] + far_ref[...] + ADAPTER_SCALE * delta
    out_ref[...] = jnp.where(row < live, value, 0.0).astype(out_ref.dtype)


def combine(blocks, live, parts, base_mine, base_far, sources, first, out):
    count = blocks.shape[0]
    rank, rows_by_block = parts[0].shape[1:]
    rows, width = base_mine.shape
    scalars = jnp.concatenate(
        [first.astype(jnp.int32)[None], blocks, live[blocks]] + [s[1] for s in sources]
    )
    specs = [pl.BlockSpec((1, rank, rows_by_block), lambda i, s: (i, 0, 0)) for _ in parts]
    specs += [pl.BlockSpec((rows_by_block, width), lambda i, s: (s[1 + i], 0))] * 2
    for number, source in enumerate(sources):
        specs.append(panel_spec((1, rank, width), source[2], 1 + count * (number + 2)))
    operands = [*parts, base_mine, base_far, *[s[0] for s in sources]]
    aliases = {}
    if out is not None:
        specs.append(pl.BlockSpec(memory_space=pl.ANY))
        operands.append(out)
        aliases = {len(operands): 0}
    return pl.pallas_call(
        functools.partial(combine_kernel, count, len(parts), len(sources)),
        grid_spec=pltpu.PrefetchScalarGridSpec(
            num_scalar_prefetch=1,
            grid=(count,),
            in_specs=specs,
            out_specs=pl.BlockSpec((rows_by_block, width), lambda i, s: (s[1 + i], 0)),
        ),
        out_shape=jax.ShapeDtypeStruct((rows, width), jnp.bfloat16),
        input_output_aliases=aliases,
        compiler_params=pltpu.CompilerParams(vmem_limit_bytes=VMEM_BYTES),
    )(scalars, *operands)


def base_sum(tokens, weight, width):
    tensor_size = lax.axis_size("tensor")
    place = lax.axis_index("tensor")
    distance = 1
    chunks = jnp.arange(tensor_size, dtype=jnp.int32)
    order = [k ^ (tensor_size - 1) for k in range(tensor_size)]
    order = sorted(order, key=lambda k: (1 - (k & 1), k), reverse=False)
    chunks = place ^ jnp.asarray(order, jnp.int32)
    half = tensor_size // 2
    sent = base_chunks(tokens, weight, chunks[:half], width)
    kept = base_chunks(tokens, weight, chunks[half:], width)
    kept_order = order[half:]
    sent_order = order[:half]
    arrived = swap(sent, "tensor", distance)
    rows_of = {k ^ 1: i for i, k in enumerate(sent_order)}
    held = {k: (kept[i], arrived[rows_of[k]]) for i, k in enumerate(kept_order)}
    held = {k: (a, b) for k, (a, b) in held.items()}
    distance = 2
    while distance < tensor_size:
        out = {k: a + b for k, (a, b) in held.items() if k & distance}
        held = {
            k: (a + b, swap(out[k | distance], "tensor", distance))
            for k, (a, b) in held.items()
            if not k & distance
        }
        distance *= 2
    return held[0]


def reduce_parts(part):
    return [part] + [swap(part, "tensor", m) for m in range(1, lax.axis_size("tensor"))]


def picks(slot_ids, holder, holder_slots, count):
    hit = slot_ids // holder_slots == holder
    rank = jnp.cumsum(hit.astype(jnp.int32)) - 1
    chosen = hit[None, :] & (rank[None, :] == jnp.arange(count, dtype=jnp.int32)[:, None])
    number = jnp.arange(slot_ids.shape[0], dtype=jnp.int32)
    blocks = jnp.sum(jnp.where(chosen, number[None, :], 0), axis=1)
    slots = jnp.sum(jnp.where(chosen, (slot_ids % holder_slots)[None, :], 0), axis=1)
    return blocks, slots


def on_line_of_four(row_blocks, down, up, names, table, live, base, capacity):
    here = lax.axis_index("pool")
    inner = (here == 1) | (here == 2)
    holder_slots, _, depth = down.shape
    up_column = depth // up.shape[2]

    def across(value, pairs):
        return lax.ppermute(value, "pool", pairs)

    inner_down = across(down, [(1, 2), (2, 1)])
    inner_up = across(up, [(1, 2), (2, 1)])
    asked = [names] + [swap(names, "pool", m) for m in range(1, 4)]
    asked = [table[a[0]] for a in asked]

    def wanted(distance, holder):
        return picks(asked[distance], holder, holder_slots, capacity)[1]

    near = across(
        pack_panels(wanted(1, here), down, up), [(0, 1), (1, 0), (2, 3), (3, 2)]
    )
    to_inner = across(pack_panels(wanted(2, here), down, up, near), [(0, 2), (3, 1)])
    to_outer = across(pack_panels(wanted(3, here), down, up, near), [(0, 3), (3, 0)])
    forwarded = across(
        pack_panels(wanted(1, here ^ 3), inner_down, inner_up), [(1, 0), (2, 3)]
    )

    ranks = jnp.arange(capacity, dtype=jnp.int32)
    base_mine, base_far = base
    always = jnp.bool_(True)
    own_blocks, own_slots = picks(asked[0], here, holder_slots, capacity)
    near_blocks, _ = picks(asked[0], here ^ 1, holder_slots, capacity)
    early_blocks, early_slots = picks(
        asked[0], here ^ jnp.where(inner, 3, 2), holder_slots, capacity
    )
    late_blocks, _ = picks(asked[0], here ^ jnp.where(inner, 2, 3), holder_slots, capacity)
    phases = [
        (own_blocks, [(down, own_slots)], [(up, own_slots, 0)], always),
        (near_blocks, [(near, ranks)], [(near, ranks, up_column)], always),
        (
            early_blocks,
            [(inner_down, early_slots), (forwarded, ranks)],
            [(inner_up, early_slots, 0), (forwarded, ranks, up_column)],
            inner,
        ),
        (
            late_blocks,
            [(to_inner, ranks), (to_outer, ranks)],
            [(to_inner, ranks, up_column), (to_outer, ranks, up_column)],
            inner,
        ),
    ]
    out = None
    for blocks, panels, ups, first in phases:
        parts = reduce_parts(shrink(row_blocks, blocks, panels, first))
        out = combine(blocks, live, parts, base_mine, base_far, ups, first, out)
    return out


def on_any_pool(row_blocks, down, up, names, table, live, base, capacity):
    pool_size = lax.axis_size("pool")
    here = lax.axis_index("pool")
    holder_slots, _, depth = down.shape
    asked = table[lax.all_gather(names[0], "pool")]
    arrived = []
    for distance in range(pool_size):
        asker = lax.rem(here + distance, pool_size)
        _, slots = picks(asked[asker], here, holder_slots, capacity)
        panels = pack_panels(slots, down, up)
        pairs = [(i, (i + distance) % pool_size) for i in range(pool_size)]
        arrived.append(lax.ppermute(panels, "pool", pairs) if distance else panels)
    arrived = jnp.concatenate(arrived)
    own = asked[here]
    owners = own // holder_slots
    blocks = jnp.arange(own.shape[0], dtype=jnp.int32)
    earlier = (owners[:, None] == owners[None, :]) & (blocks[:, None] > blocks[None, :])
    ranks = jnp.sum(earlier.astype(jnp.int32), axis=1)
    place = lax.rem(here - owners + pool_size, pool_size) * capacity + ranks
    always = jnp.bool_(True)
    parts = reduce_parts(shrink(row_blocks, blocks, [(arrived, place)], always))
    ups = [(arrived, place, depth // up.shape[2])]
    return combine(blocks, live, parts, *base, ups, always, None)


def on_device(
    tokens,
    value_weight,
    adapter_down_weight,
    adapter_up_weight,
    adapter_of_block,
    adapter_pool_slot,
    live_block_tokens,
):
    pool_size = lax.axis_size("pool")
    blocks = adapter_of_block.shape[1]
    capacity = -(-blocks // pool_size)
    down = jnp.transpose(adapter_down_weight, (0, 2, 1))
    row_blocks = tokens.reshape(blocks, tokens.shape[0] // blocks, tokens.shape[1])
    base = base_sum(tokens, value_weight, adapter_up_weight.shape[2])
    whole = pool_size == 4 and blocks == capacity * pool_size
    route = on_line_of_four if whole else on_any_pool
    return route(
        row_blocks,
        down,
        adapter_up_weight,
        adapter_of_block,
        adapter_pool_slot,
        live_block_tokens[0],
        base,
        capacity,
    )


def solution(mesh):
    return jax.shard_map(
        on_device,
        mesh=mesh,
        in_specs=(
            P(("groups", "pool"), "tensor"),
            P("tensor", None),
            P(("groups", "pool"), "tensor", None),
            P(("groups", "pool"), None, "tensor"),
            P(("groups", "pool"), None),
            P("groups"),
            P(("groups", "pool"), None),
        ),
        out_specs=P(("groups", "pool"), "tensor"),
        check_vma=False,
    )
```

time: 187 us -> 129 us (0.69)
  waiting for transfers between devices: 107 us -> 15 us
  Pallas kernels: 0 us -> 31.9 us
  other arithmetic: 3.47 us -> 26.3 us
  starting transfers between devices: 15 us -> 31.5 us
  matrix products: 15.9 us -> 0 us
  blocking collectives: 13.5 us -> 0 us
  between operations: 13.5 us -> 0.41 us
  local copies, waits for them, and re-layouts: 17.8 us -> 23.4 us
    all_to_all x3 -> x0, waiting for transfers between devices: 107 us -> none  [the longest x1 80.7 us: on_device(): lax.all_to_all(outgoing, 'pool', split_axis=0, concat_axis=0, tiled=True)]
    pallas_call x0 -> x14, Pallas kernels: none -> 31.9 us  [the longest x2 9.14 us: base_chunks(): pl.pallas_call(base_kernel, grid_spec=pltpu.PrefetchScalarGridSpec(num_sc...]
    ppermute x0 -> x23, starting transfers between devices: none -> 31.5 us  [the longest x6 16.8 us: across(): return lax.ppermute(value, 'pool', pairs)]
    dot_general x3 -> x0, matrix products: 15.9 us -> none  [the longest x1 9.88 us: on_device(): jnp.dot(tokens, value_weight, preferred_element_type=jnp.float32)]
    unnamed x6 -> x54, local copies, waits for them, and re-layouts: 0.22 us -> 16.1 us
    all_to_all x3 -> x0, starting transfers between devices: 15 us -> none  [the longest x1 6.32 us: on_device(): lax.all_to_all(requests, 'pool', split_axis=0, concat_axis=0, tiled=True)]
    ppermute x0 -> x23, waiting for transfers between devices: none -> 15 us  [the longest x6 14.2 us: across(): return lax.ppermute(value, 'pool', pairs)]
    psum x1 -> x0, blocking collectives: 13.5 us -> none  [on_device(): shrunk = lax.psum(partial_value, 'tensor').astype(jnp.bfloat16)]
  transfers between devices with their start and end apart: 4 -> 23, of which waited for: 2 -> 2; matrix products, arithmetic and copies ran while one was open for 17% -> 26% of each run, Pallas kernels for 0% -> 23%
where the time goes in v1:
time: 129 us; the launch traced here: 128 us
  Pallas kernels  31.9 us (25%)
  starting transfers between devices  31.5 us (24%)
  other arithmetic  26.3 us (20%)
  local copies, waits for them, and re-layouts  23.4 us (18%)
  waiting for transfers between devices  15 us (12%)
    ppermute x6, starting transfers between devices, across(): return lax.ppermute(value, 'pool', pairs)  16.8 us
    unnamed x54, local copies, waits for them, and re-layouts  16.1 us
    ppermute x17, starting transfers between devices, swap(): return lax.ppermute(value, axis, pairs)  14.7 us
    ppermute x6, waiting for transfers between devices, across(): return lax.ppermute(value, 'pool', pairs)  14.2 us
    pallas_call x2, Pallas kernels, base_chunks(): pl.pallas_call(base_kernel, grid_spec=pltpu.PrefetchScalarGridSpec(num_sc...  9.14 us
    pallas_call x4, Pallas kernels, combine(): pl.pallas_call(functools.partial(combine_kernel, count, len(parts), len(s...  8.84 us
    pallas_call x4, Pallas kernels, shrink(): pl.pallas_call(shrink_kernel, grid_spec=pltpu.PrefetchScalarGridSpec(num_...  8.06 us
    pallas_call x4, Pallas kernels, pack_panels(): pl.pallas_call(pack_kernel, grid_spec=pltpu.PrefetchScalarGridSpec(num_sc...  5.83 us
  transfers between devices with their start and end apart: 23, of which 2 were waited for; matrix products, arithmetic and copies ran while one was open for 26% of the time, Pallas kernels for 23%

profile of v1, /device:TPU:0, one launch (start us, length us, event | category | flops | bytes accessed | tf_op | source)
XLA Modules:
  0.0 128.4 jit_solution(15658115125281907740)
XLA Ops:
  0.0 3.0 %collective-permute-start.1 = (s32[1,8]{1,0:T(1,128)}, s32[1,8]{1,0:T(1,128)S(1)}, u32[]{:S(2)}, u32[]{:S(2)}) collective-permute-start(s32[1,8]{1,0:T(1,128)} %param.12), channel_id=1, source_target_pairs={{0,4},{4,0},{8,12},{12,8},{1,5},{5,1},{9,13},{13,9},{2,6},{6,2},{1... | collective-permute-start | bytes 104 | tf_op jit(solution)/shard_map/ppermute | solution.py:17
  3.0 2.5 %collective-permute-start.4 = (s32[1,8]{1,0:T(1,128)}, s32[1,8]{1,0:T(1,128)S(1)}, u32[]{:S(2)}, u32[]{:S(2)}) collective-permute-start(s32[1,8]{1,0:T(1,128)} %param.12), channel_id=1, source_target_pairs={{0,12},{4,8},{8,4},{12,0},{1,13},{5,9},{9,5},{13,1},{2,14},{6,10},... | collective-permute-start | bytes 104 | tf_op jit(solution)/shard_map/ppermute | solution.py:17
  5.6 1.6 %collective-permute-start.11 = (bf16[4,64,2048]{2,1,0:T(8,128)(2,1)}, bf16[4,64,2048]{2,1,0:T(8,128)(2,1)}, u32[]{:S(2)}, u32[]{:S(2)}) collective-permute-start(bf16[4,64,2048]{2,1,0:T(8,128)(2,1)} %bitcast.108), channel_id=1, source_target_pairs={{4,8},{8,4},{5,9},{9,5},{6,10},{10,6},{7,11},{11,7},{20,24},{24,20... | collective-permute-start | bytes 3145736 | tf_op jit(solution)/shard_map/ppermute | solution.py:229
  7.2 0.7 fusion.14
  7.9 0.6 gather_fusion
  10.8 2.2 %copy-done.1 = bf16[1024,2048]{1,0:T(8,128)(2,1)S(1)} copy-done((bf16[1024,2048]{1,0:T(8,128)(2,1)S(1)}, bf16[1024,2048]{1,0:T(8,128)(2,1)}, u32[]{:S(2)}) %copy-start.1) | copy-done | bytes 4194328
  12.9 1.2 copy-done.8
  14.2 1.2 shard_map.91.refs_0_
  16.1 2.2 %copy-done.2 = bf16[1024,2048]{1,0:T(8,128)(2,1)S(1)} copy-done((bf16[1024,2048]{1,0:T(8,128)(2,1)S(1)}, bf16[1024,2048]{1,0:T(8,128)(2,1)}, u32[]{:S(2)}) %copy-start.2) | copy-done | bytes 4194328
  18.3 2.2 %copy-done.6 = bf16[2048,1024]{1,0:T(8,128)(2,1)S(1)} copy-done((bf16[2048,1024]{1,0:T(8,128)(2,1)S(1)}, bf16[2048,1024]{1,0:T(8,128)(2,1)}, u32[]{:S(2)}) %copy-start.6) | copy-done | bytes 4194328
  20.5 4.6 %shard_map.87 = f32[2,1024,256]{2,1,0:T(8,128)S(1)} custom-call(s32[2]{0:T(128)S(1)} %get-tuple-element.30.chunks, bf16[1024,2048]{1,0:T(8,128)(2,1)S(1)} %copy-done.2, bf16[2048,1024]{1,0:T(8,128)(2,1)S(1)} %copy-done.6), custom_call_target="tpu_custom_call" | custom-call | flops 2147483648 | bytes 8388608 | tf_op jit(solution)/shard_map/pallas_call | solution.py:35
  25.1 4.6 %shard_map.86 = f32[2,1024,256]{2,1,0:T(8,128)S(1)} custom-call(s32[2]{0:T(128)S(1)} %get-tuple-element.29.chunks, bf16[1024,2048]{1,0:T(8,128)(2,1)S(1)} %copy-done.2, bf16[2048,1024]{1,0:T(8,128)(2,1)S(1)} %copy-done.7), custom_call_target="tpu_custom_call" | custom-call | flops 2147483648 | bytes 8388608 | tf_op jit(solution)/shard_map/pallas_call | solution.py:35
  29.7 1.3 %copy-done.10 = f32[2,1024,256]{2,1,0:T(8,128)} copy-done((f32[2,1024,256]{2,1,0:T(8,128)}, f32[2,1024,256]{2,1,0:T(8,128)S(1)}, u32[]{:S(2)}) %copy-start.10) | copy-done | bytes 2097176
  33.2 1.2 gather_fusion.3
  34.4 0.7 collective-permute-start.12
  35.1 1.2 gather_fusion.4
  36.2 1.2 and_select_fusion.7
  37.4 1.3 compare_convert_fusion.5
  38.7 1.3 %reduce-window.69 = s32[8,1]{0,1:T(1,128)} reduce-window(s32[8,1]{0,1:T(1,128)} %get-tuple-element.32, s32[]{:T(128)} %constant.111.clone.1), window={size=8x1 pad=7_0x0_0}, to_apply=%region_11.12 | reduce-window | flops 56 | bytes 68 | tf_op jit(solution)/shard_map/reduce-window.29
  40.0 1.2 add_bitcast_fusion.2
  41.2 0.7 reduce-window.66
  42.5 0.7 broadcast_compare_fusion.4
  43.2 0.8 fusion.6
  44.6 0.8 copy-done.12
  45.4 1.4 %reduce-window.67 = s32[8,1]{0,1:T(1,128)} reduce-window(s32[8,1]{0,1:T(1,128)} %get-tuple-element.33, s32[]{:T(128)} %constant.111.clone.1), window={size=8x1 pad=7_0x0_0}, to_apply=%region_6.7 | reduce-window | flops 56 | bytes 68 | tf_op jit(solution)/shard_map/reduce-window.27
  46.8 5.4 %collective-permute-start.2 = (bf16[2,64,2304]{2,1,0:T(8,128)(2,1)}, bf16[2,64,2304]{2,1,0:T(8,128)(2,1)}, u32[]{:S(2)}, u32[]{:S(2)}) collective-permute-start(bf16[2,64,2304]{2,1,0:T(8,128)(2,1)} %copy-done.12), channel_id=1, source_target_pairs={{0,4},{4,0},{8,12},{12,8},{1,5},{5,1},{9,13},{13,9},{2,6},{6,2},{1... | collective-permute-start | bytes 1769480 | tf_op jit(solution)/shard_map/ppermute | solution.py:229
  52.2 0.7 fusion.16
  53.5 1.3 %gather_fusion.2 = s32[8]{0:T(128)} fusion(s32[16]{0:T(128)S(1)} %copy-done, s32[1024]{0:T(1024)} %pad_clamp_fusion.5), kind=kCustom, calls=%fused_computation.2 | custom fusion | bytes 96 | tf_op jit(solution)/shard_map/gather | solution.py:234
  54.8 1.3 compare_convert_fusion.6
  56.1 1.4 %reduce-window.65 = s32[8,1]{0,1:T(1,128)} reduce-window(s32[8,1]{0,1:T(1,128)} %compare_convert_fusion.6, s32[]{:T(128)} %constant.111.clone.1), window={size=8x1 pad=7_0x0_0}, to_apply=%region_2.3 | reduce-window | flops 56 | bytes 68 | tf_op jit(solution)/shard_map/reduce-window.25
  58.2 0.7 and_select_fusion.11
  58.8 0.7 add_bitcast_fusion.4
  59.5 0.7 fusion.22
  60.2 3.5 %fusion = (f32[1024,256]{1,0:T(8,128)}, f32[1024,256]{1,0:T(8,128)S(1)}) fusion(f32[2,1024,256]{2,1,0:T(8,128)} %collective-permute-done.9, f32[2,1024,256]{2,1,0:T(8,128)} %copy-done.10), kind=kLoop, calls=%fused_computation.9 | loop fusion | flops 524288 | bytes 6291456 | tf_op jit(solution)/shard_map/add | solution.py:198
  63.7 1.5 %collective-permute-start.10 = (f32[1024,256]{1,0:T(8,128)}, f32[1024,256]{1,0:T(8,128)S(1)}, u32[]{:S(2)}, u32[]{:S(2)}) collective-permute-start(f32[1024,256]{1,0:T(8,128)} %get-tuple-element.17), channel_id=1, source_target_pairs={{0,2},{1,3},{2,0},{3,1},{4,6},{5,7},{6,4},{7,5},{8,10},{9,11},{10,... | collective-permute-start | bytes 3145736 | tf_op jit(solution)/shard_map/ppermute | solution.py:17
  65.3 2.4 %shard_map.88 = bf16[2,64,2304]{2,1,0:T(8,128)(2,1)} custom-call(s32[2]{0:T(128)S(1)} %get-tuple-element.11.slots, bf16[4,64,2048]{2,1,0:T(8,128)(2,1)} %collective-permute-done.11.down_ref.refs_0_, bf16[4,64,256]{2,1,0:T(8,128)(2,1)S(1)} %collective-permute-done.12.up_ref.refs_6_), custom_call_target="tpu_custom_call" | custom-call | tf_op jit(solution)/shard_map/pallas_call | solution.py:69
  67.6 1.3 collective-permute-start.13
  69.1 1.4 %shard_map.84 = bf16[2,64,2304]{2,1,0:T(8,128)(2,1)} custom-call(s32[2]{0:T(128)S(1)} %fusion.5.slots, bf16[4,64,2048]{2,1,0:T(8,128)(2,1)S(1)} %bitcast.111, bf16[4,64,256]{2,1,0:T(8,128)(2,1)S(1)} %copy-done.11, bf16[2,64,2304]{2,1,0:T(8,128)(2,1)} %collective-permute-done.2.rest_0_.refs_0_.refs_6_), custom_call_target="tpu_custom_call" | custom-call | tf_op jit(solution)/shard_map/pallas_call | solution.py:69
  70.5 4.4 %collective-permute-start.5 = (bf16[2,64,2304]{2,1,0:T(8,128)(2,1)}, bf16[2,64,2304]{2,1,0:T(8,128)(2,1)}, u32[]{:S(2)}, u32[]{:S(2)}) collective-permute-start(bf16[2,64,2304]{2,1,0:T(8,128)(2,1)} %shard_map.84), channel_id=1, source_target_pairs={{0,12},{12,0},{1,13},{13,1},{2,14},{14,2},{3,15},{15,3},{16,28},{2... | collective-permute-start | bytes 1769480 | tf_op jit(solution)/shard_map/ppermute | solution.py:229
  74.9 1.4 %shard_map.83 = bf16[2,64,2304]{2,1,0:T(8,128)(2,1)} custom-call(s32[2]{0:T(128)S(1)} %fusion.3.slots, bf16[4,64,2048]{2,1,0:T(8,128)(2,1)S(1)} %bitcast.112, bf16[4,64,256]{2,1,0:T(8,128)(2,1)S(1)} %copy-done.11, bf16[2,64,2304]{2,1,0:T(8,128)(2,1)} %collective-permute-done.2.rest_0_.refs_0_.refs_6_), custom_call_target="tpu_custom_call" | custom-call | tf_op jit(solution)/shard_map/pallas_call | solution.py:69
  76.3 3.5 %collective-permute-start.3 = (bf16[2,64,2304]{2,1,0:T(8,128)(2,1)}, bf16[2,64,2304]{2,1,0:T(8,128)(2,1)S(1)}, u32[]{:S(2)}, u32[]{:S(2)}) collective-permute-start(bf16[2,64,2304]{2,1,0:T(8,128)(2,1)} %shard_map.83), channel_id=1, source_target_pairs={{0,8},{12,4},{1,9},{13,5},{2,10},{14,6},{3,11},{15,7},{16,24},{28,... | collective-permute-start | bytes 1769480 | tf_op jit(solution)/shard_map/ppermute | solution.py:229
  79.8 0.8 gather_fusion.6
  80.6 0.8 fusion.2
  81.4 0.7 fusion.11
  82.7 14.2 %collective-permute-done.13.refs_1_.refs_7_ = bf16[2,64,2304]{2,1,0:T(8,128)(2,1)} collective-permute-done((bf16[2,64,2304]{2,1,0:T(8,128)(2,1)}, bf16[2,64,2304]{2,1,0:T(8,128)(2,1)}, u32[]{:S(2)}, u32[]{:S(2)}) %collective-permute-start.13) | collective-permute-done | bytes 589856 | tf_op jit(solution)/shard_map/ppermute | solution.py:229
  96.9 0.7 fusion.8.scalars
  97.6 0.6 gather_fusion.7
  98.2 0.6 gather_fusion.5
  98.9 2.2 %copy-done.3 = bf16[1024,2048]{1,0:T(8,128)(2,1)S(1)} copy-done((bf16[1024,2048]{1,0:T(8,128)(2,1)S(1)}, bf16[1024,2048]{1,0:T(8,128)(2,1)}, u32[]{:S(2)}) %copy-start.3) | copy-done | bytes 4194328
  101.1 2.4 %shard_map.90.refs_0_ = f32[2,64,128]{2,1,0:T(8,128)S(1)} custom-call(s32[5]{0:T(128)S(1)} %fusion.8.scalars, bf16[8,128,2048]{2,1,0:T(8,128)(2,1)S(1)} %bitcast.105, bf16[2,64,2304]{2,1,0:T(8,128)(2,1)} %collective-permute-done.2.rest_0_.refs_0_.refs_6_), custom_call_target="tpu_custom_call" | custom-call | flops 67108864 | bytes 1572864 | tf_op jit(solution)/shard_map/pallas_call | solution.py:112
  103.5 2.3 %shard_map.89.refs_0_ = f32[2,64,128]{2,1,0:T(8,128)S(1)} custom-call(s32[7]{0:T(128)S(1)} %get-tuple-element.21.scalars, bf16[8,128,2048]{2,1,0:T(8,128)(2,1)S(1)} %bitcast.106, bf16[4,64,2048]{2,1,0:T(8,128)(2,1)} %collective-permute-done.11.down_ref.refs_0_, bf16[2,64,2304]{2,1,0:T(8,128)(2,1)} %collective-permute-done.13.refs_1_.refs_7_), custom_call_target="tpu_custom_call" | custom-call | flops 67108864 | bytes 1572864 | tf_op jit(solution)/shard_map/pallas_call | solution.py:112
  106.4 0.6 collective-permute-start.17
  107.7 1.5 %collective-permute-start.18 = (f32[2,64,128]{2,1,0:T(8,128)S(1)}, f32[2,64,128]{2,1,0:T(8,128)S(1)}, u32[]{:S(2)}, u32[]{:S(2)}) collective-permute-start(f32[2,64,128]{2,1,0:T(8,128)S(1)} %shard_map.90.refs_0_), channel_id=1, source_target_pairs={{0,2},{1,3},{2,0},{3,1},{4,6},{5,7},{6,4},{7,5},{8,10},{9,11},{10,... | collective-permute-start | bytes 196616 | tf_op jit(solution)/shard_map/ppermute | solution.py:17
  109.2 0.6 collective-permute-start.14
  109.9 0.6 gather_fusion.1
  110.7 2.2 %copy-done.5 = bf16[1024,2048]{1,0:T(8,128)(2,1)S(1)} copy-done((bf16[1024,2048]{1,0:T(8,128)(2,1)S(1)}, bf16[1024,2048]{1,0:T(8,128)(2,1)}, u32[]{:S(2)}) %copy-start.5) | copy-done | bytes 4194328
  112.9 2.2 %shard_map.85.refs_0_ = f32[2,64,128]{2,1,0:T(8,128)S(1)} custom-call(s32[7]{0:T(128)S(1)} %get-tuple-element.20.scalars, bf16[8,128,2048]{2,1,0:T(8,128)(2,1)S(1)} %bitcast.107, bf16[2,64,2304]{2,1,0:T(8,128)(2,1)S(1)} %collective-permute-done.3.refs_0_.refs_6_, bf16[2,64,2304]{2,1,0:T(8,128)(2,1)} %collective-permute-done.5.refs_1_.refs_7_), custom_call_target="tpu_custom_call" | custom-call | flops 67108864 | bytes 1572864 | tf_op jit(solution)/shard_map/pallas_call | solution.py:112
  115.2 1.6 %collective-permute-start.7 = (f32[2,64,128]{2,1,0:T(8,128)S(1)}, f32[2,64,128]{2,1,0:T(8,128)S(1)}, u32[]{:S(2)}, u32[]{:S(2)}) collective-permute-start(f32[2,64,128]{2,1,0:T(8,128)S(1)} %shard_map.85.refs_0_), channel_id=1, source_target_pairs={{0,2},{1,3},{2,0},{3,1},{4,6},{5,7},{6,4},{7,5},{8,10},{9,11},{10,... | collective-permute-start | bytes 196616 | tf_op jit(solution)/shard_map/ppermute | solution.py:17
  117.0 1.5 %collective-permute-start.15 = (f32[2,64,128]{2,1,0:T(8,128)S(1)}, f32[2,64,128]{2,1,0:T(8,128)S(1)}, u32[]{:S(2)}, u32[]{:S(2)}) collective-permute-start(f32[2,64,128]{2,1,0:T(8,128)S(1)} %shard_map.89.refs_0_), channel_id=1, source_target_pairs={{0,2},{1,3},{2,0},{3,1},{4,6},{5,7},{6,4},{7,5},{8,10},{9,11},{10,... | collective-permute-start | bytes 196616 | tf_op jit(solution)/shard_map/ppermute | solution.py:17
  118.8 1.6 %shard_map.92.refs_7_ = bf16[1024,256]{1,0:T(8,128)(2,1)} custom-call(s32[7]{0:T(128)S(1)} %fusion.13.scalars, f32[2,64,128]{2,1,0:T(8,128)S(1)} %shard_map.91.refs_0_, f32[2,64,128]{2,1,0:T(8,128)S(1)} %collective-permute-done.20.refs_1_, f32[2,64,128]{2,1,0:T(8,128)S(1)} %copy-done.14, f32[2,64,128]{2,1,0:T(8,128)S(1)} %copy-done.16, ...), custom_call_target="tpu_custom_call" | custom-call | tf_op jit(solution)/shard_map/pallas_call | solution.py:165
  120.5 2.4 %shard_map.93.refs_8_ = bf16[1024,256]{1,0:T(8,128)(2,1)} custom-call(s32[7]{0:T(128)S(1)} %get-tuple-element.19.scalars, f32[2,64,128]{2,1,0:T(8,128)S(1)} %shard_map.90.refs_0_, f32[2,64,128]{2,1,0:T(8,128)S(1)} %collective-permute-done.17.refs_1_, f32[2,64,128]{2,1,0:T(8,128)S(1)} %collective-permute-done.18.refs_2_, ...), custom_call_target="tpu_custom_call", output_to_operand_aliasing={{}: (8, {})} | custom-call | tf_op jit(solution)/shard_map/pallas_call | solution.py:165
  122.9 0.7 collective-permute-done.16.refs_3_
  123.6 2.4 %shard_map.94.refs_8_ = bf16[1024,256]{1,0:T(8,128)(2,1)} custom-call(s32[9]{0:T(128)S(1)} %concatenate.26.scalars, f32[2,64,128]{2,1,0:T(8,128)S(1)} %shard_map.89.refs_0_, f32[2,64,128]{2,1,0:T(8,128)S(1)} %collective-permute-done.14.refs_1_, f32[2,64,128]{2,1,0:T(8,128)S(1)} %collective-permute-done.15.refs_2_, ...), custom_call_target="tpu_custom_call", output_to_operand_aliasing={{}: (9, {})} | custom-call | tf_op jit(solution)/shard_map/pallas_call | solution.py:165
  126.0 2.4 %shard_map.95 = bf16[1024,256]{1,0:T(8,128)(2,1)} custom-call(s32[9]{0:T(128)S(1)} %concatenate.24.scalars, f32[2,64,128]{2,1,0:T(8,128)S(1)} %shard_map.85.refs_0_, f32[2,64,128]{2,1,0:T(8,128)S(1)} %collective-permute-done.6.refs_1_, f32[2,64,128]{2,1,0:T(8,128)S(1)} %collective-permute-done.7.refs_2_, ...), custom_call_target="tpu_custom_call", output_to_operand_aliasing={{}: (9, {})} | custom-call | tf_op jit(solution)/shard_map/pallas_call | solution.py:165
  (120 shorter events, 10.7 us)
Async XLA Ops:
  0.0 7.9 %copy-start = (s32[16]{0:T(128)S(1)}, s32[16]{0:T(128)}, u32[]{:S(2)}) copy-start(s32[16]{0:T(128)} %param.13) | copy-start | bytes 196
  0.0 32.6 %collective-permute-start.1 = (s32[1,8]{1,0:T(1,128)}, s32[1,8]{1,0:T(1,128)S(1)}, u32[]{:S(2)}, u32[]{:S(2)}) collective-permute-start(s32[1,8]{1,0:T(1,128)} %param.12), channel_id=1, source_target_pairs={{0,4},{4,0},{8,12},{12,8},{1,5},{5,1},{9,13},{13,9},{2,6},{6,2},{1... | collective-permute-start | bytes 104 | tf_op jit(solution)/shard_map/ppermute | solution.py:17
  3.0 31.3 %collective-permute-start.4 = (s32[1,8]{1,0:T(1,128)}, s32[1,8]{1,0:T(1,128)S(1)}, u32[]{:S(2)}, u32[]{:S(2)}) collective-permute-start(s32[1,8]{1,0:T(1,128)} %param.12), channel_id=1, source_target_pairs={{0,12},{4,8},{8,4},{12,0},{1,13},{5,9},{9,5},{13,1},{2,14},{6,10},... | collective-permute-start | bytes 104 | tf_op jit(solution)/shard_map/ppermute | solution.py:17
  5.5 41.3 %collective-permute-start = (s32[1,8]{1,0:T(1,128)}, s32[1,8]{1,0:T(1,128)}, u32[]{:S(2)}, u32[]{:S(2)}) collective-permute-start(s32[1,8]{1,0:T(1,128)} %param.12), channel_id=1, source_target_pairs={{0,8},{4,12},{8,0},{12,4},{1,9},{5,13},{9,1},{13,5},{2,10},{6,14},... | collective-permute-start | bytes 104 | tf_op jit(solution)/shard_map/ppermute | solution.py:17
  5.6 59.7 %collective-permute-start.11 = (bf16[4,64,2048]{2,1,0:T(8,128)(2,1)}, bf16[4,64,2048]{2,1,0:T(8,128)(2,1)}, u32[]{:S(2)}, u32[]{:S(2)}) collective-permute-start(bf16[4,64,2048]{2,1,0:T(8,128)(2,1)} %bitcast.108), channel_id=1, source_target_pairs={{4,8},{8,4},{5,9},{9,5},{6,10},{10,6},{7,11},{11,7},{20,24},{24,20... | collective-permute-start | bytes 3145736 | tf_op jit(solution)/shard_map/ppermute | solution.py:229
  10.2 0.6 copy-start.20
  10.2 5.2 %copy-start.18 = (s32[2]{0:T(128)}, s32[2]{0:T(128)S(1)}, u32[]{:S(2)}) copy-start(s32[2]{0:T(128)S(1)} %get-tuple-element.5) | copy-start | bytes 28
  10.8 2.2 %copy-start.1 = (bf16[1024,2048]{1,0:T(8,128)(2,1)S(1)}, bf16[1024,2048]{1,0:T(8,128)(2,1)}, u32[]{:S(2)}) copy-start(bf16[1024,2048]{1,0:T(8,128)(2,1)} %tokens_ref.3) | copy-start | bytes 12582916
  12.9 1.2 copy-start.8
  14.2 1.9 %copy-start.25 = (s32[4]{0:T(128)S(1)}, s32[4]{0:T(128)}, u32[]{:S(2)}) copy-start(s32[4]{0:T(128)} %constant.118.clone) | copy-start | bytes 52
  15.4 66.7 %collective-permute-start.20 = (f32[2,64,128]{2,1,0:T(8,128)S(1)}, f32[2,64,128]{2,1,0:T(8,128)S(1)}, u32[]{:S(2)}, u32[]{:S(2)}) collective-permute-start(f32[2,64,128]{2,1,0:T(8,128)S(1)} %shard_map.91.refs_0_), channel_id=1, source_target_pairs={{0,1},{1,0},{2,3},{3,2},{4,5},{5,4},{6,7},{7,6},{8,9},{9,8},{10,11... | collective-permute-start | bytes 196616 | tf_op jit(solution)/shard_map/ppermute | solution.py:17
  16.1 2.2 %copy-start.2 = (bf16[1024,2048]{1,0:T(8,128)(2,1)S(1)}, bf16[1024,2048]{1,0:T(8,128)(2,1)}, u32[]{:S(2)}) copy-start(bf16[1024,2048]{1,0:T(8,128)(2,1)} %tokens_ref.3) | copy-start | bytes 12582916
  18.3 2.2 %copy-start.6 = (bf16[2048,1024]{1,0:T(8,128)(2,1)S(1)}, bf16[2048,1024]{1,0:T(8,128)(2,1)}, u32[]{:S(2)}) copy-start(bf16[2048,1024]{1,0:T(8,128)(2,1)} %weight_ref.3) | copy-start | bytes 12582916
  20.5 4.6 %copy-start.7 = (bf16[2048,1024]{1,0:T(8,128)(2,1)S(1)}, bf16[2048,1024]{1,0:T(8,128)(2,1)}, u32[]{:S(2)}) copy-start(bf16[2048,1024]{1,0:T(8,128)(2,1)} %weight_ref.3) | copy-start | bytes 12582916
  25.1 9.3 %copy-start.11 = (bf16[4,64,256]{2,1,0:T(8,128)(2,1)S(1)}, bf16[4,64,256]{2,1,0:T(8,128)(2,1)}, u32[]{:S(2)}) copy-start(bf16[4,64,256]{2,1,0:T(8,128)(2,1)} %refs_6_.1) | copy-start | bytes 393220
  25.1 18.9 %copy-start.9 = (bf16[4,2048,64]{1,2,0:T(8,128)(2,1)S(1)}, bf16[4,2048,64]{1,2,0:T(8,128)(2,1)}, u32[]{:S(2)}) copy-start(bf16[4,2048,64]{1,2,0:T(8,128)(2,1)} %param.10) | copy-start | bytes 3145732
  29.7 1.3 %copy-start.10 = (f32[2,1024,256]{2,1,0:T(8,128)}, f32[2,1024,256]{2,1,0:T(8,128)S(1)}, u32[]{:S(2)}) copy-start(f32[2,1024,256]{2,1,0:T(8,128)S(1)} %shard_map.86) | copy-start | bytes 6291460
  32.0 1.1 copy-start.24
  32.7 27.5 %collective-permute-start.9 = (f32[2,1024,256]{2,1,0:T(8,128)S(1)}, f32[2,1024,256]{2,1,0:T(8,128)}, u32[]{:S(2)}, u32[]{:S(2)}) collective-permute-start(f32[2,1024,256]{2,1,0:T(8,128)S(1)} %shard_map.87), channel_id=1, source_target_pairs={{0,1},{1,0},{2,3},{3,2},{4,5},{5,4},{6,7},{7,6},{8,9},{9,8},{10,11... | collective-permute-start | bytes 6291464 | tf_op jit(solution)/shard_map/ppermute | solution.py:17
  34.4 30.9 %collective-permute-start.12 = (bf16[4,64,256]{2,1,0:T(8,128)(2,1)S(1)}, bf16[4,64,256]{2,1,0:T(8,128)(2,1)S(1)}, u32[]{:S(2)}, u32[]{:S(2)}) collective-permute-start(bf16[4,64,256]{2,1,0:T(8,128)(2,1)S(1)} %copy-done.11), channel_id=1, source_target_pairs={{4,8},{8,4},{5,9},{9,5},{6,10},{10,6},{7,11},{11,7},{20,24},{24,20... | collective-permute-start | bytes 393224 | tf_op jit(solution)/shard_map/ppermute | solution.py:229
  44.6 0.8 copy-start.12
  46.8 22.2 %collective-permute-start.2 = (bf16[2,64,2304]{2,1,0:T(8,128)(2,1)}, bf16[2,64,2304]{2,1,0:T(8,128)(2,1)}, u32[]{:S(2)}, u32[]{:S(2)}) collective-permute-start(bf16[2,64,2304]{2,1,0:T(8,128)(2,1)} %copy-done.12), channel_id=1, source_target_pairs={{0,4},{4,0},{8,12},{12,8},{1,5},{5,1},{9,13},{13,9},{2,6},{6,2},{1... | collective-permute-start | bytes 1769480 | tf_op jit(solution)/shard_map/ppermute | solution.py:229
  60.2 5.0 %copy-start.26 = (s32[8,1]{0,1:T(1,128)S(1)}, s32[8,1]{0,1:T(1,128)}, u32[]{:S(2)}) copy-start(s32[8,1]{0,1:T(1,128)} %reduce-window.65) | copy-start | bytes 100
  63.7 54.9 %collective-permute-start.10 = (f32[1024,256]{1,0:T(8,128)}, f32[1024,256]{1,0:T(8,128)S(1)}, u32[]{:S(2)}, u32[]{:S(2)}) collective-permute-start(f32[1024,256]{1,0:T(8,128)} %get-tuple-element.17), channel_id=1, source_target_pairs={{0,2},{1,3},{2,0},{3,1},{4,6},{5,7},{6,4},{7,5},{8,10},{9,11},{10,... | collective-permute-start | bytes 3145736 | tf_op jit(solution)/shard_map/ppermute | solution.py:17
  67.6 29.3 %collective-permute-start.13 = (bf16[2,64,2304]{2,1,0:T(8,128)(2,1)}, bf16[2,64,2304]{2,1,0:T(8,128)(2,1)}, u32[]{:S(2)}, u32[]{:S(2)}) collective-permute-start(bf16[2,64,2304]{2,1,0:T(8,128)(2,1)} %shard_map.88), channel_id=1, source_target_pairs={{4,0},{8,12},{5,1},{9,13},{6,2},{10,14},{7,3},{11,15},{20,16},{24,... | collective-permute-start | bytes 1769480 | tf_op jit(solution)/shard_map/ppermute | solution.py:229
  69.0 10.8 %copy-start.23 = (s32[2]{0:T(128)S(1)}, s32[2]{0:T(128)}, u32[]{:S(2)}) copy-start(s32[2]{0:T(128)} %get-tuple-element.36) | copy-start | bytes 28
  69.0 10.8 %copy-start.17 = (s32[1,8]{1,0:T(1,128)S(1)}, s32[1,8]{1,0:T(1,128)}, u32[]{:S(2)}) copy-start(s32[1,8]{1,0:T(1,128)} %param.14) | copy-start | bytes 100
  70.5 38.7 %collective-permute-start.5 = (bf16[2,64,2304]{2,1,0:T(8,128)(2,1)}, bf16[2,64,2304]{2,1,0:T(8,128)(2,1)}, u32[]{:S(2)}, u32[]{:S(2)}) collective-permute-start(bf16[2,64,2304]{2,1,0:T(8,128)(2,1)} %shard_map.84), channel_id=1, source_target_pairs={{0,12},{12,0},{1,13},{13,1},{2,14},{14,2},{3,15},{15,3},{16,28},{2... | collective-permute-start | bytes 1769480 | tf_op jit(solution)/shard_map/ppermute | solution.py:229
  76.3 32.9 %collective-permute-start.3 = (bf16[2,64,2304]{2,1,0:T(8,128)(2,1)}, bf16[2,64,2304]{2,1,0:T(8,128)(2,1)S(1)}, u32[]{:S(2)}, u32[]{:S(2)}) collective-permute-start(bf16[2,64,2304]{2,1,0:T(8,128)(2,1)} %shard_map.83), channel_id=1, source_target_pairs={{0,8},{12,4},{1,9},{13,5},{2,10},{14,6},{3,11},{15,7},{16,24},{28,... | collective-permute-start | bytes 1769480 | tf_op jit(solution)/shard_map/ppermute | solution.py:229
  82.1 23.7 %collective-permute-start.21 = (f32[2,64,128]{2,1,0:T(8,128)S(1)}, f32[2,64,128]{2,1,0:T(8,128)S(1)}, u32[]{:S(2)}, u32[]{:S(2)}) collective-permute-start(f32[2,64,128]{2,1,0:T(8,128)S(1)} %shard_map.91.refs_0_), channel_id=1, source_target_pairs={{0,2},{1,3},{2,0},{3,1},{4,6},{5,7},{6,4},{7,5},{8,10},{9,11},{10,... | collective-permute-start | bytes 196616 | tf_op jit(solution)/shard_map/ppermute | solution.py:17
  96.9 10.2 %collective-permute-start.22 = (f32[2,64,128]{2,1,0:T(8,128)S(1)}, f32[2,64,128]{2,1,0:T(8,128)S(1)}, u32[]{:S(2)}, u32[]{:S(2)}) collective-permute-start(f32[2,64,128]{2,1,0:T(8,128)S(1)} %shard_map.91.refs_0_), channel_id=1, source_target_pairs={{0,3},{1,2},{2,1},{3,0},{4,7},{5,6},{6,5},{7,4},{8,11},{9,10},{10,... | collective-permute-start | bytes 196616 | tf_op jit(solution)/shard_map/ppermute | solution.py:17
  98.9 2.2 %copy-start.3 = (bf16[1024,2048]{1,0:T(8,128)(2,1)S(1)}, bf16[1024,2048]{1,0:T(8,128)(2,1)}, u32[]{:S(2)}) copy-start(bf16[1024,2048]{1,0:T(8,128)(2,1)} %tokens_ref.3) | copy-start | bytes 12582916
  101.1 2.4 %copy-start.4 = (bf16[1024,2048]{1,0:T(8,128)(2,1)S(1)}, bf16[1024,2048]{1,0:T(8,128)(2,1)}, u32[]{:S(2)}) copy-start(bf16[1024,2048]{1,0:T(8,128)(2,1)} %tokens_ref.3) | copy-start | bytes 12582916
  103.5 7.0 %copy-start.22 = (s32[2]{0:T(128)S(1)}, s32[2]{0:T(128)}, u32[]{:S(2)}) copy-start(s32[2]{0:T(128)} %get-tuple-element.10) | copy-start | bytes 28
  105.8 0.6 copy-start.13
  106.4 8.6 %collective-permute-start.17 = (f32[2,64,128]{2,1,0:T(8,128)S(1)}, f32[2,64,128]{2,1,0:T(8,128)S(1)}, u32[]{:S(2)}, u32[]{:S(2)}) collective-permute-start(f32[2,64,128]{2,1,0:T(8,128)S(1)} %shard_map.90.refs_0_), channel_id=1, source_target_pairs={{0,1},{1,0},{2,3},{3,2},{4,5},{5,4},{6,7},{7,6},{8,9},{9,8},{10,11... | collective-permute-start | bytes 196616 | tf_op jit(solution)/shard_map/ppermute | solution.py:17
  107.1 0.6 copy-start.15
  107.7 7.4 %collective-permute-start.18 = (f32[2,64,128]{2,1,0:T(8,128)S(1)}, f32[2,64,128]{2,1,0:T(8,128)S(1)}, u32[]{:S(2)}, u32[]{:S(2)}) collective-permute-start(f32[2,64,128]{2,1,0:T(8,128)S(1)} %shard_map.90.refs_0_), channel_id=1, source_target_pairs={{0,2},{1,3},{2,0},{3,1},{4,6},{5,7},{6,4},{7,5},{8,10},{9,11},{10,... | collective-permute-start | bytes 196616 | tf_op jit(solution)/shard_map/ppermute | solution.py:17
  109.2 7.5 %collective-permute-start.19 = (f32[2,64,128]{2,1,0:T(8,128)S(1)}, f32[2,64,128]{2,1,0:T(8,128)S(1)}, u32[]{:S(2)}, u32[]{:S(2)}) collective-permute-start(f32[2,64,128]{2,1,0:T(8,128)S(1)} %shard_map.90.refs_0_), channel_id=1, source_target_pairs={{0,3},{1,2},{2,1},{3,0},{4,7},{5,6},{6,5},{7,4},{8,11},{9,10},{10,... | collective-permute-start | bytes 196616 | tf_op jit(solution)/shard_map/ppermute | solution.py:17
  109.2 7.8 %collective-permute-start.14 = (f32[2,64,128]{2,1,0:T(8,128)S(1)}, f32[2,64,128]{2,1,0:T(8,128)S(1)}, u32[]{:S(2)}, u32[]{:S(2)}) collective-permute-start(f32[2,64,128]{2,1,0:T(8,128)S(1)} %shard_map.89.refs_0_), channel_id=1, source_target_pairs={{0,1},{1,0},{2,3},{3,2},{4,5},{5,4},{6,7},{7,6},{8,9},{9,8},{10,11... | collective-permute-start | bytes 196616 | tf_op jit(solution)/shard_map/ppermute | solution.py:17
  110.7 2.2 %copy-start.5 = (bf16[1024,2048]{1,0:T(8,128)(2,1)S(1)}, bf16[1024,2048]{1,0:T(8,128)(2,1)}, u32[]{:S(2)}) copy-start(bf16[1024,2048]{1,0:T(8,128)(2,1)} %tokens_ref.3) | copy-start | bytes 12582916
  112.9 5.9 %copy-start.19 = (s32[2]{0:T(128)S(1)}, s32[2]{0:T(128)}, u32[]{:S(2)}) copy-start(s32[2]{0:T(128)} %copy-done.18) | copy-start | bytes 28
  112.9 5.9 %copy-start.21 = (s32[2]{0:T(128)S(1)}, s32[2]{0:T(128)}, u32[]{:S(2)}) copy-start(s32[2]{0:T(128)} %copy-done.20) | copy-start | bytes 28
  112.9 5.9 %copy-start.14 = (f32[2,64,128]{2,1,0:T(8,128)S(1)}, f32[2,64,128]{2,1,0:T(8,128)}, u32[]{:S(2)}) copy-start(f32[2,64,128]{2,1,0:T(8,128)} %copy-done.13) | copy-start | bytes 196612
  112.9 6.0 %copy-start.16 = (f32[2,64,128]{2,1,0:T(8,128)S(1)}, f32[2,64,128]{2,1,0:T(8,128)}, u32[]{:S(2)}) copy-start(f32[2,64,128]{2,1,0:T(8,128)} %copy-done.15) | copy-start | bytes 196612
  115.1 10.9 %collective-permute-start.6 = (f32[2,64,128]{2,1,0:T(8,128)S(1)}, f32[2,64,128]{2,1,0:T(8,128)S(1)}, u32[]{:S(2)}, u32[]{:S(2)}) collective-permute-start(f32[2,64,128]{2,1,0:T(8,128)S(1)} %shard_map.85.refs_0_), channel_id=1, source_target_pairs={{0,1},{1,0},{2,3},{3,2},{4,5},{5,4},{6,7},{7,6},{8,9},{9,8},{10,11... | collective-permute-start | bytes 196616 | tf_op jit(solution)/shard_map/ppermute | solution.py:17
  115.2 10.8 %collective-permute-start.7 = (f32[2,64,128]{2,1,0:T(8,128)S(1)}, f32[2,64,128]{2,1,0:T(8,128)S(1)}, u32[]{:S(2)}, u32[]{:S(2)}) collective-permute-start(f32[2,64,128]{2,1,0:T(8,128)S(1)} %shard_map.85.refs_0_), channel_id=1, source_target_pairs={{0,2},{1,3},{2,0},{3,1},{4,6},{5,7},{6,4},{7,5},{8,10},{9,11},{10,... | collective-permute-start | bytes 196616 | tf_op jit(solution)/shard_map/ppermute | solution.py:17
  116.7 9.3 %collective-permute-start.8 = (f32[2,64,128]{2,1,0:T(8,128)S(1)}, f32[2,64,128]{2,1,0:T(8,128)S(1)}, u32[]{:S(2)}, u32[]{:S(2)}) collective-permute-start(f32[2,64,128]{2,1,0:T(8,128)S(1)} %shard_map.85.refs_0_), channel_id=1, source_target_pairs={{0,3},{1,2},{2,1},{3,0},{4,7},{5,6},{6,5},{7,4},{8,11},{9,10},{10,... | collective-permute-start | bytes 196616 | tf_op jit(solution)/shard_map/ppermute | solution.py:17
  117.0 5.8 %collective-permute-start.15 = (f32[2,64,128]{2,1,0:T(8,128)S(1)}, f32[2,64,128]{2,1,0:T(8,128)S(1)}, u32[]{:S(2)}, u32[]{:S(2)}) collective-permute-start(f32[2,64,128]{2,1,0:T(8,128)S(1)} %shard_map.89.refs_0_), channel_id=1, source_target_pairs={{0,2},{1,3},{2,0},{3,1},{4,6},{5,7},{6,4},{7,5},{8,10},{9,11},{10,... | collective-permute-start | bytes 196616 | tf_op jit(solution)/shard_map/ppermute | solution.py:17
  118.5 5.1 %collective-permute-start.16 = (f32[2,64,128]{2,1,0:T(8,128)S(1)}, f32[2,64,128]{2,1,0:T(8,128)S(1)}, u32[]{:S(2)}, u32[]{:S(2)}) collective-permute-start(f32[2,64,128]{2,1,0:T(8,128)S(1)} %shard_map.89.refs_0_), channel_id=1, source_target_pairs={{0,3},{1,2},{2,1},{3,0},{4,7},{5,6},{6,5},{7,4},{8,11},{9,10},{10,... | collective-permute-start | bytes 196616 | tf_op jit(solution)/shard_map/ppermute | solution.py:17

commit v2 on v0

v2 whole, which is shorter than its diff:
```python
import functools

import jax
import jax.numpy as jnp
from jax import lax
from jax.experimental import pallas as pl
from jax.experimental.pallas import tpu as pltpu
from jax.sharding import PartitionSpec as P

ADAPTER_SCALE = 0.5
ROW_TILE = 256
PARAMS = pltpu.CompilerParams(vmem_limit_bytes=16 * 1024 * 1024)
NO_COST = pl.CostEstimate(flops=0, bytes_accessed=0, transcendentals=0)
ANY = pl.BlockSpec(memory_space=pl.ANY)
SMEM = pl.BlockSpec(memory_space=pltpu.SMEM)


def swap(value, axis, distance):
    pairs = [(i, i ^ distance) for i in range(lax.axis_size(axis))]
    return lax.ppermute(value, axis, pairs)


def base_kernel(order, tokens_ref, weight_ref, *refs):
    width = refs[-1].shape[2]
    place = lax.axis_index("tensor")
    outs = refs[-2:]
    half = len(order) // 2
    for number, offset in enumerate(order):
        columns = pl.ds(pl.multiple_of((place ^ offset) * width, width), width)
        outs[number // half][number % half] = jnp.dot(
            tokens_ref[...], weight_ref[:, columns], preferred_element_type=jnp.float32
        )


def base_chunks(tokens, weight, order, width, after):
    rows, depth = tokens.shape
    tile = min(ROW_TILE, rows)
    half = len(order) // 2
    out = jax.ShapeDtypeStruct((half, rows, width), jnp.float32)
    return pl.pallas_call(
        functools.partial(base_kernel, order),
        grid=(rows // tile,),
        in_specs=[
            pl.BlockSpec((tile, depth), lambda i: (i, 0)),
            pl.BlockSpec(weight.shape, lambda i: (0, 0), pipeline_mode=pl.Buffered(1)),
        ]
        + [ANY] * len(after),
        out_specs=[pl.BlockSpec((half, tile, width), lambda i: (0, i, 0))] * 2,
        out_shape=[out, out],
        compiler_params=PARAMS,
        cost_estimate=NO_COST,
    )(tokens, weight, *after)


def add_kernel(kept_ref, arrived_ref, out_ref, mine_ref):
    half = kept_ref.shape[0] // 2
    for i in range(half):
        mine_ref[i] = kept_ref[i] + arrived_ref[i]
        out_ref[i] = kept_ref[half + i] + arrived_ref[half + i]


def add_halves(kept, arrived):
    count, rows, width = kept.shape
    tile = min(ROW_TILE, rows)
    half = count // 2
    out = jax.ShapeDtypeStruct((half, rows, width), jnp.float32)
    return pl.pallas_call(
        add_kernel,
        grid=(rows // tile,),
        in_specs=[pl.BlockSpec((count, tile, width), lambda i: (0, i, 0))] * 2,
        out_specs=[pl.BlockSpec((half, tile, width), lambda i: (0, i, 0))] * 2,
        out_shape=[out, out],
        compiler_params=PARAMS,
        cost_estimate=NO_COST,
    )(kept, arrived)


def base_sum(tokens, weight, width, after):
    size = lax.axis_size("tensor")
    kept_order = [k for k in range(size) if not k & 1]
    kept_order.sort(key=lambda k: [k >> bit & 1 for bit in range(1, size.bit_length())])
    sent, kept = base_chunks(tokens, weight, [k ^ 1 for k in kept_order] + kept_order, width, after)
    arrived = swap(sent, "tensor", 1)
    distance = 2
    while distance < size:
        sent, kept = add_halves(kept, arrived)
        arrived = swap(sent, "tensor", distance)
        distance *= 2
    return kept[0], arrived[0]


def pick(names_ref, table_ref, holder, holder_slots, count):
    blocks = [jnp.int32(0)] * count
    slots = [jnp.int32(0)] * count
    seen = jnp.int32(0)
    for j in range(names_ref.shape[1]):
        slot = table_ref[names_ref[0, j]]
        hit = lax.div(slot, jnp.int32(holder_slots)) == holder
        for k in range(count):
            chosen = hit & (seen == k)
            blocks[k] = jnp.where(chosen, jnp.int32(j), blocks[k])
            slots[k] = jnp.where(chosen, lax.rem(slot, jnp.int32(holder_slots)), slots[k])
        seen = seen + hit.astype(jnp.int32)
    return blocks, slots


def panel_copies(k, slot, down_ref, up_ref, out_ref, sems):
    depth = down_ref.shape[2]
    width = up_ref.shape[2]
    return [
        pltpu.make_async_copy(down_ref.at[slot], out_ref.at[k, :, pl.ds(0, depth)], sems.at[k, 0]),
        pltpu.make_async_copy(up_ref.at[slot], out_ref.at[k, :, pl.ds(depth, width)], sems.at[k, 1]),
    ]


def run_copies(copies):
    for copy in copies:
        copy.start()
    return copies


def plan_kernel(
    capacity,
    names_ref,
    first_ref,
    second_ref,
    third_ref,
    table_ref,
    down_ref,
    up_ref,
    near_ref,
    plan_ref,
    sems,
):
    here = lax.axis_index("pool")
    holder_slots = down_ref.shape[0]
    find = functools.partial(
        pick, table_ref=table_ref, holder_slots=holder_slots, count=capacity
    )
    copies = []
    for k, slot in enumerate(find(first_ref, holder=here)[1]):
        copies += run_copies(panel_copies(k, slot, down_ref, up_ref, near_ref, sems))
    inner = (here == 1) | (here == 2)
    own = find(names_ref, holder=here)
    near = find(names_ref, holder=here ^ 1)
    early = find(names_ref, holder=here ^ jnp.where(inner, 3, 2))
    late = find(names_ref, holder=here ^ jnp.where(inner, 2, 3))
    rows = [
        own[0],
        near[0],
        early[0],
        late[0],
        own[1],
        early[1],
        find(second_ref, holder=here)[1],
        find(third_ref, holder=here)[1],
        find(first_ref, holder=here ^ 3)[1],
        [inner.astype(jnp.int32)] * capacity,
    ]
    for number, row in enumerate(rows):
        for k in range(capacity):
            plan_ref[number * capacity + k] = row[k]
    for copy in copies:
        copy.wait()


OWN, EARLY, TO_INNER, TO_OUTER, FORWARD, INNER, PLAN_ROWS = 4, 5, 6, 7, 8, 9, 10


def make_plan(names, others, table, down, up, capacity):
    rank, depth = down.shape[1:]
    width = up.shape[2]
    return pl.pallas_call(
        functools.partial(plan_kernel, capacity),
        in_specs=[SMEM] * 5 + [ANY] * 2,
        out_specs=[ANY, SMEM],
        out_shape=[
            jax.ShapeDtypeStruct((capacity, rank, depth + width), down.dtype),
            jax.ShapeDtypeStruct((PLAN_ROWS * capacity,), jnp.int32),
        ],
        scratch_shapes=[pltpu.SemaphoreType.DMA((capacity, 2))],
        compiler_params=PARAMS,
        cost_estimate=NO_COST,
    )(names, *others, table, down, up)


def pack_kernel(starts, capacity, plan_ref, down_ref, up_ref, *rest):
    count = len(starts)
    sems = rest[-1]
    outs = rest[-1 - count : -1]
    copies = []
    for number, start in enumerate(starts):
        for k in range(capacity):
            slot = plan_ref[start + k]
            copies += run_copies(
                panel_copies(k, slot, down_ref, up_ref, outs[number], sems.at[number])
            )
    for copy in copies:
        copy.wait()


def pack_panels(plan, starts, capacity, down, up, after=()):
    rank, depth = down.shape[1:]
    width = up.shape[2]
    out = jax.ShapeDtypeStruct((capacity, rank, depth + width), down.dtype)
    return pl.pallas_call(
        functools.partial(pack_kernel, starts, capacity),
        in_specs=[SMEM] + [ANY] * (2 + len(after)),
        out_specs=[ANY] * len(starts),
        out_shape=[out] * len(starts),
        scratch_shapes=[pltpu.SemaphoreType.DMA((len(starts), capacity, 2))],
        compiler_params=PARAMS,
        cost_estimate=NO_COST,
    )(plan, down, up, *after)


def step_of(i, start, count):
    return jnp.clip(i - start, 0, count - 1)


def source_specs(phases, shape, columns):
    specs, operands, start = [], [], 0
    for (_, count, sources), places in zip(phases, columns):
        for (panels, row), column in zip(sources, places):

            def index(i, plan, *_, start=start, count=count, row=row, column=column):
                k = step_of(i, start, count)
                return (k if row is None else plan[row + k], 0, column)

            specs.append(pl.BlockSpec(shape, index))
            operands.append(panels)
        start += count
    return specs, operands


def block_index(phases):
    def index(i, plan):
        found, start = jnp.int32(0), 0
        for row, count, _ in phases:
            inside = (i >= start) & (i < start + count)
            found = jnp.where(inside, plan[row + step_of(i, start, count)], found)
            start += count
        return found

    return index


def for_phase(phases, choose, plan_ref, refs, act):
    start, at = 0, 0
    step = pl.program_id(0)
    for _, count, sources in phases:
        mine = refs[at : at + len(sources)]

        @pl.when((step >= start) & (step < start + count))
        def _(mine=mine):
            if len(mine) == 1:
                act(mine[0])
            else:
                first = plan_ref[choose] != 0
                pl.when(first)(lambda: act(mine[0]))
                pl.when(jnp.logical_not(first))(lambda: act(mine[1]))

        start += count
        at += len(sources)


def shrink_kernel(phases, choose, plan_ref, token_ref, *refs):
    out_ref = refs[-1]

    def act(panel_ref):
        out_ref[0] = lax.dot_general(
            panel_ref[0],
            token_ref[0],
            (((1,), (1,)), ((), ())),
            preferred_element_type=jnp.float32,
        )

    for_phase(phases, choose, plan_ref, refs, act)


def shrink(plan, row_blocks, phases, choose, after=()):
    rows, depth = row_blocks.shape[1:]
    rank = phases[0][2][0][0].shape[1]
    total = sum(count for _, count, _ in phases)
    columns = [[0] * len(sources) for _, _, sources in phases]
    specs, operands = source_specs(phases, (1, rank, depth), columns)
    block = block_index(phases)
    shapes = [(row, count, [None] * len(sources)) for row, count, sources in phases]
    return pl.pallas_call(
        functools.partial(shrink_kernel, shapes, choose),
        grid_spec=pltpu.PrefetchScalarGridSpec(
            num_scalar_prefetch=1,
            grid=(total,),
            in_specs=[pl.BlockSpec((1, rows, depth), lambda i, plan: (block(i, plan), 0, 0))]
            + specs
            + [ANY] * len(after),
            out_specs=pl.BlockSpec((1, rank, rows), lambda i, plan: (i, 0, 0)),
        ),
        out_shape=jax.ShapeDtypeStruct((total, rank, rows), jnp.float32),
        compiler_params=PARAMS,
        cost_estimate=NO_COST,
    )(plan, row_blocks, *operands, *after)


def exchange(part):
    return [part] + [swap(part, "tensor", m) for m in range(1, lax.axis_size("tensor"))]


def combine_kernel(phases, choose, part_count, block, plan_ref, live_ref, *refs):
    parts = refs[:part_count]
    mine_ref, far_ref = refs[part_count : part_count + 2]
    out_ref = refs[-1]
    total = parts[0][0]
    for part in parts[1:]:
        total = total + part[0]
    shrunk = total.astype(jnp.bfloat16)
    live = live_ref[block(pl.program_id(0), plan_ref)]

    def act(up_ref):
        delta = lax.dot_general(
            shrunk, up_ref[0], (((0,), (0,)), ((), ())), preferred_element_type=jnp.float32
        )
        row = lax.broadcasted_iota(jnp.int32, delta.shape, 0)
        value = mine_ref[...] + far_ref[...] + ADAPTER_SCALE * delta
        out_ref[...] = jnp.where(row < live, value, 0.0).astype(out_ref.dtype)

    for_phase(phases, choose, plan_ref, refs[part_count + 2 :], act)


def combine(plan, live, parts, base, phases, columns, choose, out=None, after=()):
    rank, block_rows = parts[0].shape[1:]
    rows, width = base[0].shape
    total = sum(count for _, count, _ in phases)
    block = block_index(phases)
    specs = [pl.BlockSpec((1, rank, block_rows), lambda i, plan, live: (i, 0, 0))] * len(parts)
    specs += [pl.BlockSpec((block_rows, width), lambda i, plan, live: (block(i, plan), 0))] * 2
    more, operands = source_specs(phases, (1, rank, width), columns)
    specs += more + [ANY] * len(after)
    operands = [*parts, *base, *operands, *after]
    aliases = {}
    if out is not None:
        specs.append(ANY)
        operands.append(out)
        aliases = {1 + len(operands): 0}
    shapes = [(row, count, [None] * len(sources)) for row, count, sources in phases]
    return pl.pallas_call(
        functools.partial(combine_kernel, shapes, choose, len(parts), block_index(shapes)),
        grid_spec=pltpu.PrefetchScalarGridSpec(
            num_scalar_prefetch=2,
            grid=(total,),
            in_specs=specs,
            out_specs=pl.BlockSpec(
                (block_rows, width), lambda i, plan, live: (block(i, plan), 0)
            ),
        ),
        out_shape=jax.ShapeDtypeStruct((rows, width), jnp.bfloat16),
        input_output_aliases=aliases,
        compiler_params=PARAMS,
        cost_estimate=NO_COST,
    )(plan, live, *operands)


def on_line_of_four(tokens, weight, row_blocks, down, up, names, table, live, capacity):
    up_column = down.shape[2] // up.shape[2]

    def across(value, pairs):
        return lax.ppermute(value, "pool", pairs)

    others = [swap(names, "pool", m) for m in range(1, 4)]
    inner_down = across(down, [(1, 2), (2, 1)])
    inner_up = across(up, [(1, 2), (2, 1)])
    near_out, plan = make_plan(names, others, table, down, up, capacity)
    near = across(near_out, [(0, 1), (1, 0), (2, 3), (3, 2)])
    base = base_sum(tokens, weight, up.shape[2], [near_out])
    inner_out, outer_out = pack_panels(
        plan, [TO_INNER * capacity, TO_OUTER * capacity], capacity, down, up, [near]
    )
    to_inner = across(inner_out, [(0, 2), (3, 1)])
    to_outer = across(outer_out, [(0, 3), (3, 0)])
    (forward_out,) = pack_panels(
        plan, [FORWARD * capacity], capacity, inner_down, inner_up, [outer_out]
    )
    forwarded = across(forward_out, [(1, 0), (2, 3)])

    choose = INNER * capacity
    first = [
        (0, capacity, [(down, OWN * capacity)]),
        (capacity, capacity, [(near, None)]),
        (2 * capacity, capacity, [(inner_down, EARLY * capacity), (forwarded, None)]),
    ]
    last = [(3 * capacity, capacity, [(to_inner, None), (to_outer, None)])]
    first_up = [
        (0, capacity, [(up, OWN * capacity)]),
        (capacity, capacity, [(near, None)]),
        (2 * capacity, capacity, [(inner_up, EARLY * capacity), (forwarded, None)]),
    ]
    first_columns = [[0], [up_column], [0, up_column]]
    first_part = shrink(plan, row_blocks, first, choose)
    first_parts = exchange(first_part)
    last_part = shrink(plan, row_blocks, last, choose, [first_part])
    last_parts = exchange(last_part)
    out = combine(
        plan, live, first_parts, base, first_up, first_columns, choose, after=[last_part]
    )
    return combine(plan, live, last_parts, base, last, [[up_column] * 2], choose, out)


def on_any_pool(tokens, weight, row_blocks, down, up, names, table, live, capacity):
    pool_size = lax.axis_size("pool")
    here = lax.axis_index("pool")
    holder_slots, _, depth = down.shape
    asked = table[lax.all_gather(names[0], "pool")]
    count = jnp.arange(capacity, dtype=jnp.int32)
    arrived = []
    for distance in range(pool_size):
        slots = asked[lax.rem(here + distance, pool_size)]
        hit = slots // holder_slots == here
        chosen = hit[None, :] & (jnp.cumsum(hit.astype(jnp.int32))[None, :] == 1 + count[:, None])
        plan = jnp.sum(jnp.where(chosen, (slots % holder_slots)[None, :], 0), axis=1)
        (panels,) = pack_panels(plan, [0], capacity, down, up)
        pairs = [(i, (i + distance) % pool_size) for i in range(pool_size)]
        arrived.append(lax.ppermute(panels, "pool", pairs) if distance else panels)
    arrived = jnp.concatenate(arrived)
    owners = asked[here] // holder_slots
    blocks = jnp.arange(owners.shape[0], dtype=jnp.int32)
    earlier = (owners[:, None] == owners[None, :]) & (blocks[:, None] > blocks[None, :])
    ranks = jnp.sum(earlier.astype(jnp.int32), axis=1)
    places = lax.rem(here - owners + pool_size, pool_size) * capacity + ranks
    plan = jnp.concatenate([blocks, places])
    base = base_sum(tokens, weight, up.shape[2], [])
    phases = [(0, blocks.shape[0], [(arrived, blocks.shape[0])])]
    parts = exchange(shrink(plan, row_blocks, phases, 0))
    return combine(plan, live, parts, base, phases, [[depth // up.shape[2]]], 0)


def on_device(
    tokens,
    value_weight,
    adapter_down_weight,
    adapter_up_weight,
    adapter_of_block,
    adapter_pool_slot,
    live_block_tokens,
):
    pool_size = lax.axis_size("pool")
    blocks = adapter_of_block.shape[1]
    capacity = -(-blocks // pool_size)
    row_blocks = tokens.reshape(blocks, tokens.shape[0] // blocks, tokens.shape[1])
    line = pool_size == 4 and blocks == capacity * pool_size
    route = on_line_of_four if line else on_any_pool
    return route(
        tokens,
        value_weight,
        row_blocks,
        jnp.transpose(adapter_down_weight, (0, 2, 1)),
        adapter_up_weight,
        adapter_of_block,
        adapter_pool_slot,
        live_block_tokens[0],
        capacity,
    )


def solution(mesh):
    return jax.shard_map(
        on_device,
        mesh=mesh,
        in_specs=(
            P(("groups", "pool"), "tensor"),
            P("tensor", None),
            P(("groups", "pool"), "tensor", None),
            P(("groups", "pool"), None, "tensor"),
            P(("groups", "pool"), None),
            P("groups"),
            P(("groups", "pool"), None),
        ),
        out_specs=P(("groups", "pool"), "tensor"),
        check_vma=False,
    )
```

time: 187 us -> 95.8 us (0.51)
  waiting for transfers between devices: 107 us -> 36.6 us
  Pallas kernels: 0 us -> 18.3 us
  starting transfers between devices: 15 us -> 32.5 us
  matrix products: 15.9 us -> 0 us
  blocking collectives: 13.5 us -> 0 us
  between operations: 13.5 us -> 0.19 us
  local copies, waits for them, and re-layouts: 17.8 us -> 7.83 us
  other arithmetic: 3.47 us -> 0 us
    all_to_all x3 -> x0, waiting for transfers between devices: 107 us -> none  [the longest x1 80.7 us: on_device(): lax.all_to_all(outgoing, 'pool', split_axis=0, concat_axis=0, tiled=True)]
    ppermute x0 -> x17, waiting for transfers between devices: none -> 36.6 us  [the longest x6 28.5 us: across(): return lax.ppermute(value, 'pool', pairs)]
    ppermute x0 -> x17, starting transfers between devices: none -> 32.5 us  [the longest x6 21.5 us: across(): return lax.ppermute(value, 'pool', pairs)]
    pallas_call x0 -> x9, Pallas kernels: none -> 18.3 us  [the longest x1 5.49 us: base_chunks(): pl.pallas_call(functools.partial(base_kernel, order), grid=(rows // tile,...]
    dot_general x3 -> x0, matrix products: 15.9 us -> none  [the longest x1 9.88 us: on_device(): jnp.dot(tokens, value_weight, preferred_element_type=jnp.float32)]
    all_to_all x3 -> x0, starting transfers between devices: 15 us -> none  [the longest x1 6.32 us: on_device(): lax.all_to_all(requests, 'pool', split_axis=0, concat_axis=0, tiled=True)]
    psum x1 -> x0, blocking collectives: 13.5 us -> none  [on_device(): shrunk = lax.psum(partial_value, 'tensor').astype(jnp.bfloat16)]
    scatter x2 -> x0, local copies, waits for them, and re-layouts: 11.6 us -> none  [the longest x1 11 us: on_device(): outgoing.at[target].set(row_blocks)]
  transfers between devices with their start and end apart: 4 -> 17, of which waited for: 2 -> 7; matrix products, arithmetic and copies ran while one was open for 17% -> 0% of each run, Pallas kernels for 0% -> 10%
where the time goes in v2:
time: 95.8 us; the launch traced here: 95.5 us
  waiting for transfers between devices  36.6 us (38%)
  starting transfers between devices  32.5 us (34%)
  Pallas kernels  18.3 us (19%)
  local copies, waits for them, and re-layouts  7.83 us (8%)
    ppermute x6, waiting for transfers between devices, across(): return lax.ppermute(value, 'pool', pairs)  28.5 us
    ppermute x6, starting transfers between devices, across(): return lax.ppermute(value, 'pool', pairs)  21.5 us
    ppermute x11, starting transfers between devices, swap(): return lax.ppermute(value, axis, pairs)  11.1 us
    ppermute x11, waiting for transfers between devices, swap(): return lax.ppermute(value, axis, pairs)  8.18 us
    unnamed x20, local copies, waits for them, and re-layouts  7.83 us
    pallas_call x1, Pallas kernels, base_chunks(): pl.pallas_call(functools.partial(base_kernel, order), grid=(rows // tile,...  5.49 us
    pallas_call x2, Pallas kernels, combine(): pl.pallas_call(functools.partial(combine_kernel, shapes, choose, len(part...  5.23 us
    pallas_call x2, Pallas kernels, shrink(): pl.pallas_call(functools.partial(shrink_kernel, shapes, choose), grid_spe...  4.05 us
  transfers between devices with their start and end apart: 17, of which 7 were waited for; matrix products, arithmetic and copies ran while one was open for 0% of the time, Pallas kernels for 10%

profile of v2, /device:TPU:0, one launch (start us, length us, event | category | flops | bytes accessed | tf_op | source)
XLA Modules:
  0.0 95.5 jit_solution(338273055532241150)
XLA Ops:
  0.0 3.0 %collective-permute-start = (s32[1,8]{1,0:T(1,128)}, s32[1,8]{1,0:T(1,128)S(1)}, u32[]{:S(2)}, u32[]{:S(2)}) collective-permute-start(s32[1,8]{1,0:T(1,128)} %names_ref.1), channel_id=1, source_target_pairs={{0,4},{4,0},{8,12},{12,8},{1,5},{5,1},{9,13},{13,9},{2,6},{6,2},{1... | collective-permute-start | bytes 104 | tf_op jit(solution)/shard_map/ppermute | solution.py:20
  3.0 2.6 %collective-permute-start.1 = (s32[1,8]{1,0:T(1,128)}, s32[1,8]{1,0:T(1,128)S(1)}, u32[]{:S(2)}, u32[]{:S(2)}) collective-permute-start(s32[1,8]{1,0:T(1,128)} %names_ref.1), channel_id=1, source_target_pairs={{0,8},{4,12},{8,0},{12,4},{1,9},{5,13},{9,1},{13,5},{2,10},{6,14},... | collective-permute-start | bytes 104 | tf_op jit(solution)/shard_map/ppermute | solution.py:20
  5.6 0.0 collective-permute-start.2
  5.6 0.0 collective-permute-done.first_ref
  5.6 2.0 %collective-permute-done.1.second_ref = s32[1,8]{1,0:T(1,128)S(1)} collective-permute-done((s32[1,8]{1,0:T(1,128)}, s32[1,8]{1,0:T(1,128)S(1)}, u32[]{:S(2)}, u32[]{:S(2)}) %collective-permute-start.1) | collective-permute-done | bytes 64 | tf_op jit(solution)/shard_map/ppermute | solution.py:20
  7.6 3.5 %collective-permute-done.2.third_ref = s32[1,8]{1,0:T(1,128)S(1)} collective-permute-done((s32[1,8]{1,0:T(1,128)}, s32[1,8]{1,0:T(1,128)S(1)}, u32[]{:S(2)}, u32[]{:S(2)}) %collective-permute-start.2) | collective-permute-done | bytes 64 | tf_op jit(solution)/shard_map/ppermute | solution.py:20
  11.1 0.0 copy-start.2
  11.1 1.2 %copy-done.2 = bf16[4,2048,64]{1,2,0:T(8,128)(2,1)S(1)} copy-done((bf16[4,2048,64]{1,2,0:T(8,128)(2,1)S(1)}, bf16[4,2048,64]{1,2,0:T(8,128)(2,1)}, u32[]{:S(2)}) %copy-start.2) | copy-done | bytes 1048600
  12.3 0.0 copy-start.5
  12.3 0.9 copy-done.5
  13.2 0.0 copy-start.8
  13.2 0.7 copy-done.8
  13.9 0.0 copy-start.9
  13.9 0.7 copy-done.9
  14.5 1.6 %shard_map.73 = (bf16[2,64,2304]{2,1,0:T(8,128)(2,1)S(1)}, s32[20]{0:T(128)S(1)}) custom-call(s32[1,8]{1,0:T(1,128)S(1)} %copy-done.8, s32[1,8]{1,0:T(1,128)S(1)} %collective-permute-done.first_ref, s32[1,8]{1,0:T(1,128)S(1)} %collective-permute-done.1.second_ref, s32[1,8]{1,0:T(1,128)S(1)} %collective-permute-done.2.third_ref, s32[16]{0:T(128)S(1)} %copy-done.9, ...), custom_call_target="tpu_custom_call" | custom-call | tf_op jit(solution)/shard_map/pallas_call | solution.py:173
  16.1 0.0 copy-start
  16.1 2.2 %copy-done = bf16[1024,2048]{1,0:T(8,128)(2,1)S(1)} copy-done((bf16[1024,2048]{1,0:T(8,128)(2,1)S(1)}, bf16[1024,2048]{1,0:T(8,128)(2,1)}, u32[]{:S(2)}) %copy-start) | copy-done | bytes 4194328
  18.3 0.0 copy-start.4
  18.3 2.2 %copy-done.4 = bf16[2048,1024]{1,0:T(8,128)(2,1)S(1)} copy-done((bf16[2048,1024]{1,0:T(8,128)(2,1)S(1)}, bf16[2048,1024]{1,0:T(8,128)(2,1)}, u32[]{:S(2)}) %copy-start.4) | copy-done | bytes 4194328
  20.5 0.0 copy-start.3
  20.5 0.0 copy-start.6
  20.5 5.5 %shard_map.78 = (f32[2,1024,256]{2,1,0:T(8,128)S(1)}, f32[2,1024,256]{2,1,0:T(8,128)S(1)}) custom-call(bf16[1024,2048]{1,0:T(8,128)(2,1)S(1)} %copy-done, bf16[2048,1024]{1,0:T(8,128)(2,1)S(1)} %copy-done.4, bf16[2,64,2304]{2,1,0:T(8,128)(2,1)S(1)} %get-tuple-element.14.refs_0_), custom_call_target="tpu_custom_call" | custom-call | tf_op jit(solution)/shard_map/pallas_call | solution.py:40
  26.0 0.1 collective-permute-start.12
  26.1 0.0 copy-done.3
  26.1 0.7 collective-permute-start.6
  26.8 0.9 collective-permute-start.3
  27.7 2.5 %collective-permute-done.12.arrived_ref = f32[2,1024,256]{2,1,0:T(8,128)S(1)} collective-permute-done((f32[2,1024,256]{2,1,0:T(8,128)S(1)}, f32[2,1024,256]{2,1,0:T(8,128)S(1)}, u32[]{:S(2)}, u32[]{:S(2)}) %collective-permute-start.12) | collective-permute-done | bytes 2097184 | tf_op jit(solution)/shard_map/ppermute | solution.py:20
  30.2 0.0 copy-start.1
  30.2 0.6 shard_map.79
  30.8 1.5 %collective-permute-start.13 = (f32[1,1024,256]{2,1,0:T(8,128)S(1)}, f32[1,1024,256]{2,1,0:T(8,128)S(1)}, u32[]{:S(2)}, u32[]{:S(2)}) collective-permute-start(f32[1,1024,256]{2,1,0:T(8,128)S(1)} %get-tuple-element.20), channel_id=1, source_target_pairs={{0,2},{1,3},{2,0},{3,1},{4,6},{5,7},{6,4},{7,5},{8,10},{9,11},{10,... | collective-permute-start | bytes 3145736 | tf_op jit(solution)/shard_map/ppermute | solution.py:20
  32.3 0.0 copy-done.6
  32.3 0.7 collective-permute-start.7
  33.0 9.6 %collective-permute-done.3.rest_0_.refs_1_.refs_7_ = bf16[2,64,2304]{2,1,0:T(8,128)(2,1)S(1)} collective-permute-done((bf16[2,64,2304]{2,1,0:T(8,128)(2,1)S(1)}, bf16[2,64,2304]{2,1,0:T(8,128)(2,1)S(1)}, u32[]{:S(2)}, u32[]{:S(2)}) %collective-permute-start.3) | collective-permute-done | bytes 589856 | tf_op jit(solution)/shard_map/ppermute | solution.py:367
  42.6 0.7 shard_map.74
  43.3 0.0 collective-permute-done.7.up_ref.refs_8_
  43.3 0.0 collective-permute-done.6.down_ref.refs_2_
  43.4 0.6 shard_map.75
  44.0 1.3 %collective-permute-start.8 = (bf16[2,64,2304]{2,1,0:T(8,128)(2,1)S(1)}, bf16[2,64,2304]{2,1,0:T(8,128)(2,1)S(1)}, u32[]{:S(2)}, u32[]{:S(2)}) collective-permute-start(bf16[2,64,2304]{2,1,0:T(8,128)(2,1)S(1)} %shard_map.75), channel_id=1, source_target_pairs={{4,0},{8,12},{5,1},{9,13},{6,2},{10,14},{7,3},{11,15},{20,16},{24,... | collective-permute-start | bytes 1769480 | tf_op jit(solution)/shard_map/ppermute | solution.py:367
  45.3 14.1 %collective-permute-start.4 = (bf16[2,64,2304]{2,1,0:T(8,128)(2,1)S(1)}, bf16[2,64,2304]{2,1,0:T(8,128)(2,1)S(1)}, u32[]{:S(2)}, u32[]{:S(2)}) collective-permute-start(bf16[2,64,2304]{2,1,0:T(8,128)(2,1)S(1)} %get-tuple-element.15), channel_id=1, source_target_pairs={{0,8},{12,4},{1,9},{13,5},{2,10},{14,6},{3,11},{15,7},{16,24},{28,... | collective-permute-start | bytes 1769480 | tf_op jit(solution)/shard_map/ppermute | solution.py:367
  59.4 3.8 %collective-permute-start.5 = (bf16[2,64,2304]{2,1,0:T(8,128)(2,1)S(1)}, bf16[2,64,2304]{2,1,0:T(8,128)(2,1)S(1)}, u32[]{:S(2)}, u32[]{:S(2)}) collective-permute-start(bf16[2,64,2304]{2,1,0:T(8,128)(2,1)S(1)} %get-tuple-element.16.rest_0_), channel_id=1, source_target_pairs={{0,12},{12,0},{1,13},{13,1},{2,14},{14,2},{3,15},{15,3},{16,28},{2... | collective-permute-start | bytes 1769480 | tf_op jit(solution)/shard_map/ppermute | solution.py:367
  63.2 6.9 %collective-permute-done.8.refs_3_.refs_9_ = bf16[2,64,2304]{2,1,0:T(8,128)(2,1)S(1)} collective-permute-done((bf16[2,64,2304]{2,1,0:T(8,128)(2,1)S(1)}, bf16[2,64,2304]{2,1,0:T(8,128)(2,1)S(1)}, u32[]{:S(2)}, u32[]{:S(2)}) %collective-permute-start.8) | collective-permute-done | bytes 589856 | tf_op jit(solution)/shard_map/ppermute | solution.py:367
  70.1 0.0 copy-done.1
  70.1 2.7 %shard_map.76.refs_2_.refs_0_ = f32[6,64,128]{2,1,0:T(8,128)S(1)} custom-call(s32[20]{0:T(128)S(1)} %get-tuple-element.13.plan_ref, bf16[8,128,2048]{2,1,0:T(8,128)(2,1)S(1)} %bitcast.5, bf16[4,64,2048]{2,1,0:T(8,128)(2,1)S(1)} %bitcast.10, bf16[2,64,2304]{2,1,0:T(8,128)(2,1)S(1)} %collective-permute-done.3.rest_0_.refs_1_.refs_7_, ...), custom_call_target="tpu_custom_call" | custom-call | tf_op jit(solution)/shard_map/pallas_call | solution.py:289
  72.8 0.0 copy-start.7
  72.8 0.1 collective-permute-start.14
  72.9 1.5 %collective-permute-start.15 = (f32[6,64,128]{2,1,0:T(8,128)S(1)}, f32[6,64,128]{2,1,0:T(8,128)S(1)}, u32[]{:S(2)}, u32[]{:S(2)}) collective-permute-start(f32[6,64,128]{2,1,0:T(8,128)S(1)} %shard_map.76.refs_2_.refs_0_), channel_id=1, source_target_pairs={{0,2},{1,3},{2,0},{3,1},{4,6},{5,7},{6,4},{7,5},{8,10},{9,11},{10,... | collective-permute-start | bytes 589832 | tf_op jit(solution)/shard_map/ppermute | solution.py:20
  74.5 0.0 collective-permute-done.4.refs_0_.refs_6_
  74.5 0.3 collective-permute-start.16
  74.8 12.0 %collective-permute-done.5.refs_1_.refs_7_ = bf16[2,64,2304]{2,1,0:T(8,128)(2,1)S(1)} collective-permute-done((bf16[2,64,2304]{2,1,0:T(8,128)(2,1)S(1)}, bf16[2,64,2304]{2,1,0:T(8,128)(2,1)S(1)}, u32[]{:S(2)}, u32[]{:S(2)}) %collective-permute-start.5) | collective-permute-done | bytes 589856 | tf_op jit(solution)/shard_map/ppermute | solution.py:367
  86.8 1.3 %shard_map.77.refs_10_.refs_0_ = f32[2,64,128]{2,1,0:T(8,128)S(1)} custom-call(s32[20]{0:T(128)S(1)} %get-tuple-element.13.plan_ref, bf16[8,128,2048]{2,1,0:T(8,128)(2,1)S(1)} %bitcast.6, bf16[2,64,2304]{2,1,0:T(8,128)(2,1)S(1)} %collective-permute-done.4.refs_0_.refs_6_, bf16[2,64,2304]{2,1,0:T(8,128)(2,1)S(1)} %collective-permute-done.5.refs_1_.refs_7_, ...), custom_call_target="tpu_custom_call" | custom-call | tf_op jit(solution)/shard_map/pallas_call | solution.py:289
  88.1 0.1 collective-permute-start.9
  88.1 0.0 collective-permute-done.14.refs_1_
  88.2 1.5 %collective-permute-start.10 = (f32[2,64,128]{2,1,0:T(8,128)S(1)}, f32[2,64,128]{2,1,0:T(8,128)S(1)}, u32[]{:S(2)}, u32[]{:S(2)}) collective-permute-start(f32[2,64,128]{2,1,0:T(8,128)S(1)} %shard_map.77.refs_10_.refs_0_), channel_id=1, source_target_pairs={{0,2},{1,3},{2,0},{3,1},{4,6},{5,7},{6,4},{7,5},{8,10},{9,11},{10,... | collective-permute-start | bytes 196616 | tf_op jit(solution)/shard_map/ppermute | solution.py:20
  89.7 0.0 collective-permute-done.15.refs_2_
  89.7 0.3 collective-permute-start.11
  90.0 0.0 collective-permute-done.16.refs_3_
  90.0 0.0 collective-permute-done.13
  90.0 0.0 copy-done.7
  90.0 3.5 %shard_map.80.refs_8_ = bf16[1024,256]{1,0:T(8,128)(2,1)} custom-call(s32[20]{0:T(128)S(1)} %get-tuple-element.13.plan_ref, s32[8]{0:T(128)S(1)} %bitcast.15, f32[6,64,128]{2,1,0:T(8,128)S(1)} %shard_map.76.refs_2_.refs_0_, f32[6,64,128]{2,1,0:T(8,128)S(1)} %collective-permute-done.14.refs_1_, f32[6,64,128]{2,1,0:T(8,128)S(1)} %collective-permute-done.15.refs_2_, ...), custom_call_target="tpu_custom_call" | custom-call | tf_op jit(solution)/shard_map/pallas_call | solution.py:346
  93.5 0.0 collective-permute-done.9.refs_1_
  93.6 0.0 collective-permute-done.10.refs_2_
  93.6 0.2 collective-permute-done.11.refs_3_
  93.8 1.7 %shard_map.81 = bf16[1024,256]{1,0:T(8,128)(2,1)} custom-call(s32[20]{0:T(128)S(1)} %get-tuple-element.13.plan_ref, s32[8]{0:T(128)S(1)} %bitcast.16, f32[2,64,128]{2,1,0:T(8,128)S(1)} %shard_map.77.refs_10_.refs_0_, f32[2,64,128]{2,1,0:T(8,128)S(1)} %collective-permute-done.9.refs_1_, ...), custom_call_target="tpu_custom_call", output_to_operand_aliasing={{}: (10, {})} | custom-call | tf_op jit(solution)/shard_map/pallas_call | solution.py:346
Async XLA Ops:
  0.0 5.6 %collective-permute-start = (s32[1,8]{1,0:T(1,128)}, s32[1,8]{1,0:T(1,128)S(1)}, u32[]{:S(2)}, u32[]{:S(2)}) collective-permute-start(s32[1,8]{1,0:T(1,128)} %names_ref.1), channel_id=1, source_target_pairs={{0,4},{4,0},{8,12},{12,8},{1,5},{5,1},{9,13},{13,9},{2,6},{6,2},{1... | collective-permute-start | bytes 104 | tf_op jit(solution)/shard_map/ppermute | solution.py:20
  3.0 4.6 %collective-permute-start.1 = (s32[1,8]{1,0:T(1,128)}, s32[1,8]{1,0:T(1,128)S(1)}, u32[]{:S(2)}, u32[]{:S(2)}) collective-permute-start(s32[1,8]{1,0:T(1,128)} %names_ref.1), channel_id=1, source_target_pairs={{0,8},{4,12},{8,0},{12,4},{1,9},{5,13},{9,1},{13,5},{2,10},{6,14},... | collective-permute-start | bytes 104 | tf_op jit(solution)/shard_map/ppermute | solution.py:20
  5.6 5.5 %collective-permute-start.2 = (s32[1,8]{1,0:T(1,128)}, s32[1,8]{1,0:T(1,128)S(1)}, u32[]{:S(2)}, u32[]{:S(2)}) collective-permute-start(s32[1,8]{1,0:T(1,128)} %names_ref.1), channel_id=1, source_target_pairs={{0,12},{4,8},{8,4},{12,0},{1,13},{5,9},{9,5},{13,1},{2,14},{6,10},... | collective-permute-start | bytes 104 | tf_op jit(solution)/shard_map/ppermute | solution.py:20
  11.1 1.2 %copy-start.2 = (bf16[4,2048,64]{1,2,0:T(8,128)(2,1)S(1)}, bf16[4,2048,64]{1,2,0:T(8,128)(2,1)}, u32[]{:S(2)}) copy-start(bf16[4,2048,64]{1,2,0:T(8,128)(2,1)} %param.9) | copy-start | bytes 3145732
  12.3 0.9 copy-start.5
  13.2 0.7 copy-start.8
  13.9 0.7 copy-start.9
  16.1 2.2 %copy-start = (bf16[1024,2048]{1,0:T(8,128)(2,1)S(1)}, bf16[1024,2048]{1,0:T(8,128)(2,1)}, u32[]{:S(2)}) copy-start(bf16[1024,2048]{1,0:T(8,128)(2,1)} %tokens_ref.1) | copy-start | bytes 12582916
  18.3 2.2 %copy-start.4 = (bf16[2048,1024]{1,0:T(8,128)(2,1)S(1)}, bf16[2048,1024]{1,0:T(8,128)(2,1)}, u32[]{:S(2)}) copy-start(bf16[2048,1024]{1,0:T(8,128)(2,1)} %weight_ref.1) | copy-start | bytes 12582916
  20.5 5.6 %copy-start.3 = (bf16[4,2048,64]{1,2,0:T(8,128)(2,1)S(1)}, bf16[4,2048,64]{1,2,0:T(8,128)(2,1)}, u32[]{:S(2)}) copy-start(bf16[4,2048,64]{1,2,0:T(8,128)(2,1)} %param.9) | copy-start | bytes 3145732
  20.5 11.8 %copy-start.6 = (bf16[4,64,256]{2,1,0:T(8,128)(2,1)S(1)}, bf16[4,64,256]{2,1,0:T(8,128)(2,1)}, u32[]{:S(2)}) copy-start(bf16[4,64,256]{2,1,0:T(8,128)(2,1)} %refs_6_.1) | copy-start | bytes 393220
  26.0 4.2 %collective-permute-start.12 = (f32[2,1024,256]{2,1,0:T(8,128)S(1)}, f32[2,1024,256]{2,1,0:T(8,128)S(1)}, u32[]{:S(2)}, u32[]{:S(2)}) collective-permute-start(f32[2,1024,256]{2,1,0:T(8,128)S(1)} %get-tuple-element.18), channel_id=1, source_target_pairs={{0,1},{1,0},{2,3},{3,2},{4,5},{5,4},{6,7},{7,6},{8,9},{9,8},{10,11... | collective-permute-start | bytes 6291464 | tf_op jit(solution)/shard_map/ppermute | solution.py:20
  26.1 17.3 %collective-permute-start.6 = (bf16[4,64,2048]{2,1,0:T(8,128)(2,1)S(1)}, bf16[4,64,2048]{2,1,0:T(8,128)(2,1)S(1)}, u32[]{:S(2)}, u32[]{:S(2)}) collective-permute-start(bf16[4,64,2048]{2,1,0:T(8,128)(2,1)S(1)} %bitcast.8), channel_id=1, source_target_pairs={{4,8},{8,4},{5,9},{9,5},{6,10},{10,6},{7,11},{11,7},{20,24},{24,20... | collective-permute-start | bytes 3145736 | tf_op jit(solution)/shard_map/ppermute | solution.py:367
  26.8 15.8 %collective-permute-start.3 = (bf16[2,64,2304]{2,1,0:T(8,128)(2,1)S(1)}, bf16[2,64,2304]{2,1,0:T(8,128)(2,1)S(1)}, u32[]{:S(2)}, u32[]{:S(2)}) collective-permute-start(bf16[2,64,2304]{2,1,0:T(8,128)(2,1)S(1)} %get-tuple-element.14.refs_0_), channel_id=1, source_target_pairs={{0,4},{4,0},{8,12},{12,8},{1,5},{5,1},{9,13},{13,9},{2,6},{6,2},{1... | collective-permute-start | bytes 1769480 | tf_op jit(solution)/shard_map/ppermute | solution.py:367
  30.2 39.9 %copy-start.1 = (bf16[1024,2048]{1,0:T(8,128)(2,1)S(1)}, bf16[1024,2048]{1,0:T(8,128)(2,1)}, u32[]{:S(2)}) copy-start(bf16[1024,2048]{1,0:T(8,128)(2,1)} %tokens_ref.1) | copy-start | bytes 12582916
  30.8 59.2 %collective-permute-start.13 = (f32[1,1024,256]{2,1,0:T(8,128)S(1)}, f32[1,1024,256]{2,1,0:T(8,128)S(1)}, u32[]{:S(2)}, u32[]{:S(2)}) collective-permute-start(f32[1,1024,256]{2,1,0:T(8,128)S(1)} %get-tuple-element.20), channel_id=1, source_target_pairs={{0,2},{1,3},{2,0},{3,1},{4,6},{5,7},{6,4},{7,5},{8,10},{9,11},{10,... | collective-permute-start | bytes 3145736 | tf_op jit(solution)/shard_map/ppermute | solution.py:20
  32.3 11.0 %collective-permute-start.7 = (bf16[4,64,256]{2,1,0:T(8,128)(2,1)S(1)}, bf16[4,64,256]{2,1,0:T(8,128)(2,1)S(1)}, u32[]{:S(2)}, u32[]{:S(2)}) collective-permute-start(bf16[4,64,256]{2,1,0:T(8,128)(2,1)S(1)} %copy-done.6), channel_id=1, source_target_pairs={{4,8},{8,4},{5,9},{9,5},{6,10},{10,6},{7,11},{11,7},{20,24},{24,20... | collective-permute-start | bytes 393224 | tf_op jit(solution)/shard_map/ppermute | solution.py:367
  44.0 26.1 %collective-permute-start.8 = (bf16[2,64,2304]{2,1,0:T(8,128)(2,1)S(1)}, bf16[2,64,2304]{2,1,0:T(8,128)(2,1)S(1)}, u32[]{:S(2)}, u32[]{:S(2)}) collective-permute-start(bf16[2,64,2304]{2,1,0:T(8,128)(2,1)S(1)} %shard_map.75), channel_id=1, source_target_pairs={{4,0},{8,12},{5,1},{9,13},{6,2},{10,14},{7,3},{11,15},{20,16},{24,... | collective-permute-start | bytes 1769480 | tf_op jit(solution)/shard_map/ppermute | solution.py:367
  45.3 29.2 %collective-permute-start.4 = (bf16[2,64,2304]{2,1,0:T(8,128)(2,1)S(1)}, bf16[2,64,2304]{2,1,0:T(8,128)(2,1)S(1)}, u32[]{:S(2)}, u32[]{:S(2)}) collective-permute-start(bf16[2,64,2304]{2,1,0:T(8,128)(2,1)S(1)} %get-tuple-element.15), channel_id=1, source_target_pairs={{0,8},{12,4},{1,9},{13,5},{2,10},{14,6},{3,11},{15,7},{16,24},{28,... | collective-permute-start | bytes 1769480 | tf_op jit(solution)/shard_map/ppermute | solution.py:367
  59.4 27.4 %collective-permute-start.5 = (bf16[2,64,2304]{2,1,0:T(8,128)(2,1)S(1)}, bf16[2,64,2304]{2,1,0:T(8,128)(2,1)S(1)}, u32[]{:S(2)}, u32[]{:S(2)}) collective-permute-start(bf16[2,64,2304]{2,1,0:T(8,128)(2,1)S(1)} %get-tuple-element.16.rest_0_), channel_id=1, source_target_pairs={{0,12},{12,0},{1,13},{13,1},{2,14},{14,2},{3,15},{15,3},{16,28},{2... | collective-permute-start | bytes 1769480 | tf_op jit(solution)/shard_map/ppermute | solution.py:367
  72.8 17.2 %copy-start.7 = (s32[1,8]{1,0:T(1,128)S(1)}, s32[1,8]{1,0:T(1,128)}, u32[]{:S(2)}) copy-start(s32[1,8]{1,0:T(1,128)} %param.13) | copy-start | bytes 100
  72.8 15.3 %collective-permute-start.14 = (f32[6,64,128]{2,1,0:T(8,128)S(1)}, f32[6,64,128]{2,1,0:T(8,128)S(1)}, u32[]{:S(2)}, u32[]{:S(2)}) collective-permute-start(f32[6,64,128]{2,1,0:T(8,128)S(1)} %shard_map.76.refs_2_.refs_0_), channel_id=1, source_target_pairs={{0,1},{1,0},{2,3},{3,2},{4,5},{5,4},{6,7},{7,6},{8,9},{9,8},{10,11... | collective-permute-start | bytes 589832 | tf_op jit(solution)/shard_map/ppermute | solution.py:20
  72.9 16.8 %collective-permute-start.15 = (f32[6,64,128]{2,1,0:T(8,128)S(1)}, f32[6,64,128]{2,1,0:T(8,128)S(1)}, u32[]{:S(2)}, u32[]{:S(2)}) collective-permute-start(f32[6,64,128]{2,1,0:T(8,128)S(1)} %shard_map.76.refs_2_.refs_0_), channel_id=1, source_target_pairs={{0,2},{1,3},{2,0},{3,1},{4,6},{5,7},{6,4},{7,5},{8,10},{9,11},{10,... | collective-permute-start | bytes 589832 | tf_op jit(solution)/shard_map/ppermute | solution.py:20
  74.5 15.5 %collective-permute-start.16 = (f32[6,64,128]{2,1,0:T(8,128)S(1)}, f32[6,64,128]{2,1,0:T(8,128)S(1)}, u32[]{:S(2)}, u32[]{:S(2)}) collective-permute-start(f32[6,64,128]{2,1,0:T(8,128)S(1)} %shard_map.76.refs_2_.refs_0_), channel_id=1, source_target_pairs={{0,3},{1,2},{2,1},{3,0},{4,7},{5,6},{6,5},{7,4},{8,11},{9,10},{10,... | collective-permute-start | bytes 589832 | tf_op jit(solution)/shard_map/ppermute | solution.py:20
  88.1 5.5 %collective-permute-start.9 = (f32[2,64,128]{2,1,0:T(8,128)S(1)}, f32[2,64,128]{2,1,0:T(8,128)S(1)}, u32[]{:S(2)}, u32[]{:S(2)}) collective-permute-start(f32[2,64,128]{2,1,0:T(8,128)S(1)} %shard_map.77.refs_10_.refs_0_), channel_id=1, source_target_pairs={{0,1},{1,0},{2,3},{3,2},{4,5},{5,4},{6,7},{7,6},{8,9},{9,8},{10,11... | collective-permute-start | bytes 196616 | tf_op jit(solution)/shard_map/ppermute | solution.py:20
  88.2 5.4 %collective-permute-start.10 = (f32[2,64,128]{2,1,0:T(8,128)S(1)}, f32[2,64,128]{2,1,0:T(8,128)S(1)}, u32[]{:S(2)}, u32[]{:S(2)}) collective-permute-start(f32[2,64,128]{2,1,0:T(8,128)S(1)} %shard_map.77.refs_10_.refs_0_), channel_id=1, source_target_pairs={{0,2},{1,3},{2,0},{3,1},{4,6},{5,7},{6,4},{7,5},{8,10},{9,11},{10,... | collective-permute-start | bytes 196616 | tf_op jit(solution)/shard_map/ppermute | solution.py:20
  89.7 4.1 %collective-permute-start.11 = (f32[2,64,128]{2,1,0:T(8,128)S(1)}, f32[2,64,128]{2,1,0:T(8,128)S(1)}, u32[]{:S(2)}, u32[]{:S(2)}) collective-permute-start(f32[2,64,128]{2,1,0:T(8,128)S(1)} %shard_map.77.refs_10_.refs_0_), channel_id=1, source_target_pairs={{0,3},{1,2},{2,1},{3,0},{4,7},{5,6},{6,5},{7,4},{8,11},{9,10},{10,... | collective-permute-start | bytes 196616 | tf_op jit(solution)/shard_map/ppermute | solution.py:20

commit v3 on v2

--- a/solution.py
+++ b/solution.py
@@ -8,11 +8,16 @@
 from jax.sharding import PartitionSpec as P
 
 ADAPTER_SCALE = 0.5
-ROW_TILE = 256
-PARAMS = pltpu.CompilerParams(vmem_limit_bytes=16 * 1024 * 1024)
+ROW_TILE = 128
+PARAMS = pltpu.CompilerParams(vmem_limit_bytes=20 * 1024 * 1024)
 NO_COST = pl.CostEstimate(flops=0, bytes_accessed=0, transcendentals=0)
+LONG = pl.CostEstimate(flops=4 * 10**10, bytes_accessed=0, transcendentals=0)
 ANY = pl.BlockSpec(memory_space=pl.ANY)
 SMEM = pl.BlockSpec(memory_space=pltpu.SMEM)
+
+
+def in_hbm(value):
+    return pltpu.with_memory_space_constraint(value, pltpu.HBM)
 
 
 def swap(value, axis, distance):
@@ -20,59 +25,85 @@
     return lax.ppermute(value, axis, pairs)
 
 
+def piece_rows(rows):
+    tile = min(ROW_TILE, rows)
+    tiles = rows // tile
+    counts = [(tiles + 2 - i) // 3 for i in range(3)]
+    return [count * tile for count in counts if count]
+
+
 def base_kernel(order, tokens_ref, weight_ref, *refs):
-    width = refs[-1].shape[2]
+    kept_ref = refs[-1]
+    half, rows, width = kept_ref.shape
+    sizes = piece_rows(rows)
+    sent_refs = refs[-1 - len(sizes) : -1]
     place = lax.axis_index("tensor")
-    outs = refs[-2:]
-    half = len(order) // 2
-    for number, offset in enumerate(order):
-        columns = pl.ds(pl.multiple_of((place ^ offset) * width, width), width)
-        outs[number // half][number % half] = jnp.dot(
-            tokens_ref[...], weight_ref[:, columns], preferred_element_type=jnp.float32
+    step = pl.program_id(0)
+    columns = place ^ jnp.where(step < half, order[0], order[half])
+    for number in range(1, half):
+        columns = jnp.where(step == number, place ^ order[number], columns)
+        columns = jnp.where(step == half + number, place ^ order[half + number], columns)
+    columns = pl.ds(pl.multiple_of(columns * width, width), width)
+    start = 0
+    for sent_ref, size in zip(sent_refs, sizes):
+        part = jnp.dot(
+            tokens_ref[start : start + size, :],
+            weight_ref[:, columns],
+            preferred_element_type=jnp.float32,
         )
+
+        @pl.when(step < half)
+        def _(sent_ref=sent_ref, part=part):
+            sent_ref[jnp.minimum(step, half - 1)] = part
+
+        @pl.when(step >= half)
+        def _(start=start, size=size, part=part):
+            kept_ref[jnp.maximum(step - half, 0), start : start + size, :] = part
+
+        start += size
 
 
 def base_chunks(tokens, weight, order, width, after):
     rows, depth = tokens.shape
-    tile = min(ROW_TILE, rows)
     half = len(order) // 2
-    out = jax.ShapeDtypeStruct((half, rows, width), jnp.float32)
-    return pl.pallas_call(
+    shapes = [(half, size, width) for size in piece_rows(rows)] + [(half, rows, width)]
+    *sent, kept = pl.pallas_call(
         functools.partial(base_kernel, order),
-        grid=(rows // tile,),
+        grid=(len(order),),
         in_specs=[
-            pl.BlockSpec((tile, depth), lambda i: (i, 0)),
+            pl.BlockSpec(tokens.shape, lambda i: (0, 0), pipeline_mode=pl.Buffered(1)),
             pl.BlockSpec(weight.shape, lambda i: (0, 0), pipeline_mode=pl.Buffered(1)),
         ]
         + [ANY] * len(after),
-        out_specs=[pl.BlockSpec((half, tile, width), lambda i: (0, i, 0))] * 2,
+        out_specs=[pl.BlockSpec(shape, lambda i: (0, 0, 0)) for shape in shapes],
+        out_shape=[jax.ShapeDtypeStruct(shape, jnp.float32) for shape in shapes],
+        compiler_params=PARAMS,
+        cost_estimate=NO_COST,
+    )(in_hbm(tokens), in_hbm(weight), *after)
+    return sent, kept
+
+
+def add_kernel(kept_ref, *refs):
+    *arrived_refs, out_ref, mine_ref = refs
+    half = kept_ref.shape[0] // 2
+    start = 0
+    for arrived_ref in arrived_refs:
+        rows = pl.ds(start, arrived_ref.shape[1])
+        for i in range(half):
+            mine_ref[i, rows, :] = kept_ref[i, rows, :] + arrived_ref[i]
+            out_ref[i, rows, :] = kept_ref[half + i, rows, :] + arrived_ref[half + i]
+        start += arrived_ref.shape[1]
+
+
+def add_halves(kept, arrived):
+    count, rows, width = kept.shape
+    out = jax.ShapeDtypeStruct((count // 2, rows, width), jnp.float32)
+    return pl.pallas_call(
+        add_kernel,
         out_shape=[out, out],
         compiler_params=PARAMS,
         cost_estimate=NO_COST,
-    )(tokens, weight, *after)
-
-
-def add_kernel(kept_ref, arrived_ref, out_ref, mine_ref):
-    half = kept_ref.shape[0] // 2
-    for i in range(half):
-        mine_ref[i] = kept_ref[i] + arrived_ref[i]
-        out_ref[i] = kept_ref[half + i] + arrived_ref[half + i]
-
-
-def add_halves(kept, arrived):
-    count, rows, width = kept.shape
-    tile = min(ROW_TILE, rows)
-    half = count // 2
-    out = jax.ShapeDtypeStruct((half, rows, width), jnp.float32)
-    return pl.pallas_call(
-        add_kernel,
-        grid=(rows // tile,),
-        in_specs=[pl.BlockSpec((count, tile, width), lambda i: (0, i, 0))] * 2,
-        out_specs=[pl.BlockSpec((half, tile, width), lambda i: (0, i, 0))] * 2,
-        out_shape=[out, out],
-        compiler_params=PARAMS,
-        cost_estimate=NO_COST,
-    )(kept, arrived)
+    )(kept, *arrived)
 
 
 def base_sum(tokens, weight, width, after):
@@ -80,13 +111,13 @@
     kept_order = [k for k in range(size) if not k & 1]
     kept_order.sort(key=lambda k: [k >> bit & 1 for bit in range(1, size.bit_length())])
     sent, kept = base_chunks(tokens, weight, [k ^ 1 for k in kept_order] + kept_order, width, after)
-    arrived = swap(sent, "tensor", 1)
+    arrived = [swap(piece, "tensor", 1) for piece in sent]
     distance = 2
     while distance < size:
         sent, kept = add_halves(kept, arrived)
-        arrived = swap(sent, "tensor", distance)
+        arrived = [swap(sent, "tensor", distance)]
         distance *= 2
-    return kept[0], arrived[0]
+    return kept[0], arrived[0][0]
 
 
 def pick(names_ref, table_ref, holder, holder_slots, count):
@@ -119,19 +150,16 @@
     return copies
 
 
-def plan_kernel(
-    capacity,
-    names_ref,
-    first_ref,
-    second_ref,
-    third_ref,
-    table_ref,
-    down_ref,
-    up_ref,
-    near_ref,
-    plan_ref,
-    sems,
-):
+def plan_kernel(capacity, *refs):
+    sources, down_ref, up_ref, near_ref, plan_ref = refs[:6], *refs[6:10]
+    scalars, scalar_sems, sems = refs[10:16], *refs[16:]
+    loads = [
+        pltpu.make_async_copy(source, scalar, scalar_sems.at[i])
+        for i, (source, scalar) in enumerate(zip(sources, scalars))
+    ]
+    for load in run_copies(loads):
+        load.wait()
+    names_ref, first_ref, second_ref, third_ref, table_ref, live_ref = scalars
     here = lax.axis_index("pool")
     holder_slots = down_ref.shape[0]
     find = functools.partial(
@@ -156,6 +184,7 @@
         find(third_ref, holder=here)[1],
         find(first_ref, holder=here ^ 3)[1],
         [inner.astype(jnp.int32)] * capacity,
+        *[[live_ref[0, block] for block in phase[0]] for phase in (own, near, early, late)],
     ]
     for number, row in enumerate(rows):
         for k in range(capacity):
@@ -164,24 +193,26 @@
         copy.wait()
 
 
-OWN, EARLY, TO_INNER, TO_OUTER, FORWARD, INNER, PLAN_ROWS = 4, 5, 6, 7, 8, 9, 10
-
-
-def make_plan(names, others, table, down, up, capacity):
+OWN, EARLY, TO_INNER, TO_OUTER, FORWARD, INNER, LIVE, PLAN_ROWS = 4, 5, 6, 7, 8, 9, 10, 14
+
+
+def make_plan(names, others, table, live, down, up, capacity):
     rank, depth = down.shape[1:]
     width = up.shape[2]
     return pl.pallas_call(
         functools.partial(plan_kernel, capacity),
-        in_specs=[SMEM] * 5 + [ANY] * 2,
+        in_specs=[ANY] * 8,
         out_specs=[ANY, SMEM],
         out_shape=[
             jax.ShapeDtypeStruct((capacity, rank, depth + width), down.dtype),
             jax.ShapeDtypeStruct((PLAN_ROWS * capacity,), jnp.int32),
         ],
-        scratch_shapes=[pltpu.SemaphoreType.DMA((capacity, 2))],
+        scratch_shapes=[pltpu.SMEM(names.shape, jnp.int32)] * 4
+        + [pltpu.SMEM(table.shape, jnp.int32), pltpu.SMEM(live.shape, jnp.int32)]
+        + [pltpu.SemaphoreType.DMA((6,)), pltpu.SemaphoreType.DMA((capacity, 2))],
         compiler_params=PARAMS,
         cost_estimate=NO_COST,
-    )(names, *others, table, down, up)
+    )(in_hbm(names), *others, *[in_hbm(a) for a in (table, live, down, up)])
 
 
 def pack_kernel(starts, capacity, plan_ref, down_ref, up_ref, *rest):
@@ -199,7 +230,7 @@
         copy.wait()
 
 
-def pack_panels(plan, starts, capacity, down, up, after=()):
+def pack_panels(plan, starts, capacity, down, up, after=(), cost=None):
     rank, depth = down.shape[1:]
     width = up.shape[2]
     out = jax.ShapeDtypeStruct((capacity, rank, depth + width), down.dtype)
@@ -210,7 +241,7 @@
         out_shape=[out] * len(starts),
         scratch_shapes=[pltpu.SemaphoreType.DMA((len(starts), capacity, 2))],
         compiler_params=PARAMS,
-        cost_estimate=NO_COST,
+        cost_estimate=cost or NO_COST,
     )(plan, down, up, *after)
 
 
@@ -306,7 +337,7 @@
     return [part] + [swap(part, "tensor", m) for m in range(1, lax.axis_size("tensor"))]
 
 
-def combine_kernel(phases, choose, part_count, block, plan_ref, live_ref, *refs):
+def combine_kernel(phases, choose, part_count, live_row, plan_ref, *refs):
     parts = refs[:part_count]
     mine_ref, far_ref = refs[part_count : part_count + 2]
     out_ref = refs[-1]
@@ -314,7 +345,7 @@
     for part in parts[1:]:
         total = total + part[0]
     shrunk = total.astype(jnp.bfloat16)
-    live = live_ref[block(pl.program_id(0), plan_ref)]
+    live = plan_ref[live_row + pl.program_id(0)]
 
     def act(up_ref):
         delta = lax.dot_general(
@@ -327,13 +358,13 @@
     for_phase(phases, choose, plan_ref, refs[part_count + 2 :], act)
 
 
-def combine(plan, live, parts, base, phases, columns, choose, out=None, after=()):
+def combine(plan, live_row, parts, base, phases, columns, choose, out=None, after=()):
     rank, block_rows = parts[0].shape[1:]
     rows, width = base[0].shape
     total = sum(count for _, count, _ in phases)
     block = block_index(phases)
-    specs = [pl.BlockSpec((1, rank, block_rows), lambda i, plan, live: (i, 0, 0))] * len(parts)
-    specs += [pl.BlockSpec((block_rows, width), lambda i, plan, live: (block(i, plan), 0))] * 2
+    specs = [pl.BlockSpec((1, rank, block_rows), lambda i, plan: (i, 0, 0))] * len(parts)
+    specs += [pl.BlockSpec((block_rows, width), lambda i, plan: (block(i, plan), 0))] * 2
     more, operands = source_specs(phases, (1, rank, width), columns)
     specs += more + [ANY] * len(after)
     operands = [*parts, *base, *operands, *after]
@@ -341,23 +372,21 @@
     if out is not None:
         specs.append(ANY)
         operands.append(out)
-        aliases = {1 + len(operands): 0}
+        aliases = {len(operands): 0}
     shapes = [(row, count, [None] * len(sources)) for row, count, sources in phases]
     return pl.pallas_call(
-        functools.partial(combine_kernel, shapes, choose, len(parts), block_index(shapes)),
+        functools.partial(combine_kernel, shapes, choose, len(parts), live_row),
         grid_spec=pltpu.PrefetchScalarGridSpec(
-            num_scalar_prefetch=2,
+            num_scalar_prefetch=1,
             grid=(total,),
             in_specs=specs,
-            out_specs=pl.BlockSpec(
-                (block_rows, width), lambda i, plan, live: (block(i, plan), 0)
-            ),
+            out_specs=pl.BlockSpec((block_rows, width), lambda i, plan: (block(i, plan), 0)),
         ),
         out_shape=jax.ShapeDtypeStruct((rows, width), jnp.bfloat16),
         input_output_aliases=aliases,
         compiler_params=PARAMS,
         cost_estimate=NO_COST,
-    )(plan, live, *operands)
+    )(plan, *operands)
 
 
 def on_line_of_four(tokens, weight, row_blocks, down, up, names, table, live, capacity):
@@ -369,40 +398,58 @@
     others = [swap(names, "pool", m) for m in range(1, 4)]
     inner_down = across(down, [(1, 2), (2, 1)])
     inner_up = across(up, [(1, 2), (2, 1)])
-    near_out, plan = make_plan(names, others, table, down, up, capacity)
+    near_out, plan = make_plan(names, others, table, live, down, up, capacity)
     near = across(near_out, [(0, 1), (1, 0), (2, 3), (3, 2)])
     base = base_sum(tokens, weight, up.shape[2], [near_out])
     inner_out, outer_out = pack_panels(
-        plan, [TO_INNER * capacity, TO_OUTER * capacity], capacity, down, up, [near]
+        plan,
+        [TO_INNER * capacity, TO_OUTER * capacity],
+        capacity,
+        in_hbm(down),
+        in_hbm(up),
+        [base[0]],
     )
     to_inner = across(inner_out, [(0, 2), (3, 1)])
     to_outer = across(outer_out, [(0, 3), (3, 0)])
-    (forward_out,) = pack_panels(
-        plan, [FORWARD * capacity], capacity, inner_down, inner_up, [outer_out]
-    )
-    forwarded = across(forward_out, [(1, 0), (2, 3)])
+    forward_out = pack_panels(
+        plan,
+        [FORWARD * capacity + k for k in range(capacity)],
+        1,
+        inner_down,
+        inner_up,
+        [outer_out, near],
+        LONG,
+    )
+    forwarded = [across(panel, [(1, 0), (2, 3)]) for panel in forward_out]
 
     choose = INNER * capacity
     first = [
         (0, capacity, [(down, OWN * capacity)]),
         (capacity, capacity, [(near, None)]),
-        (2 * capacity, capacity, [(inner_down, EARLY * capacity), (forwarded, None)]),
+        *[
+            (2 * capacity + k, 1, [(inner_down, EARLY * capacity + k), (forwarded[k], None)])
+            for k in range(capacity)
+        ],
     ]
     last = [(3 * capacity, capacity, [(to_inner, None), (to_outer, None)])]
     first_up = [
         (0, capacity, [(up, OWN * capacity)]),
         (capacity, capacity, [(near, None)]),
-        (2 * capacity, capacity, [(inner_up, EARLY * capacity), (forwarded, None)]),
+        *[
+            (2 * capacity + k, 1, [(inner_up, EARLY * capacity + k), (forwarded[k], None)])
+            for k in range(capacity)
+        ],
     ]
-    first_columns = [[0], [up_column], [0, up_column]]
-    first_part = shrink(plan, row_blocks, first, choose)
-    first_parts = exchange(first_part)
-    last_part = shrink(plan, row_blocks, last, choose, [first_part])
-    last_parts = exchange(last_part)
+    first_columns = [[0], [up_column]] + [[0, up_column]] * capacity
+    first_parts = exchange(shrink(plan, row_blocks, first, choose))
     out = combine(
-        plan, live, first_parts, base, first_up, first_columns, choose, after=[last_part]
-    )
-    return combine(plan, live, last_parts, base, last, [[up_column] * 2], choose, out)
+        plan, LIVE * capacity, first_parts, base, first_up, first_columns, choose
+    )
+    last_parts = exchange(shrink(plan, row_blocks, last, choose, [out]))
+    last_columns = [[up_column] * 2]
+    return combine(
+        plan, (LIVE + 3) * capacity, last_parts, base, last, last_columns, choose, out
+    )
 
 
 def on_any_pool(tokens, weight, row_blocks, down, up, names, table, live, capacity):
@@ -426,11 +473,12 @@
     earlier = (owners[:, None] == owners[None, :]) & (blocks[:, None] > blocks[None, :])
     ranks = jnp.sum(earlier.astype(jnp.int32), axis=1)
     places = lax.rem(here - owners + pool_size, pool_size) * capacity + ranks
-    plan = jnp.concatenate([blocks, places])
+    plan = jnp.concatenate([blocks, places, live[0]])
     base = base_sum(tokens, weight, up.shape[2], [])
     phases = [(0, blocks.shape[0], [(arrived, blocks.shape[0])])]
     parts = exchange(shrink(plan, row_blocks, phases, 0))
-    return combine(plan, live, parts, base, phases, [[depth // up.shape[2]]], 0)
+    live_row = 2 * blocks.shape[0]
+    return combine(plan, live_row, parts, base, phases, [[depth // up.shape[2]]], 0)
 
 
 def on_device(
@@ -456,7 +504,7 @@
         adapter_up_weight,
         adapter_of_block,
         adapter_pool_slot,
-        live_block_tokens[0],
+        live_block_tokens,
         capacity,
     )
 

time: 95.8 us -> 108 us (1.13)
  waiting for transfers between devices: 36.6 us -> 49.1 us
  Pallas kernels: 18.3 us -> 28 us
  local copies, waits for them, and re-layouts: 7.83 us -> 1.06 us
  starting transfers between devices: 32.5 us -> 28.9 us
    ppermute x11 -> x13, waiting for transfers between devices: 8.18 us -> 35.5 us  [swap(): return lax.ppermute(value, axis, pairs)]
    ppermute x6 -> x7, waiting for transfers between devices: 28.5 us -> 13.6 us  [across(): return lax.ppermute(value, 'pool', pairs)]
    pallas_call x3, Pallas kernels: 7.63 us -> 16.2 us  [the longest x1 13.3 us: base_chunks(): pl.pallas_call(functools.partial(base_kernel, order), grid=(len(order),),...]
    ppermute x6 -> x7, starting transfers between devices: 21.5 us -> 13.7 us  [across(): return lax.ppermute(value, 'pool', pairs)]
    unnamed x20 -> x10, local copies, waits for them, and re-layouts: 7.83 us -> 1.06 us
    ppermute x11 -> x13, starting transfers between devices: 11.1 us -> 15.2 us  [swap(): return lax.ppermute(value, axis, pairs)]
    pallas_call x2, Pallas kernels: 1.38 us -> 2.49 us  [pack_panels(): pl.pallas_call(functools.partial(pack_kernel, starts, capacity), in_specs...]
  transfers between devices with their start and end apart: 17 -> 20, of which waited for: 7 -> 10; matrix products, arithmetic and copies ran while one was open for 0% -> 0% of each run, Pallas kernels for 10% -> 23%
where the time goes in v3:
time: 108 us; the launch traced here: 107 us
  waiting for transfers between devices  49.1 us (45%)
  starting transfers between devices  28.9 us (27%)
  Pallas kernels  28 us (26%)
    ppermute x13, waiting for transfers between devices, swap(): return lax.ppermute(value, axis, pairs)  35.5 us
    ppermute x13, starting transfers between devices, swap(): return lax.ppermute(value, axis, pairs)  15.2 us
    ppermute x7, starting transfers between devices, across(): return lax.ppermute(value, 'pool', pairs)  13.7 us
    ppermute x7, waiting for transfers between devices, across(): return lax.ppermute(value, 'pool', pairs)  13.6 us
    pallas_call x1, Pallas kernels, base_chunks(): pl.pallas_call(functools.partial(base_kernel, order), grid=(len(order),),...  13.3 us
    pallas_call x2, Pallas kernels, combine(): pl.pallas_call(functools.partial(combine_kernel, shapes, choose, len(part...  5.21 us
    pallas_call x2, Pallas kernels, shrink(): pl.pallas_call(functools.partial(shrink_kernel, shapes, choose), grid_spe...  4.05 us
    pallas_call x1, Pallas kernels, make_plan(): pl.pallas_call(functools.partial(plan_kernel, capacity), in_specs=[ANY] *...  2.7 us
  transfers between devices with their start and end apart: 20, of which 10 were waited for; matrix products, arithmetic and copies ran while one was open for 0% of the time, Pallas kernels for 23%

profile of v3, /device:TPU:0, one launch (start us, length us, event | category | flops | bytes accessed | tf_op | source)
XLA Modules:
  0.0 107.3 jit_solution(253414806548222641)
XLA Ops:
  0.0 0.7 collective-permute-start.9
  0.7 5.8 %collective-permute-start = (s32[1,8]{1,0:T(1,128)}, s32[1,8]{1,0:T(1,128)S(1)}, u32[]{:S(2)}, u32[]{:S(2)}) collective-permute-start(s32[1,8]{1,0:T(1,128)} %refs_0_.1), channel_id=1, source_target_pairs={{0,4},{4,0},{8,12},{12,8},{1,5},{5,1},{9,13},{13,9},{2,6},{6,2},{1... | collective-permute-start | bytes 104 | tf_op jit(solution)/shard_map/ppermute | solution.py:25
  6.6 0.0 collective-permute-start.1
  6.6 2.4 %collective-permute-start.2 = (s32[1,8]{1,0:T(1,128)}, s32[1,8]{1,0:T(1,128)S(1)}, u32[]{:S(2)}, u32[]{:S(2)}) collective-permute-start(s32[1,8]{1,0:T(1,128)} %refs_0_.1), channel_id=1, source_target_pairs={{0,12},{4,8},{8,4},{12,0},{1,13},{5,9},{9,5},{13,1},{2,14},{6,10},... | collective-permute-start | bytes 104 | tf_op jit(solution)/shard_map/ppermute | solution.py:25
  9.0 0.0 collective-permute-done.refs_1_
  9.0 20.4 %collective-permute-done.1.refs_2_ = s32[1,8]{1,0:T(1,128)S(1)} collective-permute-done((s32[1,8]{1,0:T(1,128)}, s32[1,8]{1,0:T(1,128)S(1)}, u32[]{:S(2)}, u32[]{:S(2)}) %collective-permute-start.1) | collective-permute-done | bytes 64 | tf_op jit(solution)/shard_map/ppermute | solution.py:25
  29.5 0.0 collective-permute-done.2.refs_3_
  29.5 2.7 %shard_map.73 = (bf16[2,64,2304]{2,1,0:T(8,128)(2,1)S(1)}, s32[28]{0:T(128)S(1)}) custom-call(s32[1,8]{1,0:T(1,128)} %refs_0_.1, s32[1,8]{1,0:T(1,128)S(1)} %collective-permute-done.refs_1_, s32[1,8]{1,0:T(1,128)S(1)} %collective-permute-done.1.refs_2_, s32[1,8]{1,0:T(1,128)S(1)} %collective-permute-done.2.refs_3_, s32[16]{0:T(128)} %refs_4_.1, ...), custom_call_target="tpu_custom_call" | custom-call | tf_op jit(solution)/shard_map/pallas_call | solution.py:202
  32.2 0.0 copy-start.3
  32.2 13.3 %shard_map.74 = (f32[2,384,256]{2,1,0:T(8,128)S(1)}, f32[2,384,256]{2,1,0:T(8,128)S(1)}, f32[2,256,256]{2,1,0:T(8,128)S(1)}, f32[2,1024,256]{2,1,0:T(8,128)S(1)}) custom-call(bf16[1024,2048]{1,0:T(8,128)(2,1)} %tokens_ref.1, bf16[2048,1024]{1,0:T(8,128)(2,1)} %weight_ref.1, bf16[2,64,2304]{2,1,0:T(8,128)(2,1)S(1)} %get-tuple-element.18.refs_0_), custom_call_target="tpu_custom_call" | custom-call | tf_op jit(solution)/shard_map/pallas_call | solution.py:70
  45.5 0.1 collective-permute-start.3
  45.6 0.5 collective-permute-start.4
  46.1 0.1 collective-permute-start.5
  46.1 0.6 collective-permute-start.8
  46.8 2.9 %collective-permute-done.5.refs_2_ = f32[2,256,256]{2,1,0:T(8,128)S(1)} collective-permute-done((f32[2,256,256]{2,1,0:T(8,128)S(1)}, f32[2,256,256]{2,1,0:T(8,128)S(1)}, u32[]{:S(2)}, u32[]{:S(2)}) %collective-permute-start.5) | collective-permute-done | bytes 524320 | tf_op jit(solution)/shard_map/ppermute | solution.py:25
  49.7 0.0 copy-done.3
  49.7 0.7 collective-permute-start.10
  50.4 0.0 collective-permute-done.3.refs_0_
  50.4 0.0 collective-permute-done.4.refs_1_
  50.4 0.2 shard_map.75
  50.7 1.6 %collective-permute-start.16 = (f32[1,1024,256]{2,1,0:T(8,128)S(1)}, f32[1,1024,256]{2,1,0:T(8,128)S(1)}, u32[]{:S(2)}, u32[]{:S(2)}) collective-permute-start(f32[1,1024,256]{2,1,0:T(8,128)S(1)} %get-tuple-element.28), channel_id=1, source_target_pairs={{0,2},{1,3},{2,0},{3,1},{4,6},{5,7},{6,4},{7,5},{8,10},{9,11},{10,... | collective-permute-start | bytes 3145736 | tf_op jit(solution)/shard_map/ppermute | solution.py:25
  52.2 1.9 %shard_map.76 = (bf16[2,64,2304]{2,1,0:T(8,128)(2,1)S(1)}, bf16[2,64,2304]{2,1,0:T(8,128)(2,1)S(1)}) custom-call(s32[28]{0:T(128)S(1)} %get-tuple-element.17.plan_ref, bf16[4,64,2048]{2,1,0:T(8,128)(2,1)} %bitcast.11, bf16[4,64,256]{2,1,0:T(8,128)(2,1)} %refs_6_.1, f32[1024,256]{1,0:T(8,128)S(1)} %bitcast.6), custom_call_target="tpu_custom_call" | custom-call | tf_op jit(solution)/shard_map/pallas_call | solution.py:237
  54.1 0.0 collective-permute-done.10.up_ref.refs_8_.refs_10_
  54.1 7.7 %collective-permute-done.8.rest_1_.refs_1_.refs_7_ = bf16[2,64,2304]{2,1,0:T(8,128)(2,1)S(1)} collective-permute-done((bf16[2,64,2304]{2,1,0:T(8,128)(2,1)S(1)}, bf16[2,64,2304]{2,1,0:T(8,128)(2,1)S(1)}, u32[]{:S(2)}, u32[]{:S(2)}) %collective-permute-start.8) | collective-permute-done | bytes 589856 | tf_op jit(solution)/shard_map/ppermute | solution.py:396
  61.8 0.0 collective-permute-done.9.down_ref.refs_2_.refs_4_
  61.8 0.0 copy-start
  61.8 0.0 copy-start.1
  61.8 0.6 shard_map.77
  62.5 1.6 %collective-permute-start.11 = (bf16[1,64,2304]{2,1,0:T(8,128)(2,1)S(1)}, bf16[1,64,2304]{2,1,0:T(8,128)(2,1)S(1)}, u32[]{:S(2)}, u32[]{:S(2)}) collective-permute-start(bf16[1,64,2304]{2,1,0:T(8,128)(2,1)S(1)} %get-tuple-element.26), channel_id=1, source_target_pairs={{4,0},{8,12},{5,1},{9,13},{6,2},{10,14},{7,3},{11,15},{20,16},{24,... | collective-permute-start | bytes 884744 | tf_op jit(solution)/shard_map/ppermute | solution.py:396
  64.0 1.3 %collective-permute-start.12 = (bf16[1,64,2304]{2,1,0:T(8,128)(2,1)S(1)}, bf16[1,64,2304]{2,1,0:T(8,128)(2,1)S(1)}, u32[]{:S(2)}, u32[]{:S(2)}) collective-permute-start(bf16[1,64,2304]{2,1,0:T(8,128)(2,1)S(1)} %get-tuple-element.27), channel_id=1, source_target_pairs={{4,0},{8,12},{5,1},{9,13},{6,2},{10,14},{7,3},{11,15},{20,16},{24,... | collective-permute-start | bytes 884744 | tf_op jit(solution)/shard_map/ppermute | solution.py:396
  65.3 5.6 %collective-permute-start.6 = (bf16[2,64,2304]{2,1,0:T(8,128)(2,1)S(1)}, bf16[2,64,2304]{2,1,0:T(8,128)(2,1)S(1)}, u32[]{:S(2)}, u32[]{:S(2)}) collective-permute-start(bf16[2,64,2304]{2,1,0:T(8,128)(2,1)S(1)} %get-tuple-element.24), channel_id=1, source_target_pairs={{0,8},{12,4},{1,9},{13,5},{2,10},{14,6},{3,11},{15,7},{16,24},{28,... | collective-permute-start | bytes 1769480 | tf_op jit(solution)/shard_map/ppermute | solution.py:396
  71.0 3.3 %collective-permute-start.7 = (bf16[2,64,2304]{2,1,0:T(8,128)(2,1)S(1)}, bf16[2,64,2304]{2,1,0:T(8,128)(2,1)S(1)}, u32[]{:S(2)}, u32[]{:S(2)}) collective-permute-start(bf16[2,64,2304]{2,1,0:T(8,128)(2,1)S(1)} %get-tuple-element.25.rest_0_), channel_id=1, source_target_pairs={{0,12},{12,0},{1,13},{13,1},{2,14},{14,2},{3,15},{15,3},{16,28},{2... | collective-permute-start | bytes 1769480 | tf_op jit(solution)/shard_map/ppermute | solution.py:396
  74.2 0.3 collective-permute-done.11.refs_3_.refs_9_
  74.6 5.0 %collective-permute-done.12.refs_5_.refs_11_ = bf16[1,64,2304]{2,1,0:T(8,128)(2,1)S(1)} collective-permute-done((bf16[1,64,2304]{2,1,0:T(8,128)(2,1)S(1)}, bf16[1,64,2304]{2,1,0:T(8,128)(2,1)S(1)}, u32[]{:S(2)}, u32[]{:S(2)}) %collective-permute-start.12) | collective-permute-done | bytes 294944 | tf_op jit(solution)/shard_map/ppermute | solution.py:396
  79.5 0.0 copy-done
  79.5 0.0 copy-done.1
  79.5 0.0 copy-start.4
  79.5 2.7 %shard_map.78.refs_0_ = f32[6,64,128]{2,1,0:T(8,128)S(1)} custom-call(s32[28]{0:T(128)S(1)} %get-tuple-element.17.plan_ref, bf16[8,128,2048]{2,1,0:T(8,128)(2,1)S(1)} %bitcast.4, bf16[4,64,2048]{2,1,0:T(8,128)(2,1)S(1)} %bitcast.12, bf16[2,64,2304]{2,1,0:T(8,128)(2,1)S(1)} %collective-permute-done.8.rest_1_.refs_1_.refs_7_, ...), custom_call_target="tpu_custom_call" | custom-call | tf_op jit(solution)/shard_map/pallas_call | solution.py:320
  82.3 0.1 collective-permute-start.13
  82.4 1.6 %collective-permute-start.14 = (f32[6,64,128]{2,1,0:T(8,128)S(1)}, f32[6,64,128]{2,1,0:T(8,128)S(1)}, u32[]{:S(2)}, u32[]{:S(2)}) collective-permute-start(f32[6,64,128]{2,1,0:T(8,128)S(1)} %shard_map.78.refs_0_), channel_id=1, source_target_pairs={{0,2},{1,3},{2,0},{3,1},{4,6},{5,7},{6,4},{7,5},{8,10},{9,11},{10,... | collective-permute-start | bytes 589832 | tf_op jit(solution)/shard_map/ppermute | solution.py:25
  83.9 0.0 collective-permute-done.13.refs_1_
  83.9 1.1 %collective-permute-start.15 = (f32[6,64,128]{2,1,0:T(8,128)S(1)}, f32[6,64,128]{2,1,0:T(8,128)S(1)}, u32[]{:S(2)}, u32[]{:S(2)}) collective-permute-start(f32[6,64,128]{2,1,0:T(8,128)S(1)} %shard_map.78.refs_0_), channel_id=1, source_target_pairs={{0,3},{1,2},{2,1},{3,0},{4,7},{5,6},{6,5},{7,4},{8,11},{9,10},{10,... | collective-permute-start | bytes 589832 | tf_op jit(solution)/shard_map/ppermute | solution.py:25
  85.0 5.1 %collective-permute-done.14.refs_2_ = f32[6,64,128]{2,1,0:T(8,128)S(1)} collective-permute-done((f32[6,64,128]{2,1,0:T(8,128)S(1)}, f32[6,64,128]{2,1,0:T(8,128)S(1)}, u32[]{:S(2)}, u32[]{:S(2)}) %collective-permute-start.14) | collective-permute-done | bytes 196640 | tf_op jit(solution)/shard_map/ppermute | solution.py:25
  90.1 3.3 %collective-permute-done.15.refs_3_ = f32[6,64,128]{2,1,0:T(8,128)S(1)} collective-permute-done((f32[6,64,128]{2,1,0:T(8,128)S(1)}, f32[6,64,128]{2,1,0:T(8,128)S(1)}, u32[]{:S(2)}, u32[]{:S(2)}) %collective-permute-start.15) | collective-permute-done | bytes 196640 | tf_op jit(solution)/shard_map/ppermute | solution.py:25
  93.5 0.0 collective-permute-done.16
  93.5 0.0 copy-done.4
  93.5 3.5 %shard_map.79.refs_2_.refs_8_ = bf16[1024,256]{1,0:T(8,128)(2,1)} custom-call(s32[28]{0:T(128)S(1)} %get-tuple-element.17.plan_ref, f32[6,64,128]{2,1,0:T(8,128)S(1)} %shard_map.78.refs_0_, f32[6,64,128]{2,1,0:T(8,128)S(1)} %collective-permute-done.13.refs_1_, f32[6,64,128]{2,1,0:T(8,128)S(1)} %collective-permute-done.14.refs_2_, ...), custom_call_target="tpu_custom_call" | custom-call | tf_op jit(solution)/shard_map/pallas_call | solution.py:377
  97.0 0.0 collective-permute-done.6.refs_0_.refs_6_
  97.0 0.5 collective-permute-done.7.refs_1_.refs_7_
  97.5 0.0 copy-start.2
  97.5 1.0 copy-done.2
  98.5 1.3 %shard_map.80.refs_0_ = f32[2,64,128]{2,1,0:T(8,128)S(1)} custom-call(s32[28]{0:T(128)S(1)} %get-tuple-element.17.plan_ref, bf16[8,128,2048]{2,1,0:T(8,128)(2,1)S(1)} %bitcast.5, bf16[2,64,2304]{2,1,0:T(8,128)(2,1)S(1)} %collective-permute-done.6.refs_0_.refs_6_, bf16[2,64,2304]{2,1,0:T(8,128)(2,1)S(1)} %collective-permute-done.7.refs_1_.refs_7_, ...), custom_call_target="tpu_custom_call" | custom-call | tf_op jit(solution)/shard_map/pallas_call | solution.py:320
  99.9 0.1 collective-permute-start.17
  100.0 1.5 %collective-permute-start.18 = (f32[2,64,128]{2,1,0:T(8,128)S(1)}, f32[2,64,128]{2,1,0:T(8,128)S(1)}, u32[]{:S(2)}, u32[]{:S(2)}) collective-permute-start(f32[2,64,128]{2,1,0:T(8,128)S(1)} %shard_map.80.refs_0_), channel_id=1, source_target_pairs={{0,2},{1,3},{2,0},{3,1},{4,6},{5,7},{6,4},{7,5},{8,10},{9,11},{10,... | collective-permute-start | bytes 196616 | tf_op jit(solution)/shard_map/ppermute | solution.py:25
  101.5 0.3 collective-permute-start.19
  101.8 0.0 collective-permute-done.17.refs_1_
  101.8 2.6 %collective-permute-done.18.refs_2_ = f32[2,64,128]{2,1,0:T(8,128)S(1)} collective-permute-done((f32[2,64,128]{2,1,0:T(8,128)S(1)}, f32[2,64,128]{2,1,0:T(8,128)S(1)}, u32[]{:S(2)}, u32[]{:S(2)}) %collective-permute-start.18) | collective-permute-done | bytes 65568 | tf_op jit(solution)/shard_map/ppermute | solution.py:25
  104.4 1.1 %collective-permute-done.19.refs_3_ = f32[2,64,128]{2,1,0:T(8,128)S(1)} collective-permute-done((f32[2,64,128]{2,1,0:T(8,128)S(1)}, f32[2,64,128]{2,1,0:T(8,128)S(1)}, u32[]{:S(2)}, u32[]{:S(2)}) %collective-permute-start.19) | collective-permute-done | bytes 65568 | tf_op jit(solution)/shard_map/ppermute | solution.py:25
  105.5 1.7 %shard_map.81 = bf16[1024,256]{1,0:T(8,128)(2,1)} custom-call(s32[28]{0:T(128)S(1)} %get-tuple-element.17.plan_ref, f32[2,64,128]{2,1,0:T(8,128)S(1)} %shard_map.80.refs_0_, f32[2,64,128]{2,1,0:T(8,128)S(1)} %collective-permute-done.17.refs_1_, f32[2,64,128]{2,1,0:T(8,128)S(1)} %collective-permute-done.18.refs_2_, ...), custom_call_target="tpu_custom_call", output_to_operand_aliasing={{}: (9, {})} | custom-call | tf_op jit(solution)/shard_map/pallas_call | solution.py:377
Async XLA Ops:
  0.0 61.8 %collective-permute-start.9 = (bf16[4,64,2048]{2,1,0:T(8,128)(2,1)}, bf16[4,64,2048]{2,1,0:T(8,128)(2,1)S(1)}, u32[]{:S(2)}, u32[]{:S(2)}) collective-permute-start(bf16[4,64,2048]{2,1,0:T(8,128)(2,1)} %bitcast.9), channel_id=1, source_target_pairs={{4,8},{8,4},{5,9},{9,5},{6,10},{10,6},{7,11},{11,7},{20,24},{24,20... | collective-permute-start | bytes 3145736 | tf_op jit(solution)/shard_map/ppermute | solution.py:396
  0.7 8.3 %collective-permute-start = (s32[1,8]{1,0:T(1,128)}, s32[1,8]{1,0:T(1,128)S(1)}, u32[]{:S(2)}, u32[]{:S(2)}) collective-permute-start(s32[1,8]{1,0:T(1,128)} %refs_0_.1), channel_id=1, source_target_pairs={{0,4},{4,0},{8,12},{12,8},{1,5},{5,1},{9,13},{13,9},{2,6},{6,2},{1... | collective-permute-start | bytes 104 | tf_op jit(solution)/shard_map/ppermute | solution.py:25
  6.6 22.9 %collective-permute-start.1 = (s32[1,8]{1,0:T(1,128)}, s32[1,8]{1,0:T(1,128)S(1)}, u32[]{:S(2)}, u32[]{:S(2)}) collective-permute-start(s32[1,8]{1,0:T(1,128)} %refs_0_.1), channel_id=1, source_target_pairs={{0,8},{4,12},{8,0},{12,4},{1,9},{5,13},{9,1},{13,5},{2,10},{6,14},... | collective-permute-start | bytes 104 | tf_op jit(solution)/shard_map/ppermute | solution.py:25
  6.6 22.9 %collective-permute-start.2 = (s32[1,8]{1,0:T(1,128)}, s32[1,8]{1,0:T(1,128)S(1)}, u32[]{:S(2)}, u32[]{:S(2)}) collective-permute-start(s32[1,8]{1,0:T(1,128)} %refs_0_.1), channel_id=1, source_target_pairs={{0,12},{4,8},{8,4},{12,0},{1,13},{5,9},{9,5},{13,1},{2,14},{6,10},... | collective-permute-start | bytes 104 | tf_op jit(solution)/shard_map/ppermute | solution.py:25
  32.2 17.5 %copy-start.3 = (bf16[4,64,256]{2,1,0:T(8,128)(2,1)S(1)}, bf16[4,64,256]{2,1,0:T(8,128)(2,1)}, u32[]{:S(2)}) copy-start(bf16[4,64,256]{2,1,0:T(8,128)(2,1)} %refs_6_.1) | copy-start | bytes 393220
  45.5 4.9 %collective-permute-start.3 = (f32[2,384,256]{2,1,0:T(8,128)S(1)}, f32[2,384,256]{2,1,0:T(8,128)S(1)}, u32[]{:S(2)}, u32[]{:S(2)}) collective-permute-start(f32[2,384,256]{2,1,0:T(8,128)S(1)} %get-tuple-element.20), channel_id=1, source_target_pairs={{0,1},{1,0},{2,3},{3,2},{4,5},{5,4},{6,7},{7,6},{8,9},{9,8},{10,11... | collective-permute-start | bytes 2359304 | tf_op jit(solution)/shard_map/ppermute | solution.py:25
  45.6 4.8 %collective-permute-start.4 = (f32[2,384,256]{2,1,0:T(8,128)S(1)}, f32[2,384,256]{2,1,0:T(8,128)S(1)}, u32[]{:S(2)}, u32[]{:S(2)}) collective-permute-start(f32[2,384,256]{2,1,0:T(8,128)S(1)} %get-tuple-element.21), channel_id=1, source_target_pairs={{0,1},{1,0},{2,3},{3,2},{4,5},{5,4},{6,7},{7,6},{8,9},{9,8},{10,11... | collective-permute-start | bytes 2359304 | tf_op jit(solution)/shard_map/ppermute | solution.py:25
  46.1 3.6 %collective-permute-start.5 = (f32[2,256,256]{2,1,0:T(8,128)S(1)}, f32[2,256,256]{2,1,0:T(8,128)S(1)}, u32[]{:S(2)}, u32[]{:S(2)}) collective-permute-start(f32[2,256,256]{2,1,0:T(8,128)S(1)} %get-tuple-element.22), channel_id=1, source_target_pairs={{0,1},{1,0},{2,3},{3,2},{4,5},{5,4},{6,7},{7,6},{8,9},{9,8},{10,11... | collective-permute-start | bytes 1572872 | tf_op jit(solution)/shard_map/ppermute | solution.py:25
  46.1 15.7 %collective-permute-start.8 = (bf16[2,64,2304]{2,1,0:T(8,128)(2,1)S(1)}, bf16[2,64,2304]{2,1,0:T(8,128)(2,1)S(1)}, u32[]{:S(2)}, u32[]{:S(2)}) collective-permute-start(bf16[2,64,2304]{2,1,0:T(8,128)(2,1)S(1)} %get-tuple-element.18.refs_0_), channel_id=1, source_target_pairs={{0,4},{4,0},{8,12},{12,8},{1,5},{5,1},{9,13},{13,9},{2,6},{6,2},{1... | collective-permute-start | bytes 1769480 | tf_op jit(solution)/shard_map/ppermute | solution.py:396
  49.7 4.4 %collective-permute-start.10 = (bf16[4,64,256]{2,1,0:T(8,128)(2,1)S(1)}, bf16[4,64,256]{2,1,0:T(8,128)(2,1)S(1)}, u32[]{:S(2)}, u32[]{:S(2)}) collective-permute-start(bf16[4,64,256]{2,1,0:T(8,128)(2,1)S(1)} %copy-done.3), channel_id=1, source_target_pairs={{4,8},{8,4},{5,9},{9,5},{6,10},{10,6},{7,11},{11,7},{20,24},{24,20... | collective-permute-start | bytes 393224 | tf_op jit(solution)/shard_map/ppermute | solution.py:396
  50.7 42.8 %collective-permute-start.16 = (f32[1,1024,256]{2,1,0:T(8,128)S(1)}, f32[1,1024,256]{2,1,0:T(8,128)S(1)}, u32[]{:S(2)}, u32[]{:S(2)}) collective-permute-start(f32[1,1024,256]{2,1,0:T(8,128)S(1)} %get-tuple-element.28), channel_id=1, source_target_pairs={{0,2},{1,3},{2,0},{3,1},{4,6},{5,7},{6,4},{7,5},{8,10},{9,11},{10,... | collective-permute-start | bytes 3145736 | tf_op jit(solution)/shard_map/ppermute | solution.py:25
  61.8 17.7 %copy-start = (bf16[1024,2048]{1,0:T(8,128)(2,1)S(1)}, bf16[1024,2048]{1,0:T(8,128)(2,1)}, u32[]{:S(2)}) copy-start(bf16[1024,2048]{1,0:T(8,128)(2,1)} %tokens_ref.1) | copy-start | bytes 12582916
  61.8 17.7 %copy-start.1 = (bf16[4,2048,64]{1,2,0:T(8,128)(2,1)S(1)}, bf16[4,2048,64]{1,2,0:T(8,128)(2,1)}, u32[]{:S(2)}) copy-start(bf16[4,2048,64]{1,2,0:T(8,128)(2,1)} %param.9) | copy-start | bytes 3145732
  62.5 12.1 %collective-permute-start.11 = (bf16[1,64,2304]{2,1,0:T(8,128)(2,1)S(1)}, bf16[1,64,2304]{2,1,0:T(8,128)(2,1)S(1)}, u32[]{:S(2)}, u32[]{:S(2)}) collective-permute-start(bf16[1,64,2304]{2,1,0:T(8,128)(2,1)S(1)} %get-tuple-element.26), channel_id=1, source_target_pairs={{4,0},{8,12},{5,1},{9,13},{6,2},{10,14},{7,3},{11,15},{20,16},{24,... | collective-permute-start | bytes 884744 | tf_op jit(solution)/shard_map/ppermute | solution.py:396
  64.0 15.5 %collective-permute-start.12 = (bf16[1,64,2304]{2,1,0:T(8,128)(2,1)S(1)}, bf16[1,64,2304]{2,1,0:T(8,128)(2,1)S(1)}, u32[]{:S(2)}, u32[]{:S(2)}) collective-permute-start(bf16[1,64,2304]{2,1,0:T(8,128)(2,1)S(1)} %get-tuple-element.27), channel_id=1, source_target_pairs={{4,0},{8,12},{5,1},{9,13},{6,2},{10,14},{7,3},{11,15},{20,16},{24,... | collective-permute-start | bytes 884744 | tf_op jit(solution)/shard_map/ppermute | solution.py:396
  65.3 31.6 %collective-permute-start.6 = (bf16[2,64,2304]{2,1,0:T(8,128)(2,1)S(1)}, bf16[2,64,2304]{2,1,0:T(8,128)(2,1)S(1)}, u32[]{:S(2)}, u32[]{:S(2)}) collective-permute-start(bf16[2,64,2304]{2,1,0:T(8,128)(2,1)S(1)} %get-tuple-element.24), channel_id=1, source_target_pairs={{0,8},{12,4},{1,9},{13,5},{2,10},{14,6},{3,11},{15,7},{16,24},{28,... | collective-permute-start | bytes 1769480 | tf_op jit(solution)/shard_map/ppermute | solution.py:396
  71.0 26.5 %collective-permute-start.7 = (bf16[2,64,2304]{2,1,0:T(8,128)(2,1)S(1)}, bf16[2,64,2304]{2,1,0:T(8,128)(2,1)S(1)}, u32[]{:S(2)}, u32[]{:S(2)}) collective-permute-start(bf16[2,64,2304]{2,1,0:T(8,128)(2,1)S(1)} %get-tuple-element.25.rest_0_), channel_id=1, source_target_pairs={{0,12},{12,0},{1,13},{13,1},{2,14},{14,2},{3,15},{15,3},{16,28},{2... | collective-permute-start | bytes 1769480 | tf_op jit(solution)/shard_map/ppermute | solution.py:396
  79.5 13.9 %copy-start.4 = (bf16[4,64,256]{2,1,0:T(8,128)(2,1)S(1)}, bf16[4,64,256]{2,1,0:T(8,128)(2,1)}, u32[]{:S(2)}) copy-start(bf16[4,64,256]{2,1,0:T(8,128)(2,1)} %refs_6_.1) | copy-start | bytes 393220
  82.3 1.6 %collective-permute-start.13 = (f32[6,64,128]{2,1,0:T(8,128)S(1)}, f32[6,64,128]{2,1,0:T(8,128)S(1)}, u32[]{:S(2)}, u32[]{:S(2)}) collective-permute-start(f32[6,64,128]{2,1,0:T(8,128)S(1)} %shard_map.78.refs_0_), channel_id=1, source_target_pairs={{0,1},{1,0},{2,3},{3,2},{4,5},{5,4},{6,7},{7,6},{8,9},{9,8},{10,11... | collective-permute-start | bytes 589832 | tf_op jit(solution)/shard_map/ppermute | solution.py:25
  82.4 7.8 %collective-permute-start.14 = (f32[6,64,128]{2,1,0:T(8,128)S(1)}, f32[6,64,128]{2,1,0:T(8,128)S(1)}, u32[]{:S(2)}, u32[]{:S(2)}) collective-permute-start(f32[6,64,128]{2,1,0:T(8,128)S(1)} %shard_map.78.refs_0_), channel_id=1, source_target_pairs={{0,2},{1,3},{2,0},{3,1},{4,6},{5,7},{6,4},{7,5},{8,10},{9,11},{10,... | collective-permute-start | bytes 589832 | tf_op jit(solution)/shard_map/ppermute | solution.py:25
  83.9 9.5 %collective-permute-start.15 = (f32[6,64,128]{2,1,0:T(8,128)S(1)}, f32[6,64,128]{2,1,0:T(8,128)S(1)}, u32[]{:S(2)}, u32[]{:S(2)}) collective-permute-start(f32[6,64,128]{2,1,0:T(8,128)S(1)} %shard_map.78.refs_0_), channel_id=1, source_target_pairs={{0,3},{1,2},{2,1},{3,0},{4,7},{5,6},{6,5},{7,4},{8,11},{9,10},{10,... | collective-permute-start | bytes 589832 | tf_op jit(solution)/shard_map/ppermute | solution.py:25
  97.5 1.0 copy-start.2
  99.9 1.9 %collective-permute-start.17 = (f32[2,64,128]{2,1,0:T(8,128)S(1)}, f32[2,64,128]{2,1,0:T(8,128)S(1)}, u32[]{:S(2)}, u32[]{:S(2)}) collective-permute-start(f32[2,64,128]{2,1,0:T(8,128)S(1)} %shard_map.80.refs_0_), channel_id=1, source_target_pairs={{0,1},{1,0},{2,3},{3,2},{4,5},{5,4},{6,7},{7,6},{8,9},{9,8},{10,11... | collective-permute-start | bytes 196616 | tf_op jit(solution)/shard_map/ppermute | solution.py:25
  100.0 4.5 %collective-permute-start.18 = (f32[2,64,128]{2,1,0:T(8,128)S(1)}, f32[2,64,128]{2,1,0:T(8,128)S(1)}, u32[]{:S(2)}, u32[]{:S(2)}) collective-permute-start(f32[2,64,128]{2,1,0:T(8,128)S(1)} %shard_map.80.refs_0_), channel_id=1, source_target_pairs={{0,2},{1,3},{2,0},{3,1},{4,6},{5,7},{6,4},{7,5},{8,10},{9,11},{10,... | collective-permute-start | bytes 196616 | tf_op jit(solution)/shard_map/ppermute | solution.py:25
  101.5 4.0 %collective-permute-start.19 = (f32[2,64,128]{2,1,0:T(8,128)S(1)}, f32[2,64,128]{2,1,0:T(8,128)S(1)}, u32[]{:S(2)}, u32[]{:S(2)}) collective-permute-start(f32[2,64,128]{2,1,0:T(8,128)S(1)} %shard_map.80.refs_0_), channel_id=1, source_target_pairs={{0,3},{1,2},{2,1},{3,0},{4,7},{5,6},{6,5},{7,4},{8,11},{9,10},{10,... | collective-permute-start | bytes 196616 | tf_op jit(solution)/shard_map/ppermute | solution.py:25

commit v4 on v3

--- a/solution.py
+++ b/solution.py
@@ -8,10 +8,11 @@
 from jax.sharding import PartitionSpec as P
 
 ADAPTER_SCALE = 0.5
-ROW_TILE = 128
-PARAMS = pltpu.CompilerParams(vmem_limit_bytes=20 * 1024 * 1024)
+ROW_TILE = 256
+PARAMS = pltpu.CompilerParams(vmem_limit_bytes=16 * 1024 * 1024)
 NO_COST = pl.CostEstimate(flops=0, bytes_accessed=0, transcendentals=0)
-LONG = pl.CostEstimate(flops=4 * 10**10, bytes_accessed=0, transcendentals=0)
+SHORT = pl.CostEstimate(flops=4 * 10**9, bytes_accessed=0, transcendentals=0)
+LONG = pl.CostEstimate(flops=6 * 10**9, bytes_accessed=0, transcendentals=0)
 ANY = pl.BlockSpec(memory_space=pl.ANY)
 SMEM = pl.BlockSpec(memory_space=pltpu.SMEM)
 
@@ -26,57 +27,55 @@
 
 
 def piece_rows(rows):
-    tile = min(ROW_TILE, rows)
-    tiles = rows // tile
-    counts = [(tiles + 2 - i) // 3 for i in range(3)]
-    return [count * tile for count in counts if count]
+    large = rows * 7 // 16
+    return [large, large, rows - 2 * large]
 
 
 def base_kernel(order, tokens_ref, weight_ref, *refs):
     kept_ref = refs[-1]
-    half, rows, width = kept_ref.shape
-    sizes = piece_rows(rows)
+    half, tile, width = kept_ref.shape
+    sizes = piece_rows(tile * pl.num_programs(0))
     sent_refs = refs[-1 - len(sizes) : -1]
     place = lax.axis_index("tensor")
-    step = pl.program_id(0)
-    columns = place ^ jnp.where(step < half, order[0], order[half])
-    for number in range(1, half):
-        columns = jnp.where(step == number, place ^ order[number], columns)
-        columns = jnp.where(step == half + number, place ^ order[half + number], columns)
-    columns = pl.ds(pl.multiple_of(columns * width, width), width)
-    start = 0
-    for sent_ref, size in zip(sent_refs, sizes):
+    for number, offset in enumerate(order):
+        columns = pl.ds(pl.multiple_of((place ^ offset) * width, width), width)
         part = jnp.dot(
-            tokens_ref[start : start + size, :],
-            weight_ref[:, columns],
-            preferred_element_type=jnp.float32,
+            tokens_ref[...], weight_ref[:, columns], preferred_element_type=jnp.float32
         )
-
-        @pl.when(step < half)
-        def _(sent_ref=sent_ref, part=part):
-            sent_ref[jnp.minimum(step, half - 1)] = part
-
-        @pl.when(step >= half)
-        def _(start=start, size=size, part=part):
-            kept_ref[jnp.maximum(step - half, 0), start : start + size, :] = part
-
-        start += size
+        if number >= half:
+            kept_ref[number - half] = part
+            continue
+        for step in range(pl.num_programs(0)):
+
+            @pl.when(pl.program_id(0) == step)
+            def _(number=number, part=part, first=step * tile):
+                start = 0
+                for sent_ref, size in zip(sent_refs, sizes):
+                    low, high = max(first, start), min(first + tile, start + size)
+                    if low < high:
+                        rows = slice(low - start, high - start)
+                        sent_ref[number, rows, :] = part[low - first : high - first]
+                    start += size
 
 
 def base_chunks(tokens, weight, order, width, after):
     rows, depth = tokens.shape
+    tile = min(ROW_TILE, rows)
     half = len(order) // 2
-    shapes = [(half, size, width) for size in piece_rows(rows)] + [(half, rows, width)]
+    pieces = [(half, size, width) for size in piece_rows(rows)]
     *sent, kept = pl.pallas_call(
         functools.partial(base_kernel, order),
-        grid=(len(order),),
+        grid=(rows // tile,),
         in_specs=[
-            pl.BlockSpec(tokens.shape, lambda i: (0, 0), pipeline_mode=pl.Buffered(1)),
+            pl.BlockSpec((tile, depth), lambda i: (i, 0)),
             pl.BlockSpec(weight.shape, lambda i: (0, 0), pipeline_mode=pl.Buffered(1)),
         ]
         + [ANY] * len(after),
-        out_specs=[pl.BlockSpec(shape, lambda i: (0, 0, 0)) for shape in shapes],
-        out_shape=[jax.ShapeDtypeStruct(shape, jnp.float32) for shape in shapes],
+        out_specs=[pl.BlockSpec(shape, lambda i: (0, 0, 0)) for shape in pieces]
+        + [pl.BlockSpec((half, tile, width), lambda i: (0, i, 0))],
+        out_shape=[
+            jax.ShapeDtypeStruct(shape, jnp.float32) for shape in [*pieces, (half, rows, width)]
+        ],
         compiler_params=PARAMS,
         cost_estimate=NO_COST,
     )(in_hbm(tokens), in_hbm(weight), *after)
@@ -211,7 +210,7 @@
         + [pltpu.SMEM(table.shape, jnp.int32), pltpu.SMEM(live.shape, jnp.int32)]
         + [pltpu.SemaphoreType.DMA((6,)), pltpu.SemaphoreType.DMA((capacity, 2))],
         compiler_params=PARAMS,
-        cost_estimate=NO_COST,
+        cost_estimate=SHORT,
     )(in_hbm(names), *others, *[in_hbm(a) for a in (table, live, down, up)])
 
 
@@ -304,7 +303,7 @@
             token_ref[0],
             (((1,), (1,)), ((), ())),
             preferred_element_type=jnp.float32,
-        )
+        ).astype(out_ref.dtype)
 
     for_phase(phases, choose, plan_ref, refs, act)
 
@@ -327,7 +326,7 @@
             + [ANY] * len(after),
             out_specs=pl.BlockSpec((1, rank, rows), lambda i, plan: (i, 0, 0)),
         ),
-        out_shape=jax.ShapeDtypeStruct((total, rank, rows), jnp.float32),
+        out_shape=jax.ShapeDtypeStruct((total, rank, rows), jnp.bfloat16),
         compiler_params=PARAMS,
         cost_estimate=NO_COST,
     )(plan, row_blocks, *operands, *after)
@@ -341,9 +340,9 @@
     parts = refs[:part_count]
     mine_ref, far_ref = refs[part_count : part_count + 2]
     out_ref = refs[-1]
-    total = parts[0][0]
+    total = parts[0][0].astype(jnp.float32)
     for part in parts[1:]:
-        total = total + part[0]
+        total = total + part[0].astype(jnp.float32)
     shrunk = total.astype(jnp.bfloat16)
     live = plan_ref[live_row + pl.program_id(0)]
 
@@ -382,7 +381,7 @@
             in_specs=specs,
             out_specs=pl.BlockSpec((block_rows, width), lambda i, plan: (block(i, plan), 0)),
         ),
-        out_shape=jax.ShapeDtypeStruct((rows, width), jnp.bfloat16),
+        out_shape=pltpu.HBM((rows, width), jnp.bfloat16),
         input_output_aliases=aliases,
         compiler_params=PARAMS,
         cost_estimate=NO_COST,
@@ -423,33 +422,37 @@
     forwarded = [across(panel, [(1, 0), (2, 3)]) for panel in forward_out]
 
     choose = INNER * capacity
-    first = [
-        (0, capacity, [(down, OWN * capacity)]),
-        (capacity, capacity, [(near, None)]),
-        *[
-            (2 * capacity + k, 1, [(inner_down, EARLY * capacity + k), (forwarded[k], None)])
+
+    def phases_of(down_panels, up_panels, place):
+        early = [
+            (
+                2 * capacity + k,
+                1,
+                [(place, EARLY * capacity + k), (forwarded[k], None)],
+            )
             for k in range(capacity)
-        ],
-    ]
+        ]
+        return [
+            (0, capacity, [(down_panels, OWN * capacity)]),
+            (capacity, capacity, [(near, None)]),
+        ], early
+
+    first, early = phases_of(down, None, inner_down)
+    first_up, early_up = phases_of(up, None, inner_up)
     last = [(3 * capacity, capacity, [(to_inner, None), (to_outer, None)])]
-    first_up = [
-        (0, capacity, [(up, OWN * capacity)]),
-        (capacity, capacity, [(near, None)]),
-        *[
-            (2 * capacity + k, 1, [(inner_up, EARLY * capacity + k), (forwarded[k], None)])
-            for k in range(capacity)
-        ],
-    ]
-    first_columns = [[0], [up_column]] + [[0, up_column]] * capacity
-    first_parts = exchange(shrink(plan, row_blocks, first, choose))
+
+    first_parts = exchange(shrink(plan, row_blocks, first, choose, [outer_out]))
+    columns = [[0], [up_column]]
+    out = combine(plan, LIVE * capacity, first_parts, base, first_up, columns, choose)
+    early_part = shrink(plan, row_blocks, early, choose)
+    early_parts = exchange(early_part)
+    last_parts = exchange(shrink(plan, row_blocks, last, choose, [out, early_part]))
+    columns = [[0, up_column]] * capacity
     out = combine(
-        plan, LIVE * capacity, first_parts, base, first_up, first_columns, choose
+        plan, (LIVE + 2) * capacity, early_parts, base, early_up, columns, choose, out
     )
-    last_parts = exchange(shrink(plan, row_blocks, last, choose, [out]))
-    last_columns = [[up_column] * 2]
-    return combine(
-        plan, (LIVE + 3) * capacity, last_parts, base, last, last_columns, choose, out
-    )
+    columns = [[up_column] * 2]
+    return combine(plan, (LIVE + 3) * capacity, last_parts, base, last, columns, choose, out)
 
 
 def on_any_pool(tokens, weight, row_blocks, down, up, names, table, live, capacity):

time: 108 us -> 95 us (0.88)
  waiting for transfers between devices: 49.1 us -> 39.7 us
  starting transfers between devices: 28.9 us -> 26.4 us
    ppermute x13 -> x16, waiting for transfers between devices: 35.5 us -> 11.3 us  [swap(): return lax.ppermute(value, axis, pairs)]
    ppermute x7, waiting for transfers between devices: 13.6 us -> 28.5 us  [across(): return lax.ppermute(value, 'pool', pairs)]
    ppermute x7, starting transfers between devices: 13.7 us -> 10.8 us  [across(): return lax.ppermute(value, 'pool', pairs)]
    pallas_call x1, Pallas kernels: 13.3 us -> 11.4 us  [base_chunks(): pl.pallas_call(functools.partial(base_kernel, order), grid=(rows // tile,...]
    pallas_call x2 -> x3, Pallas kernels: 5.21 us -> 5.98 us  [combine(): pl.pallas_call(functools.partial(combine_kernel, shapes, choose, len(part...]
    pallas_call x2 -> x3, Pallas kernels: 4.05 us -> 4.5 us  [shrink(): pl.pallas_call(functools.partial(shrink_kernel, shapes, choose), grid_spe...]
    ppermute x13 -> x16, starting transfers between devices: 15.2 us -> 15.6 us  [swap(): return lax.ppermute(value, axis, pairs)]
  transfers between devices with their start and end apart: 20 -> 23, of which waited for: 10 -> 9; matrix products, arithmetic and copies ran while one was open for 0% -> 0% of each run, Pallas kernels for 23% -> 27%
where the time goes in v4:
time: 95 us; the launch traced here: 94.7 us
  waiting for transfers between devices  39.7 us (42%)
  Pallas kernels  27.3 us (29%)
  starting transfers between devices  26.4 us (28%)
  local copies, waits for them, and re-layouts  1.07 us (1%)
    ppermute x7, waiting for transfers between devices, across(): return lax.ppermute(value, 'pool', pairs)  28.5 us
    ppermute x16, starting transfers between devices, swap(): return lax.ppermute(value, axis, pairs)  15.6 us
    pallas_call x1, Pallas kernels, base_chunks(): pl.pallas_call(functools.partial(base_kernel, order), grid=(rows // tile,...  11.4 us
    ppermute x16, waiting for transfers between devices, swap(): return lax.ppermute(value, axis, pairs)  11.3 us
    ppermute x7, starting transfers between devices, across(): return lax.ppermute(value, 'pool', pairs)  10.8 us
    pallas_call x3, Pallas kernels, combine(): pl.pallas_call(functools.partial(combine_kernel, shapes, choose, len(part...  5.98 us
    pallas_call x3, Pallas kernels, shrink(): pl.pallas_call(functools.partial(shrink_kernel, shapes, choose), grid_spe...  4.5 us
    pallas_call x1, Pallas kernels, make_plan(): pl.pallas_call(functools.partial(plan_kernel, capacity), in_specs=[ANY] *...  2.7 us
  transfers between devices with their start and end apart: 23, of which 9 were waited for; matrix products, arithmetic and copies ran while one was open for 0% of the time, Pallas kernels for 27%

profile of v4, /device:TPU:0, one launch (start us, length us, event | category | flops | bytes accessed | tf_op | source)
XLA Modules:
  0.0 94.7 jit_solution(6556231416096027477)
XLA Ops:
  0.0 3.0 %collective-permute-start = (s32[1,8]{1,0:T(1,128)}, s32[1,8]{1,0:T(1,128)S(1)}, u32[]{:S(2)}, u32[]{:S(2)}) collective-permute-start(s32[1,8]{1,0:T(1,128)} %refs_0_.1), channel_id=1, source_target_pairs={{0,4},{4,0},{8,12},{12,8},{1,5},{5,1},{9,13},{13,9},{2,6},{6,2},{1... | collective-permute-start | bytes 104 | tf_op jit(solution)/shard_map/ppermute | solution.py:26
  3.0 2.6 %collective-permute-start.1 = (s32[1,8]{1,0:T(1,128)}, s32[1,8]{1,0:T(1,128)S(1)}, u32[]{:S(2)}, u32[]{:S(2)}) collective-permute-start(s32[1,8]{1,0:T(1,128)} %refs_0_.1), channel_id=1, source_target_pairs={{0,8},{4,12},{8,0},{12,4},{1,9},{5,13},{9,1},{13,5},{2,10},{6,14},... | collective-permute-start | bytes 104 | tf_op jit(solution)/shard_map/ppermute | solution.py:26
  5.6 0.0 collective-permute-start.2
  5.6 0.7 collective-permute-start.13
  6.3 0.0 collective-permute-done.refs_1_
  6.4 1.2 %collective-permute-done.1.refs_2_ = s32[1,8]{1,0:T(1,128)S(1)} collective-permute-done((s32[1,8]{1,0:T(1,128)}, s32[1,8]{1,0:T(1,128)S(1)}, u32[]{:S(2)}, u32[]{:S(2)}) %collective-permute-start.1) | collective-permute-done | bytes 64 | tf_op jit(solution)/shard_map/ppermute | solution.py:26
  7.6 3.5 %collective-permute-done.2.refs_3_ = s32[1,8]{1,0:T(1,128)S(1)} collective-permute-done((s32[1,8]{1,0:T(1,128)}, s32[1,8]{1,0:T(1,128)S(1)}, u32[]{:S(2)}, u32[]{:S(2)}) %collective-permute-start.2) | collective-permute-done | bytes 64 | tf_op jit(solution)/shard_map/ppermute | solution.py:26
  11.1 2.7 %shard_map.73 = (bf16[2,64,2304]{2,1,0:T(8,128)(2,1)S(1)}, s32[28]{0:T(128)S(1)}) custom-call(s32[1,8]{1,0:T(1,128)} %refs_0_.1, s32[1,8]{1,0:T(1,128)S(1)} %collective-permute-done.refs_1_, s32[1,8]{1,0:T(1,128)S(1)} %collective-permute-done.1.refs_2_, s32[1,8]{1,0:T(1,128)S(1)} %collective-permute-done.2.refs_3_, s32[16]{0:T(128)} %refs_4_.1, ...), custom_call_target="tpu_custom_call" | custom-call | flops 4000000000 | tf_op jit(solution)/shard_map/pallas_call | solution.py:201
  13.8 0.0 copy-start.3
  13.8 11.4 %shard_map.74 = (f32[2,448,256]{2,1,0:T(8,128)S(1)}, f32[2,448,256]{2,1,0:T(8,128)S(1)}, f32[2,128,256]{2,1,0:T(8,128)S(1)}, f32[2,1024,256]{2,1,0:T(8,128)S(1)}) custom-call(bf16[1024,2048]{1,0:T(8,128)(2,1)} %tokens_ref.1, bf16[2048,1024]{1,0:T(8,128)(2,1)} %weight_ref.1, bf16[2,64,2304]{2,1,0:T(8,128)(2,1)S(1)} %get-tuple-element.18.refs_0_), custom_call_target="tpu_custom_call" | custom-call | tf_op jit(solution)/shard_map/pallas_call | solution.py:66
  25.2 0.0 copy-start
  25.2 0.0 copy-start.2
  25.2 0.1 collective-permute-start.3
  25.3 0.5 collective-permute-start.4
  25.8 0.0 collective-permute-start.8
  25.8 0.1 collective-permute-start.5
  25.9 3.6 %collective-permute-done.5.refs_2_ = f32[2,128,256]{2,1,0:T(8,128)S(1)} collective-permute-done((f32[2,128,256]{2,1,0:T(8,128)S(1)}, f32[2,128,256]{2,1,0:T(8,128)S(1)}, u32[]{:S(2)}, u32[]{:S(2)}) %collective-permute-start.5) | collective-permute-done | bytes 262176 | tf_op jit(solution)/shard_map/ppermute | solution.py:26
  29.4 0.0 copy-done.3
  29.4 0.7 collective-permute-start.14
  30.1 0.0 collective-permute-done.3.refs_0_
  30.1 0.0 collective-permute-done.4.refs_1_
  30.1 0.2 shard_map.75
  30.3 1.6 %collective-permute-start.12 = (f32[1,1024,256]{2,1,0:T(8,128)S(1)}, f32[1,1024,256]{2,1,0:T(8,128)S(1)}, u32[]{:S(2)}, u32[]{:S(2)}) collective-permute-start(f32[1,1024,256]{2,1,0:T(8,128)S(1)} %get-tuple-element.26), channel_id=1, source_target_pairs={{0,2},{1,3},{2,0},{3,1},{4,6},{5,7},{6,4},{7,5},{8,10},{9,11},{10,... | collective-permute-start | bytes 3145736 | tf_op jit(solution)/shard_map/ppermute | solution.py:26
  31.9 1.9 %shard_map.76 = (bf16[2,64,2304]{2,1,0:T(8,128)(2,1)S(1)}, bf16[2,64,2304]{2,1,0:T(8,128)(2,1)S(1)}) custom-call(s32[28]{0:T(128)S(1)} %get-tuple-element.17.plan_ref, bf16[4,64,2048]{2,1,0:T(8,128)(2,1)} %bitcast.16, bf16[4,64,256]{2,1,0:T(8,128)(2,1)} %refs_6_.1, f32[1024,256]{1,0:T(8,128)S(1)} %bitcast.7), custom_call_target="tpu_custom_call" | custom-call | tf_op jit(solution)/shard_map/pallas_call | solution.py:236
  33.8 4.8 %collective-permute-start.6 = (bf16[2,64,2304]{2,1,0:T(8,128)(2,1)S(1)}, bf16[2,64,2304]{2,1,0:T(8,128)(2,1)S(1)}, u32[]{:S(2)}, u32[]{:S(2)}) collective-permute-start(bf16[2,64,2304]{2,1,0:T(8,128)(2,1)S(1)} %get-tuple-element.24), channel_id=1, source_target_pairs={{0,8},{12,4},{1,9},{13,5},{2,10},{14,6},{3,11},{15,7},{16,24},{28,... | collective-permute-start | bytes 1769480 | tf_op jit(solution)/shard_map/ppermute | solution.py:395
  38.6 2.5 %collective-permute-done.8.refs_1_.refs_7_.rest_1_ = bf16[2,64,2304]{2,1,0:T(8,128)(2,1)S(1)} collective-permute-done((bf16[2,64,2304]{2,1,0:T(8,128)(2,1)S(1)}, bf16[2,64,2304]{2,1,0:T(8,128)(2,1)S(1)}, u32[]{:S(2)}, u32[]{:S(2)}) %collective-permute-start.8) | collective-permute-done | bytes 589856 | tf_op jit(solution)/shard_map/ppermute | solution.py:395
  41.1 1.9 %collective-permute-start.7 = (bf16[2,64,2304]{2,1,0:T(8,128)(2,1)S(1)}, bf16[2,64,2304]{2,1,0:T(8,128)(2,1)S(1)}, u32[]{:S(2)}, u32[]{:S(2)}) collective-permute-start(bf16[2,64,2304]{2,1,0:T(8,128)(2,1)S(1)} %get-tuple-element.25.refs_2_.rest_0_), channel_id=1, source_target_pairs={{0,12},{12,0},{1,13},{13,1},{2,14},{14,2},{3,15},{15,3},{16,28},{2... | collective-permute-start | bytes 1769480 | tf_op jit(solution)/shard_map/ppermute | solution.py:395
  43.0 0.0 copy-done
  43.0 1.9 %shard_map.77.refs_0_ = bf16[4,64,128]{2,1,0:T(8,128)(2,1)S(1)} custom-call(s32[28]{0:T(128)S(1)} %get-tuple-element.17.plan_ref, bf16[8,128,2048]{2,1,0:T(8,128)(2,1)S(1)} %bitcast.4, bf16[4,64,2048]{2,1,0:T(8,128)(2,1)S(1)} %bitcast.17, bf16[2,64,2304]{2,1,0:T(8,128)(2,1)S(1)} %collective-permute-done.8.refs_1_.refs_7_.rest_1_, ...), custom_call_target="tpu_custom_call" | custom-call | tf_op jit(solution)/shard_map/pallas_call | solution.py:319
  45.0 0.0 collective-permute-done.14.up_ref.refs_6_.refs_8_
  45.0 0.1 collective-permute-start.9
  45.1 0.0 collective-permute-done.13.down_ref.refs_0_.refs_2_
  45.1 0.6 shard_map.79
  45.7 0.0 copy-start.4
  45.7 1.4 %collective-permute-start.15 = (bf16[1,64,2304]{2,1,0:T(8,128)(2,1)S(1)}, bf16[1,64,2304]{2,1,0:T(8,128)(2,1)S(1)}, u32[]{:S(2)}, u32[]{:S(2)}) collective-permute-start(bf16[1,64,2304]{2,1,0:T(8,128)(2,1)S(1)} %get-tuple-element.27), channel_id=1, source_target_pairs={{4,0},{8,12},{5,1},{9,13},{6,2},{10,14},{7,3},{11,15},{20,16},{24,... | collective-permute-start | bytes 884744 | tf_op jit(solution)/shard_map/ppermute | solution.py:395
  47.2 0.0 collective-permute-done.9.refs_1_
  47.2 1.3 %collective-permute-start.16 = (bf16[1,64,2304]{2,1,0:T(8,128)(2,1)S(1)}, bf16[1,64,2304]{2,1,0:T(8,128)(2,1)S(1)}, u32[]{:S(2)}, u32[]{:S(2)}) collective-permute-start(bf16[1,64,2304]{2,1,0:T(8,128)(2,1)S(1)} %get-tuple-element.28), channel_id=1, source_target_pairs={{4,0},{8,12},{5,1},{9,13},{6,2},{10,14},{7,3},{11,15},{20,16},{24,... | collective-permute-start | bytes 884744 | tf_op jit(solution)/shard_map/ppermute | solution.py:395
  48.5 21.6 %collective-permute-done.15.refs_1_.refs_7_ = bf16[1,64,2304]{2,1,0:T(8,128)(2,1)S(1)} collective-permute-done((bf16[1,64,2304]{2,1,0:T(8,128)(2,1)S(1)}, bf16[1,64,2304]{2,1,0:T(8,128)(2,1)S(1)}, u32[]{:S(2)}, u32[]{:S(2)}) %collective-permute-start.15) | collective-permute-done | bytes 294944 | tf_op jit(solution)/shard_map/ppermute | solution.py:395
  70.1 1.7 %collective-permute-start.10 = (bf16[4,64,128]{2,1,0:T(8,128)(2,1)S(1)}, bf16[4,64,128]{2,1,0:T(8,128)(2,1)S(1)}, u32[]{:S(2)}, u32[]{:S(2)}) collective-permute-start(bf16[4,64,128]{2,1,0:T(8,128)(2,1)S(1)} %shard_map.77.refs_0_), channel_id=1, source_target_pairs={{0,2},{1,3},{2,0},{3,1},{4,6},{5,7},{6,4},{7,5},{8,10},{9,11},{10,... | collective-permute-start | bytes 196616 | tf_op jit(solution)/shard_map/ppermute | solution.py:26
  71.8 4.3 %collective-permute-done.16.refs_3_.refs_9_ = bf16[1,64,2304]{2,1,0:T(8,128)(2,1)S(1)} collective-permute-done((bf16[1,64,2304]{2,1,0:T(8,128)(2,1)S(1)}, bf16[1,64,2304]{2,1,0:T(8,128)(2,1)S(1)}, u32[]{:S(2)}, u32[]{:S(2)}) %collective-permute-start.16) | collective-permute-done | bytes 294944 | tf_op jit(solution)/shard_map/ppermute | solution.py:395
  76.1 1.1 %collective-permute-start.11 = (bf16[4,64,128]{2,1,0:T(8,128)(2,1)S(1)}, bf16[4,64,128]{2,1,0:T(8,128)(2,1)S(1)}, u32[]{:S(2)}, u32[]{:S(2)}) collective-permute-start(bf16[4,64,128]{2,1,0:T(8,128)(2,1)S(1)} %shard_map.77.refs_0_), channel_id=1, source_target_pairs={{0,3},{1,2},{2,1},{3,0},{4,7},{5,6},{6,5},{7,4},{8,11},{9,10},{10,... | collective-permute-start | bytes 196616 | tf_op jit(solution)/shard_map/ppermute | solution.py:26
  77.2 1.3 %shard_map.80.refs_3_.refs_0_ = bf16[2,64,128]{2,1,0:T(8,128)(2,1)S(1)} custom-call(s32[28]{0:T(128)S(1)} %get-tuple-element.17.plan_ref, bf16[8,128,2048]{2,1,0:T(8,128)(2,1)S(1)} %bitcast.5, bf16[4,64,2048]{2,1,0:T(8,128)(2,1)S(1)} %collective-permute-done.13.down_ref.refs_0_.refs_2_, bf16[1,64,2304]{2,1,0:T(8,128)(2,1)S(1)} %collective-permute-done.15.refs_1_.refs_7_, ...), custom_call_target="tpu_custom_call" | custom-call | tf_op jit(solution)/shard_map/pallas_call | solution.py:319
  78.5 0.0 collective-permute-done.10.refs_2_
  78.5 0.8 collective-permute-start.20
  79.3 1.0 %collective-permute-done.11.refs_3_ = bf16[4,64,128]{2,1,0:T(8,128)(2,1)S(1)} collective-permute-done((bf16[4,64,128]{2,1,0:T(8,128)(2,1)S(1)}, bf16[4,64,128]{2,1,0:T(8,128)(2,1)S(1)}, u32[]{:S(2)}, u32[]{:S(2)}) %collective-permute-start.11) | collective-permute-done | bytes 65568 | tf_op jit(solution)/shard_map/ppermute | solution.py:26
  80.3 1.9 %collective-permute-start.21 = (bf16[2,64,128]{2,1,0:T(8,128)(2,1)S(1)}, bf16[2,64,128]{2,1,0:T(8,128)(2,1)S(1)}, u32[]{:S(2)}, u32[]{:S(2)}) collective-permute-start(bf16[2,64,128]{2,1,0:T(8,128)(2,1)S(1)} %shard_map.80.refs_3_.refs_0_), channel_id=1, source_target_pairs={{0,2},{1,3},{2,0},{3,1},{4,6},{5,7},{6,4},{7,5},{8,10},{9,11},{10,... | collective-permute-start | bytes 98312 | tf_op jit(solution)/shard_map/ppermute | solution.py:26
  82.2 0.0 collective-permute-done.12
  82.2 0.0 collective-permute-start.22
  82.2 2.6 %shard_map.78.refs_2_.refs_10_ = bf16[1024,256]{1,0:T(8,128)(2,1)} custom-call(s32[28]{0:T(128)S(1)} %get-tuple-element.17.plan_ref, bf16[4,64,128]{2,1,0:T(8,128)(2,1)S(1)} %shard_map.77.refs_0_, bf16[4,64,128]{2,1,0:T(8,128)(2,1)S(1)} %collective-permute-done.9.refs_1_, bf16[4,64,128]{2,1,0:T(8,128)(2,1)S(1)} %collective-permute-done.10.refs_2_, ...), custom_call_target="tpu_custom_call" | custom-call | tf_op jit(solution)/shard_map/pallas_call | solution.py:376
  84.7 0.0 collective-permute-done.6.refs_0_.refs_6_
  84.7 0.0 collective-permute-done.7.refs_1_.refs_7_
  84.8 1.0 %copy-done.1 = bf16[1024,256]{1,0:T(8,128)(2,1)S(1)} copy-done((bf16[1024,256]{1,0:T(8,128)(2,1)S(1)}, bf16[1024,256]{1,0:T(8,128)(2,1)}, u32[]{:S(2)}) %copy-start.1) | copy-done | bytes 524312
  85.8 1.3 %shard_map.81.refs_0_ = bf16[2,64,128]{2,1,0:T(8,128)(2,1)S(1)} custom-call(s32[28]{0:T(128)S(1)} %get-tuple-element.17.plan_ref, bf16[8,128,2048]{2,1,0:T(8,128)(2,1)S(1)} %bitcast.6, bf16[2,64,2304]{2,1,0:T(8,128)(2,1)S(1)} %collective-permute-done.6.refs_0_.refs_6_, bf16[2,64,2304]{2,1,0:T(8,128)(2,1)S(1)} %collective-permute-done.7.refs_1_.refs_7_, ...), custom_call_target="tpu_custom_call" | custom-call | tf_op jit(solution)/shard_map/pallas_call | solution.py:319
  87.1 0.3 collective-permute-start.17
  87.4 1.9 %collective-permute-start.18 = (bf16[2,64,128]{2,1,0:T(8,128)(2,1)S(1)}, bf16[2,64,128]{2,1,0:T(8,128)(2,1)S(1)}, u32[]{:S(2)}, u32[]{:S(2)}) collective-permute-start(bf16[2,64,128]{2,1,0:T(8,128)(2,1)S(1)} %shard_map.81.refs_0_), channel_id=1, source_target_pairs={{0,2},{1,3},{2,0},{3,1},{4,6},{5,7},{6,4},{7,5},{8,10},{9,11},{10,... | collective-permute-start | bytes 98312 | tf_op jit(solution)/shard_map/ppermute | solution.py:26
  89.3 0.0 collective-permute-done.20.refs_1_
  89.3 0.0 collective-permute-start.19
  89.3 0.0 collective-permute-done.21.refs_2_
  89.3 0.0 collective-permute-done.22.refs_3_
  89.3 1.7 %shard_map.82.refs_8_ = bf16[1024,256]{1,0:T(8,128)(2,1)} custom-call(s32[28]{0:T(128)S(1)} %get-tuple-element.17.plan_ref, bf16[2,64,128]{2,1,0:T(8,128)(2,1)S(1)} %shard_map.80.refs_3_.refs_0_, bf16[2,64,128]{2,1,0:T(8,128)(2,1)S(1)} %collective-permute-done.20.refs_1_, ...), custom_call_target="tpu_custom_call", output_to_operand_aliasing={{}: (11, {})} | custom-call | tf_op jit(solution)/shard_map/pallas_call | solution.py:376
  91.0 0.0 collective-permute-done.17.refs_1_
  91.0 0.3 collective-permute-done.18.refs_2_
  91.3 1.6 %collective-permute-done.19.refs_3_ = bf16[2,64,128]{2,1,0:T(8,128)(2,1)S(1)} collective-permute-done((bf16[2,64,128]{2,1,0:T(8,128)(2,1)S(1)}, bf16[2,64,128]{2,1,0:T(8,128)(2,1)S(1)}, u32[]{:S(2)}, u32[]{:S(2)}) %collective-permute-start.19) | collective-permute-done | bytes 32800 | tf_op jit(solution)/shard_map/ppermute | solution.py:26
  93.0 1.7 %shard_map.83 = bf16[1024,256]{1,0:T(8,128)(2,1)} custom-call(s32[28]{0:T(128)S(1)} %get-tuple-element.17.plan_ref, bf16[2,64,128]{2,1,0:T(8,128)(2,1)S(1)} %shard_map.81.refs_0_, bf16[2,64,128]{2,1,0:T(8,128)(2,1)S(1)} %collective-permute-done.17.refs_1_, bf16[2,64,128]{2,1,0:T(8,128)(2,1)S(1)} %collective-permute-done.18.refs_2_, ...), custom_call_target="tpu_custom_call", output_to_operand_aliasing={{}: (9, {})} | custom-call | tf_op jit(solution)/shard_map/pallas_call | solution.py:376
  (3 shorter events, 0.0 us)
Async XLA Ops:
  0.0 6.3 %collective-permute-start = (s32[1,8]{1,0:T(1,128)}, s32[1,8]{1,0:T(1,128)S(1)}, u32[]{:S(2)}, u32[]{:S(2)}) collective-permute-start(s32[1,8]{1,0:T(1,128)} %refs_0_.1), channel_id=1, source_target_pairs={{0,4},{4,0},{8,12},{12,8},{1,5},{5,1},{9,13},{13,9},{2,6},{6,2},{1... | collective-permute-start | bytes 104 | tf_op jit(solution)/shard_map/ppermute | solution.py:26
  3.0 4.6 %collective-permute-start.1 = (s32[1,8]{1,0:T(1,128)}, s32[1,8]{1,0:T(1,128)S(1)}, u32[]{:S(2)}, u32[]{:S(2)}) collective-permute-start(s32[1,8]{1,0:T(1,128)} %refs_0_.1), channel_id=1, source_target_pairs={{0,8},{4,12},{8,0},{12,4},{1,9},{5,13},{9,1},{13,5},{2,10},{6,14},... | collective-permute-start | bytes 104 | tf_op jit(solution)/shard_map/ppermute | solution.py:26
  5.6 5.5 %collective-permute-start.2 = (s32[1,8]{1,0:T(1,128)}, s32[1,8]{1,0:T(1,128)S(1)}, u32[]{:S(2)}, u32[]{:S(2)}) collective-permute-start(s32[1,8]{1,0:T(1,128)} %refs_0_.1), channel_id=1, source_target_pairs={{0,12},{4,8},{8,4},{12,0},{1,13},{5,9},{9,5},{13,1},{2,14},{6,10},... | collective-permute-start | bytes 104 | tf_op jit(solution)/shard_map/ppermute | solution.py:26
  5.6 39.5 %collective-permute-start.13 = (bf16[4,64,2048]{2,1,0:T(8,128)(2,1)}, bf16[4,64,2048]{2,1,0:T(8,128)(2,1)S(1)}, u32[]{:S(2)}, u32[]{:S(2)}) collective-permute-start(bf16[4,64,2048]{2,1,0:T(8,128)(2,1)} %bitcast.14), channel_id=1, source_target_pairs={{4,8},{8,4},{5,9},{9,5},{6,10},{10,6},{7,11},{11,7},{20,24},{24,20... | collective-permute-start | bytes 3145736 | tf_op jit(solution)/shard_map/ppermute | solution.py:395
  13.8 15.6 %copy-start.3 = (bf16[4,64,256]{2,1,0:T(8,128)(2,1)S(1)}, bf16[4,64,256]{2,1,0:T(8,128)(2,1)}, u32[]{:S(2)}) copy-start(bf16[4,64,256]{2,1,0:T(8,128)(2,1)} %refs_6_.1) | copy-start | bytes 393220
  25.2 17.8 %copy-start = (bf16[1024,2048]{1,0:T(8,128)(2,1)S(1)}, bf16[1024,2048]{1,0:T(8,128)(2,1)}, u32[]{:S(2)}) copy-start(bf16[1024,2048]{1,0:T(8,128)(2,1)} %tokens_ref.1) | copy-start | bytes 12582916
  25.2 17.8 %copy-start.2 = (bf16[4,2048,64]{1,2,0:T(8,128)(2,1)S(1)}, bf16[4,2048,64]{1,2,0:T(8,128)(2,1)}, u32[]{:S(2)}) copy-start(bf16[4,2048,64]{1,2,0:T(8,128)(2,1)} %param.9) | copy-start | bytes 3145732
  25.2 4.9 %collective-permute-start.3 = (f32[2,448,256]{2,1,0:T(8,128)S(1)}, f32[2,448,256]{2,1,0:T(8,128)S(1)}, u32[]{:S(2)}, u32[]{:S(2)}) collective-permute-start(f32[2,448,256]{2,1,0:T(8,128)S(1)} %get-tuple-element.20), channel_id=1, source_target_pairs={{0,1},{1,0},{2,3},{3,2},{4,5},{5,4},{6,7},{7,6},{8,9},{9,8},{10,11... | collective-permute-start | bytes 2752520 | tf_op jit(solution)/shard_map/ppermute | solution.py:26
  25.3 4.8 %collective-permute-start.4 = (f32[2,448,256]{2,1,0:T(8,128)S(1)}, f32[2,448,256]{2,1,0:T(8,128)S(1)}, u32[]{:S(2)}, u32[]{:S(2)}) collective-permute-start(f32[2,448,256]{2,1,0:T(8,128)S(1)} %get-tuple-element.21), channel_id=1, source_target_pairs={{0,1},{1,0},{2,3},{3,2},{4,5},{5,4},{6,7},{7,6},{8,9},{9,8},{10,11... | collective-permute-start | bytes 2752520 | tf_op jit(solution)/shard_map/ppermute | solution.py:26
  25.8 15.3 %collective-permute-start.8 = (bf16[2,64,2304]{2,1,0:T(8,128)(2,1)S(1)}, bf16[2,64,2304]{2,1,0:T(8,128)(2,1)S(1)}, u32[]{:S(2)}, u32[]{:S(2)}) collective-permute-start(bf16[2,64,2304]{2,1,0:T(8,128)(2,1)S(1)} %get-tuple-element.18.refs_0_), channel_id=1, source_target_pairs={{0,4},{4,0},{8,12},{12,8},{1,5},{5,1},{9,13},{13,9},{2,6},{6,2},{1... | collective-permute-start | bytes 1769480 | tf_op jit(solution)/shard_map/ppermute | solution.py:395
  25.8 3.6 %collective-permute-start.5 = (f32[2,128,256]{2,1,0:T(8,128)S(1)}, f32[2,128,256]{2,1,0:T(8,128)S(1)}, u32[]{:S(2)}, u32[]{:S(2)}) collective-permute-start(f32[2,128,256]{2,1,0:T(8,128)S(1)} %get-tuple-element.22), channel_id=1, source_target_pairs={{0,1},{1,0},{2,3},{3,2},{4,5},{5,4},{6,7},{7,6},{8,9},{9,8},{10,11... | collective-permute-start | bytes 786440 | tf_op jit(solution)/shard_map/ppermute | solution.py:26
  29.4 15.5 %collective-permute-start.14 = (bf16[4,64,256]{2,1,0:T(8,128)(2,1)S(1)}, bf16[4,64,256]{2,1,0:T(8,128)(2,1)S(1)}, u32[]{:S(2)}, u32[]{:S(2)}) collective-permute-start(bf16[4,64,256]{2,1,0:T(8,128)(2,1)S(1)} %copy-done.3), channel_id=1, source_target_pairs={{4,8},{8,4},{5,9},{9,5},{6,10},{10,6},{7,11},{11,7},{20,24},{24,20... | collective-permute-start | bytes 393224 | tf_op jit(solution)/shard_map/ppermute | solution.py:395
  30.3 51.8 %collective-permute-start.12 = (f32[1,1024,256]{2,1,0:T(8,128)S(1)}, f32[1,1024,256]{2,1,0:T(8,128)S(1)}, u32[]{:S(2)}, u32[]{:S(2)}) collective-permute-start(f32[1,1024,256]{2,1,0:T(8,128)S(1)} %get-tuple-element.26), channel_id=1, source_target_pairs={{0,2},{1,3},{2,0},{3,1},{4,6},{5,7},{6,4},{7,5},{8,10},{9,11},{10,... | collective-permute-start | bytes 3145736 | tf_op jit(solution)/shard_map/ppermute | solution.py:26
  33.8 51.0 %collective-permute-start.6 = (bf16[2,64,2304]{2,1,0:T(8,128)(2,1)S(1)}, bf16[2,64,2304]{2,1,0:T(8,128)(2,1)S(1)}, u32[]{:S(2)}, u32[]{:S(2)}) collective-permute-start(bf16[2,64,2304]{2,1,0:T(8,128)(2,1)S(1)} %get-tuple-element.24), channel_id=1, source_target_pairs={{0,8},{12,4},{1,9},{13,5},{2,10},{14,6},{3,11},{15,7},{16,24},{28,... | collective-permute-start | bytes 1769480 | tf_op jit(solution)/shard_map/ppermute | solution.py:395
  41.1 43.7 %collective-permute-start.7 = (bf16[2,64,2304]{2,1,0:T(8,128)(2,1)S(1)}, bf16[2,64,2304]{2,1,0:T(8,128)(2,1)S(1)}, u32[]{:S(2)}, u32[]{:S(2)}) collective-permute-start(bf16[2,64,2304]{2,1,0:T(8,128)(2,1)S(1)} %get-tuple-element.25.refs_2_.rest_0_), channel_id=1, source_target_pairs={{0,12},{12,0},{1,13},{13,1},{2,14},{14,2},{3,15},{15,3},{16,28},{2... | collective-permute-start | bytes 1769480 | tf_op jit(solution)/shard_map/ppermute | solution.py:395
  45.0 2.2 %collective-permute-start.9 = (bf16[4,64,128]{2,1,0:T(8,128)(2,1)S(1)}, bf16[4,64,128]{2,1,0:T(8,128)(2,1)S(1)}, u32[]{:S(2)}, u32[]{:S(2)}) collective-permute-start(bf16[4,64,128]{2,1,0:T(8,128)(2,1)S(1)} %shard_map.77.refs_0_), channel_id=1, source_target_pairs={{0,1},{1,0},{2,3},{3,2},{4,5},{5,4},{6,7},{7,6},{8,9},{9,8},{10,11... | collective-permute-start | bytes 196616 | tf_op jit(solution)/shard_map/ppermute | solution.py:26
  45.7 36.4 %copy-start.4 = (bf16[4,64,256]{2,1,0:T(8,128)(2,1)S(1)}, bf16[4,64,256]{2,1,0:T(8,128)(2,1)}, u32[]{:S(2)}) copy-start(bf16[4,64,256]{2,1,0:T(8,128)(2,1)} %refs_6_.1) | copy-start | bytes 393220
  45.7 24.4 %collective-permute-start.15 = (bf16[1,64,2304]{2,1,0:T(8,128)(2,1)S(1)}, bf16[1,64,2304]{2,1,0:T(8,128)(2,1)S(1)}, u32[]{:S(2)}, u32[]{:S(2)}) collective-permute-start(bf16[1,64,2304]{2,1,0:T(8,128)(2,1)S(1)} %get-tuple-element.27), channel_id=1, source_target_pairs={{4,0},{8,12},{5,1},{9,13},{6,2},{10,14},{7,3},{11,15},{20,16},{24,... | collective-permute-start | bytes 884744 | tf_op jit(solution)/shard_map/ppermute | solution.py:395
  47.2 28.9 %collective-permute-start.16 = (bf16[1,64,2304]{2,1,0:T(8,128)(2,1)S(1)}, bf16[1,64,2304]{2,1,0:T(8,128)(2,1)S(1)}, u32[]{:S(2)}, u32[]{:S(2)}) collective-permute-start(bf16[1,64,2304]{2,1,0:T(8,128)(2,1)S(1)} %get-tuple-element.28), channel_id=1, source_target_pairs={{4,0},{8,12},{5,1},{9,13},{6,2},{10,14},{7,3},{11,15},{20,16},{24,... | collective-permute-start | bytes 884744 | tf_op jit(solution)/shard_map/ppermute | solution.py:395
  70.1 8.4 %collective-permute-start.10 = (bf16[4,64,128]{2,1,0:T(8,128)(2,1)S(1)}, bf16[4,64,128]{2,1,0:T(8,128)(2,1)S(1)}, u32[]{:S(2)}, u32[]{:S(2)}) collective-permute-start(bf16[4,64,128]{2,1,0:T(8,128)(2,1)S(1)} %shard_map.77.refs_0_), channel_id=1, source_target_pairs={{0,2},{1,3},{2,0},{3,1},{4,6},{5,7},{6,4},{7,5},{8,10},{9,11},{10,... | collective-permute-start | bytes 196616 | tf_op jit(solution)/shard_map/ppermute | solution.py:26
  76.1 4.1 %collective-permute-start.11 = (bf16[4,64,128]{2,1,0:T(8,128)(2,1)S(1)}, bf16[4,64,128]{2,1,0:T(8,128)(2,1)S(1)}, u32[]{:S(2)}, u32[]{:S(2)}) collective-permute-start(bf16[4,64,128]{2,1,0:T(8,128)(2,1)S(1)} %shard_map.77.refs_0_), channel_id=1, source_target_pairs={{0,3},{1,2},{2,1},{3,0},{4,7},{5,6},{6,5},{7,4},{8,11},{9,10},{10,... | collective-permute-start | bytes 196616 | tf_op jit(solution)/shard_map/ppermute | solution.py:26
  78.5 10.8 %collective-permute-start.20 = (bf16[2,64,128]{2,1,0:T(8,128)(2,1)S(1)}, bf16[2,64,128]{2,1,0:T(8,128)(2,1)S(1)}, u32[]{:S(2)}, u32[]{:S(2)}) collective-permute-start(bf16[2,64,128]{2,1,0:T(8,128)(2,1)S(1)} %shard_map.80.refs_3_.refs_0_), channel_id=1, source_target_pairs={{0,1},{1,0},{2,3},{3,2},{4,5},{5,4},{6,7},{7,6},{8,9},{9,8},{10,11... | collective-permute-start | bytes 98312 | tf_op jit(solution)/shard_map/ppermute | solution.py:26
  80.3 9.0 %collective-permute-start.21 = (bf16[2,64,128]{2,1,0:T(8,128)(2,1)S(1)}, bf16[2,64,128]{2,1,0:T(8,128)(2,1)S(1)}, u32[]{:S(2)}, u32[]{:S(2)}) collective-permute-start(bf16[2,64,128]{2,1,0:T(8,128)(2,1)S(1)} %shard_map.80.refs_3_.refs_0_), channel_id=1, source_target_pairs={{0,2},{1,3},{2,0},{3,1},{4,6},{5,7},{6,4},{7,5},{8,10},{9,11},{10,... | collective-permute-start | bytes 98312 | tf_op jit(solution)/shard_map/ppermute | solution.py:26
  82.2 7.1 %collective-permute-start.22 = (bf16[2,64,128]{2,1,0:T(8,128)(2,1)S(1)}, bf16[2,64,128]{2,1,0:T(8,128)(2,1)S(1)}, u32[]{:S(2)}, u32[]{:S(2)}) collective-permute-start(bf16[2,64,128]{2,1,0:T(8,128)(2,1)S(1)} %shard_map.80.refs_3_.refs_0_), channel_id=1, source_target_pairs={{0,3},{1,2},{2,1},{3,0},{4,7},{5,6},{6,5},{7,4},{8,11},{9,10},{10,... | collective-permute-start | bytes 98312 | tf_op jit(solution)/shard_map/ppermute | solution.py:26
  84.8 1.0 %copy-start.1 = (bf16[1024,256]{1,0:T(8,128)(2,1)S(1)}, bf16[1024,256]{1,0:T(8,128)(2,1)}, u32[]{:S(2)}) copy-start(bf16[1024,256]{1,0:T(8,128)(2,1)} %shard_map.78.refs_2_.refs_10_) | copy-start | bytes 1572868
  87.1 3.9 %collective-permute-start.17 = (bf16[2,64,128]{2,1,0:T(8,128)(2,1)S(1)}, bf16[2,64,128]{2,1,0:T(8,128)(2,1)S(1)}, u32[]{:S(2)}, u32[]{:S(2)}) collective-permute-start(bf16[2,64,128]{2,1,0:T(8,128)(2,1)S(1)} %shard_map.81.refs_0_), channel_id=1, source_target_pairs={{0,1},{1,0},{2,3},{3,2},{4,5},{5,4},{6,7},{7,6},{8,9},{9,8},{10,11... | collective-permute-start | bytes 98312 | tf_op jit(solution)/shard_map/ppermute | solution.py:26
  87.4 3.9 %collective-permute-start.18 = (bf16[2,64,128]{2,1,0:T(8,128)(2,1)S(1)}, bf16[2,64,128]{2,1,0:T(8,128)(2,1)S(1)}, u32[]{:S(2)}, u32[]{:S(2)}) collective-permute-start(bf16[2,64,128]{2,1,0:T(8,128)(2,1)S(1)} %shard_map.81.refs_0_), channel_id=1, source_target_pairs={{0,2},{1,3},{2,0},{3,1},{4,6},{5,7},{6,4},{7,5},{8,10},{9,11},{10,... | collective-permute-start | bytes 98312 | tf_op jit(solution)/shard_map/ppermute | solution.py:26
  89.3 3.7 %collective-permute-start.19 = (bf16[2,64,128]{2,1,0:T(8,128)(2,1)S(1)}, bf16[2,64,128]{2,1,0:T(8,128)(2,1)S(1)}, u32[]{:S(2)}, u32[]{:S(2)}) collective-permute-start(bf16[2,64,128]{2,1,0:T(8,128)(2,1)S(1)} %shard_map.81.refs_0_), channel_id=1, source_target_pairs={{0,3},{1,2},{2,1},{3,0},{4,7},{5,6},{6,5},{7,4},{8,11},{9,10},{10,... | collective-permute-start | bytes 98312 | tf_op jit(solution)/shard_map/ppermute | solution.py:26

commit v5 on v4

--- a/solution.py
+++ b/solution.py
@@ -12,6 +12,7 @@
 PARAMS = pltpu.CompilerParams(vmem_limit_bytes=16 * 1024 * 1024)
 NO_COST = pl.CostEstimate(flops=0, bytes_accessed=0, transcendentals=0)
 SHORT = pl.CostEstimate(flops=4 * 10**9, bytes_accessed=0, transcendentals=0)
+MIDDLE = pl.CostEstimate(flops=0 * 10**9, bytes_accessed=0, transcendentals=0)
 LONG = pl.CostEstimate(flops=6 * 10**9, bytes_accessed=0, transcendentals=0)
 ANY = pl.BlockSpec(memory_space=pl.ANY)
 SMEM = pl.BlockSpec(memory_space=pltpu.SMEM)
@@ -27,58 +28,62 @@
 
 
 def piece_rows(rows):
-    large = rows * 7 // 16
+    large = rows * 3 // 8
     return [large, large, rows - 2 * large]
 
 
-def base_kernel(order, tokens_ref, weight_ref, *refs):
-    kept_ref = refs[-1]
-    half, tile, width = kept_ref.shape
-    sizes = piece_rows(tile * pl.num_programs(0))
-    sent_refs = refs[-1 - len(sizes) : -1]
-    place = lax.axis_index("tensor")
-    for number, offset in enumerate(order):
-        columns = pl.ds(pl.multiple_of((place ^ offset) * width, width), width)
-        part = jnp.dot(
-            tokens_ref[...], weight_ref[:, columns], preferred_element_type=jnp.float32
-        )
-        if number >= half:
-            kept_ref[number - half] = part
-            continue
-        for step in range(pl.num_programs(0)):
-
-            @pl.when(pl.program_id(0) == step)
-            def _(number=number, part=part, first=step * tile):
-                start = 0
-                for sent_ref, size in zip(sent_refs, sizes):
-                    low, high = max(first, start), min(first + tile, start + size)
-                    if low < high:
-                        rows = slice(low - start, high - start)
-                        sent_ref[number, rows, :] = part[low - first : high - first]
-                    start += size
+def base_kernel(half, chunks_ref, tokens_ref, weight_ref, *refs):
+    del chunks_ref
+    *sent_refs, kept_ref = refs[-1 - len(piece_rows(tokens_ref.shape[0])) :]
+
+    def write(out_ref, first, size):
+        for start in range(0, size, ROW_TILE):
+            stop = min(start + ROW_TILE, size)
+            out_ref[0, start:stop, :] = jnp.dot(
+                tokens_ref[first + start : first + stop, :],
+                weight_ref[...],
+                preferred_element_type=jnp.float32,
+            )
+
+    @pl.when(pl.program_id(0) < half)
+    def _():
+        first = 0
+        for sent_ref in sent_refs:
+            write(sent_ref, first, sent_ref.shape[1])
+            first += sent_ref.shape[1]
+
+    @pl.when(pl.program_id(0) >= half)
+    def _():
+        write(kept_ref, 0, kept_ref.shape[1])
 
 
 def base_chunks(tokens, weight, order, width, after):
     rows, depth = tokens.shape
-    tile = min(ROW_TILE, rows)
     half = len(order) // 2
-    pieces = [(half, size, width) for size in piece_rows(rows)]
+    sizes = piece_rows(rows)
+    chunks = lax.axis_index("tensor") ^ jnp.asarray(order, jnp.int32)
     *sent, kept = pl.pallas_call(
-        functools.partial(base_kernel, order),
-        grid=(rows // tile,),
-        in_specs=[
-            pl.BlockSpec((tile, depth), lambda i: (i, 0)),
-            pl.BlockSpec(weight.shape, lambda i: (0, 0), pipeline_mode=pl.Buffered(1)),
-        ]
-        + [ANY] * len(after),
-        out_specs=[pl.BlockSpec(shape, lambda i: (0, 0, 0)) for shape in pieces]
-        + [pl.BlockSpec((half, tile, width), lambda i: (0, i, 0))],
+        functools.partial(base_kernel, half),
+        grid_spec=pltpu.PrefetchScalarGridSpec(
+            num_scalar_prefetch=1,
+            grid=(len(order),),
+            in_specs=[
+                pl.BlockSpec(tokens.shape, lambda i, c: (0, 0), pipeline_mode=pl.Buffered(1)),
+                pl.BlockSpec((depth, width), lambda i, c: (0, c[i])),
+            ]
+            + [ANY] * len(after),
+            out_specs=[
+                pl.BlockSpec((1, size, width), lambda i, c: (jnp.minimum(i, half - 1), 0, 0))
+                for size in sizes
+            ]
+            + [pl.BlockSpec((1, rows, width), lambda i, c: (jnp.maximum(i - half, 0), 0, 0))],
+        ),
         out_shape=[
-            jax.ShapeDtypeStruct(shape, jnp.float32) for shape in [*pieces, (half, rows, width)]
+            jax.ShapeDtypeStruct((half, size, width), jnp.float32) for size in [*sizes, rows]
         ],
         compiler_params=PARAMS,
         cost_estimate=NO_COST,
-    )(in_hbm(tokens), in_hbm(weight), *after)
+    )(chunks, in_hbm(tokens), in_hbm(weight), *after)
     return sent, kept
 
 
@@ -150,8 +155,8 @@
 
 
 def plan_kernel(capacity, *refs):
-    sources, down_ref, up_ref, near_ref, plan_ref = refs[:6], *refs[6:10]
-    scalars, scalar_sems, sems = refs[10:16], *refs[16:]
+    sources, down_ref, up_ref, out_refs, plan_ref = refs[:6], *refs[6:8], refs[8:11], refs[11]
+    scalars, scalar_sems, sems = refs[12:18], *refs[18:]
     loads = [
         pltpu.make_async_copy(source, scalar, scalar_sems.at[i])
         for i, (source, scalar) in enumerate(zip(sources, scalars))
@@ -165,25 +170,24 @@
         pick, table_ref=table_ref, holder_slots=holder_slots, count=capacity
     )
     copies = []
-    for k, slot in enumerate(find(first_ref, holder=here)[1]):
-        copies += run_copies(panel_copies(k, slot, down_ref, up_ref, near_ref, sems))
+    for i, asked_ref in enumerate((third_ref, second_ref, first_ref)):
+        for k, slot in enumerate(find(asked_ref, holder=here)[1]):
+            copies += run_copies(panel_copies(k, slot, down_ref, up_ref, out_refs[i], sems.at[i]))
     inner = (here == 1) | (here == 2)
     own = find(names_ref, holder=here)
     near = find(names_ref, holder=here ^ 1)
-    early = find(names_ref, holder=here ^ jnp.where(inner, 3, 2))
-    late = find(names_ref, holder=here ^ jnp.where(inner, 2, 3))
+    across = find(names_ref, holder=here ^ 3)
+    late = find(names_ref, holder=here ^ 2)
     rows = [
         own[0],
         near[0],
-        early[0],
+        across[0],
         late[0],
         own[1],
-        early[1],
-        find(second_ref, holder=here)[1],
-        find(third_ref, holder=here)[1],
+        across[1],
         find(first_ref, holder=here ^ 3)[1],
         [inner.astype(jnp.int32)] * capacity,
-        *[[live_ref[0, block] for block in phase[0]] for phase in (own, near, early, late)],
+        *[[live_ref[0, block] for block in phase[0]] for phase in (own, near, across, late)],
     ]
     for number, row in enumerate(rows):
         for k in range(capacity):
@@ -192,7 +196,7 @@
         copy.wait()
 
 
-OWN, EARLY, TO_INNER, TO_OUTER, FORWARD, INNER, LIVE, PLAN_ROWS = 4, 5, 6, 7, 8, 9, 10, 14
+OWN, ACROSS, FORWARD, INNER, LIVE, PLAN_ROWS = 4, 5, 6, 7, 8, 12
 
 
 def make_plan(names, others, table, live, down, up, capacity):
@@ -201,14 +205,14 @@
     return pl.pallas_call(
         functools.partial(plan_kernel, capacity),
         in_specs=[ANY] * 8,
-        out_specs=[ANY, SMEM],
-        out_shape=[
-            jax.ShapeDtypeStruct((capacity, rank, depth + width), down.dtype),
+        out_specs=[ANY] * 3 + [SMEM],
+        out_shape=[jax.ShapeDtypeStruct((capacity, rank, depth + width), down.dtype)] * 3
+        + [
             jax.ShapeDtypeStruct((PLAN_ROWS * capacity,), jnp.int32),
         ],
         scratch_shapes=[pltpu.SMEM(names.shape, jnp.int32)] * 4
         + [pltpu.SMEM(table.shape, jnp.int32), pltpu.SMEM(live.shape, jnp.int32)]
-        + [pltpu.SemaphoreType.DMA((6,)), pltpu.SemaphoreType.DMA((capacity, 2))],
+        + [pltpu.SemaphoreType.DMA((6,)), pltpu.SemaphoreType.DMA((3, capacity, 2))],
         compiler_params=PARAMS,
         cost_estimate=SHORT,
     )(in_hbm(names), *others, *[in_hbm(a) for a in (table, live, down, up)])
@@ -357,7 +361,9 @@
     for_phase(phases, choose, plan_ref, refs[part_count + 2 :], act)
 
 
-def combine(plan, live_row, parts, base, phases, columns, choose, out=None, after=()):
+def combine(
+    plan, live_row, parts, base, phases, columns, choose, out=None, after=(), cost=None
+):
     rank, block_rows = parts[0].shape[1:]
     rows, width = base[0].shape
     total = sum(count for _, count, _ in phases)
@@ -384,7 +390,7 @@
         out_shape=pltpu.HBM((rows, width), jnp.bfloat16),
         input_output_aliases=aliases,
         compiler_params=PARAMS,
-        cost_estimate=NO_COST,
+        cost_estimate=cost or NO_COST,
     )(plan, *operands)
 
 
@@ -397,60 +403,34 @@
     others = [swap(names, "pool", m) for m in range(1, 4)]
     inner_down = across(down, [(1, 2), (2, 1)])
     inner_up = across(up, [(1, 2), (2, 1)])
-    near_out, plan = make_plan(names, others, table, live, down, up, capacity)
+    outer_out, inner_out, near_out, plan = make_plan(
+        names, others, table, live, down, up, capacity
+    )
+    to_outer = across(outer_out, [(0, 3), (3, 0)])
+    to_inner = across(inner_out, [(0, 2), (3, 1)])
     near = across(near_out, [(0, 1), (1, 0), (2, 3), (3, 2)])
     base = base_sum(tokens, weight, up.shape[2], [near_out])
-    inner_out, outer_out = pack_panels(
-        plan,
-        [TO_INNER * capacity, TO_OUTER * capacity],
-        capacity,
-        in_hbm(down),
-        in_hbm(up),
-        [base[0]],
+    (forward_out,) = pack_panels(
+        plan, [FORWARD * capacity], capacity, inner_down, inner_up, [base[0]], LONG
     )
-    to_inner = across(inner_out, [(0, 2), (3, 1)])
-    to_outer = across(outer_out, [(0, 3), (3, 0)])
-    forward_out = pack_panels(
-        plan,
-        [FORWARD * capacity + k for k in range(capacity)],
-        1,
-        inner_down,
-        inner_up,
-        [outer_out, near],
-        LONG,
-    )
-    forwarded = [across(panel, [(1, 0), (2, 3)]) for panel in forward_out]
+    forwarded = across(forward_out, [(1, 0), (2, 3)])
 
     choose = INNER * capacity
-
-    def phases_of(down_panels, up_panels, place):
-        early = [
-            (
-                2 * capacity + k,
-                1,
-                [(place, EARLY * capacity + k), (forwarded[k], None)],
-            )
-            for k in range(capacity)
-        ]
-        return [
-            (0, capacity, [(down_panels, OWN * capacity)]),
-            (capacity, capacity, [(near, None)]),
-        ], early
-
-    first, early = phases_of(down, None, inner_down)
-    first_up, early_up = phases_of(up, None, inner_up)
-    last = [(3 * capacity, capacity, [(to_inner, None), (to_outer, None)])]
-
-    first_parts = exchange(shrink(plan, row_blocks, first, choose, [outer_out]))
-    columns = [[0], [up_column]]
-    out = combine(plan, LIVE * capacity, first_parts, base, first_up, columns, choose)
-    early_part = shrink(plan, row_blocks, early, choose)
-    early_parts = exchange(early_part)
-    last_parts = exchange(shrink(plan, row_blocks, last, choose, [out, early_part]))
-    columns = [[0, up_column]] * capacity
-    out = combine(
-        plan, (LIVE + 2) * capacity, early_parts, base, early_up, columns, choose, out
-    )
+    first = [
+        (0, capacity, [(down, OWN * capacity)]),
+        (capacity, capacity, [(near, None)]),
+        (2 * capacity, capacity, [(inner_down, ACROSS * capacity), (to_outer, None)]),
+    ]
+    first_up = [
+        (0, capacity, [(up, OWN * capacity)]),
+        (capacity, capacity, [(near, None)]),
+        (2 * capacity, capacity, [(inner_up, ACROSS * capacity), (to_outer, None)]),
+    ]
+    last = [(3 * capacity, capacity, [(to_inner, None), (forwarded, None)])]
+    first_parts = exchange(shrink(plan, row_blocks, first, choose, [forward_out]))
+    columns = [[0], [up_column], [0, up_column]]
+    out = combine(plan, LIVE * capacity, first_parts, base, first_up, columns, choose, cost=MIDDLE)
+    last_parts = exchange(shrink(plan, row_blocks, last, choose, [in_hbm(out)]))
     columns = [[up_column] * 2]
     return combine(plan, (LIVE + 3) * capacity, last_parts, base, last, columns, choose, out)
 

time: 95 us -> 78.1 us (0.82)
  starting transfers between devices: 26.4 us -> 19.3 us
  Pallas kernels: 27.3 us -> 21.8 us
  waiting for transfers between devices: 39.7 us -> 35.9 us
  local copies, waits for them, and re-layouts: 1.07 us -> 0.01 us
    ppermute x7 -> x6, waiting for transfers between devices: 28.5 us -> 21 us  [across(): return lax.ppermute(value, 'pool', pairs)]
    ppermute x7 -> x6, starting transfers between devices: 10.8 us -> 6.75 us  [across(): return lax.ppermute(value, 'pool', pairs)]
    ppermute x16 -> x13, waiting for transfers between devices: 11.3 us -> 15 us  [swap(): return lax.ppermute(value, axis, pairs)]
    pallas_call x1, Pallas kernels: 11.4 us -> 8.18 us  [base_chunks(): pl.pallas_call(functools.partial(base_kernel, half), grid_spec=pltpu.Pref...]
    ppermute x16 -> x13, starting transfers between devices: 15.6 us -> 12.6 us  [swap(): return lax.ppermute(value, axis, pairs)]
    pallas_call x2 -> x1, Pallas kernels: 2.49 us -> 0.64 us  [pack_panels(): pl.pallas_call(functools.partial(pack_kernel, starts, capacity), in_specs...]
    unnamed x10 -> x6, local copies, waits for them, and re-layouts: 1.07 us -> 0.01 us
    pallas_call x3 -> x2, Pallas kernels: 5.98 us -> 5.22 us  [combine(): pl.pallas_call(functools.partial(combine_kernel, shapes, choose, len(part...]
  transfers between devices with their start and end apart: 23 -> 19, of which waited for: 9 -> 8; matrix products, arithmetic and copies ran while one was open for 0% -> 1% of each run, Pallas kernels for 27% -> 24%
where the time goes in v5:
time: 78.1 us; the launch traced here: 77.9 us
  waiting for transfers between devices  35.9 us (46%)
  Pallas kernels  21.8 us (28%)
  starting transfers between devices  19.3 us (25%)
    ppermute x6, waiting for transfers between devices, across(): return lax.ppermute(value, 'pool', pairs)  21 us
    ppermute x13, waiting for transfers between devices, swap(): return lax.ppermute(value, axis, pairs)  15 us
    ppermute x13, starting transfers between devices, swap(): return lax.ppermute(value, axis, pairs)  12.6 us
    pallas_call x1, Pallas kernels, base_chunks(): pl.pallas_call(functools.partial(base_kernel, half), grid_spec=pltpu.Pref...  8.18 us
    ppermute x6, starting transfers between devices, across(): return lax.ppermute(value, 'pool', pairs)  6.75 us
    pallas_call x2, Pallas kernels, combine(): pl.pallas_call(functools.partial(combine_kernel, shapes, choose, len(part...  5.22 us
    pallas_call x2, Pallas kernels, shrink(): pl.pallas_call(functools.partial(shrink_kernel, shapes, choose), grid_spe...  4.05 us
    pallas_call x1, Pallas kernels, make_plan(): pl.pallas_call(functools.partial(plan_kernel, capacity), in_specs=[ANY] *...  3.51 us
  transfers between devices with their start and end apart: 19, of which 8 were waited for; matrix products, arithmetic and copies ran while one was open for 1% of the time, Pallas kernels for 24%

profile of v5, /device:TPU:0, one launch (start us, length us, event | category | flops | bytes accessed | tf_op | source)
XLA Modules:
  0.0 77.9 jit_solution(14847851957133727929)
XLA Ops:
  0.0 3.0 %collective-permute-start = (s32[1,8]{1,0:T(1,128)}, s32[1,8]{1,0:T(1,128)S(1)}, u32[]{:S(2)}, u32[]{:S(2)}) collective-permute-start(s32[1,8]{1,0:T(1,128)} %refs_0_.1), channel_id=1, source_target_pairs={{0,4},{4,0},{8,12},{12,8},{1,5},{5,1},{9,13},{13,9},{2,6},{6,2},{1... | collective-permute-start | bytes 104 | tf_op jit(solution)/shard_map/ppermute | solution.py:27
  3.0 2.6 %collective-permute-start.1 = (s32[1,8]{1,0:T(1,128)}, s32[1,8]{1,0:T(1,128)S(1)}, u32[]{:S(2)}, u32[]{:S(2)}) collective-permute-start(s32[1,8]{1,0:T(1,128)} %refs_0_.1), channel_id=1, source_target_pairs={{0,8},{4,12},{8,0},{12,4},{1,9},{5,13},{9,1},{13,5},{2,10},{6,14},... | collective-permute-start | bytes 104 | tf_op jit(solution)/shard_map/ppermute | solution.py:27
  5.6 0.0 collective-permute-start.2
  5.6 0.7 collective-permute-start.4
  6.3 0.7 broadcast_xor_fusion.chunks_ref
  7.0 0.0 collective-permute-done.refs_1_
  7.0 0.6 collective-permute-done.1.refs_2_
  7.6 3.5 %collective-permute-done.2.refs_3_ = s32[1,8]{1,0:T(1,128)S(1)} collective-permute-done((s32[1,8]{1,0:T(1,128)}, s32[1,8]{1,0:T(1,128)S(1)}, u32[]{:S(2)}, u32[]{:S(2)}) %collective-permute-start.2) | collective-permute-done | bytes 64 | tf_op jit(solution)/shard_map/ppermute | solution.py:27
  11.1 3.5 %shard_map.82 = (bf16[2,64,2304]{2,1,0:T(8,128)(2,1)S(1)}, bf16[2,64,2304]{2,1,0:T(8,128)(2,1)S(1)}, bf16[2,64,2304]{2,1,0:T(8,128)(2,1)S(1)}, s32[24]{0:T(128)S(1)}) custom-call(s32[1,8]{1,0:T(1,128)} %refs_0_.1, s32[1,8]{1,0:T(1,128)S(1)} %collective-permute-done.refs_1_, s32[1,8]{1,0:T(1,128)S(1)} %collective-permute-done.1.refs_2_, ...), custom_call_target="tpu_custom_call" | custom-call | flops 4000000000 | tf_op jit(solution)/shard_map/pallas_call | solution.py:205
  14.6 0.0 copy-start.2
  14.6 8.2 %shard_map.83 = (f32[2,384,256]{2,1,0:T(8,128)S(1)}, f32[2,384,256]{2,1,0:T(8,128)S(1)}, f32[2,256,256]{2,1,0:T(8,128)S(1)}, f32[2,1024,256]{2,1,0:T(8,128)S(1)}) custom-call(s32[4]{0:T(128)S(1)} %broadcast_xor_fusion.chunks_ref, bf16[1024,2048]{1,0:T(8,128)(2,1)} %tokens_ref.1, bf16[2048,1024]{1,0:T(8,128)(2,1)} %weight_ref.1, ...), custom_call_target="tpu_custom_call" | custom-call | tf_op jit(solution)/shard_map/pallas_call | solution.py:65
  22.8 0.1 collective-permute-start.6
  22.9 0.5 collective-permute-start.7
  23.4 0.1 collective-permute-start.8
  23.5 0.0 copy-done.2
  23.5 0.7 collective-permute-start.5
  24.1 2.9 %collective-permute-done.8.refs_2_ = f32[2,256,256]{2,1,0:T(8,128)S(1)} collective-permute-done((f32[2,256,256]{2,1,0:T(8,128)S(1)}, f32[2,256,256]{2,1,0:T(8,128)S(1)}, u32[]{:S(2)}, u32[]{:S(2)}) %collective-permute-start.8) | collective-permute-done | bytes 524320 | tf_op jit(solution)/shard_map/ppermute | solution.py:27
  27.0 0.0 collective-permute-start.10
  27.0 0.0 collective-permute-done.6.refs_0_
  27.0 2.5 %collective-permute-start.11 = (bf16[2,64,2304]{2,1,0:T(8,128)(2,1)S(1)}, bf16[2,64,2304]{2,1,0:T(8,128)(2,1)S(1)}, u32[]{:S(2)}, u32[]{:S(2)}) collective-permute-start(bf16[2,64,2304]{2,1,0:T(8,128)(2,1)S(1)} %get-tuple-element.23), channel_id=1, source_target_pairs={{0,12},{12,0},{1,13},{13,1},{2,14},{14,2},{3,15},{15,3},{16,28},{2... | collective-permute-start | bytes 1769480 | tf_op jit(solution)/shard_map/ppermute | solution.py:401
  29.5 0.0 collective-permute-done.7.refs_1_
  29.6 1.3 %collective-permute-start.3 = (bf16[2,64,2304]{2,1,0:T(8,128)(2,1)S(1)}, bf16[2,64,2304]{2,1,0:T(8,128)(2,1)S(1)}, u32[]{:S(2)}, u32[]{:S(2)}) collective-permute-start(bf16[2,64,2304]{2,1,0:T(8,128)(2,1)S(1)} %get-tuple-element.16), channel_id=1, source_target_pairs={{0,8},{12,4},{1,9},{13,5},{2,10},{14,6},{3,11},{15,7},{16,24},{28,... | collective-permute-start | bytes 1769480 | tf_op jit(solution)/shard_map/ppermute | solution.py:401
  30.9 0.2 shard_map.84
  31.1 0.0 collective-permute-done.5.up_ref.refs_8_
  31.1 1.6 %collective-permute-start.15 = (f32[1,1024,256]{2,1,0:T(8,128)S(1)}, f32[1,1024,256]{2,1,0:T(8,128)S(1)}, u32[]{:S(2)}, u32[]{:S(2)}) collective-permute-start(f32[1,1024,256]{2,1,0:T(8,128)S(1)} %get-tuple-element.24), channel_id=1, source_target_pairs={{0,2},{1,3},{2,0},{3,1},{4,6},{5,7},{6,4},{7,5},{8,10},{9,11},{10,... | collective-permute-start | bytes 3145736 | tf_op jit(solution)/shard_map/ppermute | solution.py:27
  32.7 0.0 collective-permute-done.4.down_ref.refs_2_
  32.7 0.0 copy-start
  32.7 0.0 copy-start.1
  32.7 0.6 shard_map.85.refs_4_
  33.3 1.6 %collective-permute-start.9 = (bf16[2,64,2304]{2,1,0:T(8,128)(2,1)S(1)}, bf16[2,64,2304]{2,1,0:T(8,128)(2,1)S(1)}, u32[]{:S(2)}, u32[]{:S(2)}) collective-permute-start(bf16[2,64,2304]{2,1,0:T(8,128)(2,1)S(1)} %shard_map.85.refs_4_), channel_id=1, source_target_pairs={{4,0},{8,12},{5,1},{9,13},{6,2},{10,14},{7,3},{11,15},{20,16},{24,... | collective-permute-start | bytes 1769480 | tf_op jit(solution)/shard_map/ppermute | solution.py:401
  34.9 20.9 %collective-permute-done.10.refs_1_.refs_7_ = bf16[2,64,2304]{2,1,0:T(8,128)(2,1)S(1)} collective-permute-done((bf16[2,64,2304]{2,1,0:T(8,128)(2,1)S(1)}, bf16[2,64,2304]{2,1,0:T(8,128)(2,1)S(1)}, u32[]{:S(2)}, u32[]{:S(2)}) %collective-permute-start.10) | collective-permute-done | bytes 589856 | tf_op jit(solution)/shard_map/ppermute | solution.py:401
  55.8 0.0 collective-permute-done.11.refs_3_.refs_9_
  55.8 0.0 copy-done
  55.9 0.0 copy-done.1
  55.9 2.7 %shard_map.86.refs_0_ = bf16[6,64,128]{2,1,0:T(8,128)(2,1)S(1)} custom-call(s32[24]{0:T(128)S(1)} %get-tuple-element.15.plan_ref, bf16[8,128,2048]{2,1,0:T(8,128)(2,1)S(1)} %bitcast.4, bf16[4,64,2048]{2,1,0:T(8,128)(2,1)S(1)} %bitcast.13, bf16[2,64,2304]{2,1,0:T(8,128)(2,1)S(1)} %collective-permute-done.10.refs_1_.refs_7_, ...), custom_call_target="tpu_custom_call" | custom-call | tf_op jit(solution)/shard_map/pallas_call | solution.py:323
  58.6 0.1 collective-permute-start.12
  58.7 1.5 %collective-permute-start.13 = (bf16[6,64,128]{2,1,0:T(8,128)(2,1)S(1)}, bf16[6,64,128]{2,1,0:T(8,128)(2,1)S(1)}, u32[]{:S(2)}, u32[]{:S(2)}) collective-permute-start(bf16[6,64,128]{2,1,0:T(8,128)(2,1)S(1)} %shard_map.86.refs_0_), channel_id=1, source_target_pairs={{0,2},{1,3},{2,0},{3,1},{4,6},{5,7},{6,4},{7,5},{8,10},{9,11},{10,... | collective-permute-start | bytes 294920 | tf_op jit(solution)/shard_map/ppermute | solution.py:27
  60.2 0.0 collective-permute-done.12.refs_1_
  60.2 1.0 %collective-permute-start.14 = (bf16[6,64,128]{2,1,0:T(8,128)(2,1)S(1)}, bf16[6,64,128]{2,1,0:T(8,128)(2,1)S(1)}, u32[]{:S(2)}, u32[]{:S(2)}) collective-permute-start(bf16[6,64,128]{2,1,0:T(8,128)(2,1)S(1)} %shard_map.86.refs_0_), channel_id=1, source_target_pairs={{0,3},{1,2},{2,1},{3,0},{4,7},{5,6},{6,5},{7,4},{8,11},{9,10},{10,... | collective-permute-start | bytes 294920 | tf_op jit(solution)/shard_map/ppermute | solution.py:27
  61.2 3.1 %collective-permute-done.13.refs_2_ = bf16[6,64,128]{2,1,0:T(8,128)(2,1)S(1)} collective-permute-done((bf16[6,64,128]{2,1,0:T(8,128)(2,1)S(1)}, bf16[6,64,128]{2,1,0:T(8,128)(2,1)S(1)}, u32[]{:S(2)}, u32[]{:S(2)}) %collective-permute-start.13) | collective-permute-done | bytes 98336 | tf_op jit(solution)/shard_map/ppermute | solution.py:27
  64.3 1.2 %collective-permute-done.14.refs_3_ = bf16[6,64,128]{2,1,0:T(8,128)(2,1)S(1)} collective-permute-done((bf16[6,64,128]{2,1,0:T(8,128)(2,1)S(1)}, bf16[6,64,128]{2,1,0:T(8,128)(2,1)S(1)}, u32[]{:S(2)}, u32[]{:S(2)}) %collective-permute-start.14) | collective-permute-done | bytes 98336 | tf_op jit(solution)/shard_map/ppermute | solution.py:27
  65.6 0.0 collective-permute-done.15
  65.6 3.5 %shard_map.87.refs_2_.refs_8_ = bf16[1024,256]{1,0:T(8,128)(2,1)} custom-call(s32[24]{0:T(128)S(1)} %get-tuple-element.15.plan_ref, bf16[6,64,128]{2,1,0:T(8,128)(2,1)S(1)} %shard_map.86.refs_0_, bf16[6,64,128]{2,1,0:T(8,128)(2,1)S(1)} %collective-permute-done.12.refs_1_, bf16[6,64,128]{2,1,0:T(8,128)(2,1)S(1)} %collective-permute-done.13.refs_2_, ...), custom_call_target="tpu_custom_call" | custom-call | tf_op jit(solution)/shard_map/pallas_call | solution.py:382
  69.1 0.0 collective-permute-done.3.refs_0_.refs_6_
  69.1 0.0 collective-permute-done.9.refs_1_.refs_7_
  69.1 1.3 %shard_map.88.refs_0_ = bf16[2,64,128]{2,1,0:T(8,128)(2,1)S(1)} custom-call(s32[24]{0:T(128)S(1)} %get-tuple-element.15.plan_ref, bf16[8,128,2048]{2,1,0:T(8,128)(2,1)S(1)} %bitcast.5, bf16[2,64,2304]{2,1,0:T(8,128)(2,1)S(1)} %collective-permute-done.3.refs_0_.refs_6_, bf16[2,64,2304]{2,1,0:T(8,128)(2,1)S(1)} %collective-permute-done.9.refs_1_.refs_7_, ...), custom_call_target="tpu_custom_call" | custom-call | tf_op jit(solution)/shard_map/pallas_call | solution.py:323
  70.4 0.6 collective-permute-start.16
  71.0 1.5 %collective-permute-start.17 = (bf16[2,64,128]{2,1,0:T(8,128)(2,1)S(1)}, bf16[2,64,128]{2,1,0:T(8,128)(2,1)S(1)}, u32[]{:S(2)}, u32[]{:S(2)}) collective-permute-start(bf16[2,64,128]{2,1,0:T(8,128)(2,1)S(1)} %shard_map.88.refs_0_), channel_id=1, source_target_pairs={{0,2},{1,3},{2,0},{3,1},{4,6},{5,7},{6,4},{7,5},{8,10},{9,11},{10,... | collective-permute-start | bytes 98312 | tf_op jit(solution)/shard_map/ppermute | solution.py:27
  72.5 0.0 collective-permute-start.18
  72.5 0.0 collective-permute-done.16.refs_1_
  72.5 2.4 %collective-permute-done.17.refs_2_ = bf16[2,64,128]{2,1,0:T(8,128)(2,1)S(1)} collective-permute-done((bf16[2,64,128]{2,1,0:T(8,128)(2,1)S(1)}, bf16[2,64,128]{2,1,0:T(8,128)(2,1)S(1)}, u32[]{:S(2)}, u32[]{:S(2)}) %collective-permute-start.17) | collective-permute-done | bytes 32800 | tf_op jit(solution)/shard_map/ppermute | solution.py:27
  74.9 1.2 %collective-permute-done.18.refs_3_ = bf16[2,64,128]{2,1,0:T(8,128)(2,1)S(1)} collective-permute-done((bf16[2,64,128]{2,1,0:T(8,128)(2,1)S(1)}, bf16[2,64,128]{2,1,0:T(8,128)(2,1)S(1)}, u32[]{:S(2)}, u32[]{:S(2)}) %collective-permute-start.18) | collective-permute-done | bytes 32800 | tf_op jit(solution)/shard_map/ppermute | solution.py:27
  76.2 1.7 %shard_map.89 = bf16[1024,256]{1,0:T(8,128)(2,1)} custom-call(s32[24]{0:T(128)S(1)} %get-tuple-element.15.plan_ref, bf16[2,64,128]{2,1,0:T(8,128)(2,1)S(1)} %shard_map.88.refs_0_, bf16[2,64,128]{2,1,0:T(8,128)(2,1)S(1)} %collective-permute-done.16.refs_1_, bf16[2,64,128]{2,1,0:T(8,128)(2,1)S(1)} %collective-permute-done.17.refs_2_, ...), custom_call_target="tpu_custom_call", output_to_operand_aliasing={{}: (9, {})} | custom-call | tf_op jit(solution)/shard_map/pallas_call | solution.py:382
Async XLA Ops:
  0.0 7.0 %collective-permute-start = (s32[1,8]{1,0:T(1,128)}, s32[1,8]{1,0:T(1,128)S(1)}, u32[]{:S(2)}, u32[]{:S(2)}) collective-permute-start(s32[1,8]{1,0:T(1,128)} %refs_0_.1), channel_id=1, source_target_pairs={{0,4},{4,0},{8,12},{12,8},{1,5},{5,1},{9,13},{13,9},{2,6},{6,2},{1... | collective-permute-start | bytes 104 | tf_op jit(solution)/shard_map/ppermute | solution.py:27
  3.0 4.6 %collective-permute-start.1 = (s32[1,8]{1,0:T(1,128)}, s32[1,8]{1,0:T(1,128)S(1)}, u32[]{:S(2)}, u32[]{:S(2)}) collective-permute-start(s32[1,8]{1,0:T(1,128)} %refs_0_.1), channel_id=1, source_target_pairs={{0,8},{4,12},{8,0},{12,4},{1,9},{5,13},{9,1},{13,5},{2,10},{6,14},... | collective-permute-start | bytes 104 | tf_op jit(solution)/shard_map/ppermute | solution.py:27
  5.6 5.5 %collective-permute-start.2 = (s32[1,8]{1,0:T(1,128)}, s32[1,8]{1,0:T(1,128)S(1)}, u32[]{:S(2)}, u32[]{:S(2)}) collective-permute-start(s32[1,8]{1,0:T(1,128)} %refs_0_.1), channel_id=1, source_target_pairs={{0,12},{4,8},{8,4},{12,0},{1,13},{5,9},{9,5},{13,1},{2,14},{6,10},... | collective-permute-start | bytes 104 | tf_op jit(solution)/shard_map/ppermute | solution.py:27
  5.6 27.1 %collective-permute-start.4 = (bf16[4,64,2048]{2,1,0:T(8,128)(2,1)}, bf16[4,64,2048]{2,1,0:T(8,128)(2,1)S(1)}, u32[]{:S(2)}, u32[]{:S(2)}) collective-permute-start(bf16[4,64,2048]{2,1,0:T(8,128)(2,1)} %bitcast.11), channel_id=1, source_target_pairs={{4,8},{8,4},{5,9},{9,5},{6,10},{10,6},{7,11},{11,7},{20,24},{24,20... | collective-permute-start | bytes 3145736 | tf_op jit(solution)/shard_map/ppermute | solution.py:401
  14.6 8.9 %copy-start.2 = (bf16[4,64,256]{2,1,0:T(8,128)(2,1)S(1)}, bf16[4,64,256]{2,1,0:T(8,128)(2,1)}, u32[]{:S(2)}) copy-start(bf16[4,64,256]{2,1,0:T(8,128)(2,1)} %refs_6_.1) | copy-start | bytes 393220
  22.8 4.2 %collective-permute-start.6 = (f32[2,384,256]{2,1,0:T(8,128)S(1)}, f32[2,384,256]{2,1,0:T(8,128)S(1)}, u32[]{:S(2)}, u32[]{:S(2)}) collective-permute-start(f32[2,384,256]{2,1,0:T(8,128)S(1)} %get-tuple-element.19), channel_id=1, source_target_pairs={{0,1},{1,0},{2,3},{3,2},{4,5},{5,4},{6,7},{7,6},{8,9},{9,8},{10,11... | collective-permute-start | bytes 2359304 | tf_op jit(solution)/shard_map/ppermute | solution.py:27
  22.9 6.7 %collective-permute-start.7 = (f32[2,384,256]{2,1,0:T(8,128)S(1)}, f32[2,384,256]{2,1,0:T(8,128)S(1)}, u32[]{:S(2)}, u32[]{:S(2)}) collective-permute-start(f32[2,384,256]{2,1,0:T(8,128)S(1)} %get-tuple-element.20), channel_id=1, source_target_pairs={{0,1},{1,0},{2,3},{3,2},{4,5},{5,4},{6,7},{7,6},{8,9},{9,8},{10,11... | collective-permute-start | bytes 2359304 | tf_op jit(solution)/shard_map/ppermute | solution.py:27
  23.4 3.6 %collective-permute-start.8 = (f32[2,256,256]{2,1,0:T(8,128)S(1)}, f32[2,256,256]{2,1,0:T(8,128)S(1)}, u32[]{:S(2)}, u32[]{:S(2)}) collective-permute-start(f32[2,256,256]{2,1,0:T(8,128)S(1)} %get-tuple-element.21), channel_id=1, source_target_pairs={{0,1},{1,0},{2,3},{3,2},{4,5},{5,4},{6,7},{7,6},{8,9},{9,8},{10,11... | collective-permute-start | bytes 1572872 | tf_op jit(solution)/shard_map/ppermute | solution.py:27
  23.5 7.6 %collective-permute-start.5 = (bf16[4,64,256]{2,1,0:T(8,128)(2,1)S(1)}, bf16[4,64,256]{2,1,0:T(8,128)(2,1)S(1)}, u32[]{:S(2)}, u32[]{:S(2)}) collective-permute-start(bf16[4,64,256]{2,1,0:T(8,128)(2,1)S(1)} %copy-done.2), channel_id=1, source_target_pairs={{4,8},{8,4},{5,9},{9,5},{6,10},{10,6},{7,11},{11,7},{20,24},{24,20... | collective-permute-start | bytes 393224 | tf_op jit(solution)/shard_map/ppermute | solution.py:401
  27.0 28.8 %collective-permute-start.10 = (bf16[2,64,2304]{2,1,0:T(8,128)(2,1)S(1)}, bf16[2,64,2304]{2,1,0:T(8,128)(2,1)S(1)}, u32[]{:S(2)}, u32[]{:S(2)}) collective-permute-start(bf16[2,64,2304]{2,1,0:T(8,128)(2,1)S(1)} %get-tuple-element.17.refs_0_), channel_id=1, source_target_pairs={{0,4},{4,0},{8,12},{12,8},{1,5},{5,1},{9,13},{13,9},{2,6},{6,2},{1... | collective-permute-start | bytes 1769480 | tf_op jit(solution)/shard_map/ppermute | solution.py:401
  27.0 28.8 %collective-permute-start.11 = (bf16[2,64,2304]{2,1,0:T(8,128)(2,1)S(1)}, bf16[2,64,2304]{2,1,0:T(8,128)(2,1)S(1)}, u32[]{:S(2)}, u32[]{:S(2)}) collective-permute-start(bf16[2,64,2304]{2,1,0:T(8,128)(2,1)S(1)} %get-tuple-element.23), channel_id=1, source_target_pairs={{0,12},{12,0},{1,13},{13,1},{2,14},{14,2},{3,15},{15,3},{16,28},{2... | collective-permute-start | bytes 1769480 | tf_op jit(solution)/shard_map/ppermute | solution.py:401
  29.6 39.5 %collective-permute-start.3 = (bf16[2,64,2304]{2,1,0:T(8,128)(2,1)S(1)}, bf16[2,64,2304]{2,1,0:T(8,128)(2,1)S(1)}, u32[]{:S(2)}, u32[]{:S(2)}) collective-permute-start(bf16[2,64,2304]{2,1,0:T(8,128)(2,1)S(1)} %get-tuple-element.16), channel_id=1, source_target_pairs={{0,8},{12,4},{1,9},{13,5},{2,10},{14,6},{3,11},{15,7},{16,24},{28,... | collective-permute-start | bytes 1769480 | tf_op jit(solution)/shard_map/ppermute | solution.py:401
  31.1 34.4 %collective-permute-start.15 = (f32[1,1024,256]{2,1,0:T(8,128)S(1)}, f32[1,1024,256]{2,1,0:T(8,128)S(1)}, u32[]{:S(2)}, u32[]{:S(2)}) collective-permute-start(f32[1,1024,256]{2,1,0:T(8,128)S(1)} %get-tuple-element.24), channel_id=1, source_target_pairs={{0,2},{1,3},{2,0},{3,1},{4,6},{5,7},{6,4},{7,5},{8,10},{9,11},{10,... | collective-permute-start | bytes 3145736 | tf_op jit(solution)/shard_map/ppermute | solution.py:27
  32.7 23.2 %copy-start = (bf16[1024,2048]{1,0:T(8,128)(2,1)S(1)}, bf16[1024,2048]{1,0:T(8,128)(2,1)}, u32[]{:S(2)}) copy-start(bf16[1024,2048]{1,0:T(8,128)(2,1)} %tokens_ref.1) | copy-start | bytes 12582916
  32.7 23.2 %copy-start.1 = (bf16[4,2048,64]{1,2,0:T(8,128)(2,1)S(1)}, bf16[4,2048,64]{1,2,0:T(8,128)(2,1)}, u32[]{:S(2)}) copy-start(bf16[4,2048,64]{1,2,0:T(8,128)(2,1)} %param.10) | copy-start | bytes 3145732
  33.3 35.7 %collective-permute-start.9 = (bf16[2,64,2304]{2,1,0:T(8,128)(2,1)S(1)}, bf16[2,64,2304]{2,1,0:T(8,128)(2,1)S(1)}, u32[]{:S(2)}, u32[]{:S(2)}) collective-permute-start(bf16[2,64,2304]{2,1,0:T(8,128)(2,1)S(1)} %shard_map.85.refs_4_), channel_id=1, source_target_pairs={{4,0},{8,12},{5,1},{9,13},{6,2},{10,14},{7,3},{11,15},{20,16},{24,... | collective-permute-start | bytes 1769480 | tf_op jit(solution)/shard_map/ppermute | solution.py:401
  58.6 1.6 %collective-permute-start.12 = (bf16[6,64,128]{2,1,0:T(8,128)(2,1)S(1)}, bf16[6,64,128]{2,1,0:T(8,128)(2,1)S(1)}, u32[]{:S(2)}, u32[]{:S(2)}) collective-permute-start(bf16[6,64,128]{2,1,0:T(8,128)(2,1)S(1)} %shard_map.86.refs_0_), channel_id=1, source_target_pairs={{0,1},{1,0},{2,3},{3,2},{4,5},{5,4},{6,7},{7,6},{8,9},{9,8},{10,11... | collective-permute-start | bytes 294920 | tf_op jit(solution)/shard_map/ppermute | solution.py:27
  58.7 5.7 %collective-permute-start.13 = (bf16[6,64,128]{2,1,0:T(8,128)(2,1)S(1)}, bf16[6,64,128]{2,1,0:T(8,128)(2,1)S(1)}, u32[]{:S(2)}, u32[]{:S(2)}) collective-permute-start(bf16[6,64,128]{2,1,0:T(8,128)(2,1)S(1)} %shard_map.86.refs_0_), channel_id=1, source_target_pairs={{0,2},{1,3},{2,0},{3,1},{4,6},{5,7},{6,4},{7,5},{8,10},{9,11},{10,... | collective-permute-start | bytes 294920 | tf_op jit(solution)/shard_map/ppermute | solution.py:27
  60.2 5.3 %collective-permute-start.14 = (bf16[6,64,128]{2,1,0:T(8,128)(2,1)S(1)}, bf16[6,64,128]{2,1,0:T(8,128)(2,1)S(1)}, u32[]{:S(2)}, u32[]{:S(2)}) collective-permute-start(bf16[6,64,128]{2,1,0:T(8,128)(2,1)S(1)} %shard_map.86.refs_0_), channel_id=1, source_target_pairs={{0,3},{1,2},{2,1},{3,0},{4,7},{5,6},{6,5},{7,4},{8,11},{9,10},{10,... | collective-permute-start | bytes 294920 | tf_op jit(solution)/shard_map/ppermute | solution.py:27
  70.4 2.1 %collective-permute-start.16 = (bf16[2,64,128]{2,1,0:T(8,128)(2,1)S(1)}, bf16[2,64,128]{2,1,0:T(8,128)(2,1)S(1)}, u32[]{:S(2)}, u32[]{:S(2)}) collective-permute-start(bf16[2,64,128]{2,1,0:T(8,128)(2,1)S(1)} %shard_map.88.refs_0_), channel_id=1, source_target_pairs={{0,1},{1,0},{2,3},{3,2},{4,5},{5,4},{6,7},{7,6},{8,9},{9,8},{10,11... | collective-permute-start | bytes 98312 | tf_op jit(solution)/shard_map/ppermute | solution.py:27
  71.0 3.9 %collective-permute-start.17 = (bf16[2,64,128]{2,1,0:T(8,128)(2,1)S(1)}, bf16[2,64,128]{2,1,0:T(8,128)(2,1)S(1)}, u32[]{:S(2)}, u32[]{:S(2)}) collective-permute-start(bf16[2,64,128]{2,1,0:T(8,128)(2,1)S(1)} %shard_map.88.refs_0_), channel_id=1, source_target_pairs={{0,2},{1,3},{2,0},{3,1},{4,6},{5,7},{6,4},{7,5},{8,10},{9,11},{10,... | collective-permute-start | bytes 98312 | tf_op jit(solution)/shard_map/ppermute | solution.py:27
  72.5 3.7 %collective-permute-start.18 = (bf16[2,64,128]{2,1,0:T(8,128)(2,1)S(1)}, bf16[2,64,128]{2,1,0:T(8,128)(2,1)S(1)}, u32[]{:S(2)}, u32[]{:S(2)}) collective-permute-start(bf16[2,64,128]{2,1,0:T(8,128)(2,1)S(1)} %shard_map.88.refs_0_), channel_id=1, source_target_pairs={{0,3},{1,2},{2,1},{3,0},{4,7},{5,6},{6,5},{7,4},{8,11},{9,10},{10,... | collective-permute-start | bytes 98312 | tf_op jit(solution)/shard_map/ppermute | solution.py:27

commit v6 on v5

--- a/solution.py
+++ b/solution.py
@@ -11,7 +11,7 @@
 ROW_TILE = 256
 PARAMS = pltpu.CompilerParams(vmem_limit_bytes=16 * 1024 * 1024)
 NO_COST = pl.CostEstimate(flops=0, bytes_accessed=0, transcendentals=0)
-SHORT = pl.CostEstimate(flops=4 * 10**9, bytes_accessed=0, transcendentals=0)
+SHORT = pl.CostEstimate(flops=10 * 10**9, bytes_accessed=0, transcendentals=0)
 MIDDLE = pl.CostEstimate(flops=0 * 10**9, bytes_accessed=0, transcendentals=0)
 LONG = pl.CostEstimate(flops=6 * 10**9, bytes_accessed=0, transcendentals=0)
 ANY = pl.BlockSpec(memory_space=pl.ANY)
@@ -34,7 +34,7 @@
 
 def base_kernel(half, chunks_ref, tokens_ref, weight_ref, *refs):
     del chunks_ref
-    *sent_refs, kept_ref = refs[-1 - len(piece_rows(tokens_ref.shape[0])) :]
+    *sent_refs, kept_ref = refs
 
     def write(out_ref, first, size):
         for start in range(0, size, ROW_TILE):
@@ -57,7 +57,7 @@
         write(kept_ref, 0, kept_ref.shape[1])
 
 
-def base_chunks(tokens, weight, order, width, after):
+def base_chunks(tokens, weight, order, width):
     rows, depth = tokens.shape
     half = len(order) // 2
     sizes = piece_rows(rows)
@@ -70,8 +70,7 @@
             in_specs=[
                 pl.BlockSpec(tokens.shape, lambda i, c: (0, 0), pipeline_mode=pl.Buffered(1)),
                 pl.BlockSpec((depth, width), lambda i, c: (0, c[i])),
-            ]
-            + [ANY] * len(after),
+            ],
             out_specs=[
                 pl.BlockSpec((1, size, width), lambda i, c: (jnp.minimum(i, half - 1), 0, 0))
                 for size in sizes
@@ -83,7 +82,7 @@
         ],
         compiler_params=PARAMS,
         cost_estimate=NO_COST,
-    )(chunks, in_hbm(tokens), in_hbm(weight), *after)
+    )(chunks, in_hbm(tokens), in_hbm(weight))
     return sent, kept
 
 
@@ -110,14 +109,17 @@
     )(kept, *arrived)
 
 
-def base_sum(tokens, weight, width, after):
+def base_parts(tokens, weight, width):
     size = lax.axis_size("tensor")
     kept_order = [k for k in range(size) if not k & 1]
     kept_order.sort(key=lambda k: [k >> bit & 1 for bit in range(1, size.bit_length())])
-    sent, kept = base_chunks(tokens, weight, [k ^ 1 for k in kept_order] + kept_order, width, after)
+    return base_chunks(tokens, weight, [k ^ 1 for k in kept_order] + kept_order, width)
+
+
+def base_sum(sent, kept):
     arrived = [swap(piece, "tensor", 1) for piece in sent]
     distance = 2
-    while distance < size:
+    while distance < lax.axis_size("tensor"):
         sent, kept = add_halves(kept, arrived)
         arrived = [swap(sent, "tensor", distance)]
         distance *= 2
@@ -154,25 +156,19 @@
     return copies
 
 
-def plan_kernel(capacity, *refs):
-    sources, down_ref, up_ref, out_refs, plan_ref = refs[:6], *refs[6:8], refs[8:11], refs[11]
-    scalars, scalar_sems, sems = refs[12:18], *refs[18:]
+def plan_kernel(capacity, holder_slots, *refs):
+    sources, plan_ref, scalars, sems = refs[:6], refs[-8], refs[-7:-1], refs[-1]
     loads = [
-        pltpu.make_async_copy(source, scalar, scalar_sems.at[i])
+        pltpu.make_async_copy(source, scalar, sems.at[i])
         for i, (source, scalar) in enumerate(zip(sources, scalars))
     ]
     for load in run_copies(loads):
         load.wait()
     names_ref, first_ref, second_ref, third_ref, table_ref, live_ref = scalars
     here = lax.axis_index("pool")
-    holder_slots = down_ref.shape[0]
     find = functools.partial(
         pick, table_ref=table_ref, holder_slots=holder_slots, count=capacity
     )
-    copies = []
-    for i, asked_ref in enumerate((third_ref, second_ref, first_ref)):
-        for k, slot in enumerate(find(asked_ref, holder=here)[1]):
-            copies += run_copies(panel_copies(k, slot, down_ref, up_ref, out_refs[i], sems.at[i]))
     inner = (here == 1) | (here == 2)
     own = find(names_ref, holder=here)
     near = find(names_ref, holder=here ^ 1)
@@ -185,6 +181,9 @@
         late[0],
         own[1],
         across[1],
+        find(first_ref, holder=here)[1],
+        find(second_ref, holder=here)[1],
+        find(third_ref, holder=here)[1],
         find(first_ref, holder=here ^ 3)[1],
         [inner.astype(jnp.int32)] * capacity,
         *[[live_ref[0, block] for block in phase[0]] for phase in (own, near, across, late)],
@@ -192,30 +191,23 @@
     for number, row in enumerate(rows):
         for k in range(capacity):
             plan_ref[number * capacity + k] = row[k]
-    for copy in copies:
-        copy.wait()
-
-
-OWN, ACROSS, FORWARD, INNER, LIVE, PLAN_ROWS = 4, 5, 6, 7, 8, 12
-
-
-def make_plan(names, others, table, live, down, up, capacity):
-    rank, depth = down.shape[1:]
-    width = up.shape[2]
+
+
+OWN, ACROSS, NEAR, TO_INNER, TO_OUTER, FORWARD, INNER, LIVE, PLAN_ROWS = 4, 5, 6, 7, 8, 9, 10, 11, 15
+
+
+def make_plan(names, others, table, live, holder_slots, capacity, after):
     return pl.pallas_call(
-        functools.partial(plan_kernel, capacity),
-        in_specs=[ANY] * 8,
-        out_specs=[ANY] * 3 + [SMEM],
-        out_shape=[jax.ShapeDtypeStruct((capacity, rank, depth + width), down.dtype)] * 3
-        + [
-            jax.ShapeDtypeStruct((PLAN_ROWS * capacity,), jnp.int32),
-        ],
+        functools.partial(plan_kernel, capacity, holder_slots),
+        in_specs=[ANY] * (6 + len(after)),
+        out_specs=SMEM,
+        out_shape=jax.ShapeDtypeStruct((PLAN_ROWS * capacity,), jnp.int32),
         scratch_shapes=[pltpu.SMEM(names.shape, jnp.int32)] * 4
         + [pltpu.SMEM(table.shape, jnp.int32), pltpu.SMEM(live.shape, jnp.int32)]
-        + [pltpu.SemaphoreType.DMA((6,)), pltpu.SemaphoreType.DMA((3, capacity, 2))],
+        + [pltpu.SemaphoreType.DMA((6,))],
         compiler_params=PARAMS,
         cost_estimate=SHORT,
-    )(in_hbm(names), *others, *[in_hbm(a) for a in (table, live, down, up)])
+    )(in_hbm(names), *others, in_hbm(table), in_hbm(live), *after)
 
 
 def pack_kernel(starts, capacity, plan_ref, down_ref, up_ref, *rest):
@@ -403,36 +395,43 @@
     others = [swap(names, "pool", m) for m in range(1, 4)]
     inner_down = across(down, [(1, 2), (2, 1)])
     inner_up = across(up, [(1, 2), (2, 1)])
-    outer_out, inner_out, near_out, plan = make_plan(
-        names, others, table, live, down, up, capacity
+    sent, kept = base_parts(tokens, weight, up.shape[2])
+    plan = make_plan(names, others, table, live, down.shape[0], capacity, [inner_up])
+    near_out, outer_out, inner_out = pack_panels(
+        plan,
+        [NEAR * capacity, TO_OUTER * capacity, TO_INNER * capacity],
+        capacity,
+        in_hbm(down),
+        in_hbm(up),
+        sent[-1:],
     )
+    near = across(near_out, [(0, 1), (1, 0), (2, 3), (3, 2)])
     to_outer = across(outer_out, [(0, 3), (3, 0)])
     to_inner = across(inner_out, [(0, 2), (3, 1)])
-    near = across(near_out, [(0, 1), (1, 0), (2, 3), (3, 2)])
-    base = base_sum(tokens, weight, up.shape[2], [near_out])
+    base = base_sum(sent, kept)
     (forward_out,) = pack_panels(
         plan, [FORWARD * capacity], capacity, inner_down, inner_up, [base[0]], LONG
     )
     forwarded = across(forward_out, [(1, 0), (2, 3)])
 
     choose = INNER * capacity
-    first = [
-        (0, capacity, [(down, OWN * capacity)]),
-        (capacity, capacity, [(near, None)]),
-        (2 * capacity, capacity, [(inner_down, ACROSS * capacity), (to_outer, None)]),
-    ]
-    first_up = [
-        (0, capacity, [(up, OWN * capacity)]),
-        (capacity, capacity, [(near, None)]),
-        (2 * capacity, capacity, [(inner_up, ACROSS * capacity), (to_outer, None)]),
-    ]
+    first = [(0, capacity, [(down, OWN * capacity)]), (capacity, capacity, [(near, None)])]
+    first_up = [(0, capacity, [(up, OWN * capacity)]), first[1]]
+    middle = [(2 * capacity, capacity, [(inner_down, ACROSS * capacity), (to_outer, None)])]
+    middle_up = [(2 * capacity, capacity, [(inner_up, ACROSS * capacity), (to_outer, None)])]
     last = [(3 * capacity, capacity, [(to_inner, None), (forwarded, None)])]
+
+    def write(number, parts, phases, columns, out, cost=None):
+        live_row = (LIVE + number) * capacity
+        return combine(plan, live_row, parts, base, phases, columns, choose, out, cost=cost)
+
     first_parts = exchange(shrink(plan, row_blocks, first, choose, [forward_out]))
-    columns = [[0], [up_column], [0, up_column]]
-    out = combine(plan, LIVE * capacity, first_parts, base, first_up, columns, choose, cost=MIDDLE)
-    last_parts = exchange(shrink(plan, row_blocks, last, choose, [in_hbm(out)]))
-    columns = [[up_column] * 2]
-    return combine(plan, (LIVE + 3) * capacity, last_parts, base, last, columns, choose, out)
+    out = write(0, first_parts, first_up, [[0], [up_column]], None, MIDDLE)
+    middle_part = shrink(plan, row_blocks, middle, choose, [in_hbm(out)])
+    middle_parts = exchange(middle_part)
+    last_parts = exchange(shrink(plan, row_blocks, last, choose, [middle_part]))
+    out = write(2, middle_parts, middle_up, [[0, up_column]], out)
+    return write(3, last_parts, last, [[up_column] * 2], out)
 
 
 def on_any_pool(tokens, weight, row_blocks, down, up, names, table, live, capacity):
@@ -457,7 +456,7 @@
     ranks = jnp.sum(earlier.astype(jnp.int32), axis=1)
     places = lax.rem(here - owners + pool_size, pool_size) * capacity + ranks
     plan = jnp.concatenate([blocks, places, live[0]])
-    base = base_sum(tokens, weight, up.shape[2], [])
+    base = base_sum(*base_parts(tokens, weight, up.shape[2]))
     phases = [(0, blocks.shape[0], [(arrived, blocks.shape[0])])]
     parts = exchange(shrink(plan, row_blocks, phases, 0))
     live_row = 2 * blocks.shape[0]

time: 78.1 us -> 76.6 us (0.981)
  waiting for transfers between devices: 35.9 us -> 24.7 us
  starting transfers between devices: 19.3 us -> 27.1 us
  Pallas kernels: 21.8 us -> 23.7 us
    ppermute x6, waiting for transfers between devices: 21 us -> 4.38 us  [across(): return lax.ppermute(value, 'pool', pairs)]
    ppermute x6, starting transfers between devices: 6.75 us -> 13.7 us  [across(): return lax.ppermute(value, 'pool', pairs)]
    ppermute x13 -> x16, waiting for transfers between devices: 15 us -> 20.3 us  [swap(): return lax.ppermute(value, axis, pairs)]
    pallas_call x1 -> x2, Pallas kernels: 0.64 us -> 3.15 us  [pack_panels(): pl.pallas_call(functools.partial(pack_kernel, starts, capacity), in_specs...]
    pallas_call x1, Pallas kernels: 3.51 us -> 1.66 us  [make_plan(): pl.pallas_call(functools.partial(plan_kernel, capacity, holder_slots), in...]
    ppermute x13 -> x16, starting transfers between devices: 12.6 us -> 13.4 us  [swap(): return lax.ppermute(value, axis, pairs)]
    pallas_call x2 -> x3, Pallas kernels: 5.22 us -> 5.98 us  [combine(): pl.pallas_call(functools.partial(combine_kernel, shapes, choose, len(part...]
    pallas_call x2 -> x3, Pallas kernels: 4.05 us -> 4.51 us  [shrink(): pl.pallas_call(functools.partial(shrink_kernel, shapes, choose), grid_spe...]
  transfers between devices with their start and end apart: 19 -> 22, of which waited for: 8 -> 6; matrix products, arithmetic and copies ran while one was open for 1% -> 1% of each run, Pallas kernels for 24% -> 29%
where the time goes in v6:
time: 76.6 us; the launch traced here: 76.4 us
  starting transfers between devices  27.1 us (35%)
  waiting for transfers between devices  24.7 us (32%)
  Pallas kernels  23.7 us (31%)
    ppermute x16, waiting for transfers between devices, swap(): return lax.ppermute(value, axis, pairs)  20.3 us
    ppermute x6, starting transfers between devices, across(): return lax.ppermute(value, 'pool', pairs)  13.7 us
    ppermute x16, starting transfers between devices, swap(): return lax.ppermute(value, axis, pairs)  13.4 us
    pallas_call x1, Pallas kernels, base_chunks(): pl.pallas_call(functools.partial(base_kernel, half), grid_spec=pltpu.Pref...  8.18 us
    pallas_call x3, Pallas kernels, combine(): pl.pallas_call(functools.partial(combine_kernel, shapes, choose, len(part...  5.98 us
    pallas_call x3, Pallas kernels, shrink(): pl.pallas_call(functools.partial(shrink_kernel, shapes, choose), grid_spe...  4.51 us
    ppermute x6, waiting for transfers between devices, across(): return lax.ppermute(value, 'pool', pairs)  4.38 us
    pallas_call x2, Pallas kernels, pack_panels(): pl.pallas_call(functools.partial(pack_kernel, starts, capacity), in_specs...  3.15 us
  transfers between devices with their start and end apart: 22, of which 6 were waited for; matrix products, arithmetic and copies ran while one was open for 1% of the time, Pallas kernels for 29%

profile of v6, /device:TPU:0, one launch (start us, length us, event | category | flops | bytes accessed | tf_op | source)
XLA Modules:
  0.0 76.4 jit_solution(15303297477927231233)
XLA Ops:
  0.0 3.0 %collective-permute-start = (s32[1,8]{1,0:T(1,128)}, s32[1,8]{1,0:T(1,128)S(1)}, u32[]{:S(2)}, u32[]{:S(2)}) collective-permute-start(s32[1,8]{1,0:T(1,128)} %refs_0_.1), channel_id=1, source_target_pairs={{0,4},{4,0},{8,12},{12,8},{1,5},{5,1},{9,13},{13,9},{2,6},{6,2},{1... | collective-permute-start | bytes 104 | tf_op jit(solution)/shard_map/ppermute | solution.py:27
  3.0 2.6 %collective-permute-start.1 = (s32[1,8]{1,0:T(1,128)}, s32[1,8]{1,0:T(1,128)S(1)}, u32[]{:S(2)}, u32[]{:S(2)}) collective-permute-start(s32[1,8]{1,0:T(1,128)} %refs_0_.1), channel_id=1, source_target_pairs={{0,8},{4,12},{8,0},{12,4},{1,9},{5,13},{9,1},{13,5},{2,10},{6,14},... | collective-permute-start | bytes 104 | tf_op jit(solution)/shard_map/ppermute | solution.py:27
  5.6 0.0 collective-permute-start.2
  5.6 0.7 collective-permute-start.3
  6.3 0.7 collective-permute-start.5
  7.0 0.7 broadcast_xor_fusion.chunks_ref
  7.7 8.2 %shard_map.83 = (f32[2,384,256]{2,1,0:T(8,128)S(1)}, f32[2,384,256]{2,1,0:T(8,128)S(1)}, f32[2,256,256]{2,1,0:T(8,128)S(1)}, f32[2,1024,256]{2,1,0:T(8,128)S(1)}) custom-call(s32[4]{0:T(128)S(1)} %broadcast_xor_fusion.chunks_ref, bf16[1024,2048]{1,0:T(8,128)(2,1)} %tokens_ref.1, bf16[2048,1024]{1,0:T(8,128)(2,1)} %weight_ref.1), custom_call_target="tpu_custom_call" | custom-call | tf_op jit(solution)/shard_map/pallas_call | solution.py:65
  15.9 0.0 collective-permute-done.refs_1_
  15.9 0.1 collective-permute-start.8
  16.0 0.0 collective-permute-done.1.refs_2_
  16.0 0.5 collective-permute-start.6
  16.5 0.0 collective-permute-done.2.refs_3_
  16.5 0.1 collective-permute-start.7
  16.6 0.0 collective-permute-done.3.refs_6_.up_ref
  16.6 1.7 %shard_map.82.plan_ref = s32[30]{0:T(128)S(1)} custom-call(s32[1,8]{1,0:T(1,128)} %refs_0_.1, s32[1,8]{1,0:T(1,128)S(1)} %collective-permute-done.refs_1_, s32[1,8]{1,0:T(1,128)S(1)} %collective-permute-done.1.refs_2_, s32[1,8]{1,0:T(1,128)S(1)} %collective-permute-done.2.refs_3_, s32[16]{0:T(128)} %refs_4_.1, s32[1,8]{1,0:T(1,128)} %refs_5_.1, ...), custom_call_target="tpu_custom_call" | custom-call | flops 10000000000 | tf_op jit(solution)/shard_map/pallas_call | solution.py:200
  18.2 2.5 %shard_map.84 = (bf16[2,64,2304]{2,1,0:T(8,128)(2,1)S(1)}, bf16[2,64,2304]{2,1,0:T(8,128)(2,1)S(1)}, bf16[2,64,2304]{2,1,0:T(8,128)(2,1)S(1)}) custom-call(s32[30]{0:T(128)S(1)} %shard_map.82.plan_ref, bf16[4,64,2048]{2,1,0:T(8,128)(2,1)} %bitcast.15, bf16[4,64,256]{2,1,0:T(8,128)(2,1)} %refs_6_.1, f32[2,256,256]{2,1,0:T(8,128)S(1)} %get-tuple-element.14.rest_0_), custom_call_target="tpu_custom_call" | custom-call | tf_op jit(solution)/shard_map/pallas_call | solution.py:232
  20.7 5.1 %collective-permute-start.11 = (bf16[2,64,2304]{2,1,0:T(8,128)(2,1)S(1)}, bf16[2,64,2304]{2,1,0:T(8,128)(2,1)S(1)}, u32[]{:S(2)}, u32[]{:S(2)}) collective-permute-start(bf16[2,64,2304]{2,1,0:T(8,128)(2,1)S(1)} %get-tuple-element.21), channel_id=1, source_target_pairs={{0,4},{4,0},{8,12},{12,8},{1,5},{5,1},{9,13},{13,9},{2,6},{6,2},{1... | collective-permute-start | bytes 1769480 | tf_op jit(solution)/shard_map/ppermute | solution.py:393
  25.8 0.0 collective-permute-done.8.refs_2_
  25.8 4.4 %collective-permute-start.10 = (bf16[2,64,2304]{2,1,0:T(8,128)(2,1)S(1)}, bf16[2,64,2304]{2,1,0:T(8,128)(2,1)S(1)}, u32[]{:S(2)}, u32[]{:S(2)}) collective-permute-start(bf16[2,64,2304]{2,1,0:T(8,128)(2,1)S(1)} %get-tuple-element.20), channel_id=1, source_target_pairs={{0,12},{12,0},{1,13},{13,1},{2,14},{14,2},{3,15},{15,3},{16,28},{2... | collective-permute-start | bytes 1769480 | tf_op jit(solution)/shard_map/ppermute | solution.py:393
  30.2 0.0 collective-permute-done.6.refs_0_
  30.2 1.3 %collective-permute-start.4 = (bf16[2,64,2304]{2,1,0:T(8,128)(2,1)S(1)}, bf16[2,64,2304]{2,1,0:T(8,128)(2,1)S(1)}, u32[]{:S(2)}, u32[]{:S(2)}) collective-permute-start(bf16[2,64,2304]{2,1,0:T(8,128)(2,1)S(1)} %get-tuple-element.15), channel_id=1, source_target_pairs={{0,8},{12,4},{1,9},{13,5},{2,10},{14,6},{3,11},{15,7},{16,24},{28,... | collective-permute-start | bytes 1769480 | tf_op jit(solution)/shard_map/ppermute | solution.py:393
  31.6 0.0 collective-permute-done.7.refs_1_
  31.6 0.3 shard_map.85
  31.8 1.6 %collective-permute-start.15 = (f32[1,1024,256]{2,1,0:T(8,128)S(1)}, f32[1,1024,256]{2,1,0:T(8,128)S(1)}, u32[]{:S(2)}, u32[]{:S(2)}) collective-permute-start(f32[1,1024,256]{2,1,0:T(8,128)S(1)} %get-tuple-element.22), channel_id=1, source_target_pairs={{0,2},{1,3},{2,0},{3,1},{4,6},{5,7},{6,4},{7,5},{8,10},{9,11},{10,... | collective-permute-start | bytes 3145736 | tf_op jit(solution)/shard_map/ppermute | solution.py:27
  33.4 0.0 collective-permute-done.5.down_ref.refs_0_
  33.4 0.0 copy-start
  33.4 0.0 copy-start.1
  33.4 0.6 shard_map.86.refs_2_
  34.1 0.0 copy-start.2
  34.1 1.6 %collective-permute-start.9 = (bf16[2,64,2304]{2,1,0:T(8,128)(2,1)S(1)}, bf16[2,64,2304]{2,1,0:T(8,128)(2,1)S(1)}, u32[]{:S(2)}, u32[]{:S(2)}) collective-permute-start(bf16[2,64,2304]{2,1,0:T(8,128)(2,1)S(1)} %shard_map.86.refs_2_), channel_id=1, source_target_pairs={{4,0},{8,12},{5,1},{9,13},{6,2},{10,14},{7,3},{11,15},{20,16},{24,... | collective-permute-start | bytes 1769480 | tf_op jit(solution)/shard_map/ppermute | solution.py:393
  35.6 4.4 %collective-permute-done.11.refs_1_.refs_7_ = bf16[2,64,2304]{2,1,0:T(8,128)(2,1)S(1)} collective-permute-done((bf16[2,64,2304]{2,1,0:T(8,128)(2,1)S(1)}, bf16[2,64,2304]{2,1,0:T(8,128)(2,1)S(1)}, u32[]{:S(2)}, u32[]{:S(2)}) %collective-permute-start.11) | collective-permute-done | bytes 589856 | tf_op jit(solution)/shard_map/ppermute | solution.py:393
  40.0 0.0 copy-done
  40.0 0.0 copy-done.1
  40.0 1.9 %shard_map.87.refs_0_ = bf16[4,64,128]{2,1,0:T(8,128)(2,1)S(1)} custom-call(s32[30]{0:T(128)S(1)} %shard_map.82.plan_ref, bf16[8,128,2048]{2,1,0:T(8,128)(2,1)S(1)} %bitcast.4, bf16[4,64,2048]{2,1,0:T(8,128)(2,1)S(1)} %bitcast.16, bf16[2,64,2304]{2,1,0:T(8,128)(2,1)S(1)} %collective-permute-done.11.refs_1_.refs_7_, bf16[2,64,2304]{2,1,0:T(8,128)(2,1)S(1)} %shard_map.86.refs_2_), custom_call_target="tpu_custom_call" | custom-call | tf_op jit(solution)/shard_map/pallas_call | solution.py:315
  41.9 0.1 collective-permute-start.12
  42.0 1.2 %collective-permute-done.12.refs_1_ = bf16[4,64,128]{2,1,0:T(8,128)(2,1)S(1)} collective-permute-done((bf16[4,64,128]{2,1,0:T(8,128)(2,1)S(1)}, bf16[4,64,128]{2,1,0:T(8,128)(2,1)S(1)}, u32[]{:S(2)}, u32[]{:S(2)}) %collective-permute-start.12) | collective-permute-done | bytes 65568 | tf_op jit(solution)/shard_map/ppermute | solution.py:27
  43.3 1.5 %collective-permute-start.13 = (bf16[4,64,128]{2,1,0:T(8,128)(2,1)S(1)}, bf16[4,64,128]{2,1,0:T(8,128)(2,1)S(1)}, u32[]{:S(2)}, u32[]{:S(2)}) collective-permute-start(bf16[4,64,128]{2,1,0:T(8,128)(2,1)S(1)} %shard_map.87.refs_0_), channel_id=1, source_target_pairs={{0,2},{1,3},{2,0},{3,1},{4,6},{5,7},{6,4},{7,5},{8,10},{9,11},{10,... | collective-permute-start | bytes 196616 | tf_op jit(solution)/shard_map/ppermute | solution.py:27
  44.8 13.5 %collective-permute-done.13.refs_2_ = bf16[4,64,128]{2,1,0:T(8,128)(2,1)S(1)} collective-permute-done((bf16[4,64,128]{2,1,0:T(8,128)(2,1)S(1)}, bf16[4,64,128]{2,1,0:T(8,128)(2,1)S(1)}, u32[]{:S(2)}, u32[]{:S(2)}) %collective-permute-start.13) | collective-permute-done | bytes 65568 | tf_op jit(solution)/shard_map/ppermute | solution.py:27
  58.3 0.1 collective-permute-start.14
  58.4 4.2 %collective-permute-done.14.refs_3_ = bf16[4,64,128]{2,1,0:T(8,128)(2,1)S(1)} collective-permute-done((bf16[4,64,128]{2,1,0:T(8,128)(2,1)S(1)}, bf16[4,64,128]{2,1,0:T(8,128)(2,1)S(1)}, u32[]{:S(2)}, u32[]{:S(2)}) %collective-permute-start.14) | collective-permute-done | bytes 65568 | tf_op jit(solution)/shard_map/ppermute | solution.py:27
  62.6 0.0 collective-permute-done.15
  62.6 0.0 copy-done.2
  62.6 2.6 %shard_map.88.refs_2_.refs_8_ = bf16[1024,256]{1,0:T(8,128)(2,1)} custom-call(s32[30]{0:T(128)S(1)} %shard_map.82.plan_ref, bf16[4,64,128]{2,1,0:T(8,128)(2,1)S(1)} %shard_map.87.refs_0_, bf16[4,64,128]{2,1,0:T(8,128)(2,1)S(1)} %collective-permute-done.12.refs_1_, bf16[4,64,128]{2,1,0:T(8,128)(2,1)S(1)} %collective-permute-done.13.refs_2_, ...), custom_call_target="tpu_custom_call" | custom-call | tf_op jit(solution)/shard_map/pallas_call | solution.py:374
  65.2 0.0 collective-permute-done.10.refs_1_.refs_7_
  65.2 1.3 %shard_map.89.refs_2_.refs_0_ = bf16[2,64,128]{2,1,0:T(8,128)(2,1)S(1)} custom-call(s32[30]{0:T(128)S(1)} %shard_map.82.plan_ref, bf16[8,128,2048]{2,1,0:T(8,128)(2,1)S(1)} %bitcast.5, bf16[4,64,2048]{2,1,0:T(8,128)(2,1)S(1)} %collective-permute-done.5.down_ref.refs_0_, bf16[2,64,2304]{2,1,0:T(8,128)(2,1)S(1)} %collective-permute-done.10.refs_1_.refs_7_, ...), custom_call_target="tpu_custom_call" | custom-call | tf_op jit(solution)/shard_map/pallas_call | solution.py:315
  66.4 0.2 collective-permute-start.19
  66.7 0.8 collective-permute-start.20
  67.4 0.9 %collective-permute-start.21 = (bf16[2,64,128]{2,1,0:T(8,128)(2,1)S(1)}, bf16[2,64,128]{2,1,0:T(8,128)(2,1)S(1)}, u32[]{:S(2)}, u32[]{:S(2)}) collective-permute-start(bf16[2,64,128]{2,1,0:T(8,128)(2,1)S(1)} %shard_map.89.refs_2_.refs_0_), channel_id=1, source_target_pairs={{0,3},{1,2},{2,1},{3,0},{4,7},{5,6},{6,5},{7,4},{8,11},{9,10},{10,... | collective-permute-start | bytes 98312 | tf_op jit(solution)/shard_map/ppermute | solution.py:27
  68.4 0.0 collective-permute-done.4.refs_0_.refs_6_
  68.4 0.0 collective-permute-done.9.refs_1_.refs_7_
  68.4 1.3 %shard_map.90.refs_0_ = bf16[2,64,128]{2,1,0:T(8,128)(2,1)S(1)} custom-call(s32[30]{0:T(128)S(1)} %shard_map.82.plan_ref, bf16[8,128,2048]{2,1,0:T(8,128)(2,1)S(1)} %bitcast.6, bf16[2,64,2304]{2,1,0:T(8,128)(2,1)S(1)} %collective-permute-done.4.refs_0_.refs_6_, bf16[2,64,2304]{2,1,0:T(8,128)(2,1)S(1)} %collective-permute-done.9.refs_1_.refs_7_, ...), custom_call_target="tpu_custom_call" | custom-call | tf_op jit(solution)/shard_map/pallas_call | solution.py:315
  69.7 0.5 collective-permute-start.16
  70.2 0.8 collective-permute-start.17
  71.0 0.0 collective-permute-done.19.refs_1_
  71.0 0.7 collective-permute-start.18
  71.6 0.0 collective-permute-done.20.refs_2_
  71.6 0.0 collective-permute-done.21.refs_3_
  71.7 1.7 %shard_map.91.refs_8_ = bf16[1024,256]{1,0:T(8,128)(2,1)} custom-call(s32[30]{0:T(128)S(1)} %shard_map.82.plan_ref, bf16[2,64,128]{2,1,0:T(8,128)(2,1)S(1)} %shard_map.89.refs_2_.refs_0_, bf16[2,64,128]{2,1,0:T(8,128)(2,1)S(1)} %collective-permute-done.19.refs_1_, ...), custom_call_target="tpu_custom_call", output_to_operand_aliasing={{}: (9, {})} | custom-call | tf_op jit(solution)/shard_map/pallas_call | solution.py:374
  73.4 0.0 collective-permute-done.16.refs_1_
  73.4 0.9 %collective-permute-done.17.refs_2_ = bf16[2,64,128]{2,1,0:T(8,128)(2,1)S(1)} collective-permute-done((bf16[2,64,128]{2,1,0:T(8,128)(2,1)S(1)}, bf16[2,64,128]{2,1,0:T(8,128)(2,1)S(1)}, u32[]{:S(2)}, u32[]{:S(2)}) %collective-permute-start.17) | collective-permute-done | bytes 32800 | tf_op jit(solution)/shard_map/ppermute | solution.py:27
  74.3 0.4 collective-permute-done.18.refs_3_
  74.7 1.7 %shard_map.92 = bf16[1024,256]{1,0:T(8,128)(2,1)} custom-call(s32[30]{0:T(128)S(1)} %shard_map.82.plan_ref, bf16[2,64,128]{2,1,0:T(8,128)(2,1)S(1)} %shard_map.90.refs_0_, bf16[2,64,128]{2,1,0:T(8,128)(2,1)S(1)} %collective-permute-done.16.refs_1_, bf16[2,64,128]{2,1,0:T(8,128)(2,1)S(1)} %collective-permute-done.17.refs_2_, ...), custom_call_target="tpu_custom_call", output_to_operand_aliasing={{}: (9, {})} | custom-call | tf_op jit(solution)/shard_map/pallas_call | solution.py:374
Async XLA Ops:
  0.0 15.9 %collective-permute-start = (s32[1,8]{1,0:T(1,128)}, s32[1,8]{1,0:T(1,128)S(1)}, u32[]{:S(2)}, u32[]{:S(2)}) collective-permute-start(s32[1,8]{1,0:T(1,128)} %refs_0_.1), channel_id=1, source_target_pairs={{0,4},{4,0},{8,12},{12,8},{1,5},{5,1},{9,13},{13,9},{2,6},{6,2},{1... | collective-permute-start | bytes 104 | tf_op jit(solution)/shard_map/ppermute | solution.py:27
  3.0 12.9 %collective-permute-start.1 = (s32[1,8]{1,0:T(1,128)}, s32[1,8]{1,0:T(1,128)S(1)}, u32[]{:S(2)}, u32[]{:S(2)}) collective-permute-start(s32[1,8]{1,0:T(1,128)} %refs_0_.1), channel_id=1, source_target_pairs={{0,8},{4,12},{8,0},{12,4},{1,9},{5,13},{9,1},{13,5},{2,10},{6,14},... | collective-permute-start | bytes 104 | tf_op jit(solution)/shard_map/ppermute | solution.py:27
  5.6 10.8 %collective-permute-start.2 = (s32[1,8]{1,0:T(1,128)}, s32[1,8]{1,0:T(1,128)S(1)}, u32[]{:S(2)}, u32[]{:S(2)}) collective-permute-start(s32[1,8]{1,0:T(1,128)} %refs_0_.1), channel_id=1, source_target_pairs={{0,12},{4,8},{8,4},{12,0},{1,13},{5,9},{9,5},{13,1},{2,14},{6,10},... | collective-permute-start | bytes 104 | tf_op jit(solution)/shard_map/ppermute | solution.py:27
  5.6 10.9 %collective-permute-start.3 = (bf16[4,64,256]{2,1,0:T(8,128)(2,1)}, bf16[4,64,256]{2,1,0:T(8,128)(2,1)S(1)}, u32[]{:S(2)}, u32[]{:S(2)}) collective-permute-start(bf16[4,64,256]{2,1,0:T(8,128)(2,1)} %refs_6_.1), channel_id=1, source_target_pairs={{4,8},{8,4},{5,9},{9,5},{6,10},{10,6},{7,11},{11,7},{20,24},{24,20... | collective-permute-start | bytes 393224 | tf_op jit(solution)/shard_map/ppermute | solution.py:393
  6.3 27.1 %collective-permute-start.5 = (bf16[4,64,2048]{2,1,0:T(8,128)(2,1)}, bf16[4,64,2048]{2,1,0:T(8,128)(2,1)S(1)}, u32[]{:S(2)}, u32[]{:S(2)}) collective-permute-start(bf16[4,64,2048]{2,1,0:T(8,128)(2,1)} %bitcast.14), channel_id=1, source_target_pairs={{4,8},{8,4},{5,9},{9,5},{6,10},{10,6},{7,11},{11,7},{20,24},{24,20... | collective-permute-start | bytes 3145736 | tf_op jit(solution)/shard_map/ppermute | solution.py:393
  15.9 9.9 %collective-permute-start.8 = (f32[2,256,256]{2,1,0:T(8,128)S(1)}, f32[2,256,256]{2,1,0:T(8,128)S(1)}, u32[]{:S(2)}, u32[]{:S(2)}) collective-permute-start(f32[2,256,256]{2,1,0:T(8,128)S(1)} %get-tuple-element.14.rest_0_), channel_id=1, source_target_pairs={{0,1},{1,0},{2,3},{3,2},{4,5},{5,4},{6,7},{7,6},{8,9},{9,8},{10,11... | collective-permute-start | bytes 1572872 | tf_op jit(solution)/shard_map/ppermute | solution.py:27
  16.0 14.2 %collective-permute-start.6 = (f32[2,384,256]{2,1,0:T(8,128)S(1)}, f32[2,384,256]{2,1,0:T(8,128)S(1)}, u32[]{:S(2)}, u32[]{:S(2)}) collective-permute-start(f32[2,384,256]{2,1,0:T(8,128)S(1)} %get-tuple-element.17), channel_id=1, source_target_pairs={{0,1},{1,0},{2,3},{3,2},{4,5},{5,4},{6,7},{7,6},{8,9},{9,8},{10,11... | collective-permute-start | bytes 2359304 | tf_op jit(solution)/shard_map/ppermute | solution.py:27
  16.5 15.1 %collective-permute-start.7 = (f32[2,384,256]{2,1,0:T(8,128)S(1)}, f32[2,384,256]{2,1,0:T(8,128)S(1)}, u32[]{:S(2)}, u32[]{:S(2)}) collective-permute-start(f32[2,384,256]{2,1,0:T(8,128)S(1)} %get-tuple-element.18), channel_id=1, source_target_pairs={{0,1},{1,0},{2,3},{3,2},{4,5},{5,4},{6,7},{7,6},{8,9},{9,8},{10,11... | collective-permute-start | bytes 2359304 | tf_op jit(solution)/shard_map/ppermute | solution.py:27
  20.7 19.3 %collective-permute-start.11 = (bf16[2,64,2304]{2,1,0:T(8,128)(2,1)S(1)}, bf16[2,64,2304]{2,1,0:T(8,128)(2,1)S(1)}, u32[]{:S(2)}, u32[]{:S(2)}) collective-permute-start(bf16[2,64,2304]{2,1,0:T(8,128)(2,1)S(1)} %get-tuple-element.21), channel_id=1, source_target_pairs={{0,4},{4,0},{8,12},{12,8},{1,5},{5,1},{9,13},{13,9},{2,6},{6,2},{1... | collective-permute-start | bytes 1769480 | tf_op jit(solution)/shard_map/ppermute | solution.py:393
  25.8 39.3 %collective-permute-start.10 = (bf16[2,64,2304]{2,1,0:T(8,128)(2,1)S(1)}, bf16[2,64,2304]{2,1,0:T(8,128)(2,1)S(1)}, u32[]{:S(2)}, u32[]{:S(2)}) collective-permute-start(bf16[2,64,2304]{2,1,0:T(8,128)(2,1)S(1)} %get-tuple-element.20), channel_id=1, source_target_pairs={{0,12},{12,0},{1,13},{13,1},{2,14},{14,2},{3,15},{15,3},{16,28},{2... | collective-permute-start | bytes 1769480 | tf_op jit(solution)/shard_map/ppermute | solution.py:393
  30.2 38.1 %collective-permute-start.4 = (bf16[2,64,2304]{2,1,0:T(8,128)(2,1)S(1)}, bf16[2,64,2304]{2,1,0:T(8,128)(2,1)S(1)}, u32[]{:S(2)}, u32[]{:S(2)}) collective-permute-start(bf16[2,64,2304]{2,1,0:T(8,128)(2,1)S(1)} %get-tuple-element.15), channel_id=1, source_target_pairs={{0,8},{12,4},{1,9},{13,5},{2,10},{14,6},{3,11},{15,7},{16,24},{28,... | collective-permute-start | bytes 1769480 | tf_op jit(solution)/shard_map/ppermute | solution.py:393
  31.8 30.8 %collective-permute-start.15 = (f32[1,1024,256]{2,1,0:T(8,128)S(1)}, f32[1,1024,256]{2,1,0:T(8,128)S(1)}, u32[]{:S(2)}, u32[]{:S(2)}) collective-permute-start(f32[1,1024,256]{2,1,0:T(8,128)S(1)} %get-tuple-element.22), channel_id=1, source_target_pairs={{0,2},{1,3},{2,0},{3,1},{4,6},{5,7},{6,4},{7,5},{8,10},{9,11},{10,... | collective-permute-start | bytes 3145736 | tf_op jit(solution)/shard_map/ppermute | solution.py:27
  33.4 6.6 %copy-start = (bf16[1024,2048]{1,0:T(8,128)(2,1)S(1)}, bf16[1024,2048]{1,0:T(8,128)(2,1)}, u32[]{:S(2)}) copy-start(bf16[1024,2048]{1,0:T(8,128)(2,1)} %tokens_ref.1) | copy-start | bytes 12582916
  33.4 6.6 %copy-start.1 = (bf16[4,2048,64]{1,2,0:T(8,128)(2,1)S(1)}, bf16[4,2048,64]{1,2,0:T(8,128)(2,1)}, u32[]{:S(2)}) copy-start(bf16[4,2048,64]{1,2,0:T(8,128)(2,1)} %param.10) | copy-start | bytes 3145732
  34.1 28.5 %copy-start.2 = (bf16[4,64,256]{2,1,0:T(8,128)(2,1)S(1)}, bf16[4,64,256]{2,1,0:T(8,128)(2,1)}, u32[]{:S(2)}) copy-start(bf16[4,64,256]{2,1,0:T(8,128)(2,1)} %refs_6_.1) | copy-start | bytes 393220
  34.1 34.3 %collective-permute-start.9 = (bf16[2,64,2304]{2,1,0:T(8,128)(2,1)S(1)}, bf16[2,64,2304]{2,1,0:T(8,128)(2,1)S(1)}, u32[]{:S(2)}, u32[]{:S(2)}) collective-permute-start(bf16[2,64,2304]{2,1,0:T(8,128)(2,1)S(1)} %shard_map.86.refs_2_), channel_id=1, source_target_pairs={{4,0},{8,12},{5,1},{9,13},{6,2},{10,14},{7,3},{11,15},{20,16},{24,... | collective-permute-start | bytes 1769480 | tf_op jit(solution)/shard_map/ppermute | solution.py:393
  41.9 1.3 %collective-permute-start.12 = (bf16[4,64,128]{2,1,0:T(8,128)(2,1)S(1)}, bf16[4,64,128]{2,1,0:T(8,128)(2,1)S(1)}, u32[]{:S(2)}, u32[]{:S(2)}) collective-permute-start(bf16[4,64,128]{2,1,0:T(8,128)(2,1)S(1)} %shard_map.87.refs_0_), channel_id=1, source_target_pairs={{0,1},{1,0},{2,3},{3,2},{4,5},{5,4},{6,7},{7,6},{8,9},{9,8},{10,11... | collective-permute-start | bytes 196616 | tf_op jit(solution)/shard_map/ppermute | solution.py:27
  43.3 15.0 %collective-permute-start.13 = (bf16[4,64,128]{2,1,0:T(8,128)(2,1)S(1)}, bf16[4,64,128]{2,1,0:T(8,128)(2,1)S(1)}, u32[]{:S(2)}, u32[]{:S(2)}) collective-permute-start(bf16[4,64,128]{2,1,0:T(8,128)(2,1)S(1)} %shard_map.87.refs_0_), channel_id=1, source_target_pairs={{0,2},{1,3},{2,0},{3,1},{4,6},{5,7},{6,4},{7,5},{8,10},{9,11},{10,... | collective-permute-start | bytes 196616 | tf_op jit(solution)/shard_map/ppermute | solution.py:27
  58.3 4.3 %collective-permute-start.14 = (bf16[4,64,128]{2,1,0:T(8,128)(2,1)S(1)}, bf16[4,64,128]{2,1,0:T(8,128)(2,1)S(1)}, u32[]{:S(2)}, u32[]{:S(2)}) collective-permute-start(bf16[4,64,128]{2,1,0:T(8,128)(2,1)S(1)} %shard_map.87.refs_0_), channel_id=1, source_target_pairs={{0,3},{1,2},{2,1},{3,0},{4,7},{5,6},{6,5},{7,4},{8,11},{9,10},{10,... | collective-permute-start | bytes 196616 | tf_op jit(solution)/shard_map/ppermute | solution.py:27
  66.4 4.5 %collective-permute-start.19 = (bf16[2,64,128]{2,1,0:T(8,128)(2,1)S(1)}, bf16[2,64,128]{2,1,0:T(8,128)(2,1)S(1)}, u32[]{:S(2)}, u32[]{:S(2)}) collective-permute-start(bf16[2,64,128]{2,1,0:T(8,128)(2,1)S(1)} %shard_map.89.refs_2_.refs_0_), channel_id=1, source_target_pairs={{0,1},{1,0},{2,3},{3,2},{4,5},{5,4},{6,7},{7,6},{8,9},{9,8},{10,11... | collective-permute-start | bytes 98312 | tf_op jit(solution)/shard_map/ppermute | solution.py:27
  66.7 5.0 %collective-permute-start.20 = (bf16[2,64,128]{2,1,0:T(8,128)(2,1)S(1)}, bf16[2,64,128]{2,1,0:T(8,128)(2,1)S(1)}, u32[]{:S(2)}, u32[]{:S(2)}) collective-permute-start(bf16[2,64,128]{2,1,0:T(8,128)(2,1)S(1)} %shard_map.89.refs_2_.refs_0_), channel_id=1, source_target_pairs={{0,2},{1,3},{2,0},{3,1},{4,6},{5,7},{6,4},{7,5},{8,10},{9,11},{10,... | collective-permute-start | bytes 98312 | tf_op jit(solution)/shard_map/ppermute | solution.py:27
  67.4 4.2 %collective-permute-start.21 = (bf16[2,64,128]{2,1,0:T(8,128)(2,1)S(1)}, bf16[2,64,128]{2,1,0:T(8,128)(2,1)S(1)}, u32[]{:S(2)}, u32[]{:S(2)}) collective-permute-start(bf16[2,64,128]{2,1,0:T(8,128)(2,1)S(1)} %shard_map.89.refs_2_.refs_0_), channel_id=1, source_target_pairs={{0,3},{1,2},{2,1},{3,0},{4,7},{5,6},{6,5},{7,4},{8,11},{9,10},{10,... | collective-permute-start | bytes 98312 | tf_op jit(solution)/shard_map/ppermute | solution.py:27
  69.7 3.7 %collective-permute-start.16 = (bf16[2,64,128]{2,1,0:T(8,128)(2,1)S(1)}, bf16[2,64,128]{2,1,0:T(8,128)(2,1)S(1)}, u32[]{:S(2)}, u32[]{:S(2)}) collective-permute-start(bf16[2,64,128]{2,1,0:T(8,128)(2,1)S(1)} %shard_map.90.refs_0_), channel_id=1, source_target_pairs={{0,1},{1,0},{2,3},{3,2},{4,5},{5,4},{6,7},{7,6},{8,9},{9,8},{10,11... | collective-permute-start | bytes 98312 | tf_op jit(solution)/shard_map/ppermute | solution.py:27
  70.2 4.1 %collective-permute-start.17 = (bf16[2,64,128]{2,1,0:T(8,128)(2,1)S(1)}, bf16[2,64,128]{2,1,0:T(8,128)(2,1)S(1)}, u32[]{:S(2)}, u32[]{:S(2)}) collective-permute-start(bf16[2,64,128]{2,1,0:T(8,128)(2,1)S(1)} %shard_map.90.refs_0_), channel_id=1, source_target_pairs={{0,2},{1,3},{2,0},{3,1},{4,6},{5,7},{6,4},{7,5},{8,10},{9,11},{10,... | collective-permute-start | bytes 98312 | tf_op jit(solution)/shard_map/ppermute | solution.py:27
  71.0 3.7 %collective-permute-start.18 = (bf16[2,64,128]{2,1,0:T(8,128)(2,1)S(1)}, bf16[2,64,128]{2,1,0:T(8,128)(2,1)S(1)}, u32[]{:S(2)}, u32[]{:S(2)}) collective-permute-start(bf16[2,64,128]{2,1,0:T(8,128)(2,1)S(1)} %shard_map.90.refs_0_), channel_id=1, source_target_pairs={{0,3},{1,2},{2,1},{3,0},{4,7},{5,6},{6,5},{7,4},{8,11},{9,10},{10,... | collective-permute-start | bytes 98312 | tf_op jit(solution)/shard_map/ppermute | solution.py:27

commit v7 on v6

--- a/solution.py
+++ b/solution.py
@@ -27,6 +27,12 @@
     return lax.ppermute(value, axis, pairs)
 
 
+def run_copies(copies):
+    for copy in copies:
+        copy.start()
+    return copies
+
+
 def piece_rows(rows):
     large = rows * 3 // 8
     return [large, large, rows - 2 * large]
@@ -34,27 +40,40 @@
 
 def base_kernel(half, chunks_ref, tokens_ref, weight_ref, *refs):
     del chunks_ref
-    *sent_refs, kept_ref = refs
-
-    def write(out_ref, first, size):
-        for start in range(0, size, ROW_TILE):
-            stop = min(start + ROW_TILE, size)
-            out_ref[0, start:stop, :] = jnp.dot(
-                tokens_ref[first + start : first + stop, :],
-                weight_ref[...],
-                preferred_element_type=jnp.float32,
-            )
-
-    @pl.when(pl.program_id(0) < half)
+    *sent_refs, kept_ref, held_ref, sems = refs
+    step = pl.program_id(0)
+    tiles = sems.shape[0]
+    tile = held_ref.shape[0] // tiles
+    copies = []
+    for i in range(tiles):
+        rows = pl.ds(i * tile, tile)
+        copies.append(pltpu.make_async_copy(tokens_ref.at[rows], held_ref.at[rows], sems.at[i]))
+
+    def write(out_refs, arriving=()):
+        first = 0
+        for out_ref in out_refs:
+            for start in range(0, out_ref.shape[1], ROW_TILE):
+                stop = min(start + ROW_TILE, out_ref.shape[1])
+                while arriving and (tiles - len(arriving)) * tile < first + stop:
+                    arriving.pop(0).wait()
+                out_ref[0, start:stop, :] = jnp.dot(
+                    held_ref[first + start : first + stop, :],
+                    weight_ref[...],
+                    preferred_element_type=jnp.float32,
+                )
+            first += out_ref.shape[1]
+
+    @pl.when(step == 0)
     def _():
-        first = 0
-        for sent_ref in sent_refs:
-            write(sent_ref, first, sent_ref.shape[1])
-            first += sent_ref.shape[1]
-
-    @pl.when(pl.program_id(0) >= half)
+        write(sent_refs, run_copies(copies))
+
+    @pl.when((step > 0) & (step < half))
     def _():
-        write(kept_ref, 0, kept_ref.shape[1])
+        write(sent_refs)
+
+    @pl.when(step >= half)
+    def _():
+        write([kept_ref])
 
 
 def base_chunks(tokens, weight, order, width):
@@ -68,7 +87,7 @@
             num_scalar_prefetch=1,
             grid=(len(order),),
             in_specs=[
-                pl.BlockSpec(tokens.shape, lambda i, c: (0, 0), pipeline_mode=pl.Buffered(1)),
+                ANY,
                 pl.BlockSpec((depth, width), lambda i, c: (0, c[i])),
             ],
             out_specs=[
@@ -76,6 +95,10 @@
                 for size in sizes
             ]
             + [pl.BlockSpec((1, rows, width), lambda i, c: (jnp.maximum(i - half, 0), 0, 0))],
+            scratch_shapes=[
+                pltpu.VMEM(tokens.shape, tokens.dtype),
+                pltpu.SemaphoreType.DMA((4,)),
+            ],
         ),
         out_shape=[
             jax.ShapeDtypeStruct((half, size, width), jnp.float32) for size in [*sizes, rows]
@@ -148,12 +171,6 @@
         pltpu.make_async_copy(down_ref.at[slot], out_ref.at[k, :, pl.ds(0, depth)], sems.at[k, 0]),
         pltpu.make_async_copy(up_ref.at[slot], out_ref.at[k, :, pl.ds(depth, width)], sems.at[k, 1]),
     ]
-
-
-def run_copies(copies):
-    for copy in copies:
-        copy.start()
-    return copies
 
 
 def plan_kernel(capacity, holder_slots, *refs):

time: 76.6 us -> 77.9 us (1.017)
  Pallas kernels: 23.7 us -> 24.5 us
    pallas_call x1, Pallas kernels: 8.18 us -> 9.21 us  [base_chunks(): pl.pallas_call(functools.partial(base_kernel, half), grid_spec=pltpu.Pref...]
where the time goes in v7:
time: 77.9 us; the launch traced here: 77.8 us
  starting transfers between devices  27.8 us (36%)
  waiting for transfers between devices  24.7 us (32%)
  Pallas kernels  24.5 us (31%)
    ppermute x16, waiting for transfers between devices, swap(): return lax.ppermute(value, axis, pairs)  20.8 us
    ppermute x6, starting transfers between devices, across(): return lax.ppermute(value, 'pool', pairs)  14.4 us
    ppermute x16, starting transfers between devices, swap(): return lax.ppermute(value, axis, pairs)  13.4 us
    pallas_call x1, Pallas kernels, base_chunks(): pl.pallas_call(functools.partial(base_kernel, half), grid_spec=pltpu.Pref...  9.21 us
    pallas_call x3, Pallas kernels, combine(): pl.pallas_call(functools.partial(combine_kernel, shapes, choose, len(part...  5.98 us
    pallas_call x3, Pallas kernels, shrink(): pl.pallas_call(functools.partial(shrink_kernel, shapes, choose), grid_spe...  4.51 us
    ppermute x6, waiting for transfers between devices, across(): return lax.ppermute(value, 'pool', pairs)  3.87 us
    pallas_call x2, Pallas kernels, pack_panels(): pl.pallas_call(functools.partial(pack_kernel, starts, capacity), in_specs...  2.85 us
  transfers between devices with their start and end apart: 22, of which 6 were waited for; matrix products, arithmetic and copies ran while one was open for 1% of the time, Pallas kernels for 29%

profile of v7, /device:TPU:0, one launch (start us, length us, event | category | flops | bytes accessed | tf_op | source)
XLA Modules:
  0.0 77.8 jit_solution(5260967082062743210)
XLA Ops:
  0.0 3.0 %collective-permute-start = (s32[1,8]{1,0:T(1,128)}, s32[1,8]{1,0:T(1,128)S(1)}, u32[]{:S(2)}, u32[]{:S(2)}) collective-permute-start(s32[1,8]{1,0:T(1,128)} %refs_0_.1), channel_id=1, source_target_pairs={{0,4},{4,0},{8,12},{12,8},{1,5},{5,1},{9,13},{13,9},{2,6},{6,2},{1... | collective-permute-start | bytes 104 | tf_op jit(solution)/shard_map/ppermute | solution.py:27
  3.0 2.6 %collective-permute-start.1 = (s32[1,8]{1,0:T(1,128)}, s32[1,8]{1,0:T(1,128)S(1)}, u32[]{:S(2)}, u32[]{:S(2)}) collective-permute-start(s32[1,8]{1,0:T(1,128)} %refs_0_.1), channel_id=1, source_target_pairs={{0,8},{4,12},{8,0},{12,4},{1,9},{5,13},{9,1},{13,5},{2,10},{6,14},... | collective-permute-start | bytes 104 | tf_op jit(solution)/shard_map/ppermute | solution.py:27
  5.6 0.0 collective-permute-start.2
  5.6 0.7 collective-permute-start.3
  6.3 0.7 collective-permute-start.5
  7.0 0.7 broadcast_xor_fusion.chunks_ref
  7.7 9.2 %shard_map.83 = (f32[2,384,256]{2,1,0:T(8,128)S(1)}, f32[2,384,256]{2,1,0:T(8,128)S(1)}, f32[2,256,256]{2,1,0:T(8,128)S(1)}, f32[2,1024,256]{2,1,0:T(8,128)S(1)}) custom-call(s32[4]{0:T(128)S(1)} %broadcast_xor_fusion.chunks_ref, bf16[1024,2048]{1,0:T(8,128)(2,1)} %tokens_ref.1, bf16[2048,1024]{1,0:T(8,128)(2,1)} %weight_ref.1), custom_call_target="tpu_custom_call" | custom-call | tf_op jit(solution)/shard_map/pallas_call | solution.py:84
  16.9 0.0 collective-permute-done.refs_1_
  16.9 0.1 collective-permute-start.8
  17.0 0.0 collective-permute-done.1.refs_2_
  17.0 0.5 collective-permute-start.6
  17.5 0.0 collective-permute-done.2.refs_3_
  17.5 0.1 collective-permute-start.7
  17.6 0.0 collective-permute-done.3.refs_6_.up_ref
  17.6 1.7 %shard_map.82.plan_ref = s32[30]{0:T(128)S(1)} custom-call(s32[1,8]{1,0:T(1,128)} %refs_0_.1, s32[1,8]{1,0:T(1,128)S(1)} %collective-permute-done.refs_1_, s32[1,8]{1,0:T(1,128)S(1)} %collective-permute-done.1.refs_2_, s32[1,8]{1,0:T(1,128)S(1)} %collective-permute-done.2.refs_3_, s32[16]{0:T(128)} %refs_4_.1, s32[1,8]{1,0:T(1,128)} %refs_5_.1, ...), custom_call_target="tpu_custom_call" | custom-call | flops 10000000000 | tf_op jit(solution)/shard_map/pallas_call | solution.py:217
  19.3 2.2 %shard_map.84 = (bf16[2,64,2304]{2,1,0:T(8,128)(2,1)S(1)}, bf16[2,64,2304]{2,1,0:T(8,128)(2,1)S(1)}, bf16[2,64,2304]{2,1,0:T(8,128)(2,1)S(1)}) custom-call(s32[30]{0:T(128)S(1)} %shard_map.82.plan_ref, bf16[4,64,2048]{2,1,0:T(8,128)(2,1)} %bitcast.15, bf16[4,64,256]{2,1,0:T(8,128)(2,1)} %refs_6_.1, f32[2,256,256]{2,1,0:T(8,128)S(1)} %get-tuple-element.14.rest_0_), custom_call_target="tpu_custom_call" | custom-call | tf_op jit(solution)/shard_map/pallas_call | solution.py:249
  21.5 5.3 %collective-permute-start.11 = (bf16[2,64,2304]{2,1,0:T(8,128)(2,1)S(1)}, bf16[2,64,2304]{2,1,0:T(8,128)(2,1)S(1)}, u32[]{:S(2)}, u32[]{:S(2)}) collective-permute-start(bf16[2,64,2304]{2,1,0:T(8,128)(2,1)S(1)} %get-tuple-element.21), channel_id=1, source_target_pairs={{0,4},{4,0},{8,12},{12,8},{1,5},{5,1},{9,13},{13,9},{2,6},{6,2},{1... | collective-permute-start | bytes 1769480 | tf_op jit(solution)/shard_map/ppermute | solution.py:410
  26.8 0.0 collective-permute-done.8.refs_2_
  26.8 4.9 %collective-permute-start.10 = (bf16[2,64,2304]{2,1,0:T(8,128)(2,1)S(1)}, bf16[2,64,2304]{2,1,0:T(8,128)(2,1)S(1)}, u32[]{:S(2)}, u32[]{:S(2)}) collective-permute-start(bf16[2,64,2304]{2,1,0:T(8,128)(2,1)S(1)} %get-tuple-element.20), channel_id=1, source_target_pairs={{0,12},{12,0},{1,13},{13,1},{2,14},{14,2},{3,15},{15,3},{16,28},{2... | collective-permute-start | bytes 1769480 | tf_op jit(solution)/shard_map/ppermute | solution.py:410
  31.7 0.0 collective-permute-done.6.refs_0_
  31.7 1.3 %collective-permute-start.4 = (bf16[2,64,2304]{2,1,0:T(8,128)(2,1)S(1)}, bf16[2,64,2304]{2,1,0:T(8,128)(2,1)S(1)}, u32[]{:S(2)}, u32[]{:S(2)}) collective-permute-start(bf16[2,64,2304]{2,1,0:T(8,128)(2,1)S(1)} %get-tuple-element.15), channel_id=1, source_target_pairs={{0,8},{12,4},{1,9},{13,5},{2,10},{14,6},{3,11},{15,7},{16,24},{28,... | collective-permute-start | bytes 1769480 | tf_op jit(solution)/shard_map/ppermute | solution.py:410
  33.0 0.0 collective-permute-done.7.refs_1_
  33.0 0.3 shard_map.85
  33.3 1.6 %collective-permute-start.15 = (f32[1,1024,256]{2,1,0:T(8,128)S(1)}, f32[1,1024,256]{2,1,0:T(8,128)S(1)}, u32[]{:S(2)}, u32[]{:S(2)}) collective-permute-start(f32[1,1024,256]{2,1,0:T(8,128)S(1)} %get-tuple-element.22), channel_id=1, source_target_pairs={{0,2},{1,3},{2,0},{3,1},{4,6},{5,7},{6,4},{7,5},{8,10},{9,11},{10,... | collective-permute-start | bytes 3145736 | tf_op jit(solution)/shard_map/ppermute | solution.py:27
  34.9 0.0 collective-permute-done.5.down_ref.refs_0_
  34.9 0.0 copy-start
  34.9 0.0 copy-start.1
  34.9 0.6 shard_map.86.refs_2_
  35.5 0.0 copy-start.2
  35.5 1.6 %collective-permute-start.9 = (bf16[2,64,2304]{2,1,0:T(8,128)(2,1)S(1)}, bf16[2,64,2304]{2,1,0:T(8,128)(2,1)S(1)}, u32[]{:S(2)}, u32[]{:S(2)}) collective-permute-start(bf16[2,64,2304]{2,1,0:T(8,128)(2,1)S(1)} %shard_map.86.refs_2_), channel_id=1, source_target_pairs={{4,0},{8,12},{5,1},{9,13},{6,2},{10,14},{7,3},{11,15},{20,16},{24,... | collective-permute-start | bytes 1769480 | tf_op jit(solution)/shard_map/ppermute | solution.py:410
  37.1 3.9 %collective-permute-done.11.refs_1_.refs_7_ = bf16[2,64,2304]{2,1,0:T(8,128)(2,1)S(1)} collective-permute-done((bf16[2,64,2304]{2,1,0:T(8,128)(2,1)S(1)}, bf16[2,64,2304]{2,1,0:T(8,128)(2,1)S(1)}, u32[]{:S(2)}, u32[]{:S(2)}) %collective-permute-start.11) | collective-permute-done | bytes 589856 | tf_op jit(solution)/shard_map/ppermute | solution.py:410
  40.9 0.0 copy-done
  40.9 0.0 copy-done.1
  41.0 1.9 %shard_map.87.refs_0_ = bf16[4,64,128]{2,1,0:T(8,128)(2,1)S(1)} custom-call(s32[30]{0:T(128)S(1)} %shard_map.82.plan_ref, bf16[8,128,2048]{2,1,0:T(8,128)(2,1)S(1)} %bitcast.4, bf16[4,64,2048]{2,1,0:T(8,128)(2,1)S(1)} %bitcast.16, bf16[2,64,2304]{2,1,0:T(8,128)(2,1)S(1)} %collective-permute-done.11.refs_1_.refs_7_, bf16[2,64,2304]{2,1,0:T(8,128)(2,1)S(1)} %shard_map.86.refs_2_), custom_call_target="tpu_custom_call" | custom-call | tf_op jit(solution)/shard_map/pallas_call | solution.py:332
  42.9 0.1 collective-permute-start.12
  43.0 1.2 %collective-permute-done.12.refs_1_ = bf16[4,64,128]{2,1,0:T(8,128)(2,1)S(1)} collective-permute-done((bf16[4,64,128]{2,1,0:T(8,128)(2,1)S(1)}, bf16[4,64,128]{2,1,0:T(8,128)(2,1)S(1)}, u32[]{:S(2)}, u32[]{:S(2)}) %collective-permute-start.12) | collective-permute-done | bytes 65568 | tf_op jit(solution)/shard_map/ppermute | solution.py:27
  44.2 1.5 %collective-permute-start.13 = (bf16[4,64,128]{2,1,0:T(8,128)(2,1)S(1)}, bf16[4,64,128]{2,1,0:T(8,128)(2,1)S(1)}, u32[]{:S(2)}, u32[]{:S(2)}) collective-permute-start(bf16[4,64,128]{2,1,0:T(8,128)(2,1)S(1)} %shard_map.87.refs_0_), channel_id=1, source_target_pairs={{0,2},{1,3},{2,0},{3,1},{4,6},{5,7},{6,4},{7,5},{8,10},{9,11},{10,... | collective-permute-start | bytes 196616 | tf_op jit(solution)/shard_map/ppermute | solution.py:27
  45.7 14.0 %collective-permute-done.13.refs_2_ = bf16[4,64,128]{2,1,0:T(8,128)(2,1)S(1)} collective-permute-done((bf16[4,64,128]{2,1,0:T(8,128)(2,1)S(1)}, bf16[4,64,128]{2,1,0:T(8,128)(2,1)S(1)}, u32[]{:S(2)}, u32[]{:S(2)}) %collective-permute-start.13) | collective-permute-done | bytes 65568 | tf_op jit(solution)/shard_map/ppermute | solution.py:27
  59.7 0.1 collective-permute-start.14
  59.8 4.2 %collective-permute-done.14.refs_3_ = bf16[4,64,128]{2,1,0:T(8,128)(2,1)S(1)} collective-permute-done((bf16[4,64,128]{2,1,0:T(8,128)(2,1)S(1)}, bf16[4,64,128]{2,1,0:T(8,128)(2,1)S(1)}, u32[]{:S(2)}, u32[]{:S(2)}) %collective-permute-start.14) | collective-permute-done | bytes 65568 | tf_op jit(solution)/shard_map/ppermute | solution.py:27
  64.0 0.0 collective-permute-done.15
  64.0 0.0 copy-done.2
  64.0 2.6 %shard_map.88.refs_2_.refs_8_ = bf16[1024,256]{1,0:T(8,128)(2,1)} custom-call(s32[30]{0:T(128)S(1)} %shard_map.82.plan_ref, bf16[4,64,128]{2,1,0:T(8,128)(2,1)S(1)} %shard_map.87.refs_0_, bf16[4,64,128]{2,1,0:T(8,128)(2,1)S(1)} %collective-permute-done.12.refs_1_, bf16[4,64,128]{2,1,0:T(8,128)(2,1)S(1)} %collective-permute-done.13.refs_2_, ...), custom_call_target="tpu_custom_call" | custom-call | tf_op jit(solution)/shard_map/pallas_call | solution.py:391
  66.6 0.0 collective-permute-done.10.refs_1_.refs_7_
  66.6 1.3 %shard_map.89.refs_2_.refs_0_ = bf16[2,64,128]{2,1,0:T(8,128)(2,1)S(1)} custom-call(s32[30]{0:T(128)S(1)} %shard_map.82.plan_ref, bf16[8,128,2048]{2,1,0:T(8,128)(2,1)S(1)} %bitcast.5, bf16[4,64,2048]{2,1,0:T(8,128)(2,1)S(1)} %collective-permute-done.5.down_ref.refs_0_, bf16[2,64,2304]{2,1,0:T(8,128)(2,1)S(1)} %collective-permute-done.10.refs_1_.refs_7_, ...), custom_call_target="tpu_custom_call" | custom-call | tf_op jit(solution)/shard_map/pallas_call | solution.py:332
  67.9 0.2 collective-permute-start.19
  68.1 0.8 collective-permute-start.20
  68.9 0.9 %collective-permute-start.21 = (bf16[2,64,128]{2,1,0:T(8,128)(2,1)S(1)}, bf16[2,64,128]{2,1,0:T(8,128)(2,1)S(1)}, u32[]{:S(2)}, u32[]{:S(2)}) collective-permute-start(bf16[2,64,128]{2,1,0:T(8,128)(2,1)S(1)} %shard_map.89.refs_2_.refs_0_), channel_id=1, source_target_pairs={{0,3},{1,2},{2,1},{3,0},{4,7},{5,6},{6,5},{7,4},{8,11},{9,10},{10,... | collective-permute-start | bytes 98312 | tf_op jit(solution)/shard_map/ppermute | solution.py:27
  69.8 0.0 collective-permute-done.4.refs_0_.refs_6_
  69.8 0.0 collective-permute-done.9.refs_1_.refs_7_
  69.8 1.3 %shard_map.90.refs_0_ = bf16[2,64,128]{2,1,0:T(8,128)(2,1)S(1)} custom-call(s32[30]{0:T(128)S(1)} %shard_map.82.plan_ref, bf16[8,128,2048]{2,1,0:T(8,128)(2,1)S(1)} %bitcast.6, bf16[2,64,2304]{2,1,0:T(8,128)(2,1)S(1)} %collective-permute-done.4.refs_0_.refs_6_, bf16[2,64,2304]{2,1,0:T(8,128)(2,1)S(1)} %collective-permute-done.9.refs_1_.refs_7_, ...), custom_call_target="tpu_custom_call" | custom-call | tf_op jit(solution)/shard_map/pallas_call | solution.py:332
  71.1 0.5 collective-permute-start.16
  71.7 0.8 collective-permute-start.17
  72.4 0.0 collective-permute-done.19.refs_1_
  72.4 0.7 collective-permute-start.18
  73.1 0.0 collective-permute-done.20.refs_2_
  73.1 0.0 collective-permute-done.21.refs_3_
  73.1 1.7 %shard_map.91.refs_8_ = bf16[1024,256]{1,0:T(8,128)(2,1)} custom-call(s32[30]{0:T(128)S(1)} %shard_map.82.plan_ref, bf16[2,64,128]{2,1,0:T(8,128)(2,1)S(1)} %shard_map.89.refs_2_.refs_0_, bf16[2,64,128]{2,1,0:T(8,128)(2,1)S(1)} %collective-permute-done.19.refs_1_, ...), custom_call_target="tpu_custom_call", output_to_operand_aliasing={{}: (9, {})} | custom-call | tf_op jit(solution)/shard_map/pallas_call | solution.py:391
  74.8 0.0 collective-permute-done.16.refs_1_
  74.8 0.9 %collective-permute-done.17.refs_2_ = bf16[2,64,128]{2,1,0:T(8,128)(2,1)S(1)} collective-permute-done((bf16[2,64,128]{2,1,0:T(8,128)(2,1)S(1)}, bf16[2,64,128]{2,1,0:T(8,128)(2,1)S(1)}, u32[]{:S(2)}, u32[]{:S(2)}) %collective-permute-start.17) | collective-permute-done | bytes 32800 | tf_op jit(solution)/shard_map/ppermute | solution.py:27
  75.7 0.4 collective-permute-done.18.refs_3_
  76.1 1.7 %shard_map.92 = bf16[1024,256]{1,0:T(8,128)(2,1)} custom-call(s32[30]{0:T(128)S(1)} %shard_map.82.plan_ref, bf16[2,64,128]{2,1,0:T(8,128)(2,1)S(1)} %shard_map.90.refs_0_, bf16[2,64,128]{2,1,0:T(8,128)(2,1)S(1)} %collective-permute-done.16.refs_1_, bf16[2,64,128]{2,1,0:T(8,128)(2,1)S(1)} %collective-permute-done.17.refs_2_, ...), custom_call_target="tpu_custom_call", output_to_operand_aliasing={{}: (9, {})} | custom-call | tf_op jit(solution)/shard_map/pallas_call | solution.py:391
Async XLA Ops:
  0.0 16.9 %collective-permute-start = (s32[1,8]{1,0:T(1,128)}, s32[1,8]{1,0:T(1,128)S(1)}, u32[]{:S(2)}, u32[]{:S(2)}) collective-permute-start(s32[1,8]{1,0:T(1,128)} %refs_0_.1), channel_id=1, source_target_pairs={{0,4},{4,0},{8,12},{12,8},{1,5},{5,1},{9,13},{13,9},{2,6},{6,2},{1... | collective-permute-start | bytes 104 | tf_op jit(solution)/shard_map/ppermute | solution.py:27
  3.0 14.0 %collective-permute-start.1 = (s32[1,8]{1,0:T(1,128)}, s32[1,8]{1,0:T(1,128)S(1)}, u32[]{:S(2)}, u32[]{:S(2)}) collective-permute-start(s32[1,8]{1,0:T(1,128)} %refs_0_.1), channel_id=1, source_target_pairs={{0,8},{4,12},{8,0},{12,4},{1,9},{5,13},{9,1},{13,5},{2,10},{6,14},... | collective-permute-start | bytes 104 | tf_op jit(solution)/shard_map/ppermute | solution.py:27
  5.6 11.9 %collective-permute-start.2 = (s32[1,8]{1,0:T(1,128)}, s32[1,8]{1,0:T(1,128)S(1)}, u32[]{:S(2)}, u32[]{:S(2)}) collective-permute-start(s32[1,8]{1,0:T(1,128)} %refs_0_.1), channel_id=1, source_target_pairs={{0,12},{4,8},{8,4},{12,0},{1,13},{5,9},{9,5},{13,1},{2,14},{6,10},... | collective-permute-start | bytes 104 | tf_op jit(solution)/shard_map/ppermute | solution.py:27
  5.6 12.0 %collective-permute-start.3 = (bf16[4,64,256]{2,1,0:T(8,128)(2,1)}, bf16[4,64,256]{2,1,0:T(8,128)(2,1)S(1)}, u32[]{:S(2)}, u32[]{:S(2)}) collective-permute-start(bf16[4,64,256]{2,1,0:T(8,128)(2,1)} %refs_6_.1), channel_id=1, source_target_pairs={{4,8},{8,4},{5,9},{9,5},{6,10},{10,6},{7,11},{11,7},{20,24},{24,20... | collective-permute-start | bytes 393224 | tf_op jit(solution)/shard_map/ppermute | solution.py:410
  6.3 28.6 %collective-permute-start.5 = (bf16[4,64,2048]{2,1,0:T(8,128)(2,1)}, bf16[4,64,2048]{2,1,0:T(8,128)(2,1)S(1)}, u32[]{:S(2)}, u32[]{:S(2)}) collective-permute-start(bf16[4,64,2048]{2,1,0:T(8,128)(2,1)} %bitcast.14), channel_id=1, source_target_pairs={{4,8},{8,4},{5,9},{9,5},{6,10},{10,6},{7,11},{11,7},{20,24},{24,20... | collective-permute-start | bytes 3145736 | tf_op jit(solution)/shard_map/ppermute | solution.py:410
  16.9 9.9 %collective-permute-start.8 = (f32[2,256,256]{2,1,0:T(8,128)S(1)}, f32[2,256,256]{2,1,0:T(8,128)S(1)}, u32[]{:S(2)}, u32[]{:S(2)}) collective-permute-start(f32[2,256,256]{2,1,0:T(8,128)S(1)} %get-tuple-element.14.rest_0_), channel_id=1, source_target_pairs={{0,1},{1,0},{2,3},{3,2},{4,5},{5,4},{6,7},{7,6},{8,9},{9,8},{10,11... | collective-permute-start | bytes 1572872 | tf_op jit(solution)/shard_map/ppermute | solution.py:27
  17.0 14.7 %collective-permute-start.6 = (f32[2,384,256]{2,1,0:T(8,128)S(1)}, f32[2,384,256]{2,1,0:T(8,128)S(1)}, u32[]{:S(2)}, u32[]{:S(2)}) collective-permute-start(f32[2,384,256]{2,1,0:T(8,128)S(1)} %get-tuple-element.17), channel_id=1, source_target_pairs={{0,1},{1,0},{2,3},{3,2},{4,5},{5,4},{6,7},{7,6},{8,9},{9,8},{10,11... | collective-permute-start | bytes 2359304 | tf_op jit(solution)/shard_map/ppermute | solution.py:27
  17.5 15.5 %collective-permute-start.7 = (f32[2,384,256]{2,1,0:T(8,128)S(1)}, f32[2,384,256]{2,1,0:T(8,128)S(1)}, u32[]{:S(2)}, u32[]{:S(2)}) collective-permute-start(f32[2,384,256]{2,1,0:T(8,128)S(1)} %get-tuple-element.18), channel_id=1, source_target_pairs={{0,1},{1,0},{2,3},{3,2},{4,5},{5,4},{6,7},{7,6},{8,9},{9,8},{10,11... | collective-permute-start | bytes 2359304 | tf_op jit(solution)/shard_map/ppermute | solution.py:27
  21.5 19.5 %collective-permute-start.11 = (bf16[2,64,2304]{2,1,0:T(8,128)(2,1)S(1)}, bf16[2,64,2304]{2,1,0:T(8,128)(2,1)S(1)}, u32[]{:S(2)}, u32[]{:S(2)}) collective-permute-start(bf16[2,64,2304]{2,1,0:T(8,128)(2,1)S(1)} %get-tuple-element.21), channel_id=1, source_target_pairs={{0,4},{4,0},{8,12},{12,8},{1,5},{5,1},{9,13},{13,9},{2,6},{6,2},{1... | collective-permute-start | bytes 1769480 | tf_op jit(solution)/shard_map/ppermute | solution.py:410
  26.8 39.8 %collective-permute-start.10 = (bf16[2,64,2304]{2,1,0:T(8,128)(2,1)S(1)}, bf16[2,64,2304]{2,1,0:T(8,128)(2,1)S(1)}, u32[]{:S(2)}, u32[]{:S(2)}) collective-permute-start(bf16[2,64,2304]{2,1,0:T(8,128)(2,1)S(1)} %get-tuple-element.20), channel_id=1, source_target_pairs={{0,12},{12,0},{1,13},{13,1},{2,14},{14,2},{3,15},{15,3},{16,28},{2... | collective-permute-start | bytes 1769480 | tf_op jit(solution)/shard_map/ppermute | solution.py:410
  31.7 38.1 %collective-permute-start.4 = (bf16[2,64,2304]{2,1,0:T(8,128)(2,1)S(1)}, bf16[2,64,2304]{2,1,0:T(8,128)(2,1)S(1)}, u32[]{:S(2)}, u32[]{:S(2)}) collective-permute-start(bf16[2,64,2304]{2,1,0:T(8,128)(2,1)S(1)} %get-tuple-element.15), channel_id=1, source_target_pairs={{0,8},{12,4},{1,9},{13,5},{2,10},{14,6},{3,11},{15,7},{16,24},{28,... | collective-permute-start | bytes 1769480 | tf_op jit(solution)/shard_map/ppermute | solution.py:410
  33.3 30.8 %collective-permute-start.15 = (f32[1,1024,256]{2,1,0:T(8,128)S(1)}, f32[1,1024,256]{2,1,0:T(8,128)S(1)}, u32[]{:S(2)}, u32[]{:S(2)}) collective-permute-start(f32[1,1024,256]{2,1,0:T(8,128)S(1)} %get-tuple-element.22), channel_id=1, source_target_pairs={{0,2},{1,3},{2,0},{3,1},{4,6},{5,7},{6,4},{7,5},{8,10},{9,11},{10,... | collective-permute-start | bytes 3145736 | tf_op jit(solution)/shard_map/ppermute | solution.py:27
  34.9 6.1 %copy-start = (bf16[1024,2048]{1,0:T(8,128)(2,1)S(1)}, bf16[1024,2048]{1,0:T(8,128)(2,1)}, u32[]{:S(2)}) copy-start(bf16[1024,2048]{1,0:T(8,128)(2,1)} %tokens_ref.1) | copy-start | bytes 12582916
  34.9 6.1 %copy-start.1 = (bf16[4,2048,64]{1,2,0:T(8,128)(2,1)S(1)}, bf16[4,2048,64]{1,2,0:T(8,128)(2,1)}, u32[]{:S(2)}) copy-start(bf16[4,2048,64]{1,2,0:T(8,128)(2,1)} %param.10) | copy-start | bytes 3145732
  35.5 28.5 %copy-start.2 = (bf16[4,64,256]{2,1,0:T(8,128)(2,1)S(1)}, bf16[4,64,256]{2,1,0:T(8,128)(2,1)}, u32[]{:S(2)}) copy-start(bf16[4,64,256]{2,1,0:T(8,128)(2,1)} %refs_6_.1) | copy-start | bytes 393220
  35.5 34.3 %collective-permute-start.9 = (bf16[2,64,2304]{2,1,0:T(8,128)(2,1)S(1)}, bf16[2,64,2304]{2,1,0:T(8,128)(2,1)S(1)}, u32[]{:S(2)}, u32[]{:S(2)}) collective-permute-start(bf16[2,64,2304]{2,1,0:T(8,128)(2,1)S(1)} %shard_map.86.refs_2_), channel_id=1, source_target_pairs={{4,0},{8,12},{5,1},{9,13},{6,2},{10,14},{7,3},{11,15},{20,16},{24,... | collective-permute-start | bytes 1769480 | tf_op jit(solution)/shard_map/ppermute | solution.py:410
  42.9 1.3 %collective-permute-start.12 = (bf16[4,64,128]{2,1,0:T(8,128)(2,1)S(1)}, bf16[4,64,128]{2,1,0:T(8,128)(2,1)S(1)}, u32[]{:S(2)}, u32[]{:S(2)}) collective-permute-start(bf16[4,64,128]{2,1,0:T(8,128)(2,1)S(1)} %shard_map.87.refs_0_), channel_id=1, source_target_pairs={{0,1},{1,0},{2,3},{3,2},{4,5},{5,4},{6,7},{7,6},{8,9},{9,8},{10,11... | collective-permute-start | bytes 196616 | tf_op jit(solution)/shard_map/ppermute | solution.py:27
  44.2 15.5 %collective-permute-start.13 = (bf16[4,64,128]{2,1,0:T(8,128)(2,1)S(1)}, bf16[4,64,128]{2,1,0:T(8,128)(2,1)S(1)}, u32[]{:S(2)}, u32[]{:S(2)}) collective-permute-start(bf16[4,64,128]{2,1,0:T(8,128)(2,1)S(1)} %shard_map.87.refs_0_), channel_id=1, source_target_pairs={{0,2},{1,3},{2,0},{3,1},{4,6},{5,7},{6,4},{7,5},{8,10},{9,11},{10,... | collective-permute-start | bytes 196616 | tf_op jit(solution)/shard_map/ppermute | solution.py:27
  59.7 4.3 %collective-permute-start.14 = (bf16[4,64,128]{2,1,0:T(8,128)(2,1)S(1)}, bf16[4,64,128]{2,1,0:T(8,128)(2,1)S(1)}, u32[]{:S(2)}, u32[]{:S(2)}) collective-permute-start(bf16[4,64,128]{2,1,0:T(8,128)(2,1)S(1)} %shard_map.87.refs_0_), channel_id=1, source_target_pairs={{0,3},{1,2},{2,1},{3,0},{4,7},{5,6},{6,5},{7,4},{8,11},{9,10},{10,... | collective-permute-start | bytes 196616 | tf_op jit(solution)/shard_map/ppermute | solution.py:27
  67.9 4.5 %collective-permute-start.19 = (bf16[2,64,128]{2,1,0:T(8,128)(2,1)S(1)}, bf16[2,64,128]{2,1,0:T(8,128)(2,1)S(1)}, u32[]{:S(2)}, u32[]{:S(2)}) collective-permute-start(bf16[2,64,128]{2,1,0:T(8,128)(2,1)S(1)} %shard_map.89.refs_2_.refs_0_), channel_id=1, source_target_pairs={{0,1},{1,0},{2,3},{3,2},{4,5},{5,4},{6,7},{7,6},{8,9},{9,8},{10,11... | collective-permute-start | bytes 98312 | tf_op jit(solution)/shard_map/ppermute | solution.py:27
  68.1 5.0 %collective-permute-start.20 = (bf16[2,64,128]{2,1,0:T(8,128)(2,1)S(1)}, bf16[2,64,128]{2,1,0:T(8,128)(2,1)S(1)}, u32[]{:S(2)}, u32[]{:S(2)}) collective-permute-start(bf16[2,64,128]{2,1,0:T(8,128)(2,1)S(1)} %shard_map.89.refs_2_.refs_0_), channel_id=1, source_target_pairs={{0,2},{1,3},{2,0},{3,1},{4,6},{5,7},{6,4},{7,5},{8,10},{9,11},{10,... | collective-permute-start | bytes 98312 | tf_op jit(solution)/shard_map/ppermute | solution.py:27
  68.9 4.2 %collective-permute-start.21 = (bf16[2,64,128]{2,1,0:T(8,128)(2,1)S(1)}, bf16[2,64,128]{2,1,0:T(8,128)(2,1)S(1)}, u32[]{:S(2)}, u32[]{:S(2)}) collective-permute-start(bf16[2,64,128]{2,1,0:T(8,128)(2,1)S(1)} %shard_map.89.refs_2_.refs_0_), channel_id=1, source_target_pairs={{0,3},{1,2},{2,1},{3,0},{4,7},{5,6},{6,5},{7,4},{8,11},{9,10},{10,... | collective-permute-start | bytes 98312 | tf_op jit(solution)/shard_map/ppermute | solution.py:27
  71.1 3.7 %collective-permute-start.16 = (bf16[2,64,128]{2,1,0:T(8,128)(2,1)S(1)}, bf16[2,64,128]{2,1,0:T(8,128)(2,1)S(1)}, u32[]{:S(2)}, u32[]{:S(2)}) collective-permute-start(bf16[2,64,128]{2,1,0:T(8,128)(2,1)S(1)} %shard_map.90.refs_0_), channel_id=1, source_target_pairs={{0,1},{1,0},{2,3},{3,2},{4,5},{5,4},{6,7},{7,6},{8,9},{9,8},{10,11... | collective-permute-start | bytes 98312 | tf_op jit(solution)/shard_map/ppermute | solution.py:27
  71.7 4.1 %collective-permute-start.17 = (bf16[2,64,128]{2,1,0:T(8,128)(2,1)S(1)}, bf16[2,64,128]{2,1,0:T(8,128)(2,1)S(1)}, u32[]{:S(2)}, u32[]{:S(2)}) collective-permute-start(bf16[2,64,128]{2,1,0:T(8,128)(2,1)S(1)} %shard_map.90.refs_0_), channel_id=1, source_target_pairs={{0,2},{1,3},{2,0},{3,1},{4,6},{5,7},{6,4},{7,5},{8,10},{9,11},{10,... | collective-permute-start | bytes 98312 | tf_op jit(solution)/shard_map/ppermute | solution.py:27
  72.4 3.7 %collective-permute-start.18 = (bf16[2,64,128]{2,1,0:T(8,128)(2,1)S(1)}, bf16[2,64,128]{2,1,0:T(8,128)(2,1)S(1)}, u32[]{:S(2)}, u32[]{:S(2)}) collective-permute-start(bf16[2,64,128]{2,1,0:T(8,128)(2,1)S(1)} %shard_map.90.refs_0_), channel_id=1, source_target_pairs={{0,3},{1,2},{2,1},{3,0},{4,7},{5,6},{6,5},{7,4},{8,11},{9,10},{10,... | collective-permute-start | bytes 98312 | tf_op jit(solution)/shard_map/ppermute | solution.py:27

commit v8 on v6

--- a/solution.py
+++ b/solution.py
@@ -9,8 +9,9 @@
 
 ADAPTER_SCALE = 0.5
 ROW_TILE = 256
-PARAMS = pltpu.CompilerParams(vmem_limit_bytes=16 * 1024 * 1024)
+PARAMS = pltpu.CompilerParams(vmem_limit_bytes=20 * 1024 * 1024)
 NO_COST = pl.CostEstimate(flops=0, bytes_accessed=0, transcendentals=0)
+BASE = pl.CostEstimate(flops=4 * 10**9, bytes_accessed=0, transcendentals=0)
 SHORT = pl.CostEstimate(flops=10 * 10**9, bytes_accessed=0, transcendentals=0)
 MIDDLE = pl.CostEstimate(flops=0 * 10**9, bytes_accessed=0, transcendentals=0)
 LONG = pl.CostEstimate(flops=6 * 10**9, bytes_accessed=0, transcendentals=0)
@@ -27,62 +28,73 @@
     return lax.ppermute(value, axis, pairs)
 
 
+def run_copies(copies):
+    for copy in copies:
+        copy.start()
+    return copies
+
+
 def piece_rows(rows):
     large = rows * 3 // 8
     return [large, large, rows - 2 * large]
 
 
-def base_kernel(half, chunks_ref, tokens_ref, weight_ref, *refs):
-    del chunks_ref
-    *sent_refs, kept_ref = refs
-
-    def write(out_ref, first, size):
-        for start in range(0, size, ROW_TILE):
-            stop = min(start + ROW_TILE, size)
-            out_ref[0, start:stop, :] = jnp.dot(
-                tokens_ref[first + start : first + stop, :],
-                weight_ref[...],
+def base_kernel(order, tokens_ref, weight_ref, *refs):
+    *sent_refs, kept_ref, tokens, weight, sems = refs
+    half, rows, width = kept_ref.shape
+    place = lax.axis_index("tensor")
+    copies = []
+    for number, (source, held) in enumerate(((weight_ref, weight), (tokens_ref, tokens))):
+        tile = held.shape[0] // sems.shape[1]
+        for i in range(sems.shape[1]):
+            part = pl.ds(i * tile, tile)
+            copies.append(
+                pltpu.make_async_copy(source.at[part], held.at[part], sems.at[number, i])
+            )
+    run_copies(copies)
+    for copy in copies[: sems.shape[1]]:
+        copy.wait()
+    tile = rows // sems.shape[1]
+    for first in range(0, rows, tile):
+        copies[sems.shape[1] + first // tile].wait()
+        for number, offset in enumerate(order):
+            columns = pl.ds(pl.multiple_of((place ^ offset) * width, width), width)
+            part = jnp.dot(
+                tokens[first : first + tile, :],
+                weight[:, columns],
                 preferred_element_type=jnp.float32,
             )
-
-    @pl.when(pl.program_id(0) < half)
-    def _():
-        first = 0
-        for sent_ref in sent_refs:
-            write(sent_ref, first, sent_ref.shape[1])
-            first += sent_ref.shape[1]
-
-    @pl.when(pl.program_id(0) >= half)
-    def _():
-        write(kept_ref, 0, kept_ref.shape[1])
+            if number >= half:
+                kept_ref[number - half, first : first + tile, :] = part
+                continue
+            start = 0
+            for sent_ref in sent_refs:
+                stop = start + sent_ref.shape[1]
+                low, high = max(first, start), min(first + tile, stop)
+                if low < high:
+                    sent_ref[number, low - start : high - start, :] = part[
+                        low - first : high - first
+                    ]
+                start = stop
 
 
 def base_chunks(tokens, weight, order, width):
-    rows, depth = tokens.shape
+    rows = tokens.shape[0]
     half = len(order) // 2
-    sizes = piece_rows(rows)
-    chunks = lax.axis_index("tensor") ^ jnp.asarray(order, jnp.int32)
+    sizes = [*piece_rows(rows), rows]
     *sent, kept = pl.pallas_call(
-        functools.partial(base_kernel, half),
-        grid_spec=pltpu.PrefetchScalarGridSpec(
-            num_scalar_prefetch=1,
-            grid=(len(order),),
-            in_specs=[
-                pl.BlockSpec(tokens.shape, lambda i, c: (0, 0), pipeline_mode=pl.Buffered(1)),
-                pl.BlockSpec((depth, width), lambda i, c: (0, c[i])),
-            ],
-            out_specs=[
-                pl.BlockSpec((1, size, width), lambda i, c: (jnp.minimum(i, half - 1), 0, 0))
-                for size in sizes
-            ]
-            + [pl.BlockSpec((1, rows, width), lambda i, c: (jnp.maximum(i - half, 0), 0, 0))],
-        ),
-        out_shape=[
-            jax.ShapeDtypeStruct((half, size, width), jnp.float32) for size in [*sizes, rows]
+        functools.partial(base_kernel, order),
+        in_specs=[ANY] * 2,
+        out_specs=[pl.BlockSpec(memory_space=pltpu.VMEM)] * len(sizes),
+        out_shape=[jax.ShapeDtypeStruct((half, size, width), jnp.float32) for size in sizes],
+        scratch_shapes=[
+            pltpu.VMEM(tokens.shape, tokens.dtype),
+            pltpu.VMEM(weight.shape, weight.dtype),
+            pltpu.SemaphoreType.DMA((2, 4)),
         ],
         compiler_params=PARAMS,
-        cost_estimate=NO_COST,
-    )(chunks, in_hbm(tokens), in_hbm(weight))
+        cost_estimate=BASE,
+    )(in_hbm(tokens), in_hbm(weight))
     return sent, kept
 
 
@@ -94,16 +106,20 @@
         rows = pl.ds(start, arrived_ref.shape[1])
         for i in range(half):
             mine_ref[i, rows, :] = kept_ref[i, rows, :] + arrived_ref[i]
-            out_ref[i, rows, :] = kept_ref[half + i, rows, :] + arrived_ref[half + i]
+            out = kept_ref[half + i, rows, :] + arrived_ref[half + i]
+            out_ref[i, rows, :] = out.astype(out_ref.dtype)
         start += arrived_ref.shape[1]
 
 
-def add_halves(kept, arrived):
+def add_halves(kept, arrived, sent_type):
     count, rows, width = kept.shape
-    out = jax.ShapeDtypeStruct((count // 2, rows, width), jnp.float32)
+    shape = (count // 2, rows, width)
     return pl.pallas_call(
         add_kernel,
-        out_shape=[out, out],
+        out_shape=[
+            jax.ShapeDtypeStruct(shape, sent_type),
+            jax.ShapeDtypeStruct(shape, jnp.float32),
+        ],
         compiler_params=PARAMS,
         cost_estimate=NO_COST,
     )(kept, *arrived)
@@ -119,8 +135,10 @@
 def base_sum(sent, kept):
     arrived = [swap(piece, "tensor", 1) for piece in sent]
     distance = 2
-    while distance < lax.axis_size("tensor"):
-        sent, kept = add_halves(kept, arrived)
+    size = lax.axis_size("tensor")
+    while distance < size:
+        sent_type = jnp.bfloat16 if 2 * distance == size else jnp.float32
+        sent, kept = add_halves(kept, arrived, sent_type)
         arrived = [swap(sent, "tensor", distance)]
         distance *= 2
     return kept[0], arrived[0][0]
@@ -148,12 +166,6 @@
         pltpu.make_async_copy(down_ref.at[slot], out_ref.at[k, :, pl.ds(0, depth)], sems.at[k, 0]),
         pltpu.make_async_copy(up_ref.at[slot], out_ref.at[k, :, pl.ds(depth, width)], sems.at[k, 1]),
     ]
-
-
-def run_copies(copies):
-    for copy in copies:
-        copy.start()
-    return copies
 
 
 def plan_kernel(capacity, holder_slots, *refs):
@@ -304,7 +316,7 @@
     for_phase(phases, choose, plan_ref, refs, act)
 
 
-def shrink(plan, row_blocks, phases, choose, after=()):
+def shrink(plan, row_blocks, phases, choose, after=(), kind=jnp.float32):
     rows, depth = row_blocks.shape[1:]
     rank = phases[0][2][0][0].shape[1]
     total = sum(count for _, count, _ in phases)
@@ -322,7 +334,7 @@
             + [ANY] * len(after),
             out_specs=pl.BlockSpec((1, rank, rows), lambda i, plan: (i, 0, 0)),
         ),
-        out_shape=jax.ShapeDtypeStruct((total, rank, rows), jnp.bfloat16),
+        out_shape=jax.ShapeDtypeStruct((total, rank, rows), kind),
         compiler_params=PARAMS,
         cost_estimate=NO_COST,
     )(plan, row_blocks, *operands, *after)
@@ -429,7 +441,7 @@
     out = write(0, first_parts, first_up, [[0], [up_column]], None, MIDDLE)
     middle_part = shrink(plan, row_blocks, middle, choose, [in_hbm(out)])
     middle_parts = exchange(middle_part)
-    last_parts = exchange(shrink(plan, row_blocks, last, choose, [middle_part]))
+    last_parts = exchange(shrink(plan, row_blocks, last, choose, [middle_part], jnp.bfloat16))
     out = write(2, middle_parts, middle_up, [[0, up_column]], out)
     return write(3, last_parts, last, [[up_column] * 2], out)
 

time: 76.6 us -> 72.5 us (0.946)
  waiting for transfers between devices: 24.7 us -> 21.2 us
    ppermute x16, waiting for transfers between devices: 20.3 us -> 12.1 us  [swap(): return lax.ppermute(value, axis, pairs)]
    ppermute x6, waiting for transfers between devices: 4.38 us -> 9.07 us  [across(): return lax.ppermute(value, 'pool', pairs)]
  transfers between devices with their start and end apart: 22 -> 22, of which waited for: 6 -> 8; matrix products, arithmetic and copies ran while one was open for 1% -> 0% of each run, Pallas kernels for 29% -> 30%
where the time goes in v8:
time: 72.5 us; the launch traced here: 72 us
  starting transfers between devices  27.5 us (38%)
  Pallas kernels  23.1 us (32%)
  waiting for transfers between devices  21.2 us (29%)
    ppermute x6, starting transfers between devices, across(): return lax.ppermute(value, 'pool', pairs)  13.9 us
    ppermute x16, starting transfers between devices, swap(): return lax.ppermute(value, axis, pairs)  13.6 us
    ppermute x16, waiting for transfers between devices, swap(): return lax.ppermute(value, axis, pairs)  12.1 us
    ppermute x6, waiting for transfers between devices, across(): return lax.ppermute(value, 'pool', pairs)  9.07 us
    pallas_call x1, Pallas kernels, base_chunks(): pl.pallas_call(functools.partial(base_kernel, order), in_specs=[ANY] * 2,...  7.78 us
    pallas_call x3, Pallas kernels, combine(): pl.pallas_call(functools.partial(combine_kernel, shapes, choose, len(part...  5.99 us
    pallas_call x3, Pallas kernels, shrink(): pl.pallas_call(functools.partial(shrink_kernel, shapes, choose), grid_spe...  4.5 us
    pallas_call x2, Pallas kernels, pack_panels(): pl.pallas_call(functools.partial(pack_kernel, starts, capacity), in_specs...  2.91 us
  transfers between devices with their start and end apart: 22, of which 8 were waited for; matrix products, arithmetic and copies ran while one was open for 0% of the time, Pallas kernels for 30%

profile of v8, /device:TPU:0, one launch (start us, length us, event | category | flops | bytes accessed | tf_op | source)
XLA Modules:
  0.0 72.0 jit_solution(12029019415153535324)
XLA Ops:
  0.0 3.0 %collective-permute-start = (s32[1,8]{1,0:T(1,128)}, s32[1,8]{1,0:T(1,128)S(1)}, u32[]{:S(2)}, u32[]{:S(2)}) collective-permute-start(s32[1,8]{1,0:T(1,128)} %refs_0_.1), channel_id=1, source_target_pairs={{0,4},{4,0},{8,12},{12,8},{1,5},{5,1},{9,13},{13,9},{2,6},{6,2},{1... | collective-permute-start | bytes 104 | tf_op jit(solution)/shard_map/ppermute | solution.py:28
  3.0 2.6 %collective-permute-start.1 = (s32[1,8]{1,0:T(1,128)}, s32[1,8]{1,0:T(1,128)S(1)}, u32[]{:S(2)}, u32[]{:S(2)}) collective-permute-start(s32[1,8]{1,0:T(1,128)} %refs_0_.1), channel_id=1, source_target_pairs={{0,8},{4,12},{8,0},{12,4},{1,9},{5,13},{9,1},{13,5},{2,10},{6,14},... | collective-permute-start | bytes 104 | tf_op jit(solution)/shard_map/ppermute | solution.py:28
  5.6 0.0 collective-permute-start.2
  5.6 0.7 collective-permute-start.3
  6.3 0.7 %collective-permute-start.5 = (bf16[4,64,2048]{2,1,0:T(8,128)(2,1)}, bf16[4,64,2048]{2,1,0:T(8,128)(2,1)S(1)}, u32[]{:S(2)}, u32[]{:S(2)}) collective-permute-start(bf16[4,64,2048]{2,1,0:T(8,128)(2,1)} %bitcast.14), channel_id=1, source_target_pairs={{4,8},{8,4},{5,9},{9,5},{6,10},{10,6},{7,11},{11,7},{20,24},{24,20... | collective-permute-start | bytes 3145736 | tf_op jit(solution)/shard_map/ppermute | solution.py:405
  7.0 7.8 %shard_map.74 = (f32[2,384,256]{2,1,0:T(8,128)S(1)}, f32[2,384,256]{2,1,0:T(8,128)S(1)}, f32[2,256,256]{2,1,0:T(8,128)S(1)}, f32[2,1024,256]{2,1,0:T(8,128)S(1)}) custom-call(bf16[1024,2048]{1,0:T(8,128)(2,1)} %tokens_ref.1, bf16[2048,1024]{1,0:T(8,128)(2,1)} %weight_ref.1), custom_call_target="tpu_custom_call" | custom-call | flops 4000000000 | tf_op jit(solution)/shard_map/pallas_call | solution.py:85
  14.8 0.0 collective-permute-done.refs_1_
  14.8 0.1 collective-permute-start.8
  14.9 0.0 collective-permute-done.1.refs_2_
  14.9 0.5 collective-permute-start.6
  15.4 0.0 collective-permute-done.2.refs_3_
  15.4 0.1 collective-permute-start.7
  15.5 0.0 collective-permute-done.3.refs_6_.up_ref
  15.5 1.7 %shard_map.73.plan_ref = s32[30]{0:T(128)S(1)} custom-call(s32[1,8]{1,0:T(1,128)} %refs_0_.1, s32[1,8]{1,0:T(1,128)S(1)} %collective-permute-done.refs_1_, s32[1,8]{1,0:T(1,128)S(1)} %collective-permute-done.1.refs_2_, s32[1,8]{1,0:T(1,128)S(1)} %collective-permute-done.2.refs_3_, s32[16]{0:T(128)} %refs_4_.1, s32[1,8]{1,0:T(1,128)} %refs_5_.1, ...), custom_call_target="tpu_custom_call" | custom-call | flops 10000000000 | tf_op jit(solution)/shard_map/pallas_call | solution.py:212
  17.2 2.3 %shard_map.75 = (bf16[2,64,2304]{2,1,0:T(8,128)(2,1)S(1)}, bf16[2,64,2304]{2,1,0:T(8,128)(2,1)S(1)}, bf16[2,64,2304]{2,1,0:T(8,128)(2,1)S(1)}) custom-call(s32[30]{0:T(128)S(1)} %shard_map.73.plan_ref, bf16[4,64,2048]{2,1,0:T(8,128)(2,1)} %bitcast.15, bf16[4,64,256]{2,1,0:T(8,128)(2,1)} %refs_6_.1, f32[2,256,256]{2,1,0:T(8,128)S(1)} %get-tuple-element.14.rest_0_), custom_call_target="tpu_custom_call" | custom-call | tf_op jit(solution)/shard_map/pallas_call | solution.py:244
  19.4 5.3 %collective-permute-start.11 = (bf16[2,64,2304]{2,1,0:T(8,128)(2,1)S(1)}, bf16[2,64,2304]{2,1,0:T(8,128)(2,1)S(1)}, u32[]{:S(2)}, u32[]{:S(2)}) collective-permute-start(bf16[2,64,2304]{2,1,0:T(8,128)(2,1)S(1)} %get-tuple-element.21), channel_id=1, source_target_pairs={{0,4},{4,0},{8,12},{12,8},{1,5},{5,1},{9,13},{13,9},{2,6},{6,2},{1... | collective-permute-start | bytes 1769480 | tf_op jit(solution)/shard_map/ppermute | solution.py:405
  24.7 0.0 collective-permute-done.8.refs_2_
  24.7 4.3 %collective-permute-start.10 = (bf16[2,64,2304]{2,1,0:T(8,128)(2,1)S(1)}, bf16[2,64,2304]{2,1,0:T(8,128)(2,1)S(1)}, u32[]{:S(2)}, u32[]{:S(2)}) collective-permute-start(bf16[2,64,2304]{2,1,0:T(8,128)(2,1)S(1)} %get-tuple-element.20), channel_id=1, source_target_pairs={{0,12},{12,0},{1,13},{13,1},{2,14},{14,2},{3,15},{15,3},{16,28},{2... | collective-permute-start | bytes 1769480 | tf_op jit(solution)/shard_map/ppermute | solution.py:405
  29.1 0.0 collective-permute-done.6.refs_0_
  29.1 1.3 %collective-permute-start.4 = (bf16[2,64,2304]{2,1,0:T(8,128)(2,1)S(1)}, bf16[2,64,2304]{2,1,0:T(8,128)(2,1)S(1)}, u32[]{:S(2)}, u32[]{:S(2)}) collective-permute-start(bf16[2,64,2304]{2,1,0:T(8,128)(2,1)S(1)} %get-tuple-element.15), channel_id=1, source_target_pairs={{0,8},{12,4},{1,9},{13,5},{2,10},{14,6},{3,11},{15,7},{16,24},{28,... | collective-permute-start | bytes 1769480 | tf_op jit(solution)/shard_map/ppermute | solution.py:405
  30.4 0.0 collective-permute-done.7.refs_1_
  30.4 0.2 shard_map.76
  30.7 1.5 %collective-permute-start.15 = (bf16[1,1024,256]{2,1,0:T(8,128)(2,1)S(1)}, bf16[1,1024,256]{2,1,0:T(8,128)(2,1)S(1)}, u32[]{:S(2)}, u32[]{:S(2)}) collective-permute-start(bf16[1,1024,256]{2,1,0:T(8,128)(2,1)S(1)} %get-tuple-element.22), channel_id=1, source_target_pairs={{0,2},{1,3},{2,0},{3,1},{4,6},{5,7},{6,4},{7,5},{8,10},{9,11},{10,... | collective-permute-start | bytes 1572872 | tf_op jit(solution)/shard_map/ppermute | solution.py:28
  32.2 0.0 collective-permute-done.5.down_ref.refs_0_
  32.2 0.0 copy-start
  32.2 0.0 copy-start.1
  32.2 0.6 shard_map.77.refs_2_
  32.9 0.0 copy-start.2
  32.9 1.6 %collective-permute-start.9 = (bf16[2,64,2304]{2,1,0:T(8,128)(2,1)S(1)}, bf16[2,64,2304]{2,1,0:T(8,128)(2,1)S(1)}, u32[]{:S(2)}, u32[]{:S(2)}) collective-permute-start(bf16[2,64,2304]{2,1,0:T(8,128)(2,1)S(1)} %shard_map.77.refs_2_), channel_id=1, source_target_pairs={{4,0},{8,12},{5,1},{9,13},{6,2},{10,14},{7,3},{11,15},{20,16},{24,... | collective-permute-start | bytes 1769480 | tf_op jit(solution)/shard_map/ppermute | solution.py:405
  34.4 4.5 %collective-permute-done.11.refs_1_.refs_7_ = bf16[2,64,2304]{2,1,0:T(8,128)(2,1)S(1)} collective-permute-done((bf16[2,64,2304]{2,1,0:T(8,128)(2,1)S(1)}, bf16[2,64,2304]{2,1,0:T(8,128)(2,1)S(1)}, u32[]{:S(2)}, u32[]{:S(2)}) %collective-permute-start.11) | collective-permute-done | bytes 589856 | tf_op jit(solution)/shard_map/ppermute | solution.py:405
  38.9 0.0 copy-done
  38.9 0.0 copy-done.1
  38.9 1.9 %shard_map.78.refs_0_ = f32[4,64,128]{2,1,0:T(8,128)S(1)} custom-call(s32[30]{0:T(128)S(1)} %shard_map.73.plan_ref, bf16[8,128,2048]{2,1,0:T(8,128)(2,1)S(1)} %bitcast.4, bf16[4,64,2048]{2,1,0:T(8,128)(2,1)S(1)} %bitcast.16, bf16[2,64,2304]{2,1,0:T(8,128)(2,1)S(1)} %collective-permute-done.11.refs_1_.refs_7_, bf16[2,64,2304]{2,1,0:T(8,128)(2,1)S(1)} %shard_map.77.refs_2_), custom_call_target="tpu_custom_call" | custom-call | tf_op jit(solution)/shard_map/pallas_call | solution.py:327
  40.9 0.1 collective-permute-start.12
  40.9 1.3 %collective-permute-done.12.refs_1_ = f32[4,64,128]{2,1,0:T(8,128)S(1)} collective-permute-done((f32[4,64,128]{2,1,0:T(8,128)S(1)}, f32[4,64,128]{2,1,0:T(8,128)S(1)}, u32[]{:S(2)}, u32[]{:S(2)}) %collective-permute-start.12) | collective-permute-done | bytes 131104 | tf_op jit(solution)/shard_map/ppermute | solution.py:28
  42.3 1.5 %collective-permute-start.13 = (f32[4,64,128]{2,1,0:T(8,128)S(1)}, f32[4,64,128]{2,1,0:T(8,128)S(1)}, u32[]{:S(2)}, u32[]{:S(2)}) collective-permute-start(f32[4,64,128]{2,1,0:T(8,128)S(1)} %shard_map.78.refs_0_), channel_id=1, source_target_pairs={{0,2},{1,3},{2,0},{3,1},{4,6},{5,7},{6,4},{7,5},{8,10},{9,11},{10,... | collective-permute-start | bytes 393224 | tf_op jit(solution)/shard_map/ppermute | solution.py:28
  43.8 4.1 %collective-permute-done.13.refs_2_ = f32[4,64,128]{2,1,0:T(8,128)S(1)} collective-permute-done((f32[4,64,128]{2,1,0:T(8,128)S(1)}, f32[4,64,128]{2,1,0:T(8,128)S(1)}, u32[]{:S(2)}, u32[]{:S(2)}) %collective-permute-start.13) | collective-permute-done | bytes 131104 | tf_op jit(solution)/shard_map/ppermute | solution.py:28
  47.8 0.4 collective-permute-start.14
  48.2 5.3 %collective-permute-done.14.refs_3_ = f32[4,64,128]{2,1,0:T(8,128)S(1)} collective-permute-done((f32[4,64,128]{2,1,0:T(8,128)S(1)}, f32[4,64,128]{2,1,0:T(8,128)S(1)}, u32[]{:S(2)}, u32[]{:S(2)}) %collective-permute-start.14) | collective-permute-done | bytes 131104 | tf_op jit(solution)/shard_map/ppermute | solution.py:28
  53.6 0.0 collective-permute-done.15
  53.6 0.0 copy-done.2
  53.6 2.6 %shard_map.79.refs_2_.refs_8_ = bf16[1024,256]{1,0:T(8,128)(2,1)} custom-call(s32[30]{0:T(128)S(1)} %shard_map.73.plan_ref, f32[4,64,128]{2,1,0:T(8,128)S(1)} %shard_map.78.refs_0_, f32[4,64,128]{2,1,0:T(8,128)S(1)} %collective-permute-done.12.refs_1_, f32[4,64,128]{2,1,0:T(8,128)S(1)} %collective-permute-done.13.refs_2_, ...), custom_call_target="tpu_custom_call" | custom-call | tf_op jit(solution)/shard_map/pallas_call | solution.py:386
  56.1 0.0 collective-permute-done.10.refs_1_.refs_7_
  56.2 1.3 %shard_map.80.refs_2_.refs_0_ = f32[2,64,128]{2,1,0:T(8,128)S(1)} custom-call(s32[30]{0:T(128)S(1)} %shard_map.73.plan_ref, bf16[8,128,2048]{2,1,0:T(8,128)(2,1)S(1)} %bitcast.5, bf16[4,64,2048]{2,1,0:T(8,128)(2,1)S(1)} %collective-permute-done.5.down_ref.refs_0_, bf16[2,64,2304]{2,1,0:T(8,128)(2,1)S(1)} %collective-permute-done.10.refs_1_.refs_7_, ...), custom_call_target="tpu_custom_call" | custom-call | tf_op jit(solution)/shard_map/pallas_call | solution.py:327
  57.4 0.2 collective-permute-start.19
  57.6 0.9 %collective-permute-start.20 = (f32[2,64,128]{2,1,0:T(8,128)S(1)}, f32[2,64,128]{2,1,0:T(8,128)S(1)}, u32[]{:S(2)}, u32[]{:S(2)}) collective-permute-start(f32[2,64,128]{2,1,0:T(8,128)S(1)} %shard_map.80.refs_2_.refs_0_), channel_id=1, source_target_pairs={{0,2},{1,3},{2,0},{3,1},{4,6},{5,7},{6,4},{7,5},{8,10},{9,11},{10,... | collective-permute-start | bytes 196616 | tf_op jit(solution)/shard_map/ppermute | solution.py:28
  58.6 0.8 %collective-permute-start.21 = (f32[2,64,128]{2,1,0:T(8,128)S(1)}, f32[2,64,128]{2,1,0:T(8,128)S(1)}, u32[]{:S(2)}, u32[]{:S(2)}) collective-permute-start(f32[2,64,128]{2,1,0:T(8,128)S(1)} %shard_map.80.refs_2_.refs_0_), channel_id=1, source_target_pairs={{0,3},{1,2},{2,1},{3,0},{4,7},{5,6},{6,5},{7,4},{8,11},{9,10},{10,... | collective-permute-start | bytes 196616 | tf_op jit(solution)/shard_map/ppermute | solution.py:28
  59.4 3.9 %collective-permute-done.4.refs_0_.refs_6_ = bf16[2,64,2304]{2,1,0:T(8,128)(2,1)S(1)} collective-permute-done((bf16[2,64,2304]{2,1,0:T(8,128)(2,1)S(1)}, bf16[2,64,2304]{2,1,0:T(8,128)(2,1)S(1)}, u32[]{:S(2)}, u32[]{:S(2)}) %collective-permute-start.4) | collective-permute-done | bytes 589856 | tf_op jit(solution)/shard_map/ppermute | solution.py:405
  63.2 0.7 %collective-permute-done.9.refs_1_.refs_7_ = bf16[2,64,2304]{2,1,0:T(8,128)(2,1)S(1)} collective-permute-done((bf16[2,64,2304]{2,1,0:T(8,128)(2,1)S(1)}, bf16[2,64,2304]{2,1,0:T(8,128)(2,1)S(1)}, u32[]{:S(2)}, u32[]{:S(2)}) %collective-permute-start.9) | collective-permute-done | bytes 589856 | tf_op jit(solution)/shard_map/ppermute | solution.py:405
  63.9 1.3 %shard_map.81.refs_0_ = bf16[2,64,128]{2,1,0:T(8,128)(2,1)S(1)} custom-call(s32[30]{0:T(128)S(1)} %shard_map.73.plan_ref, bf16[8,128,2048]{2,1,0:T(8,128)(2,1)S(1)} %bitcast.6, bf16[2,64,2304]{2,1,0:T(8,128)(2,1)S(1)} %collective-permute-done.4.refs_0_.refs_6_, bf16[2,64,2304]{2,1,0:T(8,128)(2,1)S(1)} %collective-permute-done.9.refs_1_.refs_7_, ...), custom_call_target="tpu_custom_call" | custom-call | tf_op jit(solution)/shard_map/pallas_call | solution.py:327
  65.3 0.1 collective-permute-start.16
  65.3 1.6 %collective-permute-start.17 = (bf16[2,64,128]{2,1,0:T(8,128)(2,1)S(1)}, bf16[2,64,128]{2,1,0:T(8,128)(2,1)S(1)}, u32[]{:S(2)}, u32[]{:S(2)}) collective-permute-start(bf16[2,64,128]{2,1,0:T(8,128)(2,1)S(1)} %shard_map.81.refs_0_), channel_id=1, source_target_pairs={{0,2},{1,3},{2,0},{3,1},{4,6},{5,7},{6,4},{7,5},{8,10},{9,11},{10,... | collective-permute-start | bytes 98312 | tf_op jit(solution)/shard_map/ppermute | solution.py:28
  66.9 0.0 collective-permute-done.19.refs_1_
  66.9 0.3 collective-permute-start.18
  67.2 0.0 collective-permute-done.20.refs_2_
  67.2 0.0 collective-permute-done.21.refs_3_
  67.2 1.7 %shard_map.82.refs_8_ = bf16[1024,256]{1,0:T(8,128)(2,1)} custom-call(s32[30]{0:T(128)S(1)} %shard_map.73.plan_ref, f32[2,64,128]{2,1,0:T(8,128)S(1)} %shard_map.80.refs_2_.refs_0_, f32[2,64,128]{2,1,0:T(8,128)S(1)} %collective-permute-done.19.refs_1_, f32[2,64,128]{2,1,0:T(8,128)S(1)} %collective-permute-done.20.refs_2_, ...), custom_call_target="tpu_custom_call", output_to_operand_aliasing={{}: (9, {})} | custom-call | tf_op jit(solution)/shard_map/pallas_call | solution.py:386
  68.9 0.0 collective-permute-done.16.refs_1_
  68.9 0.4 collective-permute-done.17.refs_2_
  69.3 0.9 %collective-permute-done.18.refs_3_ = bf16[2,64,128]{2,1,0:T(8,128)(2,1)S(1)} collective-permute-done((bf16[2,64,128]{2,1,0:T(8,128)(2,1)S(1)}, bf16[2,64,128]{2,1,0:T(8,128)(2,1)S(1)}, u32[]{:S(2)}, u32[]{:S(2)}) %collective-permute-start.18) | collective-permute-done | bytes 32800 | tf_op jit(solution)/shard_map/ppermute | solution.py:28
  70.2 1.7 %shard_map.83 = bf16[1024,256]{1,0:T(8,128)(2,1)} custom-call(s32[30]{0:T(128)S(1)} %shard_map.73.plan_ref, bf16[2,64,128]{2,1,0:T(8,128)(2,1)S(1)} %shard_map.81.refs_0_, bf16[2,64,128]{2,1,0:T(8,128)(2,1)S(1)} %collective-permute-done.16.refs_1_, bf16[2,64,128]{2,1,0:T(8,128)(2,1)S(1)} %collective-permute-done.17.refs_2_, ...), custom_call_target="tpu_custom_call", output_to_operand_aliasing={{}: (9, {})} | custom-call | tf_op jit(solution)/shard_map/pallas_call | solution.py:386
Async XLA Ops:
  0.0 14.8 %collective-permute-start = (s32[1,8]{1,0:T(1,128)}, s32[1,8]{1,0:T(1,128)S(1)}, u32[]{:S(2)}, u32[]{:S(2)}) collective-permute-start(s32[1,8]{1,0:T(1,128)} %refs_0_.1), channel_id=1, source_target_pairs={{0,4},{4,0},{8,12},{12,8},{1,5},{5,1},{9,13},{13,9},{2,6},{6,2},{1... | collective-permute-start | bytes 104 | tf_op jit(solution)/shard_map/ppermute | solution.py:28
  3.0 11.9 %collective-permute-start.1 = (s32[1,8]{1,0:T(1,128)}, s32[1,8]{1,0:T(1,128)S(1)}, u32[]{:S(2)}, u32[]{:S(2)}) collective-permute-start(s32[1,8]{1,0:T(1,128)} %refs_0_.1), channel_id=1, source_target_pairs={{0,8},{4,12},{8,0},{12,4},{1,9},{5,13},{9,1},{13,5},{2,10},{6,14},... | collective-permute-start | bytes 104 | tf_op jit(solution)/shard_map/ppermute | solution.py:28
  5.6 9.8 %collective-permute-start.2 = (s32[1,8]{1,0:T(1,128)}, s32[1,8]{1,0:T(1,128)S(1)}, u32[]{:S(2)}, u32[]{:S(2)}) collective-permute-start(s32[1,8]{1,0:T(1,128)} %refs_0_.1), channel_id=1, source_target_pairs={{0,12},{4,8},{8,4},{12,0},{1,13},{5,9},{9,5},{13,1},{2,14},{6,10},... | collective-permute-start | bytes 104 | tf_op jit(solution)/shard_map/ppermute | solution.py:28
  5.6 9.9 %collective-permute-start.3 = (bf16[4,64,256]{2,1,0:T(8,128)(2,1)}, bf16[4,64,256]{2,1,0:T(8,128)(2,1)S(1)}, u32[]{:S(2)}, u32[]{:S(2)}) collective-permute-start(bf16[4,64,256]{2,1,0:T(8,128)(2,1)} %refs_6_.1), channel_id=1, source_target_pairs={{4,8},{8,4},{5,9},{9,5},{6,10},{10,6},{7,11},{11,7},{20,24},{24,20... | collective-permute-start | bytes 393224 | tf_op jit(solution)/shard_map/ppermute | solution.py:405
  6.3 25.9 %collective-permute-start.5 = (bf16[4,64,2048]{2,1,0:T(8,128)(2,1)}, bf16[4,64,2048]{2,1,0:T(8,128)(2,1)S(1)}, u32[]{:S(2)}, u32[]{:S(2)}) collective-permute-start(bf16[4,64,2048]{2,1,0:T(8,128)(2,1)} %bitcast.14), channel_id=1, source_target_pairs={{4,8},{8,4},{5,9},{9,5},{6,10},{10,6},{7,11},{11,7},{20,24},{24,20... | collective-permute-start | bytes 3145736 | tf_op jit(solution)/shard_map/ppermute | solution.py:405
  14.8 9.9 %collective-permute-start.8 = (f32[2,256,256]{2,1,0:T(8,128)S(1)}, f32[2,256,256]{2,1,0:T(8,128)S(1)}, u32[]{:S(2)}, u32[]{:S(2)}) collective-permute-start(f32[2,256,256]{2,1,0:T(8,128)S(1)} %get-tuple-element.14.rest_0_), channel_id=1, source_target_pairs={{0,1},{1,0},{2,3},{3,2},{4,5},{5,4},{6,7},{7,6},{8,9},{9,8},{10,11... | collective-permute-start | bytes 1572872 | tf_op jit(solution)/shard_map/ppermute | solution.py:28
  14.9 14.2 %collective-permute-start.6 = (f32[2,384,256]{2,1,0:T(8,128)S(1)}, f32[2,384,256]{2,1,0:T(8,128)S(1)}, u32[]{:S(2)}, u32[]{:S(2)}) collective-permute-start(f32[2,384,256]{2,1,0:T(8,128)S(1)} %get-tuple-element.17), channel_id=1, source_target_pairs={{0,1},{1,0},{2,3},{3,2},{4,5},{5,4},{6,7},{7,6},{8,9},{9,8},{10,11... | collective-permute-start | bytes 2359304 | tf_op jit(solution)/shard_map/ppermute | solution.py:28
  15.4 15.0 %collective-permute-start.7 = (f32[2,384,256]{2,1,0:T(8,128)S(1)}, f32[2,384,256]{2,1,0:T(8,128)S(1)}, u32[]{:S(2)}, u32[]{:S(2)}) collective-permute-start(f32[2,384,256]{2,1,0:T(8,128)S(1)} %get-tuple-element.18), channel_id=1, source_target_pairs={{0,1},{1,0},{2,3},{3,2},{4,5},{5,4},{6,7},{7,6},{8,9},{9,8},{10,11... | collective-permute-start | bytes 2359304 | tf_op jit(solution)/shard_map/ppermute | solution.py:28
  19.4 19.5 %collective-permute-start.11 = (bf16[2,64,2304]{2,1,0:T(8,128)(2,1)S(1)}, bf16[2,64,2304]{2,1,0:T(8,128)(2,1)S(1)}, u32[]{:S(2)}, u32[]{:S(2)}) collective-permute-start(bf16[2,64,2304]{2,1,0:T(8,128)(2,1)S(1)} %get-tuple-element.21), channel_id=1, source_target_pairs={{0,4},{4,0},{8,12},{12,8},{1,5},{5,1},{9,13},{13,9},{2,6},{6,2},{1... | collective-permute-start | bytes 1769480 | tf_op jit(solution)/shard_map/ppermute | solution.py:405
  24.7 31.4 %collective-permute-start.10 = (bf16[2,64,2304]{2,1,0:T(8,128)(2,1)S(1)}, bf16[2,64,2304]{2,1,0:T(8,128)(2,1)S(1)}, u32[]{:S(2)}, u32[]{:S(2)}) collective-permute-start(bf16[2,64,2304]{2,1,0:T(8,128)(2,1)S(1)} %get-tuple-element.20), channel_id=1, source_target_pairs={{0,12},{12,0},{1,13},{13,1},{2,14},{14,2},{3,15},{15,3},{16,28},{2... | collective-permute-start | bytes 1769480 | tf_op jit(solution)/shard_map/ppermute | solution.py:405
  29.1 34.1 %collective-permute-start.4 = (bf16[2,64,2304]{2,1,0:T(8,128)(2,1)S(1)}, bf16[2,64,2304]{2,1,0:T(8,128)(2,1)S(1)}, u32[]{:S(2)}, u32[]{:S(2)}) collective-permute-start(bf16[2,64,2304]{2,1,0:T(8,128)(2,1)S(1)} %get-tuple-element.15), channel_id=1, source_target_pairs={{0,8},{12,4},{1,9},{13,5},{2,10},{14,6},{3,11},{15,7},{16,24},{28,... | collective-permute-start | bytes 1769480 | tf_op jit(solution)/shard_map/ppermute | solution.py:405
  30.7 22.9 %collective-permute-start.15 = (bf16[1,1024,256]{2,1,0:T(8,128)(2,1)S(1)}, bf16[1,1024,256]{2,1,0:T(8,128)(2,1)S(1)}, u32[]{:S(2)}, u32[]{:S(2)}) collective-permute-start(bf16[1,1024,256]{2,1,0:T(8,128)(2,1)S(1)} %get-tuple-element.22), channel_id=1, source_target_pairs={{0,2},{1,3},{2,0},{3,1},{4,6},{5,7},{6,4},{7,5},{8,10},{9,11},{10,... | collective-permute-start | bytes 1572872 | tf_op jit(solution)/shard_map/ppermute | solution.py:28
  32.2 6.7 %copy-start = (bf16[1024,2048]{1,0:T(8,128)(2,1)S(1)}, bf16[1024,2048]{1,0:T(8,128)(2,1)}, u32[]{:S(2)}) copy-start(bf16[1024,2048]{1,0:T(8,128)(2,1)} %tokens_ref.1) | copy-start | bytes 12582916
  32.2 6.7 %copy-start.1 = (bf16[4,2048,64]{1,2,0:T(8,128)(2,1)S(1)}, bf16[4,2048,64]{1,2,0:T(8,128)(2,1)}, u32[]{:S(2)}) copy-start(bf16[4,2048,64]{1,2,0:T(8,128)(2,1)} %param.9) | copy-start | bytes 3145732
  32.9 20.7 %copy-start.2 = (bf16[4,64,256]{2,1,0:T(8,128)(2,1)S(1)}, bf16[4,64,256]{2,1,0:T(8,128)(2,1)}, u32[]{:S(2)}) copy-start(bf16[4,64,256]{2,1,0:T(8,128)(2,1)} %refs_6_.1) | copy-start | bytes 393220
  32.9 31.1 %collective-permute-start.9 = (bf16[2,64,2304]{2,1,0:T(8,128)(2,1)S(1)}, bf16[2,64,2304]{2,1,0:T(8,128)(2,1)S(1)}, u32[]{:S(2)}, u32[]{:S(2)}) collective-permute-start(bf16[2,64,2304]{2,1,0:T(8,128)(2,1)S(1)} %shard_map.77.refs_2_), channel_id=1, source_target_pairs={{4,0},{8,12},{5,1},{9,13},{6,2},{10,14},{7,3},{11,15},{20,16},{24,... | collective-permute-start | bytes 1769480 | tf_op jit(solution)/shard_map/ppermute | solution.py:405
  40.9 1.4 %collective-permute-start.12 = (f32[4,64,128]{2,1,0:T(8,128)S(1)}, f32[4,64,128]{2,1,0:T(8,128)S(1)}, u32[]{:S(2)}, u32[]{:S(2)}) collective-permute-start(f32[4,64,128]{2,1,0:T(8,128)S(1)} %shard_map.78.refs_0_), channel_id=1, source_target_pairs={{0,1},{1,0},{2,3},{3,2},{4,5},{5,4},{6,7},{7,6},{8,9},{9,8},{10,11... | collective-permute-start | bytes 393224 | tf_op jit(solution)/shard_map/ppermute | solution.py:28
  42.3 5.6 %collective-permute-start.13 = (f32[4,64,128]{2,1,0:T(8,128)S(1)}, f32[4,64,128]{2,1,0:T(8,128)S(1)}, u32[]{:S(2)}, u32[]{:S(2)}) collective-permute-start(f32[4,64,128]{2,1,0:T(8,128)S(1)} %shard_map.78.refs_0_), channel_id=1, source_target_pairs={{0,2},{1,3},{2,0},{3,1},{4,6},{5,7},{6,4},{7,5},{8,10},{9,11},{10,... | collective-permute-start | bytes 393224 | tf_op jit(solution)/shard_map/ppermute | solution.py:28
  47.8 5.8 %collective-permute-start.14 = (f32[4,64,128]{2,1,0:T(8,128)S(1)}, f32[4,64,128]{2,1,0:T(8,128)S(1)}, u32[]{:S(2)}, u32[]{:S(2)}) collective-permute-start(f32[4,64,128]{2,1,0:T(8,128)S(1)} %shard_map.78.refs_0_), channel_id=1, source_target_pairs={{0,3},{1,2},{2,1},{3,0},{4,7},{5,6},{6,5},{7,4},{8,11},{9,10},{10,... | collective-permute-start | bytes 393224 | tf_op jit(solution)/shard_map/ppermute | solution.py:28
  57.4 9.5 %collective-permute-start.19 = (f32[2,64,128]{2,1,0:T(8,128)S(1)}, f32[2,64,128]{2,1,0:T(8,128)S(1)}, u32[]{:S(2)}, u32[]{:S(2)}) collective-permute-start(f32[2,64,128]{2,1,0:T(8,128)S(1)} %shard_map.80.refs_2_.refs_0_), channel_id=1, source_target_pairs={{0,1},{1,0},{2,3},{3,2},{4,5},{5,4},{6,7},{7,6},{8,9},{9,8},{10,11... | collective-permute-start | bytes 196616 | tf_op jit(solution)/shard_map/ppermute | solution.py:28
  57.6 9.6 %collective-permute-start.20 = (f32[2,64,128]{2,1,0:T(8,128)S(1)}, f32[2,64,128]{2,1,0:T(8,128)S(1)}, u32[]{:S(2)}, u32[]{:S(2)}) collective-permute-start(f32[2,64,128]{2,1,0:T(8,128)S(1)} %shard_map.80.refs_2_.refs_0_), channel_id=1, source_target_pairs={{0,2},{1,3},{2,0},{3,1},{4,6},{5,7},{6,4},{7,5},{8,10},{9,11},{10,... | collective-permute-start | bytes 196616 | tf_op jit(solution)/shard_map/ppermute | solution.py:28
  58.6 8.6 %collective-permute-start.21 = (f32[2,64,128]{2,1,0:T(8,128)S(1)}, f32[2,64,128]{2,1,0:T(8,128)S(1)}, u32[]{:S(2)}, u32[]{:S(2)}) collective-permute-start(f32[2,64,128]{2,1,0:T(8,128)S(1)} %shard_map.80.refs_2_.refs_0_), channel_id=1, source_target_pairs={{0,3},{1,2},{2,1},{3,0},{4,7},{5,6},{6,5},{7,4},{8,11},{9,10},{10,... | collective-permute-start | bytes 196616 | tf_op jit(solution)/shard_map/ppermute | solution.py:28
  65.3 3.7 %collective-permute-start.16 = (bf16[2,64,128]{2,1,0:T(8,128)(2,1)S(1)}, bf16[2,64,128]{2,1,0:T(8,128)(2,1)S(1)}, u32[]{:S(2)}, u32[]{:S(2)}) collective-permute-start(bf16[2,64,128]{2,1,0:T(8,128)(2,1)S(1)} %shard_map.81.refs_0_), channel_id=1, source_target_pairs={{0,1},{1,0},{2,3},{3,2},{4,5},{5,4},{6,7},{7,6},{8,9},{9,8},{10,11... | collective-permute-start | bytes 98312 | tf_op jit(solution)/shard_map/ppermute | solution.py:28
  65.3 4.0 %collective-permute-start.17 = (bf16[2,64,128]{2,1,0:T(8,128)(2,1)S(1)}, bf16[2,64,128]{2,1,0:T(8,128)(2,1)S(1)}, u32[]{:S(2)}, u32[]{:S(2)}) collective-permute-start(bf16[2,64,128]{2,1,0:T(8,128)(2,1)S(1)} %shard_map.81.refs_0_), channel_id=1, source_target_pairs={{0,2},{1,3},{2,0},{3,1},{4,6},{5,7},{6,4},{7,5},{8,10},{9,11},{10,... | collective-permute-start | bytes 98312 | tf_op jit(solution)/shard_map/ppermute | solution.py:28
  66.9 3.3 %collective-permute-start.18 = (bf16[2,64,128]{2,1,0:T(8,128)(2,1)S(1)}, bf16[2,64,128]{2,1,0:T(8,128)(2,1)S(1)}, u32[]{:S(2)}, u32[]{:S(2)}) collective-permute-start(bf16[2,64,128]{2,1,0:T(8,128)(2,1)S(1)} %shard_map.81.refs_0_), channel_id=1, source_target_pairs={{0,3},{1,2},{2,1},{3,0},{4,7},{5,6},{6,5},{7,4},{8,11},{9,10},{10,... | collective-permute-start | bytes 98312 | tf_op jit(solution)/shard_map/ppermute | solution.py:28

commit v9 on v8

--- a/solution.py
+++ b/solution.py
@@ -11,12 +11,15 @@
 ROW_TILE = 256
 PARAMS = pltpu.CompilerParams(vmem_limit_bytes=20 * 1024 * 1024)
 NO_COST = pl.CostEstimate(flops=0, bytes_accessed=0, transcendentals=0)
-BASE = pl.CostEstimate(flops=4 * 10**9, bytes_accessed=0, transcendentals=0)
-SHORT = pl.CostEstimate(flops=10 * 10**9, bytes_accessed=0, transcendentals=0)
+BASE = pl.CostEstimate(flops=0 * 10**9, bytes_accessed=0, transcendentals=0)
+SHORT = pl.CostEstimate(flops=2 * 10**9, bytes_accessed=0, transcendentals=0)
+PACK = pl.CostEstimate(flops=3 * 10**9, bytes_accessed=0, transcendentals=0)
+FIRST = pl.CostEstimate(flops=3 * 10**9, bytes_accessed=0, transcendentals=0)
 MIDDLE = pl.CostEstimate(flops=0 * 10**9, bytes_accessed=0, transcendentals=0)
 LONG = pl.CostEstimate(flops=6 * 10**9, bytes_accessed=0, transcendentals=0)
 ANY = pl.BlockSpec(memory_space=pl.ANY)
 SMEM = pl.BlockSpec(memory_space=pltpu.SMEM)
+VMEM = pl.BlockSpec(memory_space=pltpu.VMEM)
 
 
 def in_hbm(value):
@@ -40,7 +43,8 @@
 
 
 def base_kernel(order, tokens_ref, weight_ref, *refs):
-    *sent_refs, kept_ref, tokens, weight, sems = refs
+    *refs, kept_ref, tokens, weight, sems = refs
+    sent_refs = refs[-len(piece_rows(kept_ref.shape[1])) :]
     half, rows, width = kept_ref.shape
     place = lax.axis_index("tensor")
     copies = []
@@ -78,14 +82,14 @@
                 start = stop
 
 
-def base_chunks(tokens, weight, order, width):
+def base_chunks(tokens, weight, order, width, after):
     rows = tokens.shape[0]
     half = len(order) // 2
     sizes = [*piece_rows(rows), rows]
     *sent, kept = pl.pallas_call(
         functools.partial(base_kernel, order),
-        in_specs=[ANY] * 2,
-        out_specs=[pl.BlockSpec(memory_space=pltpu.VMEM)] * len(sizes),
+        in_specs=[ANY] * (2 + len(after)),
+        out_specs=[VMEM] * len(sizes),
         out_shape=[jax.ShapeDtypeStruct((half, size, width), jnp.float32) for size in sizes],
         scratch_shapes=[
             pltpu.VMEM(tokens.shape, tokens.dtype),
@@ -94,12 +98,12 @@
         ],
         compiler_params=PARAMS,
         cost_estimate=BASE,
-    )(in_hbm(tokens), in_hbm(weight))
+    )(in_hbm(tokens), in_hbm(weight), *after)
     return sent, kept
 
 
-def add_kernel(kept_ref, *refs):
-    *arrived_refs, out_ref, mine_ref = refs
+def add_kernel(pieces, kept_ref, *refs):
+    arrived_refs, out_ref, mine_ref = refs[:pieces], *refs[-2:]
     half = kept_ref.shape[0] // 2
     start = 0
     for arrived_ref in arrived_refs:
@@ -111,34 +115,35 @@
         start += arrived_ref.shape[1]
 
 
-def add_halves(kept, arrived, sent_type):
+def add_halves(kept, arrived, sent_type, after):
     count, rows, width = kept.shape
     shape = (count // 2, rows, width)
     return pl.pallas_call(
-        add_kernel,
+        functools.partial(add_kernel, len(arrived)),
+        in_specs=[VMEM] * (1 + len(arrived)) + [ANY] * len(after),
         out_shape=[
             jax.ShapeDtypeStruct(shape, sent_type),
             jax.ShapeDtypeStruct(shape, jnp.float32),
         ],
         compiler_params=PARAMS,
         cost_estimate=NO_COST,
-    )(kept, *arrived)
-
-
-def base_parts(tokens, weight, width):
+    )(kept, *arrived, *after)
+
+
+def base_parts(tokens, weight, width, after=()):
     size = lax.axis_size("tensor")
     kept_order = [k for k in range(size) if not k & 1]
     kept_order.sort(key=lambda k: [k >> bit & 1 for bit in range(1, size.bit_length())])
-    return base_chunks(tokens, weight, [k ^ 1 for k in kept_order] + kept_order, width)
-
-
-def base_sum(sent, kept):
+    return base_chunks(tokens, weight, [k ^ 1 for k in kept_order] + kept_order, width, after)
+
+
+def base_sum(sent, kept, after=()):
     arrived = [swap(piece, "tensor", 1) for piece in sent]
     distance = 2
     size = lax.axis_size("tensor")
     while distance < size:
         sent_type = jnp.bfloat16 if 2 * distance == size else jnp.float32
-        sent, kept = add_halves(kept, arrived, sent_type)
+        sent, kept = add_halves(kept, arrived, sent_type, after)
         arrived = [swap(sent, "tensor", distance)]
         distance *= 2
     return kept[0], arrived[0][0]
@@ -208,10 +213,10 @@
 OWN, ACROSS, NEAR, TO_INNER, TO_OUTER, FORWARD, INNER, LIVE, PLAN_ROWS = 4, 5, 6, 7, 8, 9, 10, 11, 15
 
 
-def make_plan(names, others, table, live, holder_slots, capacity, after):
+def make_plan(names, others, table, live, holder_slots, capacity):
     return pl.pallas_call(
         functools.partial(plan_kernel, capacity, holder_slots),
-        in_specs=[ANY] * (6 + len(after)),
+        in_specs=[ANY] * 6,
         out_specs=SMEM,
         out_shape=jax.ShapeDtypeStruct((PLAN_ROWS * capacity,), jnp.int32),
         scratch_shapes=[pltpu.SMEM(names.shape, jnp.int32)] * 4
@@ -219,7 +224,7 @@
         + [pltpu.SemaphoreType.DMA((6,))],
         compiler_params=PARAMS,
         cost_estimate=SHORT,
-    )(in_hbm(names), *others, in_hbm(table), in_hbm(live), *after)
+    )(in_hbm(names), *others, in_hbm(table), in_hbm(live))
 
 
 def pack_kernel(starts, capacity, plan_ref, down_ref, up_ref, *rest):
@@ -252,92 +257,57 @@
     )(plan, down, up, *after)
 
 
-def step_of(i, start, count):
-    return jnp.clip(i - start, 0, count - 1)
-
-
-def source_specs(phases, shape, columns):
-    specs, operands, start = [], [], 0
-    for (_, count, sources), places in zip(phases, columns):
-        for (panels, row), column in zip(sources, places):
-
-            def index(i, plan, *_, start=start, count=count, row=row, column=column):
-                k = step_of(i, start, count)
-                return (k if row is None else plan[row + k], 0, column)
-
-            specs.append(pl.BlockSpec(shape, index))
-            operands.append(panels)
-        start += count
-    return specs, operands
-
-
-def block_index(phases):
-    def index(i, plan):
-        found, start = jnp.int32(0), 0
-        for row, count, _ in phases:
-            inside = (i >= start) & (i < start + count)
-            found = jnp.where(inside, plan[row + step_of(i, start, count)], found)
-            start += count
-        return found
-
-    return index
-
-
-def for_phase(phases, choose, plan_ref, refs, act):
-    start, at = 0, 0
-    step = pl.program_id(0)
-    for _, count, sources in phases:
-        mine = refs[at : at + len(sources)]
-
-        @pl.when((step >= start) & (step < start + count))
-        def _(mine=mine):
-            if len(mine) == 1:
-                act(mine[0])
-            else:
-                first = plan_ref[choose] != 0
-                pl.when(first)(lambda: act(mine[0]))
-                pl.when(jnp.logical_not(first))(lambda: act(mine[1]))
-
-        start += count
-        at += len(sources)
+def each_block(phases, choose, plan_ref, refs, act):
+    number = 0
+    for row, count, rows in phases:
+        mine, refs = refs[: len(rows)], refs[len(rows) :]
+
+        def run(ref, row_of, number=number, row=row, count=count):
+            for k in range(count):
+                panel = ref.at[k if row_of is None else plan_ref[row_of + k]]
+                act(number + k, plan_ref[row + k], panel)
+
+        if len(rows) == 1:
+            run(mine[0], rows[0])
+        else:
+            first = plan_ref[choose] != 0
+            pl.when(first)(functools.partial(run, mine[0], rows[0]))
+            pl.when(jnp.logical_not(first))(functools.partial(run, mine[1], rows[1]))
+        number += count
+
+
+def split_phases(phases):
+    shapes = [(row, count, [source[1] for source in sources]) for row, count, sources in phases]
+    return shapes, [source[0] for _, _, sources in phases for source in sources]
 
 
 def shrink_kernel(phases, choose, plan_ref, token_ref, *refs):
     out_ref = refs[-1]
-
-    def act(panel_ref):
-        out_ref[0] = lax.dot_general(
-            panel_ref[0],
-            token_ref[0],
+    depth = token_ref.shape[2]
+
+    def act(number, block, panel_ref):
+        out_ref[number] = lax.dot_general(
+            panel_ref[:, :depth],
+            token_ref[block],
             (((1,), (1,)), ((), ())),
             preferred_element_type=jnp.float32,
         ).astype(out_ref.dtype)
 
-    for_phase(phases, choose, plan_ref, refs, act)
-
-
-def shrink(plan, row_blocks, phases, choose, after=(), kind=jnp.float32):
-    rows, depth = row_blocks.shape[1:]
-    rank = phases[0][2][0][0].shape[1]
+    each_block(phases, choose, plan_ref, refs, act)
+
+
+def shrink(plan, row_blocks, phases, choose, after=(), kind=jnp.float32, cost=None):
+    shapes, panels = split_phases(phases)
     total = sum(count for _, count, _ in phases)
-    columns = [[0] * len(sources) for _, _, sources in phases]
-    specs, operands = source_specs(phases, (1, rank, depth), columns)
-    block = block_index(phases)
-    shapes = [(row, count, [None] * len(sources)) for row, count, sources in phases]
+    shape = (total, panels[0].shape[1], row_blocks.shape[1])
     return pl.pallas_call(
         functools.partial(shrink_kernel, shapes, choose),
-        grid_spec=pltpu.PrefetchScalarGridSpec(
-            num_scalar_prefetch=1,
-            grid=(total,),
-            in_specs=[pl.BlockSpec((1, rows, depth), lambda i, plan: (block(i, plan), 0, 0))]
-            + specs
-            + [ANY] * len(after),
-            out_specs=pl.BlockSpec((1, rank, rows), lambda i, plan: (i, 0, 0)),
-        ),
-        out_shape=jax.ShapeDtypeStruct((total, rank, rows), kind),
+        in_specs=[SMEM] + [VMEM] * (1 + len(panels)) + [ANY] * len(after),
+        out_specs=VMEM,
+        out_shape=jax.ShapeDtypeStruct(shape, kind),
         compiler_params=PARAMS,
-        cost_estimate=NO_COST,
-    )(plan, row_blocks, *operands, *after)
+        cost_estimate=cost or NO_COST,
+    )(plan, row_blocks, *panels, *after)
 
 
 def exchange(part):
@@ -347,109 +317,118 @@
 def combine_kernel(phases, choose, part_count, live_row, plan_ref, *refs):
     parts = refs[:part_count]
     mine_ref, far_ref = refs[part_count : part_count + 2]
-    out_ref = refs[-1]
-    total = parts[0][0].astype(jnp.float32)
-    for part in parts[1:]:
-        total = total + part[0].astype(jnp.float32)
-    shrunk = total.astype(jnp.bfloat16)
-    live = plan_ref[live_row + pl.program_id(0)]
-
-    def act(up_ref):
+    out_ref, held_ref, sems = refs[-3:]
+    total, block_rows, width = held_ref.shape
+
+    def copy_of(number, block):
+        rows = pl.ds(pl.multiple_of(block * block_rows, block_rows), block_rows)
+        return pltpu.make_async_copy(held_ref.at[number], out_ref.at[rows], sems.at[number])
+
+    def act(number, block, panel_ref):
+        shrunk = parts[0][number].astype(jnp.float32)
+        for part in parts[1:]:
+            shrunk = shrunk + part[number].astype(jnp.float32)
+        start = panel_ref.shape[1] - width
         delta = lax.dot_general(
-            shrunk, up_ref[0], (((0,), (0,)), ((), ())), preferred_element_type=jnp.float32
+            shrunk.astype(jnp.bfloat16),
+            panel_ref[:, start : start + width],
+            (((0,), (0,)), ((), ())),
+            preferred_element_type=jnp.float32,
         )
+        rows = pl.ds(pl.multiple_of(block * block_rows, block_rows), block_rows)
         row = lax.broadcasted_iota(jnp.int32, delta.shape, 0)
-        value = mine_ref[...] + far_ref[...] + ADAPTER_SCALE * delta
-        out_ref[...] = jnp.where(row < live, value, 0.0).astype(out_ref.dtype)
-
-    for_phase(phases, choose, plan_ref, refs[part_count + 2 :], act)
-
-
-def combine(
-    plan, live_row, parts, base, phases, columns, choose, out=None, after=(), cost=None
-):
-    rank, block_rows = parts[0].shape[1:]
+        value = mine_ref[rows, :] + far_ref[rows, :].astype(jnp.float32) + ADAPTER_SCALE * delta
+        value = jnp.where(row < plan_ref[live_row + number], value, 0.0)
+        held_ref[number] = value.astype(held_ref.dtype)
+        copy_of(number, block).start()
+
+    each_block(phases, choose, plan_ref, refs[part_count + 2 :], act)
+    number = 0
+    for row, count, _ in phases:
+        for k in range(count):
+            copy_of(number, plan_ref[row + k]).wait()
+            number += 1
+
+
+def combine(plan, live_row, parts, base, phases, choose, out=None, cost=None):
+    block_rows = parts[0].shape[2]
     rows, width = base[0].shape
+    shapes, panels = split_phases(phases)
     total = sum(count for _, count, _ in phases)
-    block = block_index(phases)
-    specs = [pl.BlockSpec((1, rank, block_rows), lambda i, plan: (i, 0, 0))] * len(parts)
-    specs += [pl.BlockSpec((block_rows, width), lambda i, plan: (block(i, plan), 0))] * 2
-    more, operands = source_specs(phases, (1, rank, width), columns)
-    specs += more + [ANY] * len(after)
-    operands = [*parts, *base, *operands, *after]
+    operands = [*parts, *base, *panels]
+    specs = [VMEM] * len(operands)
     aliases = {}
     if out is not None:
         specs.append(ANY)
         operands.append(out)
         aliases = {len(operands): 0}
-    shapes = [(row, count, [None] * len(sources)) for row, count, sources in phases]
     return pl.pallas_call(
         functools.partial(combine_kernel, shapes, choose, len(parts), live_row),
-        grid_spec=pltpu.PrefetchScalarGridSpec(
-            num_scalar_prefetch=1,
-            grid=(total,),
-            in_specs=specs,
-            out_specs=pl.BlockSpec((block_rows, width), lambda i, plan: (block(i, plan), 0)),
-        ),
+        in_specs=[SMEM] + specs,
+        out_specs=ANY,
         out_shape=pltpu.HBM((rows, width), jnp.bfloat16),
         input_output_aliases=aliases,
+        scratch_shapes=[
+            pltpu.VMEM((total, block_rows, width), jnp.bfloat16),
+            pltpu.SemaphoreType.DMA((total,)),
+        ],
         compiler_params=PARAMS,
         cost_estimate=cost or NO_COST,
     )(plan, *operands)
 
 
 def on_line_of_four(tokens, weight, row_blocks, down, up, names, table, live, capacity):
-    up_column = down.shape[2] // up.shape[2]
-
     def across(value, pairs):
         return lax.ppermute(value, "pool", pairs)
 
     others = [swap(names, "pool", m) for m in range(1, 4)]
     inner_down = across(down, [(1, 2), (2, 1)])
     inner_up = across(up, [(1, 2), (2, 1)])
-    sent, kept = base_parts(tokens, weight, up.shape[2])
-    plan = make_plan(names, others, table, live, down.shape[0], capacity, [inner_up])
+    plan = make_plan(names, others, table, live, down.shape[0], capacity)
     near_out, outer_out, inner_out = pack_panels(
         plan,
         [NEAR * capacity, TO_OUTER * capacity, TO_INNER * capacity],
         capacity,
         in_hbm(down),
         in_hbm(up),
-        sent[-1:],
+        [inner_up],
+        PACK,
     )
     near = across(near_out, [(0, 1), (1, 0), (2, 3), (3, 2)])
     to_outer = across(outer_out, [(0, 3), (3, 0)])
     to_inner = across(inner_out, [(0, 2), (3, 1)])
-    base = base_sum(sent, kept)
+    sent, kept = base_parts(tokens, weight, up.shape[2], [near_out])
+
+    choose = INNER * capacity
+    first = [(0, capacity, [(down, OWN * capacity)]), (capacity, capacity, [(near, None)])]
+    first_up = [(0, capacity, [(up, OWN * capacity)]), first[1]]
+    first_part = shrink(plan, row_blocks, first, choose, cost=FIRST)
+    base = base_sum(sent, kept, [first_part])
     (forward_out,) = pack_panels(
         plan, [FORWARD * capacity], capacity, inner_down, inner_up, [base[0]], LONG
     )
     forwarded = across(forward_out, [(1, 0), (2, 3)])
-
-    choose = INNER * capacity
-    first = [(0, capacity, [(down, OWN * capacity)]), (capacity, capacity, [(near, None)])]
-    first_up = [(0, capacity, [(up, OWN * capacity)]), first[1]]
     middle = [(2 * capacity, capacity, [(inner_down, ACROSS * capacity), (to_outer, None)])]
     middle_up = [(2 * capacity, capacity, [(inner_up, ACROSS * capacity), (to_outer, None)])]
     last = [(3 * capacity, capacity, [(to_inner, None), (forwarded, None)])]
 
-    def write(number, parts, phases, columns, out, cost=None):
+    def write(number, parts, phases, out, cost=None):
         live_row = (LIVE + number) * capacity
-        return combine(plan, live_row, parts, base, phases, columns, choose, out, cost=cost)
-
-    first_parts = exchange(shrink(plan, row_blocks, first, choose, [forward_out]))
-    out = write(0, first_parts, first_up, [[0], [up_column]], None, MIDDLE)
+        return combine(plan, live_row, parts, base, phases, choose, out, cost)
+
+    first_parts = exchange(first_part)
+    out = write(0, first_parts, first_up, None, MIDDLE)
     middle_part = shrink(plan, row_blocks, middle, choose, [in_hbm(out)])
     middle_parts = exchange(middle_part)
     last_parts = exchange(shrink(plan, row_blocks, last, choose, [middle_part], jnp.bfloat16))
-    out = write(2, middle_parts, middle_up, [[0, up_column]], out)
-    return write(3, last_parts, last, [[up_column] * 2], out)
+    out = write(2, middle_parts, middle_up, out)
+    return write(3, last_parts, last, out)
 
 
 def on_any_pool(tokens, weight, row_blocks, down, up, names, table, live, capacity):
     pool_size = lax.axis_size("pool")
     here = lax.axis_index("pool")
-    holder_slots, _, depth = down.shape
+    holder_slots = down.shape[0]
     asked = table[lax.all_gather(names[0], "pool")]
     count = jnp.arange(capacity, dtype=jnp.int32)
     arrived = []
@@ -472,7 +451,7 @@
     phases = [(0, blocks.shape[0], [(arrived, blocks.shape[0])])]
     parts = exchange(shrink(plan, row_blocks, phases, 0))
     live_row = 2 * blocks.shape[0]
-    return combine(plan, live_row, parts, base, phases, [[depth // up.shape[2]]], 0)
+    return combine(plan, live_row, parts, base, phases, 0)
 
 
 def on_device(

time: 72.5 us -> 85.6 us (1.18)
  the two profiles are of different devices: /device:TPU:0 before, /device:TPU:17 now
where the time goes in v9:
time: 85.6 us; the launch traced here: 85.3 us
  waiting for transfers between devices  38.5 us (45%)
  starting transfers between devices  25.7 us (30%)
  Pallas kernels  20.9 us (24%)
    ppermute x6, waiting for transfers between devices, across(): return lax.ppermute(value, 'pool', pairs)  27.4 us
    ppermute x16, starting transfers between devices, swap(): return lax.ppermute(value, axis, pairs)  17 us
    ppermute x16, waiting for transfers between devices, swap(): return lax.ppermute(value, axis, pairs)  11.1 us
    ppermute x6, starting transfers between devices, across(): return lax.ppermute(value, 'pool', pairs)  8.64 us
    pallas_call x1, Pallas kernels, base_chunks(): pl.pallas_call(functools.partial(base_kernel, order), in_specs=[ANY] * (2...  8.51 us
    pallas_call x3, Pallas kernels, combine(): pl.pallas_call(functools.partial(combine_kernel, shapes, choose, len(part...  4.38 us
    pallas_call x3, Pallas kernels, shrink(): pl.pallas_call(functools.partial(shrink_kernel, shapes, choose), in_specs...  3.44 us
    pallas_call x2, Pallas kernels, pack_panels(): pl.pallas_call(functools.partial(pack_kernel, starts, capacity), in_specs...  2.71 us
  transfers between devices with their start and end apart: 22, of which 7 were waited for; matrix products, arithmetic and copies ran while one was open for 0% of the time, Pallas kernels for 23%

profile of v9, /device:TPU:17, one launch (start us, length us, event | category | flops | bytes accessed | tf_op | source)
XLA Modules:
  0.0 85.3 jit_solution(15163164183792261414)
XLA Ops:
  0.0 1.3 %collective-permute-start = (s32[1,8]{1,0:T(1,128)}, s32[1,8]{1,0:T(1,128)S(1)}, u32[]{:S(2)}, u32[]{:S(2)}) collective-permute-start(s32[1,8]{1,0:T(1,128)} %refs_0_.1), channel_id=1, source_target_pairs={{0,4},{4,0},{8,12},{12,8},{1,5},{5,1},{9,13},{13,9},{2,6},{6,2},{1... | collective-permute-start | bytes 104 | tf_op jit(solution)/shard_map/ppermute | solution.py:31
  1.3 0.1 collective-permute-start.1
  1.4 1.3 %collective-permute-start.2 = (s32[1,8]{1,0:T(1,128)}, s32[1,8]{1,0:T(1,128)S(1)}, u32[]{:S(2)}, u32[]{:S(2)}) collective-permute-start(s32[1,8]{1,0:T(1,128)} %refs_0_.1), channel_id=1, source_target_pairs={{0,12},{4,8},{8,4},{12,0},{1,13},{5,9},{9,5},{13,1},{2,14},{6,10},... | collective-permute-start | bytes 104 | tf_op jit(solution)/shard_map/ppermute | solution.py:31
  2.6 2.1 %collective-permute-start.3 = (bf16[4,64,256]{2,1,0:T(8,128)(2,1)}, bf16[4,64,256]{2,1,0:T(8,128)(2,1)S(1)}, u32[]{:S(2)}, u32[]{:S(2)}) collective-permute-start(bf16[4,64,256]{2,1,0:T(8,128)(2,1)} %refs_6_.1), channel_id=1, source_target_pairs={{4,8},{8,4},{5,9},{9,5},{6,10},{10,6},{7,11},{11,7},{20,24},{24,20... | collective-permute-start | bytes 393224 | tf_op jit(solution)/shard_map/ppermute | solution.py:382
  4.7 3.2 %collective-permute-start.5 = (bf16[4,64,2048]{2,1,0:T(8,128)(2,1)}, bf16[4,64,2048]{2,1,0:T(8,128)(2,1)S(1)}, u32[]{:S(2)}, u32[]{:S(2)}) collective-permute-start(bf16[4,64,2048]{2,1,0:T(8,128)(2,1)} %bitcast.14), channel_id=1, source_target_pairs={{4,8},{8,4},{5,9},{9,5},{6,10},{10,6},{7,11},{11,7},{20,24},{24,20... | collective-permute-start | bytes 3145736 | tf_op jit(solution)/shard_map/ppermute | solution.py:382
  7.9 0.0 collective-permute-done.refs_1_
  8.0 0.0 collective-permute-done.1.refs_2_
  8.0 0.0 collective-permute-done.2.refs_3_
  8.0 1.7 %shard_map.73.plan_ref = s32[30]{0:T(128)S(1)} custom-call(s32[1,8]{1,0:T(1,128)} %refs_0_.1, s32[1,8]{1,0:T(1,128)S(1)} %collective-permute-done.refs_1_, s32[1,8]{1,0:T(1,128)S(1)} %collective-permute-done.1.refs_2_, s32[1,8]{1,0:T(1,128)S(1)} %collective-permute-done.2.refs_3_, s32[16]{0:T(128)} %refs_4_.1, s32[1,8]{1,0:T(1,128)} %refs_5_.1), custom_call_target="tpu_custom_call" | custom-call | flops 2000000000 | tf_op jit(solution)/shard_map/pallas_call | solution.py:217
  9.6 0.0 collective-permute-done.3.rest_0_.up_ref.refs_6_
  9.7 2.1 %shard_map.74 = (bf16[2,64,2304]{2,1,0:T(8,128)(2,1)S(1)}, bf16[2,64,2304]{2,1,0:T(8,128)(2,1)S(1)}, bf16[2,64,2304]{2,1,0:T(8,128)(2,1)S(1)}) custom-call(s32[30]{0:T(128)S(1)} %shard_map.73.plan_ref, bf16[4,64,2048]{2,1,0:T(8,128)(2,1)} %bitcast.15, bf16[4,64,256]{2,1,0:T(8,128)(2,1)} %refs_6_.1, ...), custom_call_target="tpu_custom_call" | custom-call | flops 3000000000 | tf_op jit(solution)/shard_map/pallas_call | solution.py:249
  11.7 0.0 copy-start
  11.7 0.0 copy-start.2
  11.8 0.1 collective-permute-start.9
  11.8 8.5 %shard_map.75 = (f32[2,384,256]{2,1,0:T(8,128)S(1)}, f32[2,384,256]{2,1,0:T(8,128)S(1)}, f32[2,256,256]{2,1,0:T(8,128)S(1)}, f32[2,1024,256]{2,1,0:T(8,128)S(1)}) custom-call(bf16[1024,2048]{1,0:T(8,128)(2,1)} %tokens_ref.1, bf16[2048,1024]{1,0:T(8,128)(2,1)} %weight_ref.1, bf16[2,64,2304]{2,1,0:T(8,128)(2,1)S(1)} %get-tuple-element.15.refs_0_), custom_call_target="tpu_custom_call" | custom-call | tf_op jit(solution)/shard_map/pallas_call | solution.py:89
  20.4 2.9 %collective-permute-start.6 = (f32[2,384,256]{2,1,0:T(8,128)S(1)}, f32[2,384,256]{2,1,0:T(8,128)S(1)}, u32[]{:S(2)}, u32[]{:S(2)}) collective-permute-start(f32[2,384,256]{2,1,0:T(8,128)S(1)} %get-tuple-element.17), channel_id=1, source_target_pairs={{0,1},{1,0},{2,3},{3,2},{4,5},{5,4},{6,7},{7,6},{8,9},{9,8},{10,11... | collective-permute-start | bytes 2359304 | tf_op jit(solution)/shard_map/ppermute | solution.py:31
  23.3 0.1 collective-permute-start.7
  23.4 0.4 collective-permute-start.8
  23.8 0.0 collective-permute-done.9.refs_1_.refs_7_
  23.8 0.7 collective-permute-start.11
  24.5 0.0 copy-done
  24.5 0.0 copy-done.2
  24.5 1.4 %shard_map.76.refs_3_.refs_0_ = f32[4,64,128]{2,1,0:T(8,128)S(1)} custom-call(s32[30]{0:T(128)S(1)} %shard_map.73.plan_ref, bf16[8,128,2048]{2,1,0:T(8,128)(2,1)S(1)} %bitcast.4, bf16[4,64,2048]{2,1,0:T(8,128)(2,1)S(1)} %bitcast.16, bf16[2,64,2304]{2,1,0:T(8,128)(2,1)S(1)} %collective-permute-done.9.refs_1_.refs_7_), custom_call_target="tpu_custom_call" | custom-call | flops 3000000000 | tf_op jit(solution)/shard_map/pallas_call | solution.py:303
  25.9 1.2 %collective-permute-done.8.refs_2_ = f32[2,256,256]{2,1,0:T(8,128)S(1)} collective-permute-done((f32[2,256,256]{2,1,0:T(8,128)S(1)}, f32[2,256,256]{2,1,0:T(8,128)S(1)}, u32[]{:S(2)}, u32[]{:S(2)}) %collective-permute-start.8) | collective-permute-done | bytes 524320 | tf_op jit(solution)/shard_map/ppermute | solution.py:31
  27.1 1.3 %collective-permute-start.4 = (bf16[2,64,2304]{2,1,0:T(8,128)(2,1)S(1)}, bf16[2,64,2304]{2,1,0:T(8,128)(2,1)S(1)}, u32[]{:S(2)}, u32[]{:S(2)}) collective-permute-start(bf16[2,64,2304]{2,1,0:T(8,128)(2,1)S(1)} %get-tuple-element.14), channel_id=1, source_target_pairs={{0,8},{12,4},{1,9},{13,5},{2,10},{14,6},{3,11},{15,7},{16,24},{28,... | collective-permute-start | bytes 1769480 | tf_op jit(solution)/shard_map/ppermute | solution.py:382
  28.4 0.0 collective-permute-done.6.refs_0_
  28.4 0.0 collective-permute-done.7.refs_1_
  28.4 0.2 shard_map.77
  28.6 1.3 %collective-permute-start.15 = (bf16[1,1024,256]{2,1,0:T(8,128)(2,1)S(1)}, bf16[1,1024,256]{2,1,0:T(8,128)(2,1)S(1)}, u32[]{:S(2)}, u32[]{:S(2)}) collective-permute-start(bf16[1,1024,256]{2,1,0:T(8,128)(2,1)S(1)} %get-tuple-element.22), channel_id=1, source_target_pairs={{0,2},{1,3},{2,0},{3,1},{4,6},{5,7},{6,4},{7,5},{8,10},{9,11},{10,... | collective-permute-start | bytes 1572872 | tf_op jit(solution)/shard_map/ppermute | solution.py:31
  29.9 27.4 %collective-permute-done.5.down_ref.refs_0_ = bf16[4,64,2048]{2,1,0:T(8,128)(2,1)S(1)} collective-permute-done((bf16[4,64,2048]{2,1,0:T(8,128)(2,1)}, bf16[4,64,2048]{2,1,0:T(8,128)(2,1)S(1)}, u32[]{:S(2)}, u32[]{:S(2)}) %collective-permute-start.5) | collective-permute-done | bytes 1048608 | tf_op jit(solution)/shard_map/ppermute | solution.py:382
  57.3 0.0 copy-start.1
  57.3 0.6 shard_map.78
  57.9 1.3 %collective-permute-start.10 = (bf16[2,64,2304]{2,1,0:T(8,128)(2,1)S(1)}, bf16[2,64,2304]{2,1,0:T(8,128)(2,1)S(1)}, u32[]{:S(2)}, u32[]{:S(2)}) collective-permute-start(bf16[2,64,2304]{2,1,0:T(8,128)(2,1)S(1)} %shard_map.78), channel_id=1, source_target_pairs={{4,0},{8,12},{5,1},{9,13},{6,2},{10,14},{7,3},{11,15},{20,16},{24,... | collective-permute-start | bytes 1769480 | tf_op jit(solution)/shard_map/ppermute | solution.py:382
  59.3 1.8 %collective-permute-start.12 = (f32[4,64,128]{2,1,0:T(8,128)S(1)}, f32[4,64,128]{2,1,0:T(8,128)S(1)}, u32[]{:S(2)}, u32[]{:S(2)}) collective-permute-start(f32[4,64,128]{2,1,0:T(8,128)S(1)} %shard_map.76.refs_3_.refs_0_), channel_id=1, source_target_pairs={{0,1},{1,0},{2,3},{3,2},{4,5},{5,4},{6,7},{7,6},{8,9},{9,8},{10,11... | collective-permute-start | bytes 393224 | tf_op jit(solution)/shard_map/ppermute | solution.py:31
  61.0 1.0 %collective-permute-done.12.refs_1_ = f32[4,64,128]{2,1,0:T(8,128)S(1)} collective-permute-done((f32[4,64,128]{2,1,0:T(8,128)S(1)}, f32[4,64,128]{2,1,0:T(8,128)S(1)}, u32[]{:S(2)}, u32[]{:S(2)}) %collective-permute-start.12) | collective-permute-done | bytes 131104 | tf_op jit(solution)/shard_map/ppermute | solution.py:31
  62.0 1.2 %collective-permute-start.13 = (f32[4,64,128]{2,1,0:T(8,128)S(1)}, f32[4,64,128]{2,1,0:T(8,128)S(1)}, u32[]{:S(2)}, u32[]{:S(2)}) collective-permute-start(f32[4,64,128]{2,1,0:T(8,128)S(1)} %shard_map.76.refs_3_.refs_0_), channel_id=1, source_target_pairs={{0,2},{1,3},{2,0},{3,1},{4,6},{5,7},{6,4},{7,5},{8,10},{9,11},{10,... | collective-permute-start | bytes 393224 | tf_op jit(solution)/shard_map/ppermute | solution.py:31
  63.2 3.5 %collective-permute-done.13.refs_2_ = f32[4,64,128]{2,1,0:T(8,128)S(1)} collective-permute-done((f32[4,64,128]{2,1,0:T(8,128)S(1)}, f32[4,64,128]{2,1,0:T(8,128)S(1)}, u32[]{:S(2)}, u32[]{:S(2)}) %collective-permute-start.13) | collective-permute-done | bytes 131104 | tf_op jit(solution)/shard_map/ppermute | solution.py:31
  66.7 2.3 %collective-permute-start.14 = (f32[4,64,128]{2,1,0:T(8,128)S(1)}, f32[4,64,128]{2,1,0:T(8,128)S(1)}, u32[]{:S(2)}, u32[]{:S(2)}) collective-permute-start(f32[4,64,128]{2,1,0:T(8,128)S(1)} %shard_map.76.refs_3_.refs_0_), channel_id=1, source_target_pairs={{0,3},{1,2},{2,1},{3,0},{4,7},{5,6},{6,5},{7,4},{8,11},{9,10},{10,... | collective-permute-start | bytes 393224 | tf_op jit(solution)/shard_map/ppermute | solution.py:31
  69.0 4.3 %collective-permute-done.14.refs_3_ = f32[4,64,128]{2,1,0:T(8,128)S(1)} collective-permute-done((f32[4,64,128]{2,1,0:T(8,128)S(1)}, f32[4,64,128]{2,1,0:T(8,128)S(1)}, u32[]{:S(2)}, u32[]{:S(2)}) %collective-permute-start.14) | collective-permute-done | bytes 131104 | tf_op jit(solution)/shard_map/ppermute | solution.py:31
  73.3 0.0 collective-permute-done.15
  73.3 0.0 copy-done.1
  73.3 1.5 %shard_map.79.refs_2_.refs_8_ = bf16[1024,256]{1,0:T(8,128)(2,1)} custom-call(s32[30]{0:T(128)S(1)} %shard_map.73.plan_ref, f32[4,64,128]{2,1,0:T(8,128)S(1)} %shard_map.76.refs_3_.refs_0_, f32[4,64,128]{2,1,0:T(8,128)S(1)} %collective-permute-done.12.refs_1_, f32[4,64,128]{2,1,0:T(8,128)S(1)} %collective-permute-done.13.refs_2_, ...), custom_call_target="tpu_custom_call" | custom-call | tf_op jit(solution)/shard_map/pallas_call | solution.py:365
  74.8 0.0 collective-permute-done.11.refs_1_.refs_7_
  74.8 1.0 %shard_map.80.refs_2_.refs_0_ = f32[2,64,128]{2,1,0:T(8,128)S(1)} custom-call(s32[30]{0:T(128)S(1)} %shard_map.73.plan_ref, bf16[8,128,2048]{2,1,0:T(8,128)(2,1)S(1)} %bitcast.5, bf16[4,64,2048]{2,1,0:T(8,128)(2,1)S(1)} %collective-permute-done.5.down_ref.refs_0_, bf16[2,64,2304]{2,1,0:T(8,128)(2,1)S(1)} %collective-permute-done.11.refs_1_.refs_7_, ...), custom_call_target="tpu_custom_call" | custom-call | tf_op jit(solution)/shard_map/pallas_call | solution.py:303
  75.8 0.5 collective-permute-start.19
  76.3 0.8 collective-permute-start.20
  77.1 1.0 %collective-permute-start.21 = (f32[2,64,128]{2,1,0:T(8,128)S(1)}, f32[2,64,128]{2,1,0:T(8,128)S(1)}, u32[]{:S(2)}, u32[]{:S(2)}) collective-permute-start(f32[2,64,128]{2,1,0:T(8,128)S(1)} %shard_map.80.refs_2_.refs_0_), channel_id=1, source_target_pairs={{0,3},{1,2},{2,1},{3,0},{4,7},{5,6},{6,5},{7,4},{8,11},{9,10},{10,... | collective-permute-start | bytes 196616 | tf_op jit(solution)/shard_map/ppermute | solution.py:31
  78.0 0.0 collective-permute-done.4.refs_0_.refs_6_
  78.1 0.0 collective-permute-done.10.refs_1_.refs_7_
  78.1 1.0 %shard_map.81.refs_0_ = bf16[2,64,128]{2,1,0:T(8,128)(2,1)S(1)} custom-call(s32[30]{0:T(128)S(1)} %shard_map.73.plan_ref, bf16[8,128,2048]{2,1,0:T(8,128)(2,1)S(1)} %bitcast.6, bf16[2,64,2304]{2,1,0:T(8,128)(2,1)S(1)} %collective-permute-done.4.refs_0_.refs_6_, bf16[2,64,2304]{2,1,0:T(8,128)(2,1)S(1)} %collective-permute-done.10.refs_1_.refs_7_, ...), custom_call_target="tpu_custom_call" | custom-call | tf_op jit(solution)/shard_map/pallas_call | solution.py:303
  79.1 0.2 collective-permute-start.16
  79.3 0.7 collective-permute-start.17
  80.0 0.0 collective-permute-done.19.refs_1_
  80.0 1.3 %collective-permute-start.18 = (bf16[2,64,128]{2,1,0:T(8,128)(2,1)S(1)}, bf16[2,64,128]{2,1,0:T(8,128)(2,1)S(1)}, u32[]{:S(2)}, u32[]{:S(2)}) collective-permute-start(bf16[2,64,128]{2,1,0:T(8,128)(2,1)S(1)} %shard_map.81.refs_0_), channel_id=1, source_target_pairs={{0,3},{1,2},{2,1},{3,0},{4,7},{5,6},{6,5},{7,4},{8,11},{9,10},{10,... | collective-permute-start | bytes 98312 | tf_op jit(solution)/shard_map/ppermute | solution.py:31
  81.3 0.0 collective-permute-done.20.refs_2_
  81.3 0.3 collective-permute-done.21.refs_3_
  81.6 1.4 %shard_map.82.refs_8_ = bf16[1024,256]{1,0:T(8,128)(2,1)} custom-call(s32[30]{0:T(128)S(1)} %shard_map.73.plan_ref, f32[2,64,128]{2,1,0:T(8,128)S(1)} %shard_map.80.refs_2_.refs_0_, f32[2,64,128]{2,1,0:T(8,128)S(1)} %collective-permute-done.19.refs_1_, f32[2,64,128]{2,1,0:T(8,128)S(1)} %collective-permute-done.20.refs_2_, ...), custom_call_target="tpu_custom_call", output_to_operand_aliasing={{}: (9, {})} | custom-call | tf_op jit(solution)/shard_map/pallas_call | solution.py:365
  83.0 0.0 collective-permute-done.16.refs_1_
  83.0 0.0 collective-permute-done.17.refs_2_
  83.0 0.9 %collective-permute-done.18.refs_3_ = bf16[2,64,128]{2,1,0:T(8,128)(2,1)S(1)} collective-permute-done((bf16[2,64,128]{2,1,0:T(8,128)(2,1)S(1)}, bf16[2,64,128]{2,1,0:T(8,128)(2,1)S(1)}, u32[]{:S(2)}, u32[]{:S(2)}) %collective-permute-start.18) | collective-permute-done | bytes 32800 | tf_op jit(solution)/shard_map/ppermute | solution.py:31
  83.9 1.4 %shard_map.83 = bf16[1024,256]{1,0:T(8,128)(2,1)} custom-call(s32[30]{0:T(128)S(1)} %shard_map.73.plan_ref, bf16[2,64,128]{2,1,0:T(8,128)(2,1)S(1)} %shard_map.81.refs_0_, bf16[2,64,128]{2,1,0:T(8,128)(2,1)S(1)} %collective-permute-done.16.refs_1_, bf16[2,64,128]{2,1,0:T(8,128)(2,1)S(1)} %collective-permute-done.17.refs_2_, ...), custom_call_target="tpu_custom_call", output_to_operand_aliasing={{}: (9, {})} | custom-call | tf_op jit(solution)/shard_map/pallas_call | solution.py:365
Async XLA Ops:
  0.0 7.9 %collective-permute-start = (s32[1,8]{1,0:T(1,128)}, s32[1,8]{1,0:T(1,128)S(1)}, u32[]{:S(2)}, u32[]{:S(2)}) collective-permute-start(s32[1,8]{1,0:T(1,128)} %refs_0_.1), channel_id=1, source_target_pairs={{0,4},{4,0},{8,12},{12,8},{1,5},{5,1},{9,13},{13,9},{2,6},{6,2},{1... | collective-permute-start | bytes 104 | tf_op jit(solution)/shard_map/ppermute | solution.py:31
  1.3 6.7 %collective-permute-start.1 = (s32[1,8]{1,0:T(1,128)}, s32[1,8]{1,0:T(1,128)S(1)}, u32[]{:S(2)}, u32[]{:S(2)}) collective-permute-start(s32[1,8]{1,0:T(1,128)} %refs_0_.1), channel_id=1, source_target_pairs={{0,8},{4,12},{8,0},{12,4},{1,9},{5,13},{9,1},{13,5},{2,10},{6,14},... | collective-permute-start | bytes 104 | tf_op jit(solution)/shard_map/ppermute | solution.py:31
  1.4 6.6 %collective-permute-start.2 = (s32[1,8]{1,0:T(1,128)}, s32[1,8]{1,0:T(1,128)S(1)}, u32[]{:S(2)}, u32[]{:S(2)}) collective-permute-start(s32[1,8]{1,0:T(1,128)} %refs_0_.1), channel_id=1, source_target_pairs={{0,12},{4,8},{8,4},{12,0},{1,13},{5,9},{9,5},{13,1},{2,14},{6,10},... | collective-permute-start | bytes 104 | tf_op jit(solution)/shard_map/ppermute | solution.py:31
  2.6 7.0 %collective-permute-start.3 = (bf16[4,64,256]{2,1,0:T(8,128)(2,1)}, bf16[4,64,256]{2,1,0:T(8,128)(2,1)S(1)}, u32[]{:S(2)}, u32[]{:S(2)}) collective-permute-start(bf16[4,64,256]{2,1,0:T(8,128)(2,1)} %refs_6_.1), channel_id=1, source_target_pairs={{4,8},{8,4},{5,9},{9,5},{6,10},{10,6},{7,11},{11,7},{20,24},{24,20... | collective-permute-start | bytes 393224 | tf_op jit(solution)/shard_map/ppermute | solution.py:382
  4.7 52.6 %collective-permute-start.5 = (bf16[4,64,2048]{2,1,0:T(8,128)(2,1)}, bf16[4,64,2048]{2,1,0:T(8,128)(2,1)S(1)}, u32[]{:S(2)}, u32[]{:S(2)}) collective-permute-start(bf16[4,64,2048]{2,1,0:T(8,128)(2,1)} %bitcast.14), channel_id=1, source_target_pairs={{4,8},{8,4},{5,9},{9,5},{6,10},{10,6},{7,11},{11,7},{20,24},{24,20... | collective-permute-start | bytes 3145736 | tf_op jit(solution)/shard_map/ppermute | solution.py:382
  11.7 12.8 %copy-start = (bf16[1024,2048]{1,0:T(8,128)(2,1)S(1)}, bf16[1024,2048]{1,0:T(8,128)(2,1)}, u32[]{:S(2)}) copy-start(bf16[1024,2048]{1,0:T(8,128)(2,1)} %tokens_ref.1) | copy-start | bytes 12582916
  11.7 12.8 %copy-start.2 = (bf16[4,2048,64]{1,2,0:T(8,128)(2,1)S(1)}, bf16[4,2048,64]{1,2,0:T(8,128)(2,1)}, u32[]{:S(2)}) copy-start(bf16[4,2048,64]{1,2,0:T(8,128)(2,1)} %param.9) | copy-start | bytes 3145732
  11.8 12.1 %collective-permute-start.9 = (bf16[2,64,2304]{2,1,0:T(8,128)(2,1)S(1)}, bf16[2,64,2304]{2,1,0:T(8,128)(2,1)S(1)}, u32[]{:S(2)}, u32[]{:S(2)}) collective-permute-start(bf16[2,64,2304]{2,1,0:T(8,128)(2,1)S(1)} %get-tuple-element.15.refs_0_), channel_id=1, source_target_pairs={{0,4},{4,0},{8,12},{12,8},{1,5},{5,1},{9,13},{13,9},{2,6},{6,2},{1... | collective-permute-start | bytes 1769480 | tf_op jit(solution)/shard_map/ppermute | solution.py:382
  20.4 8.0 %collective-permute-start.6 = (f32[2,384,256]{2,1,0:T(8,128)S(1)}, f32[2,384,256]{2,1,0:T(8,128)S(1)}, u32[]{:S(2)}, u32[]{:S(2)}) collective-permute-start(f32[2,384,256]{2,1,0:T(8,128)S(1)} %get-tuple-element.17), channel_id=1, source_target_pairs={{0,1},{1,0},{2,3},{3,2},{4,5},{5,4},{6,7},{7,6},{8,9},{9,8},{10,11... | collective-permute-start | bytes 2359304 | tf_op jit(solution)/shard_map/ppermute | solution.py:31
  23.3 5.1 %collective-permute-start.7 = (f32[2,384,256]{2,1,0:T(8,128)S(1)}, f32[2,384,256]{2,1,0:T(8,128)S(1)}, u32[]{:S(2)}, u32[]{:S(2)}) collective-permute-start(f32[2,384,256]{2,1,0:T(8,128)S(1)} %get-tuple-element.18), channel_id=1, source_target_pairs={{0,1},{1,0},{2,3},{3,2},{4,5},{5,4},{6,7},{7,6},{8,9},{9,8},{10,11... | collective-permute-start | bytes 2359304 | tf_op jit(solution)/shard_map/ppermute | solution.py:31
  23.4 3.7 %collective-permute-start.8 = (f32[2,256,256]{2,1,0:T(8,128)S(1)}, f32[2,256,256]{2,1,0:T(8,128)S(1)}, u32[]{:S(2)}, u32[]{:S(2)}) collective-permute-start(f32[2,256,256]{2,1,0:T(8,128)S(1)} %get-tuple-element.19), channel_id=1, source_target_pairs={{0,1},{1,0},{2,3},{3,2},{4,5},{5,4},{6,7},{7,6},{8,9},{9,8},{10,11... | collective-permute-start | bytes 1572872 | tf_op jit(solution)/shard_map/ppermute | solution.py:31
  23.8 51.0 %collective-permute-start.11 = (bf16[2,64,2304]{2,1,0:T(8,128)(2,1)S(1)}, bf16[2,64,2304]{2,1,0:T(8,128)(2,1)S(1)}, u32[]{:S(2)}, u32[]{:S(2)}) collective-permute-start(bf16[2,64,2304]{2,1,0:T(8,128)(2,1)S(1)} %get-tuple-element.21), channel_id=1, source_target_pairs={{0,12},{12,0},{1,13},{13,1},{2,14},{14,2},{3,15},{15,3},{16,28},{2... | collective-permute-start | bytes 1769480 | tf_op jit(solution)/shard_map/ppermute | solution.py:382
  27.1 51.0 %collective-permute-start.4 = (bf16[2,64,2304]{2,1,0:T(8,128)(2,1)S(1)}, bf16[2,64,2304]{2,1,0:T(8,128)(2,1)S(1)}, u32[]{:S(2)}, u32[]{:S(2)}) collective-permute-start(bf16[2,64,2304]{2,1,0:T(8,128)(2,1)S(1)} %get-tuple-element.14), channel_id=1, source_target_pairs={{0,8},{12,4},{1,9},{13,5},{2,10},{14,6},{3,11},{15,7},{16,24},{28,... | collective-permute-start | bytes 1769480 | tf_op jit(solution)/shard_map/ppermute | solution.py:382
  28.6 44.7 %collective-permute-start.15 = (bf16[1,1024,256]{2,1,0:T(8,128)(2,1)S(1)}, bf16[1,1024,256]{2,1,0:T(8,128)(2,1)S(1)}, u32[]{:S(2)}, u32[]{:S(2)}) collective-permute-start(bf16[1,1024,256]{2,1,0:T(8,128)(2,1)S(1)} %get-tuple-element.22), channel_id=1, source_target_pairs={{0,2},{1,3},{2,0},{3,1},{4,6},{5,7},{6,4},{7,5},{8,10},{9,11},{10,... | collective-permute-start | bytes 1572872 | tf_op jit(solution)/shard_map/ppermute | solution.py:31
  57.3 16.0 %copy-start.1 = (bf16[4,64,256]{2,1,0:T(8,128)(2,1)S(1)}, bf16[4,64,256]{2,1,0:T(8,128)(2,1)}, u32[]{:S(2)}) copy-start(bf16[4,64,256]{2,1,0:T(8,128)(2,1)} %refs_6_.1) | copy-start | bytes 393220
  57.9 20.1 %collective-permute-start.10 = (bf16[2,64,2304]{2,1,0:T(8,128)(2,1)S(1)}, bf16[2,64,2304]{2,1,0:T(8,128)(2,1)S(1)}, u32[]{:S(2)}, u32[]{:S(2)}) collective-permute-start(bf16[2,64,2304]{2,1,0:T(8,128)(2,1)S(1)} %shard_map.78), channel_id=1, source_target_pairs={{4,0},{8,12},{5,1},{9,13},{6,2},{10,14},{7,3},{11,15},{20,16},{24,... | collective-permute-start | bytes 1769480 | tf_op jit(solution)/shard_map/ppermute | solution.py:382
  59.3 2.7 %collective-permute-start.12 = (f32[4,64,128]{2,1,0:T(8,128)S(1)}, f32[4,64,128]{2,1,0:T(8,128)S(1)}, u32[]{:S(2)}, u32[]{:S(2)}) collective-permute-start(f32[4,64,128]{2,1,0:T(8,128)S(1)} %shard_map.76.refs_3_.refs_0_), channel_id=1, source_target_pairs={{0,1},{1,0},{2,3},{3,2},{4,5},{5,4},{6,7},{7,6},{8,9},{9,8},{10,11... | collective-permute-start | bytes 393224 | tf_op jit(solution)/shard_map/ppermute | solution.py:31
  62.0 4.7 %collective-permute-start.13 = (f32[4,64,128]{2,1,0:T(8,128)S(1)}, f32[4,64,128]{2,1,0:T(8,128)S(1)}, u32[]{:S(2)}, u32[]{:S(2)}) collective-permute-start(f32[4,64,128]{2,1,0:T(8,128)S(1)} %shard_map.76.refs_3_.refs_0_), channel_id=1, source_target_pairs={{0,2},{1,3},{2,0},{3,1},{4,6},{5,7},{6,4},{7,5},{8,10},{9,11},{10,... | collective-permute-start | bytes 393224 | tf_op jit(solution)/shard_map/ppermute | solution.py:31
  66.7 6.5 %collective-permute-start.14 = (f32[4,64,128]{2,1,0:T(8,128)S(1)}, f32[4,64,128]{2,1,0:T(8,128)S(1)}, u32[]{:S(2)}, u32[]{:S(2)}) collective-permute-start(f32[4,64,128]{2,1,0:T(8,128)S(1)} %shard_map.76.refs_3_.refs_0_), channel_id=1, source_target_pairs={{0,3},{1,2},{2,1},{3,0},{4,7},{5,6},{6,5},{7,4},{8,11},{9,10},{10,... | collective-permute-start | bytes 393224 | tf_op jit(solution)/shard_map/ppermute | solution.py:31
  75.8 4.2 %collective-permute-start.19 = (f32[2,64,128]{2,1,0:T(8,128)S(1)}, f32[2,64,128]{2,1,0:T(8,128)S(1)}, u32[]{:S(2)}, u32[]{:S(2)}) collective-permute-start(f32[2,64,128]{2,1,0:T(8,128)S(1)} %shard_map.80.refs_2_.refs_0_), channel_id=1, source_target_pairs={{0,1},{1,0},{2,3},{3,2},{4,5},{5,4},{6,7},{7,6},{8,9},{9,8},{10,11... | collective-permute-start | bytes 196616 | tf_op jit(solution)/shard_map/ppermute | solution.py:31
  76.3 5.0 %collective-permute-start.20 = (f32[2,64,128]{2,1,0:T(8,128)S(1)}, f32[2,64,128]{2,1,0:T(8,128)S(1)}, u32[]{:S(2)}, u32[]{:S(2)}) collective-permute-start(f32[2,64,128]{2,1,0:T(8,128)S(1)} %shard_map.80.refs_2_.refs_0_), channel_id=1, source_target_pairs={{0,2},{1,3},{2,0},{3,1},{4,6},{5,7},{6,4},{7,5},{8,10},{9,11},{10,... | collective-permute-start | bytes 196616 | tf_op jit(solution)/shard_map/ppermute | solution.py:31
  77.1 4.5 %collective-permute-start.21 = (f32[2,64,128]{2,1,0:T(8,128)S(1)}, f32[2,64,128]{2,1,0:T(8,128)S(1)}, u32[]{:S(2)}, u32[]{:S(2)}) collective-permute-start(f32[2,64,128]{2,1,0:T(8,128)S(1)} %shard_map.80.refs_2_.refs_0_), channel_id=1, source_target_pairs={{0,3},{1,2},{2,1},{3,0},{4,7},{5,6},{6,5},{7,4},{8,11},{9,10},{10,... | collective-permute-start | bytes 196616 | tf_op jit(solution)/shard_map/ppermute | solution.py:31
  79.1 3.9 %collective-permute-start.16 = (bf16[2,64,128]{2,1,0:T(8,128)(2,1)S(1)}, bf16[2,64,128]{2,1,0:T(8,128)(2,1)S(1)}, u32[]{:S(2)}, u32[]{:S(2)}) collective-permute-start(bf16[2,64,128]{2,1,0:T(8,128)(2,1)S(1)} %shard_map.81.refs_0_), channel_id=1, source_target_pairs={{0,1},{1,0},{2,3},{3,2},{4,5},{5,4},{6,7},{7,6},{8,9},{9,8},{10,11... | collective-permute-start | bytes 98312 | tf_op jit(solution)/shard_map/ppermute | solution.py:31
  79.3 3.7 %collective-permute-start.17 = (bf16[2,64,128]{2,1,0:T(8,128)(2,1)S(1)}, bf16[2,64,128]{2,1,0:T(8,128)(2,1)S(1)}, u32[]{:S(2)}, u32[]{:S(2)}) collective-permute-start(bf16[2,64,128]{2,1,0:T(8,128)(2,1)S(1)} %shard_map.81.refs_0_), channel_id=1, source_target_pairs={{0,2},{1,3},{2,0},{3,1},{4,6},{5,7},{6,4},{7,5},{8,10},{9,11},{10,... | collective-permute-start | bytes 98312 | tf_op jit(solution)/shard_map/ppermute | solution.py:31
  80.0 3.9 %collective-permute-start.18 = (bf16[2,64,128]{2,1,0:T(8,128)(2,1)S(1)}, bf16[2,64,128]{2,1,0:T(8,128)(2,1)S(1)}, u32[]{:S(2)}, u32[]{:S(2)}) collective-permute-start(bf16[2,64,128]{2,1,0:T(8,128)(2,1)S(1)} %shard_map.81.refs_0_), channel_id=1, source_target_pairs={{0,3},{1,2},{2,1},{3,0},{4,7},{5,6},{6,5},{7,4},{8,11},{9,10},{10,... | collective-permute-start | bytes 98312 | tf_op jit(solution)/shard_map/ppermute | solution.py:31

commit v10 on v9

--- a/solution.py
+++ b/solution.py
@@ -11,10 +11,8 @@
 ROW_TILE = 256
 PARAMS = pltpu.CompilerParams(vmem_limit_bytes=20 * 1024 * 1024)
 NO_COST = pl.CostEstimate(flops=0, bytes_accessed=0, transcendentals=0)
-BASE = pl.CostEstimate(flops=0 * 10**9, bytes_accessed=0, transcendentals=0)
-SHORT = pl.CostEstimate(flops=2 * 10**9, bytes_accessed=0, transcendentals=0)
-PACK = pl.CostEstimate(flops=3 * 10**9, bytes_accessed=0, transcendentals=0)
-FIRST = pl.CostEstimate(flops=3 * 10**9, bytes_accessed=0, transcendentals=0)
+BASE = pl.CostEstimate(flops=4 * 10**9, bytes_accessed=0, transcendentals=0)
+SHORT = pl.CostEstimate(flops=10 * 10**9, bytes_accessed=0, transcendentals=0)
 MIDDLE = pl.CostEstimate(flops=0 * 10**9, bytes_accessed=0, transcendentals=0)
 LONG = pl.CostEstimate(flops=6 * 10**9, bytes_accessed=0, transcendentals=0)
 ANY = pl.BlockSpec(memory_space=pl.ANY)
@@ -43,8 +41,7 @@
 
 
 def base_kernel(order, tokens_ref, weight_ref, *refs):
-    *refs, kept_ref, tokens, weight, sems = refs
-    sent_refs = refs[-len(piece_rows(kept_ref.shape[1])) :]
+    *sent_refs, kept_ref, tokens, weight, sems = refs
     half, rows, width = kept_ref.shape
     place = lax.axis_index("tensor")
     copies = []
@@ -82,13 +79,13 @@
                 start = stop
 
 
-def base_chunks(tokens, weight, order, width, after):
+def base_chunks(tokens, weight, order, width):
     rows = tokens.shape[0]
     half = len(order) // 2
     sizes = [*piece_rows(rows), rows]
     *sent, kept = pl.pallas_call(
         functools.partial(base_kernel, order),
-        in_specs=[ANY] * (2 + len(after)),
+        in_specs=[ANY] * 2,
         out_specs=[VMEM] * len(sizes),
         out_shape=[jax.ShapeDtypeStruct((half, size, width), jnp.float32) for size in sizes],
         scratch_shapes=[
@@ -98,12 +95,12 @@
         ],
         compiler_params=PARAMS,
         cost_estimate=BASE,
-    )(in_hbm(tokens), in_hbm(weight), *after)
+    )(in_hbm(tokens), in_hbm(weight))
     return sent, kept
 
 
-def add_kernel(pieces, kept_ref, *refs):
-    arrived_refs, out_ref, mine_ref = refs[:pieces], *refs[-2:]
+def add_kernel(kept_ref, *refs):
+    *arrived_refs, out_ref, mine_ref = refs
     half = kept_ref.shape[0] // 2
     start = 0
     for arrived_ref in arrived_refs:
@@ -115,35 +112,35 @@
         start += arrived_ref.shape[1]
 
 
-def add_halves(kept, arrived, sent_type, after):
+def add_halves(kept, arrived, sent_type):
     count, rows, width = kept.shape
     shape = (count // 2, rows, width)
     return pl.pallas_call(
-        functools.partial(add_kernel, len(arrived)),
-        in_specs=[VMEM] * (1 + len(arrived)) + [ANY] * len(after),
+        add_kernel,
+        in_specs=[VMEM] * (1 + len(arrived)),
         out_shape=[
             jax.ShapeDtypeStruct(shape, sent_type),
             jax.ShapeDtypeStruct(shape, jnp.float32),
         ],
         compiler_params=PARAMS,
         cost_estimate=NO_COST,
-    )(kept, *arrived, *after)
-
-
-def base_parts(tokens, weight, width, after=()):
+    )(kept, *arrived)
+
+
+def base_parts(tokens, weight, width):
     size = lax.axis_size("tensor")
     kept_order = [k for k in range(size) if not k & 1]
     kept_order.sort(key=lambda k: [k >> bit & 1 for bit in range(1, size.bit_length())])
-    return base_chunks(tokens, weight, [k ^ 1 for k in kept_order] + kept_order, width, after)
-
-
-def base_sum(sent, kept, after=()):
+    return base_chunks(tokens, weight, [k ^ 1 for k in kept_order] + kept_order, width)
+
+
+def base_sum(sent, kept):
     arrived = [swap(piece, "tensor", 1) for piece in sent]
     distance = 2
     size = lax.axis_size("tensor")
     while distance < size:
         sent_type = jnp.bfloat16 if 2 * distance == size else jnp.float32
-        sent, kept = add_halves(kept, arrived, sent_type, after)
+        sent, kept = add_halves(kept, arrived, sent_type)
         arrived = [swap(sent, "tensor", distance)]
         distance *= 2
     return kept[0], arrived[0][0]
@@ -213,10 +210,10 @@
 OWN, ACROSS, NEAR, TO_INNER, TO_OUTER, FORWARD, INNER, LIVE, PLAN_ROWS = 4, 5, 6, 7, 8, 9, 10, 11, 15
 
 
-def make_plan(names, others, table, live, holder_slots, capacity):
+def make_plan(names, others, table, live, holder_slots, capacity, after):
     return pl.pallas_call(
         functools.partial(plan_kernel, capacity, holder_slots),
-        in_specs=[ANY] * 6,
+        in_specs=[ANY] * (6 + len(after)),
         out_specs=SMEM,
         out_shape=jax.ShapeDtypeStruct((PLAN_ROWS * capacity,), jnp.int32),
         scratch_shapes=[pltpu.SMEM(names.shape, jnp.int32)] * 4
@@ -224,7 +221,7 @@
         + [pltpu.SemaphoreType.DMA((6,))],
         compiler_params=PARAMS,
         cost_estimate=SHORT,
-    )(in_hbm(names), *others, in_hbm(table), in_hbm(live))
+    )(in_hbm(names), *others, in_hbm(table), in_hbm(live), *after)
 
 
 def pack_kernel(starts, capacity, plan_ref, down_ref, up_ref, *rest):
@@ -384,26 +381,20 @@
     others = [swap(names, "pool", m) for m in range(1, 4)]
     inner_down = across(down, [(1, 2), (2, 1)])
     inner_up = across(up, [(1, 2), (2, 1)])
-    plan = make_plan(names, others, table, live, down.shape[0], capacity)
-    near_out, outer_out, inner_out = pack_panels(
-        plan,
-        [NEAR * capacity, TO_OUTER * capacity, TO_INNER * capacity],
-        capacity,
-        in_hbm(down),
-        in_hbm(up),
-        [inner_up],
-        PACK,
+    sent, kept = base_parts(tokens, weight, up.shape[2])
+    plan = make_plan(names, others, table, live, down.shape[0], capacity, [inner_up])
+    held = in_hbm(down), in_hbm(up)
+    (near_out,) = pack_panels(plan, [NEAR * capacity], capacity, *held, sent[-1:])
+    near = across(near_out, [(0, 1), (1, 0), (2, 3), (3, 2)])
+    outer_out, inner_out = pack_panels(
+        plan, [TO_OUTER * capacity, TO_INNER * capacity], capacity, *held, [near_out]
     )
-    near = across(near_out, [(0, 1), (1, 0), (2, 3), (3, 2)])
     to_outer = across(outer_out, [(0, 3), (3, 0)])
     to_inner = across(inner_out, [(0, 2), (3, 1)])
-    sent, kept = base_parts(tokens, weight, up.shape[2], [near_out])
-
     choose = INNER * capacity
     first = [(0, capacity, [(down, OWN * capacity)]), (capacity, capacity, [(near, None)])]
     first_up = [(0, capacity, [(up, OWN * capacity)]), first[1]]
-    first_part = shrink(plan, row_blocks, first, choose, cost=FIRST)
-    base = base_sum(sent, kept, [first_part])
+    base = base_sum(sent, kept)
     (forward_out,) = pack_panels(
         plan, [FORWARD * capacity], capacity, inner_down, inner_up, [base[0]], LONG
     )
@@ -416,7 +407,7 @@
         live_row = (LIVE + number) * capacity
         return combine(plan, live_row, parts, base, phases, choose, out, cost)
 
-    first_parts = exchange(first_part)
+    first_parts = exchange(shrink(plan, row_blocks, first, choose, [forward_out]))
     out = write(0, first_parts, first_up, None, MIDDLE)
     middle_part = shrink(plan, row_blocks, middle, choose, [in_hbm(out)])
     middle_parts = exchange(middle_part)

time: 85.6 us -> 71.3 us (0.83)
  the two profiles are of different devices: /device:TPU:17 before, /device:TPU:0 now
where the time goes in v10:
time: 71.3 us; the launch traced here: 71.2 us
  starting transfers between devices  27.6 us (39%)
  Pallas kernels  21.8 us (31%)
  waiting for transfers between devices  21.6 us (30%)
    ppermute x16, waiting for transfers between devices, swap(): return lax.ppermute(value, axis, pairs)  14.6 us
    ppermute x6, starting transfers between devices, across(): return lax.ppermute(value, 'pool', pairs)  14.2 us
    ppermute x16, starting transfers between devices, swap(): return lax.ppermute(value, axis, pairs)  13.4 us
    pallas_call x1, Pallas kernels, base_chunks(): pl.pallas_call(functools.partial(base_kernel, order), in_specs=[ANY] * 2,...  7.78 us
    ppermute x6, waiting for transfers between devices, across(): return lax.ppermute(value, 'pool', pairs)  7.04 us
    pallas_call x3, Pallas kernels, combine(): pl.pallas_call(functools.partial(combine_kernel, shapes, choose, len(part...  4.39 us
    pallas_call x3, Pallas kernels, pack_panels(): pl.pallas_call(functools.partial(pack_kernel, starts, capacity), in_specs...  4.21 us
    pallas_call x3, Pallas kernels, shrink(): pl.pallas_call(functools.partial(shrink_kernel, shapes, choose), in_specs...  3.44 us
  transfers between devices with their start and end apart: 22, of which 8 were waited for; matrix products, arithmetic and copies ran while one was open for 0% of the time, Pallas kernels for 29%

profile of v10, /device:TPU:0, one launch (start us, length us, event | category | flops | bytes accessed | tf_op | source)
XLA Modules:
  0.0 71.2 jit_solution(8294543949519153379)
XLA Ops:
  0.0 3.0 %collective-permute-start = (s32[1,8]{1,0:T(1,128)}, s32[1,8]{1,0:T(1,128)S(1)}, u32[]{:S(2)}, u32[]{:S(2)}) collective-permute-start(s32[1,8]{1,0:T(1,128)} %refs_0_.1), channel_id=1, source_target_pairs={{0,4},{4,0},{8,12},{12,8},{1,5},{5,1},{9,13},{13,9},{2,6},{6,2},{1... | collective-permute-start | bytes 104 | tf_op jit(solution)/shard_map/ppermute | solution.py:29
  3.0 2.6 %collective-permute-start.1 = (s32[1,8]{1,0:T(1,128)}, s32[1,8]{1,0:T(1,128)S(1)}, u32[]{:S(2)}, u32[]{:S(2)}) collective-permute-start(s32[1,8]{1,0:T(1,128)} %refs_0_.1), channel_id=1, source_target_pairs={{0,8},{4,12},{8,0},{12,4},{1,9},{5,13},{9,1},{13,5},{2,10},{6,14},... | collective-permute-start | bytes 104 | tf_op jit(solution)/shard_map/ppermute | solution.py:29
  5.6 0.0 collective-permute-start.2
  5.6 0.7 collective-permute-start.3
  6.3 0.7 %collective-permute-start.5 = (bf16[4,64,2048]{2,1,0:T(8,128)(2,1)}, bf16[4,64,2048]{2,1,0:T(8,128)(2,1)S(1)}, u32[]{:S(2)}, u32[]{:S(2)}) collective-permute-start(bf16[4,64,2048]{2,1,0:T(8,128)(2,1)} %bitcast.7), channel_id=1, source_target_pairs={{4,8},{8,4},{5,9},{9,5},{6,10},{10,6},{7,11},{11,7},{20,24},{24,20... | collective-permute-start | bytes 3145736 | tf_op jit(solution)/shard_map/ppermute | solution.py:379
  7.0 7.8 %shard_map.74 = (f32[2,384,256]{2,1,0:T(8,128)S(1)}, f32[2,384,256]{2,1,0:T(8,128)S(1)}, f32[2,256,256]{2,1,0:T(8,128)S(1)}, f32[2,1024,256]{2,1,0:T(8,128)S(1)}) custom-call(bf16[1024,2048]{1,0:T(8,128)(2,1)} %tokens_ref.1, bf16[2048,1024]{1,0:T(8,128)(2,1)} %weight_ref.1), custom_call_target="tpu_custom_call" | custom-call | flops 4000000000 | tf_op jit(solution)/shard_map/pallas_call | solution.py:86
  14.8 0.0 collective-permute-done.refs_1_
  14.8 0.1 collective-permute-start.8
  14.9 0.0 collective-permute-done.1.refs_2_
  14.9 0.5 collective-permute-start.6
  15.4 0.0 collective-permute-done.2.refs_3_
  15.4 0.1 collective-permute-start.7
  15.5 0.0 collective-permute-done.3.refs_6_.up_ref
  15.5 1.7 %shard_map.73.plan_ref = s32[30]{0:T(128)S(1)} custom-call(s32[1,8]{1,0:T(1,128)} %refs_0_.1, s32[1,8]{1,0:T(1,128)S(1)} %collective-permute-done.refs_1_, s32[1,8]{1,0:T(1,128)S(1)} %collective-permute-done.1.refs_2_, s32[1,8]{1,0:T(1,128)S(1)} %collective-permute-done.2.refs_3_, s32[16]{0:T(128)} %refs_4_.1, s32[1,8]{1,0:T(1,128)} %refs_5_.1, ...), custom_call_target="tpu_custom_call" | custom-call | flops 10000000000 | tf_op jit(solution)/shard_map/pallas_call | solution.py:214
  17.2 1.6 %shard_map.75.rest_0_ = bf16[2,64,2304]{2,1,0:T(8,128)(2,1)S(1)} custom-call(s32[30]{0:T(128)S(1)} %shard_map.73.plan_ref, bf16[4,64,2048]{2,1,0:T(8,128)(2,1)} %bitcast.8, bf16[4,64,256]{2,1,0:T(8,128)(2,1)} %refs_6_.1, f32[2,256,256]{2,1,0:T(8,128)S(1)} %get-tuple-element.13.rest_0_), custom_call_target="tpu_custom_call" | custom-call | tf_op jit(solution)/shard_map/pallas_call | solution.py:246
  18.8 5.4 %collective-permute-start.11 = (bf16[2,64,2304]{2,1,0:T(8,128)(2,1)S(1)}, bf16[2,64,2304]{2,1,0:T(8,128)(2,1)S(1)}, u32[]{:S(2)}, u32[]{:S(2)}) collective-permute-start(bf16[2,64,2304]{2,1,0:T(8,128)(2,1)S(1)} %shard_map.75.rest_0_), channel_id=1, source_target_pairs={{0,4},{4,0},{8,12},{12,8},{1,5},{5,1},{9,13},{13,9},{2,6},{6,2},{1... | collective-permute-start | bytes 1769480 | tf_op jit(solution)/shard_map/ppermute | solution.py:379
  24.2 1.9 %shard_map.76 = (bf16[2,64,2304]{2,1,0:T(8,128)(2,1)S(1)}, bf16[2,64,2304]{2,1,0:T(8,128)(2,1)S(1)}) custom-call(s32[30]{0:T(128)S(1)} %shard_map.73.plan_ref, bf16[4,64,2048]{2,1,0:T(8,128)(2,1)} %bitcast.9, bf16[4,64,256]{2,1,0:T(8,128)(2,1)} %refs_6_.1, bf16[2,64,2304]{2,1,0:T(8,128)(2,1)S(1)} %shard_map.75.rest_0_), custom_call_target="tpu_custom_call" | custom-call | tf_op jit(solution)/shard_map/pallas_call | solution.py:246
  26.2 0.0 collective-permute-done.8.refs_2_
  26.2 4.5 %collective-permute-start.10 = (bf16[2,64,2304]{2,1,0:T(8,128)(2,1)S(1)}, bf16[2,64,2304]{2,1,0:T(8,128)(2,1)S(1)}, u32[]{:S(2)}, u32[]{:S(2)}) collective-permute-start(bf16[2,64,2304]{2,1,0:T(8,128)(2,1)S(1)} %get-tuple-element.19), channel_id=1, source_target_pairs={{0,12},{12,0},{1,13},{13,1},{2,14},{14,2},{3,15},{15,3},{16,28},{2... | collective-permute-start | bytes 1769480 | tf_op jit(solution)/shard_map/ppermute | solution.py:379
  30.7 0.0 collective-permute-done.6.refs_0_
  30.7 1.3 %collective-permute-start.4 = (bf16[2,64,2304]{2,1,0:T(8,128)(2,1)S(1)}, bf16[2,64,2304]{2,1,0:T(8,128)(2,1)S(1)}, u32[]{:S(2)}, u32[]{:S(2)}) collective-permute-start(bf16[2,64,2304]{2,1,0:T(8,128)(2,1)S(1)} %get-tuple-element.14), channel_id=1, source_target_pairs={{0,8},{12,4},{1,9},{13,5},{2,10},{14,6},{3,11},{15,7},{16,24},{28,... | collective-permute-start | bytes 1769480 | tf_op jit(solution)/shard_map/ppermute | solution.py:379
  32.0 0.0 collective-permute-done.7.refs_1_
  32.0 0.3 shard_map.77
  32.3 1.5 %collective-permute-start.15 = (bf16[1,1024,256]{2,1,0:T(8,128)(2,1)S(1)}, bf16[1,1024,256]{2,1,0:T(8,128)(2,1)S(1)}, u32[]{:S(2)}, u32[]{:S(2)}) collective-permute-start(bf16[1,1024,256]{2,1,0:T(8,128)(2,1)S(1)} %get-tuple-element.20), channel_id=1, source_target_pairs={{0,2},{1,3},{2,0},{3,1},{4,6},{5,7},{6,4},{7,5},{8,10},{9,11},{10,... | collective-permute-start | bytes 1572872 | tf_op jit(solution)/shard_map/ppermute | solution.py:29
  33.9 0.0 collective-permute-done.5.down_ref.refs_0_
  33.9 0.0 copy-start
  33.9 0.0 copy-start.1
  33.9 0.6 shard_map.78.refs_2_
  34.5 0.0 copy-start.2
  34.5 1.6 %collective-permute-start.9 = (bf16[2,64,2304]{2,1,0:T(8,128)(2,1)S(1)}, bf16[2,64,2304]{2,1,0:T(8,128)(2,1)S(1)}, u32[]{:S(2)}, u32[]{:S(2)}) collective-permute-start(bf16[2,64,2304]{2,1,0:T(8,128)(2,1)S(1)} %shard_map.78.refs_2_), channel_id=1, source_target_pairs={{4,0},{8,12},{5,1},{9,13},{6,2},{10,14},{7,3},{11,15},{20,16},{24,... | collective-permute-start | bytes 1769480 | tf_op jit(solution)/shard_map/ppermute | solution.py:379
  36.1 2.0 %collective-permute-done.11.refs_1_.refs_7_ = bf16[2,64,2304]{2,1,0:T(8,128)(2,1)S(1)} collective-permute-done((bf16[2,64,2304]{2,1,0:T(8,128)(2,1)S(1)}, bf16[2,64,2304]{2,1,0:T(8,128)(2,1)S(1)}, u32[]{:S(2)}, u32[]{:S(2)}) %collective-permute-start.11) | collective-permute-done | bytes 589856 | tf_op jit(solution)/shard_map/ppermute | solution.py:379
  38.1 0.0 copy-done
  38.1 0.0 copy-done.1
  38.1 1.4 %shard_map.79.refs_0_ = f32[4,64,128]{2,1,0:T(8,128)S(1)} custom-call(s32[30]{0:T(128)S(1)} %shard_map.73.plan_ref, bf16[8,128,2048]{2,1,0:T(8,128)(2,1)S(1)} %bitcast.4, bf16[4,64,2048]{2,1,0:T(8,128)(2,1)S(1)} %bitcast.10, bf16[2,64,2304]{2,1,0:T(8,128)(2,1)S(1)} %collective-permute-done.11.refs_1_.refs_7_, bf16[2,64,2304]{2,1,0:T(8,128)(2,1)S(1)} %shard_map.78.refs_2_), custom_call_target="tpu_custom_call" | custom-call | tf_op jit(solution)/shard_map/pallas_call | solution.py:300
  39.5 0.1 collective-permute-start.12
  39.6 1.3 %collective-permute-done.12.refs_1_ = f32[4,64,128]{2,1,0:T(8,128)S(1)} collective-permute-done((f32[4,64,128]{2,1,0:T(8,128)S(1)}, f32[4,64,128]{2,1,0:T(8,128)S(1)}, u32[]{:S(2)}, u32[]{:S(2)}) %collective-permute-start.12) | collective-permute-done | bytes 131104 | tf_op jit(solution)/shard_map/ppermute | solution.py:29
  40.9 1.6 %collective-permute-start.13 = (f32[4,64,128]{2,1,0:T(8,128)S(1)}, f32[4,64,128]{2,1,0:T(8,128)S(1)}, u32[]{:S(2)}, u32[]{:S(2)}) collective-permute-start(f32[4,64,128]{2,1,0:T(8,128)S(1)} %shard_map.79.refs_0_), channel_id=1, source_target_pairs={{0,2},{1,3},{2,0},{3,1},{4,6},{5,7},{6,4},{7,5},{8,10},{9,11},{10,... | collective-permute-start | bytes 393224 | tf_op jit(solution)/shard_map/ppermute | solution.py:29
  42.5 6.4 %collective-permute-done.13.refs_2_ = f32[4,64,128]{2,1,0:T(8,128)S(1)} collective-permute-done((f32[4,64,128]{2,1,0:T(8,128)S(1)}, f32[4,64,128]{2,1,0:T(8,128)S(1)}, u32[]{:S(2)}, u32[]{:S(2)}) %collective-permute-start.13) | collective-permute-done | bytes 131104 | tf_op jit(solution)/shard_map/ppermute | solution.py:29
  48.9 0.1 collective-permute-start.14
  49.0 5.7 %collective-permute-done.14.refs_3_ = f32[4,64,128]{2,1,0:T(8,128)S(1)} collective-permute-done((f32[4,64,128]{2,1,0:T(8,128)S(1)}, f32[4,64,128]{2,1,0:T(8,128)S(1)}, u32[]{:S(2)}, u32[]{:S(2)}) %collective-permute-start.14) | collective-permute-done | bytes 131104 | tf_op jit(solution)/shard_map/ppermute | solution.py:29
  54.7 0.0 collective-permute-done.15
  54.7 0.0 copy-done.2
  54.7 1.5 %shard_map.80.refs_2_.refs_8_ = bf16[1024,256]{1,0:T(8,128)(2,1)} custom-call(s32[30]{0:T(128)S(1)} %shard_map.73.plan_ref, f32[4,64,128]{2,1,0:T(8,128)S(1)} %shard_map.79.refs_0_, f32[4,64,128]{2,1,0:T(8,128)S(1)} %collective-permute-done.12.refs_1_, f32[4,64,128]{2,1,0:T(8,128)S(1)} %collective-permute-done.13.refs_2_, ...), custom_call_target="tpu_custom_call" | custom-call | tf_op jit(solution)/shard_map/pallas_call | solution.py:362
  56.2 0.0 collective-permute-done.10.refs_1_.refs_7_
  56.2 1.0 %shard_map.81.refs_2_.refs_0_ = f32[2,64,128]{2,1,0:T(8,128)S(1)} custom-call(s32[30]{0:T(128)S(1)} %shard_map.73.plan_ref, bf16[8,128,2048]{2,1,0:T(8,128)(2,1)S(1)} %bitcast.5, bf16[4,64,2048]{2,1,0:T(8,128)(2,1)S(1)} %collective-permute-done.5.down_ref.refs_0_, bf16[2,64,2304]{2,1,0:T(8,128)(2,1)S(1)} %collective-permute-done.10.refs_1_.refs_7_, ...), custom_call_target="tpu_custom_call" | custom-call | tf_op jit(solution)/shard_map/pallas_call | solution.py:300
  57.2 0.2 collective-permute-start.19
  57.4 0.6 collective-permute-start.20
  58.1 1.1 %collective-permute-start.21 = (f32[2,64,128]{2,1,0:T(8,128)S(1)}, f32[2,64,128]{2,1,0:T(8,128)S(1)}, u32[]{:S(2)}, u32[]{:S(2)}) collective-permute-start(f32[2,64,128]{2,1,0:T(8,128)S(1)} %shard_map.81.refs_2_.refs_0_), channel_id=1, source_target_pairs={{0,3},{1,2},{2,1},{3,0},{4,7},{5,6},{6,5},{7,4},{8,11},{9,10},{10,... | collective-permute-start | bytes 196616 | tf_op jit(solution)/shard_map/ppermute | solution.py:29
  59.2 3.5 %collective-permute-done.4.refs_0_.refs_6_ = bf16[2,64,2304]{2,1,0:T(8,128)(2,1)S(1)} collective-permute-done((bf16[2,64,2304]{2,1,0:T(8,128)(2,1)S(1)}, bf16[2,64,2304]{2,1,0:T(8,128)(2,1)S(1)}, u32[]{:S(2)}, u32[]{:S(2)}) %collective-permute-start.4) | collective-permute-done | bytes 589856 | tf_op jit(solution)/shard_map/ppermute | solution.py:379
  62.7 1.5 %collective-permute-done.9.refs_1_.refs_7_ = bf16[2,64,2304]{2,1,0:T(8,128)(2,1)S(1)} collective-permute-done((bf16[2,64,2304]{2,1,0:T(8,128)(2,1)S(1)}, bf16[2,64,2304]{2,1,0:T(8,128)(2,1)S(1)}, u32[]{:S(2)}, u32[]{:S(2)}) %collective-permute-start.9) | collective-permute-done | bytes 589856 | tf_op jit(solution)/shard_map/ppermute | solution.py:379
  64.2 1.0 %shard_map.82.refs_0_ = bf16[2,64,128]{2,1,0:T(8,128)(2,1)S(1)} custom-call(s32[30]{0:T(128)S(1)} %shard_map.73.plan_ref, bf16[8,128,2048]{2,1,0:T(8,128)(2,1)S(1)} %bitcast.6, bf16[2,64,2304]{2,1,0:T(8,128)(2,1)S(1)} %collective-permute-done.4.refs_0_.refs_6_, bf16[2,64,2304]{2,1,0:T(8,128)(2,1)S(1)} %collective-permute-done.9.refs_1_.refs_7_, ...), custom_call_target="tpu_custom_call" | custom-call | tf_op jit(solution)/shard_map/pallas_call | solution.py:300
  65.2 0.1 collective-permute-start.16
  65.3 0.8 %collective-permute-start.17 = (bf16[2,64,128]{2,1,0:T(8,128)(2,1)S(1)}, bf16[2,64,128]{2,1,0:T(8,128)(2,1)S(1)}, u32[]{:S(2)}, u32[]{:S(2)}) collective-permute-start(bf16[2,64,128]{2,1,0:T(8,128)(2,1)S(1)} %shard_map.82.refs_0_), channel_id=1, source_target_pairs={{0,2},{1,3},{2,0},{3,1},{4,6},{5,7},{6,4},{7,5},{8,10},{9,11},{10,... | collective-permute-start | bytes 98312 | tf_op jit(solution)/shard_map/ppermute | solution.py:29
  66.1 0.0 collective-permute-done.19.refs_1_
  66.1 1.1 %collective-permute-start.18 = (bf16[2,64,128]{2,1,0:T(8,128)(2,1)S(1)}, bf16[2,64,128]{2,1,0:T(8,128)(2,1)S(1)}, u32[]{:S(2)}, u32[]{:S(2)}) collective-permute-start(bf16[2,64,128]{2,1,0:T(8,128)(2,1)S(1)} %shard_map.82.refs_0_), channel_id=1, source_target_pairs={{0,3},{1,2},{2,1},{3,0},{4,7},{5,6},{6,5},{7,4},{8,11},{9,10},{10,... | collective-permute-start | bytes 98312 | tf_op jit(solution)/shard_map/ppermute | solution.py:29
  67.1 0.0 collective-permute-done.20.refs_2_
  67.1 0.0 collective-permute-done.21.refs_3_
  67.1 1.4 %shard_map.83.refs_8_ = bf16[1024,256]{1,0:T(8,128)(2,1)} custom-call(s32[30]{0:T(128)S(1)} %shard_map.73.plan_ref, f32[2,64,128]{2,1,0:T(8,128)S(1)} %shard_map.81.refs_2_.refs_0_, f32[2,64,128]{2,1,0:T(8,128)S(1)} %collective-permute-done.19.refs_1_, f32[2,64,128]{2,1,0:T(8,128)S(1)} %collective-permute-done.20.refs_2_, ...), custom_call_target="tpu_custom_call", output_to_operand_aliasing={{}: (9, {})} | custom-call | tf_op jit(solution)/shard_map/pallas_call | solution.py:362
  68.6 0.0 collective-permute-done.16.refs_1_
  68.6 0.8 %collective-permute-done.17.refs_2_ = bf16[2,64,128]{2,1,0:T(8,128)(2,1)S(1)} collective-permute-done((bf16[2,64,128]{2,1,0:T(8,128)(2,1)S(1)}, bf16[2,64,128]{2,1,0:T(8,128)(2,1)S(1)}, u32[]{:S(2)}, u32[]{:S(2)}) %collective-permute-start.17) | collective-permute-done | bytes 32800 | tf_op jit(solution)/shard_map/ppermute | solution.py:29
  69.4 0.3 collective-permute-done.18.refs_3_
  69.8 1.4 %shard_map.84 = bf16[1024,256]{1,0:T(8,128)(2,1)} custom-call(s32[30]{0:T(128)S(1)} %shard_map.73.plan_ref, bf16[2,64,128]{2,1,0:T(8,128)(2,1)S(1)} %shard_map.82.refs_0_, bf16[2,64,128]{2,1,0:T(8,128)(2,1)S(1)} %collective-permute-done.16.refs_1_, bf16[2,64,128]{2,1,0:T(8,128)(2,1)S(1)} %collective-permute-done.17.refs_2_, ...), custom_call_target="tpu_custom_call", output_to_operand_aliasing={{}: (9, {})} | custom-call | tf_op jit(solution)/shard_map/pallas_call | solution.py:362
Async XLA Ops:
  0.0 14.8 %collective-permute-start = (s32[1,8]{1,0:T(1,128)}, s32[1,8]{1,0:T(1,128)S(1)}, u32[]{:S(2)}, u32[]{:S(2)}) collective-permute-start(s32[1,8]{1,0:T(1,128)} %refs_0_.1), channel_id=1, source_target_pairs={{0,4},{4,0},{8,12},{12,8},{1,5},{5,1},{9,13},{13,9},{2,6},{6,2},{1... | collective-permute-start | bytes 104 | tf_op jit(solution)/shard_map/ppermute | solution.py:29
  3.0 11.9 %collective-permute-start.1 = (s32[1,8]{1,0:T(1,128)}, s32[1,8]{1,0:T(1,128)S(1)}, u32[]{:S(2)}, u32[]{:S(2)}) collective-permute-start(s32[1,8]{1,0:T(1,128)} %refs_0_.1), channel_id=1, source_target_pairs={{0,8},{4,12},{8,0},{12,4},{1,9},{5,13},{9,1},{13,5},{2,10},{6,14},... | collective-permute-start | bytes 104 | tf_op jit(solution)/shard_map/ppermute | solution.py:29
  5.6 9.8 %collective-permute-start.2 = (s32[1,8]{1,0:T(1,128)}, s32[1,8]{1,0:T(1,128)S(1)}, u32[]{:S(2)}, u32[]{:S(2)}) collective-permute-start(s32[1,8]{1,0:T(1,128)} %refs_0_.1), channel_id=1, source_target_pairs={{0,12},{4,8},{8,4},{12,0},{1,13},{5,9},{9,5},{13,1},{2,14},{6,10},... | collective-permute-start | bytes 104 | tf_op jit(solution)/shard_map/ppermute | solution.py:29
  5.6 9.9 %collective-permute-start.3 = (bf16[4,64,256]{2,1,0:T(8,128)(2,1)}, bf16[4,64,256]{2,1,0:T(8,128)(2,1)S(1)}, u32[]{:S(2)}, u32[]{:S(2)}) collective-permute-start(bf16[4,64,256]{2,1,0:T(8,128)(2,1)} %refs_6_.1), channel_id=1, source_target_pairs={{4,8},{8,4},{5,9},{9,5},{6,10},{10,6},{7,11},{11,7},{20,24},{24,20... | collective-permute-start | bytes 393224 | tf_op jit(solution)/shard_map/ppermute | solution.py:379
  6.3 27.6 %collective-permute-start.5 = (bf16[4,64,2048]{2,1,0:T(8,128)(2,1)}, bf16[4,64,2048]{2,1,0:T(8,128)(2,1)S(1)}, u32[]{:S(2)}, u32[]{:S(2)}) collective-permute-start(bf16[4,64,2048]{2,1,0:T(8,128)(2,1)} %bitcast.7), channel_id=1, source_target_pairs={{4,8},{8,4},{5,9},{9,5},{6,10},{10,6},{7,11},{11,7},{20,24},{24,20... | collective-permute-start | bytes 3145736 | tf_op jit(solution)/shard_map/ppermute | solution.py:379
  14.8 11.3 %collective-permute-start.8 = (f32[2,256,256]{2,1,0:T(8,128)S(1)}, f32[2,256,256]{2,1,0:T(8,128)S(1)}, u32[]{:S(2)}, u32[]{:S(2)}) collective-permute-start(f32[2,256,256]{2,1,0:T(8,128)S(1)} %get-tuple-element.13.rest_0_), channel_id=1, source_target_pairs={{0,1},{1,0},{2,3},{3,2},{4,5},{5,4},{6,7},{7,6},{8,9},{9,8},{10,11... | collective-permute-start | bytes 1572872 | tf_op jit(solution)/shard_map/ppermute | solution.py:29
  14.9 15.8 %collective-permute-start.6 = (f32[2,384,256]{2,1,0:T(8,128)S(1)}, f32[2,384,256]{2,1,0:T(8,128)S(1)}, u32[]{:S(2)}, u32[]{:S(2)}) collective-permute-start(f32[2,384,256]{2,1,0:T(8,128)S(1)} %get-tuple-element.16), channel_id=1, source_target_pairs={{0,1},{1,0},{2,3},{3,2},{4,5},{5,4},{6,7},{7,6},{8,9},{9,8},{10,11... | collective-permute-start | bytes 2359304 | tf_op jit(solution)/shard_map/ppermute | solution.py:29
  15.4 16.6 %collective-permute-start.7 = (f32[2,384,256]{2,1,0:T(8,128)S(1)}, f32[2,384,256]{2,1,0:T(8,128)S(1)}, u32[]{:S(2)}, u32[]{:S(2)}) collective-permute-start(f32[2,384,256]{2,1,0:T(8,128)S(1)} %get-tuple-element.17), channel_id=1, source_target_pairs={{0,1},{1,0},{2,3},{3,2},{4,5},{5,4},{6,7},{7,6},{8,9},{9,8},{10,11... | collective-permute-start | bytes 2359304 | tf_op jit(solution)/shard_map/ppermute | solution.py:29
  18.8 19.3 %collective-permute-start.11 = (bf16[2,64,2304]{2,1,0:T(8,128)(2,1)S(1)}, bf16[2,64,2304]{2,1,0:T(8,128)(2,1)S(1)}, u32[]{:S(2)}, u32[]{:S(2)}) collective-permute-start(bf16[2,64,2304]{2,1,0:T(8,128)(2,1)S(1)} %shard_map.75.rest_0_), channel_id=1, source_target_pairs={{0,4},{4,0},{8,12},{12,8},{1,5},{5,1},{9,13},{13,9},{2,6},{6,2},{1... | collective-permute-start | bytes 1769480 | tf_op jit(solution)/shard_map/ppermute | solution.py:379
  26.2 30.0 %collective-permute-start.10 = (bf16[2,64,2304]{2,1,0:T(8,128)(2,1)S(1)}, bf16[2,64,2304]{2,1,0:T(8,128)(2,1)S(1)}, u32[]{:S(2)}, u32[]{:S(2)}) collective-permute-start(bf16[2,64,2304]{2,1,0:T(8,128)(2,1)S(1)} %get-tuple-element.19), channel_id=1, source_target_pairs={{0,12},{12,0},{1,13},{13,1},{2,14},{14,2},{3,15},{15,3},{16,28},{2... | collective-permute-start | bytes 1769480 | tf_op jit(solution)/shard_map/ppermute | solution.py:379
  30.7 32.0 %collective-permute-start.4 = (bf16[2,64,2304]{2,1,0:T(8,128)(2,1)S(1)}, bf16[2,64,2304]{2,1,0:T(8,128)(2,1)S(1)}, u32[]{:S(2)}, u32[]{:S(2)}) collective-permute-start(bf16[2,64,2304]{2,1,0:T(8,128)(2,1)S(1)} %get-tuple-element.14), channel_id=1, source_target_pairs={{0,8},{12,4},{1,9},{13,5},{2,10},{14,6},{3,11},{15,7},{16,24},{28,... | collective-permute-start | bytes 1769480 | tf_op jit(solution)/shard_map/ppermute | solution.py:379
  32.3 22.4 %collective-permute-start.15 = (bf16[1,1024,256]{2,1,0:T(8,128)(2,1)S(1)}, bf16[1,1024,256]{2,1,0:T(8,128)(2,1)S(1)}, u32[]{:S(2)}, u32[]{:S(2)}) collective-permute-start(bf16[1,1024,256]{2,1,0:T(8,128)(2,1)S(1)} %get-tuple-element.20), channel_id=1, source_target_pairs={{0,2},{1,3},{2,0},{3,1},{4,6},{5,7},{6,4},{7,5},{8,10},{9,11},{10,... | collective-permute-start | bytes 1572872 | tf_op jit(solution)/shard_map/ppermute | solution.py:29
  33.9 4.3 %copy-start = (bf16[1024,2048]{1,0:T(8,128)(2,1)S(1)}, bf16[1024,2048]{1,0:T(8,128)(2,1)}, u32[]{:S(2)}) copy-start(bf16[1024,2048]{1,0:T(8,128)(2,1)} %tokens_ref.1) | copy-start | bytes 12582916
  33.9 4.3 %copy-start.1 = (bf16[4,2048,64]{1,2,0:T(8,128)(2,1)S(1)}, bf16[4,2048,64]{1,2,0:T(8,128)(2,1)}, u32[]{:S(2)}) copy-start(bf16[4,2048,64]{1,2,0:T(8,128)(2,1)} %param.9) | copy-start | bytes 3145732
  34.5 20.2 %copy-start.2 = (bf16[4,64,256]{2,1,0:T(8,128)(2,1)S(1)}, bf16[4,64,256]{2,1,0:T(8,128)(2,1)}, u32[]{:S(2)}) copy-start(bf16[4,64,256]{2,1,0:T(8,128)(2,1)} %refs_6_.1) | copy-start | bytes 393220
  34.5 29.6 %collective-permute-start.9 = (bf16[2,64,2304]{2,1,0:T(8,128)(2,1)S(1)}, bf16[2,64,2304]{2,1,0:T(8,128)(2,1)S(1)}, u32[]{:S(2)}, u32[]{:S(2)}) collective-permute-start(bf16[2,64,2304]{2,1,0:T(8,128)(2,1)S(1)} %shard_map.78.refs_2_), channel_id=1, source_target_pairs={{4,0},{8,12},{5,1},{9,13},{6,2},{10,14},{7,3},{11,15},{20,16},{24,... | collective-permute-start | bytes 1769480 | tf_op jit(solution)/shard_map/ppermute | solution.py:379
  39.5 1.4 %collective-permute-start.12 = (f32[4,64,128]{2,1,0:T(8,128)S(1)}, f32[4,64,128]{2,1,0:T(8,128)S(1)}, u32[]{:S(2)}, u32[]{:S(2)}) collective-permute-start(f32[4,64,128]{2,1,0:T(8,128)S(1)} %shard_map.79.refs_0_), channel_id=1, source_target_pairs={{0,1},{1,0},{2,3},{3,2},{4,5},{5,4},{6,7},{7,6},{8,9},{9,8},{10,11... | collective-permute-start | bytes 393224 | tf_op jit(solution)/shard_map/ppermute | solution.py:29
  40.9 8.0 %collective-permute-start.13 = (f32[4,64,128]{2,1,0:T(8,128)S(1)}, f32[4,64,128]{2,1,0:T(8,128)S(1)}, u32[]{:S(2)}, u32[]{:S(2)}) collective-permute-start(f32[4,64,128]{2,1,0:T(8,128)S(1)} %shard_map.79.refs_0_), channel_id=1, source_target_pairs={{0,2},{1,3},{2,0},{3,1},{4,6},{5,7},{6,4},{7,5},{8,10},{9,11},{10,... | collective-permute-start | bytes 393224 | tf_op jit(solution)/shard_map/ppermute | solution.py:29
  48.9 5.8 %collective-permute-start.14 = (f32[4,64,128]{2,1,0:T(8,128)S(1)}, f32[4,64,128]{2,1,0:T(8,128)S(1)}, u32[]{:S(2)}, u32[]{:S(2)}) collective-permute-start(f32[4,64,128]{2,1,0:T(8,128)S(1)} %shard_map.79.refs_0_), channel_id=1, source_target_pairs={{0,3},{1,2},{2,1},{3,0},{4,7},{5,6},{6,5},{7,4},{8,11},{9,10},{10,... | collective-permute-start | bytes 393224 | tf_op jit(solution)/shard_map/ppermute | solution.py:29
  57.2 8.8 %collective-permute-start.19 = (f32[2,64,128]{2,1,0:T(8,128)S(1)}, f32[2,64,128]{2,1,0:T(8,128)S(1)}, u32[]{:S(2)}, u32[]{:S(2)}) collective-permute-start(f32[2,64,128]{2,1,0:T(8,128)S(1)} %shard_map.81.refs_2_.refs_0_), channel_id=1, source_target_pairs={{0,1},{1,0},{2,3},{3,2},{4,5},{5,4},{6,7},{7,6},{8,9},{9,8},{10,11... | collective-permute-start | bytes 196616 | tf_op jit(solution)/shard_map/ppermute | solution.py:29
  57.4 9.7 %collective-permute-start.20 = (f32[2,64,128]{2,1,0:T(8,128)S(1)}, f32[2,64,128]{2,1,0:T(8,128)S(1)}, u32[]{:S(2)}, u32[]{:S(2)}) collective-permute-start(f32[2,64,128]{2,1,0:T(8,128)S(1)} %shard_map.81.refs_2_.refs_0_), channel_id=1, source_target_pairs={{0,2},{1,3},{2,0},{3,1},{4,6},{5,7},{6,4},{7,5},{8,10},{9,11},{10,... | collective-permute-start | bytes 196616 | tf_op jit(solution)/shard_map/ppermute | solution.py:29
  58.1 9.1 %collective-permute-start.21 = (f32[2,64,128]{2,1,0:T(8,128)S(1)}, f32[2,64,128]{2,1,0:T(8,128)S(1)}, u32[]{:S(2)}, u32[]{:S(2)}) collective-permute-start(f32[2,64,128]{2,1,0:T(8,128)S(1)} %shard_map.81.refs_2_.refs_0_), channel_id=1, source_target_pairs={{0,3},{1,2},{2,1},{3,0},{4,7},{5,6},{6,5},{7,4},{8,11},{9,10},{10,... | collective-permute-start | bytes 196616 | tf_op jit(solution)/shard_map/ppermute | solution.py:29
  65.2 3.4 %collective-permute-start.16 = (bf16[2,64,128]{2,1,0:T(8,128)(2,1)S(1)}, bf16[2,64,128]{2,1,0:T(8,128)(2,1)S(1)}, u32[]{:S(2)}, u32[]{:S(2)}) collective-permute-start(bf16[2,64,128]{2,1,0:T(8,128)(2,1)S(1)} %shard_map.82.refs_0_), channel_id=1, source_target_pairs={{0,1},{1,0},{2,3},{3,2},{4,5},{5,4},{6,7},{7,6},{8,9},{9,8},{10,11... | collective-permute-start | bytes 98312 | tf_op jit(solution)/shard_map/ppermute | solution.py:29
  65.3 4.2 %collective-permute-start.17 = (bf16[2,64,128]{2,1,0:T(8,128)(2,1)S(1)}, bf16[2,64,128]{2,1,0:T(8,128)(2,1)S(1)}, u32[]{:S(2)}, u32[]{:S(2)}) collective-permute-start(bf16[2,64,128]{2,1,0:T(8,128)(2,1)S(1)} %shard_map.82.refs_0_), channel_id=1, source_target_pairs={{0,2},{1,3},{2,0},{3,1},{4,6},{5,7},{6,4},{7,5},{8,10},{9,11},{10,... | collective-permute-start | bytes 98312 | tf_op jit(solution)/shard_map/ppermute | solution.py:29
  66.1 3.7 %collective-permute-start.18 = (bf16[2,64,128]{2,1,0:T(8,128)(2,1)S(1)}, bf16[2,64,128]{2,1,0:T(8,128)(2,1)S(1)}, u32[]{:S(2)}, u32[]{:S(2)}) collective-permute-start(bf16[2,64,128]{2,1,0:T(8,128)(2,1)S(1)} %shard_map.82.refs_0_), channel_id=1, source_target_pairs={{0,3},{1,2},{2,1},{3,0},{4,7},{5,6},{6,5},{7,4},{8,11},{9,10},{10,... | collective-permute-start | bytes 98312 | tf_op jit(solution)/shard_map/ppermute | solution.py:29

commit v11 on v10

--- a/solution.py
+++ b/solution.py
@@ -43,40 +43,53 @@
 def base_kernel(order, tokens_ref, weight_ref, *refs):
     *sent_refs, kept_ref, tokens, weight, sems = refs
     half, rows, width = kept_ref.shape
+    parts = sems.shape[1]
+    tile, slab = rows // parts, weight.shape[0] // parts
     place = lax.axis_index("tensor")
-    copies = []
-    for number, (source, held) in enumerate(((weight_ref, weight), (tokens_ref, tokens))):
-        tile = held.shape[0] // sems.shape[1]
-        for i in range(sems.shape[1]):
-            part = pl.ds(i * tile, tile)
-            copies.append(
-                pltpu.make_async_copy(source.at[part], held.at[part], sems.at[number, i])
-            )
-    run_copies(copies)
-    for copy in copies[: sems.shape[1]]:
-        copy.wait()
-    tile = rows // sems.shape[1]
-    for first in range(0, rows, tile):
-        copies[sems.shape[1] + first // tile].wait()
+
+    def copy_of(number, source, held, size, i):
+        span = pl.ds(i * size, size)
+        return pltpu.make_async_copy(source.at[span], held.at[span], sems.at[number, i])
+
+    token_copies = [copy_of(0, tokens_ref, tokens, tile, i) for i in range(parts)]
+    weight_copies = [copy_of(1, weight_ref, weight, slab, i) for i in range(parts)]
+
+    def add(first, low, high, fresh):
         for number, offset in enumerate(order):
             columns = pl.ds(pl.multiple_of((place ^ offset) * width, width), width)
             part = jnp.dot(
-                tokens[first : first + tile, :],
-                weight[:, columns],
+                tokens[first : first + tile, low:high],
+                weight[low:high, columns],
                 preferred_element_type=jnp.float32,
             )
             if number >= half:
-                kept_ref[number - half, first : first + tile, :] = part
-                continue
-            start = 0
-            for sent_ref in sent_refs:
-                stop = start + sent_ref.shape[1]
-                low, high = max(first, start), min(first + tile, stop)
-                if low < high:
-                    sent_ref[number, low - start : high - start, :] = part[
-                        low - first : high - first
-                    ]
-                start = stop
+                targets = [(kept_ref, number - half, first, 0, tile)]
+            else:
+                targets, start = [], 0
+                for sent_ref in sent_refs:
+                    stop = start + sent_ref.shape[1]
+                    above, below = max(first, start), min(first + tile, stop)
+                    if above < below:
+                        targets.append(
+                            (sent_ref, number, above - start, above - first, below - above)
+                        )
+                    start = stop
+            for ref, index, at, source, size in targets:
+                value = part[source : source + size]
+                if not fresh:
+                    value = value + ref[index, at : at + size, :]
+                ref[index, at : at + size, :] = value
+
+    run_copies([token_copies[0], *weight_copies])
+    token_copies[0].wait()
+    for i, copy in enumerate(weight_copies):
+        copy.wait()
+        if i == 0:
+            run_copies(token_copies[1:])
+        add(0, i * slab, (i + 1) * slab, i == 0)
+    for i in range(1, parts):
+        token_copies[i].wait()
+        add(i * tile, 0, weight.shape[0], True)
 
 
 def base_chunks(tokens, weight, order, width):
@@ -224,34 +237,38 @@
     )(in_hbm(names), *others, in_hbm(table), in_hbm(live), *after)
 
 
-def pack_kernel(starts, capacity, plan_ref, down_ref, up_ref, *rest):
-    count = len(starts)
-    sems = rest[-1]
-    outs = rest[-1 - count : -1]
-    copies = []
-    for number, start in enumerate(starts):
+def pack_kernel(starts, choose, capacity, plan_ref, *refs):
+    out_ref, sems = refs[-2:]
+
+    def run(start, down_ref, up_ref):
+        copies = []
         for k in range(capacity):
             slot = plan_ref[start + k]
-            copies += run_copies(
-                panel_copies(k, slot, down_ref, up_ref, outs[number], sems.at[number])
-            )
-    for copy in copies:
-        copy.wait()
-
-
-def pack_panels(plan, starts, capacity, down, up, after=(), cost=None):
-    rank, depth = down.shape[1:]
-    width = up.shape[2]
-    out = jax.ShapeDtypeStruct((capacity, rank, depth + width), down.dtype)
+            copies += run_copies(panel_copies(k, slot, down_ref, up_ref, out_ref, sems))
+        for copy in copies:
+            copy.wait()
+
+    if len(starts) == 1:
+        run(starts[0], *refs[:2])
+    else:
+        first = plan_ref[choose] != 0
+        pl.when(first)(functools.partial(run, starts[0], *refs[:2]))
+        pl.when(jnp.logical_not(first))(functools.partial(run, starts[1], *refs[2:4]))
+
+
+def pack_panels(plan, choices, choose, capacity, after=(), cost=None):
+    sources = [a for _, *pair in choices for a in pair]
+    rank, depth = sources[0].shape[1:]
+    width = sources[1].shape[2]
     return pl.pallas_call(
-        functools.partial(pack_kernel, starts, capacity),
-        in_specs=[SMEM] + [ANY] * (2 + len(after)),
-        out_specs=[ANY] * len(starts),
-        out_shape=[out] * len(starts),
-        scratch_shapes=[pltpu.SemaphoreType.DMA((len(starts), capacity, 2))],
+        functools.partial(pack_kernel, [start for start, *_ in choices], choose, capacity),
+        in_specs=[SMEM] + [ANY] * (len(sources) + len(after)),
+        out_specs=ANY,
+        out_shape=jax.ShapeDtypeStruct((capacity, rank, depth + width), sources[0].dtype),
+        scratch_shapes=[pltpu.SemaphoreType.DMA((capacity, 2))],
         compiler_params=PARAMS,
         cost_estimate=cost or NO_COST,
-    )(plan, down, up, *after)
+    )(plan, *sources, *after)
 
 
 def each_block(phases, choose, plan_ref, refs, act):
@@ -379,35 +396,38 @@
         return lax.ppermute(value, "pool", pairs)
 
     others = [swap(names, "pool", m) for m in range(1, 4)]
-    inner_down = across(down, [(1, 2), (2, 1)])
-    inner_up = across(up, [(1, 2), (2, 1)])
+    inner_up = across(up, [(0, 0), (1, 2), (2, 1), (3, 3)])
+    inner_down = across(down, [(0, 0), (1, 2), (2, 1), (3, 3)])
     sent, kept = base_parts(tokens, weight, up.shape[2])
     plan = make_plan(names, others, table, live, down.shape[0], capacity, [inner_up])
+    choose = INNER * capacity
     held = in_hbm(down), in_hbm(up)
-    (near_out,) = pack_panels(plan, [NEAR * capacity], capacity, *held, sent[-1:])
+
+    def pack(choices, after, cost=None):
+        choices = [(row * capacity, *panels) for row, *panels in choices]
+        return pack_panels(plan, choices, choose, capacity, after, cost)
+
+    near_out = pack([(NEAR, *held)], sent[-1:])
     near = across(near_out, [(0, 1), (1, 0), (2, 3), (3, 2)])
-    outer_out, inner_out = pack_panels(
-        plan, [TO_OUTER * capacity, TO_INNER * capacity], capacity, *held, [near_out]
+    outer_out = pack([(TO_OUTER, *held)], [near_out])
+    to_outer = across(outer_out, [(0, 3), (1, 1), (2, 2), (3, 0)])
+    base = base_sum(sent, kept)
+    late_out = pack(
+        [(FORWARD, inner_down, inner_up), (TO_INNER, *held)], [base[0], outer_out], LONG
     )
-    to_outer = across(outer_out, [(0, 3), (3, 0)])
-    to_inner = across(inner_out, [(0, 2), (3, 1)])
-    choose = INNER * capacity
+    late = across(late_out, [(0, 2), (1, 0), (2, 3), (3, 1)])
+
     first = [(0, capacity, [(down, OWN * capacity)]), (capacity, capacity, [(near, None)])]
     first_up = [(0, capacity, [(up, OWN * capacity)]), first[1]]
-    base = base_sum(sent, kept)
-    (forward_out,) = pack_panels(
-        plan, [FORWARD * capacity], capacity, inner_down, inner_up, [base[0]], LONG
-    )
-    forwarded = across(forward_out, [(1, 0), (2, 3)])
     middle = [(2 * capacity, capacity, [(inner_down, ACROSS * capacity), (to_outer, None)])]
     middle_up = [(2 * capacity, capacity, [(inner_up, ACROSS * capacity), (to_outer, None)])]
-    last = [(3 * capacity, capacity, [(to_inner, None), (forwarded, None)])]
+    last = [(3 * capacity, capacity, [(late, None)])]
 
     def write(number, parts, phases, out, cost=None):
         live_row = (LIVE + number) * capacity
         return combine(plan, live_row, parts, base, phases, choose, out, cost)
 
-    first_parts = exchange(shrink(plan, row_blocks, first, choose, [forward_out]))
+    first_parts = exchange(shrink(plan, row_blocks, first, choose, [late_out]))
     out = write(0, first_parts, first_up, None, MIDDLE)
     middle_part = shrink(plan, row_blocks, middle, choose, [in_hbm(out)])
     middle_parts = exchange(middle_part)
@@ -428,7 +448,7 @@
         hit = slots // holder_slots == here
         chosen = hit[None, :] & (jnp.cumsum(hit.astype(jnp.int32))[None, :] == 1 + count[:, None])
         plan = jnp.sum(jnp.where(chosen, (slots % holder_slots)[None, :], 0), axis=1)
-        (panels,) = pack_panels(plan, [0], capacity, down, up)
+        panels = pack_panels(plan, [(0, down, up)], 0, capacity)
         pairs = [(i, (i + distance) % pool_size) for i in range(pool_size)]
         arrived.append(lax.ppermute(panels, "pool", pairs) if distance else panels)
     arrived = jnp.concatenate(arrived)

time: 71.3 us -> 72.1 us (1.011)
  starting transfers between devices: 27.6 us -> 30 us
  waiting for transfers between devices: 21.6 us -> 19.6 us
    ppermute x16, waiting for transfers between devices: 14.6 us -> 7.29 us  [swap(): return lax.ppermute(value, axis, pairs)]
    ppermute x6 -> x5, waiting for transfers between devices: 7.04 us -> 12.3 us  [across(): return lax.ppermute(value, 'pool', pairs)]
    ppermute x6 -> x5, starting transfers between devices: 14.2 us -> 15.7 us  [across(): return lax.ppermute(value, 'pool', pairs)]
    pallas_call x3, Pallas kernels: 4.21 us -> 5.16 us  [pack_panels(): pl.pallas_call(functools.partial(pack_kernel, [start for start, *_ in cho...]
    ppermute x16, starting transfers between devices: 13.4 us -> 14.3 us  [swap(): return lax.ppermute(value, axis, pairs)]
    pallas_call x1, Pallas kernels: 7.78 us -> 7.03 us  [base_chunks(): pl.pallas_call(functools.partial(base_kernel, order), in_specs=[ANY] * 2,...]
  transfers between devices with their start and end apart: 22 -> 21, of which waited for: 8 -> 7; matrix products, arithmetic and copies ran while one was open for 0% -> 0% of each run, Pallas kernels for 29% -> 29%
where the time goes in v11:
time: 72.1 us; the launch traced here: 71.8 us
  starting transfers between devices  30 us (42%)
  Pallas kernels  22 us (31%)
  waiting for transfers between devices  19.6 us (27%)
    ppermute x5, starting transfers between devices, across(): return lax.ppermute(value, 'pool', pairs)  15.7 us
    ppermute x16, starting transfers between devices, swap(): return lax.ppermute(value, axis, pairs)  14.3 us
    ppermute x5, waiting for transfers between devices, across(): return lax.ppermute(value, 'pool', pairs)  12.3 us
    ppermute x16, waiting for transfers between devices, swap(): return lax.ppermute(value, axis, pairs)  7.29 us
    pallas_call x1, Pallas kernels, base_chunks(): pl.pallas_call(functools.partial(base_kernel, order), in_specs=[ANY] * 2,...  7.03 us
    pallas_call x3, Pallas kernels, pack_panels(): pl.pallas_call(functools.partial(pack_kernel, [start for start, *_ in cho...  5.16 us
    pallas_call x3, Pallas kernels, combine(): pl.pallas_call(functools.partial(combine_kernel, shapes, choose, len(part...  4.38 us
    pallas_call x3, Pallas kernels, shrink(): pl.pallas_call(functools.partial(shrink_kernel, shapes, choose), in_specs...  3.42 us
  transfers between devices with their start and end apart: 21, of which 7 were waited for; matrix products, arithmetic and copies ran while one was open for 0% of the time, Pallas kernels for 29%

profile of v11, /device:TPU:0, one launch (start us, length us, event | category | flops | bytes accessed | tf_op | source)
XLA Modules:
  0.0 71.8 jit_solution(5688413385343772443)
XLA Ops:
  0.0 3.0 %collective-permute-start = (s32[1,8]{1,0:T(1,128)}, s32[1,8]{1,0:T(1,128)S(1)}, u32[]{:S(2)}, u32[]{:S(2)}) collective-permute-start(s32[1,8]{1,0:T(1,128)} %refs_0_.1), channel_id=1, source_target_pairs={{0,4},{4,0},{8,12},{12,8},{1,5},{5,1},{9,13},{13,9},{2,6},{6,2},{1... | collective-permute-start | bytes 104 | tf_op jit(solution)/shard_map/ppermute | solution.py:29
  3.0 2.6 %collective-permute-start.1 = (s32[1,8]{1,0:T(1,128)}, s32[1,8]{1,0:T(1,128)S(1)}, u32[]{:S(2)}, u32[]{:S(2)}) collective-permute-start(s32[1,8]{1,0:T(1,128)} %refs_0_.1), channel_id=1, source_target_pairs={{0,8},{4,12},{8,0},{12,4},{1,9},{5,13},{9,1},{13,5},{2,10},{6,14},... | collective-permute-start | bytes 104 | tf_op jit(solution)/shard_map/ppermute | solution.py:29
  5.6 0.0 collective-permute-start.2
  5.6 1.6 %collective-permute-start.3 = (bf16[4,64,256]{2,1,0:T(8,128)(2,1)}, bf16[4,64,256]{2,1,0:T(8,128)(2,1)S(1)}, u32[]{:S(2)}, u32[]{:S(2)}) collective-permute-start(bf16[4,64,256]{2,1,0:T(8,128)(2,1)} %refs_6_.1), channel_id=1, source_target_pairs={{0,0},{4,8},{8,4},{12,12},{1,1},{5,9},{9,5},{13,13},{2,2},{6,10},{... | collective-permute-start | bytes 393224 | tf_op jit(solution)/shard_map/ppermute | solution.py:396
  7.2 1.9 %collective-permute-start.4 = (bf16[4,64,2048]{2,1,0:T(8,128)(2,1)}, bf16[4,64,2048]{2,1,0:T(8,128)(2,1)S(1)}, u32[]{:S(2)}, u32[]{:S(2)}) collective-permute-start(bf16[4,64,2048]{2,1,0:T(8,128)(2,1)} %bitcast.7), channel_id=1, source_target_pairs={{0,0},{4,8},{8,4},{12,12},{1,1},{5,9},{9,5},{13,13},{2,2},{6,10},{... | collective-permute-start | bytes 3145736 | tf_op jit(solution)/shard_map/ppermute | solution.py:396
  9.0 7.0 %shard_map.74 = (f32[2,384,256]{2,1,0:T(8,128)S(1)}, f32[2,384,256]{2,1,0:T(8,128)S(1)}, f32[2,256,256]{2,1,0:T(8,128)S(1)}, f32[2,1024,256]{2,1,0:T(8,128)S(1)}) custom-call(bf16[1024,2048]{1,0:T(8,128)(2,1)} %tokens_ref.1, bf16[2048,1024]{1,0:T(8,128)(2,1)} %weight_ref.1), custom_call_target="tpu_custom_call" | custom-call | flops 4000000000 | tf_op jit(solution)/shard_map/pallas_call | solution.py:99
  16.1 0.0 collective-permute-done.refs_1_
  16.1 0.1 collective-permute-start.7
  16.2 0.0 collective-permute-done.1.refs_2_
  16.2 0.5 collective-permute-start.5
  16.7 0.0 collective-permute-done.2.refs_3_
  16.7 0.1 collective-permute-start.6
  16.8 0.0 collective-permute-done.3.refs_6_.refs_1_
  16.8 1.7 %shard_map.73.plan_ref = s32[30]{0:T(128)S(1)} custom-call(s32[1,8]{1,0:T(1,128)} %refs_0_.1, s32[1,8]{1,0:T(1,128)S(1)} %collective-permute-done.refs_1_, s32[1,8]{1,0:T(1,128)S(1)} %collective-permute-done.1.refs_2_, s32[1,8]{1,0:T(1,128)S(1)} %collective-permute-done.2.refs_3_, s32[16]{0:T(128)} %refs_4_.1, s32[1,8]{1,0:T(1,128)} %refs_5_.1, ...), custom_call_target="tpu_custom_call" | custom-call | flops 10000000000 | tf_op jit(solution)/shard_map/pallas_call | solution.py:227
  18.4 1.6 %shard_map.76.refs_2_ = bf16[2,64,2304]{2,1,0:T(8,128)(2,1)S(1)} custom-call(s32[30]{0:T(128)S(1)} %shard_map.73.plan_ref, bf16[4,64,2048]{2,1,0:T(8,128)(2,1)} %bitcast.8, bf16[4,64,256]{2,1,0:T(8,128)(2,1)} %refs_6_.1, f32[2,256,256]{2,1,0:T(8,128)S(1)} %get-tuple-element.14.refs_2_), custom_call_target="tpu_custom_call" | custom-call | tf_op jit(solution)/shard_map/pallas_call | solution.py:263
  20.1 1.6 %shard_map.77.refs_5_ = bf16[2,64,2304]{2,1,0:T(8,128)(2,1)S(1)} custom-call(s32[30]{0:T(128)S(1)} %shard_map.73.plan_ref, bf16[4,64,2048]{2,1,0:T(8,128)(2,1)} %bitcast.9, bf16[4,64,256]{2,1,0:T(8,128)(2,1)} %refs_6_.1, bf16[2,64,2304]{2,1,0:T(8,128)(2,1)S(1)} %shard_map.76.refs_2_), custom_call_target="tpu_custom_call" | custom-call | tf_op jit(solution)/shard_map/pallas_call | solution.py:263
  21.7 3.4 %collective-permute-start.10 = (bf16[2,64,2304]{2,1,0:T(8,128)(2,1)S(1)}, bf16[2,64,2304]{2,1,0:T(8,128)(2,1)S(1)}, u32[]{:S(2)}, u32[]{:S(2)}) collective-permute-start(bf16[2,64,2304]{2,1,0:T(8,128)(2,1)S(1)} %shard_map.76.refs_2_), channel_id=1, source_target_pairs={{0,4},{4,0},{8,12},{12,8},{1,5},{5,1},{9,13},{13,9},{2,6},{6,2},{1... | collective-permute-start | bytes 1769480 | tf_op jit(solution)/shard_map/ppermute | solution.py:396
  25.1 0.0 collective-permute-done.7.refs_2_
  25.2 4.3 %collective-permute-start.9 = (bf16[2,64,2304]{2,1,0:T(8,128)(2,1)S(1)}, bf16[2,64,2304]{2,1,0:T(8,128)(2,1)S(1)}, u32[]{:S(2)}, u32[]{:S(2)}) collective-permute-start(bf16[2,64,2304]{2,1,0:T(8,128)(2,1)S(1)} %shard_map.77.refs_5_), channel_id=1, source_target_pairs={{0,12},{4,4},{8,8},{12,0},{1,13},{5,5},{9,9},{13,1},{2,14},{6,6},{... | collective-permute-start | bytes 1769480 | tf_op jit(solution)/shard_map/ppermute | solution.py:396
  29.5 0.0 collective-permute-done.5.refs_0_
  29.5 0.0 collective-permute-done.6.refs_1_
  29.5 0.3 shard_map.75
  29.8 1.5 %collective-permute-start.14 = (bf16[1,1024,256]{2,1,0:T(8,128)(2,1)S(1)}, bf16[1,1024,256]{2,1,0:T(8,128)(2,1)S(1)}, u32[]{:S(2)}, u32[]{:S(2)}) collective-permute-start(bf16[1,1024,256]{2,1,0:T(8,128)(2,1)S(1)} %get-tuple-element.16), channel_id=1, source_target_pairs={{0,2},{1,3},{2,0},{3,1},{4,6},{5,7},{6,4},{7,5},{8,10},{9,11},{10,... | collective-permute-start | bytes 1572872 | tf_op jit(solution)/shard_map/ppermute | solution.py:29
  31.4 0.0 collective-permute-done.4.refs_0_
  31.4 0.0 copy-start
  31.4 0.0 copy-start.1
  31.4 1.9 %shard_map.78.refs_2_ = bf16[2,64,2304]{2,1,0:T(8,128)(2,1)S(1)} custom-call(s32[30]{0:T(128)S(1)} %shard_map.73.plan_ref, bf16[4,64,2048]{2,1,0:T(8,128)(2,1)S(1)} %collective-permute-done.4.refs_0_, bf16[4,64,256]{2,1,0:T(8,128)(2,1)S(1)} %collective-permute-done.3.refs_6_.refs_1_, bf16[4,64,2048]{2,1,0:T(8,128)(2,1)} %bitcast.10, ...), custom_call_target="tpu_custom_call" | custom-call | flops 6000000000 | tf_op jit(solution)/shard_map/pallas_call | solution.py:263
  33.3 0.0 copy-start.2
  33.3 4.5 %collective-permute-start.8 = (bf16[2,64,2304]{2,1,0:T(8,128)(2,1)S(1)}, bf16[2,64,2304]{2,1,0:T(8,128)(2,1)S(1)}, u32[]{:S(2)}, u32[]{:S(2)}) collective-permute-start(bf16[2,64,2304]{2,1,0:T(8,128)(2,1)S(1)} %shard_map.78.refs_2_), channel_id=1, source_target_pairs={{0,8},{4,0},{8,12},{12,4},{1,9},{5,1},{9,13},{13,5},{2,10},{6,2},{... | collective-permute-start | bytes 1769480 | tf_op jit(solution)/shard_map/ppermute | solution.py:396
  37.8 1.5 %collective-permute-done.10.refs_1_.refs_7_ = bf16[2,64,2304]{2,1,0:T(8,128)(2,1)S(1)} collective-permute-done((bf16[2,64,2304]{2,1,0:T(8,128)(2,1)S(1)}, bf16[2,64,2304]{2,1,0:T(8,128)(2,1)S(1)}, u32[]{:S(2)}, u32[]{:S(2)}) %collective-permute-start.10) | collective-permute-done | bytes 589856 | tf_op jit(solution)/shard_map/ppermute | solution.py:396
  39.3 0.0 copy-done
  39.3 0.0 copy-done.1
  39.3 1.4 %shard_map.79.refs_0_ = f32[4,64,128]{2,1,0:T(8,128)S(1)} custom-call(s32[30]{0:T(128)S(1)} %shard_map.73.plan_ref, bf16[8,128,2048]{2,1,0:T(8,128)(2,1)S(1)} %bitcast.4, bf16[4,64,2048]{2,1,0:T(8,128)(2,1)S(1)} %bitcast.11, bf16[2,64,2304]{2,1,0:T(8,128)(2,1)S(1)} %collective-permute-done.10.refs_1_.refs_7_, bf16[2,64,2304]{2,1,0:T(8,128)(2,1)S(1)} %shard_map.78.refs_2_), custom_call_target="tpu_custom_call" | custom-call | tf_op jit(solution)/shard_map/pallas_call | solution.py:317
  40.7 0.1 collective-permute-start.11
  40.8 1.5 %collective-permute-start.12 = (f32[4,64,128]{2,1,0:T(8,128)S(1)}, f32[4,64,128]{2,1,0:T(8,128)S(1)}, u32[]{:S(2)}, u32[]{:S(2)}) collective-permute-start(f32[4,64,128]{2,1,0:T(8,128)S(1)} %shard_map.79.refs_0_), channel_id=1, source_target_pairs={{0,2},{1,3},{2,0},{3,1},{4,6},{5,7},{6,4},{7,5},{8,10},{9,11},{10,... | collective-permute-start | bytes 393224 | tf_op jit(solution)/shard_map/ppermute | solution.py:29
  42.3 0.0 collective-permute-done.11.refs_1_
  42.3 1.0 %collective-permute-start.13 = (f32[4,64,128]{2,1,0:T(8,128)S(1)}, f32[4,64,128]{2,1,0:T(8,128)S(1)}, u32[]{:S(2)}, u32[]{:S(2)}) collective-permute-start(f32[4,64,128]{2,1,0:T(8,128)S(1)} %shard_map.79.refs_0_), channel_id=1, source_target_pairs={{0,3},{1,2},{2,1},{3,0},{4,7},{5,6},{6,5},{7,4},{8,11},{9,10},{10,... | collective-permute-start | bytes 393224 | tf_op jit(solution)/shard_map/ppermute | solution.py:29
  43.4 3.8 %collective-permute-done.12.refs_2_ = f32[4,64,128]{2,1,0:T(8,128)S(1)} collective-permute-done((f32[4,64,128]{2,1,0:T(8,128)S(1)}, f32[4,64,128]{2,1,0:T(8,128)S(1)}, u32[]{:S(2)}, u32[]{:S(2)}) %collective-permute-start.12) | collective-permute-done | bytes 131104 | tf_op jit(solution)/shard_map/ppermute | solution.py:29
  47.2 1.9 %collective-permute-done.13.refs_3_ = f32[4,64,128]{2,1,0:T(8,128)S(1)} collective-permute-done((f32[4,64,128]{2,1,0:T(8,128)S(1)}, f32[4,64,128]{2,1,0:T(8,128)S(1)}, u32[]{:S(2)}, u32[]{:S(2)}) %collective-permute-start.13) | collective-permute-done | bytes 131104 | tf_op jit(solution)/shard_map/ppermute | solution.py:29
  49.1 0.0 collective-permute-done.14
  49.1 0.0 copy-done.2
  49.1 1.5 %shard_map.80.refs_2_.refs_8_ = bf16[1024,256]{1,0:T(8,128)(2,1)} custom-call(s32[30]{0:T(128)S(1)} %shard_map.73.plan_ref, f32[4,64,128]{2,1,0:T(8,128)S(1)} %shard_map.79.refs_0_, f32[4,64,128]{2,1,0:T(8,128)S(1)} %collective-permute-done.11.refs_1_, f32[4,64,128]{2,1,0:T(8,128)S(1)} %collective-permute-done.12.refs_2_, ...), custom_call_target="tpu_custom_call" | custom-call | tf_op jit(solution)/shard_map/pallas_call | solution.py:379
  50.6 3.8 %collective-permute-done.9.refs_1_.refs_7_ = bf16[2,64,2304]{2,1,0:T(8,128)(2,1)S(1)} collective-permute-done((bf16[2,64,2304]{2,1,0:T(8,128)(2,1)S(1)}, bf16[2,64,2304]{2,1,0:T(8,128)(2,1)S(1)}, u32[]{:S(2)}, u32[]{:S(2)}) %collective-permute-start.9) | collective-permute-done | bytes 589856 | tf_op jit(solution)/shard_map/ppermute | solution.py:396
  54.4 1.0 %shard_map.81.refs_1_.refs_0_ = f32[2,64,128]{2,1,0:T(8,128)S(1)} custom-call(s32[30]{0:T(128)S(1)} %shard_map.73.plan_ref, bf16[8,128,2048]{2,1,0:T(8,128)(2,1)S(1)} %bitcast.5, bf16[4,64,2048]{2,1,0:T(8,128)(2,1)S(1)} %collective-permute-done.4.refs_0_, bf16[2,64,2304]{2,1,0:T(8,128)(2,1)S(1)} %collective-permute-done.9.refs_1_.refs_7_, ...), custom_call_target="tpu_custom_call" | custom-call | tf_op jit(solution)/shard_map/pallas_call | solution.py:317
  55.4 0.1 collective-permute-start.18
  55.5 1.5 %collective-permute-start.19 = (f32[2,64,128]{2,1,0:T(8,128)S(1)}, f32[2,64,128]{2,1,0:T(8,128)S(1)}, u32[]{:S(2)}, u32[]{:S(2)}) collective-permute-start(f32[2,64,128]{2,1,0:T(8,128)S(1)} %shard_map.81.refs_1_.refs_0_), channel_id=1, source_target_pairs={{0,2},{1,3},{2,0},{3,1},{4,6},{5,7},{6,4},{7,5},{8,10},{9,11},{10,... | collective-permute-start | bytes 196616 | tf_op jit(solution)/shard_map/ppermute | solution.py:29
  57.0 0.3 collective-permute-start.20
  57.4 7.0 %collective-permute-done.8.refs_0_.refs_6_ = bf16[2,64,2304]{2,1,0:T(8,128)(2,1)S(1)} collective-permute-done((bf16[2,64,2304]{2,1,0:T(8,128)(2,1)S(1)}, bf16[2,64,2304]{2,1,0:T(8,128)(2,1)S(1)}, u32[]{:S(2)}, u32[]{:S(2)}) %collective-permute-start.8) | collective-permute-done | bytes 589856 | tf_op jit(solution)/shard_map/ppermute | solution.py:396
  64.3 1.0 %shard_map.82.refs_0_ = bf16[2,64,128]{2,1,0:T(8,128)(2,1)S(1)} custom-call(s32[30]{0:T(128)S(1)} %shard_map.73.plan_ref, bf16[8,128,2048]{2,1,0:T(8,128)(2,1)S(1)} %bitcast.6, bf16[2,64,2304]{2,1,0:T(8,128)(2,1)S(1)} %collective-permute-done.8.refs_0_.refs_6_, f32[2,64,128]{2,1,0:T(8,128)S(1)} %shard_map.81.refs_1_.refs_0_), custom_call_target="tpu_custom_call" | custom-call | tf_op jit(solution)/shard_map/pallas_call | solution.py:317
  65.4 0.1 collective-permute-start.15
  65.5 1.5 %collective-permute-start.16 = (bf16[2,64,128]{2,1,0:T(8,128)(2,1)S(1)}, bf16[2,64,128]{2,1,0:T(8,128)(2,1)S(1)}, u32[]{:S(2)}, u32[]{:S(2)}) collective-permute-start(bf16[2,64,128]{2,1,0:T(8,128)(2,1)S(1)} %shard_map.82.refs_0_), channel_id=1, source_target_pairs={{0,2},{1,3},{2,0},{3,1},{4,6},{5,7},{6,4},{7,5},{8,10},{9,11},{10,... | collective-permute-start | bytes 98312 | tf_op jit(solution)/shard_map/ppermute | solution.py:29
  67.0 0.0 collective-permute-done.18.refs_1_
  67.0 0.3 collective-permute-start.17
  67.3 0.0 collective-permute-done.19.refs_2_
  67.3 0.0 collective-permute-done.20.refs_3_
  67.3 1.4 %shard_map.83.refs_7_ = bf16[1024,256]{1,0:T(8,128)(2,1)} custom-call(s32[30]{0:T(128)S(1)} %shard_map.73.plan_ref, f32[2,64,128]{2,1,0:T(8,128)S(1)} %shard_map.81.refs_1_.refs_0_, f32[2,64,128]{2,1,0:T(8,128)S(1)} %collective-permute-done.18.refs_1_, f32[2,64,128]{2,1,0:T(8,128)S(1)} %collective-permute-done.19.refs_2_, ...), custom_call_target="tpu_custom_call", output_to_operand_aliasing={{}: (9, {})} | custom-call | tf_op jit(solution)/shard_map/pallas_call | solution.py:379
  68.8 0.0 collective-permute-done.15.refs_1_
  68.8 0.6 collective-permute-done.16.refs_2_
  69.4 0.9 %collective-permute-done.17.refs_3_ = bf16[2,64,128]{2,1,0:T(8,128)(2,1)S(1)} collective-permute-done((bf16[2,64,128]{2,1,0:T(8,128)(2,1)S(1)}, bf16[2,64,128]{2,1,0:T(8,128)(2,1)S(1)}, u32[]{:S(2)}, u32[]{:S(2)}) %collective-permute-start.17) | collective-permute-done | bytes 32800 | tf_op jit(solution)/shard_map/ppermute | solution.py:29
  70.3 1.4 %shard_map.84 = bf16[1024,256]{1,0:T(8,128)(2,1)} custom-call(s32[30]{0:T(128)S(1)} %shard_map.73.plan_ref, bf16[2,64,128]{2,1,0:T(8,128)(2,1)S(1)} %shard_map.82.refs_0_, bf16[2,64,128]{2,1,0:T(8,128)(2,1)S(1)} %collective-permute-done.15.refs_1_, bf16[2,64,128]{2,1,0:T(8,128)(2,1)S(1)} %collective-permute-done.16.refs_2_, ...), custom_call_target="tpu_custom_call", output_to_operand_aliasing={{}: (8, {})} | custom-call | tf_op jit(solution)/shard_map/pallas_call | solution.py:379
Async XLA Ops:
  0.0 16.1 %collective-permute-start = (s32[1,8]{1,0:T(1,128)}, s32[1,8]{1,0:T(1,128)S(1)}, u32[]{:S(2)}, u32[]{:S(2)}) collective-permute-start(s32[1,8]{1,0:T(1,128)} %refs_0_.1), channel_id=1, source_target_pairs={{0,4},{4,0},{8,12},{12,8},{1,5},{5,1},{9,13},{13,9},{2,6},{6,2},{1... | collective-permute-start | bytes 104 | tf_op jit(solution)/shard_map/ppermute | solution.py:29
  3.0 13.1 %collective-permute-start.1 = (s32[1,8]{1,0:T(1,128)}, s32[1,8]{1,0:T(1,128)S(1)}, u32[]{:S(2)}, u32[]{:S(2)}) collective-permute-start(s32[1,8]{1,0:T(1,128)} %refs_0_.1), channel_id=1, source_target_pairs={{0,8},{4,12},{8,0},{12,4},{1,9},{5,13},{9,1},{13,5},{2,10},{6,14},... | collective-permute-start | bytes 104 | tf_op jit(solution)/shard_map/ppermute | solution.py:29
  5.6 11.1 %collective-permute-start.2 = (s32[1,8]{1,0:T(1,128)}, s32[1,8]{1,0:T(1,128)S(1)}, u32[]{:S(2)}, u32[]{:S(2)}) collective-permute-start(s32[1,8]{1,0:T(1,128)} %refs_0_.1), channel_id=1, source_target_pairs={{0,12},{4,8},{8,4},{12,0},{1,13},{5,9},{9,5},{13,1},{2,14},{6,10},... | collective-permute-start | bytes 104 | tf_op jit(solution)/shard_map/ppermute | solution.py:29
  5.6 11.1 %collective-permute-start.3 = (bf16[4,64,256]{2,1,0:T(8,128)(2,1)}, bf16[4,64,256]{2,1,0:T(8,128)(2,1)S(1)}, u32[]{:S(2)}, u32[]{:S(2)}) collective-permute-start(bf16[4,64,256]{2,1,0:T(8,128)(2,1)} %refs_6_.1), channel_id=1, source_target_pairs={{0,0},{4,8},{8,4},{12,12},{1,1},{5,9},{9,5},{13,13},{2,2},{6,10},{... | collective-permute-start | bytes 393224 | tf_op jit(solution)/shard_map/ppermute | solution.py:396
  7.2 24.2 %collective-permute-start.4 = (bf16[4,64,2048]{2,1,0:T(8,128)(2,1)}, bf16[4,64,2048]{2,1,0:T(8,128)(2,1)S(1)}, u32[]{:S(2)}, u32[]{:S(2)}) collective-permute-start(bf16[4,64,2048]{2,1,0:T(8,128)(2,1)} %bitcast.7), channel_id=1, source_target_pairs={{0,0},{4,8},{8,4},{12,12},{1,1},{5,9},{9,5},{13,13},{2,2},{6,10},{... | collective-permute-start | bytes 3145736 | tf_op jit(solution)/shard_map/ppermute | solution.py:396
  16.1 9.1 %collective-permute-start.7 = (f32[2,256,256]{2,1,0:T(8,128)S(1)}, f32[2,256,256]{2,1,0:T(8,128)S(1)}, u32[]{:S(2)}, u32[]{:S(2)}) collective-permute-start(f32[2,256,256]{2,1,0:T(8,128)S(1)} %get-tuple-element.14.refs_2_), channel_id=1, source_target_pairs={{0,1},{1,0},{2,3},{3,2},{4,5},{5,4},{6,7},{7,6},{8,9},{9,8},{10,11... | collective-permute-start | bytes 1572872 | tf_op jit(solution)/shard_map/ppermute | solution.py:29
  16.2 13.3 %collective-permute-start.5 = (f32[2,384,256]{2,1,0:T(8,128)S(1)}, f32[2,384,256]{2,1,0:T(8,128)S(1)}, u32[]{:S(2)}, u32[]{:S(2)}) collective-permute-start(f32[2,384,256]{2,1,0:T(8,128)S(1)} %get-tuple-element.12), channel_id=1, source_target_pairs={{0,1},{1,0},{2,3},{3,2},{4,5},{5,4},{6,7},{7,6},{8,9},{9,8},{10,11... | collective-permute-start | bytes 2359304 | tf_op jit(solution)/shard_map/ppermute | solution.py:29
  16.7 12.8 %collective-permute-start.6 = (f32[2,384,256]{2,1,0:T(8,128)S(1)}, f32[2,384,256]{2,1,0:T(8,128)S(1)}, u32[]{:S(2)}, u32[]{:S(2)}) collective-permute-start(f32[2,384,256]{2,1,0:T(8,128)S(1)} %get-tuple-element.13), channel_id=1, source_target_pairs={{0,1},{1,0},{2,3},{3,2},{4,5},{5,4},{6,7},{7,6},{8,9},{9,8},{10,11... | collective-permute-start | bytes 2359304 | tf_op jit(solution)/shard_map/ppermute | solution.py:29
  21.7 17.6 %collective-permute-start.10 = (bf16[2,64,2304]{2,1,0:T(8,128)(2,1)S(1)}, bf16[2,64,2304]{2,1,0:T(8,128)(2,1)S(1)}, u32[]{:S(2)}, u32[]{:S(2)}) collective-permute-start(bf16[2,64,2304]{2,1,0:T(8,128)(2,1)S(1)} %shard_map.76.refs_2_), channel_id=1, source_target_pairs={{0,4},{4,0},{8,12},{12,8},{1,5},{5,1},{9,13},{13,9},{2,6},{6,2},{1... | collective-permute-start | bytes 1769480 | tf_op jit(solution)/shard_map/ppermute | solution.py:396
  25.2 29.2 %collective-permute-start.9 = (bf16[2,64,2304]{2,1,0:T(8,128)(2,1)S(1)}, bf16[2,64,2304]{2,1,0:T(8,128)(2,1)S(1)}, u32[]{:S(2)}, u32[]{:S(2)}) collective-permute-start(bf16[2,64,2304]{2,1,0:T(8,128)(2,1)S(1)} %shard_map.77.refs_5_), channel_id=1, source_target_pairs={{0,12},{4,4},{8,8},{12,0},{1,13},{5,5},{9,9},{13,1},{2,14},{6,6},{... | collective-permute-start | bytes 1769480 | tf_op jit(solution)/shard_map/ppermute | solution.py:396
  29.8 19.2 %collective-permute-start.14 = (bf16[1,1024,256]{2,1,0:T(8,128)(2,1)S(1)}, bf16[1,1024,256]{2,1,0:T(8,128)(2,1)S(1)}, u32[]{:S(2)}, u32[]{:S(2)}) collective-permute-start(bf16[1,1024,256]{2,1,0:T(8,128)(2,1)S(1)} %get-tuple-element.16), channel_id=1, source_target_pairs={{0,2},{1,3},{2,0},{3,1},{4,6},{5,7},{6,4},{7,5},{8,10},{9,11},{10,... | collective-permute-start | bytes 1572872 | tf_op jit(solution)/shard_map/ppermute | solution.py:29
  31.4 8.0 %copy-start = (bf16[1024,2048]{1,0:T(8,128)(2,1)S(1)}, bf16[1024,2048]{1,0:T(8,128)(2,1)}, u32[]{:S(2)}) copy-start(bf16[1024,2048]{1,0:T(8,128)(2,1)} %tokens_ref.1) | copy-start | bytes 12582916
  31.4 8.0 %copy-start.1 = (bf16[4,2048,64]{1,2,0:T(8,128)(2,1)S(1)}, bf16[4,2048,64]{1,2,0:T(8,128)(2,1)}, u32[]{:S(2)}) copy-start(bf16[4,2048,64]{1,2,0:T(8,128)(2,1)} %param.9) | copy-start | bytes 3145732
  33.3 15.8 %copy-start.2 = (bf16[4,64,256]{2,1,0:T(8,128)(2,1)S(1)}, bf16[4,64,256]{2,1,0:T(8,128)(2,1)}, u32[]{:S(2)}) copy-start(bf16[4,64,256]{2,1,0:T(8,128)(2,1)} %refs_6_.1) | copy-start | bytes 393220
  33.3 31.1 %collective-permute-start.8 = (bf16[2,64,2304]{2,1,0:T(8,128)(2,1)S(1)}, bf16[2,64,2304]{2,1,0:T(8,128)(2,1)S(1)}, u32[]{:S(2)}, u32[]{:S(2)}) collective-permute-start(bf16[2,64,2304]{2,1,0:T(8,128)(2,1)S(1)} %shard_map.78.refs_2_), channel_id=1, source_target_pairs={{0,8},{4,0},{8,12},{12,4},{1,9},{5,1},{9,13},{13,5},{2,10},{6,2},{... | collective-permute-start | bytes 1769480 | tf_op jit(solution)/shard_map/ppermute | solution.py:396
  40.7 1.6 %collective-permute-start.11 = (f32[4,64,128]{2,1,0:T(8,128)S(1)}, f32[4,64,128]{2,1,0:T(8,128)S(1)}, u32[]{:S(2)}, u32[]{:S(2)}) collective-permute-start(f32[4,64,128]{2,1,0:T(8,128)S(1)} %shard_map.79.refs_0_), channel_id=1, source_target_pairs={{0,1},{1,0},{2,3},{3,2},{4,5},{5,4},{6,7},{7,6},{8,9},{9,8},{10,11... | collective-permute-start | bytes 393224 | tf_op jit(solution)/shard_map/ppermute | solution.py:29
  40.8 6.4 %collective-permute-start.12 = (f32[4,64,128]{2,1,0:T(8,128)S(1)}, f32[4,64,128]{2,1,0:T(8,128)S(1)}, u32[]{:S(2)}, u32[]{:S(2)}) collective-permute-start(f32[4,64,128]{2,1,0:T(8,128)S(1)} %shard_map.79.refs_0_), channel_id=1, source_target_pairs={{0,2},{1,3},{2,0},{3,1},{4,6},{5,7},{6,4},{7,5},{8,10},{9,11},{10,... | collective-permute-start | bytes 393224 | tf_op jit(solution)/shard_map/ppermute | solution.py:29
  42.3 6.7 %collective-permute-start.13 = (f32[4,64,128]{2,1,0:T(8,128)S(1)}, f32[4,64,128]{2,1,0:T(8,128)S(1)}, u32[]{:S(2)}, u32[]{:S(2)}) collective-permute-start(f32[4,64,128]{2,1,0:T(8,128)S(1)} %shard_map.79.refs_0_), channel_id=1, source_target_pairs={{0,3},{1,2},{2,1},{3,0},{4,7},{5,6},{6,5},{7,4},{8,11},{9,10},{10,... | collective-permute-start | bytes 393224 | tf_op jit(solution)/shard_map/ppermute | solution.py:29
  55.4 11.6 %collective-permute-start.18 = (f32[2,64,128]{2,1,0:T(8,128)S(1)}, f32[2,64,128]{2,1,0:T(8,128)S(1)}, u32[]{:S(2)}, u32[]{:S(2)}) collective-permute-start(f32[2,64,128]{2,1,0:T(8,128)S(1)} %shard_map.81.refs_1_.refs_0_), channel_id=1, source_target_pairs={{0,1},{1,0},{2,3},{3,2},{4,5},{5,4},{6,7},{7,6},{8,9},{9,8},{10,11... | collective-permute-start | bytes 196616 | tf_op jit(solution)/shard_map/ppermute | solution.py:29
  55.5 11.8 %collective-permute-start.19 = (f32[2,64,128]{2,1,0:T(8,128)S(1)}, f32[2,64,128]{2,1,0:T(8,128)S(1)}, u32[]{:S(2)}, u32[]{:S(2)}) collective-permute-start(f32[2,64,128]{2,1,0:T(8,128)S(1)} %shard_map.81.refs_1_.refs_0_), channel_id=1, source_target_pairs={{0,2},{1,3},{2,0},{3,1},{4,6},{5,7},{6,4},{7,5},{8,10},{9,11},{10,... | collective-permute-start | bytes 196616 | tf_op jit(solution)/shard_map/ppermute | solution.py:29
  57.0 10.3 %collective-permute-start.20 = (f32[2,64,128]{2,1,0:T(8,128)S(1)}, f32[2,64,128]{2,1,0:T(8,128)S(1)}, u32[]{:S(2)}, u32[]{:S(2)}) collective-permute-start(f32[2,64,128]{2,1,0:T(8,128)S(1)} %shard_map.81.refs_1_.refs_0_), channel_id=1, source_target_pairs={{0,3},{1,2},{2,1},{3,0},{4,7},{5,6},{6,5},{7,4},{8,11},{9,10},{10,... | collective-permute-start | bytes 196616 | tf_op jit(solution)/shard_map/ppermute | solution.py:29
  65.4 3.4 %collective-permute-start.15 = (bf16[2,64,128]{2,1,0:T(8,128)(2,1)S(1)}, bf16[2,64,128]{2,1,0:T(8,128)(2,1)S(1)}, u32[]{:S(2)}, u32[]{:S(2)}) collective-permute-start(bf16[2,64,128]{2,1,0:T(8,128)(2,1)S(1)} %shard_map.82.refs_0_), channel_id=1, source_target_pairs={{0,1},{1,0},{2,3},{3,2},{4,5},{5,4},{6,7},{7,6},{8,9},{9,8},{10,11... | collective-permute-start | bytes 98312 | tf_op jit(solution)/shard_map/ppermute | solution.py:29
  65.5 4.0 %collective-permute-start.16 = (bf16[2,64,128]{2,1,0:T(8,128)(2,1)S(1)}, bf16[2,64,128]{2,1,0:T(8,128)(2,1)S(1)}, u32[]{:S(2)}, u32[]{:S(2)}) collective-permute-start(bf16[2,64,128]{2,1,0:T(8,128)(2,1)S(1)} %shard_map.82.refs_0_), channel_id=1, source_target_pairs={{0,2},{1,3},{2,0},{3,1},{4,6},{5,7},{6,4},{7,5},{8,10},{9,11},{10,... | collective-permute-start | bytes 98312 | tf_op jit(solution)/shard_map/ppermute | solution.py:29
  67.0 3.3 %collective-permute-start.17 = (bf16[2,64,128]{2,1,0:T(8,128)(2,1)S(1)}, bf16[2,64,128]{2,1,0:T(8,128)(2,1)S(1)}, u32[]{:S(2)}, u32[]{:S(2)}) collective-permute-start(bf16[2,64,128]{2,1,0:T(8,128)(2,1)S(1)} %shard_map.82.refs_0_), channel_id=1, source_target_pairs={{0,3},{1,2},{2,1},{3,0},{4,7},{5,6},{6,5},{7,4},{8,11},{9,10},{10,... | collective-permute-start | bytes 98312 | tf_op jit(solution)/shard_map/ppermute | solution.py:29

commit v12 on v11

--- a/solution.py
+++ b/solution.py
@@ -183,10 +183,12 @@
     ]
 
 
-def plan_kernel(capacity, holder_slots, *refs):
-    sources, plan_ref, scalars, sems = refs[:6], refs[-8], refs[-7:-1], refs[-1]
+def plan_kernel(capacity, *refs):
+    sources, down_ref, up_ref = refs[:6], *refs[6:8]
+    near_ref, plan_ref, *scalars, scalar_sems, sems = refs[-10:]
+    holder_slots = down_ref.shape[0]
     loads = [
-        pltpu.make_async_copy(source, scalar, sems.at[i])
+        pltpu.make_async_copy(source, scalar, scalar_sems.at[i])
         for i, (source, scalar) in enumerate(zip(sources, scalars))
     ]
     for load in run_copies(loads):
@@ -196,6 +198,10 @@
     find = functools.partial(
         pick, table_ref=table_ref, holder_slots=holder_slots, count=capacity
     )
+    near_slots = find(first_ref, holder=here)[1]
+    copies = []
+    for k, slot in enumerate(near_slots):
+        copies += run_copies(panel_copies(k, slot, down_ref, up_ref, near_ref, sems))
     inner = (here == 1) | (here == 2)
     own = find(names_ref, holder=here)
     near = find(names_ref, holder=here ^ 1)
@@ -208,7 +214,6 @@
         late[0],
         own[1],
         across[1],
-        find(first_ref, holder=here)[1],
         find(second_ref, holder=here)[1],
         find(third_ref, holder=here)[1],
         find(first_ref, holder=here ^ 3)[1],
@@ -218,23 +223,29 @@
     for number, row in enumerate(rows):
         for k in range(capacity):
             plan_ref[number * capacity + k] = row[k]
-
-
-OWN, ACROSS, NEAR, TO_INNER, TO_OUTER, FORWARD, INNER, LIVE, PLAN_ROWS = 4, 5, 6, 7, 8, 9, 10, 11, 15
-
-
-def make_plan(names, others, table, live, holder_slots, capacity, after):
+    for copy in copies:
+        copy.wait()
+
+
+OWN, ACROSS, TO_INNER, TO_OUTER, FORWARD, INNER, LIVE, PLAN_ROWS = 4, 5, 6, 7, 8, 9, 10, 14
+
+
+def make_plan(names, others, table, live, down, up, capacity, after):
+    rank, depth = down.shape[1:]
     return pl.pallas_call(
-        functools.partial(plan_kernel, capacity, holder_slots),
-        in_specs=[ANY] * (6 + len(after)),
-        out_specs=SMEM,
-        out_shape=jax.ShapeDtypeStruct((PLAN_ROWS * capacity,), jnp.int32),
+        functools.partial(plan_kernel, capacity),
+        in_specs=[ANY] * (8 + len(after)),
+        out_specs=[ANY, SMEM],
+        out_shape=[
+            jax.ShapeDtypeStruct((capacity, rank, depth + up.shape[2]), down.dtype),
+            jax.ShapeDtypeStruct((PLAN_ROWS * capacity,), jnp.int32),
+        ],
         scratch_shapes=[pltpu.SMEM(names.shape, jnp.int32)] * 4
         + [pltpu.SMEM(table.shape, jnp.int32), pltpu.SMEM(live.shape, jnp.int32)]
-        + [pltpu.SemaphoreType.DMA((6,))],
+        + [pltpu.SemaphoreType.DMA((6,)), pltpu.SemaphoreType.DMA((capacity, 2))],
         compiler_params=PARAMS,
         cost_estimate=SHORT,
-    )(in_hbm(names), *others, in_hbm(table), in_hbm(live), *after)
+    )(in_hbm(names), *others, in_hbm(table), in_hbm(live), down, up, *after)
 
 
 def pack_kernel(starts, choose, capacity, plan_ref, *refs):
@@ -399,21 +410,22 @@
     inner_up = across(up, [(0, 0), (1, 2), (2, 1), (3, 3)])
     inner_down = across(down, [(0, 0), (1, 2), (2, 1), (3, 3)])
     sent, kept = base_parts(tokens, weight, up.shape[2])
-    plan = make_plan(names, others, table, live, down.shape[0], capacity, [inner_up])
     choose = INNER * capacity
     held = in_hbm(down), in_hbm(up)
+    near_out, plan = make_plan(
+        names, others, table, live, *held, capacity, [inner_up, sent[-1]]
+    )
 
     def pack(choices, after, cost=None):
         choices = [(row * capacity, *panels) for row, *panels in choices]
         return pack_panels(plan, choices, choose, capacity, after, cost)
 
-    near_out = pack([(NEAR, *held)], sent[-1:])
     near = across(near_out, [(0, 1), (1, 0), (2, 3), (3, 2)])
-    outer_out = pack([(TO_OUTER, *held)], [near_out])
+    base = base_sum(sent, kept)
+    outer_out = pack([(TO_OUTER, *held)], [base[0]])
     to_outer = across(outer_out, [(0, 3), (1, 1), (2, 2), (3, 0)])
-    base = base_sum(sent, kept)
     late_out = pack(
-        [(FORWARD, inner_down, inner_up), (TO_INNER, *held)], [base[0], outer_out], LONG
+        [(FORWARD, inner_down, inner_up), (TO_INNER, *held)], [outer_out], LONG
     )
     late = across(late_out, [(0, 2), (1, 0), (2, 3), (3, 1)])
 

time: 72.1 us -> 69.9 us (0.969)
  waiting for transfers between devices: 19.6 us -> 17.3 us
  Pallas kernels: 22 us -> 21.1 us
  starting transfers between devices: 30 us -> 30.9 us
    ppermute x5, waiting for transfers between devices: 12.3 us -> 10.1 us  [across(): return lax.ppermute(value, 'pool', pairs)]
    pallas_call x3 -> x2, Pallas kernels: 5.16 us -> 3.31 us  [pack_panels(): pl.pallas_call(functools.partial(pack_kernel, [start for start, *_ in cho...]
    pallas_call x1, Pallas kernels: 1.66 us -> 2.7 us  [make_plan(): pl.pallas_call(functools.partial(plan_kernel, capacity), in_specs=[ANY] *...]
    ppermute x5, starting transfers between devices: 15.7 us -> 16.6 us  [across(): return lax.ppermute(value, 'pool', pairs)]
  transfers between devices with their start and end apart: 21 -> 21, of which waited for: 7 -> 6; matrix products, arithmetic and copies ran while one was open for 0% -> 0% of each run, Pallas kernels for 29% -> 28%
where the time goes in v12:
time: 69.9 us; the launch traced here: 69.5 us
  starting transfers between devices  30.9 us (44%)
  Pallas kernels  21.1 us (30%)
  waiting for transfers between devices  17.3 us (25%)
    ppermute x5, starting transfers between devices, across(): return lax.ppermute(value, 'pool', pairs)  16.6 us
    ppermute x16, starting transfers between devices, swap(): return lax.ppermute(value, axis, pairs)  14.3 us
    ppermute x5, waiting for transfers between devices, across(): return lax.ppermute(value, 'pool', pairs)  10.1 us
    ppermute x16, waiting for transfers between devices, swap(): return lax.ppermute(value, axis, pairs)  7.27 us
    pallas_call x1, Pallas kernels, base_chunks(): pl.pallas_call(functools.partial(base_kernel, order), in_specs=[ANY] * 2,...  7.03 us
    pallas_call x3, Pallas kernels, combine(): pl.pallas_call(functools.partial(combine_kernel, shapes, choose, len(part...  4.38 us
    pallas_call x3, Pallas kernels, shrink(): pl.pallas_call(functools.partial(shrink_kernel, shapes, choose), in_specs...  3.42 us
    pallas_call x2, Pallas kernels, pack_panels(): pl.pallas_call(functools.partial(pack_kernel, [start for start, *_ in cho...  3.31 us
  transfers between devices with their start and end apart: 21, of which 6 were waited for; matrix products, arithmetic and copies ran while one was open for 0% of the time, Pallas kernels for 28%

profile of v12, /device:TPU:0, one launch (start us, length us, event | category | flops | bytes accessed | tf_op | source)
XLA Modules:
  0.0 69.5 jit_solution(10540422992420438819)
XLA Ops:
  0.0 3.0 %collective-permute-start = (s32[1,8]{1,0:T(1,128)}, s32[1,8]{1,0:T(1,128)S(1)}, u32[]{:S(2)}, u32[]{:S(2)}) collective-permute-start(s32[1,8]{1,0:T(1,128)} %refs_0_.1), channel_id=1, source_target_pairs={{0,4},{4,0},{8,12},{12,8},{1,5},{5,1},{9,13},{13,9},{2,6},{6,2},{1... | collective-permute-start | bytes 104 | tf_op jit(solution)/shard_map/ppermute | solution.py:29
  3.0 2.6 %collective-permute-start.1 = (s32[1,8]{1,0:T(1,128)}, s32[1,8]{1,0:T(1,128)S(1)}, u32[]{:S(2)}, u32[]{:S(2)}) collective-permute-start(s32[1,8]{1,0:T(1,128)} %refs_0_.1), channel_id=1, source_target_pairs={{0,8},{4,12},{8,0},{12,4},{1,9},{5,13},{9,1},{13,5},{2,10},{6,14},... | collective-permute-start | bytes 104 | tf_op jit(solution)/shard_map/ppermute | solution.py:29
  5.6 0.0 collective-permute-start.2
  5.6 1.6 %collective-permute-start.3 = (bf16[4,64,256]{2,1,0:T(8,128)(2,1)}, bf16[4,64,256]{2,1,0:T(8,128)(2,1)S(1)}, u32[]{:S(2)}, u32[]{:S(2)}) collective-permute-start(bf16[4,64,256]{2,1,0:T(8,128)(2,1)} %refs_6_.1), channel_id=1, source_target_pairs={{0,0},{4,8},{8,4},{12,12},{1,1},{5,9},{9,5},{13,13},{2,2},{6,10},{... | collective-permute-start | bytes 393224 | tf_op jit(solution)/shard_map/ppermute | solution.py:407
  7.2 1.9 %collective-permute-start.4 = (bf16[4,64,2048]{2,1,0:T(8,128)(2,1)}, bf16[4,64,2048]{2,1,0:T(8,128)(2,1)S(1)}, u32[]{:S(2)}, u32[]{:S(2)}) collective-permute-start(bf16[4,64,2048]{2,1,0:T(8,128)(2,1)} %bitcast.14), channel_id=1, source_target_pairs={{0,0},{4,8},{8,4},{12,12},{1,1},{5,9},{9,5},{13,13},{2,2},{6,10},{... | collective-permute-start | bytes 3145736 | tf_op jit(solution)/shard_map/ppermute | solution.py:407
  9.0 7.0 %shard_map.73 = (f32[2,384,256]{2,1,0:T(8,128)S(1)}, f32[2,384,256]{2,1,0:T(8,128)S(1)}, f32[2,256,256]{2,1,0:T(8,128)S(1)}, f32[2,1024,256]{2,1,0:T(8,128)S(1)}) custom-call(bf16[1024,2048]{1,0:T(8,128)(2,1)} %tokens_ref.1, bf16[2048,1024]{1,0:T(8,128)(2,1)} %weight_ref.1), custom_call_target="tpu_custom_call" | custom-call | flops 4000000000 | tf_op jit(solution)/shard_map/pallas_call | solution.py:99
  16.1 0.0 collective-permute-done.refs_1_
  16.1 0.1 collective-permute-start.7
  16.2 0.0 collective-permute-done.1.refs_2_
  16.2 0.5 collective-permute-start.5
  16.7 0.0 collective-permute-done.2.refs_3_
  16.7 0.1 collective-permute-start.6
  16.8 0.0 collective-permute-done.3.refs_8_.refs_1_.refs_6_
  16.8 2.7 %shard_map.74 = (bf16[2,64,2304]{2,1,0:T(8,128)(2,1)S(1)}, s32[28]{0:T(128)S(1)}) custom-call(s32[1,8]{1,0:T(1,128)} %refs_0_.1, s32[1,8]{1,0:T(1,128)S(1)} %collective-permute-done.refs_1_, s32[1,8]{1,0:T(1,128)S(1)} %collective-permute-done.1.refs_2_, s32[1,8]{1,0:T(1,128)S(1)} %collective-permute-done.2.refs_3_, s32[16]{0:T(128)} %refs_4_.1, ...), custom_call_target="tpu_custom_call" | custom-call | flops 10000000000 | tf_op jit(solution)/shard_map/pallas_call | solution.py:235
  19.5 3.4 %collective-permute-start.10 = (bf16[2,64,2304]{2,1,0:T(8,128)(2,1)S(1)}, bf16[2,64,2304]{2,1,0:T(8,128)(2,1)S(1)}, u32[]{:S(2)}, u32[]{:S(2)}) collective-permute-start(bf16[2,64,2304]{2,1,0:T(8,128)(2,1)S(1)} %get-tuple-element.19), channel_id=1, source_target_pairs={{0,4},{4,0},{8,12},{12,8},{1,5},{5,1},{9,13},{13,9},{2,6},{6,2},{1... | collective-permute-start | bytes 1769480 | tf_op jit(solution)/shard_map/ppermute | solution.py:407
  22.9 0.0 collective-permute-done.7.refs_2_
  22.9 0.0 collective-permute-done.5.refs_0_
  22.9 0.0 collective-permute-done.6.refs_1_
  22.9 0.2 shard_map.75
  23.1 1.5 %collective-permute-start.14 = (bf16[1,1024,256]{2,1,0:T(8,128)(2,1)S(1)}, bf16[1,1024,256]{2,1,0:T(8,128)(2,1)S(1)}, u32[]{:S(2)}, u32[]{:S(2)}) collective-permute-start(bf16[1,1024,256]{2,1,0:T(8,128)(2,1)S(1)} %get-tuple-element.20), channel_id=1, source_target_pairs={{0,2},{1,3},{2,0},{3,1},{4,6},{5,7},{6,4},{7,5},{8,10},{9,11},{10,... | collective-permute-start | bytes 1572872 | tf_op jit(solution)/shard_map/ppermute | solution.py:29
  24.7 1.6 %shard_map.76.refs_4_ = bf16[2,64,2304]{2,1,0:T(8,128)(2,1)S(1)} custom-call(s32[28]{0:T(128)S(1)} %get-tuple-element.14.plan_ref, bf16[4,64,2048]{2,1,0:T(8,128)(2,1)} %bitcast.16, bf16[4,64,256]{2,1,0:T(8,128)(2,1)} %refs_6_.1, f32[1024,256]{1,0:T(8,128)S(1)} %bitcast.7), custom_call_target="tpu_custom_call" | custom-call | tf_op jit(solution)/shard_map/pallas_call | solution.py:274
  26.3 0.0 copy-start
  26.3 0.0 copy-start.1
  26.3 4.6 %collective-permute-start.9 = (bf16[2,64,2304]{2,1,0:T(8,128)(2,1)S(1)}, bf16[2,64,2304]{2,1,0:T(8,128)(2,1)S(1)}, u32[]{:S(2)}, u32[]{:S(2)}) collective-permute-start(bf16[2,64,2304]{2,1,0:T(8,128)(2,1)S(1)} %shard_map.76.refs_4_), channel_id=1, source_target_pairs={{0,12},{4,4},{8,8},{12,0},{1,13},{5,5},{9,9},{13,1},{2,14},{6,6},{... | collective-permute-start | bytes 1769480 | tf_op jit(solution)/shard_map/ppermute | solution.py:407
  31.0 0.0 collective-permute-done.4.refs_0_
  31.0 1.7 %shard_map.77.refs_2_ = bf16[2,64,2304]{2,1,0:T(8,128)(2,1)S(1)} custom-call(s32[28]{0:T(128)S(1)} %get-tuple-element.14.plan_ref, bf16[4,64,2048]{2,1,0:T(8,128)(2,1)S(1)} %collective-permute-done.4.refs_0_, bf16[4,64,256]{2,1,0:T(8,128)(2,1)S(1)} %collective-permute-done.3.refs_8_.refs_1_.refs_6_, bf16[4,64,2048]{2,1,0:T(8,128)(2,1)} %bitcast.17, ...), custom_call_target="tpu_custom_call" | custom-call | flops 6000000000 | tf_op jit(solution)/shard_map/pallas_call | solution.py:274
  32.6 0.0 copy-start.2
  32.7 5.1 %collective-permute-start.8 = (bf16[2,64,2304]{2,1,0:T(8,128)(2,1)S(1)}, bf16[2,64,2304]{2,1,0:T(8,128)(2,1)S(1)}, u32[]{:S(2)}, u32[]{:S(2)}) collective-permute-start(bf16[2,64,2304]{2,1,0:T(8,128)(2,1)S(1)} %shard_map.77.refs_2_), channel_id=1, source_target_pairs={{0,8},{4,0},{8,12},{12,4},{1,9},{5,1},{9,13},{13,5},{2,10},{6,2},{... | collective-permute-start | bytes 1769480 | tf_op jit(solution)/shard_map/ppermute | solution.py:407
  37.8 0.0 collective-permute-done.10.refs_1_.refs_7_
  37.8 0.0 copy-done
  37.8 0.0 copy-done.1
  37.8 1.4 %shard_map.78.refs_0_ = f32[4,64,128]{2,1,0:T(8,128)S(1)} custom-call(s32[28]{0:T(128)S(1)} %get-tuple-element.14.plan_ref, bf16[8,128,2048]{2,1,0:T(8,128)(2,1)S(1)} %bitcast.4, bf16[4,64,2048]{2,1,0:T(8,128)(2,1)S(1)} %bitcast.18, bf16[2,64,2304]{2,1,0:T(8,128)(2,1)S(1)} %collective-permute-done.10.refs_1_.refs_7_, bf16[2,64,2304]{2,1,0:T(8,128)(2,1)S(1)} %shard_map.77.refs_2_), custom_call_target="tpu_custom_call" | custom-call | tf_op jit(solution)/shard_map/pallas_call | solution.py:328
  39.2 0.1 collective-permute-start.11
  39.3 1.6 %collective-permute-start.12 = (f32[4,64,128]{2,1,0:T(8,128)S(1)}, f32[4,64,128]{2,1,0:T(8,128)S(1)}, u32[]{:S(2)}, u32[]{:S(2)}) collective-permute-start(f32[4,64,128]{2,1,0:T(8,128)S(1)} %shard_map.78.refs_0_), channel_id=1, source_target_pairs={{0,2},{1,3},{2,0},{3,1},{4,6},{5,7},{6,4},{7,5},{8,10},{9,11},{10,... | collective-permute-start | bytes 393224 | tf_op jit(solution)/shard_map/ppermute | solution.py:29
  40.8 0.0 collective-permute-done.11.refs_1_
  40.8 1.0 %collective-permute-start.13 = (f32[4,64,128]{2,1,0:T(8,128)S(1)}, f32[4,64,128]{2,1,0:T(8,128)S(1)}, u32[]{:S(2)}, u32[]{:S(2)}) collective-permute-start(f32[4,64,128]{2,1,0:T(8,128)S(1)} %shard_map.78.refs_0_), channel_id=1, source_target_pairs={{0,3},{1,2},{2,1},{3,0},{4,7},{5,6},{6,5},{7,4},{8,11},{9,10},{10,... | collective-permute-start | bytes 393224 | tf_op jit(solution)/shard_map/ppermute | solution.py:29
  41.8 3.8 %collective-permute-done.12.refs_2_ = f32[4,64,128]{2,1,0:T(8,128)S(1)} collective-permute-done((f32[4,64,128]{2,1,0:T(8,128)S(1)}, f32[4,64,128]{2,1,0:T(8,128)S(1)}, u32[]{:S(2)}, u32[]{:S(2)}) %collective-permute-start.12) | collective-permute-done | bytes 131104 | tf_op jit(solution)/shard_map/ppermute | solution.py:29
  45.6 1.9 %collective-permute-done.13.refs_3_ = f32[4,64,128]{2,1,0:T(8,128)S(1)} collective-permute-done((f32[4,64,128]{2,1,0:T(8,128)S(1)}, f32[4,64,128]{2,1,0:T(8,128)S(1)}, u32[]{:S(2)}, u32[]{:S(2)}) %collective-permute-start.13) | collective-permute-done | bytes 131104 | tf_op jit(solution)/shard_map/ppermute | solution.py:29
  47.5 0.0 collective-permute-done.14
  47.5 0.0 copy-done.2
  47.5 1.5 %shard_map.79.refs_2_.refs_8_ = bf16[1024,256]{1,0:T(8,128)(2,1)} custom-call(s32[28]{0:T(128)S(1)} %get-tuple-element.14.plan_ref, f32[4,64,128]{2,1,0:T(8,128)S(1)} %shard_map.78.refs_0_, f32[4,64,128]{2,1,0:T(8,128)S(1)} %collective-permute-done.11.refs_1_, f32[4,64,128]{2,1,0:T(8,128)S(1)} %collective-permute-done.12.refs_2_, ...), custom_call_target="tpu_custom_call" | custom-call | tf_op jit(solution)/shard_map/pallas_call | solution.py:390
  49.0 3.1 %collective-permute-done.9.refs_1_.refs_7_ = bf16[2,64,2304]{2,1,0:T(8,128)(2,1)S(1)} collective-permute-done((bf16[2,64,2304]{2,1,0:T(8,128)(2,1)S(1)}, bf16[2,64,2304]{2,1,0:T(8,128)(2,1)S(1)}, u32[]{:S(2)}, u32[]{:S(2)}) %collective-permute-start.9) | collective-permute-done | bytes 589856 | tf_op jit(solution)/shard_map/ppermute | solution.py:407
  52.1 1.0 %shard_map.80.refs_1_.refs_0_ = f32[2,64,128]{2,1,0:T(8,128)S(1)} custom-call(s32[28]{0:T(128)S(1)} %get-tuple-element.14.plan_ref, bf16[8,128,2048]{2,1,0:T(8,128)(2,1)S(1)} %bitcast.5, bf16[4,64,2048]{2,1,0:T(8,128)(2,1)S(1)} %collective-permute-done.4.refs_0_, bf16[2,64,2304]{2,1,0:T(8,128)(2,1)S(1)} %collective-permute-done.9.refs_1_.refs_7_, ...), custom_call_target="tpu_custom_call" | custom-call | tf_op jit(solution)/shard_map/pallas_call | solution.py:328
  53.2 0.1 collective-permute-start.18
  53.3 1.5 %collective-permute-start.19 = (f32[2,64,128]{2,1,0:T(8,128)S(1)}, f32[2,64,128]{2,1,0:T(8,128)S(1)}, u32[]{:S(2)}, u32[]{:S(2)}) collective-permute-start(f32[2,64,128]{2,1,0:T(8,128)S(1)} %shard_map.80.refs_1_.refs_0_), channel_id=1, source_target_pairs={{0,2},{1,3},{2,0},{3,1},{4,6},{5,7},{6,4},{7,5},{8,10},{9,11},{10,... | collective-permute-start | bytes 196616 | tf_op jit(solution)/shard_map/ppermute | solution.py:29
  54.8 0.3 collective-permute-start.20
  55.1 7.0 %collective-permute-done.8.refs_0_.refs_6_ = bf16[2,64,2304]{2,1,0:T(8,128)(2,1)S(1)} collective-permute-done((bf16[2,64,2304]{2,1,0:T(8,128)(2,1)S(1)}, bf16[2,64,2304]{2,1,0:T(8,128)(2,1)S(1)}, u32[]{:S(2)}, u32[]{:S(2)}) %collective-permute-start.8) | collective-permute-done | bytes 589856 | tf_op jit(solution)/shard_map/ppermute | solution.py:407
  62.1 1.0 %shard_map.81.refs_0_ = bf16[2,64,128]{2,1,0:T(8,128)(2,1)S(1)} custom-call(s32[28]{0:T(128)S(1)} %get-tuple-element.14.plan_ref, bf16[8,128,2048]{2,1,0:T(8,128)(2,1)S(1)} %bitcast.6, bf16[2,64,2304]{2,1,0:T(8,128)(2,1)S(1)} %collective-permute-done.8.refs_0_.refs_6_, f32[2,64,128]{2,1,0:T(8,128)S(1)} %shard_map.80.refs_1_.refs_0_), custom_call_target="tpu_custom_call" | custom-call | tf_op jit(solution)/shard_map/pallas_call | solution.py:328
  63.1 0.1 collective-permute-start.15
  63.2 1.5 %collective-permute-start.16 = (bf16[2,64,128]{2,1,0:T(8,128)(2,1)S(1)}, bf16[2,64,128]{2,1,0:T(8,128)(2,1)S(1)}, u32[]{:S(2)}, u32[]{:S(2)}) collective-permute-start(bf16[2,64,128]{2,1,0:T(8,128)(2,1)S(1)} %shard_map.81.refs_0_), channel_id=1, source_target_pairs={{0,2},{1,3},{2,0},{3,1},{4,6},{5,7},{6,4},{7,5},{8,10},{9,11},{10,... | collective-permute-start | bytes 98312 | tf_op jit(solution)/shard_map/ppermute | solution.py:29
  64.7 0.0 collective-permute-done.18.refs_1_
  64.7 0.3 collective-permute-start.17
  65.0 0.0 collective-permute-done.19.refs_2_
  65.0 0.0 collective-permute-done.20.refs_3_
  65.0 1.4 %shard_map.82.refs_7_ = bf16[1024,256]{1,0:T(8,128)(2,1)} custom-call(s32[28]{0:T(128)S(1)} %get-tuple-element.14.plan_ref, f32[2,64,128]{2,1,0:T(8,128)S(1)} %shard_map.80.refs_1_.refs_0_, f32[2,64,128]{2,1,0:T(8,128)S(1)} %collective-permute-done.18.refs_1_, f32[2,64,128]{2,1,0:T(8,128)S(1)} %collective-permute-done.19.refs_2_, ...), custom_call_target="tpu_custom_call", output_to_operand_aliasing={{}: (9, {})} | custom-call | tf_op jit(solution)/shard_map/pallas_call | solution.py:390
  66.5 0.0 collective-permute-done.15.refs_1_
  66.5 0.6 collective-permute-done.16.refs_2_
  67.2 0.9 %collective-permute-done.17.refs_3_ = bf16[2,64,128]{2,1,0:T(8,128)(2,1)S(1)} collective-permute-done((bf16[2,64,128]{2,1,0:T(8,128)(2,1)S(1)}, bf16[2,64,128]{2,1,0:T(8,128)(2,1)S(1)}, u32[]{:S(2)}, u32[]{:S(2)}) %collective-permute-start.17) | collective-permute-done | bytes 32800 | tf_op jit(solution)/shard_map/ppermute | solution.py:29
  68.1 1.4 %shard_map.83 = bf16[1024,256]{1,0:T(8,128)(2,1)} custom-call(s32[28]{0:T(128)S(1)} %get-tuple-element.14.plan_ref, bf16[2,64,128]{2,1,0:T(8,128)(2,1)S(1)} %shard_map.81.refs_0_, bf16[2,64,128]{2,1,0:T(8,128)(2,1)S(1)} %collective-permute-done.15.refs_1_, bf16[2,64,128]{2,1,0:T(8,128)(2,1)S(1)} %collective-permute-done.16.refs_2_, ...), custom_call_target="tpu_custom_call", output_to_operand_aliasing={{}: (8, {})} | custom-call | tf_op jit(solution)/shard_map/pallas_call | solution.py:390
Async XLA Ops:
  0.0 16.1 %collective-permute-start = (s32[1,8]{1,0:T(1,128)}, s32[1,8]{1,0:T(1,128)S(1)}, u32[]{:S(2)}, u32[]{:S(2)}) collective-permute-start(s32[1,8]{1,0:T(1,128)} %refs_0_.1), channel_id=1, source_target_pairs={{0,4},{4,0},{8,12},{12,8},{1,5},{5,1},{9,13},{13,9},{2,6},{6,2},{1... | collective-permute-start | bytes 104 | tf_op jit(solution)/shard_map/ppermute | solution.py:29
  3.0 13.1 %collective-permute-start.1 = (s32[1,8]{1,0:T(1,128)}, s32[1,8]{1,0:T(1,128)S(1)}, u32[]{:S(2)}, u32[]{:S(2)}) collective-permute-start(s32[1,8]{1,0:T(1,128)} %refs_0_.1), channel_id=1, source_target_pairs={{0,8},{4,12},{8,0},{12,4},{1,9},{5,13},{9,1},{13,5},{2,10},{6,14},... | collective-permute-start | bytes 104 | tf_op jit(solution)/shard_map/ppermute | solution.py:29
  5.6 11.1 %collective-permute-start.2 = (s32[1,8]{1,0:T(1,128)}, s32[1,8]{1,0:T(1,128)S(1)}, u32[]{:S(2)}, u32[]{:S(2)}) collective-permute-start(s32[1,8]{1,0:T(1,128)} %refs_0_.1), channel_id=1, source_target_pairs={{0,12},{4,8},{8,4},{12,0},{1,13},{5,9},{9,5},{13,1},{2,14},{6,10},... | collective-permute-start | bytes 104 | tf_op jit(solution)/shard_map/ppermute | solution.py:29
  5.6 11.1 %collective-permute-start.3 = (bf16[4,64,256]{2,1,0:T(8,128)(2,1)}, bf16[4,64,256]{2,1,0:T(8,128)(2,1)S(1)}, u32[]{:S(2)}, u32[]{:S(2)}) collective-permute-start(bf16[4,64,256]{2,1,0:T(8,128)(2,1)} %refs_6_.1), channel_id=1, source_target_pairs={{0,0},{4,8},{8,4},{12,12},{1,1},{5,9},{9,5},{13,13},{2,2},{6,10},{... | collective-permute-start | bytes 393224 | tf_op jit(solution)/shard_map/ppermute | solution.py:407
  7.2 23.8 %collective-permute-start.4 = (bf16[4,64,2048]{2,1,0:T(8,128)(2,1)}, bf16[4,64,2048]{2,1,0:T(8,128)(2,1)S(1)}, u32[]{:S(2)}, u32[]{:S(2)}) collective-permute-start(bf16[4,64,2048]{2,1,0:T(8,128)(2,1)} %bitcast.14), channel_id=1, source_target_pairs={{0,0},{4,8},{8,4},{12,12},{1,1},{5,9},{9,5},{13,13},{2,2},{6,10},{... | collective-permute-start | bytes 3145736 | tf_op jit(solution)/shard_map/ppermute | solution.py:407
  16.1 6.8 %collective-permute-start.7 = (f32[2,256,256]{2,1,0:T(8,128)S(1)}, f32[2,256,256]{2,1,0:T(8,128)S(1)}, u32[]{:S(2)}, u32[]{:S(2)}) collective-permute-start(f32[2,256,256]{2,1,0:T(8,128)S(1)} %get-tuple-element.13.refs_9_), channel_id=1, source_target_pairs={{0,1},{1,0},{2,3},{3,2},{4,5},{5,4},{6,7},{7,6},{8,9},{9,8},{10,11... | collective-permute-start | bytes 1572872 | tf_op jit(solution)/shard_map/ppermute | solution.py:29
  16.2 6.7 %collective-permute-start.5 = (f32[2,384,256]{2,1,0:T(8,128)S(1)}, f32[2,384,256]{2,1,0:T(8,128)S(1)}, u32[]{:S(2)}, u32[]{:S(2)}) collective-permute-start(f32[2,384,256]{2,1,0:T(8,128)S(1)} %get-tuple-element.16), channel_id=1, source_target_pairs={{0,1},{1,0},{2,3},{3,2},{4,5},{5,4},{6,7},{7,6},{8,9},{9,8},{10,11... | collective-permute-start | bytes 2359304 | tf_op jit(solution)/shard_map/ppermute | solution.py:29
  16.7 6.2 %collective-permute-start.6 = (f32[2,384,256]{2,1,0:T(8,128)S(1)}, f32[2,384,256]{2,1,0:T(8,128)S(1)}, u32[]{:S(2)}, u32[]{:S(2)}) collective-permute-start(f32[2,384,256]{2,1,0:T(8,128)S(1)} %get-tuple-element.17), channel_id=1, source_target_pairs={{0,1},{1,0},{2,3},{3,2},{4,5},{5,4},{6,7},{7,6},{8,9},{9,8},{10,11... | collective-permute-start | bytes 2359304 | tf_op jit(solution)/shard_map/ppermute | solution.py:29
  19.5 18.3 %collective-permute-start.10 = (bf16[2,64,2304]{2,1,0:T(8,128)(2,1)S(1)}, bf16[2,64,2304]{2,1,0:T(8,128)(2,1)S(1)}, u32[]{:S(2)}, u32[]{:S(2)}) collective-permute-start(bf16[2,64,2304]{2,1,0:T(8,128)(2,1)S(1)} %get-tuple-element.19), channel_id=1, source_target_pairs={{0,4},{4,0},{8,12},{12,8},{1,5},{5,1},{9,13},{13,9},{2,6},{6,2},{1... | collective-permute-start | bytes 1769480 | tf_op jit(solution)/shard_map/ppermute | solution.py:407
  23.1 24.4 %collective-permute-start.14 = (bf16[1,1024,256]{2,1,0:T(8,128)(2,1)S(1)}, bf16[1,1024,256]{2,1,0:T(8,128)(2,1)S(1)}, u32[]{:S(2)}, u32[]{:S(2)}) collective-permute-start(bf16[1,1024,256]{2,1,0:T(8,128)(2,1)S(1)} %get-tuple-element.20), channel_id=1, source_target_pairs={{0,2},{1,3},{2,0},{3,1},{4,6},{5,7},{6,4},{7,5},{8,10},{9,11},{10,... | collective-permute-start | bytes 1572872 | tf_op jit(solution)/shard_map/ppermute | solution.py:29
  26.3 11.5 %copy-start = (bf16[1024,2048]{1,0:T(8,128)(2,1)S(1)}, bf16[1024,2048]{1,0:T(8,128)(2,1)}, u32[]{:S(2)}) copy-start(bf16[1024,2048]{1,0:T(8,128)(2,1)} %tokens_ref.1) | copy-start | bytes 12582916
  26.3 11.5 %copy-start.1 = (bf16[4,2048,64]{1,2,0:T(8,128)(2,1)S(1)}, bf16[4,2048,64]{1,2,0:T(8,128)(2,1)}, u32[]{:S(2)}) copy-start(bf16[4,2048,64]{1,2,0:T(8,128)(2,1)} %param.9) | copy-start | bytes 3145732
  26.3 25.8 %collective-permute-start.9 = (bf16[2,64,2304]{2,1,0:T(8,128)(2,1)S(1)}, bf16[2,64,2304]{2,1,0:T(8,128)(2,1)S(1)}, u32[]{:S(2)}, u32[]{:S(2)}) collective-permute-start(bf16[2,64,2304]{2,1,0:T(8,128)(2,1)S(1)} %shard_map.76.refs_4_), channel_id=1, source_target_pairs={{0,12},{4,4},{8,8},{12,0},{1,13},{5,5},{9,9},{13,1},{2,14},{6,6},{... | collective-permute-start | bytes 1769480 | tf_op jit(solution)/shard_map/ppermute | solution.py:407
  32.6 14.9 %copy-start.2 = (bf16[4,64,256]{2,1,0:T(8,128)(2,1)S(1)}, bf16[4,64,256]{2,1,0:T(8,128)(2,1)}, u32[]{:S(2)}) copy-start(bf16[4,64,256]{2,1,0:T(8,128)(2,1)} %refs_6_.1) | copy-start | bytes 393220
  32.7 29.4 %collective-permute-start.8 = (bf16[2,64,2304]{2,1,0:T(8,128)(2,1)S(1)}, bf16[2,64,2304]{2,1,0:T(8,128)(2,1)S(1)}, u32[]{:S(2)}, u32[]{:S(2)}) collective-permute-start(bf16[2,64,2304]{2,1,0:T(8,128)(2,1)S(1)} %shard_map.77.refs_2_), channel_id=1, source_target_pairs={{0,8},{4,0},{8,12},{12,4},{1,9},{5,1},{9,13},{13,5},{2,10},{6,2},{... | collective-permute-start | bytes 1769480 | tf_op jit(solution)/shard_map/ppermute | solution.py:407
  39.2 1.6 %collective-permute-start.11 = (f32[4,64,128]{2,1,0:T(8,128)S(1)}, f32[4,64,128]{2,1,0:T(8,128)S(1)}, u32[]{:S(2)}, u32[]{:S(2)}) collective-permute-start(f32[4,64,128]{2,1,0:T(8,128)S(1)} %shard_map.78.refs_0_), channel_id=1, source_target_pairs={{0,1},{1,0},{2,3},{3,2},{4,5},{5,4},{6,7},{7,6},{8,9},{9,8},{10,11... | collective-permute-start | bytes 393224 | tf_op jit(solution)/shard_map/ppermute | solution.py:29
  39.3 6.4 %collective-permute-start.12 = (f32[4,64,128]{2,1,0:T(8,128)S(1)}, f32[4,64,128]{2,1,0:T(8,128)S(1)}, u32[]{:S(2)}, u32[]{:S(2)}) collective-permute-start(f32[4,64,128]{2,1,0:T(8,128)S(1)} %shard_map.78.refs_0_), channel_id=1, source_target_pairs={{0,2},{1,3},{2,0},{3,1},{4,6},{5,7},{6,4},{7,5},{8,10},{9,11},{10,... | collective-permute-start | bytes 393224 | tf_op jit(solution)/shard_map/ppermute | solution.py:29
  40.8 6.7 %collective-permute-start.13 = (f32[4,64,128]{2,1,0:T(8,128)S(1)}, f32[4,64,128]{2,1,0:T(8,128)S(1)}, u32[]{:S(2)}, u32[]{:S(2)}) collective-permute-start(f32[4,64,128]{2,1,0:T(8,128)S(1)} %shard_map.78.refs_0_), channel_id=1, source_target_pairs={{0,3},{1,2},{2,1},{3,0},{4,7},{5,6},{6,5},{7,4},{8,11},{9,10},{10,... | collective-permute-start | bytes 393224 | tf_op jit(solution)/shard_map/ppermute | solution.py:29
  53.2 11.5 %collective-permute-start.18 = (f32[2,64,128]{2,1,0:T(8,128)S(1)}, f32[2,64,128]{2,1,0:T(8,128)S(1)}, u32[]{:S(2)}, u32[]{:S(2)}) collective-permute-start(f32[2,64,128]{2,1,0:T(8,128)S(1)} %shard_map.80.refs_1_.refs_0_), channel_id=1, source_target_pairs={{0,1},{1,0},{2,3},{3,2},{4,5},{5,4},{6,7},{7,6},{8,9},{9,8},{10,11... | collective-permute-start | bytes 196616 | tf_op jit(solution)/shard_map/ppermute | solution.py:29
  53.3 11.8 %collective-permute-start.19 = (f32[2,64,128]{2,1,0:T(8,128)S(1)}, f32[2,64,128]{2,1,0:T(8,128)S(1)}, u32[]{:S(2)}, u32[]{:S(2)}) collective-permute-start(f32[2,64,128]{2,1,0:T(8,128)S(1)} %shard_map.80.refs_1_.refs_0_), channel_id=1, source_target_pairs={{0,2},{1,3},{2,0},{3,1},{4,6},{5,7},{6,4},{7,5},{8,10},{9,11},{10,... | collective-permute-start | bytes 196616 | tf_op jit(solution)/shard_map/ppermute | solution.py:29
  54.8 10.3 %collective-permute-start.20 = (f32[2,64,128]{2,1,0:T(8,128)S(1)}, f32[2,64,128]{2,1,0:T(8,128)S(1)}, u32[]{:S(2)}, u32[]{:S(2)}) collective-permute-start(f32[2,64,128]{2,1,0:T(8,128)S(1)} %shard_map.80.refs_1_.refs_0_), channel_id=1, source_target_pairs={{0,3},{1,2},{2,1},{3,0},{4,7},{5,6},{6,5},{7,4},{8,11},{9,10},{10,... | collective-permute-start | bytes 196616 | tf_op jit(solution)/shard_map/ppermute | solution.py:29
  63.1 3.4 %collective-permute-start.15 = (bf16[2,64,128]{2,1,0:T(8,128)(2,1)S(1)}, bf16[2,64,128]{2,1,0:T(8,128)(2,1)S(1)}, u32[]{:S(2)}, u32[]{:S(2)}) collective-permute-start(bf16[2,64,128]{2,1,0:T(8,128)(2,1)S(1)} %shard_map.81.refs_0_), channel_id=1, source_target_pairs={{0,1},{1,0},{2,3},{3,2},{4,5},{5,4},{6,7},{7,6},{8,9},{9,8},{10,11... | collective-permute-start | bytes 98312 | tf_op jit(solution)/shard_map/ppermute | solution.py:29
  63.2 4.0 %collective-permute-start.16 = (bf16[2,64,128]{2,1,0:T(8,128)(2,1)S(1)}, bf16[2,64,128]{2,1,0:T(8,128)(2,1)S(1)}, u32[]{:S(2)}, u32[]{:S(2)}) collective-permute-start(bf16[2,64,128]{2,1,0:T(8,128)(2,1)S(1)} %shard_map.81.refs_0_), channel_id=1, source_target_pairs={{0,2},{1,3},{2,0},{3,1},{4,6},{5,7},{6,4},{7,5},{8,10},{9,11},{10,... | collective-permute-start | bytes 98312 | tf_op jit(solution)/shard_map/ppermute | solution.py:29
  64.7 3.3 %collective-permute-start.17 = (bf16[2,64,128]{2,1,0:T(8,128)(2,1)S(1)}, bf16[2,64,128]{2,1,0:T(8,128)(2,1)S(1)}, u32[]{:S(2)}, u32[]{:S(2)}) collective-permute-start(bf16[2,64,128]{2,1,0:T(8,128)(2,1)S(1)} %shard_map.81.refs_0_), channel_id=1, source_target_pairs={{0,3},{1,2},{2,1},{3,0},{4,7},{5,6},{6,5},{7,4},{8,11},{9,10},{10,... | collective-permute-start | bytes 98312 | tf_op jit(solution)/shard_map/ppermute | solution.py:29

commit v13 on v12

--- a/solution.py
+++ b/solution.py
@@ -174,12 +174,12 @@
     return blocks, slots
 
 
-def panel_copies(k, slot, down_ref, up_ref, out_ref, sems):
+def panel_copies(slot, down_ref, up_ref, out_ref, sems):
     depth = down_ref.shape[2]
     width = up_ref.shape[2]
     return [
-        pltpu.make_async_copy(down_ref.at[slot], out_ref.at[k, :, pl.ds(0, depth)], sems.at[k, 0]),
-        pltpu.make_async_copy(up_ref.at[slot], out_ref.at[k, :, pl.ds(depth, width)], sems.at[k, 1]),
+        pltpu.make_async_copy(down_ref.at[slot], out_ref.at[:, pl.ds(0, depth)], sems.at[0]),
+        pltpu.make_async_copy(up_ref.at[slot], out_ref.at[:, pl.ds(depth, width)], sems.at[1]),
     ]
 
 
@@ -201,7 +201,7 @@
     near_slots = find(first_ref, holder=here)[1]
     copies = []
     for k, slot in enumerate(near_slots):
-        copies += run_copies(panel_copies(k, slot, down_ref, up_ref, near_ref, sems))
+        copies += run_copies(panel_copies(slot, down_ref, up_ref, near_ref.at[k], sems.at[k]))
     inner = (here == 1) | (here == 2)
     own = find(names_ref, holder=here)
     near = find(names_ref, holder=here ^ 1)
@@ -248,14 +248,15 @@
     )(in_hbm(names), *others, in_hbm(table), in_hbm(live), down, up, *after)
 
 
-def pack_kernel(starts, choose, capacity, plan_ref, *refs):
-    out_ref, sems = refs[-2:]
+def pack_kernel(starts, choose, capacity, outs, plan_ref, *refs):
+    *out_refs, sems = refs[-1 - outs :]
 
     def run(start, down_ref, up_ref):
         copies = []
         for k in range(capacity):
             slot = plan_ref[start + k]
-            copies += run_copies(panel_copies(k, slot, down_ref, up_ref, out_ref, sems))
+            out_ref = out_refs[k * outs // capacity].at[k % (capacity // outs)]
+            copies += run_copies(panel_copies(slot, down_ref, up_ref, out_ref, sems.at[k]))
         for copy in copies:
             copy.wait()
 
@@ -267,15 +268,16 @@
         pl.when(jnp.logical_not(first))(functools.partial(run, starts[1], *refs[2:4]))
 
 
-def pack_panels(plan, choices, choose, capacity, after=(), cost=None):
+def pack_panels(plan, choices, choose, capacity, outs=1, after=(), cost=None):
     sources = [a for _, *pair in choices for a in pair]
     rank, depth = sources[0].shape[1:]
     width = sources[1].shape[2]
     return pl.pallas_call(
-        functools.partial(pack_kernel, [start for start, *_ in choices], choose, capacity),
+        functools.partial(pack_kernel, [start for start, *_ in choices], choose, capacity, outs),
         in_specs=[SMEM] + [ANY] * (len(sources) + len(after)),
-        out_specs=ANY,
-        out_shape=jax.ShapeDtypeStruct((capacity, rank, depth + width), sources[0].dtype),
+        out_specs=[ANY] * outs,
+        out_shape=[jax.ShapeDtypeStruct((capacity // outs, rank, depth + width), sources[0].dtype)]
+        * outs,
         scratch_shapes=[pltpu.SemaphoreType.DMA((capacity, 2))],
         compiler_params=PARAMS,
         cost_estimate=cost or NO_COST,
@@ -416,36 +418,41 @@
         names, others, table, live, *held, capacity, [inner_up, sent[-1]]
     )
 
-    def pack(choices, after, cost=None):
+    def pack(choices, outs, after, cost=None):
         choices = [(row * capacity, *panels) for row, *panels in choices]
-        return pack_panels(plan, choices, choose, capacity, after, cost)
+        return pack_panels(plan, choices, choose, capacity, outs, after, cost)
 
     near = across(near_out, [(0, 1), (1, 0), (2, 3), (3, 2)])
     base = base_sum(sent, kept)
-    outer_out = pack([(TO_OUTER, *held)], [base[0]])
+    (outer_out,) = pack([(TO_OUTER, *held)], 1, [base[0]])
     to_outer = across(outer_out, [(0, 3), (1, 1), (2, 2), (3, 0)])
     late_out = pack(
-        [(FORWARD, inner_down, inner_up), (TO_INNER, *held)], [outer_out], LONG
+        [(FORWARD, inner_down, inner_up), (TO_INNER, *held)], capacity, [outer_out], LONG
     )
-    late = across(late_out, [(0, 2), (1, 0), (2, 3), (3, 1)])
+    late = [across(panel, [(0, 2), (1, 0), (2, 3), (3, 1)]) for panel in late_out]
 
     first = [(0, capacity, [(down, OWN * capacity)]), (capacity, capacity, [(near, None)])]
     first_up = [(0, capacity, [(up, OWN * capacity)]), first[1]]
     middle = [(2 * capacity, capacity, [(inner_down, ACROSS * capacity), (to_outer, None)])]
     middle_up = [(2 * capacity, capacity, [(inner_up, ACROSS * capacity), (to_outer, None)])]
-    last = [(3 * capacity, capacity, [(late, None)])]
 
     def write(number, parts, phases, out, cost=None):
-        live_row = (LIVE + number) * capacity
+        live_row = LIVE * capacity + number
         return combine(plan, live_row, parts, base, phases, choose, out, cost)
 
-    first_parts = exchange(shrink(plan, row_blocks, first, choose, [late_out]))
+    first_parts = exchange(shrink(plan, row_blocks, first, choose, late_out[:1]))
     out = write(0, first_parts, first_up, None, MIDDLE)
-    middle_part = shrink(plan, row_blocks, middle, choose, [in_hbm(out)])
-    middle_parts = exchange(middle_part)
-    last_parts = exchange(shrink(plan, row_blocks, last, choose, [middle_part], jnp.bfloat16))
-    out = write(2, middle_parts, middle_up, out)
-    return write(3, last_parts, last, out)
+    number, phases = 2 * capacity, middle_up
+    part = shrink(plan, row_blocks, middle, choose, [in_hbm(out)])
+    parts = exchange(part)
+    for k in range(capacity):
+        last = [(3 * capacity + k, 1, [(late[k], None)])]
+        kind = jnp.bfloat16 if k == capacity - 1 else jnp.float32
+        part = shrink(plan, row_blocks, last, choose, [part, in_hbm(out)], kind)
+        sums = exchange(part)
+        out = write(number, parts, phases, out)
+        number, parts, phases = 3 * capacity + k, sums, last
+    return write(number, parts, phases, out)
 
 
 def on_any_pool(tokens, weight, row_blocks, down, up, names, table, live, capacity):
@@ -460,7 +467,7 @@
         hit = slots // holder_slots == here
         chosen = hit[None, :] & (jnp.cumsum(hit.astype(jnp.int32))[None, :] == 1 + count[:, None])
         plan = jnp.sum(jnp.where(chosen, (slots % holder_slots)[None, :], 0), axis=1)
-        panels = pack_panels(plan, [(0, down, up)], 0, capacity)
+        (panels,) = pack_panels(plan, [(0, down, up)], 0, capacity)
         pairs = [(i, (i + distance) % pool_size) for i in range(pool_size)]
         arrived.append(lax.ppermute(panels, "pool", pairs) if distance else panels)
     arrived = jnp.concatenate(arrived)

time: 69.9 us -> 71.6 us (1.024)
  Pallas kernels: 21.1 us -> 23 us
    ppermute x5 -> x6, starting transfers between devices: 16.6 us -> 14.7 us  [across(): return lax.ppermute(value, 'pool', pairs)]
    ppermute x16 -> x19, starting transfers between devices: 14.3 us -> 16 us  [swap(): return lax.ppermute(value, axis, pairs)]
    pallas_call x3 -> x4, Pallas kernels: 4.38 us -> 5.72 us  [combine(): pl.pallas_call(functools.partial(combine_kernel, shapes, choose, len(part...]
    pallas_call x3 -> x4, Pallas kernels: 3.42 us -> 4.08 us  [shrink(): pl.pallas_call(functools.partial(shrink_kernel, shapes, choose), in_specs...]
    ppermute x5 -> x6, waiting for transfers between devices: 10.1 us -> 9.73 us  [across(): return lax.ppermute(value, 'pool', pairs)]
    ppermute x16 -> x19, waiting for transfers between devices: 7.27 us -> 7.6 us  [swap(): return lax.ppermute(value, axis, pairs)]
  transfers between devices with their start and end apart: 21 -> 25, of which waited for: 6 -> 8; matrix products, arithmetic and copies ran while one was open for 0% -> 0% of each run, Pallas kernels for 28% -> 30%
where the time goes in v13:
time: 71.6 us; the launch traced here: 71.3 us
  starting transfers between devices  30.7 us (43%)
  Pallas kernels  23 us (32%)
  waiting for transfers between devices  17.3 us (24%)
    ppermute x19, starting transfers between devices, swap(): return lax.ppermute(value, axis, pairs)  16 us
    ppermute x6, starting transfers between devices, across(): return lax.ppermute(value, 'pool', pairs)  14.7 us
    ppermute x6, waiting for transfers between devices, across(): return lax.ppermute(value, 'pool', pairs)  9.73 us
    ppermute x19, waiting for transfers between devices, swap(): return lax.ppermute(value, axis, pairs)  7.6 us
    pallas_call x1, Pallas kernels, base_chunks(): pl.pallas_call(functools.partial(base_kernel, order), in_specs=[ANY] * 2,...  7.03 us
    pallas_call x4, Pallas kernels, combine(): pl.pallas_call(functools.partial(combine_kernel, shapes, choose, len(part...  5.72 us
    pallas_call x4, Pallas kernels, shrink(): pl.pallas_call(functools.partial(shrink_kernel, shapes, choose), in_specs...  4.08 us
    pallas_call x2, Pallas kernels, pack_panels(): pl.pallas_call(functools.partial(pack_kernel, [start for start, *_ in cho...  3.27 us
  transfers between devices with their start and end apart: 25, of which 8 were waited for; matrix products, arithmetic and copies ran while one was open for 0% of the time, Pallas kernels for 30%

profile of v13, /device:TPU:0, one launch (start us, length us, event | category | flops | bytes accessed | tf_op | source)
XLA Modules:
  0.0 71.3 jit_solution(17540836510564095392)
XLA Ops:
  0.0 3.0 %collective-permute-start = (s32[1,8]{1,0:T(1,128)}, s32[1,8]{1,0:T(1,128)S(1)}, u32[]{:S(2)}, u32[]{:S(2)}) collective-permute-start(s32[1,8]{1,0:T(1,128)} %refs_0_.1), channel_id=1, source_target_pairs={{0,4},{4,0},{8,12},{12,8},{1,5},{5,1},{9,13},{13,9},{2,6},{6,2},{1... | collective-permute-start | bytes 104 | tf_op jit(solution)/shard_map/ppermute | solution.py:29
  3.0 2.6 %collective-permute-start.1 = (s32[1,8]{1,0:T(1,128)}, s32[1,8]{1,0:T(1,128)S(1)}, u32[]{:S(2)}, u32[]{:S(2)}) collective-permute-start(s32[1,8]{1,0:T(1,128)} %refs_0_.1), channel_id=1, source_target_pairs={{0,8},{4,12},{8,0},{12,4},{1,9},{5,13},{9,1},{13,5},{2,10},{6,14},... | collective-permute-start | bytes 104 | tf_op jit(solution)/shard_map/ppermute | solution.py:29
  5.6 0.0 collective-permute-start.2
  5.6 1.6 %collective-permute-start.3 = (bf16[4,64,256]{2,1,0:T(8,128)(2,1)}, bf16[4,64,256]{2,1,0:T(8,128)(2,1)S(1)}, u32[]{:S(2)}, u32[]{:S(2)}) collective-permute-start(bf16[4,64,256]{2,1,0:T(8,128)(2,1)} %refs_6_.1), channel_id=1, source_target_pairs={{0,0},{4,8},{8,4},{12,12},{1,1},{5,9},{9,5},{13,13},{2,2},{6,10},{... | collective-permute-start | bytes 393224 | tf_op jit(solution)/shard_map/ppermute | solution.py:409
  7.2 1.9 %collective-permute-start.4 = (bf16[4,64,2048]{2,1,0:T(8,128)(2,1)}, bf16[4,64,2048]{2,1,0:T(8,128)(2,1)S(1)}, u32[]{:S(2)}, u32[]{:S(2)}) collective-permute-start(bf16[4,64,2048]{2,1,0:T(8,128)(2,1)} %bitcast.17), channel_id=1, source_target_pairs={{0,0},{4,8},{8,4},{12,12},{1,1},{5,9},{9,5},{13,13},{2,2},{6,10},{... | collective-permute-start | bytes 3145736 | tf_op jit(solution)/shard_map/ppermute | solution.py:409
  9.0 7.0 %shard_map.73 = (f32[2,384,256]{2,1,0:T(8,128)S(1)}, f32[2,384,256]{2,1,0:T(8,128)S(1)}, f32[2,256,256]{2,1,0:T(8,128)S(1)}, f32[2,1024,256]{2,1,0:T(8,128)S(1)}) custom-call(bf16[1024,2048]{1,0:T(8,128)(2,1)} %tokens_ref.1, bf16[2048,1024]{1,0:T(8,128)(2,1)} %weight_ref.1), custom_call_target="tpu_custom_call" | custom-call | flops 4000000000 | tf_op jit(solution)/shard_map/pallas_call | solution.py:99
  16.1 0.0 collective-permute-done.refs_1_
  16.1 0.1 collective-permute-start.7
  16.2 0.0 collective-permute-done.1.refs_2_
  16.2 0.5 collective-permute-start.5
  16.7 0.0 collective-permute-done.2.refs_3_
  16.7 0.1 collective-permute-start.6
  16.8 0.0 collective-permute-done.3.refs_8_.refs_1_.refs_6_
  16.8 2.7 %shard_map.74 = (bf16[2,64,2304]{2,1,0:T(8,128)(2,1)S(1)}, s32[28]{0:T(128)S(1)}) custom-call(s32[1,8]{1,0:T(1,128)} %refs_0_.1, s32[1,8]{1,0:T(1,128)S(1)} %collective-permute-done.refs_1_, s32[1,8]{1,0:T(1,128)S(1)} %collective-permute-done.1.refs_2_, s32[1,8]{1,0:T(1,128)S(1)} %collective-permute-done.2.refs_3_, s32[16]{0:T(128)} %refs_4_.1, ...), custom_call_target="tpu_custom_call" | custom-call | flops 10000000000 | tf_op jit(solution)/shard_map/pallas_call | solution.py:235
  19.5 3.4 %collective-permute-start.11 = (bf16[2,64,2304]{2,1,0:T(8,128)(2,1)S(1)}, bf16[2,64,2304]{2,1,0:T(8,128)(2,1)S(1)}, u32[]{:S(2)}, u32[]{:S(2)}) collective-permute-start(bf16[2,64,2304]{2,1,0:T(8,128)(2,1)S(1)} %get-tuple-element.23), channel_id=1, source_target_pairs={{0,4},{4,0},{8,12},{12,8},{1,5},{5,1},{9,13},{13,9},{2,6},{6,2},{1... | collective-permute-start | bytes 1769480 | tf_op jit(solution)/shard_map/ppermute | solution.py:409
  22.9 0.0 collective-permute-done.7.refs_2_
  22.9 0.0 collective-permute-done.5.refs_0_
  22.9 0.2 shard_map.75
  23.1 1.5 %collective-permute-start.15 = (bf16[1,1024,256]{2,1,0:T(8,128)(2,1)S(1)}, bf16[1,1024,256]{2,1,0:T(8,128)(2,1)S(1)}, u32[]{:S(2)}, u32[]{:S(2)}) collective-permute-start(bf16[1,1024,256]{2,1,0:T(8,128)(2,1)S(1)} %get-tuple-element.24), channel_id=1, source_target_pairs={{0,2},{1,3},{2,0},{3,1},{4,6},{5,7},{6,4},{7,5},{8,10},{9,11},{10,... | collective-permute-start | bytes 1572872 | tf_op jit(solution)/shard_map/ppermute | solution.py:29
  24.7 1.6 %shard_map.76.refs_4_ = bf16[2,64,2304]{2,1,0:T(8,128)(2,1)S(1)} custom-call(s32[28]{0:T(128)S(1)} %get-tuple-element.16.plan_ref, bf16[4,64,2048]{2,1,0:T(8,128)(2,1)} %bitcast.19, bf16[4,64,256]{2,1,0:T(8,128)(2,1)} %refs_6_.1, f32[1024,256]{1,0:T(8,128)S(1)} %bitcast.8), custom_call_target="tpu_custom_call" | custom-call | tf_op jit(solution)/shard_map/pallas_call | solution.py:275
  26.3 0.0 copy-start
  26.3 0.0 copy-start.1
  26.3 4.7 %collective-permute-start.10 = (bf16[2,64,2304]{2,1,0:T(8,128)(2,1)S(1)}, bf16[2,64,2304]{2,1,0:T(8,128)(2,1)S(1)}, u32[]{:S(2)}, u32[]{:S(2)}) collective-permute-start(bf16[2,64,2304]{2,1,0:T(8,128)(2,1)S(1)} %shard_map.76.refs_4_), channel_id=1, source_target_pairs={{0,12},{4,4},{8,8},{12,0},{1,13},{5,5},{9,9},{13,1},{2,14},{6,6},{... | collective-permute-start | bytes 1769480 | tf_op jit(solution)/shard_map/ppermute | solution.py:409
  31.0 0.0 collective-permute-done.4.refs_0_
  31.0 1.6 %shard_map.77 = (bf16[1,64,2304]{2,1,0:T(8,128)(2,1)S(1)}, bf16[1,64,2304]{2,1,0:T(8,128)(2,1)S(1)}) custom-call(s32[28]{0:T(128)S(1)} %get-tuple-element.16.plan_ref, bf16[4,64,2048]{2,1,0:T(8,128)(2,1)S(1)} %collective-permute-done.4.refs_0_, bf16[4,64,256]{2,1,0:T(8,128)(2,1)S(1)} %collective-permute-done.3.refs_8_.refs_1_.refs_6_, ...), custom_call_target="tpu_custom_call" | custom-call | flops 6000000000 | tf_op jit(solution)/shard_map/pallas_call | solution.py:275
  32.7 0.0 copy-start.2
  32.7 4.1 %collective-permute-done.11.refs_1_.refs_7_ = bf16[2,64,2304]{2,1,0:T(8,128)(2,1)S(1)} collective-permute-done((bf16[2,64,2304]{2,1,0:T(8,128)(2,1)S(1)}, bf16[2,64,2304]{2,1,0:T(8,128)(2,1)S(1)}, u32[]{:S(2)}, u32[]{:S(2)}) %collective-permute-start.11) | collective-permute-done | bytes 589856 | tf_op jit(solution)/shard_map/ppermute | solution.py:409
  36.8 1.4 %shard_map.78.refs_0_ = f32[4,64,128]{2,1,0:T(8,128)S(1)} custom-call(s32[28]{0:T(128)S(1)} %get-tuple-element.16.plan_ref, bf16[8,128,2048]{2,1,0:T(8,128)(2,1)S(1)} %bitcast.4, bf16[4,64,2048]{2,1,0:T(8,128)(2,1)S(1)} %bitcast.21, bf16[2,64,2304]{2,1,0:T(8,128)(2,1)S(1)} %collective-permute-done.11.refs_1_.refs_7_, ...), custom_call_target="tpu_custom_call" | custom-call | tf_op jit(solution)/shard_map/pallas_call | solution.py:330
  38.2 0.1 collective-permute-start.12
  38.3 1.5 %collective-permute-start.13 = (f32[4,64,128]{2,1,0:T(8,128)S(1)}, f32[4,64,128]{2,1,0:T(8,128)S(1)}, u32[]{:S(2)}, u32[]{:S(2)}) collective-permute-start(f32[4,64,128]{2,1,0:T(8,128)S(1)} %shard_map.78.refs_0_), channel_id=1, source_target_pairs={{0,2},{1,3},{2,0},{3,1},{4,6},{5,7},{6,4},{7,5},{8,10},{9,11},{10,... | collective-permute-start | bytes 393224 | tf_op jit(solution)/shard_map/ppermute | solution.py:29
  39.8 3.2 %collective-permute-start.9 = (bf16[1,64,2304]{2,1,0:T(8,128)(2,1)S(1)}, bf16[1,64,2304]{2,1,0:T(8,128)(2,1)S(1)}, u32[]{:S(2)}, u32[]{:S(2)}) collective-permute-start(bf16[1,64,2304]{2,1,0:T(8,128)(2,1)S(1)} %get-tuple-element.22.refs_2_), channel_id=1, source_target_pairs={{0,8},{4,0},{8,12},{12,4},{1,9},{5,1},{9,13},{13,5},{2,10},{6,2},{... | collective-permute-start | bytes 884744 | tf_op jit(solution)/shard_map/ppermute | solution.py:409
  43.0 0.0 collective-permute-done.12.refs_1_
  43.0 0.0 collective-permute-start.8
  43.1 1.1 %collective-permute-done.13.refs_2_ = f32[4,64,128]{2,1,0:T(8,128)S(1)} collective-permute-done((f32[4,64,128]{2,1,0:T(8,128)S(1)}, f32[4,64,128]{2,1,0:T(8,128)S(1)}, u32[]{:S(2)}, u32[]{:S(2)}) %collective-permute-start.13) | collective-permute-done | bytes 131104 | tf_op jit(solution)/shard_map/ppermute | solution.py:29
  44.2 0.7 %collective-permute-start.14 = (f32[4,64,128]{2,1,0:T(8,128)S(1)}, f32[4,64,128]{2,1,0:T(8,128)S(1)}, u32[]{:S(2)}, u32[]{:S(2)}) collective-permute-start(f32[4,64,128]{2,1,0:T(8,128)S(1)} %shard_map.78.refs_0_), channel_id=1, source_target_pairs={{0,3},{1,2},{2,1},{3,0},{4,7},{5,6},{6,5},{7,4},{8,11},{9,10},{10,... | collective-permute-start | bytes 393224 | tf_op jit(solution)/shard_map/ppermute | solution.py:29
  44.9 5.0 %collective-permute-done.14.refs_3_ = f32[4,64,128]{2,1,0:T(8,128)S(1)} collective-permute-done((f32[4,64,128]{2,1,0:T(8,128)S(1)}, f32[4,64,128]{2,1,0:T(8,128)S(1)}, u32[]{:S(2)}, u32[]{:S(2)}) %collective-permute-start.14) | collective-permute-done | bytes 131104 | tf_op jit(solution)/shard_map/ppermute | solution.py:29
  49.9 0.0 collective-permute-done.15
  49.9 1.5 %shard_map.79.refs_2_.refs_8_ = bf16[1024,256]{1,0:T(8,128)(2,1)} custom-call(s32[28]{0:T(128)S(1)} %get-tuple-element.16.plan_ref, f32[4,64,128]{2,1,0:T(8,128)S(1)} %shard_map.78.refs_0_, f32[4,64,128]{2,1,0:T(8,128)S(1)} %collective-permute-done.12.refs_1_, f32[4,64,128]{2,1,0:T(8,128)S(1)} %collective-permute-done.13.refs_2_, ...), custom_call_target="tpu_custom_call" | custom-call | tf_op jit(solution)/shard_map/pallas_call | solution.py:392
  51.4 0.7 collective-permute-done.10.refs_1_.refs_7_
  52.1 1.0 %shard_map.80.refs_1_.refs_0_ = f32[2,64,128]{2,1,0:T(8,128)S(1)} custom-call(s32[28]{0:T(128)S(1)} %get-tuple-element.16.plan_ref, bf16[8,128,2048]{2,1,0:T(8,128)(2,1)S(1)} %bitcast.5, bf16[4,64,2048]{2,1,0:T(8,128)(2,1)S(1)} %collective-permute-done.4.refs_0_, bf16[2,64,2304]{2,1,0:T(8,128)(2,1)S(1)} %collective-permute-done.10.refs_1_.refs_7_, ...), custom_call_target="tpu_custom_call" | custom-call | tf_op jit(solution)/shard_map/pallas_call | solution.py:330
  53.2 0.1 collective-permute-start.16
  53.3 1.5 %collective-permute-start.17 = (f32[2,64,128]{2,1,0:T(8,128)S(1)}, f32[2,64,128]{2,1,0:T(8,128)S(1)}, u32[]{:S(2)}, u32[]{:S(2)}) collective-permute-start(f32[2,64,128]{2,1,0:T(8,128)S(1)} %shard_map.80.refs_1_.refs_0_), channel_id=1, source_target_pairs={{0,2},{1,3},{2,0},{3,1},{4,6},{5,7},{6,4},{7,5},{8,10},{9,11},{10,... | collective-permute-start | bytes 196616 | tf_op jit(solution)/shard_map/ppermute | solution.py:29
  54.8 0.3 collective-permute-start.18
  55.1 2.9 %collective-permute-done.9.refs_0_.refs_6_ = bf16[1,64,2304]{2,1,0:T(8,128)(2,1)S(1)} collective-permute-done((bf16[1,64,2304]{2,1,0:T(8,128)(2,1)S(1)}, bf16[1,64,2304]{2,1,0:T(8,128)(2,1)S(1)}, u32[]{:S(2)}, u32[]{:S(2)}) %collective-permute-start.9) | collective-permute-done | bytes 294944 | tf_op jit(solution)/shard_map/ppermute | solution.py:409
  58.0 0.8 %shard_map.81.refs_1_.refs_0_ = f32[1,64,128]{2,1,0:T(8,128)S(1)} custom-call(s32[28]{0:T(128)S(1)} %get-tuple-element.16.plan_ref, bf16[8,128,2048]{2,1,0:T(8,128)(2,1)S(1)} %bitcast.6, bf16[1,64,2304]{2,1,0:T(8,128)(2,1)S(1)} %collective-permute-done.9.refs_0_.refs_6_, f32[2,64,128]{2,1,0:T(8,128)S(1)} %shard_map.80.refs_1_.refs_0_, ...), custom_call_target="tpu_custom_call" | custom-call | tf_op jit(solution)/shard_map/pallas_call | solution.py:330
  58.8 0.1 collective-permute-start.22
  58.9 0.0 collective-permute-done.16.refs_1_
  58.9 1.5 %collective-permute-start.23 = (f32[1,64,128]{2,1,0:T(8,128)S(1)}, f32[1,64,128]{2,1,0:T(8,128)S(1)}, u32[]{:S(2)}, u32[]{:S(2)}) collective-permute-start(f32[1,64,128]{2,1,0:T(8,128)S(1)} %shard_map.81.refs_1_.refs_0_), channel_id=1, source_target_pairs={{0,2},{1,3},{2,0},{3,1},{4,6},{5,7},{6,4},{7,5},{8,10},{9,11},{10,... | collective-permute-start | bytes 98312 | tf_op jit(solution)/shard_map/ppermute | solution.py:29
  60.5 0.3 collective-permute-start.24
  60.8 0.0 collective-permute-done.18.refs_3_
  60.8 1.4 %shard_map.82.refs_2_.refs_7_ = bf16[1024,256]{1,0:T(8,128)(2,1)} custom-call(s32[28]{0:T(128)S(1)} %get-tuple-element.16.plan_ref, f32[2,64,128]{2,1,0:T(8,128)S(1)} %shard_map.80.refs_1_.refs_0_, f32[2,64,128]{2,1,0:T(8,128)S(1)} %collective-permute-done.16.refs_1_, ...), custom_call_target="tpu_custom_call", output_to_operand_aliasing={{}: (9, {})} | custom-call | tf_op jit(solution)/shard_map/pallas_call | solution.py:392
  62.3 2.0 %collective-permute-done.8.refs_0_.refs_6_ = bf16[1,64,2304]{2,1,0:T(8,128)(2,1)S(1)} collective-permute-done((bf16[1,64,2304]{2,1,0:T(8,128)(2,1)S(1)}, bf16[1,64,2304]{2,1,0:T(8,128)(2,1)S(1)}, u32[]{:S(2)}, u32[]{:S(2)}) %collective-permute-start.8) | collective-permute-done | bytes 294944 | tf_op jit(solution)/shard_map/ppermute | solution.py:409
  64.3 0.8 %shard_map.83.refs_0_ = bf16[1,64,128]{2,1,0:T(8,128)(2,1)S(1)} custom-call(s32[28]{0:T(128)S(1)} %get-tuple-element.16.plan_ref, bf16[8,128,2048]{2,1,0:T(8,128)(2,1)S(1)} %bitcast.7, bf16[1,64,2304]{2,1,0:T(8,128)(2,1)S(1)} %collective-permute-done.8.refs_0_.refs_6_, f32[1,64,128]{2,1,0:T(8,128)S(1)} %shard_map.81.refs_1_.refs_0_, ...), custom_call_target="tpu_custom_call" | custom-call | tf_op jit(solution)/shard_map/pallas_call | solution.py:330
  65.1 0.1 collective-permute-start.19
  65.3 1.5 %collective-permute-start.20 = (bf16[1,64,128]{2,1,0:T(8,128)(2,1)S(1)}, bf16[1,64,128]{2,1,0:T(8,128)(2,1)S(1)}, u32[]{:S(2)}, u32[]{:S(2)}) collective-permute-start(bf16[1,64,128]{2,1,0:T(8,128)(2,1)S(1)} %shard_map.83.refs_0_), channel_id=1, source_target_pairs={{0,2},{1,3},{2,0},{3,1},{4,6},{5,7},{6,4},{7,5},{8,10},{9,11},{10,... | collective-permute-start | bytes 49160 | tf_op jit(solution)/shard_map/ppermute | solution.py:29
  66.7 0.0 collective-permute-done.22.refs_1_
  66.7 0.3 collective-permute-start.21
  67.1 0.0 collective-permute-done.23.refs_2_
  67.1 0.0 collective-permute-done.24.refs_3_
  67.1 1.4 %shard_map.84.refs_7_ = bf16[1024,256]{1,0:T(8,128)(2,1)} custom-call(s32[28]{0:T(128)S(1)} %get-tuple-element.16.plan_ref, f32[1,64,128]{2,1,0:T(8,128)S(1)} %shard_map.81.refs_1_.refs_0_, f32[1,64,128]{2,1,0:T(8,128)S(1)} %collective-permute-done.22.refs_1_, f32[1,64,128]{2,1,0:T(8,128)S(1)} %collective-permute-done.23.refs_2_, ...), custom_call_target="tpu_custom_call", output_to_operand_aliasing={{}: (8, {})} | custom-call | tf_op jit(solution)/shard_map/pallas_call | solution.py:392
  68.5 0.0 collective-permute-done.19.refs_1_
  68.5 0.5 collective-permute-done.20.refs_2_
  69.0 0.9 %collective-permute-done.21.refs_3_ = bf16[1,64,128]{2,1,0:T(8,128)(2,1)S(1)} collective-permute-done((bf16[1,64,128]{2,1,0:T(8,128)(2,1)S(1)}, bf16[1,64,128]{2,1,0:T(8,128)(2,1)S(1)}, u32[]{:S(2)}, u32[]{:S(2)}) %collective-permute-start.21) | collective-permute-done | bytes 16416 | tf_op jit(solution)/shard_map/ppermute | solution.py:29
  69.9 1.4 %shard_map.85 = bf16[1024,256]{1,0:T(8,128)(2,1)} custom-call(s32[28]{0:T(128)S(1)} %get-tuple-element.16.plan_ref, bf16[1,64,128]{2,1,0:T(8,128)(2,1)S(1)} %shard_map.83.refs_0_, bf16[1,64,128]{2,1,0:T(8,128)(2,1)S(1)} %collective-permute-done.19.refs_1_, bf16[1,64,128]{2,1,0:T(8,128)(2,1)S(1)} %collective-permute-done.20.refs_2_, ...), custom_call_target="tpu_custom_call", output_to_operand_aliasing={{}: (8, {})} | custom-call | tf_op jit(solution)/shard_map/pallas_call | solution.py:392
  (5 shorter events, 0.0 us)
Async XLA Ops:
  0.0 16.1 %collective-permute-start = (s32[1,8]{1,0:T(1,128)}, s32[1,8]{1,0:T(1,128)S(1)}, u32[]{:S(2)}, u32[]{:S(2)}) collective-permute-start(s32[1,8]{1,0:T(1,128)} %refs_0_.1), channel_id=1, source_target_pairs={{0,4},{4,0},{8,12},{12,8},{1,5},{5,1},{9,13},{13,9},{2,6},{6,2},{1... | collective-permute-start | bytes 104 | tf_op jit(solution)/shard_map/ppermute | solution.py:29
  3.0 13.1 %collective-permute-start.1 = (s32[1,8]{1,0:T(1,128)}, s32[1,8]{1,0:T(1,128)S(1)}, u32[]{:S(2)}, u32[]{:S(2)}) collective-permute-start(s32[1,8]{1,0:T(1,128)} %refs_0_.1), channel_id=1, source_target_pairs={{0,8},{4,12},{8,0},{12,4},{1,9},{5,13},{9,1},{13,5},{2,10},{6,14},... | collective-permute-start | bytes 104 | tf_op jit(solution)/shard_map/ppermute | solution.py:29
  5.6 11.1 %collective-permute-start.2 = (s32[1,8]{1,0:T(1,128)}, s32[1,8]{1,0:T(1,128)S(1)}, u32[]{:S(2)}, u32[]{:S(2)}) collective-permute-start(s32[1,8]{1,0:T(1,128)} %refs_0_.1), channel_id=1, source_target_pairs={{0,12},{4,8},{8,4},{12,0},{1,13},{5,9},{9,5},{13,1},{2,14},{6,10},... | collective-permute-start | bytes 104 | tf_op jit(solution)/shard_map/ppermute | solution.py:29
  5.6 11.1 %collective-permute-start.3 = (bf16[4,64,256]{2,1,0:T(8,128)(2,1)}, bf16[4,64,256]{2,1,0:T(8,128)(2,1)S(1)}, u32[]{:S(2)}, u32[]{:S(2)}) collective-permute-start(bf16[4,64,256]{2,1,0:T(8,128)(2,1)} %refs_6_.1), channel_id=1, source_target_pairs={{0,0},{4,8},{8,4},{12,12},{1,1},{5,9},{9,5},{13,13},{2,2},{6,10},{... | collective-permute-start | bytes 393224 | tf_op jit(solution)/shard_map/ppermute | solution.py:409
  7.2 23.8 %collective-permute-start.4 = (bf16[4,64,2048]{2,1,0:T(8,128)(2,1)}, bf16[4,64,2048]{2,1,0:T(8,128)(2,1)S(1)}, u32[]{:S(2)}, u32[]{:S(2)}) collective-permute-start(bf16[4,64,2048]{2,1,0:T(8,128)(2,1)} %bitcast.17), channel_id=1, source_target_pairs={{0,0},{4,8},{8,4},{12,12},{1,1},{5,9},{9,5},{13,13},{2,2},{6,10},{... | collective-permute-start | bytes 3145736 | tf_op jit(solution)/shard_map/ppermute | solution.py:409
  16.1 6.8 %collective-permute-start.7 = (f32[2,256,256]{2,1,0:T(8,128)S(1)}, f32[2,256,256]{2,1,0:T(8,128)S(1)}, u32[]{:S(2)}, u32[]{:S(2)}) collective-permute-start(f32[2,256,256]{2,1,0:T(8,128)S(1)} %get-tuple-element.15.refs_9_), channel_id=1, source_target_pairs={{0,1},{1,0},{2,3},{3,2},{4,5},{5,4},{6,7},{7,6},{8,9},{9,8},{10,11... | collective-permute-start | bytes 1572872 | tf_op jit(solution)/shard_map/ppermute | solution.py:29
  16.2 6.7 %collective-permute-start.5 = (f32[2,384,256]{2,1,0:T(8,128)S(1)}, f32[2,384,256]{2,1,0:T(8,128)S(1)}, u32[]{:S(2)}, u32[]{:S(2)}) collective-permute-start(f32[2,384,256]{2,1,0:T(8,128)S(1)} %get-tuple-element.18), channel_id=1, source_target_pairs={{0,1},{1,0},{2,3},{3,2},{4,5},{5,4},{6,7},{7,6},{8,9},{9,8},{10,11... | collective-permute-start | bytes 2359304 | tf_op jit(solution)/shard_map/ppermute | solution.py:29
  16.7 6.2 %collective-permute-start.6 = (f32[2,384,256]{2,1,0:T(8,128)S(1)}, f32[2,384,256]{2,1,0:T(8,128)S(1)}, u32[]{:S(2)}, u32[]{:S(2)}) collective-permute-start(f32[2,384,256]{2,1,0:T(8,128)S(1)} %get-tuple-element.19), channel_id=1, source_target_pairs={{0,1},{1,0},{2,3},{3,2},{4,5},{5,4},{6,7},{7,6},{8,9},{9,8},{10,11... | collective-permute-start | bytes 2359304 | tf_op jit(solution)/shard_map/ppermute | solution.py:29
  19.5 17.3 %collective-permute-start.11 = (bf16[2,64,2304]{2,1,0:T(8,128)(2,1)S(1)}, bf16[2,64,2304]{2,1,0:T(8,128)(2,1)S(1)}, u32[]{:S(2)}, u32[]{:S(2)}) collective-permute-start(bf16[2,64,2304]{2,1,0:T(8,128)(2,1)S(1)} %get-tuple-element.23), channel_id=1, source_target_pairs={{0,4},{4,0},{8,12},{12,8},{1,5},{5,1},{9,13},{13,9},{2,6},{6,2},{1... | collective-permute-start | bytes 1769480 | tf_op jit(solution)/shard_map/ppermute | solution.py:409
  23.1 26.8 %collective-permute-start.15 = (bf16[1,1024,256]{2,1,0:T(8,128)(2,1)S(1)}, bf16[1,1024,256]{2,1,0:T(8,128)(2,1)S(1)}, u32[]{:S(2)}, u32[]{:S(2)}) collective-permute-start(bf16[1,1024,256]{2,1,0:T(8,128)(2,1)S(1)} %get-tuple-element.24), channel_id=1, source_target_pairs={{0,2},{1,3},{2,0},{3,1},{4,6},{5,7},{6,4},{7,5},{8,10},{9,11},{10,... | collective-permute-start | bytes 1572872 | tf_op jit(solution)/shard_map/ppermute | solution.py:29
  26.3 10.5 %copy-start = (bf16[1024,2048]{1,0:T(8,128)(2,1)S(1)}, bf16[1024,2048]{1,0:T(8,128)(2,1)}, u32[]{:S(2)}) copy-start(bf16[1024,2048]{1,0:T(8,128)(2,1)} %tokens_ref.1) | copy-start | bytes 12582916
  26.3 10.5 %copy-start.1 = (bf16[4,2048,64]{1,2,0:T(8,128)(2,1)S(1)}, bf16[4,2048,64]{1,2,0:T(8,128)(2,1)}, u32[]{:S(2)}) copy-start(bf16[4,2048,64]{1,2,0:T(8,128)(2,1)} %param.9) | copy-start | bytes 3145732
  26.3 25.8 %collective-permute-start.10 = (bf16[2,64,2304]{2,1,0:T(8,128)(2,1)S(1)}, bf16[2,64,2304]{2,1,0:T(8,128)(2,1)S(1)}, u32[]{:S(2)}, u32[]{:S(2)}) collective-permute-start(bf16[2,64,2304]{2,1,0:T(8,128)(2,1)S(1)} %shard_map.76.refs_4_), channel_id=1, source_target_pairs={{0,12},{4,4},{8,8},{12,0},{1,13},{5,5},{9,9},{13,1},{2,14},{6,6},{... | collective-permute-start | bytes 1769480 | tf_op jit(solution)/shard_map/ppermute | solution.py:409
  32.7 17.3 %copy-start.2 = (bf16[4,64,256]{2,1,0:T(8,128)(2,1)S(1)}, bf16[4,64,256]{2,1,0:T(8,128)(2,1)}, u32[]{:S(2)}) copy-start(bf16[4,64,256]{2,1,0:T(8,128)(2,1)} %refs_6_.1) | copy-start | bytes 393220
  38.2 4.8 %collective-permute-start.12 = (f32[4,64,128]{2,1,0:T(8,128)S(1)}, f32[4,64,128]{2,1,0:T(8,128)S(1)}, u32[]{:S(2)}, u32[]{:S(2)}) collective-permute-start(f32[4,64,128]{2,1,0:T(8,128)S(1)} %shard_map.78.refs_0_), channel_id=1, source_target_pairs={{0,1},{1,0},{2,3},{3,2},{4,5},{5,4},{6,7},{7,6},{8,9},{9,8},{10,11... | collective-permute-start | bytes 393224 | tf_op jit(solution)/shard_map/ppermute | solution.py:29
  38.3 5.9 %collective-permute-start.13 = (f32[4,64,128]{2,1,0:T(8,128)S(1)}, f32[4,64,128]{2,1,0:T(8,128)S(1)}, u32[]{:S(2)}, u32[]{:S(2)}) collective-permute-start(f32[4,64,128]{2,1,0:T(8,128)S(1)} %shard_map.78.refs_0_), channel_id=1, source_target_pairs={{0,2},{1,3},{2,0},{3,1},{4,6},{5,7},{6,4},{7,5},{8,10},{9,11},{10,... | collective-permute-start | bytes 393224 | tf_op jit(solution)/shard_map/ppermute | solution.py:29
  39.8 18.2 %collective-permute-start.9 = (bf16[1,64,2304]{2,1,0:T(8,128)(2,1)S(1)}, bf16[1,64,2304]{2,1,0:T(8,128)(2,1)S(1)}, u32[]{:S(2)}, u32[]{:S(2)}) collective-permute-start(bf16[1,64,2304]{2,1,0:T(8,128)(2,1)S(1)} %get-tuple-element.22.refs_2_), channel_id=1, source_target_pairs={{0,8},{4,0},{8,12},{12,4},{1,9},{5,1},{9,13},{13,5},{2,10},{6,2},{... | collective-permute-start | bytes 884744 | tf_op jit(solution)/shard_map/ppermute | solution.py:409
  43.0 21.2 %collective-permute-start.8 = (bf16[1,64,2304]{2,1,0:T(8,128)(2,1)S(1)}, bf16[1,64,2304]{2,1,0:T(8,128)(2,1)S(1)}, u32[]{:S(2)}, u32[]{:S(2)}) collective-permute-start(bf16[1,64,2304]{2,1,0:T(8,128)(2,1)S(1)} %get-tuple-element.21), channel_id=1, source_target_pairs={{0,8},{4,0},{8,12},{12,4},{1,9},{5,1},{9,13},{13,5},{2,10},{6,2},{... | collective-permute-start | bytes 884744 | tf_op jit(solution)/shard_map/ppermute | solution.py:409
  44.2 5.8 %collective-permute-start.14 = (f32[4,64,128]{2,1,0:T(8,128)S(1)}, f32[4,64,128]{2,1,0:T(8,128)S(1)}, u32[]{:S(2)}, u32[]{:S(2)}) collective-permute-start(f32[4,64,128]{2,1,0:T(8,128)S(1)} %shard_map.78.refs_0_), channel_id=1, source_target_pairs={{0,3},{1,2},{2,1},{3,0},{4,7},{5,6},{6,5},{7,4},{8,11},{9,10},{10,... | collective-permute-start | bytes 393224 | tf_op jit(solution)/shard_map/ppermute | solution.py:29
  53.2 5.8 %collective-permute-start.16 = (f32[2,64,128]{2,1,0:T(8,128)S(1)}, f32[2,64,128]{2,1,0:T(8,128)S(1)}, u32[]{:S(2)}, u32[]{:S(2)}) collective-permute-start(f32[2,64,128]{2,1,0:T(8,128)S(1)} %shard_map.80.refs_1_.refs_0_), channel_id=1, source_target_pairs={{0,1},{1,0},{2,3},{3,2},{4,5},{5,4},{6,7},{7,6},{8,9},{9,8},{10,11... | collective-permute-start | bytes 196616 | tf_op jit(solution)/shard_map/ppermute | solution.py:29
  53.3 7.2 %collective-permute-start.17 = (f32[2,64,128]{2,1,0:T(8,128)S(1)}, f32[2,64,128]{2,1,0:T(8,128)S(1)}, u32[]{:S(2)}, u32[]{:S(2)}) collective-permute-start(f32[2,64,128]{2,1,0:T(8,128)S(1)} %shard_map.80.refs_1_.refs_0_), channel_id=1, source_target_pairs={{0,2},{1,3},{2,0},{3,1},{4,6},{5,7},{6,4},{7,5},{8,10},{9,11},{10,... | collective-permute-start | bytes 196616 | tf_op jit(solution)/shard_map/ppermute | solution.py:29
  54.8 6.0 %collective-permute-start.18 = (f32[2,64,128]{2,1,0:T(8,128)S(1)}, f32[2,64,128]{2,1,0:T(8,128)S(1)}, u32[]{:S(2)}, u32[]{:S(2)}) collective-permute-start(f32[2,64,128]{2,1,0:T(8,128)S(1)} %shard_map.80.refs_1_.refs_0_), channel_id=1, source_target_pairs={{0,3},{1,2},{2,1},{3,0},{4,7},{5,6},{6,5},{7,4},{8,11},{9,10},{10,... | collective-permute-start | bytes 196616 | tf_op jit(solution)/shard_map/ppermute | solution.py:29
  58.8 7.9 %collective-permute-start.22 = (f32[1,64,128]{2,1,0:T(8,128)S(1)}, f32[1,64,128]{2,1,0:T(8,128)S(1)}, u32[]{:S(2)}, u32[]{:S(2)}) collective-permute-start(f32[1,64,128]{2,1,0:T(8,128)S(1)} %shard_map.81.refs_1_.refs_0_), channel_id=1, source_target_pairs={{0,1},{1,0},{2,3},{3,2},{4,5},{5,4},{6,7},{7,6},{8,9},{9,8},{10,11... | collective-permute-start | bytes 98312 | tf_op jit(solution)/shard_map/ppermute | solution.py:29
  58.9 8.1 %collective-permute-start.23 = (f32[1,64,128]{2,1,0:T(8,128)S(1)}, f32[1,64,128]{2,1,0:T(8,128)S(1)}, u32[]{:S(2)}, u32[]{:S(2)}) collective-permute-start(f32[1,64,128]{2,1,0:T(8,128)S(1)} %shard_map.81.refs_1_.refs_0_), channel_id=1, source_target_pairs={{0,2},{1,3},{2,0},{3,1},{4,6},{5,7},{6,4},{7,5},{8,10},{9,11},{10,... | collective-permute-start | bytes 98312 | tf_op jit(solution)/shard_map/ppermute | solution.py:29
  60.5 6.6 %collective-permute-start.24 = (f32[1,64,128]{2,1,0:T(8,128)S(1)}, f32[1,64,128]{2,1,0:T(8,128)S(1)}, u32[]{:S(2)}, u32[]{:S(2)}) collective-permute-start(f32[1,64,128]{2,1,0:T(8,128)S(1)} %shard_map.81.refs_1_.refs_0_), channel_id=1, source_target_pairs={{0,3},{1,2},{2,1},{3,0},{4,7},{5,6},{6,5},{7,4},{8,11},{9,10},{10,... | collective-permute-start | bytes 98312 | tf_op jit(solution)/shard_map/ppermute | solution.py:29
  65.1 3.3 %collective-permute-start.19 = (bf16[1,64,128]{2,1,0:T(8,128)(2,1)S(1)}, bf16[1,64,128]{2,1,0:T(8,128)(2,1)S(1)}, u32[]{:S(2)}, u32[]{:S(2)}) collective-permute-start(bf16[1,64,128]{2,1,0:T(8,128)(2,1)S(1)} %shard_map.83.refs_0_), channel_id=1, source_target_pairs={{0,1},{1,0},{2,3},{3,2},{4,5},{5,4},{6,7},{7,6},{8,9},{9,8},{10,11... | collective-permute-start | bytes 49160 | tf_op jit(solution)/shard_map/ppermute | solution.py:29
  65.3 3.8 %collective-permute-start.20 = (bf16[1,64,128]{2,1,0:T(8,128)(2,1)S(1)}, bf16[1,64,128]{2,1,0:T(8,128)(2,1)S(1)}, u32[]{:S(2)}, u32[]{:S(2)}) collective-permute-start(bf16[1,64,128]{2,1,0:T(8,128)(2,1)S(1)} %shard_map.83.refs_0_), channel_id=1, source_target_pairs={{0,2},{1,3},{2,0},{3,1},{4,6},{5,7},{6,4},{7,5},{8,10},{9,11},{10,... | collective-permute-start | bytes 49160 | tf_op jit(solution)/shard_map/ppermute | solution.py:29
  66.7 3.2 %collective-permute-start.21 = (bf16[1,64,128]{2,1,0:T(8,128)(2,1)S(1)}, bf16[1,64,128]{2,1,0:T(8,128)(2,1)S(1)}, u32[]{:S(2)}, u32[]{:S(2)}) collective-permute-start(bf16[1,64,128]{2,1,0:T(8,128)(2,1)S(1)} %shard_map.83.refs_0_), channel_id=1, source_target_pairs={{0,3},{1,2},{2,1},{3,0},{4,7},{5,6},{6,5},{7,4},{8,11},{9,10},{10,... | collective-permute-start | bytes 49160 | tf_op jit(solution)/shard_map/ppermute | solution.py:29

commit v14 on v11

--- a/solution.py
+++ b/solution.py
@@ -40,7 +40,17 @@
     return [large, large, rows - 2 * large]
 
 
-def base_kernel(order, tokens_ref, weight_ref, *refs):
+def base_kernel(order, capacity, tokens_ref, weight_ref, *refs):
+    if capacity:
+        *asked, down_ref, up_ref = refs[:8]
+        *scalars, scalar_sems, panel_sems = refs[-8:]
+        near_ref, plan_ref, *held = refs[-13:-8]
+        refs = [*refs[-17:-13], *held]
+        loads = [
+            pltpu.make_async_copy(source, scalar, scalar_sems.at[i])
+            for i, (source, scalar) in enumerate(zip(asked, scalars))
+        ]
+        run_copies(loads)
     *sent_refs, kept_ref, tokens, weight, sems = refs
     half, rows, width = kept_ref.shape
     parts = sems.shape[1]
@@ -81,6 +91,13 @@
                 ref[index, at : at + size, :] = value
 
     run_copies([token_copies[0], *weight_copies])
+    packing = []
+    if capacity:
+        for load in loads:
+            load.wait()
+        packing = write_plan(
+            capacity, scalars, down_ref, up_ref, near_ref, plan_ref, panel_sems
+        )
     token_copies[0].wait()
     for i, copy in enumerate(weight_copies):
         copy.wait()
@@ -90,26 +107,41 @@
     for i in range(1, parts):
         token_copies[i].wait()
         add(i * tile, 0, weight.shape[0], True)
-
-
-def base_chunks(tokens, weight, order, width):
+    for copy in packing:
+        copy.wait()
+
+
+def base_chunks(tokens, weight, order, width, planning=None, after=()):
     rows = tokens.shape[0]
     half = len(order) // 2
     sizes = [*piece_rows(rows), rows]
-    *sent, kept = pl.pallas_call(
-        functools.partial(base_kernel, order),
-        in_specs=[ANY] * 2,
-        out_specs=[VMEM] * len(sizes),
-        out_shape=[jax.ShapeDtypeStruct((half, size, width), jnp.float32) for size in sizes],
-        scratch_shapes=[
-            pltpu.VMEM(tokens.shape, tokens.dtype),
-            pltpu.VMEM(weight.shape, weight.dtype),
-            pltpu.SemaphoreType.DMA((2, 4)),
-        ],
+    specs = [VMEM] * len(sizes)
+    shapes = [jax.ShapeDtypeStruct((half, size, width), jnp.float32) for size in sizes]
+    scratch = [
+        pltpu.VMEM(tokens.shape, tokens.dtype),
+        pltpu.VMEM(weight.shape, weight.dtype),
+        pltpu.SemaphoreType.DMA((2, 4)),
+    ]
+    operands, capacity = [], 0
+    if planning is not None:
+        *operands, capacity = planning
+        down, up = operands[-2:]
+        specs += [ANY, SMEM]
+        shapes += [
+            jax.ShapeDtypeStruct((capacity, down.shape[1], down.shape[2] + width), down.dtype),
+            jax.ShapeDtypeStruct((PLAN_ROWS * capacity,), jnp.int32),
+        ]
+        scratch += [pltpu.SMEM(operand.shape, operand.dtype) for operand in operands[:6]]
+        scratch += [pltpu.SemaphoreType.DMA((6,)), pltpu.SemaphoreType.DMA((capacity, 2))]
+    return pl.pallas_call(
+        functools.partial(base_kernel, order, capacity),
+        in_specs=[ANY] * (2 + len(operands) + len(after)),
+        out_specs=specs,
+        out_shape=shapes,
+        scratch_shapes=scratch,
         compiler_params=PARAMS,
         cost_estimate=BASE,
-    )(in_hbm(tokens), in_hbm(weight))
-    return sent, kept
+    )(in_hbm(tokens), in_hbm(weight), *operands, *after)
 
 
 def add_kernel(kept_ref, *refs):
@@ -140,11 +172,11 @@
     )(kept, *arrived)
 
 
-def base_parts(tokens, weight, width):
+def base_parts(tokens, weight, width, planning=None, after=()):
     size = lax.axis_size("tensor")
     kept_order = [k for k in range(size) if not k & 1]
     kept_order.sort(key=lambda k: [k >> bit & 1 for bit in range(1, size.bit_length())])
-    return base_chunks(tokens, weight, [k ^ 1 for k in kept_order] + kept_order, width)
+    return base_chunks(tokens, weight, [k ^ 1 for k in kept_order] + kept_order, width, planning, after)
 
 
 def base_sum(sent, kept):
@@ -183,19 +215,17 @@
     ]
 
 
-def plan_kernel(capacity, holder_slots, *refs):
-    sources, plan_ref, scalars, sems = refs[:6], refs[-8], refs[-7:-1], refs[-1]
-    loads = [
-        pltpu.make_async_copy(source, scalar, sems.at[i])
-        for i, (source, scalar) in enumerate(zip(sources, scalars))
-    ]
-    for load in run_copies(loads):
-        load.wait()
+def write_plan(capacity, scalars, down_ref, up_ref, near_ref, plan_ref, sems):
+    holder_slots = down_ref.shape[0]
     names_ref, first_ref, second_ref, third_ref, table_ref, live_ref = scalars
     here = lax.axis_index("pool")
     find = functools.partial(
         pick, table_ref=table_ref, holder_slots=holder_slots, count=capacity
     )
+    near_slots = find(first_ref, holder=here)[1]
+    copies = []
+    for k, slot in enumerate(near_slots):
+        copies += run_copies(panel_copies(k, slot, down_ref, up_ref, near_ref, sems))
     inner = (here == 1) | (here == 2)
     own = find(names_ref, holder=here)
     near = find(names_ref, holder=here ^ 1)
@@ -208,7 +238,6 @@
         late[0],
         own[1],
         across[1],
-        find(first_ref, holder=here)[1],
         find(second_ref, holder=here)[1],
         find(third_ref, holder=here)[1],
         find(first_ref, holder=here ^ 3)[1],
@@ -218,27 +247,14 @@
     for number, row in enumerate(rows):
         for k in range(capacity):
             plan_ref[number * capacity + k] = row[k]
-
-
-OWN, ACROSS, NEAR, TO_INNER, TO_OUTER, FORWARD, INNER, LIVE, PLAN_ROWS = 4, 5, 6, 7, 8, 9, 10, 11, 15
-
-
-def make_plan(names, others, table, live, holder_slots, capacity, after):
-    return pl.pallas_call(
-        functools.partial(plan_kernel, capacity, holder_slots),
-        in_specs=[ANY] * (6 + len(after)),
-        out_specs=SMEM,
-        out_shape=jax.ShapeDtypeStruct((PLAN_ROWS * capacity,), jnp.int32),
-        scratch_shapes=[pltpu.SMEM(names.shape, jnp.int32)] * 4
-        + [pltpu.SMEM(table.shape, jnp.int32), pltpu.SMEM(live.shape, jnp.int32)]
-        + [pltpu.SemaphoreType.DMA((6,))],
-        compiler_params=PARAMS,
-        cost_estimate=SHORT,
-    )(in_hbm(names), *others, in_hbm(table), in_hbm(live), *after)
-
-
-def pack_kernel(starts, choose, capacity, plan_ref, *refs):
-    out_ref, sems = refs[-2:]
+    return copies
+
+
+OWN, ACROSS, TO_INNER, TO_OUTER, FORWARD, INNER, LIVE, PLAN_ROWS = 4, 5, 6, 7, 8, 9, 10, 14
+
+
+def pack_kernel(starts, choose, capacity, inputs, plan_ref, *refs):
+    out_ref, sems = refs[inputs], refs[-1]
 
     def run(start, down_ref, up_ref):
         copies = []
@@ -256,19 +272,28 @@
         pl.when(jnp.logical_not(first))(functools.partial(run, starts[1], *refs[2:4]))
 
 
-def pack_panels(plan, choices, choose, capacity, after=(), cost=None):
+def pack_panels(plan, choices, choose, capacity, after=(), cost=None, carried=None):
     sources = [a for _, *pair in choices for a in pair]
     rank, depth = sources[0].shape[1:]
     width = sources[1].shape[2]
-    return pl.pallas_call(
-        functools.partial(pack_kernel, [start for start, *_ in choices], choose, capacity),
-        in_specs=[SMEM] + [ANY] * (len(sources) + len(after)),
-        out_specs=ANY,
-        out_shape=jax.ShapeDtypeStruct((capacity, rank, depth + width), sources[0].dtype),
+    operands = [plan, *sources, *after]
+    out = jax.ShapeDtypeStruct((capacity, rank, depth + width), sources[0].dtype)
+    outs, aliases = [out], {}
+    if carried is not None:
+        aliases = {len(operands): 1}
+        operands.append(carried)
+        outs.append(jax.ShapeDtypeStruct(carried.shape, carried.dtype))
+    results = pl.pallas_call(
+        functools.partial(pack_kernel, [start for start, *_ in choices], choose, capacity, len(operands) - 1),
+        in_specs=[SMEM] + [ANY] * (len(operands) - 1),
+        out_specs=[ANY] * len(outs),
+        out_shape=outs,
+        input_output_aliases=aliases,
         scratch_shapes=[pltpu.SemaphoreType.DMA((capacity, 2))],
         compiler_params=PARAMS,
         cost_estimate=cost or NO_COST,
-    )(plan, *sources, *after)
+    )(*operands)
+    return results[0] if carried is None else results
 
 
 def each_block(phases, choose, plan_ref, refs, act):
@@ -398,18 +423,17 @@
     others = [swap(names, "pool", m) for m in range(1, 4)]
     inner_up = across(up, [(0, 0), (1, 2), (2, 1), (3, 3)])
     inner_down = across(down, [(0, 0), (1, 2), (2, 1), (3, 3)])
-    sent, kept = base_parts(tokens, weight, up.shape[2])
-    plan = make_plan(names, others, table, live, down.shape[0], capacity, [inner_up])
     choose = INNER * capacity
     held = in_hbm(down), in_hbm(up)
-
-    def pack(choices, after, cost=None):
+    planning = [in_hbm(names), *others, in_hbm(table), in_hbm(live), *held, capacity]
+    *sent, kept, near_out, plan = base_parts(tokens, weight, up.shape[2], planning, [inner_up])
+
+    def pack(choices, after, cost=None, carried=None):
         choices = [(row * capacity, *panels) for row, *panels in choices]
-        return pack_panels(plan, choices, choose, capacity, after, cost)
-
-    near_out = pack([(NEAR, *held)], sent[-1:])
+        return pack_panels(plan, choices, choose, capacity, after, cost, carried)
+
+    outer_out, near_out = pack([(TO_OUTER, *held)], [], carried=near_out)
     near = across(near_out, [(0, 1), (1, 0), (2, 3), (3, 2)])
-    outer_out = pack([(TO_OUTER, *held)], [near_out])
     to_outer = across(outer_out, [(0, 3), (1, 1), (2, 2), (3, 0)])
     base = base_sum(sent, kept)
     late_out = pack(
@@ -458,7 +482,8 @@
     ranks = jnp.sum(earlier.astype(jnp.int32), axis=1)
     places = lax.rem(here - owners + pool_size, pool_size) * capacity + ranks
     plan = jnp.concatenate([blocks, places, live[0]])
-    base = base_sum(*base_parts(tokens, weight, up.shape[2]))
+    *sent, kept = base_parts(tokens, weight, up.shape[2])
+    base = base_sum(sent, kept)
     phases = [(0, blocks.shape[0], [(arrived, blocks.shape[0])])]
     parts = exchange(shrink(plan, row_blocks, phases, 0))
     live_row = 2 * blocks.shape[0]

time: 72.1 us -> 74.3 us (1.031)
  waiting for transfers between devices: 19.6 us -> 26.3 us
  Pallas kernels: 22 us -> 19.5 us
  starting transfers between devices: 30 us -> 28.1 us
    ppermute x16, waiting for transfers between devices: 7.29 us -> 11.5 us  [swap(): return lax.ppermute(value, axis, pairs)]
    ppermute x5, starting transfers between devices: 15.7 us -> 11.5 us  [across(): return lax.ppermute(value, 'pool', pairs)]
    ppermute x5, waiting for transfers between devices: 12.3 us -> 14.8 us  [across(): return lax.ppermute(value, 'pool', pairs)]
    ppermute x16, starting transfers between devices: 14.3 us -> 16.6 us  [swap(): return lax.ppermute(value, axis, pairs)]
    pallas_call x3 -> x2, Pallas kernels: 5.16 us -> 3.53 us  [pack_panels(): pl.pallas_call(functools.partial(pack_kernel, [start for start, *_ in cho...]
    pallas_call x2 -> x1, Pallas kernels: 8.69 us -> 7.88 us  [base_chunks(): pl.pallas_call(functools.partial(base_kernel, order, capacity), in_specs=...]
  transfers between devices with their start and end apart: 21 -> 21, of which waited for: 7 -> 8; matrix products, arithmetic and copies ran while one was open for 0% -> 0% of each run, Pallas kernels for 29% -> 24%
where the time goes in v14:
time: 74.3 us; the launch traced here: 74.1 us
  starting transfers between devices  28.1 us (38%)
  waiting for transfers between devices  26.3 us (35%)
  Pallas kernels  19.5 us (26%)
    ppermute x16, starting transfers between devices, swap(): return lax.ppermute(value, axis, pairs)  16.6 us
    ppermute x5, waiting for transfers between devices, across(): return lax.ppermute(value, 'pool', pairs)  14.8 us
    ppermute x16, waiting for transfers between devices, swap(): return lax.ppermute(value, axis, pairs)  11.5 us
    ppermute x5, starting transfers between devices, across(): return lax.ppermute(value, 'pool', pairs)  11.5 us
    pallas_call x1, Pallas kernels, base_chunks(): pl.pallas_call(functools.partial(base_kernel, order, capacity), in_specs=...  7.88 us
    pallas_call x3, Pallas kernels, combine(): pl.pallas_call(functools.partial(combine_kernel, shapes, choose, len(part...  4.38 us
    pallas_call x2, Pallas kernels, pack_panels(): pl.pallas_call(functools.partial(pack_kernel, [start for start, *_ in cho...  3.53 us
    pallas_call x3, Pallas kernels, shrink(): pl.pallas_call(functools.partial(shrink_kernel, shapes, choose), in_specs...  3.43 us
  transfers between devices with their start and end apart: 21, of which 8 were waited for; matrix products, arithmetic and copies ran while one was open for 0% of the time, Pallas kernels for 24%

profile of v14, /device:TPU:0, one launch (start us, length us, event | category | flops | bytes accessed | tf_op | source)
XLA Modules:
  0.0 74.1 jit_solution(5682594277044146321)
XLA Ops:
  0.0 1.6 %collective-permute-start.3 = (bf16[4,64,256]{2,1,0:T(8,128)(2,1)}, bf16[4,64,256]{2,1,0:T(8,128)(2,1)S(1)}, u32[]{:S(2)}, u32[]{:S(2)}) collective-permute-start(bf16[4,64,256]{2,1,0:T(8,128)(2,1)} %refs_6_.1), channel_id=1, source_target_pairs={{0,0},{4,8},{8,4},{12,12},{1,1},{5,9},{9,5},{13,13},{2,2},{6,10},{... | collective-permute-start | bytes 393224 | tf_op jit(solution)/shard_map/ppermute | solution.py:421
  1.6 5.0 %collective-permute-start = (s32[1,8]{1,0:T(1,128)}, s32[1,8]{1,0:T(1,128)S(1)}, u32[]{:S(2)}, u32[]{:S(2)}) collective-permute-start(s32[1,8]{1,0:T(1,128)} %refs_0_.1), channel_id=1, source_target_pairs={{0,4},{4,0},{8,12},{12,8},{1,5},{5,1},{9,13},{13,9},{2,6},{6,2},{1... | collective-permute-start | bytes 104 | tf_op jit(solution)/shard_map/ppermute | solution.py:29
  6.6 0.6 collective-permute-start.1
  7.2 1.8 %collective-permute-start.2 = (s32[1,8]{1,0:T(1,128)}, s32[1,8]{1,0:T(1,128)S(1)}, u32[]{:S(2)}, u32[]{:S(2)}) collective-permute-start(s32[1,8]{1,0:T(1,128)} %refs_0_.1), channel_id=1, source_target_pairs={{0,12},{4,8},{8,4},{12,0},{1,13},{5,9},{9,5},{13,1},{2,14},{6,10},... | collective-permute-start | bytes 104 | tf_op jit(solution)/shard_map/ppermute | solution.py:29
  9.0 1.9 %collective-permute-start.4 = (bf16[4,64,2048]{2,1,0:T(8,128)(2,1)}, bf16[4,64,2048]{2,1,0:T(8,128)(2,1)S(1)}, u32[]{:S(2)}, u32[]{:S(2)}) collective-permute-start(bf16[4,64,2048]{2,1,0:T(8,128)(2,1)} %bitcast.14), channel_id=1, source_target_pairs={{0,0},{4,8},{8,4},{12,12},{1,1},{5,9},{9,5},{13,13},{2,2},{6,10},{... | collective-permute-start | bytes 3145736 | tf_op jit(solution)/shard_map/ppermute | solution.py:421
  10.9 0.0 collective-permute-done.refs_1_
  10.9 0.3 collective-permute-done.1.refs_2_
  11.1 1.5 %collective-permute-done.2.refs_3_ = s32[1,8]{1,0:T(1,128)S(1)} collective-permute-done((s32[1,8]{1,0:T(1,128)}, s32[1,8]{1,0:T(1,128)S(1)}, u32[]{:S(2)}, u32[]{:S(2)}) %collective-permute-start.2) | collective-permute-done | bytes 64 | tf_op jit(solution)/shard_map/ppermute | solution.py:29
  12.6 0.0 collective-permute-done.3.refs_8_.refs_1_.refs_6_
  12.6 7.9 %shard_map.73 = (f32[2,384,256]{2,1,0:T(8,128)S(1)}, f32[2,384,256]{2,1,0:T(8,128)S(1)}, f32[2,256,256]{2,1,0:T(8,128)S(1)}, f32[2,1024,256]{2,1,0:T(8,128)S(1)}...) custom-call(bf16[1024,2048]{1,0:T(8,128)(2,1)} %tokens_ref.1, bf16[2048,1024]{1,0:T(8,128)(2,1)} %weight_ref.1, ...), custom_call_target="tpu_custom_call" | custom-call | flops 4000000000 | tf_op jit(solution)/shard_map/pallas_call | solution.py:136
  20.5 0.1 collective-permute-start.5
  20.6 0.5 collective-permute-start.6
  21.1 0.1 collective-permute-start.7
  21.2 1.6 %shard_map.75 = (bf16[2,64,2304]{2,1,0:T(8,128)(2,1)S(1)}, bf16[2,64,2304]{2,1,0:T(8,128)(2,1)S(1)}) custom-call(s32[28]{0:T(128)S(1)} %get-tuple-element.15.plan_ref, bf16[4,64,2048]{2,1,0:T(8,128)(2,1)} %bitcast.16, bf16[4,64,256]{2,1,0:T(8,128)(2,1)} %refs_6_.1, bf16[2,64,2304]{2,1,0:T(8,128)(2,1)S(1)} %get-tuple-element.21.refs_2_), custom_call_target="tpu_custom_call", output_to_operand_aliasing={{1}: (3, {})} | custom-call | tf_op jit(solution)/shard_map/pallas_call | solution.py:286
  22.8 0.1 collective-permute-start.10
  22.9 1.9 %collective-permute-done.7.refs_2_ = f32[2,256,256]{2,1,0:T(8,128)S(1)} collective-permute-done((f32[2,256,256]{2,1,0:T(8,128)S(1)}, f32[2,256,256]{2,1,0:T(8,128)S(1)}, u32[]{:S(2)}, u32[]{:S(2)}) %collective-permute-start.7) | collective-permute-done | bytes 524320 | tf_op jit(solution)/shard_map/ppermute | solution.py:29
  24.8 3.7 %collective-permute-start.9 = (bf16[2,64,2304]{2,1,0:T(8,128)(2,1)S(1)}, bf16[2,64,2304]{2,1,0:T(8,128)(2,1)S(1)}, u32[]{:S(2)}, u32[]{:S(2)}) collective-permute-start(bf16[2,64,2304]{2,1,0:T(8,128)(2,1)S(1)} %get-tuple-element.22.refs_5_), channel_id=1, source_target_pairs={{0,12},{4,4},{8,8},{12,0},{1,13},{5,5},{9,9},{13,1},{2,14},{6,6},{... | collective-permute-start | bytes 1769480 | tf_op jit(solution)/shard_map/ppermute | solution.py:421
  28.5 0.0 collective-permute-done.5.refs_0_
  28.5 0.0 collective-permute-done.6.refs_1_
  28.5 0.3 shard_map.74
  28.8 1.6 %collective-permute-start.14 = (bf16[1,1024,256]{2,1,0:T(8,128)(2,1)S(1)}, bf16[1,1024,256]{2,1,0:T(8,128)(2,1)S(1)}, u32[]{:S(2)}, u32[]{:S(2)}) collective-permute-start(bf16[1,1024,256]{2,1,0:T(8,128)(2,1)S(1)} %get-tuple-element.24), channel_id=1, source_target_pairs={{0,2},{1,3},{2,0},{3,1},{4,6},{5,7},{6,4},{7,5},{8,10},{9,11},{10,... | collective-permute-start | bytes 1572872 | tf_op jit(solution)/shard_map/ppermute | solution.py:29
  30.4 0.0 collective-permute-done.4.refs_0_
  30.4 0.0 copy-start
  30.4 0.0 copy-start.1
  30.4 1.9 %shard_map.76.refs_2_ = bf16[2,64,2304]{2,1,0:T(8,128)(2,1)S(1)} custom-call(s32[28]{0:T(128)S(1)} %get-tuple-element.15.plan_ref, bf16[4,64,2048]{2,1,0:T(8,128)(2,1)S(1)} %collective-permute-done.4.refs_0_, bf16[4,64,256]{2,1,0:T(8,128)(2,1)S(1)} %collective-permute-done.3.refs_8_.refs_1_.refs_6_, bf16[4,64,2048]{2,1,0:T(8,128)(2,1)} %bitcast.17, ...), custom_call_target="tpu_custom_call" | custom-call | flops 6000000000 | tf_op jit(solution)/shard_map/pallas_call | solution.py:286
  32.3 0.0 copy-start.2
  32.3 4.2 %collective-permute-start.8 = (bf16[2,64,2304]{2,1,0:T(8,128)(2,1)S(1)}, bf16[2,64,2304]{2,1,0:T(8,128)(2,1)S(1)}, u32[]{:S(2)}, u32[]{:S(2)}) collective-permute-start(bf16[2,64,2304]{2,1,0:T(8,128)(2,1)S(1)} %shard_map.76.refs_2_), channel_id=1, source_target_pairs={{0,8},{4,0},{8,12},{12,4},{1,9},{5,1},{9,13},{13,5},{2,10},{6,2},{... | collective-permute-start | bytes 1769480 | tf_op jit(solution)/shard_map/ppermute | solution.py:421
  36.6 14.7 %collective-permute-done.10.refs_1_.refs_7_ = bf16[2,64,2304]{2,1,0:T(8,128)(2,1)S(1)} collective-permute-done((bf16[2,64,2304]{2,1,0:T(8,128)(2,1)S(1)}, bf16[2,64,2304]{2,1,0:T(8,128)(2,1)S(1)}, u32[]{:S(2)}, u32[]{:S(2)}) %collective-permute-start.10) | collective-permute-done | bytes 589856 | tf_op jit(solution)/shard_map/ppermute | solution.py:421
  51.3 0.0 copy-done
  51.3 0.0 copy-done.1
  51.3 1.4 %shard_map.77.refs_0_ = f32[4,64,128]{2,1,0:T(8,128)S(1)} custom-call(s32[28]{0:T(128)S(1)} %get-tuple-element.15.plan_ref, bf16[8,128,2048]{2,1,0:T(8,128)(2,1)S(1)} %bitcast.4, bf16[4,64,2048]{2,1,0:T(8,128)(2,1)S(1)} %bitcast.18, bf16[2,64,2304]{2,1,0:T(8,128)(2,1)S(1)} %collective-permute-done.10.refs_1_.refs_7_, bf16[2,64,2304]{2,1,0:T(8,128)(2,1)S(1)} %shard_map.76.refs_2_), custom_call_target="tpu_custom_call" | custom-call | tf_op jit(solution)/shard_map/pallas_call | solution.py:342
  52.7 0.1 collective-permute-start.11
  52.8 1.5 %collective-permute-start.12 = (f32[4,64,128]{2,1,0:T(8,128)S(1)}, f32[4,64,128]{2,1,0:T(8,128)S(1)}, u32[]{:S(2)}, u32[]{:S(2)}) collective-permute-start(f32[4,64,128]{2,1,0:T(8,128)S(1)} %shard_map.77.refs_0_), channel_id=1, source_target_pairs={{0,2},{1,3},{2,0},{3,1},{4,6},{5,7},{6,4},{7,5},{8,10},{9,11},{10,... | collective-permute-start | bytes 393224 | tf_op jit(solution)/shard_map/ppermute | solution.py:29
  54.3 0.0 collective-permute-done.11.refs_1_
  54.3 1.0 %collective-permute-start.13 = (f32[4,64,128]{2,1,0:T(8,128)S(1)}, f32[4,64,128]{2,1,0:T(8,128)S(1)}, u32[]{:S(2)}, u32[]{:S(2)}) collective-permute-start(f32[4,64,128]{2,1,0:T(8,128)S(1)} %shard_map.77.refs_0_), channel_id=1, source_target_pairs={{0,3},{1,2},{2,1},{3,0},{4,7},{5,6},{6,5},{7,4},{8,11},{9,10},{10,... | collective-permute-start | bytes 393224 | tf_op jit(solution)/shard_map/ppermute | solution.py:29
  55.4 3.8 %collective-permute-done.12.refs_2_ = f32[4,64,128]{2,1,0:T(8,128)S(1)} collective-permute-done((f32[4,64,128]{2,1,0:T(8,128)S(1)}, f32[4,64,128]{2,1,0:T(8,128)S(1)}, u32[]{:S(2)}, u32[]{:S(2)}) %collective-permute-start.12) | collective-permute-done | bytes 131104 | tf_op jit(solution)/shard_map/ppermute | solution.py:29
  59.1 1.9 %collective-permute-done.13.refs_3_ = f32[4,64,128]{2,1,0:T(8,128)S(1)} collective-permute-done((f32[4,64,128]{2,1,0:T(8,128)S(1)}, f32[4,64,128]{2,1,0:T(8,128)S(1)}, u32[]{:S(2)}, u32[]{:S(2)}) %collective-permute-start.13) | collective-permute-done | bytes 131104 | tf_op jit(solution)/shard_map/ppermute | solution.py:29
  61.0 0.0 collective-permute-done.14
  61.1 0.0 copy-done.2
  61.1 1.5 %shard_map.78.refs_2_.refs_8_ = bf16[1024,256]{1,0:T(8,128)(2,1)} custom-call(s32[28]{0:T(128)S(1)} %get-tuple-element.15.plan_ref, f32[4,64,128]{2,1,0:T(8,128)S(1)} %shard_map.77.refs_0_, f32[4,64,128]{2,1,0:T(8,128)S(1)} %collective-permute-done.11.refs_1_, f32[4,64,128]{2,1,0:T(8,128)S(1)} %collective-permute-done.12.refs_2_, ...), custom_call_target="tpu_custom_call" | custom-call | tf_op jit(solution)/shard_map/pallas_call | solution.py:404
  62.6 0.0 collective-permute-done.9.refs_1_.refs_7_
  62.6 1.0 %shard_map.79.refs_1_.refs_0_ = f32[2,64,128]{2,1,0:T(8,128)S(1)} custom-call(s32[28]{0:T(128)S(1)} %get-tuple-element.15.plan_ref, bf16[8,128,2048]{2,1,0:T(8,128)(2,1)S(1)} %bitcast.5, bf16[4,64,2048]{2,1,0:T(8,128)(2,1)S(1)} %collective-permute-done.4.refs_0_, bf16[2,64,2304]{2,1,0:T(8,128)(2,1)S(1)} %collective-permute-done.9.refs_1_.refs_7_, ...), custom_call_target="tpu_custom_call" | custom-call | tf_op jit(solution)/shard_map/pallas_call | solution.py:342
  63.6 0.6 collective-permute-start.18
  64.2 1.5 %collective-permute-start.19 = (f32[2,64,128]{2,1,0:T(8,128)S(1)}, f32[2,64,128]{2,1,0:T(8,128)S(1)}, u32[]{:S(2)}, u32[]{:S(2)}) collective-permute-start(f32[2,64,128]{2,1,0:T(8,128)S(1)} %shard_map.79.refs_1_.refs_0_), channel_id=1, source_target_pairs={{0,2},{1,3},{2,0},{3,1},{4,6},{5,7},{6,4},{7,5},{8,10},{9,11},{10,... | collective-permute-start | bytes 196616 | tf_op jit(solution)/shard_map/ppermute | solution.py:29
  65.7 0.0 collective-permute-start.20
  65.7 0.0 collective-permute-done.8.refs_0_.refs_6_
  65.7 1.0 %shard_map.80.refs_0_ = bf16[2,64,128]{2,1,0:T(8,128)(2,1)S(1)} custom-call(s32[28]{0:T(128)S(1)} %get-tuple-element.15.plan_ref, bf16[8,128,2048]{2,1,0:T(8,128)(2,1)S(1)} %bitcast.6, bf16[2,64,2304]{2,1,0:T(8,128)(2,1)S(1)} %collective-permute-done.8.refs_0_.refs_6_, f32[2,64,128]{2,1,0:T(8,128)S(1)} %shard_map.79.refs_1_.refs_0_), custom_call_target="tpu_custom_call" | custom-call | tf_op jit(solution)/shard_map/pallas_call | solution.py:342
  66.8 0.7 collective-permute-start.15
  67.5 1.5 %collective-permute-start.16 = (bf16[2,64,128]{2,1,0:T(8,128)(2,1)S(1)}, bf16[2,64,128]{2,1,0:T(8,128)(2,1)S(1)}, u32[]{:S(2)}, u32[]{:S(2)}) collective-permute-start(bf16[2,64,128]{2,1,0:T(8,128)(2,1)S(1)} %shard_map.80.refs_0_), channel_id=1, source_target_pairs={{0,2},{1,3},{2,0},{3,1},{4,6},{5,7},{6,4},{7,5},{8,10},{9,11},{10,... | collective-permute-start | bytes 98312 | tf_op jit(solution)/shard_map/ppermute | solution.py:29
  69.0 0.0 collective-permute-done.18.refs_1_
  69.0 0.0 collective-permute-start.17
  69.0 0.0 collective-permute-done.19.refs_2_
  69.0 1.1 %collective-permute-done.20.refs_3_ = f32[2,64,128]{2,1,0:T(8,128)S(1)} collective-permute-done((f32[2,64,128]{2,1,0:T(8,128)S(1)}, f32[2,64,128]{2,1,0:T(8,128)S(1)}, u32[]{:S(2)}, u32[]{:S(2)}) %collective-permute-start.20) | collective-permute-done | bytes 65568 | tf_op jit(solution)/shard_map/ppermute | solution.py:29
  70.1 1.4 %shard_map.81.refs_7_ = bf16[1024,256]{1,0:T(8,128)(2,1)} custom-call(s32[28]{0:T(128)S(1)} %get-tuple-element.15.plan_ref, f32[2,64,128]{2,1,0:T(8,128)S(1)} %shard_map.79.refs_1_.refs_0_, f32[2,64,128]{2,1,0:T(8,128)S(1)} %collective-permute-done.18.refs_1_, f32[2,64,128]{2,1,0:T(8,128)S(1)} %collective-permute-done.19.refs_2_, ...), custom_call_target="tpu_custom_call", output_to_operand_aliasing={{}: (9, {})} | custom-call | tf_op jit(solution)/shard_map/pallas_call | solution.py:404
  71.5 0.0 collective-permute-done.15.refs_1_
  71.6 0.0 collective-permute-done.16.refs_2_
  71.6 1.1 %collective-permute-done.17.refs_3_ = bf16[2,64,128]{2,1,0:T(8,128)(2,1)S(1)} collective-permute-done((bf16[2,64,128]{2,1,0:T(8,128)(2,1)S(1)}, bf16[2,64,128]{2,1,0:T(8,128)(2,1)S(1)}, u32[]{:S(2)}, u32[]{:S(2)}) %collective-permute-start.17) | collective-permute-done | bytes 32800 | tf_op jit(solution)/shard_map/ppermute | solution.py:29
  72.6 1.4 %shard_map.82 = bf16[1024,256]{1,0:T(8,128)(2,1)} custom-call(s32[28]{0:T(128)S(1)} %get-tuple-element.15.plan_ref, bf16[2,64,128]{2,1,0:T(8,128)(2,1)S(1)} %shard_map.80.refs_0_, bf16[2,64,128]{2,1,0:T(8,128)(2,1)S(1)} %collective-permute-done.15.refs_1_, bf16[2,64,128]{2,1,0:T(8,128)(2,1)S(1)} %collective-permute-done.16.refs_2_, ...), custom_call_target="tpu_custom_call", output_to_operand_aliasing={{}: (8, {})} | custom-call | tf_op jit(solution)/shard_map/pallas_call | solution.py:404
Async XLA Ops:
  0.0 12.6 %collective-permute-start.3 = (bf16[4,64,256]{2,1,0:T(8,128)(2,1)}, bf16[4,64,256]{2,1,0:T(8,128)(2,1)S(1)}, u32[]{:S(2)}, u32[]{:S(2)}) collective-permute-start(bf16[4,64,256]{2,1,0:T(8,128)(2,1)} %refs_6_.1), channel_id=1, source_target_pairs={{0,0},{4,8},{8,4},{12,12},{1,1},{5,9},{9,5},{13,13},{2,2},{6,10},{... | collective-permute-start | bytes 393224 | tf_op jit(solution)/shard_map/ppermute | solution.py:421
  1.6 9.3 %collective-permute-start = (s32[1,8]{1,0:T(1,128)}, s32[1,8]{1,0:T(1,128)S(1)}, u32[]{:S(2)}, u32[]{:S(2)}) collective-permute-start(s32[1,8]{1,0:T(1,128)} %refs_0_.1), channel_id=1, source_target_pairs={{0,4},{4,0},{8,12},{12,8},{1,5},{5,1},{9,13},{13,9},{2,6},{6,2},{1... | collective-permute-start | bytes 104 | tf_op jit(solution)/shard_map/ppermute | solution.py:29
  6.6 4.6 %collective-permute-start.1 = (s32[1,8]{1,0:T(1,128)}, s32[1,8]{1,0:T(1,128)S(1)}, u32[]{:S(2)}, u32[]{:S(2)}) collective-permute-start(s32[1,8]{1,0:T(1,128)} %refs_0_.1), channel_id=1, source_target_pairs={{0,8},{4,12},{8,0},{12,4},{1,9},{5,13},{9,1},{13,5},{2,10},{6,14},... | collective-permute-start | bytes 104 | tf_op jit(solution)/shard_map/ppermute | solution.py:29
  7.2 5.5 %collective-permute-start.2 = (s32[1,8]{1,0:T(1,128)}, s32[1,8]{1,0:T(1,128)S(1)}, u32[]{:S(2)}, u32[]{:S(2)}) collective-permute-start(s32[1,8]{1,0:T(1,128)} %refs_0_.1), channel_id=1, source_target_pairs={{0,12},{4,8},{8,4},{12,0},{1,13},{5,9},{9,5},{13,1},{2,14},{6,10},... | collective-permute-start | bytes 104 | tf_op jit(solution)/shard_map/ppermute | solution.py:29
  9.0 21.4 %collective-permute-start.4 = (bf16[4,64,2048]{2,1,0:T(8,128)(2,1)}, bf16[4,64,2048]{2,1,0:T(8,128)(2,1)S(1)}, u32[]{:S(2)}, u32[]{:S(2)}) collective-permute-start(bf16[4,64,2048]{2,1,0:T(8,128)(2,1)} %bitcast.14), channel_id=1, source_target_pairs={{0,0},{4,8},{8,4},{12,12},{1,1},{5,9},{9,5},{13,13},{2,2},{6,10},{... | collective-permute-start | bytes 3145736 | tf_op jit(solution)/shard_map/ppermute | solution.py:421
  20.5 8.0 %collective-permute-start.5 = (f32[2,384,256]{2,1,0:T(8,128)S(1)}, f32[2,384,256]{2,1,0:T(8,128)S(1)}, u32[]{:S(2)}, u32[]{:S(2)}) collective-permute-start(f32[2,384,256]{2,1,0:T(8,128)S(1)} %get-tuple-element.17), channel_id=1, source_target_pairs={{0,1},{1,0},{2,3},{3,2},{4,5},{5,4},{6,7},{7,6},{8,9},{9,8},{10,11... | collective-permute-start | bytes 2359304 | tf_op jit(solution)/shard_map/ppermute | solution.py:29
  20.6 7.9 %collective-permute-start.6 = (f32[2,384,256]{2,1,0:T(8,128)S(1)}, f32[2,384,256]{2,1,0:T(8,128)S(1)}, u32[]{:S(2)}, u32[]{:S(2)}) collective-permute-start(f32[2,384,256]{2,1,0:T(8,128)S(1)} %get-tuple-element.18), channel_id=1, source_target_pairs={{0,1},{1,0},{2,3},{3,2},{4,5},{5,4},{6,7},{7,6},{8,9},{9,8},{10,11... | collective-permute-start | bytes 2359304 | tf_op jit(solution)/shard_map/ppermute | solution.py:29
  21.1 3.6 %collective-permute-start.7 = (f32[2,256,256]{2,1,0:T(8,128)S(1)}, f32[2,256,256]{2,1,0:T(8,128)S(1)}, u32[]{:S(2)}, u32[]{:S(2)}) collective-permute-start(f32[2,256,256]{2,1,0:T(8,128)S(1)} %get-tuple-element.19), channel_id=1, source_target_pairs={{0,1},{1,0},{2,3},{3,2},{4,5},{5,4},{6,7},{7,6},{8,9},{9,8},{10,11... | collective-permute-start | bytes 1572872 | tf_op jit(solution)/shard_map/ppermute | solution.py:29
  22.8 28.5 %collective-permute-start.10 = (bf16[2,64,2304]{2,1,0:T(8,128)(2,1)S(1)}, bf16[2,64,2304]{2,1,0:T(8,128)(2,1)S(1)}, u32[]{:S(2)}, u32[]{:S(2)}) collective-permute-start(bf16[2,64,2304]{2,1,0:T(8,128)(2,1)S(1)} %get-tuple-element.23), channel_id=1, source_target_pairs={{0,4},{4,0},{8,12},{12,8},{1,5},{5,1},{9,13},{13,9},{2,6},{6,2},{1... | collective-permute-start | bytes 1769480 | tf_op jit(solution)/shard_map/ppermute | solution.py:421
  24.8 37.8 %collective-permute-start.9 = (bf16[2,64,2304]{2,1,0:T(8,128)(2,1)S(1)}, bf16[2,64,2304]{2,1,0:T(8,128)(2,1)S(1)}, u32[]{:S(2)}, u32[]{:S(2)}) collective-permute-start(bf16[2,64,2304]{2,1,0:T(8,128)(2,1)S(1)} %get-tuple-element.22.refs_5_), channel_id=1, source_target_pairs={{0,12},{4,4},{8,8},{12,0},{1,13},{5,5},{9,9},{13,1},{2,14},{6,6},{... | collective-permute-start | bytes 1769480 | tf_op jit(solution)/shard_map/ppermute | solution.py:421
  28.8 32.2 %collective-permute-start.14 = (bf16[1,1024,256]{2,1,0:T(8,128)(2,1)S(1)}, bf16[1,1024,256]{2,1,0:T(8,128)(2,1)S(1)}, u32[]{:S(2)}, u32[]{:S(2)}) collective-permute-start(bf16[1,1024,256]{2,1,0:T(8,128)(2,1)S(1)} %get-tuple-element.24), channel_id=1, source_target_pairs={{0,2},{1,3},{2,0},{3,1},{4,6},{5,7},{6,4},{7,5},{8,10},{9,11},{10,... | collective-permute-start | bytes 1572872 | tf_op jit(solution)/shard_map/ppermute | solution.py:29
  30.4 20.9 %copy-start = (bf16[1024,2048]{1,0:T(8,128)(2,1)S(1)}, bf16[1024,2048]{1,0:T(8,128)(2,1)}, u32[]{:S(2)}) copy-start(bf16[1024,2048]{1,0:T(8,128)(2,1)} %tokens_ref.1) | copy-start | bytes 12582916
  30.4 20.9 %copy-start.1 = (bf16[4,2048,64]{1,2,0:T(8,128)(2,1)S(1)}, bf16[4,2048,64]{1,2,0:T(8,128)(2,1)}, u32[]{:S(2)}) copy-start(bf16[4,2048,64]{1,2,0:T(8,128)(2,1)} %param.9) | copy-start | bytes 3145732
  32.3 28.7 %copy-start.2 = (bf16[4,64,256]{2,1,0:T(8,128)(2,1)S(1)}, bf16[4,64,256]{2,1,0:T(8,128)(2,1)}, u32[]{:S(2)}) copy-start(bf16[4,64,256]{2,1,0:T(8,128)(2,1)} %refs_6_.1) | copy-start | bytes 393220
  32.3 33.4 %collective-permute-start.8 = (bf16[2,64,2304]{2,1,0:T(8,128)(2,1)S(1)}, bf16[2,64,2304]{2,1,0:T(8,128)(2,1)S(1)}, u32[]{:S(2)}, u32[]{:S(2)}) collective-permute-start(bf16[2,64,2304]{2,1,0:T(8,128)(2,1)S(1)} %shard_map.76.refs_2_), channel_id=1, source_target_pairs={{0,8},{4,0},{8,12},{12,4},{1,9},{5,1},{9,13},{13,5},{2,10},{6,2},{... | collective-permute-start | bytes 1769480 | tf_op jit(solution)/shard_map/ppermute | solution.py:421
  52.7 1.6 %collective-permute-start.11 = (f32[4,64,128]{2,1,0:T(8,128)S(1)}, f32[4,64,128]{2,1,0:T(8,128)S(1)}, u32[]{:S(2)}, u32[]{:S(2)}) collective-permute-start(f32[4,64,128]{2,1,0:T(8,128)S(1)} %shard_map.77.refs_0_), channel_id=1, source_target_pairs={{0,1},{1,0},{2,3},{3,2},{4,5},{5,4},{6,7},{7,6},{8,9},{9,8},{10,11... | collective-permute-start | bytes 393224 | tf_op jit(solution)/shard_map/ppermute | solution.py:29
  52.8 6.4 %collective-permute-start.12 = (f32[4,64,128]{2,1,0:T(8,128)S(1)}, f32[4,64,128]{2,1,0:T(8,128)S(1)}, u32[]{:S(2)}, u32[]{:S(2)}) collective-permute-start(f32[4,64,128]{2,1,0:T(8,128)S(1)} %shard_map.77.refs_0_), channel_id=1, source_target_pairs={{0,2},{1,3},{2,0},{3,1},{4,6},{5,7},{6,4},{7,5},{8,10},{9,11},{10,... | collective-permute-start | bytes 393224 | tf_op jit(solution)/shard_map/ppermute | solution.py:29
  54.3 6.7 %collective-permute-start.13 = (f32[4,64,128]{2,1,0:T(8,128)S(1)}, f32[4,64,128]{2,1,0:T(8,128)S(1)}, u32[]{:S(2)}, u32[]{:S(2)}) collective-permute-start(f32[4,64,128]{2,1,0:T(8,128)S(1)} %shard_map.77.refs_0_), channel_id=1, source_target_pairs={{0,3},{1,2},{2,1},{3,0},{4,7},{5,6},{6,5},{7,4},{8,11},{9,10},{10,... | collective-permute-start | bytes 393224 | tf_op jit(solution)/shard_map/ppermute | solution.py:29
  63.6 5.4 %collective-permute-start.18 = (f32[2,64,128]{2,1,0:T(8,128)S(1)}, f32[2,64,128]{2,1,0:T(8,128)S(1)}, u32[]{:S(2)}, u32[]{:S(2)}) collective-permute-start(f32[2,64,128]{2,1,0:T(8,128)S(1)} %shard_map.79.refs_1_.refs_0_), channel_id=1, source_target_pairs={{0,1},{1,0},{2,3},{3,2},{4,5},{5,4},{6,7},{7,6},{8,9},{9,8},{10,11... | collective-permute-start | bytes 196616 | tf_op jit(solution)/shard_map/ppermute | solution.py:29
  64.2 4.7 %collective-permute-start.19 = (f32[2,64,128]{2,1,0:T(8,128)S(1)}, f32[2,64,128]{2,1,0:T(8,128)S(1)}, u32[]{:S(2)}, u32[]{:S(2)}) collective-permute-start(f32[2,64,128]{2,1,0:T(8,128)S(1)} %shard_map.79.refs_1_.refs_0_), channel_id=1, source_target_pairs={{0,2},{1,3},{2,0},{3,1},{4,6},{5,7},{6,4},{7,5},{8,10},{9,11},{10,... | collective-permute-start | bytes 196616 | tf_op jit(solution)/shard_map/ppermute | solution.py:29
  65.7 4.4 %collective-permute-start.20 = (f32[2,64,128]{2,1,0:T(8,128)S(1)}, f32[2,64,128]{2,1,0:T(8,128)S(1)}, u32[]{:S(2)}, u32[]{:S(2)}) collective-permute-start(f32[2,64,128]{2,1,0:T(8,128)S(1)} %shard_map.79.refs_1_.refs_0_), channel_id=1, source_target_pairs={{0,3},{1,2},{2,1},{3,0},{4,7},{5,6},{6,5},{7,4},{8,11},{9,10},{10,... | collective-permute-start | bytes 196616 | tf_op jit(solution)/shard_map/ppermute | solution.py:29
  66.8 4.8 %collective-permute-start.15 = (bf16[2,64,128]{2,1,0:T(8,128)(2,1)S(1)}, bf16[2,64,128]{2,1,0:T(8,128)(2,1)S(1)}, u32[]{:S(2)}, u32[]{:S(2)}) collective-permute-start(bf16[2,64,128]{2,1,0:T(8,128)(2,1)S(1)} %shard_map.80.refs_0_), channel_id=1, source_target_pairs={{0,1},{1,0},{2,3},{3,2},{4,5},{5,4},{6,7},{7,6},{8,9},{9,8},{10,11... | collective-permute-start | bytes 98312 | tf_op jit(solution)/shard_map/ppermute | solution.py:29
  67.5 4.1 %collective-permute-start.16 = (bf16[2,64,128]{2,1,0:T(8,128)(2,1)S(1)}, bf16[2,64,128]{2,1,0:T(8,128)(2,1)S(1)}, u32[]{:S(2)}, u32[]{:S(2)}) collective-permute-start(bf16[2,64,128]{2,1,0:T(8,128)(2,1)S(1)} %shard_map.80.refs_0_), channel_id=1, source_target_pairs={{0,2},{1,3},{2,0},{3,1},{4,6},{5,7},{6,4},{7,5},{8,10},{9,11},{10,... | collective-permute-start | bytes 98312 | tf_op jit(solution)/shard_map/ppermute | solution.py:29
  69.0 3.7 %collective-permute-start.17 = (bf16[2,64,128]{2,1,0:T(8,128)(2,1)S(1)}, bf16[2,64,128]{2,1,0:T(8,128)(2,1)S(1)}, u32[]{:S(2)}, u32[]{:S(2)}) collective-permute-start(bf16[2,64,128]{2,1,0:T(8,128)(2,1)S(1)} %shard_map.80.refs_0_), channel_id=1, source_target_pairs={{0,3},{1,2},{2,1},{3,0},{4,7},{5,6},{6,5},{7,4},{8,11},{9,10},{10,... | collective-permute-start | bytes 98312 | tf_op jit(solution)/shard_map/ppermute | solution.py:29

commit v15 on v14

--- a/solution.py
+++ b/solution.py
@@ -12,7 +12,7 @@
 PARAMS = pltpu.CompilerParams(vmem_limit_bytes=20 * 1024 * 1024)
 NO_COST = pl.CostEstimate(flops=0, bytes_accessed=0, transcendentals=0)
 BASE = pl.CostEstimate(flops=4 * 10**9, bytes_accessed=0, transcendentals=0)
-SHORT = pl.CostEstimate(flops=10 * 10**9, bytes_accessed=0, transcendentals=0)
+SHORT = pl.CostEstimate(flops=2 * 10**9, bytes_accessed=0, transcendentals=0)
 MIDDLE = pl.CostEstimate(flops=0 * 10**9, bytes_accessed=0, transcendentals=0)
 LONG = pl.CostEstimate(flops=6 * 10**9, bytes_accessed=0, transcendentals=0)
 ANY = pl.BlockSpec(memory_space=pl.ANY)
@@ -42,10 +42,10 @@
 
 def base_kernel(order, capacity, tokens_ref, weight_ref, *refs):
     if capacity:
-        *asked, down_ref, up_ref = refs[:8]
-        *scalars, scalar_sems, panel_sems = refs[-8:]
-        near_ref, plan_ref, *held = refs[-13:-8]
-        refs = [*refs[-17:-13], *held]
+        *asked, down_ref, up_ref = refs[:6]
+        *scalars, scalar_sems, panel_sems = refs[-6:]
+        near_ref, plan_ref, *held = refs[-11:-6]
+        refs = [*refs[-15:-11], *held]
         loads = [
             pltpu.make_async_copy(source, scalar, scalar_sems.at[i])
             for i, (source, scalar) in enumerate(zip(asked, scalars))
@@ -131,8 +131,8 @@
             jax.ShapeDtypeStruct((capacity, down.shape[1], down.shape[2] + width), down.dtype),
             jax.ShapeDtypeStruct((PLAN_ROWS * capacity,), jnp.int32),
         ]
-        scratch += [pltpu.SMEM(operand.shape, operand.dtype) for operand in operands[:6]]
-        scratch += [pltpu.SemaphoreType.DMA((6,)), pltpu.SemaphoreType.DMA((capacity, 2))]
+        scratch += [pltpu.SMEM(operand.shape, operand.dtype) for operand in operands[:4]]
+        scratch += [pltpu.SemaphoreType.DMA((4,)), pltpu.SemaphoreType.DMA((capacity, 2))]
     return pl.pallas_call(
         functools.partial(base_kernel, order, capacity),
         in_specs=[ANY] * (2 + len(operands) + len(after)),
@@ -191,12 +191,12 @@
     return kept[0], arrived[0][0]
 
 
-def pick(names_ref, table_ref, holder, holder_slots, count):
+def pick(asked_ref, index, table_ref, holder, holder_slots, count):
     blocks = [jnp.int32(0)] * count
     slots = [jnp.int32(0)] * count
     seen = jnp.int32(0)
-    for j in range(names_ref.shape[1]):
-        slot = table_ref[names_ref[0, j]]
+    for j in range(asked_ref.shape[1]):
+        slot = table_ref[asked_ref[index, j]]
         hit = lax.div(slot, jnp.int32(holder_slots)) == holder
         for k in range(count):
             chosen = hit & (seen == k)
@@ -215,22 +215,38 @@
     ]
 
 
+def join_kernel(*refs):
+    *row_refs, out_ref = refs
+    for i, row_ref in enumerate(row_refs):
+        out_ref[i : i + 1, :] = row_ref[...]
+
+
+def join(rows):
+    return pl.pallas_call(
+        join_kernel,
+        in_specs=[VMEM] * len(rows),
+        out_specs=VMEM,
+        out_shape=jax.ShapeDtypeStruct((len(rows), rows[0].shape[1]), rows[0].dtype),
+        cost_estimate=SHORT,
+    )(*rows)
+
+
 def write_plan(capacity, scalars, down_ref, up_ref, near_ref, plan_ref, sems):
     holder_slots = down_ref.shape[0]
-    names_ref, first_ref, second_ref, third_ref, table_ref, live_ref = scalars
+    names_ref, asked_ref, table_ref, live_ref = scalars
     here = lax.axis_index("pool")
     find = functools.partial(
         pick, table_ref=table_ref, holder_slots=holder_slots, count=capacity
     )
-    near_slots = find(first_ref, holder=here)[1]
+    near_slots = find(asked_ref, 0, holder=here)[1]
     copies = []
     for k, slot in enumerate(near_slots):
         copies += run_copies(panel_copies(k, slot, down_ref, up_ref, near_ref, sems))
     inner = (here == 1) | (here == 2)
-    own = find(names_ref, holder=here)
-    near = find(names_ref, holder=here ^ 1)
-    across = find(names_ref, holder=here ^ 3)
-    late = find(names_ref, holder=here ^ 2)
+    own = find(names_ref, 0, holder=here)
+    near = find(names_ref, 0, holder=here ^ 1)
+    across = find(names_ref, 0, holder=here ^ 3)
+    late = find(names_ref, 0, holder=here ^ 2)
     rows = [
         own[0],
         near[0],
@@ -238,9 +254,9 @@
         late[0],
         own[1],
         across[1],
-        find(second_ref, holder=here)[1],
-        find(third_ref, holder=here)[1],
-        find(first_ref, holder=here ^ 3)[1],
+        find(asked_ref, 1, holder=here)[1],
+        find(asked_ref, 2, holder=here)[1],
+        find(asked_ref, 0, holder=here ^ 3)[1],
         [inner.astype(jnp.int32)] * capacity,
         *[[live_ref[0, block] for block in phase[0]] for phase in (own, near, across, late)],
     ]
@@ -425,19 +441,19 @@
     inner_down = across(down, [(0, 0), (1, 2), (2, 1), (3, 3)])
     choose = INNER * capacity
     held = in_hbm(down), in_hbm(up)
-    planning = [in_hbm(names), *others, in_hbm(table), in_hbm(live), *held, capacity]
+    planning = [in_hbm(names), join(others), in_hbm(table), in_hbm(live), *held, capacity]
     *sent, kept, near_out, plan = base_parts(tokens, weight, up.shape[2], planning, [inner_up])
 
     def pack(choices, after, cost=None, carried=None):
         choices = [(row * capacity, *panels) for row, *panels in choices]
         return pack_panels(plan, choices, choose, capacity, after, cost, carried)
 
-    outer_out, near_out = pack([(TO_OUTER, *held)], [], carried=near_out)
     near = across(near_out, [(0, 1), (1, 0), (2, 3), (3, 2)])
+    base = base_sum(sent, kept)
+    outer_out = pack([(TO_OUTER, *held)], [base[0]])
     to_outer = across(outer_out, [(0, 3), (1, 1), (2, 2), (3, 0)])
-    base = base_sum(sent, kept)
     late_out = pack(
-        [(FORWARD, inner_down, inner_up), (TO_INNER, *held)], [base[0], outer_out], LONG
+        [(FORWARD, inner_down, inner_up), (TO_INNER, *held)], [outer_out], LONG
     )
     late = across(late_out, [(0, 2), (1, 0), (2, 3), (3, 1)])
 

time: 74.3 us -> 71.1 us (0.957)
  waiting for transfers between devices: 26.3 us -> 22.1 us
  starting transfers between devices: 28.1 us -> 26.6 us
  local copies, waits for them, and re-layouts: 0.01 us -> 1.3 us
  Pallas kernels: 19.5 us -> 20.5 us
    ppermute x5, waiting for transfers between devices: 14.8 us -> 11.2 us  [across(): return lax.ppermute(value, 'pool', pairs)]
    ppermute x16, starting transfers between devices: 16.6 us -> 14.5 us  [swap(): return lax.ppermute(value, axis, pairs)]
    unnamed x6 -> x14, local copies, waits for them, and re-layouts: 0.01 us -> 1.3 us
    pallas_call x0 -> x1, Pallas kernels: none -> 1.27 us  [join(): pl.pallas_call(join_kernel, in_specs=[VMEM] * len(rows), out_specs=VMEM,...]
  transfers between devices with their start and end apart: 21 -> 21, of which waited for: 8 -> 9; matrix products, arithmetic and copies ran while one was open for 0% -> 0% of each run, Pallas kernels for 24% -> 27%
where the time goes in v15:
time: 71.1 us; the launch traced here: 70.7 us
  starting transfers between devices  26.6 us (37%)
  waiting for transfers between devices  22.1 us (31%)
  Pallas kernels  20.5 us (29%)
  local copies, waits for them, and re-layouts  1.3 us (2%)
    ppermute x16, starting transfers between devices, swap(): return lax.ppermute(value, axis, pairs)  14.5 us
    ppermute x5, starting transfers between devices, across(): return lax.ppermute(value, 'pool', pairs)  12.1 us
    ppermute x5, waiting for transfers between devices, across(): return lax.ppermute(value, 'pool', pairs)  11.2 us
    ppermute x16, waiting for transfers between devices, swap(): return lax.ppermute(value, axis, pairs)  10.9 us
    pallas_call x1, Pallas kernels, base_chunks(): pl.pallas_call(functools.partial(base_kernel, order, capacity), in_specs=...  7.86 us
    pallas_call x3, Pallas kernels, combine(): pl.pallas_call(functools.partial(combine_kernel, shapes, choose, len(part...  4.38 us
    pallas_call x3, Pallas kernels, shrink(): pl.pallas_call(functools.partial(shrink_kernel, shapes, choose), in_specs...  3.42 us
    pallas_call x2, Pallas kernels, pack_panels(): pl.pallas_call(functools.partial(pack_kernel, [start for start, *_ in cho...  3.27 us
  transfers between devices with their start and end apart: 21, of which 9 were waited for; matrix products, arithmetic and copies ran while one was open for 0% of the time, Pallas kernels for 27%

profile of v15, /device:TPU:0, one launch (start us, length us, event | category | flops | bytes accessed | tf_op | source)
XLA Modules:
  0.0 70.7 jit_solution(11031349833517035525)
XLA Ops:
  0.0 3.0 %collective-permute-start = (s32[1,8]{1,0:T(1,128)}, s32[1,8]{1,0:T(1,128)S(1)}, u32[]{:S(2)}, u32[]{:S(2)}) collective-permute-start(s32[1,8]{1,0:T(1,128)} %refs_0_.1), channel_id=1, source_target_pairs={{0,4},{4,0},{8,12},{12,8},{1,5},{5,1},{9,13},{13,9},{2,6},{6,2},{1... | collective-permute-start | bytes 104 | tf_op jit(solution)/shard_map/ppermute | solution.py:29
  3.0 2.6 %collective-permute-start.1 = (s32[1,8]{1,0:T(1,128)}, s32[1,8]{1,0:T(1,128)S(1)}, u32[]{:S(2)}, u32[]{:S(2)}) collective-permute-start(s32[1,8]{1,0:T(1,128)} %refs_0_.1), channel_id=1, source_target_pairs={{0,8},{4,12},{8,0},{12,4},{1,9},{5,13},{9,1},{13,5},{2,10},{6,14},... | collective-permute-start | bytes 104 | tf_op jit(solution)/shard_map/ppermute | solution.py:29
  5.6 0.0 collective-permute-start.2
  5.6 1.6 %collective-permute-start.3 = (bf16[4,64,256]{2,1,0:T(8,128)(2,1)}, bf16[4,64,256]{2,1,0:T(8,128)(2,1)S(1)}, u32[]{:S(2)}, u32[]{:S(2)}) collective-permute-start(bf16[4,64,256]{2,1,0:T(8,128)(2,1)} %refs_6_.1), channel_id=1, source_target_pairs={{0,0},{4,8},{8,4},{12,12},{1,1},{5,9},{9,5},{13,13},{2,2},{6,10},{... | collective-permute-start | bytes 393224 | tf_op jit(solution)/shard_map/ppermute | solution.py:437
  7.2 1.9 %collective-permute-start.4 = (bf16[4,64,2048]{2,1,0:T(8,128)(2,1)}, bf16[4,64,2048]{2,1,0:T(8,128)(2,1)S(1)}, u32[]{:S(2)}, u32[]{:S(2)}) collective-permute-start(bf16[4,64,2048]{2,1,0:T(8,128)(2,1)} %bitcast.14), channel_id=1, source_target_pairs={{0,0},{4,8},{8,4},{12,12},{1,1},{5,9},{9,5},{13,13},{2,2},{6,10},{... | collective-permute-start | bytes 3145736 | tf_op jit(solution)/shard_map/ppermute | solution.py:437
  9.0 0.0 collective-permute-done.refs_0_
  9.0 0.0 collective-permute-done.1.refs_1_
  9.1 0.0 copy-start.5
  9.1 2.0 %collective-permute-done.2.refs_2_ = s32[1,8]{1,0:T(1,128)S(1)} collective-permute-done((s32[1,8]{1,0:T(1,128)}, s32[1,8]{1,0:T(1,128)S(1)}, u32[]{:S(2)}, u32[]{:S(2)}) %collective-permute-start.2) | collective-permute-done | bytes 64 | tf_op jit(solution)/shard_map/ppermute | solution.py:29
  11.1 0.0 copy-done.4
  11.1 0.0 copy-done.5
  11.1 0.6 copy-done.6
  11.7 1.3 %shard_map.73.refs_1_ = s32[3,8]{1,0:T(4,128)} custom-call(s32[1,8]{1,0:T(1,128)} %copy-done.4, s32[1,8]{1,0:T(1,128)} %copy-done.5, s32[1,8]{1,0:T(1,128)} %copy-done.6), custom_call_target="tpu_custom_call" | custom-call | flops 2000000000 | tf_op jit(solution)/shard_map/pallas_call | solution.py:225
  13.0 0.0 collective-permute-done.3.refs_6_.refs_1_
  13.0 0.7 copy-done.3
  13.6 7.9 %shard_map.74 = (f32[2,384,256]{2,1,0:T(8,128)S(1)}, f32[2,384,256]{2,1,0:T(8,128)S(1)}, f32[2,256,256]{2,1,0:T(8,128)S(1)}, f32[2,1024,256]{2,1,0:T(8,128)S(1)}...) custom-call(bf16[1024,2048]{1,0:T(8,128)(2,1)} %tokens_ref.1, bf16[2048,1024]{1,0:T(8,128)(2,1)} %weight_ref.1, ...), custom_call_target="tpu_custom_call" | custom-call | flops 4000000000 | tf_op jit(solution)/shard_map/pallas_call | solution.py:136
  21.5 0.1 collective-permute-start.5
  21.6 0.5 collective-permute-start.6
  22.1 0.1 collective-permute-start.7
  22.2 1.8 %collective-permute-start.10 = (bf16[2,64,2304]{2,1,0:T(8,128)(2,1)S(1)}, bf16[2,64,2304]{2,1,0:T(8,128)(2,1)S(1)}, u32[]{:S(2)}, u32[]{:S(2)}) collective-permute-start(bf16[2,64,2304]{2,1,0:T(8,128)(2,1)S(1)} %get-tuple-element.19), channel_id=1, source_target_pairs={{0,4},{4,0},{8,12},{12,8},{1,5},{5,1},{9,13},{13,9},{2,6},{6,2},{1... | collective-permute-start | bytes 1769480 | tf_op jit(solution)/shard_map/ppermute | solution.py:437
  24.0 1.7 %collective-permute-done.7.refs_2_ = f32[2,256,256]{2,1,0:T(8,128)S(1)} collective-permute-done((f32[2,256,256]{2,1,0:T(8,128)S(1)}, f32[2,256,256]{2,1,0:T(8,128)S(1)}, u32[]{:S(2)}, u32[]{:S(2)}) %collective-permute-start.7) | collective-permute-done | bytes 524320 | tf_op jit(solution)/shard_map/ppermute | solution.py:29
  25.7 0.0 collective-permute-done.5.refs_0_
  25.7 0.0 collective-permute-done.6.refs_1_
  25.7 0.3 shard_map.75
  26.0 1.5 %collective-permute-start.14 = (bf16[1,1024,256]{2,1,0:T(8,128)(2,1)S(1)}, bf16[1,1024,256]{2,1,0:T(8,128)(2,1)S(1)}, u32[]{:S(2)}, u32[]{:S(2)}) collective-permute-start(bf16[1,1024,256]{2,1,0:T(8,128)(2,1)S(1)} %get-tuple-element.20), channel_id=1, source_target_pairs={{0,2},{1,3},{2,0},{3,1},{4,6},{5,7},{6,4},{7,5},{8,10},{9,11},{10,... | collective-permute-start | bytes 1572872 | tf_op jit(solution)/shard_map/ppermute | solution.py:29
  27.6 1.6 %shard_map.76.refs_4_ = bf16[2,64,2304]{2,1,0:T(8,128)(2,1)S(1)} custom-call(s32[28]{0:T(128)S(1)} %get-tuple-element.13.plan_ref, bf16[4,64,2048]{2,1,0:T(8,128)(2,1)} %bitcast.16, bf16[4,64,256]{2,1,0:T(8,128)(2,1)} %refs_6_.1, f32[1024,256]{1,0:T(8,128)S(1)} %bitcast.7), custom_call_target="tpu_custom_call" | custom-call | tf_op jit(solution)/shard_map/pallas_call | solution.py:302
  29.2 0.0 copy-start
  29.2 0.0 copy-start.1
  29.2 4.5 %collective-permute-start.9 = (bf16[2,64,2304]{2,1,0:T(8,128)(2,1)S(1)}, bf16[2,64,2304]{2,1,0:T(8,128)(2,1)S(1)}, u32[]{:S(2)}, u32[]{:S(2)}) collective-permute-start(bf16[2,64,2304]{2,1,0:T(8,128)(2,1)S(1)} %shard_map.76.refs_4_), channel_id=1, source_target_pairs={{0,12},{4,4},{8,8},{12,0},{1,13},{5,5},{9,9},{13,1},{2,14},{6,6},{... | collective-permute-start | bytes 1769480 | tf_op jit(solution)/shard_map/ppermute | solution.py:437
  33.8 0.0 collective-permute-done.4.refs_0_
  33.8 1.6 %shard_map.77.refs_2_ = bf16[2,64,2304]{2,1,0:T(8,128)(2,1)S(1)} custom-call(s32[28]{0:T(128)S(1)} %get-tuple-element.13.plan_ref, bf16[4,64,2048]{2,1,0:T(8,128)(2,1)S(1)} %collective-permute-done.4.refs_0_, bf16[4,64,256]{2,1,0:T(8,128)(2,1)S(1)} %collective-permute-done.3.refs_6_.refs_1_, bf16[4,64,2048]{2,1,0:T(8,128)(2,1)} %bitcast.17, ...), custom_call_target="tpu_custom_call" | custom-call | flops 6000000000 | tf_op jit(solution)/shard_map/pallas_call | solution.py:302
  35.4 0.0 copy-start.2
  35.5 2.3 %collective-permute-start.8 = (bf16[2,64,2304]{2,1,0:T(8,128)(2,1)S(1)}, bf16[2,64,2304]{2,1,0:T(8,128)(2,1)S(1)}, u32[]{:S(2)}, u32[]{:S(2)}) collective-permute-start(bf16[2,64,2304]{2,1,0:T(8,128)(2,1)S(1)} %shard_map.77.refs_2_), channel_id=1, source_target_pairs={{0,8},{4,0},{8,12},{12,4},{1,9},{5,1},{9,13},{13,5},{2,10},{6,2},{... | collective-permute-start | bytes 1769480 | tf_op jit(solution)/shard_map/ppermute | solution.py:437
  37.8 0.3 collective-permute-done.10.refs_1_.refs_7_
  38.1 0.0 copy-done
  38.1 0.0 copy-done.1
  38.1 1.4 %shard_map.78.refs_0_ = f32[4,64,128]{2,1,0:T(8,128)S(1)} custom-call(s32[28]{0:T(128)S(1)} %get-tuple-element.13.plan_ref, bf16[8,128,2048]{2,1,0:T(8,128)(2,1)S(1)} %bitcast.4, bf16[4,64,2048]{2,1,0:T(8,128)(2,1)S(1)} %bitcast.18, bf16[2,64,2304]{2,1,0:T(8,128)(2,1)S(1)} %collective-permute-done.10.refs_1_.refs_7_, bf16[2,64,2304]{2,1,0:T(8,128)(2,1)S(1)} %shard_map.77.refs_2_), custom_call_target="tpu_custom_call" | custom-call | tf_op jit(solution)/shard_map/pallas_call | solution.py:358
  39.5 0.1 collective-permute-start.11
  39.6 1.7 %collective-permute-start.12 = (f32[4,64,128]{2,1,0:T(8,128)S(1)}, f32[4,64,128]{2,1,0:T(8,128)S(1)}, u32[]{:S(2)}, u32[]{:S(2)}) collective-permute-start(f32[4,64,128]{2,1,0:T(8,128)S(1)} %shard_map.78.refs_0_), channel_id=1, source_target_pairs={{0,2},{1,3},{2,0},{3,1},{4,6},{5,7},{6,4},{7,5},{8,10},{9,11},{10,... | collective-permute-start | bytes 393224 | tf_op jit(solution)/shard_map/ppermute | solution.py:29
  41.3 0.0 collective-permute-done.11.refs_1_
  41.3 1.0 %collective-permute-start.13 = (f32[4,64,128]{2,1,0:T(8,128)S(1)}, f32[4,64,128]{2,1,0:T(8,128)S(1)}, u32[]{:S(2)}, u32[]{:S(2)}) collective-permute-start(f32[4,64,128]{2,1,0:T(8,128)S(1)} %shard_map.78.refs_0_), channel_id=1, source_target_pairs={{0,3},{1,2},{2,1},{3,0},{4,7},{5,6},{6,5},{7,4},{8,11},{9,10},{10,... | collective-permute-start | bytes 393224 | tf_op jit(solution)/shard_map/ppermute | solution.py:29
  42.3 3.6 %collective-permute-done.12.refs_2_ = f32[4,64,128]{2,1,0:T(8,128)S(1)} collective-permute-done((f32[4,64,128]{2,1,0:T(8,128)S(1)}, f32[4,64,128]{2,1,0:T(8,128)S(1)}, u32[]{:S(2)}, u32[]{:S(2)}) %collective-permute-start.12) | collective-permute-done | bytes 131104 | tf_op jit(solution)/shard_map/ppermute | solution.py:29
  46.0 1.9 %collective-permute-done.13.refs_3_ = f32[4,64,128]{2,1,0:T(8,128)S(1)} collective-permute-done((f32[4,64,128]{2,1,0:T(8,128)S(1)}, f32[4,64,128]{2,1,0:T(8,128)S(1)}, u32[]{:S(2)}, u32[]{:S(2)}) %collective-permute-start.13) | collective-permute-done | bytes 131104 | tf_op jit(solution)/shard_map/ppermute | solution.py:29
  47.9 0.0 collective-permute-done.14
  47.9 0.0 copy-done.2
  47.9 1.5 %shard_map.79.refs_2_.refs_8_ = bf16[1024,256]{1,0:T(8,128)(2,1)} custom-call(s32[28]{0:T(128)S(1)} %get-tuple-element.13.plan_ref, f32[4,64,128]{2,1,0:T(8,128)S(1)} %shard_map.78.refs_0_, f32[4,64,128]{2,1,0:T(8,128)S(1)} %collective-permute-done.11.refs_1_, f32[4,64,128]{2,1,0:T(8,128)S(1)} %collective-permute-done.12.refs_2_, ...), custom_call_target="tpu_custom_call" | custom-call | tf_op jit(solution)/shard_map/pallas_call | solution.py:420
  49.4 4.0 %collective-permute-done.9.refs_1_.refs_7_ = bf16[2,64,2304]{2,1,0:T(8,128)(2,1)S(1)} collective-permute-done((bf16[2,64,2304]{2,1,0:T(8,128)(2,1)S(1)}, bf16[2,64,2304]{2,1,0:T(8,128)(2,1)S(1)}, u32[]{:S(2)}, u32[]{:S(2)}) %collective-permute-start.9) | collective-permute-done | bytes 589856 | tf_op jit(solution)/shard_map/ppermute | solution.py:437
  53.3 1.0 %shard_map.80.refs_1_.refs_0_ = f32[2,64,128]{2,1,0:T(8,128)S(1)} custom-call(s32[28]{0:T(128)S(1)} %get-tuple-element.13.plan_ref, bf16[8,128,2048]{2,1,0:T(8,128)(2,1)S(1)} %bitcast.5, bf16[4,64,2048]{2,1,0:T(8,128)(2,1)S(1)} %collective-permute-done.4.refs_0_, bf16[2,64,2304]{2,1,0:T(8,128)(2,1)S(1)} %collective-permute-done.9.refs_1_.refs_7_, ...), custom_call_target="tpu_custom_call" | custom-call | tf_op jit(solution)/shard_map/pallas_call | solution.py:358
  54.4 0.1 collective-permute-start.18
  54.4 1.6 %collective-permute-start.19 = (f32[2,64,128]{2,1,0:T(8,128)S(1)}, f32[2,64,128]{2,1,0:T(8,128)S(1)}, u32[]{:S(2)}, u32[]{:S(2)}) collective-permute-start(f32[2,64,128]{2,1,0:T(8,128)S(1)} %shard_map.80.refs_1_.refs_0_), channel_id=1, source_target_pairs={{0,2},{1,3},{2,0},{3,1},{4,6},{5,7},{6,4},{7,5},{8,10},{9,11},{10,... | collective-permute-start | bytes 196616 | tf_op jit(solution)/shard_map/ppermute | solution.py:29
  56.0 0.3 collective-permute-start.20
  56.3 6.9 %collective-permute-done.8.refs_0_.refs_6_ = bf16[2,64,2304]{2,1,0:T(8,128)(2,1)S(1)} collective-permute-done((bf16[2,64,2304]{2,1,0:T(8,128)(2,1)S(1)}, bf16[2,64,2304]{2,1,0:T(8,128)(2,1)S(1)}, u32[]{:S(2)}, u32[]{:S(2)}) %collective-permute-start.8) | collective-permute-done | bytes 589856 | tf_op jit(solution)/shard_map/ppermute | solution.py:437
  63.2 1.0 %shard_map.81.refs_0_ = bf16[2,64,128]{2,1,0:T(8,128)(2,1)S(1)} custom-call(s32[28]{0:T(128)S(1)} %get-tuple-element.13.plan_ref, bf16[8,128,2048]{2,1,0:T(8,128)(2,1)S(1)} %bitcast.6, bf16[2,64,2304]{2,1,0:T(8,128)(2,1)S(1)} %collective-permute-done.8.refs_0_.refs_6_, f32[2,64,128]{2,1,0:T(8,128)S(1)} %shard_map.80.refs_1_.refs_0_), custom_call_target="tpu_custom_call" | custom-call | tf_op jit(solution)/shard_map/pallas_call | solution.py:358
  64.2 0.1 collective-permute-start.15
  64.3 1.6 %collective-permute-start.16 = (bf16[2,64,128]{2,1,0:T(8,128)(2,1)S(1)}, bf16[2,64,128]{2,1,0:T(8,128)(2,1)S(1)}, u32[]{:S(2)}, u32[]{:S(2)}) collective-permute-start(bf16[2,64,128]{2,1,0:T(8,128)(2,1)S(1)} %shard_map.81.refs_0_), channel_id=1, source_target_pairs={{0,2},{1,3},{2,0},{3,1},{4,6},{5,7},{6,4},{7,5},{8,10},{9,11},{10,... | collective-permute-start | bytes 98312 | tf_op jit(solution)/shard_map/ppermute | solution.py:29
  65.9 0.0 collective-permute-done.18.refs_1_
  65.9 0.3 collective-permute-start.17
  66.2 0.0 collective-permute-done.19.refs_2_
  66.2 0.0 collective-permute-done.20.refs_3_
  66.2 1.4 %shard_map.82.refs_7_ = bf16[1024,256]{1,0:T(8,128)(2,1)} custom-call(s32[28]{0:T(128)S(1)} %get-tuple-element.13.plan_ref, f32[2,64,128]{2,1,0:T(8,128)S(1)} %shard_map.80.refs_1_.refs_0_, f32[2,64,128]{2,1,0:T(8,128)S(1)} %collective-permute-done.18.refs_1_, f32[2,64,128]{2,1,0:T(8,128)S(1)} %collective-permute-done.19.refs_2_, ...), custom_call_target="tpu_custom_call", output_to_operand_aliasing={{}: (9, {})} | custom-call | tf_op jit(solution)/shard_map/pallas_call | solution.py:420
  67.7 0.0 collective-permute-done.15.refs_1_
  67.7 0.6 collective-permute-done.16.refs_2_
  68.3 0.9 %collective-permute-done.17.refs_3_ = bf16[2,64,128]{2,1,0:T(8,128)(2,1)S(1)} collective-permute-done((bf16[2,64,128]{2,1,0:T(8,128)(2,1)S(1)}, bf16[2,64,128]{2,1,0:T(8,128)(2,1)S(1)}, u32[]{:S(2)}, u32[]{:S(2)}) %collective-permute-start.17) | collective-permute-done | bytes 32800 | tf_op jit(solution)/shard_map/ppermute | solution.py:29
  69.2 1.4 %shard_map.83 = bf16[1024,256]{1,0:T(8,128)(2,1)} custom-call(s32[28]{0:T(128)S(1)} %get-tuple-element.13.plan_ref, bf16[2,64,128]{2,1,0:T(8,128)(2,1)S(1)} %shard_map.81.refs_0_, bf16[2,64,128]{2,1,0:T(8,128)(2,1)S(1)} %collective-permute-done.15.refs_1_, bf16[2,64,128]{2,1,0:T(8,128)(2,1)S(1)} %collective-permute-done.16.refs_2_, ...), custom_call_target="tpu_custom_call", output_to_operand_aliasing={{}: (8, {})} | custom-call | tf_op jit(solution)/shard_map/pallas_call | solution.py:420
  (3 shorter events, 0.0 us)
Async XLA Ops:
  0.0 9.0 %collective-permute-start = (s32[1,8]{1,0:T(1,128)}, s32[1,8]{1,0:T(1,128)S(1)}, u32[]{:S(2)}, u32[]{:S(2)}) collective-permute-start(s32[1,8]{1,0:T(1,128)} %refs_0_.1), channel_id=1, source_target_pairs={{0,4},{4,0},{8,12},{12,8},{1,5},{5,1},{9,13},{13,9},{2,6},{6,2},{1... | collective-permute-start | bytes 104 | tf_op jit(solution)/shard_map/ppermute | solution.py:29
  3.0 6.0 %collective-permute-start.1 = (s32[1,8]{1,0:T(1,128)}, s32[1,8]{1,0:T(1,128)S(1)}, u32[]{:S(2)}, u32[]{:S(2)}) collective-permute-start(s32[1,8]{1,0:T(1,128)} %refs_0_.1), channel_id=1, source_target_pairs={{0,8},{4,12},{8,0},{12,4},{1,9},{5,13},{9,1},{13,5},{2,10},{6,14},... | collective-permute-start | bytes 104 | tf_op jit(solution)/shard_map/ppermute | solution.py:29
  5.6 5.5 %collective-permute-start.2 = (s32[1,8]{1,0:T(1,128)}, s32[1,8]{1,0:T(1,128)S(1)}, u32[]{:S(2)}, u32[]{:S(2)}) collective-permute-start(s32[1,8]{1,0:T(1,128)} %refs_0_.1), channel_id=1, source_target_pairs={{0,12},{4,8},{8,4},{12,0},{1,13},{5,9},{9,5},{13,1},{2,14},{6,10},... | collective-permute-start | bytes 104 | tf_op jit(solution)/shard_map/ppermute | solution.py:29
  5.6 7.3 %collective-permute-start.3 = (bf16[4,64,256]{2,1,0:T(8,128)(2,1)}, bf16[4,64,256]{2,1,0:T(8,128)(2,1)S(1)}, u32[]{:S(2)}, u32[]{:S(2)}) collective-permute-start(bf16[4,64,256]{2,1,0:T(8,128)(2,1)} %refs_6_.1), channel_id=1, source_target_pairs={{0,0},{4,8},{8,4},{12,12},{1,1},{5,9},{9,5},{13,13},{2,2},{6,10},{... | collective-permute-start | bytes 393224 | tf_op jit(solution)/shard_map/ppermute | solution.py:437
  7.2 26.6 %collective-permute-start.4 = (bf16[4,64,2048]{2,1,0:T(8,128)(2,1)}, bf16[4,64,2048]{2,1,0:T(8,128)(2,1)S(1)}, u32[]{:S(2)}, u32[]{:S(2)}) collective-permute-start(bf16[4,64,2048]{2,1,0:T(8,128)(2,1)} %bitcast.14), channel_id=1, source_target_pairs={{0,0},{4,8},{8,4},{12,12},{1,1},{5,9},{9,5},{13,13},{2,2},{6,10},{... | collective-permute-start | bytes 3145736 | tf_op jit(solution)/shard_map/ppermute | solution.py:437
  9.0 2.0 %copy-start.4 = (s32[1,8]{1,0:T(1,128)}, s32[1,8]{1,0:T(1,128)S(1)}, u32[]{:S(2)}) copy-start(s32[1,8]{1,0:T(1,128)S(1)} %collective-permute-done.refs_0_) | copy-start | bytes 100
  9.1 2.0 %copy-start.5 = (s32[1,8]{1,0:T(1,128)}, s32[1,8]{1,0:T(1,128)S(1)}, u32[]{:S(2)}) copy-start(s32[1,8]{1,0:T(1,128)S(1)} %collective-permute-done.1.refs_1_) | copy-start | bytes 100
  11.1 0.6 copy-start.6
  13.0 0.7 copy-start.3
  21.5 4.2 %collective-permute-start.5 = (f32[2,384,256]{2,1,0:T(8,128)S(1)}, f32[2,384,256]{2,1,0:T(8,128)S(1)}, u32[]{:S(2)}, u32[]{:S(2)}) collective-permute-start(f32[2,384,256]{2,1,0:T(8,128)S(1)} %get-tuple-element.15), channel_id=1, source_target_pairs={{0,1},{1,0},{2,3},{3,2},{4,5},{5,4},{6,7},{7,6},{8,9},{9,8},{10,11... | collective-permute-start | bytes 2359304 | tf_op jit(solution)/shard_map/ppermute | solution.py:29
  21.6 4.2 %collective-permute-start.6 = (f32[2,384,256]{2,1,0:T(8,128)S(1)}, f32[2,384,256]{2,1,0:T(8,128)S(1)}, u32[]{:S(2)}, u32[]{:S(2)}) collective-permute-start(f32[2,384,256]{2,1,0:T(8,128)S(1)} %get-tuple-element.16), channel_id=1, source_target_pairs={{0,1},{1,0},{2,3},{3,2},{4,5},{5,4},{6,7},{7,6},{8,9},{9,8},{10,11... | collective-permute-start | bytes 2359304 | tf_op jit(solution)/shard_map/ppermute | solution.py:29
  22.1 3.6 %collective-permute-start.7 = (f32[2,256,256]{2,1,0:T(8,128)S(1)}, f32[2,256,256]{2,1,0:T(8,128)S(1)}, u32[]{:S(2)}, u32[]{:S(2)}) collective-permute-start(f32[2,256,256]{2,1,0:T(8,128)S(1)} %get-tuple-element.17), channel_id=1, source_target_pairs={{0,1},{1,0},{2,3},{3,2},{4,5},{5,4},{6,7},{7,6},{8,9},{9,8},{10,11... | collective-permute-start | bytes 1572872 | tf_op jit(solution)/shard_map/ppermute | solution.py:29
  22.2 16.0 %collective-permute-start.10 = (bf16[2,64,2304]{2,1,0:T(8,128)(2,1)S(1)}, bf16[2,64,2304]{2,1,0:T(8,128)(2,1)S(1)}, u32[]{:S(2)}, u32[]{:S(2)}) collective-permute-start(bf16[2,64,2304]{2,1,0:T(8,128)(2,1)S(1)} %get-tuple-element.19), channel_id=1, source_target_pairs={{0,4},{4,0},{8,12},{12,8},{1,5},{5,1},{9,13},{13,9},{2,6},{6,2},{1... | collective-permute-start | bytes 1769480 | tf_op jit(solution)/shard_map/ppermute | solution.py:437
  26.0 21.8 %collective-permute-start.14 = (bf16[1,1024,256]{2,1,0:T(8,128)(2,1)S(1)}, bf16[1,1024,256]{2,1,0:T(8,128)(2,1)S(1)}, u32[]{:S(2)}, u32[]{:S(2)}) collective-permute-start(bf16[1,1024,256]{2,1,0:T(8,128)(2,1)S(1)} %get-tuple-element.20), channel_id=1, source_target_pairs={{0,2},{1,3},{2,0},{3,1},{4,6},{5,7},{6,4},{7,5},{8,10},{9,11},{10,... | collective-permute-start | bytes 1572872 | tf_op jit(solution)/shard_map/ppermute | solution.py:29
  29.2 8.9 %copy-start = (bf16[1024,2048]{1,0:T(8,128)(2,1)S(1)}, bf16[1024,2048]{1,0:T(8,128)(2,1)}, u32[]{:S(2)}) copy-start(bf16[1024,2048]{1,0:T(8,128)(2,1)} %tokens_ref.1) | copy-start | bytes 12582916
  29.2 8.9 %copy-start.1 = (bf16[4,2048,64]{1,2,0:T(8,128)(2,1)S(1)}, bf16[4,2048,64]{1,2,0:T(8,128)(2,1)}, u32[]{:S(2)}) copy-start(bf16[4,2048,64]{1,2,0:T(8,128)(2,1)} %param.9) | copy-start | bytes 3145732
  29.2 24.1 %collective-permute-start.9 = (bf16[2,64,2304]{2,1,0:T(8,128)(2,1)S(1)}, bf16[2,64,2304]{2,1,0:T(8,128)(2,1)S(1)}, u32[]{:S(2)}, u32[]{:S(2)}) collective-permute-start(bf16[2,64,2304]{2,1,0:T(8,128)(2,1)S(1)} %shard_map.76.refs_4_), channel_id=1, source_target_pairs={{0,12},{4,4},{8,8},{12,0},{1,13},{5,5},{9,9},{13,1},{2,14},{6,6},{... | collective-permute-start | bytes 1769480 | tf_op jit(solution)/shard_map/ppermute | solution.py:437
  35.4 12.4 %copy-start.2 = (bf16[4,64,256]{2,1,0:T(8,128)(2,1)S(1)}, bf16[4,64,256]{2,1,0:T(8,128)(2,1)}, u32[]{:S(2)}) copy-start(bf16[4,64,256]{2,1,0:T(8,128)(2,1)} %refs_6_.1) | copy-start | bytes 393220
  35.5 27.8 %collective-permute-start.8 = (bf16[2,64,2304]{2,1,0:T(8,128)(2,1)S(1)}, bf16[2,64,2304]{2,1,0:T(8,128)(2,1)S(1)}, u32[]{:S(2)}, u32[]{:S(2)}) collective-permute-start(bf16[2,64,2304]{2,1,0:T(8,128)(2,1)S(1)} %shard_map.77.refs_2_), channel_id=1, source_target_pairs={{0,8},{4,0},{8,12},{12,4},{1,9},{5,1},{9,13},{13,5},{2,10},{6,2},{... | collective-permute-start | bytes 1769480 | tf_op jit(solution)/shard_map/ppermute | solution.py:437
  39.5 1.8 %collective-permute-start.11 = (f32[4,64,128]{2,1,0:T(8,128)S(1)}, f32[4,64,128]{2,1,0:T(8,128)S(1)}, u32[]{:S(2)}, u32[]{:S(2)}) collective-permute-start(f32[4,64,128]{2,1,0:T(8,128)S(1)} %shard_map.78.refs_0_), channel_id=1, source_target_pairs={{0,1},{1,0},{2,3},{3,2},{4,5},{5,4},{6,7},{7,6},{8,9},{9,8},{10,11... | collective-permute-start | bytes 393224 | tf_op jit(solution)/shard_map/ppermute | solution.py:29
  39.6 6.4 %collective-permute-start.12 = (f32[4,64,128]{2,1,0:T(8,128)S(1)}, f32[4,64,128]{2,1,0:T(8,128)S(1)}, u32[]{:S(2)}, u32[]{:S(2)}) collective-permute-start(f32[4,64,128]{2,1,0:T(8,128)S(1)} %shard_map.78.refs_0_), channel_id=1, source_target_pairs={{0,2},{1,3},{2,0},{3,1},{4,6},{5,7},{6,4},{7,5},{8,10},{9,11},{10,... | collective-permute-start | bytes 393224 | tf_op jit(solution)/shard_map/ppermute | solution.py:29
  41.3 6.6 %collective-permute-start.13 = (f32[4,64,128]{2,1,0:T(8,128)S(1)}, f32[4,64,128]{2,1,0:T(8,128)S(1)}, u32[]{:S(2)}, u32[]{:S(2)}) collective-permute-start(f32[4,64,128]{2,1,0:T(8,128)S(1)} %shard_map.78.refs_0_), channel_id=1, source_target_pairs={{0,3},{1,2},{2,1},{3,0},{4,7},{5,6},{6,5},{7,4},{8,11},{9,10},{10,... | collective-permute-start | bytes 393224 | tf_op jit(solution)/shard_map/ppermute | solution.py:29
  54.4 11.5 %collective-permute-start.18 = (f32[2,64,128]{2,1,0:T(8,128)S(1)}, f32[2,64,128]{2,1,0:T(8,128)S(1)}, u32[]{:S(2)}, u32[]{:S(2)}) collective-permute-start(f32[2,64,128]{2,1,0:T(8,128)S(1)} %shard_map.80.refs_1_.refs_0_), channel_id=1, source_target_pairs={{0,1},{1,0},{2,3},{3,2},{4,5},{5,4},{6,7},{7,6},{8,9},{9,8},{10,11... | collective-permute-start | bytes 196616 | tf_op jit(solution)/shard_map/ppermute | solution.py:29
  54.4 11.7 %collective-permute-start.19 = (f32[2,64,128]{2,1,0:T(8,128)S(1)}, f32[2,64,128]{2,1,0:T(8,128)S(1)}, u32[]{:S(2)}, u32[]{:S(2)}) collective-permute-start(f32[2,64,128]{2,1,0:T(8,128)S(1)} %shard_map.80.refs_1_.refs_0_), channel_id=1, source_target_pairs={{0,2},{1,3},{2,0},{3,1},{4,6},{5,7},{6,4},{7,5},{8,10},{9,11},{10,... | collective-permute-start | bytes 196616 | tf_op jit(solution)/shard_map/ppermute | solution.py:29
  56.0 10.2 %collective-permute-start.20 = (f32[2,64,128]{2,1,0:T(8,128)S(1)}, f32[2,64,128]{2,1,0:T(8,128)S(1)}, u32[]{:S(2)}, u32[]{:S(2)}) collective-permute-start(f32[2,64,128]{2,1,0:T(8,128)S(1)} %shard_map.80.refs_1_.refs_0_), channel_id=1, source_target_pairs={{0,3},{1,2},{2,1},{3,0},{4,7},{5,6},{6,5},{7,4},{8,11},{9,10},{10,... | collective-permute-start | bytes 196616 | tf_op jit(solution)/shard_map/ppermute | solution.py:29
  64.2 3.4 %collective-permute-start.15 = (bf16[2,64,128]{2,1,0:T(8,128)(2,1)S(1)}, bf16[2,64,128]{2,1,0:T(8,128)(2,1)S(1)}, u32[]{:S(2)}, u32[]{:S(2)}) collective-permute-start(bf16[2,64,128]{2,1,0:T(8,128)(2,1)S(1)} %shard_map.81.refs_0_), channel_id=1, source_target_pairs={{0,1},{1,0},{2,3},{3,2},{4,5},{5,4},{6,7},{7,6},{8,9},{9,8},{10,11... | collective-permute-start | bytes 98312 | tf_op jit(solution)/shard_map/ppermute | solution.py:29
  64.3 4.0 %collective-permute-start.16 = (bf16[2,64,128]{2,1,0:T(8,128)(2,1)S(1)}, bf16[2,64,128]{2,1,0:T(8,128)(2,1)S(1)}, u32[]{:S(2)}, u32[]{:S(2)}) collective-permute-start(bf16[2,64,128]{2,1,0:T(8,128)(2,1)S(1)} %shard_map.81.refs_0_), channel_id=1, source_target_pairs={{0,2},{1,3},{2,0},{3,1},{4,6},{5,7},{6,4},{7,5},{8,10},{9,11},{10,... | collective-permute-start | bytes 98312 | tf_op jit(solution)/shard_map/ppermute | solution.py:29
  65.9 3.3 %collective-permute-start.17 = (bf16[2,64,128]{2,1,0:T(8,128)(2,1)S(1)}, bf16[2,64,128]{2,1,0:T(8,128)(2,1)S(1)}, u32[]{:S(2)}, u32[]{:S(2)}) collective-permute-start(bf16[2,64,128]{2,1,0:T(8,128)(2,1)S(1)} %shard_map.81.refs_0_), channel_id=1, source_target_pairs={{0,3},{1,2},{2,1},{3,0},{4,7},{5,6},{6,5},{7,4},{8,11},{9,10},{10,... | collective-permute-start | bytes 98312 | tf_op jit(solution)/shard_map/ppermute | solution.py:29

commit v16 on v15

--- a/solution.py
+++ b/solution.py
@@ -42,10 +42,10 @@
 
 def base_kernel(order, capacity, tokens_ref, weight_ref, *refs):
     if capacity:
-        *asked, down_ref, up_ref = refs[:6]
-        *scalars, scalar_sems, panel_sems = refs[-6:]
-        near_ref, plan_ref, *held = refs[-11:-6]
-        refs = [*refs[-15:-11], *held]
+        *asked, down_ref, up_ref = refs[:4]
+        *scalars, scalar_sems, panel_sems = refs[-4:]
+        near_ref, plan_ref, *held = refs[-9:-4]
+        refs = [*refs[-13:-9], *held]
         loads = [
             pltpu.make_async_copy(source, scalar, scalar_sems.at[i])
             for i, (source, scalar) in enumerate(zip(asked, scalars))
@@ -131,8 +131,8 @@
             jax.ShapeDtypeStruct((capacity, down.shape[1], down.shape[2] + width), down.dtype),
             jax.ShapeDtypeStruct((PLAN_ROWS * capacity,), jnp.int32),
         ]
-        scratch += [pltpu.SMEM(operand.shape, operand.dtype) for operand in operands[:4]]
-        scratch += [pltpu.SemaphoreType.DMA((4,)), pltpu.SemaphoreType.DMA((capacity, 2))]
+        scratch += [pltpu.SMEM(operand.shape, operand.dtype) for operand in operands[:2]]
+        scratch += [pltpu.SemaphoreType.DMA((2,)), pltpu.SemaphoreType.DMA((capacity, 2))]
     return pl.pallas_call(
         functools.partial(base_kernel, order, capacity),
         in_specs=[ANY] * (2 + len(operands) + len(after)),
@@ -191,12 +191,12 @@
     return kept[0], arrived[0][0]
 
 
-def pick(asked_ref, index, table_ref, holder, holder_slots, count):
+def pick(asked_ref, index, holder, holder_slots, count):
     blocks = [jnp.int32(0)] * count
     slots = [jnp.int32(0)] * count
     seen = jnp.int32(0)
     for j in range(asked_ref.shape[1]):
-        slot = table_ref[asked_ref[index, j]]
+        slot = asked_ref[index, j]
         hit = lax.div(slot, jnp.int32(holder_slots)) == holder
         for k in range(count):
             chosen = hit & (seen == k)
@@ -215,38 +215,22 @@
     ]
 
 
-def join_kernel(*refs):
-    *row_refs, out_ref = refs
-    for i, row_ref in enumerate(row_refs):
-        out_ref[i : i + 1, :] = row_ref[...]
-
-
-def join(rows):
-    return pl.pallas_call(
-        join_kernel,
-        in_specs=[VMEM] * len(rows),
-        out_specs=VMEM,
-        out_shape=jax.ShapeDtypeStruct((len(rows), rows[0].shape[1]), rows[0].dtype),
-        cost_estimate=SHORT,
-    )(*rows)
-
-
 def write_plan(capacity, scalars, down_ref, up_ref, near_ref, plan_ref, sems):
     holder_slots = down_ref.shape[0]
-    names_ref, asked_ref, table_ref, live_ref = scalars
+    asked_ref, live_ref = scalars
     here = lax.axis_index("pool")
     find = functools.partial(
-        pick, table_ref=table_ref, holder_slots=holder_slots, count=capacity
+        pick, holder_slots=holder_slots, count=capacity
     )
-    near_slots = find(asked_ref, 0, holder=here)[1]
+    near_slots = find(asked_ref, 1, holder=here)[1]
     copies = []
     for k, slot in enumerate(near_slots):
         copies += run_copies(panel_copies(k, slot, down_ref, up_ref, near_ref, sems))
     inner = (here == 1) | (here == 2)
-    own = find(names_ref, 0, holder=here)
-    near = find(names_ref, 0, holder=here ^ 1)
-    across = find(names_ref, 0, holder=here ^ 3)
-    late = find(names_ref, 0, holder=here ^ 2)
+    own = find(asked_ref, 0, holder=here)
+    near = find(asked_ref, 0, holder=here ^ 1)
+    across = find(asked_ref, 0, holder=here ^ 3)
+    late = find(asked_ref, 0, holder=here ^ 2)
     rows = [
         own[0],
         near[0],
@@ -254,9 +238,9 @@
         late[0],
         own[1],
         across[1],
-        find(asked_ref, 1, holder=here)[1],
         find(asked_ref, 2, holder=here)[1],
-        find(asked_ref, 0, holder=here ^ 3)[1],
+        find(asked_ref, 3, holder=here)[1],
+        find(asked_ref, 1, holder=here ^ 3)[1],
         [inner.astype(jnp.int32)] * capacity,
         *[[live_ref[0, block] for block in phase[0]] for phase in (own, near, across, late)],
     ]
@@ -441,7 +425,10 @@
     inner_down = across(down, [(0, 0), (1, 2), (2, 1), (3, 3)])
     choose = INNER * capacity
     held = in_hbm(down), in_hbm(up)
-    planning = [in_hbm(names), join(others), in_hbm(table), in_hbm(live), *held, capacity]
+    asked = jnp.concatenate([names, *others])
+    hits = asked[:, :, None] == jnp.arange(table.shape[0], dtype=jnp.int32)
+    asked_slots = jnp.sum(jnp.where(hits, table, 0), axis=2)
+    planning = [asked_slots, in_hbm(live), *held, capacity]
     *sent, kept, near_out, plan = base_parts(tokens, weight, up.shape[2], planning, [inner_up])
 
     def pack(choices, after, cost=None, carried=None):

time: 71.1 us -> 70.4 us (level)
  other arithmetic: 0 us -> 1.53 us
  Pallas kernels: 20.5 us -> 19.2 us
  local copies, waits for them, and re-layouts: 1.3 us -> 0.02 us
    unnamed x14 -> x6, local copies, waits for them, and re-layouts: 1.3 us -> 0.02 us
    pallas_call x1 -> x0, Pallas kernels: 1.27 us -> none  [join(): pl.pallas_call(join_kernel, in_specs=[VMEM] * len(rows), out_specs=VMEM,...]
    ppermute x5, waiting for transfers between devices: 11.2 us -> 10.1 us  [across(): return lax.ppermute(value, 'pool', pairs)]
    reduce_sum x0 -> x1, other arithmetic: none -> 0.86 us  [on_line_of_four(): asked_slots = jnp.sum(jnp.where(hits, table, 0), axis=2)]
  transfers between devices with their start and end apart: 21 -> 21, of which waited for: 9 -> 8; matrix products, arithmetic and copies ran while one was open for 0% -> 2% of each run, Pallas kernels for 27% -> 26%
where the time goes in v16:
time: 70.4 us; the launch traced here: 69.6 us
  starting transfers between devices  27.1 us (38%)
  waiting for transfers between devices  21.6 us (31%)
  Pallas kernels  19.2 us (27%)
  other arithmetic  1.53 us (2%)
    ppermute x16, starting transfers between devices, swap(): return lax.ppermute(value, axis, pairs)  14.3 us
    ppermute x5, starting transfers between devices, across(): return lax.ppermute(value, 'pool', pairs)  12.7 us
    ppermute x16, waiting for transfers between devices, swap(): return lax.ppermute(value, axis, pairs)  11.5 us
    ppermute x5, waiting for transfers between devices, across(): return lax.ppermute(value, 'pool', pairs)  10.1 us
    pallas_call x1, Pallas kernels, base_chunks(): pl.pallas_call(functools.partial(base_kernel, order, capacity), in_specs=...  7.86 us
    pallas_call x3, Pallas kernels, combine(): pl.pallas_call(functools.partial(combine_kernel, shapes, choose, len(part...  4.38 us
    pallas_call x3, Pallas kernels, shrink(): pl.pallas_call(functools.partial(shrink_kernel, shapes, choose), in_specs...  3.42 us
    pallas_call x2, Pallas kernels, pack_panels(): pl.pallas_call(functools.partial(pack_kernel, [start for start, *_ in cho...  3.27 us
  transfers between devices with their start and end apart: 21, of which 8 were waited for; matrix products, arithmetic and copies ran while one was open for 2% of the time, Pallas kernels for 26%

profile of v16, /device:TPU:0, one launch (start us, length us, event | category | flops | bytes accessed | tf_op | source)
XLA Modules:
  0.0 69.6 jit_solution(13113694442908373937)
XLA Ops:
  0.0 3.0 %collective-permute-start = (s32[1,8]{1,0:T(1,128)}, s32[1,8]{1,0:T(1,128)S(1)}, u32[]{:S(2)}, u32[]{:S(2)}) collective-permute-start(s32[1,8]{1,0:T(1,128)} %param.11), channel_id=1, source_target_pairs={{0,4},{4,0},{8,12},{12,8},{1,5},{5,1},{9,13},{13,9},{2,6},{6,2},{1... | collective-permute-start | bytes 104 | tf_op jit(solution)/shard_map/ppermute | solution.py:29
  3.0 2.6 %collective-permute-start.1 = (s32[1,8]{1,0:T(1,128)}, s32[1,8]{1,0:T(1,128)S(1)}, u32[]{:S(2)}, u32[]{:S(2)}) collective-permute-start(s32[1,8]{1,0:T(1,128)} %param.11), channel_id=1, source_target_pairs={{0,8},{4,12},{8,0},{12,4},{1,9},{5,13},{9,1},{13,5},{2,10},{6,14},... | collective-permute-start | bytes 104 | tf_op jit(solution)/shard_map/ppermute | solution.py:29
  5.6 0.0 collective-permute-start.2
  5.6 1.6 %collective-permute-start.3 = (bf16[4,64,256]{2,1,0:T(8,128)(2,1)}, bf16[4,64,256]{2,1,0:T(8,128)(2,1)S(1)}, u32[]{:S(2)}, u32[]{:S(2)}) collective-permute-start(bf16[4,64,256]{2,1,0:T(8,128)(2,1)} %refs_6_.1), channel_id=1, source_target_pairs={{0,0},{4,8},{8,4},{12,12},{1,1},{5,9},{9,5},{13,13},{2,2},{6,10},{... | collective-permute-start | bytes 393224 | tf_op jit(solution)/shard_map/ppermute | solution.py:421
  7.2 1.9 %collective-permute-start.4 = (bf16[4,64,2048]{2,1,0:T(8,128)(2,1)}, bf16[4,64,2048]{2,1,0:T(8,128)(2,1)S(1)}, u32[]{:S(2)}, u32[]{:S(2)}) collective-permute-start(bf16[4,64,2048]{2,1,0:T(8,128)(2,1)} %bitcast.14), channel_id=1, source_target_pairs={{0,0},{4,8},{8,4},{12,12},{1,1},{5,9},{9,5},{13,13},{2,2},{6,10},{... | collective-permute-start | bytes 3145736 | tf_op jit(solution)/shard_map/ppermute | solution.py:421
  9.0 0.0 collective-permute-done
  9.0 0.0 collective-permute-done.1
  9.1 2.0 %collective-permute-done.2 = s32[1,8]{1,0:T(1,128)S(1)} collective-permute-done((s32[1,8]{1,0:T(1,128)}, s32[1,8]{1,0:T(1,128)S(1)}, u32[]{:S(2)}, u32[]{:S(2)}) %collective-permute-start.2) | collective-permute-done | bytes 64 | tf_op jit(solution)/shard_map/ppermute | solution.py:29
  11.1 0.7 pad_add_fusion
  11.8 0.9 %select_reduce_fusion.refs_0_ = s32[4,8]{1,0:T(4,128)S(1)} fusion(s32[16]{0:T(128)} %param.12, s32[4,8]{1,0:T(4,128)S(1)} %pad_add_fusion), kind=kLoop, calls=%fused_computation | loop fusion | flops 1504 | bytes 320 | tf_op jit(solution)/shard_map/reduce_sum | solution.py:430
  12.6 0.0 collective-permute-done.3.refs_4_.refs_1_.refs_6_
  12.6 7.9 %shard_map.73 = (f32[2,384,256]{2,1,0:T(8,128)S(1)}, f32[2,384,256]{2,1,0:T(8,128)S(1)}, f32[2,256,256]{2,1,0:T(8,128)S(1)}, f32[2,1024,256]{2,1,0:T(8,128)S(1)}...) custom-call(bf16[1024,2048]{1,0:T(8,128)(2,1)} %tokens_ref.1, bf16[2048,1024]{1,0:T(8,128)(2,1)} %weight_ref.1, ...), custom_call_target="tpu_custom_call" | custom-call | flops 4000000000 | tf_op jit(solution)/shard_map/pallas_call | solution.py:136
  20.5 0.1 collective-permute-start.5
  20.6 0.5 collective-permute-start.6
  21.1 0.1 collective-permute-start.7
  21.1 1.4 %collective-permute-start.10 = (bf16[2,64,2304]{2,1,0:T(8,128)(2,1)S(1)}, bf16[2,64,2304]{2,1,0:T(8,128)(2,1)S(1)}, u32[]{:S(2)}, u32[]{:S(2)}) collective-permute-start(bf16[2,64,2304]{2,1,0:T(8,128)(2,1)S(1)} %get-tuple-element.19), channel_id=1, source_target_pairs={{0,4},{4,0},{8,12},{12,8},{1,5},{5,1},{9,13},{13,9},{2,6},{6,2},{1... | collective-permute-start | bytes 1769480 | tf_op jit(solution)/shard_map/ppermute | solution.py:421
  22.6 2.1 %collective-permute-done.7.refs_2_ = f32[2,256,256]{2,1,0:T(8,128)S(1)} collective-permute-done((f32[2,256,256]{2,1,0:T(8,128)S(1)}, f32[2,256,256]{2,1,0:T(8,128)S(1)}, u32[]{:S(2)}, u32[]{:S(2)}) %collective-permute-start.7) | collective-permute-done | bytes 524320 | tf_op jit(solution)/shard_map/ppermute | solution.py:29
  24.7 0.0 collective-permute-done.5.refs_0_
  24.7 0.0 collective-permute-done.6.refs_1_
  24.7 0.3 shard_map.74
  25.0 1.6 %collective-permute-start.14 = (bf16[1,1024,256]{2,1,0:T(8,128)(2,1)S(1)}, bf16[1,1024,256]{2,1,0:T(8,128)(2,1)S(1)}, u32[]{:S(2)}, u32[]{:S(2)}) collective-permute-start(bf16[1,1024,256]{2,1,0:T(8,128)(2,1)S(1)} %get-tuple-element.20), channel_id=1, source_target_pairs={{0,2},{1,3},{2,0},{3,1},{4,6},{5,7},{6,4},{7,5},{8,10},{9,11},{10,... | collective-permute-start | bytes 1572872 | tf_op jit(solution)/shard_map/ppermute | solution.py:29
  26.6 1.6 %shard_map.75.refs_4_ = bf16[2,64,2304]{2,1,0:T(8,128)(2,1)S(1)} custom-call(s32[28]{0:T(128)S(1)} %get-tuple-element.13.plan_ref, bf16[4,64,2048]{2,1,0:T(8,128)(2,1)} %bitcast.16, bf16[4,64,256]{2,1,0:T(8,128)(2,1)} %refs_6_.1, f32[1024,256]{1,0:T(8,128)S(1)} %bitcast.7), custom_call_target="tpu_custom_call" | custom-call | tf_op jit(solution)/shard_map/pallas_call | solution.py:286
  28.2 0.0 copy-start
  28.2 0.0 copy-start.1
  28.2 4.0 %collective-permute-start.9 = (bf16[2,64,2304]{2,1,0:T(8,128)(2,1)S(1)}, bf16[2,64,2304]{2,1,0:T(8,128)(2,1)S(1)}, u32[]{:S(2)}, u32[]{:S(2)}) collective-permute-start(bf16[2,64,2304]{2,1,0:T(8,128)(2,1)S(1)} %shard_map.75.refs_4_), channel_id=1, source_target_pairs={{0,12},{4,4},{8,8},{12,0},{1,13},{5,5},{9,9},{13,1},{2,14},{6,6},{... | collective-permute-start | bytes 1769480 | tf_op jit(solution)/shard_map/ppermute | solution.py:421
  32.2 0.0 collective-permute-done.4.refs_0_
  32.2 1.6 %shard_map.76.refs_2_ = bf16[2,64,2304]{2,1,0:T(8,128)(2,1)S(1)} custom-call(s32[28]{0:T(128)S(1)} %get-tuple-element.13.plan_ref, bf16[4,64,2048]{2,1,0:T(8,128)(2,1)S(1)} %collective-permute-done.4.refs_0_, bf16[4,64,256]{2,1,0:T(8,128)(2,1)S(1)} %collective-permute-done.3.refs_4_.refs_1_.refs_6_, bf16[4,64,2048]{2,1,0:T(8,128)(2,1)} %bitcast.17, ...), custom_call_target="tpu_custom_call" | custom-call | flops 6000000000 | tf_op jit(solution)/shard_map/pallas_call | solution.py:286
  33.9 0.0 copy-start.2
  33.9 3.9 %collective-permute-start.8 = (bf16[2,64,2304]{2,1,0:T(8,128)(2,1)S(1)}, bf16[2,64,2304]{2,1,0:T(8,128)(2,1)S(1)}, u32[]{:S(2)}, u32[]{:S(2)}) collective-permute-start(bf16[2,64,2304]{2,1,0:T(8,128)(2,1)S(1)} %shard_map.76.refs_2_), channel_id=1, source_target_pairs={{0,8},{4,0},{8,12},{12,4},{1,9},{5,1},{9,13},{13,5},{2,10},{6,2},{... | collective-permute-start | bytes 1769480 | tf_op jit(solution)/shard_map/ppermute | solution.py:421
  37.8 0.0 collective-permute-done.10.refs_1_.refs_7_
  37.8 0.0 copy-done
  37.8 0.0 copy-done.1
  37.8 1.4 %shard_map.77.refs_0_ = f32[4,64,128]{2,1,0:T(8,128)S(1)} custom-call(s32[28]{0:T(128)S(1)} %get-tuple-element.13.plan_ref, bf16[8,128,2048]{2,1,0:T(8,128)(2,1)S(1)} %bitcast.4, bf16[4,64,2048]{2,1,0:T(8,128)(2,1)S(1)} %bitcast.18, bf16[2,64,2304]{2,1,0:T(8,128)(2,1)S(1)} %collective-permute-done.10.refs_1_.refs_7_, bf16[2,64,2304]{2,1,0:T(8,128)(2,1)S(1)} %shard_map.76.refs_2_), custom_call_target="tpu_custom_call" | custom-call | tf_op jit(solution)/shard_map/pallas_call | solution.py:342
  39.2 0.1 collective-permute-start.11
  39.3 1.6 %collective-permute-start.12 = (f32[4,64,128]{2,1,0:T(8,128)S(1)}, f32[4,64,128]{2,1,0:T(8,128)S(1)}, u32[]{:S(2)}, u32[]{:S(2)}) collective-permute-start(f32[4,64,128]{2,1,0:T(8,128)S(1)} %shard_map.77.refs_0_), channel_id=1, source_target_pairs={{0,2},{1,3},{2,0},{3,1},{4,6},{5,7},{6,4},{7,5},{8,10},{9,11},{10,... | collective-permute-start | bytes 393224 | tf_op jit(solution)/shard_map/ppermute | solution.py:29
  40.8 0.0 collective-permute-done.11.refs_1_
  40.8 1.0 %collective-permute-start.13 = (f32[4,64,128]{2,1,0:T(8,128)S(1)}, f32[4,64,128]{2,1,0:T(8,128)S(1)}, u32[]{:S(2)}, u32[]{:S(2)}) collective-permute-start(f32[4,64,128]{2,1,0:T(8,128)S(1)} %shard_map.77.refs_0_), channel_id=1, source_target_pairs={{0,3},{1,2},{2,1},{3,0},{4,7},{5,6},{6,5},{7,4},{8,11},{9,10},{10,... | collective-permute-start | bytes 393224 | tf_op jit(solution)/shard_map/ppermute | solution.py:29
  41.8 3.8 %collective-permute-done.12.refs_2_ = f32[4,64,128]{2,1,0:T(8,128)S(1)} collective-permute-done((f32[4,64,128]{2,1,0:T(8,128)S(1)}, f32[4,64,128]{2,1,0:T(8,128)S(1)}, u32[]{:S(2)}, u32[]{:S(2)}) %collective-permute-start.12) | collective-permute-done | bytes 131104 | tf_op jit(solution)/shard_map/ppermute | solution.py:29
  45.6 1.9 %collective-permute-done.13.refs_3_ = f32[4,64,128]{2,1,0:T(8,128)S(1)} collective-permute-done((f32[4,64,128]{2,1,0:T(8,128)S(1)}, f32[4,64,128]{2,1,0:T(8,128)S(1)}, u32[]{:S(2)}, u32[]{:S(2)}) %collective-permute-start.13) | collective-permute-done | bytes 131104 | tf_op jit(solution)/shard_map/ppermute | solution.py:29
  47.5 0.0 collective-permute-done.14
  47.5 0.0 copy-done.2
  47.5 1.5 %shard_map.78.refs_2_.refs_8_ = bf16[1024,256]{1,0:T(8,128)(2,1)} custom-call(s32[28]{0:T(128)S(1)} %get-tuple-element.13.plan_ref, f32[4,64,128]{2,1,0:T(8,128)S(1)} %shard_map.77.refs_0_, f32[4,64,128]{2,1,0:T(8,128)S(1)} %collective-permute-done.11.refs_1_, f32[4,64,128]{2,1,0:T(8,128)S(1)} %collective-permute-done.12.refs_2_, ...), custom_call_target="tpu_custom_call" | custom-call | tf_op jit(solution)/shard_map/pallas_call | solution.py:404
  49.0 3.6 %collective-permute-done.9.refs_1_.refs_7_ = bf16[2,64,2304]{2,1,0:T(8,128)(2,1)S(1)} collective-permute-done((bf16[2,64,2304]{2,1,0:T(8,128)(2,1)S(1)}, bf16[2,64,2304]{2,1,0:T(8,128)(2,1)S(1)}, u32[]{:S(2)}, u32[]{:S(2)}) %collective-permute-start.9) | collective-permute-done | bytes 589856 | tf_op jit(solution)/shard_map/ppermute | solution.py:421
  52.6 1.0 %shard_map.79.refs_1_.refs_0_ = f32[2,64,128]{2,1,0:T(8,128)S(1)} custom-call(s32[28]{0:T(128)S(1)} %get-tuple-element.13.plan_ref, bf16[8,128,2048]{2,1,0:T(8,128)(2,1)S(1)} %bitcast.5, bf16[4,64,2048]{2,1,0:T(8,128)(2,1)S(1)} %collective-permute-done.4.refs_0_, bf16[2,64,2304]{2,1,0:T(8,128)(2,1)S(1)} %collective-permute-done.9.refs_1_.refs_7_, ...), custom_call_target="tpu_custom_call" | custom-call | tf_op jit(solution)/shard_map/pallas_call | solution.py:342
  53.7 0.1 collective-permute-start.18
  53.7 1.6 %collective-permute-start.19 = (f32[2,64,128]{2,1,0:T(8,128)S(1)}, f32[2,64,128]{2,1,0:T(8,128)S(1)}, u32[]{:S(2)}, u32[]{:S(2)}) collective-permute-start(f32[2,64,128]{2,1,0:T(8,128)S(1)} %shard_map.79.refs_1_.refs_0_), channel_id=1, source_target_pairs={{0,2},{1,3},{2,0},{3,1},{4,6},{5,7},{6,4},{7,5},{8,10},{9,11},{10,... | collective-permute-start | bytes 196616 | tf_op jit(solution)/shard_map/ppermute | solution.py:29
  55.3 0.3 collective-permute-start.20
  55.6 6.5 %collective-permute-done.8.refs_0_.refs_6_ = bf16[2,64,2304]{2,1,0:T(8,128)(2,1)S(1)} collective-permute-done((bf16[2,64,2304]{2,1,0:T(8,128)(2,1)S(1)}, bf16[2,64,2304]{2,1,0:T(8,128)(2,1)S(1)}, u32[]{:S(2)}, u32[]{:S(2)}) %collective-permute-start.8) | collective-permute-done | bytes 589856 | tf_op jit(solution)/shard_map/ppermute | solution.py:421
  62.1 1.0 %shard_map.80.refs_0_ = bf16[2,64,128]{2,1,0:T(8,128)(2,1)S(1)} custom-call(s32[28]{0:T(128)S(1)} %get-tuple-element.13.plan_ref, bf16[8,128,2048]{2,1,0:T(8,128)(2,1)S(1)} %bitcast.6, bf16[2,64,2304]{2,1,0:T(8,128)(2,1)S(1)} %collective-permute-done.8.refs_0_.refs_6_, f32[2,64,128]{2,1,0:T(8,128)S(1)} %shard_map.79.refs_1_.refs_0_), custom_call_target="tpu_custom_call" | custom-call | tf_op jit(solution)/shard_map/pallas_call | solution.py:342
  63.1 0.1 collective-permute-start.15
  63.2 1.6 %collective-permute-start.16 = (bf16[2,64,128]{2,1,0:T(8,128)(2,1)S(1)}, bf16[2,64,128]{2,1,0:T(8,128)(2,1)S(1)}, u32[]{:S(2)}, u32[]{:S(2)}) collective-permute-start(bf16[2,64,128]{2,1,0:T(8,128)(2,1)S(1)} %shard_map.80.refs_0_), channel_id=1, source_target_pairs={{0,2},{1,3},{2,0},{3,1},{4,6},{5,7},{6,4},{7,5},{8,10},{9,11},{10,... | collective-permute-start | bytes 98312 | tf_op jit(solution)/shard_map/ppermute | solution.py:29
  64.8 0.0 collective-permute-done.18.refs_1_
  64.8 0.3 collective-permute-start.17
  65.1 0.0 collective-permute-done.19.refs_2_
  65.1 0.0 collective-permute-done.20.refs_3_
  65.1 1.4 %shard_map.81.refs_7_ = bf16[1024,256]{1,0:T(8,128)(2,1)} custom-call(s32[28]{0:T(128)S(1)} %get-tuple-element.13.plan_ref, f32[2,64,128]{2,1,0:T(8,128)S(1)} %shard_map.79.refs_1_.refs_0_, f32[2,64,128]{2,1,0:T(8,128)S(1)} %collective-permute-done.18.refs_1_, f32[2,64,128]{2,1,0:T(8,128)S(1)} %collective-permute-done.19.refs_2_, ...), custom_call_target="tpu_custom_call", output_to_operand_aliasing={{}: (9, {})} | custom-call | tf_op jit(solution)/shard_map/pallas_call | solution.py:404
  66.5 0.0 collective-permute-done.15.refs_1_
  66.5 0.6 collective-permute-done.16.refs_2_
  67.2 0.9 %collective-permute-done.17.refs_3_ = bf16[2,64,128]{2,1,0:T(8,128)(2,1)S(1)} collective-permute-done((bf16[2,64,128]{2,1,0:T(8,128)(2,1)S(1)}, bf16[2,64,128]{2,1,0:T(8,128)(2,1)S(1)}, u32[]{:S(2)}, u32[]{:S(2)}) %collective-permute-start.17) | collective-permute-done | bytes 32800 | tf_op jit(solution)/shard_map/ppermute | solution.py:29
  68.1 1.4 %shard_map.82 = bf16[1024,256]{1,0:T(8,128)(2,1)} custom-call(s32[28]{0:T(128)S(1)} %get-tuple-element.13.plan_ref, bf16[2,64,128]{2,1,0:T(8,128)(2,1)S(1)} %shard_map.80.refs_0_, bf16[2,64,128]{2,1,0:T(8,128)(2,1)S(1)} %collective-permute-done.15.refs_1_, bf16[2,64,128]{2,1,0:T(8,128)(2,1)S(1)} %collective-permute-done.16.refs_2_, ...), custom_call_target="tpu_custom_call", output_to_operand_aliasing={{}: (8, {})} | custom-call | tf_op jit(solution)/shard_map/pallas_call | solution.py:404
Async XLA Ops:
  0.0 9.0 %collective-permute-start = (s32[1,8]{1,0:T(1,128)}, s32[1,8]{1,0:T(1,128)S(1)}, u32[]{:S(2)}, u32[]{:S(2)}) collective-permute-start(s32[1,8]{1,0:T(1,128)} %param.11), channel_id=1, source_target_pairs={{0,4},{4,0},{8,12},{12,8},{1,5},{5,1},{9,13},{13,9},{2,6},{6,2},{1... | collective-permute-start | bytes 104 | tf_op jit(solution)/shard_map/ppermute | solution.py:29
  3.0 6.0 %collective-permute-start.1 = (s32[1,8]{1,0:T(1,128)}, s32[1,8]{1,0:T(1,128)S(1)}, u32[]{:S(2)}, u32[]{:S(2)}) collective-permute-start(s32[1,8]{1,0:T(1,128)} %param.11), channel_id=1, source_target_pairs={{0,8},{4,12},{8,0},{12,4},{1,9},{5,13},{9,1},{13,5},{2,10},{6,14},... | collective-permute-start | bytes 104 | tf_op jit(solution)/shard_map/ppermute | solution.py:29
  5.6 5.5 %collective-permute-start.2 = (s32[1,8]{1,0:T(1,128)}, s32[1,8]{1,0:T(1,128)S(1)}, u32[]{:S(2)}, u32[]{:S(2)}) collective-permute-start(s32[1,8]{1,0:T(1,128)} %param.11), channel_id=1, source_target_pairs={{0,12},{4,8},{8,4},{12,0},{1,13},{5,9},{9,5},{13,1},{2,14},{6,10},... | collective-permute-start | bytes 104 | tf_op jit(solution)/shard_map/ppermute | solution.py:29
  5.6 7.0 %collective-permute-start.3 = (bf16[4,64,256]{2,1,0:T(8,128)(2,1)}, bf16[4,64,256]{2,1,0:T(8,128)(2,1)S(1)}, u32[]{:S(2)}, u32[]{:S(2)}) collective-permute-start(bf16[4,64,256]{2,1,0:T(8,128)(2,1)} %refs_6_.1), channel_id=1, source_target_pairs={{0,0},{4,8},{8,4},{12,12},{1,1},{5,9},{9,5},{13,13},{2,2},{6,10},{... | collective-permute-start | bytes 393224 | tf_op jit(solution)/shard_map/ppermute | solution.py:421
  7.2 25.0 %collective-permute-start.4 = (bf16[4,64,2048]{2,1,0:T(8,128)(2,1)}, bf16[4,64,2048]{2,1,0:T(8,128)(2,1)S(1)}, u32[]{:S(2)}, u32[]{:S(2)}) collective-permute-start(bf16[4,64,2048]{2,1,0:T(8,128)(2,1)} %bitcast.14), channel_id=1, source_target_pairs={{0,0},{4,8},{8,4},{12,12},{1,1},{5,9},{9,5},{13,13},{2,2},{6,10},{... | collective-permute-start | bytes 3145736 | tf_op jit(solution)/shard_map/ppermute | solution.py:421
  20.5 4.2 %collective-permute-start.5 = (f32[2,384,256]{2,1,0:T(8,128)S(1)}, f32[2,384,256]{2,1,0:T(8,128)S(1)}, u32[]{:S(2)}, u32[]{:S(2)}) collective-permute-start(f32[2,384,256]{2,1,0:T(8,128)S(1)} %get-tuple-element.15), channel_id=1, source_target_pairs={{0,1},{1,0},{2,3},{3,2},{4,5},{5,4},{6,7},{7,6},{8,9},{9,8},{10,11... | collective-permute-start | bytes 2359304 | tf_op jit(solution)/shard_map/ppermute | solution.py:29
  20.6 4.2 %collective-permute-start.6 = (f32[2,384,256]{2,1,0:T(8,128)S(1)}, f32[2,384,256]{2,1,0:T(8,128)S(1)}, u32[]{:S(2)}, u32[]{:S(2)}) collective-permute-start(f32[2,384,256]{2,1,0:T(8,128)S(1)} %get-tuple-element.16), channel_id=1, source_target_pairs={{0,1},{1,0},{2,3},{3,2},{4,5},{5,4},{6,7},{7,6},{8,9},{9,8},{10,11... | collective-permute-start | bytes 2359304 | tf_op jit(solution)/shard_map/ppermute | solution.py:29
  21.1 3.6 %collective-permute-start.7 = (f32[2,256,256]{2,1,0:T(8,128)S(1)}, f32[2,256,256]{2,1,0:T(8,128)S(1)}, u32[]{:S(2)}, u32[]{:S(2)}) collective-permute-start(f32[2,256,256]{2,1,0:T(8,128)S(1)} %get-tuple-element.17), channel_id=1, source_target_pairs={{0,1},{1,0},{2,3},{3,2},{4,5},{5,4},{6,7},{7,6},{8,9},{9,8},{10,11... | collective-permute-start | bytes 1572872 | tf_op jit(solution)/shard_map/ppermute | solution.py:29
  21.1 16.6 %collective-permute-start.10 = (bf16[2,64,2304]{2,1,0:T(8,128)(2,1)S(1)}, bf16[2,64,2304]{2,1,0:T(8,128)(2,1)S(1)}, u32[]{:S(2)}, u32[]{:S(2)}) collective-permute-start(bf16[2,64,2304]{2,1,0:T(8,128)(2,1)S(1)} %get-tuple-element.19), channel_id=1, source_target_pairs={{0,4},{4,0},{8,12},{12,8},{1,5},{5,1},{9,13},{13,9},{2,6},{6,2},{1... | collective-permute-start | bytes 1769480 | tf_op jit(solution)/shard_map/ppermute | solution.py:421
  25.0 22.5 %collective-permute-start.14 = (bf16[1,1024,256]{2,1,0:T(8,128)(2,1)S(1)}, bf16[1,1024,256]{2,1,0:T(8,128)(2,1)S(1)}, u32[]{:S(2)}, u32[]{:S(2)}) collective-permute-start(bf16[1,1024,256]{2,1,0:T(8,128)(2,1)S(1)} %get-tuple-element.20), channel_id=1, source_target_pairs={{0,2},{1,3},{2,0},{3,1},{4,6},{5,7},{6,4},{7,5},{8,10},{9,11},{10,... | collective-permute-start | bytes 1572872 | tf_op jit(solution)/shard_map/ppermute | solution.py:29
  28.2 9.6 %copy-start = (bf16[1024,2048]{1,0:T(8,128)(2,1)S(1)}, bf16[1024,2048]{1,0:T(8,128)(2,1)}, u32[]{:S(2)}) copy-start(bf16[1024,2048]{1,0:T(8,128)(2,1)} %tokens_ref.1) | copy-start | bytes 12582916
  28.2 9.6 %copy-start.1 = (bf16[4,2048,64]{1,2,0:T(8,128)(2,1)S(1)}, bf16[4,2048,64]{1,2,0:T(8,128)(2,1)}, u32[]{:S(2)}) copy-start(bf16[4,2048,64]{1,2,0:T(8,128)(2,1)} %param.9) | copy-start | bytes 3145732
  28.2 24.4 %collective-permute-start.9 = (bf16[2,64,2304]{2,1,0:T(8,128)(2,1)S(1)}, bf16[2,64,2304]{2,1,0:T(8,128)(2,1)S(1)}, u32[]{:S(2)}, u32[]{:S(2)}) collective-permute-start(bf16[2,64,2304]{2,1,0:T(8,128)(2,1)S(1)} %shard_map.75.refs_4_), channel_id=1, source_target_pairs={{0,12},{4,4},{8,8},{12,0},{1,13},{5,5},{9,9},{13,1},{2,14},{6,6},{... | collective-permute-start | bytes 1769480 | tf_op jit(solution)/shard_map/ppermute | solution.py:421
  33.9 13.7 %copy-start.2 = (bf16[4,64,256]{2,1,0:T(8,128)(2,1)S(1)}, bf16[4,64,256]{2,1,0:T(8,128)(2,1)}, u32[]{:S(2)}) copy-start(bf16[4,64,256]{2,1,0:T(8,128)(2,1)} %refs_6_.1) | copy-start | bytes 393220
  33.9 28.2 %collective-permute-start.8 = (bf16[2,64,2304]{2,1,0:T(8,128)(2,1)S(1)}, bf16[2,64,2304]{2,1,0:T(8,128)(2,1)S(1)}, u32[]{:S(2)}, u32[]{:S(2)}) collective-permute-start(bf16[2,64,2304]{2,1,0:T(8,128)(2,1)S(1)} %shard_map.76.refs_2_), channel_id=1, source_target_pairs={{0,8},{4,0},{8,12},{12,4},{1,9},{5,1},{9,13},{13,5},{2,10},{6,2},{... | collective-permute-start | bytes 1769480 | tf_op jit(solution)/shard_map/ppermute | solution.py:421
  39.2 1.6 %collective-permute-start.11 = (f32[4,64,128]{2,1,0:T(8,128)S(1)}, f32[4,64,128]{2,1,0:T(8,128)S(1)}, u32[]{:S(2)}, u32[]{:S(2)}) collective-permute-start(f32[4,64,128]{2,1,0:T(8,128)S(1)} %shard_map.77.refs_0_), channel_id=1, source_target_pairs={{0,1},{1,0},{2,3},{3,2},{4,5},{5,4},{6,7},{7,6},{8,9},{9,8},{10,11... | collective-permute-start | bytes 393224 | tf_op jit(solution)/shard_map/ppermute | solution.py:29
  39.3 6.4 %collective-permute-start.12 = (f32[4,64,128]{2,1,0:T(8,128)S(1)}, f32[4,64,128]{2,1,0:T(8,128)S(1)}, u32[]{:S(2)}, u32[]{:S(2)}) collective-permute-start(f32[4,64,128]{2,1,0:T(8,128)S(1)} %shard_map.77.refs_0_), channel_id=1, source_target_pairs={{0,2},{1,3},{2,0},{3,1},{4,6},{5,7},{6,4},{7,5},{8,10},{9,11},{10,... | collective-permute-start | bytes 393224 | tf_op jit(solution)/shard_map/ppermute | solution.py:29
  40.8 6.7 %collective-permute-start.13 = (f32[4,64,128]{2,1,0:T(8,128)S(1)}, f32[4,64,128]{2,1,0:T(8,128)S(1)}, u32[]{:S(2)}, u32[]{:S(2)}) collective-permute-start(f32[4,64,128]{2,1,0:T(8,128)S(1)} %shard_map.77.refs_0_), channel_id=1, source_target_pairs={{0,3},{1,2},{2,1},{3,0},{4,7},{5,6},{6,5},{7,4},{8,11},{9,10},{10,... | collective-permute-start | bytes 393224 | tf_op jit(solution)/shard_map/ppermute | solution.py:29
  53.7 11.1 %collective-permute-start.18 = (f32[2,64,128]{2,1,0:T(8,128)S(1)}, f32[2,64,128]{2,1,0:T(8,128)S(1)}, u32[]{:S(2)}, u32[]{:S(2)}) collective-permute-start(f32[2,64,128]{2,1,0:T(8,128)S(1)} %shard_map.79.refs_1_.refs_0_), channel_id=1, source_target_pairs={{0,1},{1,0},{2,3},{3,2},{4,5},{5,4},{6,7},{7,6},{8,9},{9,8},{10,11... | collective-permute-start | bytes 196616 | tf_op jit(solution)/shard_map/ppermute | solution.py:29
  53.7 11.3 %collective-permute-start.19 = (f32[2,64,128]{2,1,0:T(8,128)S(1)}, f32[2,64,128]{2,1,0:T(8,128)S(1)}, u32[]{:S(2)}, u32[]{:S(2)}) collective-permute-start(f32[2,64,128]{2,1,0:T(8,128)S(1)} %shard_map.79.refs_1_.refs_0_), channel_id=1, source_target_pairs={{0,2},{1,3},{2,0},{3,1},{4,6},{5,7},{6,4},{7,5},{8,10},{9,11},{10,... | collective-permute-start | bytes 196616 | tf_op jit(solution)/shard_map/ppermute | solution.py:29
  55.3 9.8 %collective-permute-start.20 = (f32[2,64,128]{2,1,0:T(8,128)S(1)}, f32[2,64,128]{2,1,0:T(8,128)S(1)}, u32[]{:S(2)}, u32[]{:S(2)}) collective-permute-start(f32[2,64,128]{2,1,0:T(8,128)S(1)} %shard_map.79.refs_1_.refs_0_), channel_id=1, source_target_pairs={{0,3},{1,2},{2,1},{3,0},{4,7},{5,6},{6,5},{7,4},{8,11},{9,10},{10,... | collective-permute-start | bytes 196616 | tf_op jit(solution)/shard_map/ppermute | solution.py:29
  63.1 3.4 %collective-permute-start.15 = (bf16[2,64,128]{2,1,0:T(8,128)(2,1)S(1)}, bf16[2,64,128]{2,1,0:T(8,128)(2,1)S(1)}, u32[]{:S(2)}, u32[]{:S(2)}) collective-permute-start(bf16[2,64,128]{2,1,0:T(8,128)(2,1)S(1)} %shard_map.80.refs_0_), channel_id=1, source_target_pairs={{0,1},{1,0},{2,3},{3,2},{4,5},{5,4},{6,7},{7,6},{8,9},{9,8},{10,11... | collective-permute-start | bytes 98312 | tf_op jit(solution)/shard_map/ppermute | solution.py:29
  63.2 4.0 %collective-permute-start.16 = (bf16[2,64,128]{2,1,0:T(8,128)(2,1)S(1)}, bf16[2,64,128]{2,1,0:T(8,128)(2,1)S(1)}, u32[]{:S(2)}, u32[]{:S(2)}) collective-permute-start(bf16[2,64,128]{2,1,0:T(8,128)(2,1)S(1)} %shard_map.80.refs_0_), channel_id=1, source_target_pairs={{0,2},{1,3},{2,0},{3,1},{4,6},{5,7},{6,4},{7,5},{8,10},{9,11},{10,... | collective-permute-start | bytes 98312 | tf_op jit(solution)/shard_map/ppermute | solution.py:29
  64.8 3.3 %collective-permute-start.17 = (bf16[2,64,128]{2,1,0:T(8,128)(2,1)S(1)}, bf16[2,64,128]{2,1,0:T(8,128)(2,1)S(1)}, u32[]{:S(2)}, u32[]{:S(2)}) collective-permute-start(bf16[2,64,128]{2,1,0:T(8,128)(2,1)S(1)} %shard_map.80.refs_0_), channel_id=1, source_target_pairs={{0,3},{1,2},{2,1},{3,0},{4,7},{5,6},{6,5},{7,4},{8,11},{9,10},{10,... | collective-permute-start | bytes 98312 | tf_op jit(solution)/shard_map/ppermute | solution.py:29

commit v17 on v12

--- a/solution.py
+++ b/solution.py
@@ -87,9 +87,20 @@
         if i == 0:
             run_copies(token_copies[1:])
         add(0, i * slab, (i + 1) * slab, i == 0)
-    for i in range(1, parts):
-        token_copies[i].wait()
-        add(i * tile, 0, weight.shape[0], True)
+    for copy in token_copies[1:]:
+        copy.wait()
+    for number, offset in enumerate(order):
+        columns = pl.ds(pl.multiple_of((place ^ offset) * width, width), width)
+        targets = [(kept_ref, number - half, 0)] if number >= half else []
+        start = 0
+        for sent_ref in sent_refs if number < half else []:
+            targets.append((sent_ref, number, start))
+            start += sent_ref.shape[1]
+        for ref, index, start in targets:
+            low, high = max(tile, start), start + ref.shape[1]
+            ref[index, low - start :, :] = jnp.dot(
+                tokens[low:high, :], weight[:, columns], preferred_element_type=jnp.float32
+            )
 
 
 def base_chunks(tokens, weight, order, width):

time: 69.9 us -> 70.1 us (level)
  no operation moved by 1% of the time
where the time goes in v17:
time: 70.1 us; the launch traced here: 69.7 us
  starting transfers between devices  30.7 us (44%)
  Pallas kernels  21.2 us (30%)
  waiting for transfers between devices  17.5 us (25%)
    ppermute x5, starting transfers between devices, across(): return lax.ppermute(value, 'pool', pairs)  16.4 us
    ppermute x16, starting transfers between devices, swap(): return lax.ppermute(value, axis, pairs)  14.3 us
    ppermute x5, waiting for transfers between devices, across(): return lax.ppermute(value, 'pool', pairs)  10.2 us
    ppermute x16, waiting for transfers between devices, swap(): return lax.ppermute(value, axis, pairs)  7.28 us
    pallas_call x1, Pallas kernels, base_chunks(): pl.pallas_call(functools.partial(base_kernel, order), in_specs=[ANY] * 2,...  7.22 us
    pallas_call x3, Pallas kernels, combine(): pl.pallas_call(functools.partial(combine_kernel, shapes, choose, len(part...  4.38 us
    pallas_call x3, Pallas kernels, shrink(): pl.pallas_call(functools.partial(shrink_kernel, shapes, choose), in_specs...  3.42 us
    pallas_call x2, Pallas kernels, pack_panels(): pl.pallas_call(functools.partial(pack_kernel, [start for start, *_ in cho...  3.27 us
  transfers between devices with their start and end apart: 21, of which 6 were waited for; matrix products, arithmetic and copies ran while one was open for 0% of the time, Pallas kernels for 28%

profile of v17, /device:TPU:0, one launch (start us, length us, event | category | flops | bytes accessed | tf_op | source)
XLA Modules:
  0.0 69.7 jit_solution(5629848238165649767)
XLA Ops:
  0.0 3.0 %collective-permute-start = (s32[1,8]{1,0:T(1,128)}, s32[1,8]{1,0:T(1,128)S(1)}, u32[]{:S(2)}, u32[]{:S(2)}) collective-permute-start(s32[1,8]{1,0:T(1,128)} %refs_0_.1), channel_id=1, source_target_pairs={{0,4},{4,0},{8,12},{12,8},{1,5},{5,1},{9,13},{13,9},{2,6},{6,2},{1... | collective-permute-start | bytes 104 | tf_op jit(solution)/shard_map/ppermute | solution.py:29
  3.0 2.6 %collective-permute-start.1 = (s32[1,8]{1,0:T(1,128)}, s32[1,8]{1,0:T(1,128)S(1)}, u32[]{:S(2)}, u32[]{:S(2)}) collective-permute-start(s32[1,8]{1,0:T(1,128)} %refs_0_.1), channel_id=1, source_target_pairs={{0,8},{4,12},{8,0},{12,4},{1,9},{5,13},{9,1},{13,5},{2,10},{6,14},... | collective-permute-start | bytes 104 | tf_op jit(solution)/shard_map/ppermute | solution.py:29
  5.6 0.0 collective-permute-start.2
  5.6 1.6 %collective-permute-start.3 = (bf16[4,64,256]{2,1,0:T(8,128)(2,1)}, bf16[4,64,256]{2,1,0:T(8,128)(2,1)S(1)}, u32[]{:S(2)}, u32[]{:S(2)}) collective-permute-start(bf16[4,64,256]{2,1,0:T(8,128)(2,1)} %refs_6_.1), channel_id=1, source_target_pairs={{0,0},{4,8},{8,4},{12,12},{1,1},{5,9},{9,5},{13,13},{2,2},{6,10},{... | collective-permute-start | bytes 393224 | tf_op jit(solution)/shard_map/ppermute | solution.py:418
  7.2 1.9 %collective-permute-start.4 = (bf16[4,64,2048]{2,1,0:T(8,128)(2,1)}, bf16[4,64,2048]{2,1,0:T(8,128)(2,1)S(1)}, u32[]{:S(2)}, u32[]{:S(2)}) collective-permute-start(bf16[4,64,2048]{2,1,0:T(8,128)(2,1)} %bitcast.14), channel_id=1, source_target_pairs={{0,0},{4,8},{8,4},{12,12},{1,1},{5,9},{9,5},{13,13},{2,2},{6,10},{... | collective-permute-start | bytes 3145736 | tf_op jit(solution)/shard_map/ppermute | solution.py:418
  9.0 7.2 %shard_map.73 = (f32[2,384,256]{2,1,0:T(8,128)S(1)}, f32[2,384,256]{2,1,0:T(8,128)S(1)}, f32[2,256,256]{2,1,0:T(8,128)S(1)}, f32[2,1024,256]{2,1,0:T(8,128)S(1)}) custom-call(bf16[1024,2048]{1,0:T(8,128)(2,1)} %tokens_ref.1, bf16[2048,1024]{1,0:T(8,128)(2,1)} %weight_ref.1), custom_call_target="tpu_custom_call" | custom-call | flops 4000000000 | tf_op jit(solution)/shard_map/pallas_call | solution.py:110
  16.3 0.0 collective-permute-done.refs_1_
  16.3 0.1 collective-permute-start.7
  16.4 0.0 collective-permute-done.1.refs_2_
  16.4 0.5 collective-permute-start.5
  16.9 0.0 collective-permute-done.2.refs_3_
  16.9 0.1 collective-permute-start.6
  17.0 0.0 collective-permute-done.3.refs_8_.refs_1_.refs_6_
  17.0 2.7 %shard_map.74 = (bf16[2,64,2304]{2,1,0:T(8,128)(2,1)S(1)}, s32[28]{0:T(128)S(1)}) custom-call(s32[1,8]{1,0:T(1,128)} %refs_0_.1, s32[1,8]{1,0:T(1,128)S(1)} %collective-permute-done.refs_1_, s32[1,8]{1,0:T(1,128)S(1)} %collective-permute-done.1.refs_2_, s32[1,8]{1,0:T(1,128)S(1)} %collective-permute-done.2.refs_3_, s32[16]{0:T(128)} %refs_4_.1, ...), custom_call_target="tpu_custom_call" | custom-call | flops 10000000000 | tf_op jit(solution)/shard_map/pallas_call | solution.py:246
  19.7 3.4 %collective-permute-start.10 = (bf16[2,64,2304]{2,1,0:T(8,128)(2,1)S(1)}, bf16[2,64,2304]{2,1,0:T(8,128)(2,1)S(1)}, u32[]{:S(2)}, u32[]{:S(2)}) collective-permute-start(bf16[2,64,2304]{2,1,0:T(8,128)(2,1)S(1)} %get-tuple-element.19), channel_id=1, source_target_pairs={{0,4},{4,0},{8,12},{12,8},{1,5},{5,1},{9,13},{13,9},{2,6},{6,2},{1... | collective-permute-start | bytes 1769480 | tf_op jit(solution)/shard_map/ppermute | solution.py:418
  23.1 0.0 collective-permute-done.7.refs_2_
  23.1 0.0 collective-permute-done.5.refs_0_
  23.1 0.0 collective-permute-done.6.refs_1_
  23.1 0.2 shard_map.75
  23.3 1.5 %collective-permute-start.14 = (bf16[1,1024,256]{2,1,0:T(8,128)(2,1)S(1)}, bf16[1,1024,256]{2,1,0:T(8,128)(2,1)S(1)}, u32[]{:S(2)}, u32[]{:S(2)}) collective-permute-start(bf16[1,1024,256]{2,1,0:T(8,128)(2,1)S(1)} %get-tuple-element.20), channel_id=1, source_target_pairs={{0,2},{1,3},{2,0},{3,1},{4,6},{5,7},{6,4},{7,5},{8,10},{9,11},{10,... | collective-permute-start | bytes 1572872 | tf_op jit(solution)/shard_map/ppermute | solution.py:29
  24.9 1.6 %shard_map.76.refs_4_ = bf16[2,64,2304]{2,1,0:T(8,128)(2,1)S(1)} custom-call(s32[28]{0:T(128)S(1)} %get-tuple-element.14.plan_ref, bf16[4,64,2048]{2,1,0:T(8,128)(2,1)} %bitcast.16, bf16[4,64,256]{2,1,0:T(8,128)(2,1)} %refs_6_.1, f32[1024,256]{1,0:T(8,128)S(1)} %bitcast.7), custom_call_target="tpu_custom_call" | custom-call | tf_op jit(solution)/shard_map/pallas_call | solution.py:285
  26.5 0.0 copy-start
  26.5 0.0 copy-start.1
  26.5 4.7 %collective-permute-start.9 = (bf16[2,64,2304]{2,1,0:T(8,128)(2,1)S(1)}, bf16[2,64,2304]{2,1,0:T(8,128)(2,1)S(1)}, u32[]{:S(2)}, u32[]{:S(2)}) collective-permute-start(bf16[2,64,2304]{2,1,0:T(8,128)(2,1)S(1)} %shard_map.76.refs_4_), channel_id=1, source_target_pairs={{0,12},{4,4},{8,8},{12,0},{1,13},{5,5},{9,9},{13,1},{2,14},{6,6},{... | collective-permute-start | bytes 1769480 | tf_op jit(solution)/shard_map/ppermute | solution.py:418
  31.2 0.0 collective-permute-done.4.refs_0_
  31.2 1.6 %shard_map.77.refs_2_ = bf16[2,64,2304]{2,1,0:T(8,128)(2,1)S(1)} custom-call(s32[28]{0:T(128)S(1)} %get-tuple-element.14.plan_ref, bf16[4,64,2048]{2,1,0:T(8,128)(2,1)S(1)} %collective-permute-done.4.refs_0_, bf16[4,64,256]{2,1,0:T(8,128)(2,1)S(1)} %collective-permute-done.3.refs_8_.refs_1_.refs_6_, bf16[4,64,2048]{2,1,0:T(8,128)(2,1)} %bitcast.17, ...), custom_call_target="tpu_custom_call" | custom-call | flops 6000000000 | tf_op jit(solution)/shard_map/pallas_call | solution.py:285
  32.8 0.0 copy-start.2
  32.9 4.9 %collective-permute-start.8 = (bf16[2,64,2304]{2,1,0:T(8,128)(2,1)S(1)}, bf16[2,64,2304]{2,1,0:T(8,128)(2,1)S(1)}, u32[]{:S(2)}, u32[]{:S(2)}) collective-permute-start(bf16[2,64,2304]{2,1,0:T(8,128)(2,1)S(1)} %shard_map.77.refs_2_), channel_id=1, source_target_pairs={{0,8},{4,0},{8,12},{12,4},{1,9},{5,1},{9,13},{13,5},{2,10},{6,2},{... | collective-permute-start | bytes 1769480 | tf_op jit(solution)/shard_map/ppermute | solution.py:418
  37.8 0.0 collective-permute-done.10.refs_1_.refs_7_
  37.8 0.0 copy-done
  37.8 0.0 copy-done.1
  37.8 1.4 %shard_map.78.refs_0_ = f32[4,64,128]{2,1,0:T(8,128)S(1)} custom-call(s32[28]{0:T(128)S(1)} %get-tuple-element.14.plan_ref, bf16[8,128,2048]{2,1,0:T(8,128)(2,1)S(1)} %bitcast.4, bf16[4,64,2048]{2,1,0:T(8,128)(2,1)S(1)} %bitcast.18, bf16[2,64,2304]{2,1,0:T(8,128)(2,1)S(1)} %collective-permute-done.10.refs_1_.refs_7_, bf16[2,64,2304]{2,1,0:T(8,128)(2,1)S(1)} %shard_map.77.refs_2_), custom_call_target="tpu_custom_call" | custom-call | tf_op jit(solution)/shard_map/pallas_call | solution.py:339
  39.2 0.1 collective-permute-start.11
  39.3 1.6 %collective-permute-start.12 = (f32[4,64,128]{2,1,0:T(8,128)S(1)}, f32[4,64,128]{2,1,0:T(8,128)S(1)}, u32[]{:S(2)}, u32[]{:S(2)}) collective-permute-start(f32[4,64,128]{2,1,0:T(8,128)S(1)} %shard_map.78.refs_0_), channel_id=1, source_target_pairs={{0,2},{1,3},{2,0},{3,1},{4,6},{5,7},{6,4},{7,5},{8,10},{9,11},{10,... | collective-permute-start | bytes 393224 | tf_op jit(solution)/shard_map/ppermute | solution.py:29
  40.8 0.0 collective-permute-done.11.refs_1_
  40.8 1.0 %collective-permute-start.13 = (f32[4,64,128]{2,1,0:T(8,128)S(1)}, f32[4,64,128]{2,1,0:T(8,128)S(1)}, u32[]{:S(2)}, u32[]{:S(2)}) collective-permute-start(f32[4,64,128]{2,1,0:T(8,128)S(1)} %shard_map.78.refs_0_), channel_id=1, source_target_pairs={{0,3},{1,2},{2,1},{3,0},{4,7},{5,6},{6,5},{7,4},{8,11},{9,10},{10,... | collective-permute-start | bytes 393224 | tf_op jit(solution)/shard_map/ppermute | solution.py:29
  41.8 3.8 %collective-permute-done.12.refs_2_ = f32[4,64,128]{2,1,0:T(8,128)S(1)} collective-permute-done((f32[4,64,128]{2,1,0:T(8,128)S(1)}, f32[4,64,128]{2,1,0:T(8,128)S(1)}, u32[]{:S(2)}, u32[]{:S(2)}) %collective-permute-start.12) | collective-permute-done | bytes 131104 | tf_op jit(solution)/shard_map/ppermute | solution.py:29
  45.6 1.9 %collective-permute-done.13.refs_3_ = f32[4,64,128]{2,1,0:T(8,128)S(1)} collective-permute-done((f32[4,64,128]{2,1,0:T(8,128)S(1)}, f32[4,64,128]{2,1,0:T(8,128)S(1)}, u32[]{:S(2)}, u32[]{:S(2)}) %collective-permute-start.13) | collective-permute-done | bytes 131104 | tf_op jit(solution)/shard_map/ppermute | solution.py:29
  47.5 0.0 collective-permute-done.14
  47.5 0.0 copy-done.2
  47.5 1.5 %shard_map.79.refs_2_.refs_8_ = bf16[1024,256]{1,0:T(8,128)(2,1)} custom-call(s32[28]{0:T(128)S(1)} %get-tuple-element.14.plan_ref, f32[4,64,128]{2,1,0:T(8,128)S(1)} %shard_map.78.refs_0_, f32[4,64,128]{2,1,0:T(8,128)S(1)} %collective-permute-done.11.refs_1_, f32[4,64,128]{2,1,0:T(8,128)S(1)} %collective-permute-done.12.refs_2_, ...), custom_call_target="tpu_custom_call" | custom-call | tf_op jit(solution)/shard_map/pallas_call | solution.py:401
  49.0 3.3 %collective-permute-done.9.refs_1_.refs_7_ = bf16[2,64,2304]{2,1,0:T(8,128)(2,1)S(1)} collective-permute-done((bf16[2,64,2304]{2,1,0:T(8,128)(2,1)S(1)}, bf16[2,64,2304]{2,1,0:T(8,128)(2,1)S(1)}, u32[]{:S(2)}, u32[]{:S(2)}) %collective-permute-start.9) | collective-permute-done | bytes 589856 | tf_op jit(solution)/shard_map/ppermute | solution.py:418
  52.3 1.0 %shard_map.80.refs_1_.refs_0_ = f32[2,64,128]{2,1,0:T(8,128)S(1)} custom-call(s32[28]{0:T(128)S(1)} %get-tuple-element.14.plan_ref, bf16[8,128,2048]{2,1,0:T(8,128)(2,1)S(1)} %bitcast.5, bf16[4,64,2048]{2,1,0:T(8,128)(2,1)S(1)} %collective-permute-done.4.refs_0_, bf16[2,64,2304]{2,1,0:T(8,128)(2,1)S(1)} %collective-permute-done.9.refs_1_.refs_7_, ...), custom_call_target="tpu_custom_call" | custom-call | tf_op jit(solution)/shard_map/pallas_call | solution.py:339
  53.4 0.1 collective-permute-start.18
  53.4 1.6 %collective-permute-start.19 = (f32[2,64,128]{2,1,0:T(8,128)S(1)}, f32[2,64,128]{2,1,0:T(8,128)S(1)}, u32[]{:S(2)}, u32[]{:S(2)}) collective-permute-start(f32[2,64,128]{2,1,0:T(8,128)S(1)} %shard_map.80.refs_1_.refs_0_), channel_id=1, source_target_pairs={{0,2},{1,3},{2,0},{3,1},{4,6},{5,7},{6,4},{7,5},{8,10},{9,11},{10,... | collective-permute-start | bytes 196616 | tf_op jit(solution)/shard_map/ppermute | solution.py:29
  55.0 0.3 collective-permute-start.20
  55.3 7.0 %collective-permute-done.8.refs_0_.refs_6_ = bf16[2,64,2304]{2,1,0:T(8,128)(2,1)S(1)} collective-permute-done((bf16[2,64,2304]{2,1,0:T(8,128)(2,1)S(1)}, bf16[2,64,2304]{2,1,0:T(8,128)(2,1)S(1)}, u32[]{:S(2)}, u32[]{:S(2)}) %collective-permute-start.8) | collective-permute-done | bytes 589856 | tf_op jit(solution)/shard_map/ppermute | solution.py:418
  62.3 1.0 %shard_map.81.refs_0_ = bf16[2,64,128]{2,1,0:T(8,128)(2,1)S(1)} custom-call(s32[28]{0:T(128)S(1)} %get-tuple-element.14.plan_ref, bf16[8,128,2048]{2,1,0:T(8,128)(2,1)S(1)} %bitcast.6, bf16[2,64,2304]{2,1,0:T(8,128)(2,1)S(1)} %collective-permute-done.8.refs_0_.refs_6_, f32[2,64,128]{2,1,0:T(8,128)S(1)} %shard_map.80.refs_1_.refs_0_), custom_call_target="tpu_custom_call" | custom-call | tf_op jit(solution)/shard_map/pallas_call | solution.py:339
  63.3 0.1 collective-permute-start.15
  63.4 1.6 %collective-permute-start.16 = (bf16[2,64,128]{2,1,0:T(8,128)(2,1)S(1)}, bf16[2,64,128]{2,1,0:T(8,128)(2,1)S(1)}, u32[]{:S(2)}, u32[]{:S(2)}) collective-permute-start(bf16[2,64,128]{2,1,0:T(8,128)(2,1)S(1)} %shard_map.81.refs_0_), channel_id=1, source_target_pairs={{0,2},{1,3},{2,0},{3,1},{4,6},{5,7},{6,4},{7,5},{8,10},{9,11},{10,... | collective-permute-start | bytes 98312 | tf_op jit(solution)/shard_map/ppermute | solution.py:29
  64.9 0.0 collective-permute-done.18.refs_1_
  64.9 0.3 collective-permute-start.17
  65.2 0.0 collective-permute-done.19.refs_2_
  65.2 0.0 collective-permute-done.20.refs_3_
  65.2 1.4 %shard_map.82.refs_7_ = bf16[1024,256]{1,0:T(8,128)(2,1)} custom-call(s32[28]{0:T(128)S(1)} %get-tuple-element.14.plan_ref, f32[2,64,128]{2,1,0:T(8,128)S(1)} %shard_map.80.refs_1_.refs_0_, f32[2,64,128]{2,1,0:T(8,128)S(1)} %collective-permute-done.18.refs_1_, f32[2,64,128]{2,1,0:T(8,128)S(1)} %collective-permute-done.19.refs_2_, ...), custom_call_target="tpu_custom_call", output_to_operand_aliasing={{}: (9, {})} | custom-call | tf_op jit(solution)/shard_map/pallas_call | solution.py:401
  66.7 0.0 collective-permute-done.15.refs_1_
  66.7 0.6 collective-permute-done.16.refs_2_
  67.3 0.9 %collective-permute-done.17.refs_3_ = bf16[2,64,128]{2,1,0:T(8,128)(2,1)S(1)} collective-permute-done((bf16[2,64,128]{2,1,0:T(8,128)(2,1)S(1)}, bf16[2,64,128]{2,1,0:T(8,128)(2,1)S(1)}, u32[]{:S(2)}, u32[]{:S(2)}) %collective-permute-start.17) | collective-permute-done | bytes 32800 | tf_op jit(solution)/shard_map/ppermute | solution.py:29
  68.3 1.4 %shard_map.83 = bf16[1024,256]{1,0:T(8,128)(2,1)} custom-call(s32[28]{0:T(128)S(1)} %get-tuple-element.14.plan_ref, bf16[2,64,128]{2,1,0:T(8,128)(2,1)S(1)} %shard_map.81.refs_0_, bf16[2,64,128]{2,1,0:T(8,128)(2,1)S(1)} %collective-permute-done.15.refs_1_, bf16[2,64,128]{2,1,0:T(8,128)(2,1)S(1)} %collective-permute-done.16.refs_2_, ...), custom_call_target="tpu_custom_call", output_to_operand_aliasing={{}: (8, {})} | custom-call | tf_op jit(solution)/shard_map/pallas_call | solution.py:401
Async XLA Ops:
  0.0 16.3 %collective-permute-start = (s32[1,8]{1,0:T(1,128)}, s32[1,8]{1,0:T(1,128)S(1)}, u32[]{:S(2)}, u32[]{:S(2)}) collective-permute-start(s32[1,8]{1,0:T(1,128)} %refs_0_.1), channel_id=1, source_target_pairs={{0,4},{4,0},{8,12},{12,8},{1,5},{5,1},{9,13},{13,9},{2,6},{6,2},{1... | collective-permute-start | bytes 104 | tf_op jit(solution)/shard_map/ppermute | solution.py:29
  3.0 13.3 %collective-permute-start.1 = (s32[1,8]{1,0:T(1,128)}, s32[1,8]{1,0:T(1,128)S(1)}, u32[]{:S(2)}, u32[]{:S(2)}) collective-permute-start(s32[1,8]{1,0:T(1,128)} %refs_0_.1), channel_id=1, source_target_pairs={{0,8},{4,12},{8,0},{12,4},{1,9},{5,13},{9,1},{13,5},{2,10},{6,14},... | collective-permute-start | bytes 104 | tf_op jit(solution)/shard_map/ppermute | solution.py:29
  5.6 11.3 %collective-permute-start.2 = (s32[1,8]{1,0:T(1,128)}, s32[1,8]{1,0:T(1,128)S(1)}, u32[]{:S(2)}, u32[]{:S(2)}) collective-permute-start(s32[1,8]{1,0:T(1,128)} %refs_0_.1), channel_id=1, source_target_pairs={{0,12},{4,8},{8,4},{12,0},{1,13},{5,9},{9,5},{13,1},{2,14},{6,10},... | collective-permute-start | bytes 104 | tf_op jit(solution)/shard_map/ppermute | solution.py:29
  5.6 11.3 %collective-permute-start.3 = (bf16[4,64,256]{2,1,0:T(8,128)(2,1)}, bf16[4,64,256]{2,1,0:T(8,128)(2,1)S(1)}, u32[]{:S(2)}, u32[]{:S(2)}) collective-permute-start(bf16[4,64,256]{2,1,0:T(8,128)(2,1)} %refs_6_.1), channel_id=1, source_target_pairs={{0,0},{4,8},{8,4},{12,12},{1,1},{5,9},{9,5},{13,13},{2,2},{6,10},{... | collective-permute-start | bytes 393224 | tf_op jit(solution)/shard_map/ppermute | solution.py:418
  7.2 24.0 %collective-permute-start.4 = (bf16[4,64,2048]{2,1,0:T(8,128)(2,1)}, bf16[4,64,2048]{2,1,0:T(8,128)(2,1)S(1)}, u32[]{:S(2)}, u32[]{:S(2)}) collective-permute-start(bf16[4,64,2048]{2,1,0:T(8,128)(2,1)} %bitcast.14), channel_id=1, source_target_pairs={{0,0},{4,8},{8,4},{12,12},{1,1},{5,9},{9,5},{13,13},{2,2},{6,10},{... | collective-permute-start | bytes 3145736 | tf_op jit(solution)/shard_map/ppermute | solution.py:418
  16.3 6.8 %collective-permute-start.7 = (f32[2,256,256]{2,1,0:T(8,128)S(1)}, f32[2,256,256]{2,1,0:T(8,128)S(1)}, u32[]{:S(2)}, u32[]{:S(2)}) collective-permute-start(f32[2,256,256]{2,1,0:T(8,128)S(1)} %get-tuple-element.13.refs_9_), channel_id=1, source_target_pairs={{0,1},{1,0},{2,3},{3,2},{4,5},{5,4},{6,7},{7,6},{8,9},{9,8},{10,11... | collective-permute-start | bytes 1572872 | tf_op jit(solution)/shard_map/ppermute | solution.py:29
  16.4 6.7 %collective-permute-start.5 = (f32[2,384,256]{2,1,0:T(8,128)S(1)}, f32[2,384,256]{2,1,0:T(8,128)S(1)}, u32[]{:S(2)}, u32[]{:S(2)}) collective-permute-start(f32[2,384,256]{2,1,0:T(8,128)S(1)} %get-tuple-element.16), channel_id=1, source_target_pairs={{0,1},{1,0},{2,3},{3,2},{4,5},{5,4},{6,7},{7,6},{8,9},{9,8},{10,11... | collective-permute-start | bytes 2359304 | tf_op jit(solution)/shard_map/ppermute | solution.py:29
  16.9 6.2 %collective-permute-start.6 = (f32[2,384,256]{2,1,0:T(8,128)S(1)}, f32[2,384,256]{2,1,0:T(8,128)S(1)}, u32[]{:S(2)}, u32[]{:S(2)}) collective-permute-start(f32[2,384,256]{2,1,0:T(8,128)S(1)} %get-tuple-element.17), channel_id=1, source_target_pairs={{0,1},{1,0},{2,3},{3,2},{4,5},{5,4},{6,7},{7,6},{8,9},{9,8},{10,11... | collective-permute-start | bytes 2359304 | tf_op jit(solution)/shard_map/ppermute | solution.py:29
  19.7 18.1 %collective-permute-start.10 = (bf16[2,64,2304]{2,1,0:T(8,128)(2,1)S(1)}, bf16[2,64,2304]{2,1,0:T(8,128)(2,1)S(1)}, u32[]{:S(2)}, u32[]{:S(2)}) collective-permute-start(bf16[2,64,2304]{2,1,0:T(8,128)(2,1)S(1)} %get-tuple-element.19), channel_id=1, source_target_pairs={{0,4},{4,0},{8,12},{12,8},{1,5},{5,1},{9,13},{13,9},{2,6},{6,2},{1... | collective-permute-start | bytes 1769480 | tf_op jit(solution)/shard_map/ppermute | solution.py:418
  23.3 24.2 %collective-permute-start.14 = (bf16[1,1024,256]{2,1,0:T(8,128)(2,1)S(1)}, bf16[1,1024,256]{2,1,0:T(8,128)(2,1)S(1)}, u32[]{:S(2)}, u32[]{:S(2)}) collective-permute-start(bf16[1,1024,256]{2,1,0:T(8,128)(2,1)S(1)} %get-tuple-element.20), channel_id=1, source_target_pairs={{0,2},{1,3},{2,0},{3,1},{4,6},{5,7},{6,4},{7,5},{8,10},{9,11},{10,... | collective-permute-start | bytes 1572872 | tf_op jit(solution)/shard_map/ppermute | solution.py:29
  26.5 11.3 %copy-start = (bf16[1024,2048]{1,0:T(8,128)(2,1)S(1)}, bf16[1024,2048]{1,0:T(8,128)(2,1)}, u32[]{:S(2)}) copy-start(bf16[1024,2048]{1,0:T(8,128)(2,1)} %tokens_ref.1) | copy-start | bytes 12582916
  26.5 11.3 %copy-start.1 = (bf16[4,2048,64]{1,2,0:T(8,128)(2,1)S(1)}, bf16[4,2048,64]{1,2,0:T(8,128)(2,1)}, u32[]{:S(2)}) copy-start(bf16[4,2048,64]{1,2,0:T(8,128)(2,1)} %param.9) | copy-start | bytes 3145732
  26.5 25.8 %collective-permute-start.9 = (bf16[2,64,2304]{2,1,0:T(8,128)(2,1)S(1)}, bf16[2,64,2304]{2,1,0:T(8,128)(2,1)S(1)}, u32[]{:S(2)}, u32[]{:S(2)}) collective-permute-start(bf16[2,64,2304]{2,1,0:T(8,128)(2,1)S(1)} %shard_map.76.refs_4_), channel_id=1, source_target_pairs={{0,12},{4,4},{8,8},{12,0},{1,13},{5,5},{9,9},{13,1},{2,14},{6,6},{... | collective-permute-start | bytes 1769480 | tf_op jit(solution)/shard_map/ppermute | solution.py:418
  32.8 14.7 %copy-start.2 = (bf16[4,64,256]{2,1,0:T(8,128)(2,1)S(1)}, bf16[4,64,256]{2,1,0:T(8,128)(2,1)}, u32[]{:S(2)}) copy-start(bf16[4,64,256]{2,1,0:T(8,128)(2,1)} %refs_6_.1) | copy-start | bytes 393220
  32.9 29.4 %collective-permute-start.8 = (bf16[2,64,2304]{2,1,0:T(8,128)(2,1)S(1)}, bf16[2,64,2304]{2,1,0:T(8,128)(2,1)S(1)}, u32[]{:S(2)}, u32[]{:S(2)}) collective-permute-start(bf16[2,64,2304]{2,1,0:T(8,128)(2,1)S(1)} %shard_map.77.refs_2_), channel_id=1, source_target_pairs={{0,8},{4,0},{8,12},{12,4},{1,9},{5,1},{9,13},{13,5},{2,10},{6,2},{... | collective-permute-start | bytes 1769480 | tf_op jit(solution)/shard_map/ppermute | solution.py:418
  39.2 1.6 %collective-permute-start.11 = (f32[4,64,128]{2,1,0:T(8,128)S(1)}, f32[4,64,128]{2,1,0:T(8,128)S(1)}, u32[]{:S(2)}, u32[]{:S(2)}) collective-permute-start(f32[4,64,128]{2,1,0:T(8,128)S(1)} %shard_map.78.refs_0_), channel_id=1, source_target_pairs={{0,1},{1,0},{2,3},{3,2},{4,5},{5,4},{6,7},{7,6},{8,9},{9,8},{10,11... | collective-permute-start | bytes 393224 | tf_op jit(solution)/shard_map/ppermute | solution.py:29
  39.3 6.4 %collective-permute-start.12 = (f32[4,64,128]{2,1,0:T(8,128)S(1)}, f32[4,64,128]{2,1,0:T(8,128)S(1)}, u32[]{:S(2)}, u32[]{:S(2)}) collective-permute-start(f32[4,64,128]{2,1,0:T(8,128)S(1)} %shard_map.78.refs_0_), channel_id=1, source_target_pairs={{0,2},{1,3},{2,0},{3,1},{4,6},{5,7},{6,4},{7,5},{8,10},{9,11},{10,... | collective-permute-start | bytes 393224 | tf_op jit(solution)/shard_map/ppermute | solution.py:29
  40.8 6.7 %collective-permute-start.13 = (f32[4,64,128]{2,1,0:T(8,128)S(1)}, f32[4,64,128]{2,1,0:T(8,128)S(1)}, u32[]{:S(2)}, u32[]{:S(2)}) collective-permute-start(f32[4,64,128]{2,1,0:T(8,128)S(1)} %shard_map.78.refs_0_), channel_id=1, source_target_pairs={{0,3},{1,2},{2,1},{3,0},{4,7},{5,6},{6,5},{7,4},{8,11},{9,10},{10,... | collective-permute-start | bytes 393224 | tf_op jit(solution)/shard_map/ppermute | solution.py:29
  53.4 11.6 %collective-permute-start.18 = (f32[2,64,128]{2,1,0:T(8,128)S(1)}, f32[2,64,128]{2,1,0:T(8,128)S(1)}, u32[]{:S(2)}, u32[]{:S(2)}) collective-permute-start(f32[2,64,128]{2,1,0:T(8,128)S(1)} %shard_map.80.refs_1_.refs_0_), channel_id=1, source_target_pairs={{0,1},{1,0},{2,3},{3,2},{4,5},{5,4},{6,7},{7,6},{8,9},{9,8},{10,11... | collective-permute-start | bytes 196616 | tf_op jit(solution)/shard_map/ppermute | solution.py:29
  53.4 11.8 %collective-permute-start.19 = (f32[2,64,128]{2,1,0:T(8,128)S(1)}, f32[2,64,128]{2,1,0:T(8,128)S(1)}, u32[]{:S(2)}, u32[]{:S(2)}) collective-permute-start(f32[2,64,128]{2,1,0:T(8,128)S(1)} %shard_map.80.refs_1_.refs_0_), channel_id=1, source_target_pairs={{0,2},{1,3},{2,0},{3,1},{4,6},{5,7},{6,4},{7,5},{8,10},{9,11},{10,... | collective-permute-start | bytes 196616 | tf_op jit(solution)/shard_map/ppermute | solution.py:29
  55.0 10.2 %collective-permute-start.20 = (f32[2,64,128]{2,1,0:T(8,128)S(1)}, f32[2,64,128]{2,1,0:T(8,128)S(1)}, u32[]{:S(2)}, u32[]{:S(2)}) collective-permute-start(f32[2,64,128]{2,1,0:T(8,128)S(1)} %shard_map.80.refs_1_.refs_0_), channel_id=1, source_target_pairs={{0,3},{1,2},{2,1},{3,0},{4,7},{5,6},{6,5},{7,4},{8,11},{9,10},{10,... | collective-permute-start | bytes 196616 | tf_op jit(solution)/shard_map/ppermute | solution.py:29
  63.3 3.4 %collective-permute-start.15 = (bf16[2,64,128]{2,1,0:T(8,128)(2,1)S(1)}, bf16[2,64,128]{2,1,0:T(8,128)(2,1)S(1)}, u32[]{:S(2)}, u32[]{:S(2)}) collective-permute-start(bf16[2,64,128]{2,1,0:T(8,128)(2,1)S(1)} %shard_map.81.refs_0_), channel_id=1, source_target_pairs={{0,1},{1,0},{2,3},{3,2},{4,5},{5,4},{6,7},{7,6},{8,9},{9,8},{10,11... | collective-permute-start | bytes 98312 | tf_op jit(solution)/shard_map/ppermute | solution.py:29
  63.4 4.0 %collective-permute-start.16 = (bf16[2,64,128]{2,1,0:T(8,128)(2,1)S(1)}, bf16[2,64,128]{2,1,0:T(8,128)(2,1)S(1)}, u32[]{:S(2)}, u32[]{:S(2)}) collective-permute-start(bf16[2,64,128]{2,1,0:T(8,128)(2,1)S(1)} %shard_map.81.refs_0_), channel_id=1, source_target_pairs={{0,2},{1,3},{2,0},{3,1},{4,6},{5,7},{6,4},{7,5},{8,10},{9,11},{10,... | collective-permute-start | bytes 98312 | tf_op jit(solution)/shard_map/ppermute | solution.py:29
  64.9 3.3 %collective-permute-start.17 = (bf16[2,64,128]{2,1,0:T(8,128)(2,1)S(1)}, bf16[2,64,128]{2,1,0:T(8,128)(2,1)S(1)}, u32[]{:S(2)}, u32[]{:S(2)}) collective-permute-start(bf16[2,64,128]{2,1,0:T(8,128)(2,1)S(1)} %shard_map.81.refs_0_), channel_id=1, source_target_pairs={{0,3},{1,2},{2,1},{3,0},{4,7},{5,6},{6,5},{7,4},{8,11},{9,10},{10,... | collective-permute-start | bytes 98312 | tf_op jit(solution)/shard_map/ppermute | solution.py:29

commit v18 on v12

--- a/solution.py
+++ b/solution.py
@@ -9,6 +9,7 @@
 
 ADAPTER_SCALE = 0.5
 ROW_TILE = 256
+PANEL_PIECES = 4
 PARAMS = pltpu.CompilerParams(vmem_limit_bytes=20 * 1024 * 1024)
 NO_COST = pl.CostEstimate(flops=0, bytes_accessed=0, transcendentals=0)
 BASE = pl.CostEstimate(flops=4 * 10**9, bytes_accessed=0, transcendentals=0)
@@ -177,10 +178,21 @@
 def panel_copies(k, slot, down_ref, up_ref, out_ref, sems):
     depth = down_ref.shape[2]
     width = up_ref.shape[2]
-    return [
-        pltpu.make_async_copy(down_ref.at[slot], out_ref.at[k, :, pl.ds(0, depth)], sems.at[k, 0]),
-        pltpu.make_async_copy(up_ref.at[slot], out_ref.at[k, :, pl.ds(depth, width)], sems.at[k, 1]),
-    ]
+    rows = down_ref.shape[1] // PANEL_PIECES
+    copies = []
+    for i in range(PANEL_PIECES):
+        part = pl.ds(i * rows, rows)
+        copies.append(
+            pltpu.make_async_copy(
+                down_ref.at[slot, part], out_ref.at[k, part, pl.ds(0, depth)], sems.at[k, i]
+            )
+        )
+    copies.append(
+        pltpu.make_async_copy(
+            up_ref.at[slot], out_ref.at[k, :, pl.ds(depth, width)], sems.at[k, PANEL_PIECES]
+        )
+    )
+    return copies
 
 
 def plan_kernel(capacity, *refs):
@@ -242,7 +254,7 @@
         ],
         scratch_shapes=[pltpu.SMEM(names.shape, jnp.int32)] * 4
         + [pltpu.SMEM(table.shape, jnp.int32), pltpu.SMEM(live.shape, jnp.int32)]
-        + [pltpu.SemaphoreType.DMA((6,)), pltpu.SemaphoreType.DMA((capacity, 2))],
+        + [pltpu.SemaphoreType.DMA((6,)), pltpu.SemaphoreType.DMA((capacity, PANEL_PIECES + 1))],
         compiler_params=PARAMS,
         cost_estimate=SHORT,
     )(in_hbm(names), *others, in_hbm(table), in_hbm(live), down, up, *after)
@@ -276,7 +288,7 @@
         in_specs=[SMEM] + [ANY] * (len(sources) + len(after)),
         out_specs=ANY,
         out_shape=jax.ShapeDtypeStruct((capacity, rank, depth + width), sources[0].dtype),
-        scratch_shapes=[pltpu.SemaphoreType.DMA((capacity, 2))],
+        scratch_shapes=[pltpu.SemaphoreType.DMA((capacity, PANEL_PIECES + 1))],
         compiler_params=PARAMS,
         cost_estimate=cost or NO_COST,
     )(plan, *sources, *after)

time: 69.9 us -> 70.1 us (level)
  transfers between devices with their start and end apart: 21 -> 21, of which waited for: 6 -> 6; matrix products, arithmetic and copies ran while one was open for 0% -> 0% of each run, Pallas kernels for 28% -> 29%
where the time goes in v18:
time: 70.1 us; the launch traced here: 69.6 us
  starting transfers between devices  31 us (44%)
  Pallas kernels  21.3 us (30%)
  waiting for transfers between devices  17.1 us (24%)
    ppermute x5, starting transfers between devices, across(): return lax.ppermute(value, 'pool', pairs)  16.7 us
    ppermute x16, starting transfers between devices, swap(): return lax.ppermute(value, axis, pairs)  14.3 us
    ppermute x5, waiting for transfers between devices, across(): return lax.ppermute(value, 'pool', pairs)  9.81 us
    ppermute x16, waiting for transfers between devices, swap(): return lax.ppermute(value, axis, pairs)  7.27 us
    pallas_call x1, Pallas kernels, base_chunks(): pl.pallas_call(functools.partial(base_kernel, order), in_specs=[ANY] * 2,...  7.03 us
    pallas_call x3, Pallas kernels, combine(): pl.pallas_call(functools.partial(combine_kernel, shapes, choose, len(part...  4.38 us
    pallas_call x2, Pallas kernels, pack_panels(): pl.pallas_call(functools.partial(pack_kernel, [start for start, *_ in cho...  3.43 us
    pallas_call x3, Pallas kernels, shrink(): pl.pallas_call(functools.partial(shrink_kernel, shapes, choose), in_specs...  3.43 us
  transfers between devices with their start and end apart: 21, of which 6 were waited for; matrix products, arithmetic and copies ran while one was open for 0% of the time, Pallas kernels for 29%

profile of v18, /device:TPU:0, one launch (start us, length us, event | category | flops | bytes accessed | tf_op | source)
XLA Modules:
  0.0 69.6 jit_solution(16579478122822212268)
XLA Ops:
  0.0 3.0 %collective-permute-start = (s32[1,8]{1,0:T(1,128)}, s32[1,8]{1,0:T(1,128)S(1)}, u32[]{:S(2)}, u32[]{:S(2)}) collective-permute-start(s32[1,8]{1,0:T(1,128)} %refs_0_.1), channel_id=1, source_target_pairs={{0,4},{4,0},{8,12},{12,8},{1,5},{5,1},{9,13},{13,9},{2,6},{6,2},{1... | collective-permute-start | bytes 104 | tf_op jit(solution)/shard_map/ppermute | solution.py:30
  3.0 2.6 %collective-permute-start.1 = (s32[1,8]{1,0:T(1,128)}, s32[1,8]{1,0:T(1,128)S(1)}, u32[]{:S(2)}, u32[]{:S(2)}) collective-permute-start(s32[1,8]{1,0:T(1,128)} %refs_0_.1), channel_id=1, source_target_pairs={{0,8},{4,12},{8,0},{12,4},{1,9},{5,13},{9,1},{13,5},{2,10},{6,14},... | collective-permute-start | bytes 104 | tf_op jit(solution)/shard_map/ppermute | solution.py:30
  5.6 0.0 collective-permute-start.2
  5.6 1.6 %collective-permute-start.3 = (bf16[4,64,256]{2,1,0:T(8,128)(2,1)}, bf16[4,64,256]{2,1,0:T(8,128)(2,1)S(1)}, u32[]{:S(2)}, u32[]{:S(2)}) collective-permute-start(bf16[4,64,256]{2,1,0:T(8,128)(2,1)} %refs_6_.1), channel_id=1, source_target_pairs={{0,0},{4,8},{8,4},{12,12},{1,1},{5,9},{9,5},{13,13},{2,2},{6,10},{... | collective-permute-start | bytes 393224 | tf_op jit(solution)/shard_map/ppermute | solution.py:419
  7.2 1.9 %collective-permute-start.4 = (bf16[4,64,2048]{2,1,0:T(8,128)(2,1)}, bf16[4,64,2048]{2,1,0:T(8,128)(2,1)S(1)}, u32[]{:S(2)}, u32[]{:S(2)}) collective-permute-start(bf16[4,64,2048]{2,1,0:T(8,128)(2,1)} %bitcast.14), channel_id=1, source_target_pairs={{0,0},{4,8},{8,4},{12,12},{1,1},{5,9},{9,5},{13,13},{2,2},{6,10},{... | collective-permute-start | bytes 3145736 | tf_op jit(solution)/shard_map/ppermute | solution.py:419
  9.0 7.0 %shard_map.73 = (f32[2,384,256]{2,1,0:T(8,128)S(1)}, f32[2,384,256]{2,1,0:T(8,128)S(1)}, f32[2,256,256]{2,1,0:T(8,128)S(1)}, f32[2,1024,256]{2,1,0:T(8,128)S(1)}) custom-call(bf16[1024,2048]{1,0:T(8,128)(2,1)} %tokens_ref.1, bf16[2048,1024]{1,0:T(8,128)(2,1)} %weight_ref.1), custom_call_target="tpu_custom_call" | custom-call | flops 4000000000 | tf_op jit(solution)/shard_map/pallas_call | solution.py:100
  16.1 0.0 collective-permute-done.refs_1_
  16.1 0.1 collective-permute-start.7
  16.2 0.0 collective-permute-done.1.refs_2_
  16.2 0.5 collective-permute-start.5
  16.7 0.0 collective-permute-done.2.refs_3_
  16.7 0.1 collective-permute-start.6
  16.8 0.0 collective-permute-done.3.refs_8_.refs_1_.refs_6_
  16.8 2.8 %shard_map.74 = (bf16[2,64,2304]{2,1,0:T(8,128)(2,1)S(1)}, s32[28]{0:T(128)S(1)}) custom-call(s32[1,8]{1,0:T(1,128)} %refs_0_.1, s32[1,8]{1,0:T(1,128)S(1)} %collective-permute-done.refs_1_, s32[1,8]{1,0:T(1,128)S(1)} %collective-permute-done.1.refs_2_, s32[1,8]{1,0:T(1,128)S(1)} %collective-permute-done.2.refs_3_, s32[16]{0:T(128)} %refs_4_.1, ...), custom_call_target="tpu_custom_call" | custom-call | flops 10000000000 | tf_op jit(solution)/shard_map/pallas_call | solution.py:247
  19.6 3.4 %collective-permute-start.10 = (bf16[2,64,2304]{2,1,0:T(8,128)(2,1)S(1)}, bf16[2,64,2304]{2,1,0:T(8,128)(2,1)S(1)}, u32[]{:S(2)}, u32[]{:S(2)}) collective-permute-start(bf16[2,64,2304]{2,1,0:T(8,128)(2,1)S(1)} %get-tuple-element.19), channel_id=1, source_target_pairs={{0,4},{4,0},{8,12},{12,8},{1,5},{5,1},{9,13},{13,9},{2,6},{6,2},{1... | collective-permute-start | bytes 1769480 | tf_op jit(solution)/shard_map/ppermute | solution.py:419
  23.0 0.0 collective-permute-done.7.refs_2_
  23.0 0.0 collective-permute-done.5.refs_0_
  23.0 0.0 collective-permute-done.6.refs_1_
  23.0 0.2 shard_map.75
  23.2 1.5 %collective-permute-start.14 = (bf16[1,1024,256]{2,1,0:T(8,128)(2,1)S(1)}, bf16[1,1024,256]{2,1,0:T(8,128)(2,1)S(1)}, u32[]{:S(2)}, u32[]{:S(2)}) collective-permute-start(bf16[1,1024,256]{2,1,0:T(8,128)(2,1)S(1)} %get-tuple-element.20), channel_id=1, source_target_pairs={{0,2},{1,3},{2,0},{3,1},{4,6},{5,7},{6,4},{7,5},{8,10},{9,11},{10,... | collective-permute-start | bytes 1572872 | tf_op jit(solution)/shard_map/ppermute | solution.py:30
  24.8 1.7 %shard_map.76.refs_4_ = bf16[2,64,2304]{2,1,0:T(8,128)(2,1)S(1)} custom-call(s32[28]{0:T(128)S(1)} %get-tuple-element.14.plan_ref, bf16[4,64,2048]{2,1,0:T(8,128)(2,1)} %bitcast.16, bf16[4,64,256]{2,1,0:T(8,128)(2,1)} %refs_6_.1, f32[1024,256]{1,0:T(8,128)S(1)} %bitcast.7), custom_call_target="tpu_custom_call" | custom-call | tf_op jit(solution)/shard_map/pallas_call | solution.py:286
  26.5 0.0 copy-start
  26.5 0.0 copy-start.1
  26.5 4.6 %collective-permute-start.9 = (bf16[2,64,2304]{2,1,0:T(8,128)(2,1)S(1)}, bf16[2,64,2304]{2,1,0:T(8,128)(2,1)S(1)}, u32[]{:S(2)}, u32[]{:S(2)}) collective-permute-start(bf16[2,64,2304]{2,1,0:T(8,128)(2,1)S(1)} %shard_map.76.refs_4_), channel_id=1, source_target_pairs={{0,12},{4,4},{8,8},{12,0},{1,13},{5,5},{9,9},{13,1},{2,14},{6,6},{... | collective-permute-start | bytes 1769480 | tf_op jit(solution)/shard_map/ppermute | solution.py:419
  31.2 0.0 collective-permute-done.4.refs_0_
  31.2 1.7 %shard_map.77.refs_2_ = bf16[2,64,2304]{2,1,0:T(8,128)(2,1)S(1)} custom-call(s32[28]{0:T(128)S(1)} %get-tuple-element.14.plan_ref, bf16[4,64,2048]{2,1,0:T(8,128)(2,1)S(1)} %collective-permute-done.4.refs_0_, bf16[4,64,256]{2,1,0:T(8,128)(2,1)S(1)} %collective-permute-done.3.refs_8_.refs_1_.refs_6_, bf16[4,64,2048]{2,1,0:T(8,128)(2,1)} %bitcast.17, ...), custom_call_target="tpu_custom_call" | custom-call | flops 6000000000 | tf_op jit(solution)/shard_map/pallas_call | solution.py:286
  32.9 0.0 copy-start.2
  32.9 5.2 %collective-permute-start.8 = (bf16[2,64,2304]{2,1,0:T(8,128)(2,1)S(1)}, bf16[2,64,2304]{2,1,0:T(8,128)(2,1)S(1)}, u32[]{:S(2)}, u32[]{:S(2)}) collective-permute-start(bf16[2,64,2304]{2,1,0:T(8,128)(2,1)S(1)} %shard_map.77.refs_2_), channel_id=1, source_target_pairs={{0,8},{4,0},{8,12},{12,4},{1,9},{5,1},{9,13},{13,5},{2,10},{6,2},{... | collective-permute-start | bytes 1769480 | tf_op jit(solution)/shard_map/ppermute | solution.py:419
  38.2 0.0 collective-permute-done.10.refs_1_.refs_7_
  38.2 0.0 copy-done
  38.2 0.0 copy-done.1
  38.2 1.4 %shard_map.78.refs_0_ = f32[4,64,128]{2,1,0:T(8,128)S(1)} custom-call(s32[28]{0:T(128)S(1)} %get-tuple-element.14.plan_ref, bf16[8,128,2048]{2,1,0:T(8,128)(2,1)S(1)} %bitcast.4, bf16[4,64,2048]{2,1,0:T(8,128)(2,1)S(1)} %bitcast.18, bf16[2,64,2304]{2,1,0:T(8,128)(2,1)S(1)} %collective-permute-done.10.refs_1_.refs_7_, bf16[2,64,2304]{2,1,0:T(8,128)(2,1)S(1)} %shard_map.77.refs_2_), custom_call_target="tpu_custom_call" | custom-call | tf_op jit(solution)/shard_map/pallas_call | solution.py:340
  39.6 0.1 collective-permute-start.11
  39.6 1.6 %collective-permute-start.12 = (f32[4,64,128]{2,1,0:T(8,128)S(1)}, f32[4,64,128]{2,1,0:T(8,128)S(1)}, u32[]{:S(2)}, u32[]{:S(2)}) collective-permute-start(f32[4,64,128]{2,1,0:T(8,128)S(1)} %shard_map.78.refs_0_), channel_id=1, source_target_pairs={{0,2},{1,3},{2,0},{3,1},{4,6},{5,7},{6,4},{7,5},{8,10},{9,11},{10,... | collective-permute-start | bytes 393224 | tf_op jit(solution)/shard_map/ppermute | solution.py:30
  41.2 0.0 collective-permute-done.11.refs_1_
  41.2 1.0 %collective-permute-start.13 = (f32[4,64,128]{2,1,0:T(8,128)S(1)}, f32[4,64,128]{2,1,0:T(8,128)S(1)}, u32[]{:S(2)}, u32[]{:S(2)}) collective-permute-start(f32[4,64,128]{2,1,0:T(8,128)S(1)} %shard_map.78.refs_0_), channel_id=1, source_target_pairs={{0,3},{1,2},{2,1},{3,0},{4,7},{5,6},{6,5},{7,4},{8,11},{9,10},{10,... | collective-permute-start | bytes 393224 | tf_op jit(solution)/shard_map/ppermute | solution.py:30
  42.2 3.8 %collective-permute-done.12.refs_2_ = f32[4,64,128]{2,1,0:T(8,128)S(1)} collective-permute-done((f32[4,64,128]{2,1,0:T(8,128)S(1)}, f32[4,64,128]{2,1,0:T(8,128)S(1)}, u32[]{:S(2)}, u32[]{:S(2)}) %collective-permute-start.12) | collective-permute-done | bytes 131104 | tf_op jit(solution)/shard_map/ppermute | solution.py:30
  46.0 1.9 %collective-permute-done.13.refs_3_ = f32[4,64,128]{2,1,0:T(8,128)S(1)} collective-permute-done((f32[4,64,128]{2,1,0:T(8,128)S(1)}, f32[4,64,128]{2,1,0:T(8,128)S(1)}, u32[]{:S(2)}, u32[]{:S(2)}) %collective-permute-start.13) | collective-permute-done | bytes 131104 | tf_op jit(solution)/shard_map/ppermute | solution.py:30
  47.9 0.0 collective-permute-done.14
  47.9 0.0 copy-done.2
  47.9 1.5 %shard_map.79.refs_2_.refs_8_ = bf16[1024,256]{1,0:T(8,128)(2,1)} custom-call(s32[28]{0:T(128)S(1)} %get-tuple-element.14.plan_ref, f32[4,64,128]{2,1,0:T(8,128)S(1)} %shard_map.78.refs_0_, f32[4,64,128]{2,1,0:T(8,128)S(1)} %collective-permute-done.11.refs_1_, f32[4,64,128]{2,1,0:T(8,128)S(1)} %collective-permute-done.12.refs_2_, ...), custom_call_target="tpu_custom_call" | custom-call | tf_op jit(solution)/shard_map/pallas_call | solution.py:402
  49.4 2.9 %collective-permute-done.9.refs_1_.refs_7_ = bf16[2,64,2304]{2,1,0:T(8,128)(2,1)S(1)} collective-permute-done((bf16[2,64,2304]{2,1,0:T(8,128)(2,1)S(1)}, bf16[2,64,2304]{2,1,0:T(8,128)(2,1)S(1)}, u32[]{:S(2)}, u32[]{:S(2)}) %collective-permute-start.9) | collective-permute-done | bytes 589856 | tf_op jit(solution)/shard_map/ppermute | solution.py:419
  52.3 1.0 %shard_map.80.refs_1_.refs_0_ = f32[2,64,128]{2,1,0:T(8,128)S(1)} custom-call(s32[28]{0:T(128)S(1)} %get-tuple-element.14.plan_ref, bf16[8,128,2048]{2,1,0:T(8,128)(2,1)S(1)} %bitcast.5, bf16[4,64,2048]{2,1,0:T(8,128)(2,1)S(1)} %collective-permute-done.4.refs_0_, bf16[2,64,2304]{2,1,0:T(8,128)(2,1)S(1)} %collective-permute-done.9.refs_1_.refs_7_, ...), custom_call_target="tpu_custom_call" | custom-call | tf_op jit(solution)/shard_map/pallas_call | solution.py:340
  53.3 0.1 collective-permute-start.18
  53.4 1.5 %collective-permute-start.19 = (f32[2,64,128]{2,1,0:T(8,128)S(1)}, f32[2,64,128]{2,1,0:T(8,128)S(1)}, u32[]{:S(2)}, u32[]{:S(2)}) collective-permute-start(f32[2,64,128]{2,1,0:T(8,128)S(1)} %shard_map.80.refs_1_.refs_0_), channel_id=1, source_target_pairs={{0,2},{1,3},{2,0},{3,1},{4,6},{5,7},{6,4},{7,5},{8,10},{9,11},{10,... | collective-permute-start | bytes 196616 | tf_op jit(solution)/shard_map/ppermute | solution.py:30
  54.9 0.3 collective-permute-start.20
  55.2 7.0 %collective-permute-done.8.refs_0_.refs_6_ = bf16[2,64,2304]{2,1,0:T(8,128)(2,1)S(1)} collective-permute-done((bf16[2,64,2304]{2,1,0:T(8,128)(2,1)S(1)}, bf16[2,64,2304]{2,1,0:T(8,128)(2,1)S(1)}, u32[]{:S(2)}, u32[]{:S(2)}) %collective-permute-start.8) | collective-permute-done | bytes 589856 | tf_op jit(solution)/shard_map/ppermute | solution.py:419
  62.2 1.0 %shard_map.81.refs_0_ = bf16[2,64,128]{2,1,0:T(8,128)(2,1)S(1)} custom-call(s32[28]{0:T(128)S(1)} %get-tuple-element.14.plan_ref, bf16[8,128,2048]{2,1,0:T(8,128)(2,1)S(1)} %bitcast.6, bf16[2,64,2304]{2,1,0:T(8,128)(2,1)S(1)} %collective-permute-done.8.refs_0_.refs_6_, f32[2,64,128]{2,1,0:T(8,128)S(1)} %shard_map.80.refs_1_.refs_0_), custom_call_target="tpu_custom_call" | custom-call | tf_op jit(solution)/shard_map/pallas_call | solution.py:340
  63.2 0.1 collective-permute-start.15
  63.3 1.5 %collective-permute-start.16 = (bf16[2,64,128]{2,1,0:T(8,128)(2,1)S(1)}, bf16[2,64,128]{2,1,0:T(8,128)(2,1)S(1)}, u32[]{:S(2)}, u32[]{:S(2)}) collective-permute-start(bf16[2,64,128]{2,1,0:T(8,128)(2,1)S(1)} %shard_map.81.refs_0_), channel_id=1, source_target_pairs={{0,2},{1,3},{2,0},{3,1},{4,6},{5,7},{6,4},{7,5},{8,10},{9,11},{10,... | collective-permute-start | bytes 98312 | tf_op jit(solution)/shard_map/ppermute | solution.py:30
  64.8 0.0 collective-permute-done.18.refs_1_
  64.8 0.3 collective-permute-start.17
  65.2 0.0 collective-permute-done.19.refs_2_
  65.2 0.0 collective-permute-done.20.refs_3_
  65.2 1.4 %shard_map.82.refs_7_ = bf16[1024,256]{1,0:T(8,128)(2,1)} custom-call(s32[28]{0:T(128)S(1)} %get-tuple-element.14.plan_ref, f32[2,64,128]{2,1,0:T(8,128)S(1)} %shard_map.80.refs_1_.refs_0_, f32[2,64,128]{2,1,0:T(8,128)S(1)} %collective-permute-done.18.refs_1_, f32[2,64,128]{2,1,0:T(8,128)S(1)} %collective-permute-done.19.refs_2_, ...), custom_call_target="tpu_custom_call", output_to_operand_aliasing={{}: (9, {})} | custom-call | tf_op jit(solution)/shard_map/pallas_call | solution.py:402
  66.6 0.0 collective-permute-done.15.refs_1_
  66.6 0.6 collective-permute-done.16.refs_2_
  67.3 0.9 %collective-permute-done.17.refs_3_ = bf16[2,64,128]{2,1,0:T(8,128)(2,1)S(1)} collective-permute-done((bf16[2,64,128]{2,1,0:T(8,128)(2,1)S(1)}, bf16[2,64,128]{2,1,0:T(8,128)(2,1)S(1)}, u32[]{:S(2)}, u32[]{:S(2)}) %collective-permute-start.17) | collective-permute-done | bytes 32800 | tf_op jit(solution)/shard_map/ppermute | solution.py:30
  68.2 1.4 %shard_map.83 = bf16[1024,256]{1,0:T(8,128)(2,1)} custom-call(s32[28]{0:T(128)S(1)} %get-tuple-element.14.plan_ref, bf16[2,64,128]{2,1,0:T(8,128)(2,1)S(1)} %shard_map.81.refs_0_, bf16[2,64,128]{2,1,0:T(8,128)(2,1)S(1)} %collective-permute-done.15.refs_1_, bf16[2,64,128]{2,1,0:T(8,128)(2,1)S(1)} %collective-permute-done.16.refs_2_, ...), custom_call_target="tpu_custom_call", output_to_operand_aliasing={{}: (8, {})} | custom-call | tf_op jit(solution)/shard_map/pallas_call | solution.py:402
Async XLA Ops:
  0.0 16.1 %collective-permute-start = (s32[1,8]{1,0:T(1,128)}, s32[1,8]{1,0:T(1,128)S(1)}, u32[]{:S(2)}, u32[]{:S(2)}) collective-permute-start(s32[1,8]{1,0:T(1,128)} %refs_0_.1), channel_id=1, source_target_pairs={{0,4},{4,0},{8,12},{12,8},{1,5},{5,1},{9,13},{13,9},{2,6},{6,2},{1... | collective-permute-start | bytes 104 | tf_op jit(solution)/shard_map/ppermute | solution.py:30
  3.0 13.1 %collective-permute-start.1 = (s32[1,8]{1,0:T(1,128)}, s32[1,8]{1,0:T(1,128)S(1)}, u32[]{:S(2)}, u32[]{:S(2)}) collective-permute-start(s32[1,8]{1,0:T(1,128)} %refs_0_.1), channel_id=1, source_target_pairs={{0,8},{4,12},{8,0},{12,4},{1,9},{5,13},{9,1},{13,5},{2,10},{6,14},... | collective-permute-start | bytes 104 | tf_op jit(solution)/shard_map/ppermute | solution.py:30
  5.6 11.1 %collective-permute-start.2 = (s32[1,8]{1,0:T(1,128)}, s32[1,8]{1,0:T(1,128)S(1)}, u32[]{:S(2)}, u32[]{:S(2)}) collective-permute-start(s32[1,8]{1,0:T(1,128)} %refs_0_.1), channel_id=1, source_target_pairs={{0,12},{4,8},{8,4},{12,0},{1,13},{5,9},{9,5},{13,1},{2,14},{6,10},... | collective-permute-start | bytes 104 | tf_op jit(solution)/shard_map/ppermute | solution.py:30
  5.6 11.1 %collective-permute-start.3 = (bf16[4,64,256]{2,1,0:T(8,128)(2,1)}, bf16[4,64,256]{2,1,0:T(8,128)(2,1)S(1)}, u32[]{:S(2)}, u32[]{:S(2)}) collective-permute-start(bf16[4,64,256]{2,1,0:T(8,128)(2,1)} %refs_6_.1), channel_id=1, source_target_pairs={{0,0},{4,8},{8,4},{12,12},{1,1},{5,9},{9,5},{13,13},{2,2},{6,10},{... | collective-permute-start | bytes 393224 | tf_op jit(solution)/shard_map/ppermute | solution.py:419
  7.2 24.0 %collective-permute-start.4 = (bf16[4,64,2048]{2,1,0:T(8,128)(2,1)}, bf16[4,64,2048]{2,1,0:T(8,128)(2,1)S(1)}, u32[]{:S(2)}, u32[]{:S(2)}) collective-permute-start(bf16[4,64,2048]{2,1,0:T(8,128)(2,1)} %bitcast.14), channel_id=1, source_target_pairs={{0,0},{4,8},{8,4},{12,12},{1,1},{5,9},{9,5},{13,13},{2,2},{6,10},{... | collective-permute-start | bytes 3145736 | tf_op jit(solution)/shard_map/ppermute | solution.py:419
  16.1 6.9 %collective-permute-start.7 = (f32[2,256,256]{2,1,0:T(8,128)S(1)}, f32[2,256,256]{2,1,0:T(8,128)S(1)}, u32[]{:S(2)}, u32[]{:S(2)}) collective-permute-start(f32[2,256,256]{2,1,0:T(8,128)S(1)} %get-tuple-element.13.refs_9_), channel_id=1, source_target_pairs={{0,1},{1,0},{2,3},{3,2},{4,5},{5,4},{6,7},{7,6},{8,9},{9,8},{10,11... | collective-permute-start | bytes 1572872 | tf_op jit(solution)/shard_map/ppermute | solution.py:30
  16.2 6.8 %collective-permute-start.5 = (f32[2,384,256]{2,1,0:T(8,128)S(1)}, f32[2,384,256]{2,1,0:T(8,128)S(1)}, u32[]{:S(2)}, u32[]{:S(2)}) collective-permute-start(f32[2,384,256]{2,1,0:T(8,128)S(1)} %get-tuple-element.16), channel_id=1, source_target_pairs={{0,1},{1,0},{2,3},{3,2},{4,5},{5,4},{6,7},{7,6},{8,9},{9,8},{10,11... | collective-permute-start | bytes 2359304 | tf_op jit(solution)/shard_map/ppermute | solution.py:30
  16.7 6.3 %collective-permute-start.6 = (f32[2,384,256]{2,1,0:T(8,128)S(1)}, f32[2,384,256]{2,1,0:T(8,128)S(1)}, u32[]{:S(2)}, u32[]{:S(2)}) collective-permute-start(f32[2,384,256]{2,1,0:T(8,128)S(1)} %get-tuple-element.17), channel_id=1, source_target_pairs={{0,1},{1,0},{2,3},{3,2},{4,5},{5,4},{6,7},{7,6},{8,9},{9,8},{10,11... | collective-permute-start | bytes 2359304 | tf_op jit(solution)/shard_map/ppermute | solution.py:30
  19.6 18.6 %collective-permute-start.10 = (bf16[2,64,2304]{2,1,0:T(8,128)(2,1)S(1)}, bf16[2,64,2304]{2,1,0:T(8,128)(2,1)S(1)}, u32[]{:S(2)}, u32[]{:S(2)}) collective-permute-start(bf16[2,64,2304]{2,1,0:T(8,128)(2,1)S(1)} %get-tuple-element.19), channel_id=1, source_target_pairs={{0,4},{4,0},{8,12},{12,8},{1,5},{5,1},{9,13},{13,9},{2,6},{6,2},{1... | collective-permute-start | bytes 1769480 | tf_op jit(solution)/shard_map/ppermute | solution.py:419
  23.2 24.7 %collective-permute-start.14 = (bf16[1,1024,256]{2,1,0:T(8,128)(2,1)S(1)}, bf16[1,1024,256]{2,1,0:T(8,128)(2,1)S(1)}, u32[]{:S(2)}, u32[]{:S(2)}) collective-permute-start(bf16[1,1024,256]{2,1,0:T(8,128)(2,1)S(1)} %get-tuple-element.20), channel_id=1, source_target_pairs={{0,2},{1,3},{2,0},{3,1},{4,6},{5,7},{6,4},{7,5},{8,10},{9,11},{10,... | collective-permute-start | bytes 1572872 | tf_op jit(solution)/shard_map/ppermute | solution.py:30
  26.5 11.7 %copy-start = (bf16[1024,2048]{1,0:T(8,128)(2,1)S(1)}, bf16[1024,2048]{1,0:T(8,128)(2,1)}, u32[]{:S(2)}) copy-start(bf16[1024,2048]{1,0:T(8,128)(2,1)} %tokens_ref.1) | copy-start | bytes 12582916
  26.5 11.7 %copy-start.1 = (bf16[4,2048,64]{1,2,0:T(8,128)(2,1)S(1)}, bf16[4,2048,64]{1,2,0:T(8,128)(2,1)}, u32[]{:S(2)}) copy-start(bf16[4,2048,64]{1,2,0:T(8,128)(2,1)} %param.9) | copy-start | bytes 3145732
  26.5 25.7 %collective-permute-start.9 = (bf16[2,64,2304]{2,1,0:T(8,128)(2,1)S(1)}, bf16[2,64,2304]{2,1,0:T(8,128)(2,1)S(1)}, u32[]{:S(2)}, u32[]{:S(2)}) collective-permute-start(bf16[2,64,2304]{2,1,0:T(8,128)(2,1)S(1)} %shard_map.76.refs_4_), channel_id=1, source_target_pairs={{0,12},{4,4},{8,8},{12,0},{1,13},{5,5},{9,9},{13,1},{2,14},{6,6},{... | collective-permute-start | bytes 1769480 | tf_op jit(solution)/shard_map/ppermute | solution.py:419
  32.9 15.0 %copy-start.2 = (bf16[4,64,256]{2,1,0:T(8,128)(2,1)S(1)}, bf16[4,64,256]{2,1,0:T(8,128)(2,1)}, u32[]{:S(2)}) copy-start(bf16[4,64,256]{2,1,0:T(8,128)(2,1)} %refs_6_.1) | copy-start | bytes 393220
  32.9 29.3 %collective-permute-start.8 = (bf16[2,64,2304]{2,1,0:T(8,128)(2,1)S(1)}, bf16[2,64,2304]{2,1,0:T(8,128)(2,1)S(1)}, u32[]{:S(2)}, u32[]{:S(2)}) collective-permute-start(bf16[2,64,2304]{2,1,0:T(8,128)(2,1)S(1)} %shard_map.77.refs_2_), channel_id=1, source_target_pairs={{0,8},{4,0},{8,12},{12,4},{1,9},{5,1},{9,13},{13,5},{2,10},{6,2},{... | collective-permute-start | bytes 1769480 | tf_op jit(solution)/shard_map/ppermute | solution.py:419
  39.6 1.6 %collective-permute-start.11 = (f32[4,64,128]{2,1,0:T(8,128)S(1)}, f32[4,64,128]{2,1,0:T(8,128)S(1)}, u32[]{:S(2)}, u32[]{:S(2)}) collective-permute-start(f32[4,64,128]{2,1,0:T(8,128)S(1)} %shard_map.78.refs_0_), channel_id=1, source_target_pairs={{0,1},{1,0},{2,3},{3,2},{4,5},{5,4},{6,7},{7,6},{8,9},{9,8},{10,11... | collective-permute-start | bytes 393224 | tf_op jit(solution)/shard_map/ppermute | solution.py:30
  39.6 6.4 %collective-permute-start.12 = (f32[4,64,128]{2,1,0:T(8,128)S(1)}, f32[4,64,128]{2,1,0:T(8,128)S(1)}, u32[]{:S(2)}, u32[]{:S(2)}) collective-permute-start(f32[4,64,128]{2,1,0:T(8,128)S(1)} %shard_map.78.refs_0_), channel_id=1, source_target_pairs={{0,2},{1,3},{2,0},{3,1},{4,6},{5,7},{6,4},{7,5},{8,10},{9,11},{10,... | collective-permute-start | bytes 393224 | tf_op jit(solution)/shard_map/ppermute | solution.py:30
  41.2 6.7 %collective-permute-start.13 = (f32[4,64,128]{2,1,0:T(8,128)S(1)}, f32[4,64,128]{2,1,0:T(8,128)S(1)}, u32[]{:S(2)}, u32[]{:S(2)}) collective-permute-start(f32[4,64,128]{2,1,0:T(8,128)S(1)} %shard_map.78.refs_0_), channel_id=1, source_target_pairs={{0,3},{1,2},{2,1},{3,0},{4,7},{5,6},{6,5},{7,4},{8,11},{9,10},{10,... | collective-permute-start | bytes 393224 | tf_op jit(solution)/shard_map/ppermute | solution.py:30
  53.3 11.5 %collective-permute-start.18 = (f32[2,64,128]{2,1,0:T(8,128)S(1)}, f32[2,64,128]{2,1,0:T(8,128)S(1)}, u32[]{:S(2)}, u32[]{:S(2)}) collective-permute-start(f32[2,64,128]{2,1,0:T(8,128)S(1)} %shard_map.80.refs_1_.refs_0_), channel_id=1, source_target_pairs={{0,1},{1,0},{2,3},{3,2},{4,5},{5,4},{6,7},{7,6},{8,9},{9,8},{10,11... | collective-permute-start | bytes 196616 | tf_op jit(solution)/shard_map/ppermute | solution.py:30
  53.4 11.8 %collective-permute-start.19 = (f32[2,64,128]{2,1,0:T(8,128)S(1)}, f32[2,64,128]{2,1,0:T(8,128)S(1)}, u32[]{:S(2)}, u32[]{:S(2)}) collective-permute-start(f32[2,64,128]{2,1,0:T(8,128)S(1)} %shard_map.80.refs_1_.refs_0_), channel_id=1, source_target_pairs={{0,2},{1,3},{2,0},{3,1},{4,6},{5,7},{6,4},{7,5},{8,10},{9,11},{10,... | collective-permute-start | bytes 196616 | tf_op jit(solution)/shard_map/ppermute | solution.py:30
  54.9 10.3 %collective-permute-start.20 = (f32[2,64,128]{2,1,0:T(8,128)S(1)}, f32[2,64,128]{2,1,0:T(8,128)S(1)}, u32[]{:S(2)}, u32[]{:S(2)}) collective-permute-start(f32[2,64,128]{2,1,0:T(8,128)S(1)} %shard_map.80.refs_1_.refs_0_), channel_id=1, source_target_pairs={{0,3},{1,2},{2,1},{3,0},{4,7},{5,6},{6,5},{7,4},{8,11},{9,10},{10,... | collective-permute-start | bytes 196616 | tf_op jit(solution)/shard_map/ppermute | solution.py:30
  63.2 3.4 %collective-permute-start.15 = (bf16[2,64,128]{2,1,0:T(8,128)(2,1)S(1)}, bf16[2,64,128]{2,1,0:T(8,128)(2,1)S(1)}, u32[]{:S(2)}, u32[]{:S(2)}) collective-permute-start(bf16[2,64,128]{2,1,0:T(8,128)(2,1)S(1)} %shard_map.81.refs_0_), channel_id=1, source_target_pairs={{0,1},{1,0},{2,3},{3,2},{4,5},{5,4},{6,7},{7,6},{8,9},{9,8},{10,11... | collective-permute-start | bytes 98312 | tf_op jit(solution)/shard_map/ppermute | solution.py:30
  63.3 4.0 %collective-permute-start.16 = (bf16[2,64,128]{2,1,0:T(8,128)(2,1)S(1)}, bf16[2,64,128]{2,1,0:T(8,128)(2,1)S(1)}, u32[]{:S(2)}, u32[]{:S(2)}) collective-permute-start(bf16[2,64,128]{2,1,0:T(8,128)(2,1)S(1)} %shard_map.81.refs_0_), channel_id=1, source_target_pairs={{0,2},{1,3},{2,0},{3,1},{4,6},{5,7},{6,4},{7,5},{8,10},{9,11},{10,... | collective-permute-start | bytes 98312 | tf_op jit(solution)/shard_map/ppermute | solution.py:30
  64.8 3.3 %collective-permute-start.17 = (bf16[2,64,128]{2,1,0:T(8,128)(2,1)S(1)}, bf16[2,64,128]{2,1,0:T(8,128)(2,1)S(1)}, u32[]{:S(2)}, u32[]{:S(2)}) collective-permute-start(bf16[2,64,128]{2,1,0:T(8,128)(2,1)S(1)} %shard_map.81.refs_0_), channel_id=1, source_target_pairs={{0,3},{1,2},{2,1},{3,0},{4,7},{5,6},{6,5},{7,4},{8,11},{9,10},{10,... | collective-permute-start | bytes 98312 | tf_op jit(solution)/shard_map/ppermute | solution.py:30

commit v19 on v12

--- a/solution.py
+++ b/solution.py
@@ -411,7 +411,7 @@
     inner_down = across(down, [(0, 0), (1, 2), (2, 1), (3, 3)])
     sent, kept = base_parts(tokens, weight, up.shape[2])
     choose = INNER * capacity
-    held = in_hbm(down), in_hbm(up)
+    held = down, up
     near_out, plan = make_plan(
         names, others, table, live, *held, capacity, [inner_up, sent[-1]]
     )

time: 69.9 us -> 69 us (0.987)
  Pallas kernels: 21.1 us -> 18.1 us
  starting transfers between devices: 30.9 us -> 33.8 us
  waiting for transfers between devices: 17.3 us -> 16.6 us
    ppermute x5, starting transfers between devices: 16.6 us -> 19.5 us  [across(): return lax.ppermute(value, 'pool', pairs)]
    pallas_call x2, Pallas kernels: 3.31 us -> 1.29 us  [pack_panels(): pl.pallas_call(functools.partial(pack_kernel, [start for start, *_ in cho...]
    pallas_call x1, Pallas kernels: 2.7 us -> 1.77 us  [make_plan(): pl.pallas_call(functools.partial(plan_kernel, capacity), in_specs=[ANY] *...]
    ppermute x5, waiting for transfers between devices: 10.1 us -> 9.3 us  [across(): return lax.ppermute(value, 'pool', pairs)]
  transfers between devices with their start and end apart: 21 -> 21, of which waited for: 6 -> 6; matrix products, arithmetic and copies ran while one was open for 0% -> 0% of each run, Pallas kernels for 28% -> 24%
where the time goes in v19:
time: 69 us; the launch traced here: 68.7 us
  starting transfers between devices  33.8 us (49%)
  Pallas kernels  18.1 us (26%)
  waiting for transfers between devices  16.6 us (24%)
    ppermute x5, starting transfers between devices, across(): return lax.ppermute(value, 'pool', pairs)  19.5 us
    ppermute x16, starting transfers between devices, swap(): return lax.ppermute(value, axis, pairs)  14.3 us
    ppermute x5, waiting for transfers between devices, across(): return lax.ppermute(value, 'pool', pairs)  9.3 us
    ppermute x16, waiting for transfers between devices, swap(): return lax.ppermute(value, axis, pairs)  7.29 us
    pallas_call x1, Pallas kernels, base_chunks(): pl.pallas_call(functools.partial(base_kernel, order), in_specs=[ANY] * 2,...  7.04 us
    pallas_call x3, Pallas kernels, combine(): pl.pallas_call(functools.partial(combine_kernel, shapes, choose, len(part...  4.38 us
    pallas_call x3, Pallas kernels, shrink(): pl.pallas_call(functools.partial(shrink_kernel, shapes, choose), in_specs...  3.43 us
    pallas_call x1, Pallas kernels, make_plan(): pl.pallas_call(functools.partial(plan_kernel, capacity), in_specs=[ANY] *...  1.77 us
  transfers between devices with their start and end apart: 21, of which 6 were waited for; matrix products, arithmetic and copies ran while one was open for 0% of the time, Pallas kernels for 24%

profile of v19, /device:TPU:0, one launch (start us, length us, event | category | flops | bytes accessed | tf_op | source)
XLA Modules:
  0.0 68.7 jit_solution(17788077957784127566)
XLA Ops:
  0.0 3.0 %collective-permute-start = (s32[1,8]{1,0:T(1,128)}, s32[1,8]{1,0:T(1,128)S(1)}, u32[]{:S(2)}, u32[]{:S(2)}) collective-permute-start(s32[1,8]{1,0:T(1,128)} %refs_0_.1), channel_id=1, source_target_pairs={{0,4},{4,0},{8,12},{12,8},{1,5},{5,1},{9,13},{13,9},{2,6},{6,2},{1... | collective-permute-start | bytes 104 | tf_op jit(solution)/shard_map/ppermute | solution.py:29
  3.0 2.6 %collective-permute-start.1 = (s32[1,8]{1,0:T(1,128)}, s32[1,8]{1,0:T(1,128)S(1)}, u32[]{:S(2)}, u32[]{:S(2)}) collective-permute-start(s32[1,8]{1,0:T(1,128)} %refs_0_.1), channel_id=1, source_target_pairs={{0,8},{4,12},{8,0},{12,4},{1,9},{5,13},{9,1},{13,5},{2,10},{6,14},... | collective-permute-start | bytes 104 | tf_op jit(solution)/shard_map/ppermute | solution.py:29
  5.6 0.0 collective-permute-start.2
  5.6 1.6 %collective-permute-start.3 = (bf16[4,64,256]{2,1,0:T(8,128)(2,1)}, bf16[4,64,256]{2,1,0:T(8,128)(2,1)S(1)}, u32[]{:S(2)}, u32[]{:S(2)}) collective-permute-start(bf16[4,64,256]{2,1,0:T(8,128)(2,1)} %refs_6_.1), channel_id=1, source_target_pairs={{0,0},{4,8},{8,4},{12,12},{1,1},{5,9},{9,5},{13,13},{2,2},{6,10},{... | collective-permute-start | bytes 393224 | tf_op jit(solution)/shard_map/ppermute | solution.py:407
  7.2 0.0 copy-start.1
  7.2 0.0 copy-start.2
  7.2 2.0 %collective-permute-start.4 = (bf16[4,64,2048]{2,1,0:T(8,128)(2,1)}, bf16[4,64,2048]{2,1,0:T(8,128)(2,1)S(1)}, u32[]{:S(2)}, u32[]{:S(2)}) collective-permute-start(bf16[4,64,2048]{2,1,0:T(8,128)(2,1)} %bitcast.14), channel_id=1, source_target_pairs={{0,0},{4,8},{8,4},{12,12},{1,1},{5,9},{9,5},{13,13},{2,2},{6,10},{... | collective-permute-start | bytes 3145736 | tf_op jit(solution)/shard_map/ppermute | solution.py:407
  9.2 7.0 %shard_map.73 = (f32[2,384,256]{2,1,0:T(8,128)S(1)}, f32[2,384,256]{2,1,0:T(8,128)S(1)}, f32[2,256,256]{2,1,0:T(8,128)S(1)}, f32[2,1024,256]{2,1,0:T(8,128)S(1)}) custom-call(bf16[1024,2048]{1,0:T(8,128)(2,1)} %tokens_ref.1, bf16[2048,1024]{1,0:T(8,128)(2,1)} %weight_ref.1), custom_call_target="tpu_custom_call" | custom-call | flops 4000000000 | tf_op jit(solution)/shard_map/pallas_call | solution.py:99
  16.2 0.0 collective-permute-done.refs_1_
  16.2 0.1 collective-permute-start.7
  16.3 0.0 collective-permute-done.1.refs_2_
  16.3 0.5 collective-permute-start.5
  16.8 0.0 collective-permute-done.2.refs_3_
  16.8 0.1 collective-permute-start.6
  16.9 0.0 collective-permute-done.3.refs_8_.refs_1_.refs_6_
  16.9 0.0 copy-done.1
  16.9 0.0 copy-done.2
  16.9 1.8 %shard_map.74 = (bf16[2,64,2304]{2,1,0:T(8,128)(2,1)S(1)}, s32[28]{0:T(128)S(1)}) custom-call(s32[1,8]{1,0:T(1,128)} %refs_0_.1, s32[1,8]{1,0:T(1,128)S(1)} %collective-permute-done.refs_1_, s32[1,8]{1,0:T(1,128)S(1)} %collective-permute-done.1.refs_2_, s32[1,8]{1,0:T(1,128)S(1)} %collective-permute-done.2.refs_3_, s32[16]{0:T(128)} %refs_4_.1, ...), custom_call_target="tpu_custom_call" | custom-call | flops 10000000000 | tf_op jit(solution)/shard_map/pallas_call | solution.py:235
  18.7 3.4 %collective-permute-start.10 = (bf16[2,64,2304]{2,1,0:T(8,128)(2,1)S(1)}, bf16[2,64,2304]{2,1,0:T(8,128)(2,1)S(1)}, u32[]{:S(2)}, u32[]{:S(2)}) collective-permute-start(bf16[2,64,2304]{2,1,0:T(8,128)(2,1)S(1)} %get-tuple-element.19), channel_id=1, source_target_pairs={{0,4},{4,0},{8,12},{12,8},{1,5},{5,1},{9,13},{13,9},{2,6},{6,2},{1... | collective-permute-start | bytes 1769480 | tf_op jit(solution)/shard_map/ppermute | solution.py:407
  22.1 0.0 collective-permute-done.7.refs_2_
  22.1 0.0 collective-permute-done.5.refs_0_
  22.1 0.0 collective-permute-done.6.refs_1_
  22.1 0.2 shard_map.75
  22.3 1.6 %collective-permute-start.14 = (bf16[1,1024,256]{2,1,0:T(8,128)(2,1)S(1)}, bf16[1,1024,256]{2,1,0:T(8,128)(2,1)S(1)}, u32[]{:S(2)}, u32[]{:S(2)}) collective-permute-start(bf16[1,1024,256]{2,1,0:T(8,128)(2,1)S(1)} %get-tuple-element.20), channel_id=1, source_target_pairs={{0,2},{1,3},{2,0},{3,1},{4,6},{5,7},{6,4},{7,5},{8,10},{9,11},{10,... | collective-permute-start | bytes 1572872 | tf_op jit(solution)/shard_map/ppermute | solution.py:29
  23.9 0.6 shard_map.76.refs_4_
  24.5 0.0 copy-start
  24.5 4.6 %collective-permute-start.9 = (bf16[2,64,2304]{2,1,0:T(8,128)(2,1)S(1)}, bf16[2,64,2304]{2,1,0:T(8,128)(2,1)S(1)}, u32[]{:S(2)}, u32[]{:S(2)}) collective-permute-start(bf16[2,64,2304]{2,1,0:T(8,128)(2,1)S(1)} %shard_map.76.refs_4_), channel_id=1, source_target_pairs={{0,12},{4,4},{8,8},{12,0},{1,13},{5,5},{9,9},{13,1},{2,14},{6,6},{... | collective-permute-start | bytes 1769480 | tf_op jit(solution)/shard_map/ppermute | solution.py:407
  29.2 0.0 collective-permute-done.4.refs_0_
  29.2 0.7 shard_map.77.refs_2_
  29.8 7.9 %collective-permute-start.8 = (bf16[2,64,2304]{2,1,0:T(8,128)(2,1)S(1)}, bf16[2,64,2304]{2,1,0:T(8,128)(2,1)S(1)}, u32[]{:S(2)}, u32[]{:S(2)}) collective-permute-start(bf16[2,64,2304]{2,1,0:T(8,128)(2,1)S(1)} %shard_map.77.refs_2_), channel_id=1, source_target_pairs={{0,8},{4,0},{8,12},{12,4},{1,9},{5,1},{9,13},{13,5},{2,10},{6,2},{... | collective-permute-start | bytes 1769480 | tf_op jit(solution)/shard_map/ppermute | solution.py:407
  37.8 0.0 collective-permute-done.10.refs_1_.refs_7_
  37.8 0.0 copy-done
  37.8 1.4 %shard_map.78.refs_0_ = f32[4,64,128]{2,1,0:T(8,128)S(1)} custom-call(s32[28]{0:T(128)S(1)} %get-tuple-element.14.plan_ref, bf16[8,128,2048]{2,1,0:T(8,128)(2,1)S(1)} %bitcast.4, bf16[4,64,2048]{2,1,0:T(8,128)(2,1)S(1)} %bitcast.18, bf16[2,64,2304]{2,1,0:T(8,128)(2,1)S(1)} %collective-permute-done.10.refs_1_.refs_7_, bf16[2,64,2304]{2,1,0:T(8,128)(2,1)S(1)} %shard_map.77.refs_2_), custom_call_target="tpu_custom_call" | custom-call | tf_op jit(solution)/shard_map/pallas_call | solution.py:328
  39.2 0.1 collective-permute-start.11
  39.2 1.6 %collective-permute-start.12 = (f32[4,64,128]{2,1,0:T(8,128)S(1)}, f32[4,64,128]{2,1,0:T(8,128)S(1)}, u32[]{:S(2)}, u32[]{:S(2)}) collective-permute-start(f32[4,64,128]{2,1,0:T(8,128)S(1)} %shard_map.78.refs_0_), channel_id=1, source_target_pairs={{0,2},{1,3},{2,0},{3,1},{4,6},{5,7},{6,4},{7,5},{8,10},{9,11},{10,... | collective-permute-start | bytes 393224 | tf_op jit(solution)/shard_map/ppermute | solution.py:29
  40.8 0.0 collective-permute-done.11.refs_1_
  40.8 1.0 %collective-permute-start.13 = (f32[4,64,128]{2,1,0:T(8,128)S(1)}, f32[4,64,128]{2,1,0:T(8,128)S(1)}, u32[]{:S(2)}, u32[]{:S(2)}) collective-permute-start(f32[4,64,128]{2,1,0:T(8,128)S(1)} %shard_map.78.refs_0_), channel_id=1, source_target_pairs={{0,3},{1,2},{2,1},{3,0},{4,7},{5,6},{6,5},{7,4},{8,11},{9,10},{10,... | collective-permute-start | bytes 393224 | tf_op jit(solution)/shard_map/ppermute | solution.py:29
  41.8 3.8 %collective-permute-done.12.refs_2_ = f32[4,64,128]{2,1,0:T(8,128)S(1)} collective-permute-done((f32[4,64,128]{2,1,0:T(8,128)S(1)}, f32[4,64,128]{2,1,0:T(8,128)S(1)}, u32[]{:S(2)}, u32[]{:S(2)}) %collective-permute-start.12) | collective-permute-done | bytes 131104 | tf_op jit(solution)/shard_map/ppermute | solution.py:29
  45.6 1.9 %collective-permute-done.13.refs_3_ = f32[4,64,128]{2,1,0:T(8,128)S(1)} collective-permute-done((f32[4,64,128]{2,1,0:T(8,128)S(1)}, f32[4,64,128]{2,1,0:T(8,128)S(1)}, u32[]{:S(2)}, u32[]{:S(2)}) %collective-permute-start.13) | collective-permute-done | bytes 131104 | tf_op jit(solution)/shard_map/ppermute | solution.py:29
  47.5 0.0 collective-permute-done.14
  47.5 1.5 %shard_map.79.refs_2_.refs_8_ = bf16[1024,256]{1,0:T(8,128)(2,1)} custom-call(s32[28]{0:T(128)S(1)} %get-tuple-element.14.plan_ref, f32[4,64,128]{2,1,0:T(8,128)S(1)} %shard_map.78.refs_0_, f32[4,64,128]{2,1,0:T(8,128)S(1)} %collective-permute-done.11.refs_1_, f32[4,64,128]{2,1,0:T(8,128)S(1)} %collective-permute-done.12.refs_2_, ...), custom_call_target="tpu_custom_call" | custom-call | tf_op jit(solution)/shard_map/pallas_call | solution.py:390
  49.0 2.4 %collective-permute-done.9.refs_1_.refs_7_ = bf16[2,64,2304]{2,1,0:T(8,128)(2,1)S(1)} collective-permute-done((bf16[2,64,2304]{2,1,0:T(8,128)(2,1)S(1)}, bf16[2,64,2304]{2,1,0:T(8,128)(2,1)S(1)}, u32[]{:S(2)}, u32[]{:S(2)}) %collective-permute-start.9) | collective-permute-done | bytes 589856 | tf_op jit(solution)/shard_map/ppermute | solution.py:407
  51.4 1.0 %shard_map.80.refs_1_.refs_0_ = f32[2,64,128]{2,1,0:T(8,128)S(1)} custom-call(s32[28]{0:T(128)S(1)} %get-tuple-element.14.plan_ref, bf16[8,128,2048]{2,1,0:T(8,128)(2,1)S(1)} %bitcast.5, bf16[4,64,2048]{2,1,0:T(8,128)(2,1)S(1)} %collective-permute-done.4.refs_0_, bf16[2,64,2304]{2,1,0:T(8,128)(2,1)S(1)} %collective-permute-done.9.refs_1_.refs_7_, ...), custom_call_target="tpu_custom_call" | custom-call | tf_op jit(solution)/shard_map/pallas_call | solution.py:328
  52.4 0.1 collective-permute-start.18
  52.5 1.5 %collective-permute-start.19 = (f32[2,64,128]{2,1,0:T(8,128)S(1)}, f32[2,64,128]{2,1,0:T(8,128)S(1)}, u32[]{:S(2)}, u32[]{:S(2)}) collective-permute-start(f32[2,64,128]{2,1,0:T(8,128)S(1)} %shard_map.80.refs_1_.refs_0_), channel_id=1, source_target_pairs={{0,2},{1,3},{2,0},{3,1},{4,6},{5,7},{6,4},{7,5},{8,10},{9,11},{10,... | collective-permute-start | bytes 196616 | tf_op jit(solution)/shard_map/ppermute | solution.py:29
  54.0 0.3 collective-permute-start.20
  54.3 6.9 %collective-permute-done.8.refs_0_.refs_6_ = bf16[2,64,2304]{2,1,0:T(8,128)(2,1)S(1)} collective-permute-done((bf16[2,64,2304]{2,1,0:T(8,128)(2,1)S(1)}, bf16[2,64,2304]{2,1,0:T(8,128)(2,1)S(1)}, u32[]{:S(2)}, u32[]{:S(2)}) %collective-permute-start.8) | collective-permute-done | bytes 589856 | tf_op jit(solution)/shard_map/ppermute | solution.py:407
  61.3 1.0 %shard_map.81.refs_0_ = bf16[2,64,128]{2,1,0:T(8,128)(2,1)S(1)} custom-call(s32[28]{0:T(128)S(1)} %get-tuple-element.14.plan_ref, bf16[8,128,2048]{2,1,0:T(8,128)(2,1)S(1)} %bitcast.6, bf16[2,64,2304]{2,1,0:T(8,128)(2,1)S(1)} %collective-permute-done.8.refs_0_.refs_6_, f32[2,64,128]{2,1,0:T(8,128)S(1)} %shard_map.80.refs_1_.refs_0_), custom_call_target="tpu_custom_call" | custom-call | tf_op jit(solution)/shard_map/pallas_call | solution.py:328
  62.3 0.1 collective-permute-start.15
  62.4 1.6 %collective-permute-start.16 = (bf16[2,64,128]{2,1,0:T(8,128)(2,1)S(1)}, bf16[2,64,128]{2,1,0:T(8,128)(2,1)S(1)}, u32[]{:S(2)}, u32[]{:S(2)}) collective-permute-start(bf16[2,64,128]{2,1,0:T(8,128)(2,1)S(1)} %shard_map.81.refs_0_), channel_id=1, source_target_pairs={{0,2},{1,3},{2,0},{3,1},{4,6},{5,7},{6,4},{7,5},{8,10},{9,11},{10,... | collective-permute-start | bytes 98312 | tf_op jit(solution)/shard_map/ppermute | solution.py:29
  63.9 0.0 collective-permute-done.18.refs_1_
  63.9 0.3 collective-permute-start.17
  64.2 0.0 collective-permute-done.19.refs_2_
  64.3 0.0 collective-permute-done.20.refs_3_
  64.3 1.4 %shard_map.82.refs_7_ = bf16[1024,256]{1,0:T(8,128)(2,1)} custom-call(s32[28]{0:T(128)S(1)} %get-tuple-element.14.plan_ref, f32[2,64,128]{2,1,0:T(8,128)S(1)} %shard_map.80.refs_1_.refs_0_, f32[2,64,128]{2,1,0:T(8,128)S(1)} %collective-permute-done.18.refs_1_, f32[2,64,128]{2,1,0:T(8,128)S(1)} %collective-permute-done.19.refs_2_, ...), custom_call_target="tpu_custom_call", output_to_operand_aliasing={{}: (9, {})} | custom-call | tf_op jit(solution)/shard_map/pallas_call | solution.py:390
  65.7 0.0 collective-permute-done.15.refs_1_
  65.7 0.6 collective-permute-done.16.refs_2_
  66.4 0.9 %collective-permute-done.17.refs_3_ = bf16[2,64,128]{2,1,0:T(8,128)(2,1)S(1)} collective-permute-done((bf16[2,64,128]{2,1,0:T(8,128)(2,1)S(1)}, bf16[2,64,128]{2,1,0:T(8,128)(2,1)S(1)}, u32[]{:S(2)}, u32[]{:S(2)}) %collective-permute-start.17) | collective-permute-done | bytes 32800 | tf_op jit(solution)/shard_map/ppermute | solution.py:29
  67.3 1.4 %shard_map.83 = bf16[1024,256]{1,0:T(8,128)(2,1)} custom-call(s32[28]{0:T(128)S(1)} %get-tuple-element.14.plan_ref, bf16[2,64,128]{2,1,0:T(8,128)(2,1)S(1)} %shard_map.81.refs_0_, bf16[2,64,128]{2,1,0:T(8,128)(2,1)S(1)} %collective-permute-done.15.refs_1_, bf16[2,64,128]{2,1,0:T(8,128)(2,1)S(1)} %collective-permute-done.16.refs_2_, ...), custom_call_target="tpu_custom_call", output_to_operand_aliasing={{}: (8, {})} | custom-call | tf_op jit(solution)/shard_map/pallas_call | solution.py:390
Async XLA Ops:
  0.0 16.2 %collective-permute-start = (s32[1,8]{1,0:T(1,128)}, s32[1,8]{1,0:T(1,128)S(1)}, u32[]{:S(2)}, u32[]{:S(2)}) collective-permute-start(s32[1,8]{1,0:T(1,128)} %refs_0_.1), channel_id=1, source_target_pairs={{0,4},{4,0},{8,12},{12,8},{1,5},{5,1},{9,13},{13,9},{2,6},{6,2},{1... | collective-permute-start | bytes 104 | tf_op jit(solution)/shard_map/ppermute | solution.py:29
  3.0 13.3 %collective-permute-start.1 = (s32[1,8]{1,0:T(1,128)}, s32[1,8]{1,0:T(1,128)S(1)}, u32[]{:S(2)}, u32[]{:S(2)}) collective-permute-start(s32[1,8]{1,0:T(1,128)} %refs_0_.1), channel_id=1, source_target_pairs={{0,8},{4,12},{8,0},{12,4},{1,9},{5,13},{9,1},{13,5},{2,10},{6,14},... | collective-permute-start | bytes 104 | tf_op jit(solution)/shard_map/ppermute | solution.py:29
  5.6 11.2 %collective-permute-start.2 = (s32[1,8]{1,0:T(1,128)}, s32[1,8]{1,0:T(1,128)S(1)}, u32[]{:S(2)}, u32[]{:S(2)}) collective-permute-start(s32[1,8]{1,0:T(1,128)} %refs_0_.1), channel_id=1, source_target_pairs={{0,12},{4,8},{8,4},{12,0},{1,13},{5,9},{9,5},{13,1},{2,14},{6,10},... | collective-permute-start | bytes 104 | tf_op jit(solution)/shard_map/ppermute | solution.py:29
  5.6 11.3 %collective-permute-start.3 = (bf16[4,64,256]{2,1,0:T(8,128)(2,1)}, bf16[4,64,256]{2,1,0:T(8,128)(2,1)S(1)}, u32[]{:S(2)}, u32[]{:S(2)}) collective-permute-start(bf16[4,64,256]{2,1,0:T(8,128)(2,1)} %refs_6_.1), channel_id=1, source_target_pairs={{0,0},{4,8},{8,4},{12,12},{1,1},{5,9},{9,5},{13,13},{2,2},{6,10},{... | collective-permute-start | bytes 393224 | tf_op jit(solution)/shard_map/ppermute | solution.py:407
  7.2 9.7 %copy-start.1 = (bf16[4,2048,64]{1,2,0:T(8,128)(2,1)S(1)}, bf16[4,2048,64]{1,2,0:T(8,128)(2,1)}, u32[]{:S(2)}) copy-start(bf16[4,2048,64]{1,2,0:T(8,128)(2,1)} %param.9) | copy-start | bytes 3145732
  7.2 9.7 %copy-start.2 = (bf16[4,64,256]{2,1,0:T(8,128)(2,1)S(1)}, bf16[4,64,256]{2,1,0:T(8,128)(2,1)}, u32[]{:S(2)}) copy-start(bf16[4,64,256]{2,1,0:T(8,128)(2,1)} %refs_6_.1) | copy-start | bytes 393220
  7.2 22.0 %collective-permute-start.4 = (bf16[4,64,2048]{2,1,0:T(8,128)(2,1)}, bf16[4,64,2048]{2,1,0:T(8,128)(2,1)S(1)}, u32[]{:S(2)}, u32[]{:S(2)}) collective-permute-start(bf16[4,64,2048]{2,1,0:T(8,128)(2,1)} %bitcast.14), channel_id=1, source_target_pairs={{0,0},{4,8},{8,4},{12,12},{1,1},{5,9},{9,5},{13,13},{2,2},{6,10},{... | collective-permute-start | bytes 3145736 | tf_op jit(solution)/shard_map/ppermute | solution.py:407
  16.2 5.9 %collective-permute-start.7 = (f32[2,256,256]{2,1,0:T(8,128)S(1)}, f32[2,256,256]{2,1,0:T(8,128)S(1)}, u32[]{:S(2)}, u32[]{:S(2)}) collective-permute-start(f32[2,256,256]{2,1,0:T(8,128)S(1)} %get-tuple-element.13.refs_9_), channel_id=1, source_target_pairs={{0,1},{1,0},{2,3},{3,2},{4,5},{5,4},{6,7},{7,6},{8,9},{9,8},{10,11... | collective-permute-start | bytes 1572872 | tf_op jit(solution)/shard_map/ppermute | solution.py:29
  16.3 5.8 %collective-permute-start.5 = (f32[2,384,256]{2,1,0:T(8,128)S(1)}, f32[2,384,256]{2,1,0:T(8,128)S(1)}, u32[]{:S(2)}, u32[]{:S(2)}) collective-permute-start(f32[2,384,256]{2,1,0:T(8,128)S(1)} %get-tuple-element.16), channel_id=1, source_target_pairs={{0,1},{1,0},{2,3},{3,2},{4,5},{5,4},{6,7},{7,6},{8,9},{9,8},{10,11... | collective-permute-start | bytes 2359304 | tf_op jit(solution)/shard_map/ppermute | solution.py:29
  16.8 5.3 %collective-permute-start.6 = (f32[2,384,256]{2,1,0:T(8,128)S(1)}, f32[2,384,256]{2,1,0:T(8,128)S(1)}, u32[]{:S(2)}, u32[]{:S(2)}) collective-permute-start(f32[2,384,256]{2,1,0:T(8,128)S(1)} %get-tuple-element.17), channel_id=1, source_target_pairs={{0,1},{1,0},{2,3},{3,2},{4,5},{5,4},{6,7},{7,6},{8,9},{9,8},{10,11... | collective-permute-start | bytes 2359304 | tf_op jit(solution)/shard_map/ppermute | solution.py:29
  18.7 19.1 %collective-permute-start.10 = (bf16[2,64,2304]{2,1,0:T(8,128)(2,1)S(1)}, bf16[2,64,2304]{2,1,0:T(8,128)(2,1)S(1)}, u32[]{:S(2)}, u32[]{:S(2)}) collective-permute-start(bf16[2,64,2304]{2,1,0:T(8,128)(2,1)S(1)} %get-tuple-element.19), channel_id=1, source_target_pairs={{0,4},{4,0},{8,12},{12,8},{1,5},{5,1},{9,13},{13,9},{2,6},{6,2},{1... | collective-permute-start | bytes 1769480 | tf_op jit(solution)/shard_map/ppermute | solution.py:407
  22.3 25.2 %collective-permute-start.14 = (bf16[1,1024,256]{2,1,0:T(8,128)(2,1)S(1)}, bf16[1,1024,256]{2,1,0:T(8,128)(2,1)S(1)}, u32[]{:S(2)}, u32[]{:S(2)}) collective-permute-start(bf16[1,1024,256]{2,1,0:T(8,128)(2,1)S(1)} %get-tuple-element.20), channel_id=1, source_target_pairs={{0,2},{1,3},{2,0},{3,1},{4,6},{5,7},{6,4},{7,5},{8,10},{9,11},{10,... | collective-permute-start | bytes 1572872 | tf_op jit(solution)/shard_map/ppermute | solution.py:29
  24.5 13.3 %copy-start = (bf16[1024,2048]{1,0:T(8,128)(2,1)S(1)}, bf16[1024,2048]{1,0:T(8,128)(2,1)}, u32[]{:S(2)}) copy-start(bf16[1024,2048]{1,0:T(8,128)(2,1)} %tokens_ref.1) | copy-start | bytes 12582916
  24.5 26.8 %collective-permute-start.9 = (bf16[2,64,2304]{2,1,0:T(8,128)(2,1)S(1)}, bf16[2,64,2304]{2,1,0:T(8,128)(2,1)S(1)}, u32[]{:S(2)}, u32[]{:S(2)}) collective-permute-start(bf16[2,64,2304]{2,1,0:T(8,128)(2,1)S(1)} %shard_map.76.refs_4_), channel_id=1, source_target_pairs={{0,12},{4,4},{8,8},{12,0},{1,13},{5,5},{9,9},{13,1},{2,14},{6,6},{... | collective-permute-start | bytes 1769480 | tf_op jit(solution)/shard_map/ppermute | solution.py:407
  29.8 31.4 %collective-permute-start.8 = (bf16[2,64,2304]{2,1,0:T(8,128)(2,1)S(1)}, bf16[2,64,2304]{2,1,0:T(8,128)(2,1)S(1)}, u32[]{:S(2)}, u32[]{:S(2)}) collective-permute-start(bf16[2,64,2304]{2,1,0:T(8,128)(2,1)S(1)} %shard_map.77.refs_2_), channel_id=1, source_target_pairs={{0,8},{4,0},{8,12},{12,4},{1,9},{5,1},{9,13},{13,5},{2,10},{6,2},{... | collective-permute-start | bytes 1769480 | tf_op jit(solution)/shard_map/ppermute | solution.py:407
  39.2 1.6 %collective-permute-start.11 = (f32[4,64,128]{2,1,0:T(8,128)S(1)}, f32[4,64,128]{2,1,0:T(8,128)S(1)}, u32[]{:S(2)}, u32[]{:S(2)}) collective-permute-start(f32[4,64,128]{2,1,0:T(8,128)S(1)} %shard_map.78.refs_0_), channel_id=1, source_target_pairs={{0,1},{1,0},{2,3},{3,2},{4,5},{5,4},{6,7},{7,6},{8,9},{9,8},{10,11... | collective-permute-start | bytes 393224 | tf_op jit(solution)/shard_map/ppermute | solution.py:29
  39.2 6.4 %collective-permute-start.12 = (f32[4,64,128]{2,1,0:T(8,128)S(1)}, f32[4,64,128]{2,1,0:T(8,128)S(1)}, u32[]{:S(2)}, u32[]{:S(2)}) collective-permute-start(f32[4,64,128]{2,1,0:T(8,128)S(1)} %shard_map.78.refs_0_), channel_id=1, source_target_pairs={{0,2},{1,3},{2,0},{3,1},{4,6},{5,7},{6,4},{7,5},{8,10},{9,11},{10,... | collective-permute-start | bytes 393224 | tf_op jit(solution)/shard_map/ppermute | solution.py:29
  40.8 6.7 %collective-permute-start.13 = (f32[4,64,128]{2,1,0:T(8,128)S(1)}, f32[4,64,128]{2,1,0:T(8,128)S(1)}, u32[]{:S(2)}, u32[]{:S(2)}) collective-permute-start(f32[4,64,128]{2,1,0:T(8,128)S(1)} %shard_map.78.refs_0_), channel_id=1, source_target_pairs={{0,3},{1,2},{2,1},{3,0},{4,7},{5,6},{6,5},{7,4},{8,11},{9,10},{10,... | collective-permute-start | bytes 393224 | tf_op jit(solution)/shard_map/ppermute | solution.py:29
  52.4 11.6 %collective-permute-start.18 = (f32[2,64,128]{2,1,0:T(8,128)S(1)}, f32[2,64,128]{2,1,0:T(8,128)S(1)}, u32[]{:S(2)}, u32[]{:S(2)}) collective-permute-start(f32[2,64,128]{2,1,0:T(8,128)S(1)} %shard_map.80.refs_1_.refs_0_), channel_id=1, source_target_pairs={{0,1},{1,0},{2,3},{3,2},{4,5},{5,4},{6,7},{7,6},{8,9},{9,8},{10,11... | collective-permute-start | bytes 196616 | tf_op jit(solution)/shard_map/ppermute | solution.py:29
  52.5 11.8 %collective-permute-start.19 = (f32[2,64,128]{2,1,0:T(8,128)S(1)}, f32[2,64,128]{2,1,0:T(8,128)S(1)}, u32[]{:S(2)}, u32[]{:S(2)}) collective-permute-start(f32[2,64,128]{2,1,0:T(8,128)S(1)} %shard_map.80.refs_1_.refs_0_), channel_id=1, source_target_pairs={{0,2},{1,3},{2,0},{3,1},{4,6},{5,7},{6,4},{7,5},{8,10},{9,11},{10,... | collective-permute-start | bytes 196616 | tf_op jit(solution)/shard_map/ppermute | solution.py:29
  54.0 10.2 %collective-permute-start.20 = (f32[2,64,128]{2,1,0:T(8,128)S(1)}, f32[2,64,128]{2,1,0:T(8,128)S(1)}, u32[]{:S(2)}, u32[]{:S(2)}) collective-permute-start(f32[2,64,128]{2,1,0:T(8,128)S(1)} %shard_map.80.refs_1_.refs_0_), channel_id=1, source_target_pairs={{0,3},{1,2},{2,1},{3,0},{4,7},{5,6},{6,5},{7,4},{8,11},{9,10},{10,... | collective-permute-start | bytes 196616 | tf_op jit(solution)/shard_map/ppermute | solution.py:29
  62.3 3.4 %collective-permute-start.15 = (bf16[2,64,128]{2,1,0:T(8,128)(2,1)S(1)}, bf16[2,64,128]{2,1,0:T(8,128)(2,1)S(1)}, u32[]{:S(2)}, u32[]{:S(2)}) collective-permute-start(bf16[2,64,128]{2,1,0:T(8,128)(2,1)S(1)} %shard_map.81.refs_0_), channel_id=1, source_target_pairs={{0,1},{1,0},{2,3},{3,2},{4,5},{5,4},{6,7},{7,6},{8,9},{9,8},{10,11... | collective-permute-start | bytes 98312 | tf_op jit(solution)/shard_map/ppermute | solution.py:29
  62.4 4.0 %collective-permute-start.16 = (bf16[2,64,128]{2,1,0:T(8,128)(2,1)S(1)}, bf16[2,64,128]{2,1,0:T(8,128)(2,1)S(1)}, u32[]{:S(2)}, u32[]{:S(2)}) collective-permute-start(bf16[2,64,128]{2,1,0:T(8,128)(2,1)S(1)} %shard_map.81.refs_0_), channel_id=1, source_target_pairs={{0,2},{1,3},{2,0},{3,1},{4,6},{5,7},{6,4},{7,5},{8,10},{9,11},{10,... | collective-permute-start | bytes 98312 | tf_op jit(solution)/shard_map/ppermute | solution.py:29
  63.9 3.3 %collective-permute-start.17 = (bf16[2,64,128]{2,1,0:T(8,128)(2,1)S(1)}, bf16[2,64,128]{2,1,0:T(8,128)(2,1)S(1)}, u32[]{:S(2)}, u32[]{:S(2)}) collective-permute-start(bf16[2,64,128]{2,1,0:T(8,128)(2,1)S(1)} %shard_map.81.refs_0_), channel_id=1, source_target_pairs={{0,3},{1,2},{2,1},{3,0},{4,7},{5,6},{6,5},{7,4},{8,11},{9,10},{10,... | collective-permute-start | bytes 98312 | tf_op jit(solution)/shard_map/ppermute | solution.py:29
